TPU v7x, 32 devices: a whole 2x2x4 slice. The times are simulated.
32 devices in a mesh: row: 4 (over z), col: 8 (over y, x, core).
Axes of the slice: x: 2, y: 2, z: 4, core: 2. Of those that a mesh axis runs over, the one named last changes fastest.
Arguments:
- pair: bfloat16 [512, 512, 128], P('row', 'col'), may hold values from -6 to 6
- grad_x: bfloat16 [512, 512, 64], P('row', 'col'), may hold values from -0.19921875 to 0.19921875
- norm_gain: float32 [128], replicated, may hold values from 0.1 to 1.9
- norm_bias: float32 [128], replicated, may hold values from -3 to 3
- proj_weight: bfloat16 [128, 256], replicated, may hold values from -0.5 to 0.5
- tile_mask: int32 [4, 4], replicated, may hold values 0 or 1
Outputs:
- grad_pair: bfloat16 [512, 512, 128], P('row', 'col')
All inputs are finite; a program needn't handle non-finite values.
Results may differ from a plain program's by a relative error of at most 0.012.
Values may be sent and summed in bfloat16 or wider, within the bound.
No kernel may reach another device: no remote copies, remote signals or barrier semaphores. Data moves between devices by JAX's collectives and lax.ppermute only.
A program may use at most 128 MiB of HBM per device.

v0:
```python
import jax
import jax.numpy as jnp
from jax import lax
from jax.sharding import PartitionSpec as P

BLK = 128


def normalize(pair, norm_gain, norm_bias):
    values = pair.astype(jnp.float32)
    centred = values - jnp.mean(values, axis=-1, keepdims=True)
    variance = jnp.mean(centred * centred, axis=-1, keepdims=True)
    inverse = lax.rsqrt(variance + 1e-05)
    scaled = centred * inverse
    normed = (scaled * norm_gain + norm_bias).astype(jnp.bfloat16)
    return (scaled, inverse, normed)


def block_onehot(first_index, length, blocks):
    positions = first_index + jnp.arange(length, dtype=jnp.int32)
    block_range = jnp.arange(blocks, dtype=jnp.int32)
    return ((positions // BLK)[:, None] == block_range[None, :]).astype(jnp.float32)


def shards(pair, grad_x, norm_gain, norm_bias, proj_weight, tile_mask):
    row_count = pair.shape[0]
    col_count = pair.shape[1]
    hidden = grad_x.shape[2]
    total_rows = row_count * lax.axis_size("row")
    row_first = lax.axis_index("row") * row_count
    col_first = lax.axis_index("col") * col_count
    scaled, inverse, normed = normalize(pair, norm_gain, norm_bias)
    projected = jnp.einsum("ijc,cd->ijd", normed, proj_weight, preferred_element_type=jnp.float32)
    blocks = total_rows // BLK
    row_onehot = block_onehot(row_first, row_count, blocks)
    col_onehot = block_onehot(col_first, col_count, blocks)
    valid_tile = jnp.dot(jnp.dot(row_onehot, tile_mask.astype(jnp.float32)), col_onehot.T)[
        :, :, None
    ]
    lin_left = projected[:, :, 0:hidden]
    gate_left = projected[:, :, hidden : 2 * hidden]
    lin_right = projected[:, :, 2 * hidden : 3 * hidden]
    gate_right = projected[:, :, 3 * hidden : 4 * hidden]
    sig_left = jax.nn.sigmoid(gate_left)
    sig_right = jax.nn.sigmoid(gate_right)
    left_act = (valid_tile * sig_left * lin_left).astype(jnp.bfloat16)
    right_act = (valid_tile * sig_right * lin_right).astype(jnp.bfloat16)
    right_panel = lax.all_gather(right_act, "row", axis=0, tiled=True)
    grad_panel = lax.all_gather(grad_x, "col", axis=1, tiled=True)
    grad_left = jnp.einsum(
        "ijc,jkc->ikc", grad_panel, right_panel, preferred_element_type=jnp.float32
    )
    grad_right = lax.psum_scatter(
        jnp.einsum("ijc,ikc->jkc", grad_panel, left_act, preferred_element_type=jnp.float32).astype(
            jnp.bfloat16
        ),
        "row",
        scatter_dimension=0,
        tiled=True,
    ).astype(jnp.float32)
    grad_proj = jnp.concatenate(
        [
            grad_left * valid_tile * sig_left,
            grad_left * valid_tile * lin_left * sig_left * (1.0 - sig_left),
            grad_right * valid_tile * sig_right,
            grad_right * valid_tile * lin_right * sig_right * (1.0 - sig_right),
        ],
        axis=-1,
    ).astype(jnp.bfloat16)
    grad_normed = jnp.einsum(
        "ijd,cd->ijc", grad_proj, proj_weight, preferred_element_type=jnp.float32
    )
    scaled_grad = grad_normed * norm_gain
    result = inverse * (
        scaled_grad
        - jnp.mean(scaled_grad, axis=-1, keepdims=True)
        - scaled * jnp.mean(scaled_grad * scaled, axis=-1, keepdims=True)
    )
    return result.astype(jnp.bfloat16)


def solution(mesh):
    placed = (P("row", "col", None), P("row", "col", None), P(), P(), P(), P())
    return jax.shard_map(
        shards, mesh=mesh, in_specs=placed, out_specs=P("row", "col", None), check_vma=False
    )
```

profile of v0, /device:TPU:0, one launch (start us, length us, event | category | flops | bytes accessed | tf_op | source)
XLA Modules:
  0.0 300.5 jit_solution(13250947203571921999)
XLA Ops:
  6.5 0.0 copy-start
  6.5 0.0 all-gather.3.cloned.1.call-start
  6.6 0.0 copy-start.8
  6.6 0.0 copy-start.6
  6.6 0.0 copy-start.7
  6.6 3.3 %copy.28 = bf16[128,64,128]{0,2,1:T(8,128)(2,1)S(1)} copy(bf16[128,64,128]{2,1,0:T(8,128)(2,1)} %param.6) | data formatting | bytes 4194304 | tf_op args[0]
  10.0 0.5 convert_reduce_fusion
  10.5 0.8 fusion.11
  11.3 0.0 copy-done.8
  11.3 0.3 fusion.34
  11.6 0.0 copy-done
  11.6 0.0 copy-done.6
  11.7 0.0 copy-done.7
  11.7 1.4 fusion.22
  13.0 0.0 copy-start.2
  13.1 3.2 %copy-done.2 = f32[128,64,256]{0,2,1:T(8,128)} copy-done((f32[128,64,256]{0,2,1:T(8,128)}, f32[128,64,256]{0,2,1:T(8,128)S(1)}, u32[]{:S(2)}) %copy-start.2) | copy-done | bytes 8388632
  16.3 0.0 copy-start.5
  16.3 1.6 multiply_convert_fusion.5
  17.9 0.0 all-gather.3.cloned.1.call-update
  17.9 0.0 all-gather.5.cloned.1.call-start
  18.0 0.0 copy-done.5
  18.0 1.6 copy.32
  19.6 0.0 all-gather.5.cloned.1.call-update
  19.6 0.2 reduce-scatter.4.cloned.1.call-start
  19.9 81.5 %all-gather.3.cloned.1.call-done = bf16[512,64,64]{0,2,1:T(8,128)(2,1)} async-done(((bf16[128,64,64]{0,2,1:T(8,128)(2,1)}), bf16[512,64,64]{0,2,1:T(8,128)(2,1)}) %all-gather.3.cloned.1.call-update) | async-done | bytes 4194320 | tf_op jit(solution)/shard_map/all_gather | solution.py:48
  101.3 54.5 %all-gather.5.cloned.1.call-done = bf16[128,512,64]{0,1,2:T(8,128)(2,1)} async-done(((bf16[128,64,64]{0,1,2:T(8,128)(2,1)}), bf16[128,512,64]{0,1,2:T(8,128)(2,1)}) %all-gather.5.cloned.1.call-update) | async-done | bytes 8388624 | tf_op jit(solution)/shard_map/all_gather | solution.py:49
  155.8 9.5 %fusion.20 = f32[64,64,128]{2,1,0:T(8,128)S(1)} fusion(bf16[128,512,64]{0,1,2:T(8,128)(2,1)} %all-gather.5.cloned.1.call-done, bf16[512,64,64]{0,2,1:T(8,128)(2,1)} %all-gather.3.cloned.1.call-done), kind=kOutput, calls=%fused_computation.22 | convolution fusion | flops 536870912 | bytes 14680064 | tf_op jit(solution)/shard_map/ijc,jkc->ikc/dot_general | solution.py:50
  165.3 0.0 copy-start.1
  165.3 5.6 %multiply_convert_fusion.4 = (bf16[128,64,64]{0,2,1:T(8,128)(2,1)}, bf16[128,64,64]{0,2,1:T(8,128)(2,1)}, bf16[128,64,64]{0,2,1:T(8,128)(2,1)S(1)}) fusion(f32[64,64,128]{2,1,0:T(8,128)S(1)} %fusion.20, f32[128,64]{0,1:T(8,128)S(1)} %fusion.34, f32[128,64,256]{0,2,1:T(8,128)} %copy-done.2), kind=kLoop, calls=%fused_computation.41 | loop fusion | flops 7340032 | bytes 9469952 | tf_op jit(solution)/shard_map/convert
  170.9 0.0 copy-done.1
  170.9 5.0 %convert_bitcast_fusion = bf16[512,64,64]{0,1,2:T(8,128)(2,1)} fusion(bf16[128,512,64]{0,1,2:T(8,128)(2,1)S(1)} %copy-done.1, bf16[128,64,64]{0,2,1:T(8,128)(2,1)S(1)} %get-tuple-element.11), kind=kOutput, calls=%fused_computation.24 | convolution fusion | flops 538968064 | bytes 13631488 | tf_op jit(solution)/shard_map/ijc,ikc->jkc/dot_general | solution.py:54
  175.9 15.6 %copy.44 = bf16[512,64,64]{2,1,0:T(8,128)(2,1)} copy(bf16[512,64,64]{0,1,2:T(8,128)(2,1)} %convert_bitcast_fusion) | data formatting | bytes 8388608
  191.5 12.0 %reshape.62 = bf16[512,4096]{1,0:T(8,128)(2,1)} reshape(bf16[512,64,64]{2,1,0:T(8,128)(2,1)} %copy.44) | data formatting | bytes 8388608
  203.5 0.0 reduce-scatter.4.cloned.1.call-update
  203.6 76.9 %reduce-scatter.4.cloned.1.call-done = bf16[128,4096]{1,0:T(8,128)(2,1)} async-done(((bf16[512,4096]{1,0:T(8,128)(2,1)}), bf16[128,4096]{1,0:T(8,128)(2,1)}) %reduce-scatter.4.cloned.1.call-update) | async-done | bytes 1048592
  280.5 1.6 copy.47
  282.1 0.0 copy-start.3
  282.1 0.0 copy-start.4
  282.1 3.3 %multiply_convert_fusion.1 = (bf16[128,64,64]{0,2,1:T(8,128)(2,1)S(1)}, bf16[128,64,64]{0,2,1:T(8,128)(2,1)S(1)}) fusion(bf16[128,64,64]{0,2,1:T(8,128)(2,1)S(1)} %bitcast.19, f32[128,64]{0,1:T(8,128)S(1)} %fusion.34, f32[128,64,256]{0,2,1:T(8,128)} %copy-done.2), kind=kLoop, calls=%fused_computation.37 | loop fusion | flops 6291456 | bytes 7372800 | tf_op jit(solution)/shard_map/convert.2
  285.4 0.0 copy-done.3
  285.4 0.0 copy-done.4
  285.5 1.5 multiply_reduce_fusion
  287.0 2.8 fusion.10
  289.8 4.1 %copy.40 = bf16[128,64,128]{2,1,0:T(8,128)(2,1)} copy(bf16[128,64,128]{0,2,1:T(8,128)(2,1)} %fusion.10) | data formatting | bytes 4194304 | tf_op jit(solution)/shard_map/convert_element_type | solution.py:79
  (5 shorter events, 0.0 us)
Async XLA Ops:
  6.5 5.1 %copy-start = (bf16[128,256]{1,0:T(8,128)(2,1)S(1)}, bf16[128,256]{1,0:T(8,128)(2,1)}, u32[]{:S(2)}) copy-start(bf16[128,256]{1,0:T(8,128)(2,1)} %param.10) | copy-start | bytes 196612
  6.5 94.8 %all-gather.3.cloned.1.call-start = ((), (), s32[]{:S(2)}) async-start(), calls=%async_computation.1 | async-start | bytes 5242880 | tf_op jit(solution)/shard_map/all_gather | solution.py:48
  6.6 4.7 %copy-start.8 = (s32[4,4]{1,0:T(4,128)S(1)}, s32[4,4]{1,0:T(4,128)}, u32[]{:S(2)}) copy-start(s32[4,4]{1,0:T(4,128)} %param.11) | copy-start | bytes 196
  6.6 5.1 %copy-start.6 = (f32[128]{0:T(128)S(1)}, f32[128]{0:T(128)}, u32[]{:S(2)}) copy-start(f32[128]{0:T(128)} %param.8) | copy-start | bytes 1540
  6.6 5.1 %copy-start.7 = (f32[128]{0:T(128)S(1)}, f32[128]{0:T(128)}, u32[]{:S(2)}) copy-start(f32[128]{0:T(128)} %param.9) | copy-start | bytes 1540
  13.0 3.2 %copy-start.2 = (f32[128,64,256]{0,2,1:T(8,128)}, f32[128,64,256]{0,2,1:T(8,128)S(1)}, u32[]{:S(2)}) copy-start(f32[128,64,256]{0,2,1:T(8,128)S(1)} %fusion.22) | copy-start | bytes 25165828
  16.3 1.7 copy-start.5
  17.9 137.9 %all-gather.5.cloned.1.call-start = ((), (), s32[]{:S(2)}) async-start(), calls=%async_computation.2 | async-start | bytes 9437184 | tf_op jit(solution)/shard_map/all_gather | solution.py:49
  19.6 260.9 %reduce-scatter.4.cloned.1.call-start = ((), (), s32[]{:S(2)}) async-start(), calls=%async_computation.3 | async-start | bytes 5242880
  165.3 5.6 %copy-start.1 = (bf16[128,512,64]{0,1,2:T(8,128)(2,1)S(1)}, bf16[128,512,64]{0,1,2:T(8,128)(2,1)}, u32[]{:S(2)}) copy-start(bf16[128,512,64]{0,1,2:T(8,128)(2,1)} %all-gather.5.cloned.1.call-done) | copy-start | bytes 25165828
  282.1 3.3 %copy-start.3 = (bf16[128,64,64]{0,2,1:T(8,128)(2,1)S(1)}, bf16[128,64,64]{0,2,1:T(8,128)(2,1)}, u32[]{:S(2)}) copy-start(bf16[128,64,64]{0,2,1:T(8,128)(2,1)} %get-tuple-element.7) | copy-start | bytes 3145732
  282.1 3.3 %copy-start.4 = (bf16[128,64,64]{0,2,1:T(8,128)(2,1)S(1)}, bf16[128,64,64]{0,2,1:T(8,128)(2,1)}, u32[]{:S(2)}) copy-start(bf16[128,64,64]{0,2,1:T(8,128)(2,1)} %get-tuple-element.8) | copy-start | bytes 3145732
Sparse Core Ops, SparseCore 0:
  18.0 83.2 all-gather.2
  103.2 52.5 all-gather.4
  203.7 76.7 reduce-scatter.3
where the time goes:
time: 301 us; the launch traced here: 300 us
  waiting for transfers between devices  213 us (71%)
  local copies, waits for them, and re-layouts  41.6 us (14%)
  matrix products  17.7 us (6%)
  other arithmetic  14.6 us (5%)
  between operations  13.3 us (4%)
    all_gather x1, waiting for transfers between devices, shards(): right_panel = lax.all_gather(right_act, 'row', axis=0, tiled=True)  81.5 us
    unnamed x4, waiting for transfers between devices  77 us
    all_gather x1, waiting for transfers between devices, shards(): grad_panel = lax.all_gather(grad_x, 'col', axis=1, tiled=True)  54.5 us
    unnamed x23, local copies, waits for them, and re-layouts  37.5 us
    dot_general x1, matrix products, shards(): jnp.einsum('ijc,jkc->ikc', grad_panel, right_panel, preferred_element_typ...  9.5 us
    another operation x2, other arithmetic  8.89 us
  transfers between devices with their start and end apart: 3, of which 3 were waited for; matrix products, arithmetic and copies ran while one was open for 1% of the time, Pallas kernels for 0%

commit v1 on v0

v1 whole, which is shorter than its diff:
```python
import functools

import jax
import jax.numpy as jnp
from jax import lax
from jax.experimental import pallas as pl
from jax.experimental.pallas import tpu as pltpu
from jax.sharding import PartitionSpec as P

BLK = 128
CHUNKS = 2
SUBS = 2
VMEM_LIMIT = 48 * 1024 * 1024


def exchange(value, axis, size, mask):
    return lax.ppermute(value, axis, [(d, d ^ mask) for d in range(size)])


def gather_columns(block, size, order):
    slots = {0: block}
    for bit in order:
        for m in list(slots):
            slots[m | bit] = exchange(slots[m], "col", size, bit)
    return [slots[m] for m in range(size)]


def copy_panel(g_refs, panel, sems, col, subs, slots):
    copies = []
    sub_len, cols = g_refs[0].shape[0], g_refs[0].shape[1]
    for s in range(subs):
        for m in range(slots):
            place = pl.multiple_of(jnp.bitwise_xor(col, m) * cols, cols)
            copies.append(
                pltpu.make_async_copy(
                    g_refs[s * slots + m],
                    panel.at[pl.ds(s * sub_len, sub_len), pl.ds(place, cols), :],
                    sems.at[s * slots + m],
                )
            )
    return copies


def partial_kernel(subs, slots, n, ids, left, *refs):
    g_refs, outs, (panel, sems) = refs[: subs * slots], refs[subs * slots : subs * slots + n], refs[subs * slots + n :]
    row, col = ids[0], ids[1]
    copies = copy_panel(g_refs, panel, sems, col, subs, slots)
    for c in copies:
        c.start()
    for c in copies:
        c.wait()
    rows = left.shape[2]

    def body(c, carry):
        lhs = left[c]
        for s in range(n):
            b = lax.rem(row + s, n)
            rhs = panel[c, pl.ds(pl.multiple_of(b * rows, rows), rows), :]
            out = lax.dot_general(lhs, rhs, (((1,), (1,)), ((), ())), preferred_element_type=jnp.float32)
            outs[s][c] = out.astype(jnp.bfloat16)
        return carry

    lax.fori_loop(0, left.shape[0], body, 0, unroll=4)


def partial_products(ids, left, g_slots, n):
    subs, slots = len(g_slots), len(g_slots[0])
    chans, ks, rows = left.shape
    sub_len, cols, _ = g_slots[0][0].shape
    flat = [g for sub in g_slots for g in sub]
    out = jax.ShapeDtypeStruct((chans, ks, rows), jnp.bfloat16)
    return pl.pallas_call(
        functools.partial(partial_kernel, subs, slots, n),
        out_shape=[out] * n,
        in_specs=[pl.BlockSpec(memory_space=pltpu.SMEM), pl.BlockSpec(memory_space=pltpu.VMEM)]
        + [pl.BlockSpec(memory_space=pl.ANY)] * len(flat),
        out_specs=[pl.BlockSpec(memory_space=pltpu.VMEM)] * n,
        scratch_shapes=[
            pltpu.VMEM((chans, slots * cols, rows), jnp.bfloat16),
            pltpu.SemaphoreType.DMA((len(flat),)),
        ],
        compiler_params=pltpu.CompilerParams(vmem_limit_bytes=VMEM_LIMIT),
        cost_estimate=pl.CostEstimate(
            flops=2 * chans * ks * rows * n * rows, bytes_accessed=2 * chans * rows * (slots * cols + ks * (n + 1)), transcendentals=0
        ),
        name="right_partials",
    )(ids, left, *flat)


def left_kernel(subs, slots, n, ids, own, *refs):
    ups, downs, refs = refs[: n - 1], refs[n - 1 : 2 * n - 2], refs[2 * n - 2 :]
    g_refs, (out, panel, acts, sems, act_sems) = refs[: subs * slots], refs[subs * slots :]
    row, col = ids[0], ids[1]
    copies = copy_panel(g_refs, panel, sems, col, subs, slots)
    for c in copies:
        c.start()
    rows = own.shape[2]

    def place(b):
        return acts.at[:, :, pl.ds(pl.multiple_of(b * rows, rows), rows)]

    moved = [(None, pltpu.make_async_copy(own, place(row), act_sems.at[0]))]
    for h in range(1, n):
        moved.append((row >= h, pltpu.make_async_copy(ups[h - 1], place(jnp.maximum(row - h, 0)), act_sems.at[h])))
        moved.append(
            (row + h < n, pltpu.make_async_copy(downs[h - 1], place(jnp.minimum(row + h, n - 1)), act_sems.at[n - 1 + h]))
        )
    for use, c in moved:
        if use is None:
            c.start()
        else:
            pl.when(use)(c.start)
    for use, c in moved:
        if use is None:
            c.wait()
        else:
            pl.when(use)(c.wait)
    for c in copies:
        c.wait()

    def body(c, carry):
        out[c] = jnp.dot(acts[c], panel[c], preferred_element_type=jnp.float32)
        return carry

    lax.fori_loop(0, out.shape[0], body, 0, unroll=4)


def left_products(ids, own, ups, downs, g_slots, n):
    subs, slots = len(g_slots), len(g_slots[0])
    chans, ks, rows = own.shape
    sub_len, cols, _ = g_slots[0][0].shape
    flat = [g for sub in g_slots for g in sub]
    return pl.pallas_call(
        functools.partial(left_kernel, subs, slots, n),
        out_shape=jax.ShapeDtypeStruct((chans, ks, rows), jnp.float32),
        in_specs=[pl.BlockSpec(memory_space=pltpu.SMEM)] + [pl.BlockSpec(memory_space=pl.ANY)] * (2 * n - 1 + len(flat)),
        out_specs=pl.BlockSpec(memory_space=pltpu.VMEM),
        scratch_shapes=[
            pltpu.VMEM((chans, slots * cols, rows), jnp.bfloat16),
            pltpu.VMEM((chans, ks, n * rows), jnp.bfloat16),
            pltpu.SemaphoreType.DMA((len(flat),)),
            pltpu.SemaphoreType.DMA((2 * n - 1,)),
        ],
        compiler_params=pltpu.CompilerParams(vmem_limit_bytes=VMEM_LIMIT),
        cost_estimate=pl.CostEstimate(
            flops=2 * chans * ks * rows * n * rows, bytes_accessed=2 * chans * rows * (slots * cols + ks * (n + 2)), transcendentals=0
        ),
        name="left_products",
    )(ids, own, *ups, *downs, *flat)


def shards(pair, grad_x, norm_gain, norm_bias, proj_weight, tile_mask):
    row_count, col_count, _ = pair.shape
    hidden = grad_x.shape[2]
    n, n_col = lax.axis_size("row"), lax.axis_size("col")
    row, col = lax.axis_index("row"), lax.axis_index("col")
    ids = jnp.stack([row, col]).astype(jnp.int32)
    part = hidden // CHUNKS
    sub = part // SUBS

    grad_t = jnp.transpose(grad_x, (2, 1, 0))
    bits = [1 << b for b in range(1, n_col.bit_length() - 1)]
    g_slots = []
    for chunk in range(CHUNKS):
        subs = []
        for s in range(SUBS):
            first = chunk * part + s * sub
            turn = s % max(len(bits), 1)
            order = bits[turn:] + bits[:turn] + [1]
            subs.append(gather_columns(grad_t[first : first + sub], n_col, order))
        g_slots.append(subs)

    values = jnp.transpose(pair, (1, 2, 0)).astype(jnp.float32)
    centred = values - jnp.mean(values, axis=1, keepdims=True)
    inverse = lax.rsqrt(jnp.mean(centred * centred, axis=1, keepdims=True) + 1e-05)
    scaled = centred * inverse
    normed = (scaled * norm_gain[None, :, None] + norm_bias[None, :, None]).astype(jnp.bfloat16)
    projected = jnp.einsum("kca,cd->kda", normed, proj_weight, preferred_element_type=jnp.float32)
    row_block = (row * row_count + jnp.arange(row_count, dtype=jnp.int32)) // BLK
    col_block = (col * col_count + jnp.arange(col_count, dtype=jnp.int32)) // BLK
    blocks = jnp.arange(tile_mask.shape[0], dtype=jnp.int32)
    row_onehot = (row_block[:, None] == blocks[None, :]).astype(jnp.float32)
    col_onehot = (col_block[:, None] == blocks[None, :]).astype(jnp.float32)
    valid = jnp.dot(jnp.dot(col_onehot, tile_mask.astype(jnp.float32).T), row_onehot.T)[:, None, :]
    lin_left = projected[:, 0:hidden]
    gate_left = projected[:, hidden : 2 * hidden]
    lin_right = projected[:, 2 * hidden : 3 * hidden]
    gate_right = projected[:, 3 * hidden : 4 * hidden]
    sig_left = jax.nn.sigmoid(gate_left)
    sig_right = jax.nn.sigmoid(gate_right)
    left_act = jnp.transpose((valid * sig_left * lin_left).astype(jnp.bfloat16), (1, 0, 2))
    right_act = jnp.transpose((valid * sig_right * lin_right).astype(jnp.bfloat16), (1, 0, 2))

    lefts, rights = [], []
    for chunk in range(CHUNKS):
        cut = slice(chunk * part, (chunk + 1) * part)
        own = right_act[cut]
        ups, downs = [], []
        up, down = own, own
        for h in range(1, n):
            up = lax.ppermute(up, "row", [(r, r + 1) for r in range(h - 1, n - 1)])
            down = lax.ppermute(down, "row", [(r, r - 1) for r in range(1, n - h + 1)])
            ups.append(up)
            downs.append(down)
        partials = partial_products(ids, left_act[cut], g_slots[chunk], n)
        up = down = None
        for step in range(1, n):
            away = n - step
            up_sum, down_sum = partials[away], partials[n - away]
            if up is not None:
                up_sum = (up_sum.astype(jnp.float32) + up.astype(jnp.float32)).astype(jnp.bfloat16)
                down_sum = (down_sum.astype(jnp.float32) + down.astype(jnp.float32)).astype(jnp.bfloat16)
            up = lax.ppermute(up_sum, "row", [(r, r + 1) for r in range(step)])
            down = lax.ppermute(down_sum, "row", [(r, r - 1) for r in range(n - step, n)])
        rights.append((partials[0], up, down))
        lefts.append(left_products(ids, own, ups, downs, g_slots[chunk], n))

    grad_left = jnp.transpose(jnp.concatenate(lefts, axis=0), (1, 0, 2))
    grad_right = jnp.concatenate(
        [p.astype(jnp.float32) + u.astype(jnp.float32) + d.astype(jnp.float32) for p, u, d in rights], axis=0
    )
    grad_right = jnp.transpose(grad_right, (1, 0, 2))
    grad_proj = jnp.concatenate(
        [
            grad_left * valid * sig_left,
            grad_left * valid * lin_left * sig_left * (1.0 - sig_left),
            grad_right * valid * sig_right,
            grad_right * valid * lin_right * sig_right * (1.0 - sig_right),
        ],
        axis=1,
    ).astype(jnp.bfloat16)
    grad_normed = jnp.einsum("kda,cd->kca", grad_proj, proj_weight, preferred_element_type=jnp.float32)
    scaled_grad = grad_normed * norm_gain[None, :, None]
    result = inverse * (
        scaled_grad
        - jnp.mean(scaled_grad, axis=1, keepdims=True)
        - scaled * jnp.mean(scaled_grad * scaled, axis=1, keepdims=True)
    )
    return jnp.transpose(result.astype(jnp.bfloat16), (2, 0, 1))


def solution(mesh):
    placed = (P("row", "col", None), P("row", "col", None), P(), P(), P(), P())
    return jax.shard_map(
        shards, mesh=mesh, in_specs=placed, out_specs=P("row", "col", None), check_vma=False
    )
```

time: 301 us -> 219 us (0.73)
  waiting for transfers between devices: 213 us -> 85.3 us
  starting transfers between devices: 0.27 us -> 61.7 us
  Pallas kernels: 0 us -> 22.7 us
  local copies, waits for them, and re-layouts: 41.6 us -> 22.8 us
  between operations: 13.3 us -> 0.76 us
  matrix products: 17.7 us -> 8.22 us
    all_gather x2 -> x0, waiting for transfers between devices: 136 us -> none  [the longest x1 81.5 us: shards(): right_panel = lax.all_gather(right_act, 'row', axis=0, tiled=True)]
    ppermute x0 -> x52, waiting for transfers between devices: none -> 85.3 us  [the longest x6 37.2 us: shards(): down = lax.ppermute(down, 'row', [(r, r - 1) for r in range(1, n - h + 1)])]
    unnamed x4 -> x0, waiting for transfers between devices: 77 us -> none
    ppermute x0 -> x52, starting transfers between devices: none -> 61.7 us  [the longest x6 20.7 us: shards(): up = lax.ppermute(up_sum, 'row', [(r, r + 1) for r in range(step)])]
    unnamed x23 -> x40, local copies, waits for them, and re-layouts: 37.5 us -> 8.74 us
    pallas_call x0 -> x4, Pallas kernels: none -> 22.7 us  [the longest x2 12 us: partial_products(): pl.pallas_call(functools.partial(partial_kernel, subs, slots, n), out_sha...]
    dot_general x5 -> x3, matrix products: 17.7 us -> 8.22 us  [the longest x1 4.72 us: shards(): jnp.einsum('kca,cd->kda', normed, proj_weight, preferred_element_type=jnp...]
    dot_general x0 -> x1, local copies, waits for them, and re-layouts: none -> 8.74 us  [shards(): jnp.einsum('kca,cd->kda', normed, proj_weight, preferred_element_type=jnp...]
  transfers between devices with their start and end apart: 3 -> 52, of which waited for: 3 -> 18; matrix products, arithmetic and copies ran while one was open for 1% -> 12% of each run, Pallas kernels for 0% -> 5%
where the time goes in v1:
time: 219 us; the launch traced here: 218 us
  waiting for transfers between devices  85.3 us (39%)
  starting transfers between devices  61.7 us (28%)
  local copies, waits for them, and re-layouts  22.8 us (10%)
  Pallas kernels  22.7 us (10%)
  other arithmetic  16.1 us (7%)
  matrix products  8.22 us (4%)
    ppermute x6, waiting for transfers between devices, shards(): down = lax.ppermute(down, 'row', [(r, r - 1) for r in range(1, n - h + 1)])  37.2 us
    ppermute x6, waiting for transfers between devices, shards(): up = lax.ppermute(up_sum, 'row', [(r, r + 1) for r in range(step)])  33.7 us
    ppermute x6, starting transfers between devices, shards(): up = lax.ppermute(up_sum, 'row', [(r, r + 1) for r in range(step)])  20.7 us
    ppermute x28, starting transfers between devices, exchange(): return lax.ppermute(value, axis, [(d, d ^ mask) for d in range(size)])  17.8 us
    pallas_call x2, Pallas kernels, partial_products(): pl.pallas_call(functools.partial(partial_kernel, subs, slots, n), out_sha...  12 us
    pallas_call x2, Pallas kernels, left_products(): pl.pallas_call(functools.partial(left_kernel, subs, slots, n), out_shape=...  10.6 us
    ppermute x6, starting transfers between devices, shards(): up = lax.ppermute(up, 'row', [(r, r + 1) for r in range(h - 1, n - 1)])  9.76 us
    unnamed x40, local copies, waits for them, and re-layouts  8.74 us
  transfers between devices with their start and end apart: 52, of which 18 were waited for; matrix products, arithmetic and copies ran while one was open for 12% of the time, Pallas kernels for 5%

profile of v1, /device:TPU:0, one launch (start us, length us, event | category | flops | bytes accessed | tf_op | source)
XLA Modules:
  0.0 217.6 jit_solution(5126600671251347518)
XLA Ops:
  0.0 1.9 copy.19
  2.0 3.0 %collective-permute-start.7 = (bf16[16,64,128]{2,1,0:T(8,128)(2,1)S(1)}, bf16[16,64,128]{2,1,0:T(8,128)(2,1)S(1)}, u32[]{:S(2)}, u32[]{:S(2)}) collective-permute-start(bf16[16,64,128]{2,1,0:T(8,128)(2,1)S(1)} %get-tuple-element.33.refs_6_.refs_0_), channel_id=1, source_target_pairs={{0,2},{1,3},{2,0},{3,1},{4,6},{5,7},{6,4},{7,5},{8,10},{9,11},{10,... | collective-permute-start | bytes 786440 | tf_op jit(solution)/shard_map/ppermute | solution.py:17
  5.0 1.5 collective-permute-start.9
  7.1 4.2 %copy.7 = bf16[128,64,128]{0,2,1:T(8,128)(2,1)} copy(bf16[128,64,128]{2,1,0:T(8,128)(2,1)} %param.6) | data formatting | bytes 4194304 | tf_op args[0]
  11.3 2.2 %fusion.1 = f32[64,128]{1,0:T(8,128)S(1)} fusion(bf16[128,64,128]{0,2,1:T(8,128)(2,1)} %copy.7), kind=kLoop, calls=%fused_computation.3 | loop fusion | flops 2088960 | bytes 2129920 | tf_op jit(solution)/shard_map/reduce_sum | solution.py:174
  14.5 4.7 %fusion.17 = f32[64,128,256]{2,1,0:T(8,128)} fusion(bf16[128,64,128]{0,2,1:T(8,128)(2,1)S(1)} %copy-done.1, f32[128]{0:T(128)S(1)} %copy-done.15, f32[128]{0:T(128)S(1)} %copy-done.14, f32[64,128]{1,0:T(8,128)S(1)} %get-tuple-element.41, f32[64,128]{1,0:T(8,128)S(1)} %get-tuple-element.43, bf16[128,256]{1,0:T(8,128)(2,1)S(1)} %copy-done), kind=kOutput, calls=%fused_computation.22 | convolution fusion | flops 543162368 | bytes 10617856 | tf_op jit(solution)/shard_map/kca,cd->kda/dot_general | solution.py:178
  19.2 8.7 %copy.9 = f32[64,128,256]{1,0,2:T(8,128)} copy(f32[64,128,256]{2,1,0:T(8,128)} %fusion.17) | data formatting | bytes 16777216 | tf_op jit(solution)/shard_map/kca,cd->kda/dot_general | solution.py:178
  28.3 2.8 %fusion.38 = bf16[64,64,128]{2,1,0:T(8,128)(2,1)S(1)} fusion(f32[64,256,128]{2,0,1:T(8,128)} %bitcast.67, f32[64,128]{1,0:T(8,128)S(1)} %fusion.31), kind=kLoop, calls=%fused_computation.55 | loop fusion | flops 3145728 | bytes 5275648 | tf_op jit(solution)/shard_map/transpose | solution.py:192
  31.7 1.9 collective-permute-start.27
  33.7 1.6 collective-permute-start.36
  35.8 3.5 %collective-permute-start = (bf16[32,64,128]{2,1,0:T(8,128)(2,1)S(1)}, bf16[32,64,128]{2,1,0:T(8,128)(2,1)S(1)}, u32[]{:S(2)}, u32[]{:S(2)}) collective-permute-start(bf16[32,64,128]{2,1,0:T(8,128)(2,1)S(1)} %get-tuple-element.28.own), channel_id=1, source_target_pairs={{0,8},{8,16},{16,24},{1,9},{9,17},{17,25},{2,10},{10,18},{18,26},{... | collective-permute-start | bytes 1572872 | tf_op jit(solution)/shard_map/ppermute | solution.py:201
  39.3 1.3 collective-permute-start.3
  40.7 1.3 collective-permute-start.34
  43.0 4.4 %collective-permute-done.29.refs_10_.refs_4_ = bf16[16,64,128]{2,1,0:T(8,128)(2,1)S(1)} collective-permute-done((bf16[16,64,128]{2,1,0:T(8,128)(2,1)S(1)}, bf16[16,64,128]{2,1,0:T(8,128)(2,1)S(1)}, u32[]{:S(2)}, u32[]{:S(2)}) %collective-permute-start.29) | collective-permute-done | bytes 262176 | tf_op jit(solution)/shard_map/ppermute | solution.py:17
  47.9 1.5 collective-permute-start.11
  49.4 1.5 collective-permute-start.18
  50.9 3.5 %collective-permute-start.20 = (bf16[32,64,128]{2,1,0:T(8,128)(2,1)S(1)}, bf16[32,64,128]{2,1,0:T(8,128)(2,1)S(1)}, u32[]{:S(2)}, u32[]{:S(2)}) collective-permute-start(bf16[32,64,128]{2,1,0:T(8,128)(2,1)S(1)} %get-tuple-element.29.own), channel_id=1, source_target_pairs={{0,8},{8,16},{16,24},{1,9},{9,17},{17,25},{2,10},{10,18},{18,26},{... | collective-permute-start | bytes 1572872 | tf_op jit(solution)/shard_map/ppermute | solution.py:201
  54.5 1.3 collective-permute-start.23
  57.9 1.3 collective-permute-start.31
  59.8 6.5 %collective-permute-done.20.refs_0_ = bf16[32,64,128]{2,1,0:T(8,128)(2,1)S(1)} collective-permute-done((bf16[32,64,128]{2,1,0:T(8,128)(2,1)S(1)}, bf16[32,64,128]{2,1,0:T(8,128)(2,1)S(1)}, u32[]{:S(2)}, u32[]{:S(2)}) %collective-permute-start.20) | collective-permute-done | bytes 524320 | tf_op jit(solution)/shard_map/ppermute | solution.py:201
  66.9 3.5 %collective-permute-done.23.refs_3_ = bf16[32,64,128]{2,1,0:T(8,128)(2,1)S(1)} collective-permute-done((bf16[32,64,128]{2,1,0:T(8,128)(2,1)S(1)}, bf16[32,64,128]{2,1,0:T(8,128)(2,1)S(1)}, u32[]{:S(2)}, u32[]{:S(2)}) %collective-permute-start.23) | collective-permute-done | bytes 524320 | tf_op jit(solution)/shard_map/ppermute | solution.py:202
  73.3 1.3 collective-permute-start.24
  75.5 11.6 %collective-permute-done.4.refs_4_ = bf16[32,64,128]{2,1,0:T(8,128)(2,1)S(1)} collective-permute-done((bf16[32,64,128]{2,1,0:T(8,128)(2,1)S(1)}, bf16[32,64,128]{2,1,0:T(8,128)(2,1)S(1)}, u32[]{:S(2)}, u32[]{:S(2)}) %collective-permute-start.4) | collective-permute-done | bytes 524320 | tf_op jit(solution)/shard_map/ppermute | solution.py:202
  89.2 9.1 %collective-permute-done.24.refs_4_ = bf16[32,64,128]{2,1,0:T(8,128)(2,1)S(1)} collective-permute-done((bf16[32,64,128]{2,1,0:T(8,128)(2,1)S(1)}, bf16[32,64,128]{2,1,0:T(8,128)(2,1)S(1)}, u32[]{:S(2)}, u32[]{:S(2)}) %collective-permute-start.24) | collective-permute-done | bytes 524320 | tf_op jit(solution)/shard_map/ppermute | solution.py:202
  100.3 9.4 %collective-permute-done.5.refs_5_ = bf16[32,64,128]{2,1,0:T(8,128)(2,1)S(1)} collective-permute-done((bf16[32,64,128]{2,1,0:T(8,128)(2,1)S(1)}, bf16[32,64,128]{2,1,0:T(8,128)(2,1)S(1)}, u32[]{:S(2)}, u32[]{:S(2)}) %collective-permute-start.5) | collective-permute-done | bytes 524320 | tf_op jit(solution)/shard_map/ppermute | solution.py:202
  110.4 5.3 %left_products.2 = f32[32,64,128]{2,1,0:T(8,128)} custom-call(s32[2]{0:T(128)S(1)} %pad_add_fusion.ids, bf16[32,64,128]{2,1,0:T(8,128)(2,1)S(1)} %get-tuple-element.28.own, bf16[32,64,128]{2,1,0:T(8,128)(2,1)S(1)} %collective-permute-done.refs_0_, bf16[32,64,128]{2,1,0:T(8,128)(2,1)S(1)} %collective-permute-done.1.refs_1_, bf16[32,64,128]{2,1,0:T(8,128)(2,1)} %copy-done.11, ...), custom_call_target="tpu_custom_call" | custom-call | flops 268435456 | bytes 7340032 | tf_op jit(solution)/shard_map/left_products/pallas_call | solution.py:133
  115.8 3.6 %collective-permute-done.25.refs_5_ = bf16[32,64,128]{2,1,0:T(8,128)(2,1)S(1)} collective-permute-done((bf16[32,64,128]{2,1,0:T(8,128)(2,1)S(1)}, bf16[32,64,128]{2,1,0:T(8,128)(2,1)S(1)}, u32[]{:S(2)}, u32[]{:S(2)}) %collective-permute-start.25) | collective-permute-done | bytes 524320 | tf_op jit(solution)/shard_map/ppermute | solution.py:202
  120.2 5.4 %left_products.3 = f32[32,64,128]{2,1,0:T(8,128)} custom-call(s32[2]{0:T(128)S(1)} %pad_add_fusion.ids, bf16[32,64,128]{2,1,0:T(8,128)(2,1)S(1)} %get-tuple-element.29.own, bf16[32,64,128]{2,1,0:T(8,128)(2,1)S(1)} %collective-permute-done.20.refs_0_, bf16[32,64,128]{2,1,0:T(8,128)(2,1)S(1)} %collective-permute-done.21.refs_1_, ...), custom_call_target="tpu_custom_call" | custom-call | flops 268435456 | bytes 7340032 | tf_op jit(solution)/shard_map/left_products/pallas_call | solution.py:133
  125.6 3.7 %multiply_convert_fusion.4 = (bf16[64,64,128]{2,0,1:T(8,128)(2,1)S(1)}, bf16[64,64,128]{2,0,1:T(8,128)(2,1)S(1)}, bf16[64,64,128]{2,1,0:T(8,128)(2,1)S(1)}) fusion(f32[32,64,128]{2,1,0:T(8,128)} %left_products.3, f32[32,64,128]{2,1,0:T(8,128)S(1)} %copy-done.3, f32[64,128]{1,0:T(8,128)S(1)} %fusion.31, f32[64,256,128]{2,0,1:T(8,128)} %bitcast.68), kind=kLoop, calls=%fused_computation.39 | loop fusion | flops 7864320 | bytes 9502720 | tf_op jit(solution)/shard_map/convert.1
  130.4 6.0 %right_partials.2 = (bf16[32,64,128]{2,1,0:T(8,128)(2,1)S(1)}, bf16[32,64,128]{2,1,0:T(8,128)(2,1)S(1)}, bf16[32,64,128]{2,1,0:T(8,128)(2,1)S(1)}, bf16[32,64,128]{2,1,0:T(8,128)(2,1)}) custom-call(s32[2]{0:T(128)S(1)} %pad_add_fusion.ids, bf16[32,64,128]{2,1,0:T(8,128)(2,1)} %get-tuple-element.34.left, ...), custom_call_target="tpu_custom_call" | custom-call | flops 268435456 | bytes 6815744 | tf_op jit(solution)/shard_map/right_partials/pallas_call | solution.py:72
  136.4 1.4 collective-permute-start.40
  138.5 6.0 %right_partials.3 = (bf16[32,64,128]{2,1,0:T(8,128)(2,1)S(1)}, bf16[32,64,128]{2,1,0:T(8,128)(2,1)S(1)}, bf16[32,64,128]{2,1,0:T(8,128)(2,1)S(1)}, bf16[32,64,128]{2,1,0:T(8,128)(2,1)}) custom-call(s32[2]{0:T(128)S(1)} %pad_add_fusion.ids, bf16[32,64,128]{2,1,0:T(8,128)(2,1)} %get-tuple-element.35.left, ...), custom_call_target="tpu_custom_call" | custom-call | flops 268435456 | bytes 6815744 | tf_op jit(solution)/shard_map/right_partials/pallas_call | solution.py:72
  144.6 1.3 collective-permute-start.46
  146.6 3.9 %collective-permute-done.40 = bf16[32,64,128]{2,1,0:T(8,128)(2,1)S(1)} collective-permute-done((bf16[32,64,128]{2,1,0:T(8,128)(2,1)}, bf16[32,64,128]{2,1,0:T(8,128)(2,1)S(1)}, u32[]{:S(2)}, u32[]{:S(2)}) %collective-permute-start.40) | collective-permute-done | bytes 524320 | tf_op jit(solution)/shard_map/ppermute | solution.py:213
  150.8 4.6 %collective-permute-start.41 = (bf16[32,64,128]{2,1,0:T(8,128)(2,1)S(1)}, bf16[32,64,128]{2,1,0:T(8,128)(2,1)S(1)}, u32[]{:S(2)}, u32[]{:S(2)}) collective-permute-start(bf16[32,64,128]{2,1,0:T(8,128)(2,1)S(1)} %get-tuple-element.36), channel_id=1, source_target_pairs={{0,8},{8,16},{1,9},{9,17},{2,10},{10,18},{3,11},{11,19},{4,12},{12... | collective-permute-start | bytes 1572872 | tf_op jit(solution)/shard_map/ppermute | solution.py:213
  156.0 5.7 %collective-permute-done.46 = bf16[32,64,128]{2,1,0:T(8,128)(2,1)S(1)} collective-permute-done((bf16[32,64,128]{2,1,0:T(8,128)(2,1)}, bf16[32,64,128]{2,1,0:T(8,128)(2,1)S(1)}, u32[]{:S(2)}, u32[]{:S(2)}) %collective-permute-start.46) | collective-permute-done | bytes 524320 | tf_op jit(solution)/shard_map/ppermute | solution.py:213
  162.0 4.3 %collective-permute-start.47 = (bf16[32,64,128]{2,1,0:T(8,128)(2,1)S(1)}, bf16[32,64,128]{2,1,0:T(8,128)(2,1)S(1)}, u32[]{:S(2)}, u32[]{:S(2)}) collective-permute-start(bf16[32,64,128]{2,1,0:T(8,128)(2,1)S(1)} %get-tuple-element.38), channel_id=1, source_target_pairs={{0,8},{8,16},{1,9},{9,17},{2,10},{10,18},{3,11},{11,19},{4,12},{12... | collective-permute-start | bytes 1572872 | tf_op jit(solution)/shard_map/ppermute | solution.py:213
  167.2 5.6 %collective-permute-done.41 = bf16[32,64,128]{2,1,0:T(8,128)(2,1)S(1)} collective-permute-done((bf16[32,64,128]{2,1,0:T(8,128)(2,1)S(1)}, bf16[32,64,128]{2,1,0:T(8,128)(2,1)S(1)}, u32[]{:S(2)}, u32[]{:S(2)}) %collective-permute-start.41) | collective-permute-done | bytes 524320 | tf_op jit(solution)/shard_map/ppermute | solution.py:213
  173.0 4.7 %collective-permute-start.42 = (bf16[32,64,128]{2,1,0:T(8,128)(2,1)S(1)}, bf16[32,64,128]{2,1,0:T(8,128)(2,1)S(1)}, u32[]{:S(2)}, u32[]{:S(2)}) collective-permute-start(bf16[32,64,128]{2,1,0:T(8,128)(2,1)S(1)} %add_convert_fusion.3), channel_id=1, source_target_pairs={{0,8},{8,16},{16,24},{1,9},{9,17},{17,25},{2,10},{10,18},{18,26},{... | collective-permute-start | bytes 1572872 | tf_op jit(solution)/shard_map/ppermute | solution.py:213
  177.9 1.3 collective-permute-start.45
  179.2 4.8 %collective-permute-done.47 = bf16[32,64,128]{2,1,0:T(8,128)(2,1)S(1)} collective-permute-done((bf16[32,64,128]{2,1,0:T(8,128)(2,1)S(1)}, bf16[32,64,128]{2,1,0:T(8,128)(2,1)S(1)}, u32[]{:S(2)}, u32[]{:S(2)}) %collective-permute-start.47) | collective-permute-done | bytes 524320 | tf_op jit(solution)/shard_map/ppermute | solution.py:213
  184.3 4.4 %collective-permute-start.48 = (bf16[32,64,128]{2,1,0:T(8,128)(2,1)S(1)}, bf16[32,64,128]{2,1,0:T(8,128)(2,1)S(1)}, u32[]{:S(2)}, u32[]{:S(2)}) collective-permute-start(bf16[32,64,128]{2,1,0:T(8,128)(2,1)S(1)} %add_convert_fusion.1), channel_id=1, source_target_pairs={{0,8},{8,16},{16,24},{1,9},{9,17},{17,25},{2,10},{10,18},{18,26},{... | collective-permute-start | bytes 1572872 | tf_op jit(solution)/shard_map/ppermute | solution.py:213
  188.9 1.5 collective-permute-start.51
  190.4 4.9 %collective-permute-done.42 = bf16[32,64,128]{2,1,0:T(8,128)(2,1)S(1)} collective-permute-done((bf16[32,64,128]{2,1,0:T(8,128)(2,1)S(1)}, bf16[32,64,128]{2,1,0:T(8,128)(2,1)S(1)}, u32[]{:S(2)}, u32[]{:S(2)}) %collective-permute-start.42) | collective-permute-done | bytes 524320 | tf_op jit(solution)/shard_map/ppermute | solution.py:213
  195.6 8.8 %collective-permute-done.48 = bf16[32,64,128]{2,1,0:T(8,128)(2,1)S(1)} collective-permute-done((bf16[32,64,128]{2,1,0:T(8,128)(2,1)S(1)}, bf16[32,64,128]{2,1,0:T(8,128)(2,1)S(1)}, u32[]{:S(2)}, u32[]{:S(2)}) %collective-permute-start.48) | collective-permute-done | bytes 524320 | tf_op jit(solution)/shard_map/ppermute | solution.py:213
  207.5 3.2 %bitcast_reduce_fusion = (f32[64,128]{1,0:T(8,128)S(1)}, f32[64,128]{1,0:T(8,128)S(1)}, f32[64,128,128]{1,2,0:T(8,128)S(1)}) fusion(f32[128]{0:T(128)S(1)} %copy-done.14, f32[64,128]{1,0:T(8,128)S(1)} %get-tuple-element.41, f32[64,128]{1,0:T(8,128)S(1)} %get-tuple-element.43, bf16[128,64,128]{0,2,1:T(8,128)(2,1)S(1)} %copy-done.2, ...), kind=kOutput, calls=%fused_computation.18 | convolution fusion | flops 544194560 | bytes 10682880 | tf_op jit(solution)/shard_map/kda,cd->kca/dot_general | solution.py:232
  210.7 2.8 %fusion.14 = bf16[128,64,128]{0,2,1:T(8,128)(2,1)} fusion(bf16[128,64,128]{0,2,1:T(8,128)(2,1)S(1)} %copy-done.2, f32[64,128,128]{1,2,0:T(8,128)S(1)} %get-tuple-element.44, f32[128,64]{0,1:T(8,128)S(1)} %get-tuple-element.45, f32[128,64]{0,1:T(8,128)S(1)} %get-tuple-element.42, f32[128,64]{0,1:T(8,128)S(1)} %get-tuple-element.46, f32[128]{0:T(128)S(1)} %copy-done.14, ...), kind=kLoop, calls=%fused_computation.16 | loop fusion | flops 9437184 | bytes 8520192 | tf_op jit(solution)/shard_map/convert_element_type | solution.py:239
  213.5 4.1 %copy.12 = bf16[128,64,128]{2,1,0:T(8,128)(2,1)} copy(bf16[128,64,128]{0,2,1:T(8,128)(2,1)} %fusion.14) | data formatting | bytes 4194304 | tf_op jit(solution)/shard_map/convert_element_type | solution.py:239
  (130 shorter events, 25.9 us)
Async XLA Ops:
  2.0 29.1 %collective-permute-start.7 = (bf16[16,64,128]{2,1,0:T(8,128)(2,1)S(1)}, bf16[16,64,128]{2,1,0:T(8,128)(2,1)S(1)}, u32[]{:S(2)}, u32[]{:S(2)}) collective-permute-start(bf16[16,64,128]{2,1,0:T(8,128)(2,1)S(1)} %get-tuple-element.33.refs_6_.refs_0_), channel_id=1, source_target_pairs={{0,2},{1,3},{2,0},{3,1},{4,6},{5,7},{6,4},{7,5},{8,10},{9,11},{10,... | collective-permute-start | bytes 786440 | tf_op jit(solution)/shard_map/ppermute | solution.py:17
  5.0 28.7 %collective-permute-start.9 = (bf16[16,64,128]{2,1,0:T(8,128)(2,1)S(1)}, bf16[16,64,128]{2,1,0:T(8,128)(2,1)S(1)}, u32[]{:S(2)}, u32[]{:S(2)}) collective-permute-start(bf16[16,64,128]{2,1,0:T(8,128)(2,1)S(1)} %get-tuple-element.33.refs_6_.refs_0_), channel_id=1, source_target_pairs={{0,4},{1,5},{2,6},{3,7},{4,0},{5,1},{6,2},{7,3},{8,12},{9,13},{10,... | collective-permute-start | bytes 786440 | tf_op jit(solution)/shard_map/ppermute | solution.py:17
  6.5 25.2 %collective-permute-start.16 = (bf16[16,64,128]{2,1,0:T(8,128)(2,1)S(1)}, bf16[16,64,128]{2,1,0:T(8,128)(2,1)S(1)}, u32[]{:S(2)}, u32[]{:S(2)}) collective-permute-start(bf16[16,64,128]{2,1,0:T(8,128)(2,1)S(1)} %get-tuple-element.30.refs_14_.refs_8_), channel_id=1, source_target_pairs={{0,4},{1,5},{2,6},{3,7},{4,0},{5,1},{6,2},{7,3},{8,12},{9,13},{10,... | collective-permute-start | bytes 786440 | tf_op jit(solution)/shard_map/ppermute | solution.py:17
  7.1 28.3 %collective-permute-start.14 = (bf16[16,64,128]{2,1,0:T(8,128)(2,1)S(1)}, bf16[16,64,128]{2,1,0:T(8,128)(2,1)S(1)}, u32[]{:S(2)}, u32[]{:S(2)}) collective-permute-start(bf16[16,64,128]{2,1,0:T(8,128)(2,1)S(1)} %get-tuple-element.30.refs_14_.refs_8_), channel_id=1, source_target_pairs={{0,2},{1,3},{2,0},{3,1},{4,6},{5,7},{6,4},{7,5},{8,10},{9,11},{10,... | collective-permute-start | bytes 786440 | tf_op jit(solution)/shard_map/ppermute | solution.py:17
  7.1 28.7 %collective-permute-start.13 = (bf16[16,64,128]{2,1,0:T(8,128)(2,1)S(1)}, bf16[16,64,128]{2,1,0:T(8,128)(2,1)S(1)}, u32[]{:S(2)}, u32[]{:S(2)}) collective-permute-start(bf16[16,64,128]{2,1,0:T(8,128)(2,1)S(1)} %get-tuple-element.30.refs_14_.refs_8_), channel_id=1, source_target_pairs={{0,1},{1,0},{2,3},{3,2},{4,5},{5,4},{6,7},{7,6},{8,9},{9,8},{10,11... | collective-permute-start | bytes 786440 | tf_op jit(solution)/shard_map/ppermute | solution.py:17
  31.1 8.2 %collective-permute-start.6 = (bf16[16,64,128]{2,1,0:T(8,128)(2,1)S(1)}, bf16[16,64,128]{2,1,0:T(8,128)(2,1)S(1)}, u32[]{:S(2)}, u32[]{:S(2)}) collective-permute-start(bf16[16,64,128]{2,1,0:T(8,128)(2,1)S(1)} %get-tuple-element.33.refs_6_.refs_0_), channel_id=1, source_target_pairs={{0,1},{1,0},{2,3},{3,2},{4,5},{5,4},{6,7},{7,6},{8,9},{9,8},{10,11... | collective-permute-start | bytes 786440 | tf_op jit(solution)/shard_map/ppermute | solution.py:17
  31.7 9.0 %collective-permute-start.27 = (bf16[16,64,128]{2,1,0:T(8,128)(2,1)S(1)}, bf16[16,64,128]{2,1,0:T(8,128)(2,1)S(1)}, u32[]{:S(2)}, u32[]{:S(2)}) collective-permute-start(bf16[16,64,128]{2,1,0:T(8,128)(2,1)S(1)} %get-tuple-element.32.refs_6_.refs_0_), channel_id=1, source_target_pairs={{0,2},{1,3},{2,0},{3,1},{4,6},{5,7},{6,4},{7,5},{8,10},{9,11},{10,... | collective-permute-start | bytes 786440 | tf_op jit(solution)/shard_map/ppermute | solution.py:17
  33.7 9.3 %collective-permute-start.36 = (bf16[16,64,128]{2,1,0:T(8,128)(2,1)S(1)}, bf16[16,64,128]{2,1,0:T(8,128)(2,1)S(1)}, u32[]{:S(2)}, u32[]{:S(2)}) collective-permute-start(bf16[16,64,128]{2,1,0:T(8,128)(2,1)S(1)} %get-tuple-element.31.refs_14_.refs_8_), channel_id=1, source_target_pairs={{0,4},{1,5},{2,6},{3,7},{4,0},{5,1},{6,2},{7,3},{8,12},{9,13},{10,... | collective-permute-start | bytes 786440 | tf_op jit(solution)/shard_map/ppermute | solution.py:17
  35.3 12.1 %collective-permute-start.29 = (bf16[16,64,128]{2,1,0:T(8,128)(2,1)S(1)}, bf16[16,64,128]{2,1,0:T(8,128)(2,1)S(1)}, u32[]{:S(2)}, u32[]{:S(2)}) collective-permute-start(bf16[16,64,128]{2,1,0:T(8,128)(2,1)S(1)} %get-tuple-element.32.refs_6_.refs_0_), channel_id=1, source_target_pairs={{0,4},{1,5},{2,6},{3,7},{4,0},{5,1},{6,2},{7,3},{8,12},{9,13},{10,... | collective-permute-start | bytes 786440 | tf_op jit(solution)/shard_map/ppermute | solution.py:17
  35.8 15.1 %collective-permute-start = (bf16[32,64,128]{2,1,0:T(8,128)(2,1)S(1)}, bf16[32,64,128]{2,1,0:T(8,128)(2,1)S(1)}, u32[]{:S(2)}, u32[]{:S(2)}) collective-permute-start(bf16[32,64,128]{2,1,0:T(8,128)(2,1)S(1)} %get-tuple-element.28.own), channel_id=1, source_target_pairs={{0,8},{8,16},{16,24},{1,9},{9,17},{17,25},{2,10},{10,18},{18,26},{... | collective-permute-start | bytes 1572872 | tf_op jit(solution)/shard_map/ppermute | solution.py:201
  39.3 15.1 %collective-permute-start.3 = (bf16[32,64,128]{2,1,0:T(8,128)(2,1)S(1)}, bf16[32,64,128]{2,1,0:T(8,128)(2,1)S(1)}, u32[]{:S(2)}, u32[]{:S(2)}) collective-permute-start(bf16[32,64,128]{2,1,0:T(8,128)(2,1)S(1)} %get-tuple-element.28.own), channel_id=1, source_target_pairs={{8,0},{16,8},{24,16},{9,1},{17,9},{25,17},{10,2},{18,10},{26,18},{... | collective-permute-start | bytes 1572872 | tf_op jit(solution)/shard_map/ppermute | solution.py:202
  40.7 7.2 %collective-permute-start.34 = (bf16[16,64,128]{2,1,0:T(8,128)(2,1)S(1)}, bf16[16,64,128]{2,1,0:T(8,128)(2,1)S(1)}, u32[]{:S(2)}, u32[]{:S(2)}) collective-permute-start(bf16[16,64,128]{2,1,0:T(8,128)(2,1)S(1)} %get-tuple-element.31.refs_14_.refs_8_), channel_id=1, source_target_pairs={{0,2},{1,3},{2,0},{3,1},{4,6},{5,7},{6,4},{7,5},{8,10},{9,11},{10,... | collective-permute-start | bytes 786440 | tf_op jit(solution)/shard_map/ppermute | solution.py:17
  43.0 6.4 %collective-permute-start.26 = (bf16[16,64,128]{2,1,0:T(8,128)(2,1)S(1)}, bf16[16,64,128]{2,1,0:T(8,128)(2,1)S(1)}, u32[]{:S(2)}, u32[]{:S(2)}) collective-permute-start(bf16[16,64,128]{2,1,0:T(8,128)(2,1)S(1)} %get-tuple-element.32.refs_6_.refs_0_), channel_id=1, source_target_pairs={{0,1},{1,0},{2,3},{3,2},{4,5},{5,4},{6,7},{7,6},{8,9},{9,8},{10,11... | collective-permute-start | bytes 786440 | tf_op jit(solution)/shard_map/ppermute | solution.py:17
  47.4 3.5 %collective-permute-start.33 = (bf16[16,64,128]{2,1,0:T(8,128)(2,1)S(1)}, bf16[16,64,128]{2,1,0:T(8,128)(2,1)S(1)}, u32[]{:S(2)}, u32[]{:S(2)}) collective-permute-start(bf16[16,64,128]{2,1,0:T(8,128)(2,1)S(1)} %get-tuple-element.31.refs_14_.refs_8_), channel_id=1, source_target_pairs={{0,1},{1,0},{2,3},{3,2},{4,5},{5,4},{6,7},{7,6},{8,9},{9,8},{10,11... | collective-permute-start | bytes 786440 | tf_op jit(solution)/shard_map/ppermute | solution.py:17
  47.9 8.3 %collective-permute-start.11 = (bf16[16,64,128]{2,1,0:T(8,128)(2,1)S(1)}, bf16[16,64,128]{2,1,0:T(8,128)(2,1)S(1)}, u32[]{:S(2)}, u32[]{:S(2)}) collective-permute-start(bf16[16,64,128]{2,1,0:T(8,128)(2,1)S(1)} %collective-permute-done.7.refs_8_.refs_2_), channel_id=1, source_target_pairs={{0,4},{1,5},{2,6},{3,7},{4,0},{5,1},{6,2},{7,3},{8,12},{9,13},{10,... | collective-permute-start | bytes 786440 | tf_op jit(solution)/shard_map/ppermute | solution.py:17
  49.4 8.0 %collective-permute-start.18 = (bf16[16,64,128]{2,1,0:T(8,128)(2,1)S(1)}, bf16[16,64,128]{2,1,0:T(8,128)(2,1)S(1)}, u32[]{:S(2)}, u32[]{:S(2)}) collective-permute-start(bf16[16,64,128]{2,1,0:T(8,128)(2,1)S(1)} %collective-permute-done.16.refs_18_.refs_12_), channel_id=1, source_target_pairs={{0,2},{1,3},{2,0},{3,1},{4,6},{5,7},{6,4},{7,5},{8,10},{9,11},{10,... | collective-permute-start | bytes 786440 | tf_op jit(solution)/shard_map/ppermute | solution.py:17
  50.9 6.5 %collective-permute-start.17 = (bf16[16,64,128]{2,1,0:T(8,128)(2,1)S(1)}, bf16[16,64,128]{2,1,0:T(8,128)(2,1)S(1)}, u32[]{:S(2)}, u32[]{:S(2)}) collective-permute-start(bf16[16,64,128]{2,1,0:T(8,128)(2,1)S(1)} %collective-permute-done.16.refs_18_.refs_12_), channel_id=1, source_target_pairs={{0,1},{1,0},{2,3},{3,2},{4,5},{5,4},{6,7},{7,6},{8,9},{9,8},{10,11... | collective-permute-start | bytes 786440 | tf_op jit(solution)/shard_map/ppermute | solution.py:17
  50.9 15.3 %collective-permute-start.20 = (bf16[32,64,128]{2,1,0:T(8,128)(2,1)S(1)}, bf16[32,64,128]{2,1,0:T(8,128)(2,1)S(1)}, u32[]{:S(2)}, u32[]{:S(2)}) collective-permute-start(bf16[32,64,128]{2,1,0:T(8,128)(2,1)S(1)} %get-tuple-element.29.own), channel_id=1, source_target_pairs={{0,8},{8,16},{16,24},{1,9},{9,17},{17,25},{2,10},{10,18},{18,26},{... | collective-permute-start | bytes 1572872 | tf_op jit(solution)/shard_map/ppermute | solution.py:201
  54.5 15.9 %collective-permute-start.23 = (bf16[32,64,128]{2,1,0:T(8,128)(2,1)S(1)}, bf16[32,64,128]{2,1,0:T(8,128)(2,1)S(1)}, u32[]{:S(2)}, u32[]{:S(2)}) collective-permute-start(bf16[32,64,128]{2,1,0:T(8,128)(2,1)S(1)} %get-tuple-element.29.own), channel_id=1, source_target_pairs={{8,0},{16,8},{24,16},{9,1},{17,9},{25,17},{10,2},{18,10},{26,18},{... | collective-permute-start | bytes 1572872 | tf_op jit(solution)/shard_map/ppermute | solution.py:202
  57.9 13.8 %collective-permute-start.31 = (bf16[16,64,128]{2,1,0:T(8,128)(2,1)S(1)}, bf16[16,64,128]{2,1,0:T(8,128)(2,1)S(1)}, u32[]{:S(2)}, u32[]{:S(2)}) collective-permute-start(bf16[16,64,128]{2,1,0:T(8,128)(2,1)S(1)} %collective-permute-done.27.refs_8_.refs_2_), channel_id=1, source_target_pairs={{0,4},{1,5},{2,6},{3,7},{4,0},{5,1},{6,2},{7,3},{8,12},{9,13},{10,... | collective-permute-start | bytes 786440 | tf_op jit(solution)/shard_map/ppermute | solution.py:17
  59.2 12.6 %collective-permute-start.38 = (bf16[16,64,128]{2,1,0:T(8,128)(2,1)S(1)}, bf16[16,64,128]{2,1,0:T(8,128)(2,1)S(1)}, u32[]{:S(2)}, u32[]{:S(2)}) collective-permute-start(bf16[16,64,128]{2,1,0:T(8,128)(2,1)S(1)} %collective-permute-done.36.refs_18_.refs_12_), channel_id=1, source_target_pairs={{0,2},{1,3},{2,0},{3,1},{4,6},{5,7},{6,4},{7,5},{8,10},{9,11},{10,... | collective-permute-start | bytes 786440 | tf_op jit(solution)/shard_map/ppermute | solution.py:17
  59.8 12.5 %collective-permute-start.28 = (bf16[16,64,128]{2,1,0:T(8,128)(2,1)S(1)}, bf16[16,64,128]{2,1,0:T(8,128)(2,1)S(1)}, u32[]{:S(2)}, u32[]{:S(2)}) collective-permute-start(bf16[16,64,128]{2,1,0:T(8,128)(2,1)S(1)} %collective-permute-done.27.refs_8_.refs_2_), channel_id=1, source_target_pairs={{0,1},{1,0},{2,3},{3,2},{4,5},{5,4},{6,7},{7,6},{8,9},{9,8},{10,11... | collective-permute-start | bytes 786440 | tf_op jit(solution)/shard_map/ppermute | solution.py:17
  66.2 8.6 %collective-permute-start.1 = (bf16[32,64,128]{2,1,0:T(8,128)(2,1)S(1)}, bf16[32,64,128]{2,1,0:T(8,128)(2,1)S(1)}, u32[]{:S(2)}, u32[]{:S(2)}) collective-permute-start(bf16[32,64,128]{2,1,0:T(8,128)(2,1)S(1)} %collective-permute-done.refs_0_), channel_id=1, source_target_pairs={{8,16},{16,24},{9,17},{17,25},{10,18},{18,26},{11,19},{19,27},{12,... | collective-permute-start | bytes 1572872 | tf_op jit(solution)/shard_map/ppermute | solution.py:201
  70.4 16.7 %collective-permute-start.4 = (bf16[32,64,128]{2,1,0:T(8,128)(2,1)S(1)}, bf16[32,64,128]{2,1,0:T(8,128)(2,1)S(1)}, u32[]{:S(2)}, u32[]{:S(2)}) collective-permute-start(bf16[32,64,128]{2,1,0:T(8,128)(2,1)S(1)} %collective-permute-done.3.refs_3_), channel_id=1, source_target_pairs={{8,0},{16,8},{9,1},{17,9},{10,2},{18,10},{11,3},{19,11},{12,4},{20... | collective-permute-start | bytes 1572872 | tf_op jit(solution)/shard_map/ppermute | solution.py:202
  71.8 2.8 %collective-permute-start.30 = (bf16[16,64,128]{2,1,0:T(8,128)(2,1)S(1)}, bf16[16,64,128]{2,1,0:T(8,128)(2,1)S(1)}, u32[]{:S(2)}, u32[]{:S(2)}) collective-permute-start(bf16[16,64,128]{2,1,0:T(8,128)(2,1)S(1)} %collective-permute-done.29.refs_10_.refs_4_), channel_id=1, source_target_pairs={{0,1},{1,0},{2,3},{3,2},{4,5},{5,4},{6,7},{7,6},{8,9},{9,8},{10,11... | collective-permute-start | bytes 786440 | tf_op jit(solution)/shard_map/ppermute | solution.py:17
  72.3 16.2 %collective-permute-start.21 = (bf16[32,64,128]{2,1,0:T(8,128)(2,1)S(1)}, bf16[32,64,128]{2,1,0:T(8,128)(2,1)S(1)}, u32[]{:S(2)}, u32[]{:S(2)}) collective-permute-start(bf16[32,64,128]{2,1,0:T(8,128)(2,1)S(1)} %collective-permute-done.20.refs_0_), channel_id=1, source_target_pairs={{8,16},{16,24},{9,17},{17,25},{10,18},{18,26},{11,19},{19,27},{12,... | collective-permute-start | bytes 1572872 | tf_op jit(solution)/shard_map/ppermute | solution.py:201
  73.3 25.1 %collective-permute-start.24 = (bf16[32,64,128]{2,1,0:T(8,128)(2,1)S(1)}, bf16[32,64,128]{2,1,0:T(8,128)(2,1)S(1)}, u32[]{:S(2)}, u32[]{:S(2)}) collective-permute-start(bf16[32,64,128]{2,1,0:T(8,128)(2,1)S(1)} %collective-permute-done.23.refs_3_), channel_id=1, source_target_pairs={{8,0},{16,8},{9,1},{17,9},{10,2},{18,10},{11,3},{19,11},{12,4},{20... | collective-permute-start | bytes 1572872 | tf_op jit(solution)/shard_map/ppermute | solution.py:202
  74.6 13.8 %collective-permute-start.12 = (bf16[16,64,128]{2,1,0:T(8,128)(2,1)S(1)}, bf16[16,64,128]{2,1,0:T(8,128)(2,1)S(1)}, u32[]{:S(2)}, u32[]{:S(2)}) collective-permute-start(bf16[16,64,128]{2,1,0:T(8,128)(2,1)S(1)} %collective-permute-done.11.refs_12_.refs_6_), channel_id=1, source_target_pairs={{0,1},{1,0},{2,3},{3,2},{4,5},{5,4},{6,7},{7,6},{8,9},{9,8},{10,11... | collective-permute-start | bytes 786440 | tf_op jit(solution)/shard_map/ppermute | solution.py:17
  74.8 24.9 %collective-permute-start.2 = (bf16[32,64,128]{2,1,0:T(8,128)(2,1)S(1)}, bf16[32,64,128]{2,1,0:T(8,128)(2,1)S(1)}, u32[]{:S(2)}, u32[]{:S(2)}) collective-permute-start(bf16[32,64,128]{2,1,0:T(8,128)(2,1)S(1)} %collective-permute-done.1.refs_1_), channel_id=1, source_target_pairs={{16,24},{17,25},{18,26},{19,27},{20,28},{21,29},{22,30},{23,31}} | collective-permute-start | bytes 1572872 | tf_op jit(solution)/shard_map/ppermute | solution.py:201
  87.1 22.5 %collective-permute-start.5 = (bf16[32,64,128]{2,1,0:T(8,128)(2,1)S(1)}, bf16[32,64,128]{2,1,0:T(8,128)(2,1)S(1)}, u32[]{:S(2)}, u32[]{:S(2)}) collective-permute-start(bf16[32,64,128]{2,1,0:T(8,128)(2,1)S(1)} %collective-permute-done.4.refs_4_), channel_id=1, source_target_pairs={{8,0},{9,1},{10,2},{11,3},{12,4},{13,5},{14,6},{15,7}} | collective-permute-start | bytes 1572872 | tf_op jit(solution)/shard_map/ppermute | solution.py:202
  88.4 11.2 %collective-permute-start.19 = (bf16[16,64,128]{2,1,0:T(8,128)(2,1)S(1)}, bf16[16,64,128]{2,1,0:T(8,128)(2,1)S(1)}, u32[]{:S(2)}, u32[]{:S(2)}) collective-permute-start(bf16[16,64,128]{2,1,0:T(8,128)(2,1)S(1)} %collective-permute-done.18.refs_20_.refs_14_), channel_id=1, source_target_pairs={{0,1},{1,0},{2,3},{3,2},{4,5},{5,4},{6,7},{7,6},{8,9},{9,8},{10,11... | collective-permute-start | bytes 786440 | tf_op jit(solution)/shard_map/ppermute | solution.py:17
  88.5 27.3 %collective-permute-start.22 = (bf16[32,64,128]{2,1,0:T(8,128)(2,1)S(1)}, bf16[32,64,128]{2,1,0:T(8,128)(2,1)S(1)}, u32[]{:S(2)}, u32[]{:S(2)}) collective-permute-start(bf16[32,64,128]{2,1,0:T(8,128)(2,1)S(1)} %collective-permute-done.21.refs_1_), channel_id=1, source_target_pairs={{16,24},{17,25},{18,26},{19,27},{20,28},{21,29},{22,30},{23,31}} | collective-permute-start | bytes 1572872 | tf_op jit(solution)/shard_map/ppermute | solution.py:201
  98.4 21.0 %collective-permute-start.25 = (bf16[32,64,128]{2,1,0:T(8,128)(2,1)S(1)}, bf16[32,64,128]{2,1,0:T(8,128)(2,1)S(1)}, u32[]{:S(2)}, u32[]{:S(2)}) collective-permute-start(bf16[32,64,128]{2,1,0:T(8,128)(2,1)S(1)} %collective-permute-done.24.refs_4_), channel_id=1, source_target_pairs={{8,0},{9,1},{10,2},{11,3},{12,4},{13,5},{14,6},{15,7}} | collective-permute-start | bytes 1572872 | tf_op jit(solution)/shard_map/ppermute | solution.py:202
  99.7 16.1 %collective-permute-start.35 = (bf16[16,64,128]{2,1,0:T(8,128)(2,1)S(1)}, bf16[16,64,128]{2,1,0:T(8,128)(2,1)S(1)}, u32[]{:S(2)}, u32[]{:S(2)}) collective-permute-start(bf16[16,64,128]{2,1,0:T(8,128)(2,1)S(1)} %collective-permute-done.34.refs_16_.refs_10_), channel_id=1, source_target_pairs={{0,1},{1,0},{2,3},{3,2},{4,5},{5,4},{6,7},{7,6},{8,9},{9,8},{10,11... | collective-permute-start | bytes 786440 | tf_op jit(solution)/shard_map/ppermute | solution.py:17
  99.8 16.0 %collective-permute-start.32 = (bf16[16,64,128]{2,1,0:T(8,128)(2,1)S(1)}, bf16[16,64,128]{2,1,0:T(8,128)(2,1)S(1)}, u32[]{:S(2)}, u32[]{:S(2)}) collective-permute-start(bf16[16,64,128]{2,1,0:T(8,128)(2,1)S(1)} %collective-permute-done.31.refs_12_.refs_6_), channel_id=1, source_target_pairs={{0,1},{1,0},{2,3},{3,2},{4,5},{5,4},{6,7},{7,6},{8,9},{9,8},{10,11... | collective-permute-start | bytes 786440 | tf_op jit(solution)/shard_map/ppermute | solution.py:17
  109.6 6.2 %collective-permute-start.39 = (bf16[16,64,128]{2,1,0:T(8,128)(2,1)S(1)}, bf16[16,64,128]{2,1,0:T(8,128)(2,1)S(1)}, u32[]{:S(2)}, u32[]{:S(2)}) collective-permute-start(bf16[16,64,128]{2,1,0:T(8,128)(2,1)S(1)} %collective-permute-done.38.refs_20_.refs_14_), channel_id=1, source_target_pairs={{0,1},{1,0},{2,3},{3,2},{4,5},{5,4},{6,7},{7,6},{8,9},{9,8},{10,11... | collective-permute-start | bytes 786440 | tf_op jit(solution)/shard_map/ppermute | solution.py:17
  136.4 14.1 %collective-permute-start.40 = (bf16[32,64,128]{2,1,0:T(8,128)(2,1)}, bf16[32,64,128]{2,1,0:T(8,128)(2,1)S(1)}, u32[]{:S(2)}, u32[]{:S(2)}) collective-permute-start(bf16[32,64,128]{2,1,0:T(8,128)(2,1)} %get-tuple-element.16), channel_id=1, source_target_pairs={{0,8},{1,9},{2,10},{3,11},{4,12},{5,13},{6,14},{7,15}} | collective-permute-start | bytes 1572872 | tf_op jit(solution)/shard_map/ppermute | solution.py:213
  137.8 12.7 %collective-permute-start.43 = (bf16[32,64,128]{2,1,0:T(8,128)(2,1)S(1)}, bf16[32,64,128]{2,1,0:T(8,128)(2,1)S(1)}, u32[]{:S(2)}, u32[]{:S(2)}) collective-permute-start(bf16[32,64,128]{2,1,0:T(8,128)(2,1)S(1)} %get-tuple-element.14), channel_id=1, source_target_pairs={{24,16},{25,17},{26,18},{27,19},{28,20},{29,21},{30,22},{31,23}} | collective-permute-start | bytes 1572872 | tf_op jit(solution)/shard_map/ppermute | solution.py:214
  144.6 17.1 %collective-permute-start.46 = (bf16[32,64,128]{2,1,0:T(8,128)(2,1)}, bf16[32,64,128]{2,1,0:T(8,128)(2,1)S(1)}, u32[]{:S(2)}, u32[]{:S(2)}) collective-permute-start(bf16[32,64,128]{2,1,0:T(8,128)(2,1)} %get-tuple-element.20), channel_id=1, source_target_pairs={{0,8},{1,9},{2,10},{3,11},{4,12},{5,13},{6,14},{7,15}} | collective-permute-start | bytes 1572872 | tf_op jit(solution)/shard_map/ppermute | solution.py:213
  145.9 15.8 %collective-permute-start.49 = (bf16[32,64,128]{2,1,0:T(8,128)(2,1)S(1)}, bf16[32,64,128]{2,1,0:T(8,128)(2,1)S(1)}, u32[]{:S(2)}, u32[]{:S(2)}) collective-permute-start(bf16[32,64,128]{2,1,0:T(8,128)(2,1)S(1)} %get-tuple-element.18), channel_id=1, source_target_pairs={{24,16},{25,17},{26,18},{27,19},{28,20},{29,21},{30,22},{31,23}} | collective-permute-start | bytes 1572872 | tf_op jit(solution)/shard_map/ppermute | solution.py:214
  150.8 22.1 %collective-permute-start.41 = (bf16[32,64,128]{2,1,0:T(8,128)(2,1)S(1)}, bf16[32,64,128]{2,1,0:T(8,128)(2,1)S(1)}, u32[]{:S(2)}, u32[]{:S(2)}) collective-permute-start(bf16[32,64,128]{2,1,0:T(8,128)(2,1)S(1)} %get-tuple-element.36), channel_id=1, source_target_pairs={{0,8},{8,16},{1,9},{9,17},{2,10},{10,18},{3,11},{11,19},{4,12},{12... | collective-permute-start | bytes 1572872 | tf_op jit(solution)/shard_map/ppermute | solution.py:213
  155.3 22.4 %collective-permute-start.44 = (bf16[32,64,128]{2,1,0:T(8,128)(2,1)S(1)}, bf16[32,64,128]{2,1,0:T(8,128)(2,1)S(1)}, u32[]{:S(2)}, u32[]{:S(2)}) collective-permute-start(bf16[32,64,128]{2,1,0:T(8,128)(2,1)S(1)} %get-tuple-element.37), channel_id=1, source_target_pairs={{16,8},{24,16},{17,9},{25,17},{18,10},{26,18},{19,11},{27,19},{20,... | collective-permute-start | bytes 1572872 | tf_op jit(solution)/shard_map/ppermute | solution.py:214
  162.0 22.0 %collective-permute-start.47 = (bf16[32,64,128]{2,1,0:T(8,128)(2,1)S(1)}, bf16[32,64,128]{2,1,0:T(8,128)(2,1)S(1)}, u32[]{:S(2)}, u32[]{:S(2)}) collective-permute-start(bf16[32,64,128]{2,1,0:T(8,128)(2,1)S(1)} %get-tuple-element.38), channel_id=1, source_target_pairs={{0,8},{8,16},{1,9},{9,17},{2,10},{10,18},{3,11},{11,19},{4,12},{12... | collective-permute-start | bytes 1572872 | tf_op jit(solution)/shard_map/ppermute | solution.py:213
  166.4 22.3 %collective-permute-start.50 = (bf16[32,64,128]{2,1,0:T(8,128)(2,1)S(1)}, bf16[32,64,128]{2,1,0:T(8,128)(2,1)S(1)}, u32[]{:S(2)}, u32[]{:S(2)}) collective-permute-start(bf16[32,64,128]{2,1,0:T(8,128)(2,1)S(1)} %get-tuple-element.39), channel_id=1, source_target_pairs={{16,8},{24,16},{17,9},{25,17},{18,10},{26,18},{19,11},{27,19},{20,... | collective-permute-start | bytes 1572872 | tf_op jit(solution)/shard_map/ppermute | solution.py:214
  173.0 22.3 %collective-permute-start.42 = (bf16[32,64,128]{2,1,0:T(8,128)(2,1)S(1)}, bf16[32,64,128]{2,1,0:T(8,128)(2,1)S(1)}, u32[]{:S(2)}, u32[]{:S(2)}) collective-permute-start(bf16[32,64,128]{2,1,0:T(8,128)(2,1)S(1)} %add_convert_fusion.3), channel_id=1, source_target_pairs={{0,8},{8,16},{16,24},{1,9},{9,17},{17,25},{2,10},{10,18},{18,26},{... | collective-permute-start | bytes 1572872 | tf_op jit(solution)/shard_map/ppermute | solution.py:213
  177.9 17.4 %collective-permute-start.45 = (bf16[32,64,128]{2,1,0:T(8,128)(2,1)S(1)}, bf16[32,64,128]{2,1,0:T(8,128)(2,1)S(1)}, u32[]{:S(2)}, u32[]{:S(2)}) collective-permute-start(bf16[32,64,128]{2,1,0:T(8,128)(2,1)S(1)} %add_convert_fusion.2), channel_id=1, source_target_pairs={{8,0},{16,8},{24,16},{9,1},{17,9},{25,17},{10,2},{18,10},{26,18},{... | collective-permute-start | bytes 1572872 | tf_op jit(solution)/shard_map/ppermute | solution.py:214
  184.3 20.1 %collective-permute-start.48 = (bf16[32,64,128]{2,1,0:T(8,128)(2,1)S(1)}, bf16[32,64,128]{2,1,0:T(8,128)(2,1)S(1)}, u32[]{:S(2)}, u32[]{:S(2)}) collective-permute-start(bf16[32,64,128]{2,1,0:T(8,128)(2,1)S(1)} %add_convert_fusion.1), channel_id=1, source_target_pairs={{0,8},{8,16},{16,24},{1,9},{9,17},{17,25},{2,10},{10,18},{18,26},{... | collective-permute-start | bytes 1572872 | tf_op jit(solution)/shard_map/ppermute | solution.py:213
  188.9 15.4 %collective-permute-start.51 = (bf16[32,64,128]{2,1,0:T(8,128)(2,1)S(1)}, bf16[32,64,128]{2,1,0:T(8,128)(2,1)S(1)}, u32[]{:S(2)}, u32[]{:S(2)}) collective-permute-start(bf16[32,64,128]{2,1,0:T(8,128)(2,1)S(1)} %add_convert_fusion), channel_id=1, source_target_pairs={{8,0},{16,8},{24,16},{9,1},{17,9},{25,17},{10,2},{18,10},{26,18},{... | collective-permute-start | bytes 1572872 | tf_op jit(solution)/shard_map/ppermute | solution.py:214
  (23 other events, 330.6 us)

commit v2 on v0

v2 whole, which is shorter than its diff:
```python
import functools

import jax
import jax.numpy as jnp
from jax import lax
from jax.experimental import pallas as pl
from jax.experimental.pallas import tpu as pltpu
from jax.sharding import PartitionSpec as P

BLK = 128
CHUNKS = 2
STEP = 8
KEYS = 16
VMEM_LIMIT = 48 * 1024 * 1024
PARAMS = pltpu.CompilerParams(vmem_limit_bytes=VMEM_LIMIT)
BY_LAST = (((1,), (1,)), ((), ()))


def identity(size):
    return (
        lax.broadcasted_iota(jnp.int32, (size, size), 0) == lax.broadcasted_iota(jnp.int32, (size, size), 1)
    ).astype(jnp.bfloat16)


def column(vector_ref, rows):
    return jnp.broadcast_to(vector_ref[...], (rows, vector_ref.shape[1])).T


def unit_mask(mask_ref, rows, cols):
    row, col = lax.axis_index("row"), lax.axis_index("col")
    return mask_ref[(row * rows) // BLK, (col * cols) // BLK].astype(jnp.float32)


def spread(pair_ref, wide):
    rows, keys, chans = pair_ref.shape
    wide[...] = pair_ref[...].astype(jnp.float32).reshape(rows * keys, chans)


def normalize(wide, eye, key, keys, rows):
    cells = wide[pl.ds(key, rows, stride=keys), :].astype(jnp.bfloat16)
    values = lax.dot_general(eye, cells, BY_LAST, preferred_element_type=jnp.float32)
    centred = values - jnp.mean(values, axis=0, keepdims=True)
    inverse = lax.rsqrt(jnp.mean(centred * centred, axis=0, keepdims=True) + 1e-05)
    return centred * inverse, inverse


def front_kernel(mask, pair, gain, bias, weight, *refs):
    outs, (wide, flat, gain_col, bias_col, weight_t) = refs[:CHUNKS], refs[CHUNKS:]
    rows, keys, chans = pair.shape
    hidden = weight.shape[1] // 2
    part = hidden // CHUNKS

    @pl.when(pl.program_id(0) == 0)
    def _():
        gain_col[...] = column(gain, rows)
        bias_col[...] = column(bias, rows)
        weight_t[...] = weight[...].astype(jnp.float32).T.astype(jnp.bfloat16)

    cols = pl.num_programs(0) * keys
    valid = unit_mask(mask, rows, cols)
    eye = identity(chans)
    spread(pair, wide)
    for key in range(keys):
        scaled, _ = normalize(wide, eye, key, keys, rows)
        normed = (scaled * gain_col[...] + bias_col[...]).astype(jnp.bfloat16)
        projected = jnp.dot(weight_t[...], normed, preferred_element_type=jnp.float32)
        flat[pl.ds(key, hidden, stride=keys), :] = valid * jax.nn.sigmoid(projected[hidden:]) * projected[:hidden]
    for chunk in range(CHUNKS):
        outs[chunk][...] = (
            flat[chunk * part * keys : (chunk + 1) * part * keys, :].reshape(part, keys, rows).astype(jnp.bfloat16)
        )


def front(pair, gain, bias, proj_weight, tile_mask, side):
    rows, cols, chans = pair.shape
    width = proj_weight.shape[1] // 2
    part = width // 2 // CHUNKS
    whole = lambda shape: pl.BlockSpec(shape, lambda g: (0, 0))
    return pl.pallas_call(
        front_kernel,
        out_shape=[jax.ShapeDtypeStruct((part, cols, rows), jnp.bfloat16)] * CHUNKS,
        grid=(cols // KEYS,),
        in_specs=[
            pl.BlockSpec(memory_space=pltpu.SMEM),
            pl.BlockSpec((rows, KEYS, chans), lambda g: (0, g, 0)),
            whole((1, chans)),
            whole((1, chans)),
            pl.BlockSpec((chans, width), lambda g: (0, side)),
        ],
        out_specs=[pl.BlockSpec((part, KEYS, rows), lambda g: (0, g, 0))] * CHUNKS,
        scratch_shapes=[
            pltpu.VMEM((rows * KEYS, chans), jnp.float32),
            pltpu.VMEM((width // 2 * KEYS, rows), jnp.float32),
            pltpu.VMEM((chans, rows), jnp.float32),
            pltpu.VMEM((chans, rows), jnp.float32),
            pltpu.VMEM((width, chans), jnp.bfloat16),
        ],
        compiler_params=PARAMS,
        cost_estimate=pl.CostEstimate(
            flops=4 * rows * cols * chans * width, bytes_accessed=6 * rows * cols * chans, transcendentals=rows * cols * width
        ),
        name="left_front" if side == 0 else "right_front",
    )(tile_mask, pair, gain, bias, proj_weight)


def tail_kernel(mask, pair, gain, bias, weight, *refs):
    lefts, refs = refs[:CHUNKS], refs[CHUNKS:]
    rights, refs = refs[: 3 * CHUNKS], refs[3 * CHUNKS :]
    out, wide, right_flat, left_flat, gain_col, bias_col, weight_t = refs
    rows, keys, chans = pair.shape
    hidden = weight.shape[1] // 4
    part = hidden // CHUNKS

    @pl.when(pl.program_id(0) == 0)
    def _():
        gain_col[...] = column(gain, rows)
        bias_col[...] = column(bias, rows)
        weight_t[...] = weight[...].astype(jnp.float32).T.astype(jnp.bfloat16)

    cols = pl.num_programs(0) * keys
    valid = unit_mask(mask, rows, cols)
    eye = identity(chans)
    row_eye = eye if rows == chans else identity(rows)
    spread(pair, wide)
    for chunk in range(CHUNKS):
        own, up, down = (rights[i * CHUNKS + chunk][...].astype(jnp.float32) for i in range(3))
        place = slice(chunk * part * keys, (chunk + 1) * part * keys)
        right_flat[place, :] = (own + up + down).reshape(part * keys, rows)
        left_flat[place, :] = lefts[chunk][...].reshape(part * keys, rows)
    for key in range(keys):
        scaled, inverse = normalize(wide, eye, key, keys, rows)
        normed = (scaled * gain_col[...] + bias_col[...]).astype(jnp.bfloat16)
        projected = jnp.dot(weight_t[...], normed, preferred_element_type=jnp.float32)
        grads = []
        for side, source in enumerate((left_flat, right_flat)):
            lin = projected[2 * side * hidden : (2 * side + 1) * hidden]
            sig = jax.nn.sigmoid(projected[(2 * side + 1) * hidden : (2 * side + 2) * hidden])
            through = source[pl.ds(key, hidden, stride=keys), :] * valid * sig
            grads += [through.astype(jnp.bfloat16), (through * lin * (1.0 - sig)).astype(jnp.bfloat16)]
        grad_normed = jnp.dot(weight[...], jnp.concatenate(grads, axis=0), preferred_element_type=jnp.float32)
        scaled_grad = grad_normed * gain_col[...]
        result = inverse * (
            scaled_grad
            - jnp.mean(scaled_grad, axis=0, keepdims=True)
            - scaled * jnp.mean(scaled_grad * scaled, axis=0, keepdims=True)
        )
        wide[pl.ds(key, rows, stride=keys), :] = lax.dot_general(
            row_eye, result.astype(jnp.bfloat16), BY_LAST, preferred_element_type=jnp.float32
        )
    out[...] = wide[...].reshape(rows, keys, chans).astype(jnp.bfloat16)


def tail(pair, gain, bias, proj_weight, tile_mask, lefts, rights):
    rows, cols, chans = pair.shape
    width = proj_weight.shape[1]
    part = width // 4 // CHUNKS
    whole = lambda shape: pl.BlockSpec(shape, lambda g: (0, 0))
    cells = pl.BlockSpec((rows, KEYS, chans), lambda g: (0, g, 0))
    small = pl.BlockSpec((part, KEYS, rows), lambda g: (0, g, 0))
    return pl.pallas_call(
        tail_kernel,
        out_shape=jax.ShapeDtypeStruct(pair.shape, jnp.bfloat16),
        grid=(cols // KEYS,),
        in_specs=[
            pl.BlockSpec(memory_space=pltpu.SMEM),
            cells,
            whole((1, chans)),
            whole((1, chans)),
            whole((chans, width)),
        ]
        + [small] * (4 * CHUNKS),
        out_specs=cells,
        scratch_shapes=[
            pltpu.VMEM((rows * KEYS, chans), jnp.float32),
            pltpu.VMEM((width // 4 * KEYS, rows), jnp.float32),
            pltpu.VMEM((width // 4 * KEYS, rows), jnp.float32),
            pltpu.VMEM((chans, rows), jnp.float32),
            pltpu.VMEM((chans, rows), jnp.float32),
            pltpu.VMEM((width, chans), jnp.bfloat16),
        ],
        compiler_params=PARAMS,
        cost_estimate=pl.CostEstimate(
            flops=8 * rows * cols * chans * width, bytes_accessed=10 * rows * cols * chans, transcendentals=rows * cols * width
        ),
        name="tail",
    )(tile_mask, pair, gain, bias, proj_weight, *lefts, *rights)


def column_devices(n_col):
    return [m for m in range(0, n_col, 2)] + [m for m in range(1, n_col, 2)]


def gather_columns(block, n_col):
    def exchange(value, mask):
        return lax.ppermute(value, "col", [(d, d ^ mask) for d in range(n_col)])

    same = [block] + [exchange(block, m) for m in range(2, n_col, 2)]
    return same + [exchange(value, 1) for value in same]


def load_panel(blocks, panel, sems, first, chans, masks):
    col = lax.axis_index("col")
    cols = blocks[0].shape[1]
    copies = []
    for p, m in enumerate(masks):
        place = pl.multiple_of(jnp.bitwise_xor(col, m) * cols, cols)
        copies.append(
            pltpu.make_async_copy(
                blocks[p].at[pl.ds(first, chans)], panel.at[pl.ds(first, chans), pl.ds(place, cols), :], sems.at[p]
            )
        )
    return copies


def fill_panel(blocks, panel, sems, masks):
    steps = pl.num_programs(0)
    step = pl.program_id(0)
    total = panel.shape[0] // STEP

    @pl.when(step == 0)
    def _():
        for g in range(total):
            for c in load_panel(blocks, panel, sems.at[g], g * STEP, STEP, masks):
                c.start()

    for c in load_panel(blocks, panel, sems.at[step], pl.multiple_of(step * STEP, STEP), STEP, masks):
        c.wait()
    del steps


def partial_kernel(n, masks, left, *refs):
    blocks, refs = refs[: len(masks)], refs[len(masks) :]
    outs, (panel, sems) = refs[:n], refs[n:]
    fill_panel(blocks, panel, sems, masks)
    row = lax.axis_index("row")
    rows = left.shape[2]
    first = pl.program_id(0) * STEP
    for c in range(STEP):
        lhs = left[c]
        for s in range(n):
            b = lax.rem(row + s, n)
            rhs = panel[first + c, pl.ds(pl.multiple_of(b * rows, rows), rows), :]
            outs[s][c] = lax.dot_general(lhs, rhs, BY_LAST, preferred_element_type=jnp.float32).astype(jnp.bfloat16)


def partial_products(left, blocks, n):
    chans, ks, rows = left.shape
    masks = column_devices(len(blocks))
    total = len(blocks) * blocks[0].shape[1]
    small = pl.BlockSpec((STEP, ks, rows), lambda g: (g, 0, 0))
    return pl.pallas_call(
        functools.partial(partial_kernel, n, masks),
        out_shape=[jax.ShapeDtypeStruct((chans, ks, rows), jnp.bfloat16)] * n,
        grid=(chans // STEP,),
        in_specs=[small] + [pl.BlockSpec(memory_space=pl.ANY)] * len(masks),
        out_specs=[small] * n,
        scratch_shapes=[
            pltpu.VMEM((chans, total, rows), jnp.bfloat16),
            pltpu.SemaphoreType.DMA((chans // STEP, len(masks))),
        ],
        compiler_params=PARAMS,
        cost_estimate=pl.CostEstimate(
            flops=2 * chans * ks * rows * total, bytes_accessed=2 * chans * rows * (total + ks * (n + 1)), transcendentals=0
        ),
        name="right_partials",
    )(left, *blocks)


def left_kernel(n, masks, own, *refs):
    ups, downs, refs = refs[: n - 1], refs[n - 1 : 2 * n - 2], refs[2 * n - 2 :]
    blocks, (out, panel, sems) = refs[: len(masks)], refs[len(masks) :]
    fill_panel(blocks, panel, sems, masks)
    row = lax.axis_index("row")
    rows = own.shape[2]
    first = pl.program_id(0) * STEP
    for c in range(STEP):
        acts, grads = [], []
        for s in range(n):
            b = lax.rem(row + s, n)
            grads.append(panel[first + c, pl.ds(pl.multiple_of(b * rows, rows), rows), :])
            acts.append(own[c] if s == 0 else jnp.where(row + s < n, downs[s - 1][c], ups[n - s - 1][c]))
        out[c] = jnp.dot(
            jnp.concatenate(acts, axis=1), jnp.concatenate(grads, axis=0), preferred_element_type=jnp.float32
        )


def left_products(own, ups, downs, blocks, n):
    chans, ks, rows = own.shape
    masks = column_devices(len(blocks))
    total = len(blocks) * blocks[0].shape[1]
    small = pl.BlockSpec((STEP, ks, rows), lambda g: (g, 0, 0))
    return pl.pallas_call(
        functools.partial(left_kernel, n, masks),
        out_shape=jax.ShapeDtypeStruct((chans, ks, rows), jnp.float32),
        grid=(chans // STEP,),
        in_specs=[small] * (2 * n - 1) + [pl.BlockSpec(memory_space=pl.ANY)] * len(masks),
        out_specs=small,
        scratch_shapes=[
            pltpu.VMEM((chans, total, rows), jnp.bfloat16),
            pltpu.SemaphoreType.DMA((chans // STEP, len(masks))),
        ],
        compiler_params=PARAMS,
        cost_estimate=pl.CostEstimate(
            flops=2 * chans * ks * rows * total, bytes_accessed=2 * chans * rows * (total + ks * (n + 2)), transcendentals=0
        ),
        name="left_products",
    )(own, *ups, *downs, *blocks)


def shards(pair, grad_x, norm_gain, norm_bias, proj_weight, tile_mask):
    hidden = grad_x.shape[2]
    n, n_col = lax.axis_size("row"), lax.axis_size("col")
    part = hidden // CHUNKS
    gain, bias = norm_gain[None, :], norm_bias[None, :]

    grad_t = jnp.transpose(grad_x, (2, 1, 0))
    blocks = [gather_columns(grad_t[chunk * part : (chunk + 1) * part], n_col) for chunk in range(CHUNKS)]

    owns = front(pair, gain, bias, proj_weight, tile_mask, 1)
    left_acts = front(pair, gain, bias, proj_weight, tile_mask, 0)

    ups, downs = [], []
    for own in owns:
        up_list, down_list = [], []
        up, down = own, own
        for h in range(1, n):
            up = lax.ppermute(up, "row", [(r, r + 1) for r in range(h - 1, n - 1)])
            down = lax.ppermute(down, "row", [(r, r - 1) for r in range(1, n - h + 1)])
            up_list.append(up)
            down_list.append(down)
        ups.append(up_list)
        downs.append(down_list)

    partials, up_sums, down_sums, firsts = [], [], [], []
    for chunk in range(CHUNKS):
        sums = partial_products(left_acts[chunk], blocks[chunk], n)
        up = down = None
        for step in range(1, n):
            away = n - step
            up_sum, down_sum = sums[away], sums[n - away]
            if up is not None:
                up_sum = (up_sum.astype(jnp.float32) + up.astype(jnp.float32)).astype(jnp.bfloat16)
                down_sum = (down_sum.astype(jnp.float32) + down.astype(jnp.float32)).astype(jnp.bfloat16)
            up = lax.ppermute(up_sum, "row", [(r, r + 1) for r in range(step)])
            down = lax.ppermute(down_sum, "row", [(r, r - 1) for r in range(n - step, n)])
            if step == 1:
                firsts.append(up)
        partials.append(sums[0])
        up_sums.append(up)
        down_sums.append(down)

    lefts = []
    for chunk in range(CHUNKS):
        own, _ = lax.optimization_barrier((owns[chunk], firsts[chunk]))
        lefts.append(left_products(own, ups[chunk], downs[chunk], blocks[chunk], n))

    return tail(pair, gain, bias, proj_weight, tile_mask, lefts, partials + up_sums + down_sums)


def solution(mesh):
    placed = (P("row", "col", None), P("row", "col", None), P(), P(), P(), P())
    return jax.shard_map(
        shards, mesh=mesh, in_specs=placed, out_specs=P("row", "col", None), check_vma=False
    )
```

time: 301 us -> 247 us (0.82)
  waiting for transfers between devices: 213 us -> 85 us
  Pallas kernels: 0 us -> 81.4 us
  starting transfers between devices: 0.27 us -> 71.5 us
  local copies, waits for them, and re-layouts: 41.6 us -> 5.13 us
  matrix products: 17.7 us -> 0 us
  between operations: 13.3 us -> 0.55 us
  other arithmetic: 14.6 us -> 2.92 us
    all_gather x2 -> x0, waiting for transfers between devices: 136 us -> none  [the longest x1 81.5 us: shards(): right_panel = lax.all_gather(right_act, 'row', axis=0, tiled=True)]
    ppermute x0 -> x38, waiting for transfers between devices: none -> 85 us  [the longest x14 40.5 us: exchange(): return lax.ppermute(value, 'col', [(d, d ^ mask) for d in range(n_col)])]
    pallas_call x0 -> x7, Pallas kernels: none -> 81.4 us  [the longest x2 33.7 us: front(): pl.pallas_call(front_kernel, out_shape=[jax.ShapeDtypeStruct((part, cols,...]
    unnamed x4 -> x0, waiting for transfers between devices: 77 us -> none
    ppermute x0 -> x38, starting transfers between devices: none -> 71.5 us  [the longest x6 39 us: shards(): up = lax.ppermute(up_sum, 'row', [(r, r + 1) for r in range(step)])]
    unnamed x23 -> x31, local copies, waits for them, and re-layouts: 37.5 us -> 5.06 us
    dot_general x5 -> x0, matrix products: 17.7 us -> none  [the longest x1 9.5 us: shards(): jnp.einsum('ijc,jkc->ikc', grad_panel, right_panel, preferred_element_typ...]
    another operation x2 -> x0, other arithmetic: 8.89 us -> none
  transfers between devices with their start and end apart: 3 -> 38, of which waited for: 3 -> 12; matrix products, arithmetic and copies ran while one was open for 1% -> 1% of each run, Pallas kernels for 0% -> 21%
where the time goes in v2:
time: 247 us; the launch traced here: 246 us
  waiting for transfers between devices  85 us (34%)
  Pallas kernels  81.4 us (33%)
  starting transfers between devices  71.5 us (29%)
  local copies, waits for them, and re-layouts  5.13 us (2%)
  other arithmetic  2.92 us (1%)
    ppermute x14, waiting for transfers between devices, exchange(): return lax.ppermute(value, 'col', [(d, d ^ mask) for d in range(n_col)])  40.5 us
    ppermute x6, starting transfers between devices, shards(): up = lax.ppermute(up_sum, 'row', [(r, r + 1) for r in range(step)])  39 us
    pallas_call x2, Pallas kernels, front(): pl.pallas_call(front_kernel, out_shape=[jax.ShapeDtypeStruct((part, cols,...  33.7 us
    pallas_call x1, Pallas kernels, tail(): pl.pallas_call(tail_kernel, out_shape=jax.ShapeDtypeStruct(pair.shape, jn...  30.1 us
    ppermute x6, waiting for transfers between devices, shards(): up = lax.ppermute(up_sum, 'row', [(r, r + 1) for r in range(step)])  29.2 us
    ppermute x14, starting transfers between devices, exchange(): return lax.ppermute(value, 'col', [(d, d ^ mask) for d in range(n_col)])  10.6 us
    pallas_call x2, Pallas kernels, partial_products(): pl.pallas_call(functools.partial(partial_kernel, n, masks), out_shape=[ja...  9.34 us
    ppermute x6, starting transfers between devices, shards(): up = lax.ppermute(up, 'row', [(r, r + 1) for r in range(h - 1, n - 1)])  8.64 us
  transfers between devices with their start and end apart: 38, of which 12 were waited for; matrix products, arithmetic and copies ran while one was open for 1% of the time, Pallas kernels for 21%

profile of v2, /device:TPU:0, one launch (start us, length us, event | category | flops | bytes accessed | tf_op | source)
XLA Modules:
  0.0 246.4 jit_solution(12695684932202776912)
XLA Ops:
  0.0 2.1 copy.9
  2.1 3.0 %collective-permute-start = (bf16[32,64,128]{2,1,0:T(8,128)(2,1)S(1)}, bf16[32,64,128]{2,1,0:T(8,128)(2,1)S(1)}, u32[]{:S(2)}, u32[]{:S(2)}) collective-permute-start(bf16[32,64,128]{2,1,0:T(8,128)(2,1)S(1)} %get-tuple-element.34.refs_0_.refs_6_), channel_id=1, source_target_pairs={{0,2},{1,3},{2,0},{3,1},{4,6},{5,7},{6,4},{7,5},{8,10},{9,11},{10,... | collective-permute-start | bytes 1572872 | tf_op jit(solution)/shard_map/ppermute | solution.py:195
  5.2 1.5 collective-permute-start.1
  6.7 1.9 collective-permute-start.14
  8.7 9.3 %collective-permute-done.refs_1_.refs_7_ = bf16[32,64,128]{2,1,0:T(8,128)(2,1)S(1)} collective-permute-done((bf16[32,64,128]{2,1,0:T(8,128)(2,1)S(1)}, bf16[32,64,128]{2,1,0:T(8,128)(2,1)S(1)}, u32[]{:S(2)}, u32[]{:S(2)}) %collective-permute-start) | collective-permute-done | bytes 524320 | tf_op jit(solution)/shard_map/ppermute | solution.py:195
  17.9 2.1 collective-permute-start.15
  20.0 10.2 %collective-permute-done.1.refs_2_.refs_8_ = bf16[32,64,128]{2,1,0:T(8,128)(2,1)S(1)} collective-permute-done((bf16[32,64,128]{2,1,0:T(8,128)(2,1)S(1)}, bf16[32,64,128]{2,1,0:T(8,128)(2,1)S(1)}, u32[]{:S(2)}, u32[]{:S(2)}) %collective-permute-start.1) | collective-permute-done | bytes 524320 | tf_op jit(solution)/shard_map/ppermute | solution.py:195
  31.2 9.2 %collective-permute-done.14.refs_1_.refs_7_ = bf16[32,64,128]{2,1,0:T(8,128)(2,1)S(1)} collective-permute-done((bf16[32,64,128]{2,1,0:T(8,128)(2,1)S(1)}, bf16[32,64,128]{2,1,0:T(8,128)(2,1)S(1)}, u32[]{:S(2)}, u32[]{:S(2)}) %collective-permute-start.14) | collective-permute-done | bytes 524320 | tf_op jit(solution)/shard_map/ppermute | solution.py:195
  40.4 11.8 %collective-permute-done.15.refs_2_.refs_8_ = bf16[32,64,128]{2,1,0:T(8,128)(2,1)S(1)} collective-permute-done((bf16[32,64,128]{2,1,0:T(8,128)(2,1)S(1)}, bf16[32,64,128]{2,1,0:T(8,128)(2,1)S(1)}, u32[]{:S(2)}, u32[]{:S(2)}) %collective-permute-start.15) | collective-permute-done | bytes 524320 | tf_op jit(solution)/shard_map/ppermute | solution.py:195
  53.3 16.9 %left_front.1 = (bf16[32,64,128]{2,1,0:T(8,128)(2,1)S(1)}, bf16[32,64,128]{2,1,0:T(8,128)(2,1)S(1)}) custom-call(s32[4,4]{1,0:T(4,128)S(1)} %copy-done.8, bf16[128,64,128]{2,1,0:T(8,128)(2,1)S(1)} %copy-done, f32[1,128]{1,0:T(1,128)S(1)} %bitcast.5, f32[1,128]{1,0:T(1,128)S(1)} %bitcast.8, bf16[128,256]{1,0:T(8,128)(2,1)S(1)} %copy-done.7), custom_call_target="tpu_custom_call" | custom-call | flops 536870912 | bytes 6291456 | tf_op jit(solution)/shard_map/left_front/pallas_call | solution.py:79
  70.2 0.8 copy-done.12
  71.0 4.7 %right_partials.2 = (bf16[32,64,128]{2,1,0:T(8,128)(2,1)S(1)}, bf16[32,64,128]{2,1,0:T(8,128)(2,1)S(1)}, bf16[32,64,128]{2,1,0:T(8,128)(2,1)S(1)}, bf16[32,64,128]{2,1,0:T(8,128)(2,1)S(1)}) custom-call(bf16[32,64,128]{2,1,0:T(8,128)(2,1)S(1)} %get-tuple-element.20.left, bf16[32,64,128]{2,1,0:T(8,128)(2,1)S(1)} %get-tuple-element.34.refs_0_.refs_6_, ...), custom_call_target="tpu_custom_call" | custom-call | flops 268435456 | bytes 6815744 | tf_op jit(solution)/shard_map/right_partials/pallas_call | solution.py:251
  75.7 3.5 %collective-permute-start.7 = (bf16[32,64,128]{2,1,0:T(8,128)(2,1)S(1)}, bf16[32,64,128]{2,1,0:T(8,128)(2,1)S(1)}, u32[]{:S(2)}, u32[]{:S(2)}) collective-permute-start(bf16[32,64,128]{2,1,0:T(8,128)(2,1)S(1)} %get-tuple-element.21), channel_id=1, source_target_pairs={{0,8},{1,9},{2,10},{3,11},{4,12},{5,13},{6,14},{7,15}} | collective-permute-start | bytes 1572872 | tf_op jit(solution)/shard_map/ppermute | solution.py:344
  79.2 0.7 collective-permute-start.32
  80.0 16.9 %right_front.1 = (bf16[32,64,128]{2,1,0:T(8,128)(2,1)S(1)}, bf16[32,64,128]{2,1,0:T(8,128)(2,1)S(1)}) custom-call(s32[4,4]{1,0:T(4,128)S(1)} %copy-done.8, bf16[128,64,128]{2,1,0:T(8,128)(2,1)S(1)} %copy-done, f32[1,128]{1,0:T(1,128)S(1)} %bitcast.6, f32[1,128]{1,0:T(1,128)S(1)} %bitcast.9, bf16[128,256]{1,0:T(8,128)(2,1)S(1)} %copy-done.7), custom_call_target="tpu_custom_call" | custom-call | flops 536870912 | bytes 6291456 | tf_op jit(solution)/shard_map/right_front/pallas_call | solution.py:79
  96.8 1.3 collective-permute-start.8
  98.2 0.8 copy-done.13
  99.2 4.7 %right_partials.3 = (bf16[32,64,128]{2,1,0:T(8,128)(2,1)S(1)}, bf16[32,64,128]{2,1,0:T(8,128)(2,1)S(1)}, bf16[32,64,128]{2,1,0:T(8,128)(2,1)S(1)}, bf16[32,64,128]{2,1,0:T(8,128)(2,1)S(1)}) custom-call(bf16[32,64,128]{2,1,0:T(8,128)(2,1)S(1)} %get-tuple-element.24.left, bf16[32,64,128]{2,1,0:T(8,128)(2,1)S(1)} %get-tuple-element.33.refs_0_.refs_6_, ...), custom_call_target="tpu_custom_call" | custom-call | flops 268435456 | bytes 6815744 | tf_op jit(solution)/shard_map/right_partials/pallas_call | solution.py:251
  103.9 3.4 %collective-permute-start.21 = (bf16[32,64,128]{2,1,0:T(8,128)(2,1)S(1)}, bf16[32,64,128]{2,1,0:T(8,128)(2,1)S(1)}, u32[]{:S(2)}, u32[]{:S(2)}) collective-permute-start(bf16[32,64,128]{2,1,0:T(8,128)(2,1)S(1)} %get-tuple-element.25), channel_id=1, source_target_pairs={{0,8},{1,9},{2,10},{3,11},{4,12},{5,13},{6,14},{7,15}} | collective-permute-start | bytes 1572872 | tf_op jit(solution)/shard_map/ppermute | solution.py:344
  107.3 0.7 collective-permute-start.35
  108.0 1.3 collective-permute-start.11
  109.3 4.6 %collective-permute-start.22 = (bf16[32,64,128]{2,1,0:T(8,128)(2,1)S(1)}, bf16[32,64,128]{2,1,0:T(8,128)(2,1)S(1)}, u32[]{:S(2)}, u32[]{:S(2)}) collective-permute-start(bf16[32,64,128]{2,1,0:T(8,128)(2,1)S(1)} %get-tuple-element.26.own), channel_id=1, source_target_pairs={{0,8},{8,16},{16,24},{1,9},{9,17},{17,25},{2,10},{10,18},{18,26},{... | collective-permute-start | bytes 1572872 | tf_op jit(solution)/shard_map/ppermute | solution.py:327
  114.3 1.3 collective-permute-start.25
  115.6 6.1 %collective-permute-done.21 = bf16[32,64,128]{2,1,0:T(8,128)(2,1)S(1)} collective-permute-done((bf16[32,64,128]{2,1,0:T(8,128)(2,1)S(1)}, bf16[32,64,128]{2,1,0:T(8,128)(2,1)S(1)}, u32[]{:S(2)}, u32[]{:S(2)}) %collective-permute-start.21) | collective-permute-done | bytes 524320 | tf_op jit(solution)/shard_map/ppermute | solution.py:344
  122.4 5.0 %collective-permute-start.28 = (bf16[32,64,128]{2,1,0:T(8,128)(2,1)S(1)}, bf16[32,64,128]{2,1,0:T(8,128)(2,1)S(1)}, u32[]{:S(2)}, u32[]{:S(2)}) collective-permute-start(bf16[32,64,128]{2,1,0:T(8,128)(2,1)S(1)} %get-tuple-element.38), channel_id=1, source_target_pairs={{0,8},{8,16},{1,9},{9,17},{2,10},{10,18},{3,11},{11,19},{4,12},{12... | collective-permute-start | bytes 1572872 | tf_op jit(solution)/shard_map/ppermute | solution.py:344
  127.7 1.9 collective-permute-start.30
  129.6 3.3 %collective-permute-done.22.refs_0_ = bf16[32,64,128]{2,1,0:T(8,128)(2,1)S(1)} collective-permute-done((bf16[32,64,128]{2,1,0:T(8,128)(2,1)S(1)}, bf16[32,64,128]{2,1,0:T(8,128)(2,1)S(1)}, u32[]{:S(2)}, u32[]{:S(2)}) %collective-permute-start.22) | collective-permute-done | bytes 524320 | tf_op jit(solution)/shard_map/ppermute | solution.py:327
  132.9 1.3 collective-permute-start.12
  135.2 1.3 collective-permute-start.26
  136.5 7.6 %collective-permute-done.28 = bf16[32,64,128]{2,1,0:T(8,128)(2,1)S(1)} collective-permute-done((bf16[32,64,128]{2,1,0:T(8,128)(2,1)S(1)}, bf16[32,64,128]{2,1,0:T(8,128)(2,1)S(1)}, u32[]{:S(2)}, u32[]{:S(2)}) %collective-permute-start.28) | collective-permute-done | bytes 524320 | tf_op jit(solution)/shard_map/ppermute | solution.py:344
  145.0 9.5 %collective-permute-done.30 = bf16[32,64,128]{2,1,0:T(8,128)(2,1)S(1)} collective-permute-done((bf16[32,64,128]{2,1,0:T(8,128)(2,1)S(1)}, bf16[32,64,128]{2,1,0:T(8,128)(2,1)S(1)}, u32[]{:S(2)}, u32[]{:S(2)}) %collective-permute-start.30) | collective-permute-done | bytes 524320 | tf_op jit(solution)/shard_map/ppermute | solution.py:344
  155.4 0.7 collective-permute-start.10
  156.1 1.3 collective-permute-start.13
  157.4 3.3 %collective-permute-done.26.refs_4_ = bf16[32,64,128]{2,1,0:T(8,128)(2,1)S(1)} collective-permute-done((bf16[32,64,128]{2,1,0:T(8,128)(2,1)S(1)}, bf16[32,64,128]{2,1,0:T(8,128)(2,1)S(1)}, u32[]{:S(2)}, u32[]{:S(2)}) %collective-permute-start.26) | collective-permute-done | bytes 524320 | tf_op jit(solution)/shard_map/ppermute | solution.py:328
  160.7 0.7 collective-permute-start.24
  161.4 1.3 collective-permute-start.27
  162.7 1.0 add_convert_fusion.1
  163.7 23.1 %collective-permute-start.29 = (bf16[32,64,128]{2,1,0:T(8,128)(2,1)S(1)}, bf16[32,64,128]{2,1,0:T(8,128)(2,1)S(1)}, u32[]{:S(2)}, u32[]{:S(2)}) collective-permute-start(bf16[32,64,128]{2,1,0:T(8,128)(2,1)S(1)} %add_convert_fusion.3), channel_id=1, source_target_pairs={{0,8},{8,16},{16,24},{1,9},{9,17},{17,25},{2,10},{10,18},{18,26},{... | collective-permute-start | bytes 1572872 | tf_op jit(solution)/shard_map/ppermute | solution.py:344
  186.9 1.0 add_convert_fusion
  187.9 1.9 collective-permute-start.31
  189.8 1.3 collective-permute-start.34
  191.1 1.5 collective-permute-start.37
  192.6 4.0 %left_products.2.refs_0_ = f32[32,64,128]{2,1,0:T(8,128)} custom-call(bf16[32,64,128]{2,1,0:T(8,128)(2,1)S(1)} %get-tuple-element.22.own, bf16[32,64,128]{2,1,0:T(8,128)(2,1)S(1)} %collective-permute-done.8.refs_0_, bf16[32,64,128]{2,1,0:T(8,128)(2,1)S(1)} %collective-permute-done.9.refs_1_, bf16[32,64,128]{2,1,0:T(8,128)(2,1)S(1)} %collective-permute-done.10.refs_2_, ...), custom_call_target="tpu_custom_call" | custom-call | flops 268435456 | bytes 7340032 | tf_op jit(solution)/shard_map/left_products/pallas_call | solution.py:292
  196.6 4.1 %left_products.3.refs_1_ = f32[32,64,128]{2,1,0:T(8,128)} custom-call(bf16[32,64,128]{2,1,0:T(8,128)(2,1)S(1)} %get-tuple-element.26.own, bf16[32,64,128]{2,1,0:T(8,128)(2,1)S(1)} %collective-permute-done.22.refs_0_, bf16[32,64,128]{2,1,0:T(8,128)(2,1)S(1)} %collective-permute-done.23.refs_1_, bf16[32,64,128]{2,1,0:T(8,128)(2,1)S(1)} %collective-permute-done.24.refs_2_, ...), custom_call_target="tpu_custom_call" | custom-call | flops 268435456 | bytes 7340032 | tf_op jit(solution)/shard_map/left_products/pallas_call | solution.py:292
  200.8 6.0 %collective-permute-done.31.refs_5_ = bf16[32,64,128]{2,1,0:T(8,128)(2,1)S(1)} collective-permute-done((bf16[32,64,128]{2,1,0:T(8,128)(2,1)S(1)}, bf16[32,64,128]{2,1,0:T(8,128)(2,1)S(1)}, u32[]{:S(2)}, u32[]{:S(2)}) %collective-permute-start.31) | collective-permute-done | bytes 524320 | tf_op jit(solution)/shard_map/ppermute | solution.py:344
  206.8 8.3 %collective-permute-done.37.refs_7_ = bf16[32,64,128]{2,1,0:T(8,128)(2,1)S(1)} collective-permute-done((bf16[32,64,128]{2,1,0:T(8,128)(2,1)}, bf16[32,64,128]{2,1,0:T(8,128)(2,1)S(1)}, u32[]{:S(2)}, u32[]{:S(2)}) %collective-permute-start.37) | collective-permute-done | bytes 524320 | tf_op jit(solution)/shard_map/ppermute | solution.py:345
  215.1 1.2 copy-done.2
  216.3 30.1 %tail.1 = bf16[128,64,128]{2,1,0:T(8,128)(2,1)} custom-call(s32[4,4]{1,0:T(4,128)S(1)} %copy-done.8, bf16[128,64,128]{2,1,0:T(8,128)(2,1)} %pair.5, f32[1,128]{1,0:T(1,128)S(1)} %bitcast.7, f32[1,128]{1,0:T(1,128)S(1)} %bitcast.10, bf16[128,256]{1,0:T(8,128)(2,1)S(1)} %copy-done.7, f32[32,64,128]{2,1,0:T(8,128)S(1)} %copy-done.1, ...), custom_call_target="tpu_custom_call" | custom-call | flops 2147483648 | bytes 10485760 | tf_op jit(solution)/shard_map/tail/pallas_call | solution.py:160
  (73 shorter events, 6.5 us)
Async XLA Ops:
  0.0 53.3 %copy-start.8 = (s32[4,4]{1,0:T(4,128)S(1)}, s32[4,4]{1,0:T(4,128)}, u32[]{:S(2)}) copy-start(s32[4,4]{1,0:T(4,128)} %mask.5) | copy-start | bytes 196
  0.0 53.3 %copy-start = (bf16[128,64,128]{2,1,0:T(8,128)(2,1)S(1)}, bf16[128,64,128]{2,1,0:T(8,128)(2,1)}, u32[]{:S(2)}) copy-start(bf16[128,64,128]{2,1,0:T(8,128)(2,1)} %pair.5) | copy-start | bytes 6291460
  0.0 53.3 %copy-start.9 = (f32[128]{0:T(128)S(1)}, f32[128]{0:T(128)}, u32[]{:S(2)}) copy-start(f32[128]{0:T(128)} %param.8) | copy-start | bytes 1540
  0.0 53.3 %copy-start.10 = (f32[128]{0:T(128)S(1)}, f32[128]{0:T(128)}, u32[]{:S(2)}) copy-start(f32[128]{0:T(128)} %param.9) | copy-start | bytes 1540
  0.0 53.3 %copy-start.7 = (bf16[128,256]{1,0:T(8,128)(2,1)S(1)}, bf16[128,256]{1,0:T(8,128)(2,1)}, u32[]{:S(2)}) copy-start(bf16[128,256]{1,0:T(8,128)(2,1)} %weight.5) | copy-start | bytes 196612
  2.1 15.8 %collective-permute-start = (bf16[32,64,128]{2,1,0:T(8,128)(2,1)S(1)}, bf16[32,64,128]{2,1,0:T(8,128)(2,1)S(1)}, u32[]{:S(2)}, u32[]{:S(2)}) collective-permute-start(bf16[32,64,128]{2,1,0:T(8,128)(2,1)S(1)} %get-tuple-element.34.refs_0_.refs_6_), channel_id=1, source_target_pairs={{0,2},{1,3},{2,0},{3,1},{4,6},{5,7},{6,4},{7,5},{8,10},{9,11},{10,... | collective-permute-start | bytes 1572872 | tf_op jit(solution)/shard_map/ppermute | solution.py:195
  5.2 25.0 %collective-permute-start.1 = (bf16[32,64,128]{2,1,0:T(8,128)(2,1)S(1)}, bf16[32,64,128]{2,1,0:T(8,128)(2,1)S(1)}, u32[]{:S(2)}, u32[]{:S(2)}) collective-permute-start(bf16[32,64,128]{2,1,0:T(8,128)(2,1)S(1)} %get-tuple-element.34.refs_0_.refs_6_), channel_id=1, source_target_pairs={{0,4},{1,5},{2,6},{3,7},{4,0},{5,1},{6,2},{7,3},{8,12},{9,13},{10,... | collective-permute-start | bytes 1572872 | tf_op jit(solution)/shard_map/ppermute | solution.py:195
  6.7 24.0 %collective-permute-start.2 = (bf16[32,64,128]{2,1,0:T(8,128)(2,1)S(1)}, bf16[32,64,128]{2,1,0:T(8,128)(2,1)S(1)}, u32[]{:S(2)}, u32[]{:S(2)}) collective-permute-start(bf16[32,64,128]{2,1,0:T(8,128)(2,1)S(1)} %get-tuple-element.34.refs_0_.refs_6_), channel_id=1, source_target_pairs={{0,6},{1,7},{2,4},{3,5},{4,2},{5,3},{6,0},{7,1},{8,14},{9,15},{10,... | collective-permute-start | bytes 1572872 | tf_op jit(solution)/shard_map/ppermute | solution.py:195
  6.7 24.0 %collective-permute-start.3 = (bf16[32,64,128]{2,1,0:T(8,128)(2,1)S(1)}, bf16[32,64,128]{2,1,0:T(8,128)(2,1)S(1)}, u32[]{:S(2)}, u32[]{:S(2)}) collective-permute-start(bf16[32,64,128]{2,1,0:T(8,128)(2,1)S(1)} %get-tuple-element.34.refs_0_.refs_6_), channel_id=1, source_target_pairs={{0,1},{1,0},{2,3},{3,2},{4,5},{5,4},{6,7},{7,6},{8,9},{9,8},{10,11... | collective-permute-start | bytes 1572872 | tf_op jit(solution)/shard_map/ppermute | solution.py:195
  6.7 33.7 %collective-permute-start.14 = (bf16[32,64,128]{2,1,0:T(8,128)(2,1)S(1)}, bf16[32,64,128]{2,1,0:T(8,128)(2,1)S(1)}, u32[]{:S(2)}, u32[]{:S(2)}) collective-permute-start(bf16[32,64,128]{2,1,0:T(8,128)(2,1)S(1)} %get-tuple-element.33.refs_0_.refs_6_), channel_id=1, source_target_pairs={{0,2},{1,3},{2,0},{3,1},{4,6},{5,7},{6,4},{7,5},{8,10},{9,11},{10,... | collective-permute-start | bytes 1572872 | tf_op jit(solution)/shard_map/ppermute | solution.py:195
  17.9 34.3 %collective-permute-start.15 = (bf16[32,64,128]{2,1,0:T(8,128)(2,1)S(1)}, bf16[32,64,128]{2,1,0:T(8,128)(2,1)S(1)}, u32[]{:S(2)}, u32[]{:S(2)}) collective-permute-start(bf16[32,64,128]{2,1,0:T(8,128)(2,1)S(1)} %get-tuple-element.33.refs_0_.refs_6_), channel_id=1, source_target_pairs={{0,4},{1,5},{2,6},{3,7},{4,0},{5,1},{6,2},{7,3},{8,12},{9,13},{10,... | collective-permute-start | bytes 1572872 | tf_op jit(solution)/shard_map/ppermute | solution.py:195
  30.2 22.1 %collective-permute-start.16 = (bf16[32,64,128]{2,1,0:T(8,128)(2,1)S(1)}, bf16[32,64,128]{2,1,0:T(8,128)(2,1)S(1)}, u32[]{:S(2)}, u32[]{:S(2)}) collective-permute-start(bf16[32,64,128]{2,1,0:T(8,128)(2,1)S(1)} %get-tuple-element.33.refs_0_.refs_6_), channel_id=1, source_target_pairs={{0,6},{1,7},{2,4},{3,5},{4,2},{5,3},{6,0},{7,1},{8,14},{9,15},{10,... | collective-permute-start | bytes 1572872 | tf_op jit(solution)/shard_map/ppermute | solution.py:195
  30.7 22.1 %collective-permute-start.4 = (bf16[32,64,128]{2,1,0:T(8,128)(2,1)S(1)}, bf16[32,64,128]{2,1,0:T(8,128)(2,1)S(1)}, u32[]{:S(2)}, u32[]{:S(2)}) collective-permute-start(bf16[32,64,128]{2,1,0:T(8,128)(2,1)S(1)} %collective-permute-done.refs_1_.refs_7_), channel_id=1, source_target_pairs={{0,1},{1,0},{2,3},{3,2},{4,5},{5,4},{6,7},{7,6},{8,9},{9,8},{10,11... | collective-permute-start | bytes 1572872 | tf_op jit(solution)/shard_map/ppermute | solution.py:195
  30.7 45.0 %copy-start.3 = (bf16[32,64,128]{2,1,0:T(8,128)(2,1)}, bf16[32,64,128]{2,1,0:T(8,128)(2,1)S(1)}, u32[]{:S(2)}) copy-start(bf16[32,64,128]{2,1,0:T(8,128)(2,1)S(1)} %collective-permute-done.3.refs_4_.refs_10_) | copy-start | bytes 1572868
  30.7 22.1 %collective-permute-start.5 = (bf16[32,64,128]{2,1,0:T(8,128)(2,1)S(1)}, bf16[32,64,128]{2,1,0:T(8,128)(2,1)S(1)}, u32[]{:S(2)}, u32[]{:S(2)}) collective-permute-start(bf16[32,64,128]{2,1,0:T(8,128)(2,1)S(1)} %collective-permute-done.1.refs_2_.refs_8_), channel_id=1, source_target_pairs={{0,1},{1,0},{2,3},{3,2},{4,5},{5,4},{6,7},{7,6},{8,9},{9,8},{10,11... | collective-permute-start | bytes 1572872 | tf_op jit(solution)/shard_map/ppermute | solution.py:195
  40.4 29.8 %collective-permute-start.6 = (bf16[32,64,128]{2,1,0:T(8,128)(2,1)S(1)}, bf16[32,64,128]{2,1,0:T(8,128)(2,1)S(1)}, u32[]{:S(2)}, u32[]{:S(2)}) collective-permute-start(bf16[32,64,128]{2,1,0:T(8,128)(2,1)S(1)} %collective-permute-done.2.refs_3_.refs_9_), channel_id=1, source_target_pairs={{0,1},{1,0},{2,3},{3,2},{4,5},{5,4},{6,7},{7,6},{8,9},{9,8},{10,11... | collective-permute-start | bytes 1572872 | tf_op jit(solution)/shard_map/ppermute | solution.py:195
  52.3 27.0 %collective-permute-start.17 = (bf16[32,64,128]{2,1,0:T(8,128)(2,1)S(1)}, bf16[32,64,128]{2,1,0:T(8,128)(2,1)S(1)}, u32[]{:S(2)}, u32[]{:S(2)}) collective-permute-start(bf16[32,64,128]{2,1,0:T(8,128)(2,1)S(1)} %get-tuple-element.33.refs_0_.refs_6_), channel_id=1, source_target_pairs={{0,1},{1,0},{2,3},{3,2},{4,5},{5,4},{6,7},{7,6},{8,9},{9,8},{10,11... | collective-permute-start | bytes 1572872 | tf_op jit(solution)/shard_map/ppermute | solution.py:195
  52.3 44.6 %collective-permute-start.18 = (bf16[32,64,128]{2,1,0:T(8,128)(2,1)S(1)}, bf16[32,64,128]{2,1,0:T(8,128)(2,1)S(1)}, u32[]{:S(2)}, u32[]{:S(2)}) collective-permute-start(bf16[32,64,128]{2,1,0:T(8,128)(2,1)S(1)} %collective-permute-done.14.refs_1_.refs_7_), channel_id=1, source_target_pairs={{0,1},{1,0},{2,3},{3,2},{4,5},{5,4},{6,7},{7,6},{8,9},{9,8},{10,11... | collective-permute-start | bytes 1572872 | tf_op jit(solution)/shard_map/ppermute | solution.py:195
  52.8 22.9 %copy-start.4 = (bf16[32,64,128]{2,1,0:T(8,128)(2,1)}, bf16[32,64,128]{2,1,0:T(8,128)(2,1)S(1)}, u32[]{:S(2)}) copy-start(bf16[32,64,128]{2,1,0:T(8,128)(2,1)S(1)} %collective-permute-done.4.refs_5_.refs_11_) | copy-start | bytes 1572868
  52.8 45.4 %collective-permute-start.19 = (bf16[32,64,128]{2,1,0:T(8,128)(2,1)S(1)}, bf16[32,64,128]{2,1,0:T(8,128)(2,1)S(1)}, u32[]{:S(2)}, u32[]{:S(2)}) collective-permute-start(bf16[32,64,128]{2,1,0:T(8,128)(2,1)S(1)} %collective-permute-done.15.refs_2_.refs_8_), channel_id=1, source_target_pairs={{0,1},{1,0},{2,3},{3,2},{4,5},{5,4},{6,7},{7,6},{8,9},{9,8},{10,11... | collective-permute-start | bytes 1572872 | tf_op jit(solution)/shard_map/ppermute | solution.py:195
  52.9 17.4 %copy-start.11 = (bf16[32,64,128]{2,1,0:T(8,128)(2,1)}, bf16[32,64,128]{2,1,0:T(8,128)(2,1)S(1)}, u32[]{:S(2)}) copy-start(bf16[32,64,128]{2,1,0:T(8,128)(2,1)S(1)} %collective-permute-done.5.refs_6_.refs_12_) | copy-start | bytes 1572868
  52.9 45.3 %collective-permute-start.20 = (bf16[32,64,128]{2,1,0:T(8,128)(2,1)S(1)}, bf16[32,64,128]{2,1,0:T(8,128)(2,1)S(1)}, u32[]{:S(2)}, u32[]{:S(2)}) collective-permute-start(bf16[32,64,128]{2,1,0:T(8,128)(2,1)S(1)} %collective-permute-done.16.refs_3_.refs_9_), channel_id=1, source_target_pairs={{0,1},{1,0},{2,3},{3,2},{4,5},{5,4},{6,7},{7,6},{8,9},{9,8},{10,11... | collective-permute-start | bytes 1572872 | tf_op jit(solution)/shard_map/ppermute | solution.py:195
  75.7 32.3 %collective-permute-start.7 = (bf16[32,64,128]{2,1,0:T(8,128)(2,1)S(1)}, bf16[32,64,128]{2,1,0:T(8,128)(2,1)S(1)}, u32[]{:S(2)}, u32[]{:S(2)}) collective-permute-start(bf16[32,64,128]{2,1,0:T(8,128)(2,1)S(1)} %get-tuple-element.21), channel_id=1, source_target_pairs={{0,8},{1,9},{2,10},{3,11},{4,12},{5,13},{6,14},{7,15}} | collective-permute-start | bytes 1572872 | tf_op jit(solution)/shard_map/ppermute | solution.py:344
  79.2 24.6 %copy-start.5 = (bf16[32,64,128]{2,1,0:T(8,128)(2,1)}, bf16[32,64,128]{2,1,0:T(8,128)(2,1)S(1)}, u32[]{:S(2)}) copy-start(bf16[32,64,128]{2,1,0:T(8,128)(2,1)S(1)} %collective-permute-done.17.refs_4_.refs_10_) | copy-start | bytes 1572868
  79.2 30.1 %collective-permute-start.32 = (bf16[32,64,128]{2,1,0:T(8,128)(2,1)S(1)}, bf16[32,64,128]{2,1,0:T(8,128)(2,1)S(1)}, u32[]{:S(2)}, u32[]{:S(2)}) collective-permute-start(bf16[32,64,128]{2,1,0:T(8,128)(2,1)S(1)} %get-tuple-element.29), channel_id=1, source_target_pairs={{24,16},{25,17},{26,18},{27,19},{28,20},{29,21},{30,22},{31,23}} | collective-permute-start | bytes 1572872 | tf_op jit(solution)/shard_map/ppermute | solution.py:345
  96.8 17.4 %collective-permute-start.8 = (bf16[32,64,128]{2,1,0:T(8,128)(2,1)S(1)}, bf16[32,64,128]{2,1,0:T(8,128)(2,1)S(1)}, u32[]{:S(2)}, u32[]{:S(2)}) collective-permute-start(bf16[32,64,128]{2,1,0:T(8,128)(2,1)S(1)} %get-tuple-element.22.own), channel_id=1, source_target_pairs={{0,8},{8,16},{16,24},{1,9},{9,17},{17,25},{2,10},{10,18},{18,26},{... | collective-permute-start | bytes 1572872 | tf_op jit(solution)/shard_map/ppermute | solution.py:327
  103.9 17.8 %collective-permute-start.21 = (bf16[32,64,128]{2,1,0:T(8,128)(2,1)S(1)}, bf16[32,64,128]{2,1,0:T(8,128)(2,1)S(1)}, u32[]{:S(2)}, u32[]{:S(2)}) collective-permute-start(bf16[32,64,128]{2,1,0:T(8,128)(2,1)S(1)} %get-tuple-element.25), channel_id=1, source_target_pairs={{0,8},{1,9},{2,10},{3,11},{4,12},{5,13},{6,14},{7,15}} | collective-permute-start | bytes 1572872 | tf_op jit(solution)/shard_map/ppermute | solution.py:344
  107.3 15.0 %collective-permute-start.35 = (bf16[32,64,128]{2,1,0:T(8,128)(2,1)S(1)}, bf16[32,64,128]{2,1,0:T(8,128)(2,1)S(1)}, u32[]{:S(2)}, u32[]{:S(2)}) collective-permute-start(bf16[32,64,128]{2,1,0:T(8,128)(2,1)S(1)} %get-tuple-element.31), channel_id=1, source_target_pairs={{24,16},{25,17},{26,18},{27,19},{28,20},{29,21},{30,22},{31,23}} | collective-permute-start | bytes 1572872 | tf_op jit(solution)/shard_map/ppermute | solution.py:345
  108.0 19.7 %collective-permute-start.11 = (bf16[32,64,128]{2,1,0:T(8,128)(2,1)S(1)}, bf16[32,64,128]{2,1,0:T(8,128)(2,1)S(1)}, u32[]{:S(2)}, u32[]{:S(2)}) collective-permute-start(bf16[32,64,128]{2,1,0:T(8,128)(2,1)S(1)} %get-tuple-element.22.own), channel_id=1, source_target_pairs={{8,0},{16,8},{24,16},{9,1},{17,9},{25,17},{10,2},{18,10},{26,18},{... | collective-permute-start | bytes 1572872 | tf_op jit(solution)/shard_map/ppermute | solution.py:328
  109.3 23.6 %collective-permute-start.22 = (bf16[32,64,128]{2,1,0:T(8,128)(2,1)S(1)}, bf16[32,64,128]{2,1,0:T(8,128)(2,1)S(1)}, u32[]{:S(2)}, u32[]{:S(2)}) collective-permute-start(bf16[32,64,128]{2,1,0:T(8,128)(2,1)S(1)} %get-tuple-element.26.own), channel_id=1, source_target_pairs={{0,8},{8,16},{16,24},{1,9},{9,17},{17,25},{2,10},{10,18},{18,26},{... | collective-permute-start | bytes 1572872 | tf_op jit(solution)/shard_map/ppermute | solution.py:327
  114.3 20.2 %collective-permute-start.25 = (bf16[32,64,128]{2,1,0:T(8,128)(2,1)S(1)}, bf16[32,64,128]{2,1,0:T(8,128)(2,1)S(1)}, u32[]{:S(2)}, u32[]{:S(2)}) collective-permute-start(bf16[32,64,128]{2,1,0:T(8,128)(2,1)S(1)} %get-tuple-element.26.own), channel_id=1, source_target_pairs={{8,0},{16,8},{24,16},{9,1},{17,9},{25,17},{10,2},{18,10},{26,18},{... | collective-permute-start | bytes 1572872 | tf_op jit(solution)/shard_map/ppermute | solution.py:328
  121.7 13.5 %collective-permute-start.9 = (bf16[32,64,128]{2,1,0:T(8,128)(2,1)S(1)}, bf16[32,64,128]{2,1,0:T(8,128)(2,1)S(1)}, u32[]{:S(2)}, u32[]{:S(2)}) collective-permute-start(bf16[32,64,128]{2,1,0:T(8,128)(2,1)S(1)} %collective-permute-done.8.refs_0_), channel_id=1, source_target_pairs={{8,16},{16,24},{9,17},{17,25},{10,18},{18,26},{11,19},{19,27},{12,... | collective-permute-start | bytes 1572872 | tf_op jit(solution)/shard_map/ppermute | solution.py:327
  122.4 21.8 %collective-permute-start.28 = (bf16[32,64,128]{2,1,0:T(8,128)(2,1)S(1)}, bf16[32,64,128]{2,1,0:T(8,128)(2,1)S(1)}, u32[]{:S(2)}, u32[]{:S(2)}) collective-permute-start(bf16[32,64,128]{2,1,0:T(8,128)(2,1)S(1)} %get-tuple-element.38), channel_id=1, source_target_pairs={{0,8},{8,16},{1,9},{9,17},{2,10},{10,18},{3,11},{11,19},{4,12},{12... | collective-permute-start | bytes 1572872 | tf_op jit(solution)/shard_map/ppermute | solution.py:344
  127.7 26.8 %collective-permute-start.30 = (bf16[32,64,128]{2,1,0:T(8,128)(2,1)S(1)}, bf16[32,64,128]{2,1,0:T(8,128)(2,1)S(1)}, u32[]{:S(2)}, u32[]{:S(2)}) collective-permute-start(bf16[32,64,128]{2,1,0:T(8,128)(2,1)S(1)} %get-tuple-element.36), channel_id=1, source_target_pairs={{0,8},{8,16},{1,9},{9,17},{2,10},{10,18},{3,11},{11,19},{4,12},{12... | collective-permute-start | bytes 1572872 | tf_op jit(solution)/shard_map/ppermute | solution.py:344
  132.9 22.5 %collective-permute-start.12 = (bf16[32,64,128]{2,1,0:T(8,128)(2,1)S(1)}, bf16[32,64,128]{2,1,0:T(8,128)(2,1)S(1)}, u32[]{:S(2)}, u32[]{:S(2)}) collective-permute-start(bf16[32,64,128]{2,1,0:T(8,128)(2,1)S(1)} %collective-permute-done.11.refs_3_), channel_id=1, source_target_pairs={{8,0},{16,8},{9,1},{17,9},{10,2},{18,10},{11,3},{19,11},{12,4},{20... | collective-permute-start | bytes 1572872 | tf_op jit(solution)/shard_map/ppermute | solution.py:328
  134.5 21.6 %collective-permute-start.23 = (bf16[32,64,128]{2,1,0:T(8,128)(2,1)S(1)}, bf16[32,64,128]{2,1,0:T(8,128)(2,1)S(1)}, u32[]{:S(2)}, u32[]{:S(2)}) collective-permute-start(bf16[32,64,128]{2,1,0:T(8,128)(2,1)S(1)} %collective-permute-done.22.refs_0_), channel_id=1, source_target_pairs={{8,16},{16,24},{9,17},{17,25},{10,18},{18,26},{11,19},{19,27},{12,... | collective-permute-start | bytes 1572872 | tf_op jit(solution)/shard_map/ppermute | solution.py:327
  135.2 25.5 %collective-permute-start.26 = (bf16[32,64,128]{2,1,0:T(8,128)(2,1)S(1)}, bf16[32,64,128]{2,1,0:T(8,128)(2,1)S(1)}, u32[]{:S(2)}, u32[]{:S(2)}) collective-permute-start(bf16[32,64,128]{2,1,0:T(8,128)(2,1)S(1)} %collective-permute-done.25.refs_3_), channel_id=1, source_target_pairs={{8,0},{16,8},{9,1},{17,9},{10,2},{18,10},{11,3},{19,11},{12,4},{20... | collective-permute-start | bytes 1572872 | tf_op jit(solution)/shard_map/ppermute | solution.py:328
  144.1 17.3 %collective-permute-start.33 = (bf16[32,64,128]{2,1,0:T(8,128)(2,1)S(1)}, bf16[32,64,128]{2,1,0:T(8,128)(2,1)S(1)}, u32[]{:S(2)}, u32[]{:S(2)}) collective-permute-start(bf16[32,64,128]{2,1,0:T(8,128)(2,1)S(1)} %get-tuple-element.37), channel_id=1, source_target_pairs={{16,8},{24,16},{17,9},{25,17},{18,10},{26,18},{19,11},{27,19},{20,... | collective-permute-start | bytes 1572872 | tf_op jit(solution)/shard_map/ppermute | solution.py:345
  154.5 9.2 %collective-permute-start.36 = (bf16[32,64,128]{2,1,0:T(8,128)(2,1)S(1)}, bf16[32,64,128]{2,1,0:T(8,128)(2,1)S(1)}, u32[]{:S(2)}, u32[]{:S(2)}) collective-permute-start(bf16[32,64,128]{2,1,0:T(8,128)(2,1)S(1)} %get-tuple-element.35), channel_id=1, source_target_pairs={{16,8},{24,16},{17,9},{25,17},{18,10},{26,18},{19,11},{27,19},{20,... | collective-permute-start | bytes 1572872 | tf_op jit(solution)/shard_map/ppermute | solution.py:345
  155.4 32.5 %collective-permute-start.10 = (bf16[32,64,128]{2,1,0:T(8,128)(2,1)S(1)}, bf16[32,64,128]{2,1,0:T(8,128)(2,1)S(1)}, u32[]{:S(2)}, u32[]{:S(2)}) collective-permute-start(bf16[32,64,128]{2,1,0:T(8,128)(2,1)S(1)} %collective-permute-done.9.refs_1_), channel_id=1, source_target_pairs={{16,24},{17,25},{18,26},{19,27},{20,28},{21,29},{22,30},{23,31}} | collective-permute-start | bytes 1572872 | tf_op jit(solution)/shard_map/ppermute | solution.py:327
  156.1 33.7 %collective-permute-start.13 = (bf16[32,64,128]{2,1,0:T(8,128)(2,1)S(1)}, bf16[32,64,128]{2,1,0:T(8,128)(2,1)S(1)}, u32[]{:S(2)}, u32[]{:S(2)}) collective-permute-start(bf16[32,64,128]{2,1,0:T(8,128)(2,1)S(1)} %collective-permute-done.12.refs_4_), channel_id=1, source_target_pairs={{8,0},{9,1},{10,2},{11,3},{12,4},{13,5},{14,6},{15,7}} | collective-permute-start | bytes 1572872 | tf_op jit(solution)/shard_map/ppermute | solution.py:328
  160.7 30.4 %collective-permute-start.24 = (bf16[32,64,128]{2,1,0:T(8,128)(2,1)S(1)}, bf16[32,64,128]{2,1,0:T(8,128)(2,1)S(1)}, u32[]{:S(2)}, u32[]{:S(2)}) collective-permute-start(bf16[32,64,128]{2,1,0:T(8,128)(2,1)S(1)} %collective-permute-done.23.refs_1_), channel_id=1, source_target_pairs={{16,24},{17,25},{18,26},{19,27},{20,28},{21,29},{22,30},{23,31}} | collective-permute-start | bytes 1572872 | tf_op jit(solution)/shard_map/ppermute | solution.py:327
  161.4 35.2 %collective-permute-start.27 = (bf16[32,64,128]{2,1,0:T(8,128)(2,1)S(1)}, bf16[32,64,128]{2,1,0:T(8,128)(2,1)S(1)}, u32[]{:S(2)}, u32[]{:S(2)}) collective-permute-start(bf16[32,64,128]{2,1,0:T(8,128)(2,1)S(1)} %collective-permute-done.26.refs_4_), channel_id=1, source_target_pairs={{8,0},{9,1},{10,2},{11,3},{12,4},{13,5},{14,6},{15,7}} | collective-permute-start | bytes 1572872 | tf_op jit(solution)/shard_map/ppermute | solution.py:328
  163.7 37.1 %collective-permute-start.29 = (bf16[32,64,128]{2,1,0:T(8,128)(2,1)S(1)}, bf16[32,64,128]{2,1,0:T(8,128)(2,1)S(1)}, u32[]{:S(2)}, u32[]{:S(2)}) collective-permute-start(bf16[32,64,128]{2,1,0:T(8,128)(2,1)S(1)} %add_convert_fusion.3), channel_id=1, source_target_pairs={{0,8},{8,16},{16,24},{1,9},{9,17},{17,25},{2,10},{10,18},{18,26},{... | collective-permute-start | bytes 1572872 | tf_op jit(solution)/shard_map/ppermute | solution.py:344
  187.9 18.9 %collective-permute-start.31 = (bf16[32,64,128]{2,1,0:T(8,128)(2,1)S(1)}, bf16[32,64,128]{2,1,0:T(8,128)(2,1)S(1)}, u32[]{:S(2)}, u32[]{:S(2)}) collective-permute-start(bf16[32,64,128]{2,1,0:T(8,128)(2,1)S(1)} %add_convert_fusion.2), channel_id=1, source_target_pairs={{0,8},{8,16},{16,24},{1,9},{9,17},{17,25},{2,10},{10,18},{18,26},{... | collective-permute-start | bytes 1572872 | tf_op jit(solution)/shard_map/ppermute | solution.py:344
  189.8 17.0 %collective-permute-start.34 = (bf16[32,64,128]{2,1,0:T(8,128)(2,1)}, bf16[32,64,128]{2,1,0:T(8,128)(2,1)S(1)}, u32[]{:S(2)}, u32[]{:S(2)}) collective-permute-start(bf16[32,64,128]{2,1,0:T(8,128)(2,1)} %add_convert_fusion.1), channel_id=1, source_target_pairs={{8,0},{16,8},{24,16},{9,1},{17,9},{25,17},{10,2},{18,10},{26,18},{... | collective-permute-start | bytes 1572872 | tf_op jit(solution)/shard_map/ppermute | solution.py:345
  191.1 24.0 %collective-permute-start.37 = (bf16[32,64,128]{2,1,0:T(8,128)(2,1)}, bf16[32,64,128]{2,1,0:T(8,128)(2,1)S(1)}, u32[]{:S(2)}, u32[]{:S(2)}) collective-permute-start(bf16[32,64,128]{2,1,0:T(8,128)(2,1)} %add_convert_fusion), channel_id=1, source_target_pairs={{8,0},{16,8},{24,16},{9,1},{17,9},{25,17},{10,2},{18,10},{26,18},{... | collective-permute-start | bytes 1572872 | tf_op jit(solution)/shard_map/ppermute | solution.py:345
  196.6 18.5 %copy-start.1 = (f32[32,64,128]{2,1,0:T(8,128)S(1)}, f32[32,64,128]{2,1,0:T(8,128)}, u32[]{:S(2)}) copy-start(f32[32,64,128]{2,1,0:T(8,128)} %left_products.2.refs_0_) | copy-start | bytes 3145732
  (5 other events, 10.8 us)

commit v3 on v2

--- a/solution.py
+++ b/solution.py
@@ -31,44 +31,43 @@
     return mask_ref[(row * rows) // BLK, (col * cols) // BLK].astype(jnp.float32)
 
 
-def spread(pair_ref, wide):
-    rows, keys, chans = pair_ref.shape
-    wide[...] = pair_ref[...].astype(jnp.float32).reshape(rows * keys, chans)
-
-
-def normalize(wide, eye, key, keys, rows):
-    cells = wide[pl.ds(key, rows, stride=keys), :].astype(jnp.bfloat16)
-    values = lax.dot_general(eye, cells, BY_LAST, preferred_element_type=jnp.float32)
-    centred = values - jnp.mean(values, axis=0, keepdims=True)
-    inverse = lax.rsqrt(jnp.mean(centred * centred, axis=0, keepdims=True) + 1e-05)
+def turn(pair, flipped, turned):
+    flipped[...] = jnp.transpose(pair[...], (1, 0, 2))
+    eye = identity(pair.shape[2])
+    for key in range(pair.shape[1]):
+        turned[key] = lax.dot_general(eye, flipped[key], BY_LAST, preferred_element_type=jnp.float32)
+
+
+def normalize(values):
+    centred = values - jnp.mean(values, axis=1, keepdims=True)
+    inverse = lax.rsqrt(jnp.mean(centred * centred, axis=1, keepdims=True) + 1e-05)
     return centred * inverse, inverse
 
 
+def set_columns(gain, bias, weight, gain_col, bias_col, weight_t):
+    @pl.when(pl.program_id(0) == 0)
+    def _():
+        gain_col[...] = column(gain, gain_col.shape[1])
+        bias_col[...] = column(bias, bias_col.shape[1])
+        weight_t[...] = weight[...].astype(jnp.float32).T.astype(jnp.bfloat16)
+
+
 def front_kernel(mask, pair, gain, bias, weight, *refs):
-    outs, (wide, flat, gain_col, bias_col, weight_t) = refs[:CHUNKS], refs[CHUNKS:]
-    rows, keys, chans = pair.shape
+    outs, (flipped, turned, normed, acts, gain_col, bias_col, weight_t) = refs[:CHUNKS], refs[CHUNKS:]
+    rows, keys, _ = pair.shape
     hidden = weight.shape[1] // 2
     part = hidden // CHUNKS
-
-    @pl.when(pl.program_id(0) == 0)
-    def _():
-        gain_col[...] = column(gain, rows)
-        bias_col[...] = column(bias, rows)
-        weight_t[...] = weight[...].astype(jnp.float32).T.astype(jnp.bfloat16)
-
-    cols = pl.num_programs(0) * keys
-    valid = unit_mask(mask, rows, cols)
-    eye = identity(chans)
-    spread(pair, wide)
+    set_columns(gain, bias, weight, gain_col, bias_col, weight_t)
+    valid = unit_mask(mask, rows, pl.num_programs(0) * keys)
+    turn(pair, flipped, turned)
+    scaled, _ = normalize(turned[...])
+    normed[...] = (scaled * gain_col[...] + bias_col[...]).astype(jnp.bfloat16)
     for key in range(keys):
-        scaled, _ = normalize(wide, eye, key, keys, rows)
-        normed = (scaled * gain_col[...] + bias_col[...]).astype(jnp.bfloat16)
-        projected = jnp.dot(weight_t[...], normed, preferred_element_type=jnp.float32)
-        flat[pl.ds(key, hidden, stride=keys), :] = valid * jax.nn.sigmoid(projected[hidden:]) * projected[:hidden]
+        projected = jnp.dot(weight_t[...], normed[key], preferred_element_type=jnp.float32)
+        acts[key] = (valid * jax.nn.sigmoid(projected[hidden:]) * projected[:hidden]).astype(jnp.bfloat16)
+    whole = jnp.transpose(acts[...], (1, 0, 2))
     for chunk in range(CHUNKS):
-        outs[chunk][...] = (
-            flat[chunk * part * keys : (chunk + 1) * part * keys, :].reshape(part, keys, rows).astype(jnp.bfloat16)
-        )
+        outs[chunk][...] = whole[chunk * part : (chunk + 1) * part]
 
 
 def front(pair, gain, bias, proj_weight, tile_mask, side):
@@ -89,8 +88,10 @@
         ],
         out_specs=[pl.BlockSpec((part, KEYS, rows), lambda g: (0, g, 0))] * CHUNKS,
         scratch_shapes=[
-            pltpu.VMEM((rows * KEYS, chans), jnp.float32),
-            pltpu.VMEM((width // 2 * KEYS, rows), jnp.float32),
+            pltpu.VMEM((KEYS, rows, chans), jnp.bfloat16),
+            pltpu.VMEM((KEYS, chans, rows), jnp.float32),
+            pltpu.VMEM((KEYS, chans, rows), jnp.bfloat16),
+            pltpu.VMEM((KEYS, width // 2, rows), jnp.bfloat16),
             pltpu.VMEM((chans, rows), jnp.float32),
             pltpu.VMEM((chans, rows), jnp.float32),
             pltpu.VMEM((width, chans), jnp.bfloat16),
@@ -106,48 +107,45 @@
 def tail_kernel(mask, pair, gain, bias, weight, *refs):
     lefts, refs = refs[:CHUNKS], refs[CHUNKS:]
     rights, refs = refs[: 3 * CHUNKS], refs[3 * CHUNKS :]
-    out, wide, right_flat, left_flat, gain_col, bias_col, weight_t = refs
-    rows, keys, chans = pair.shape
+    out, flipped, turned, normed, inverses, grads, right_flat, left_flat, gain_col, bias_col, weight_t = refs
+    rows, keys, _ = pair.shape
     hidden = weight.shape[1] // 4
     part = hidden // CHUNKS
-
-    @pl.when(pl.program_id(0) == 0)
-    def _():
-        gain_col[...] = column(gain, rows)
-        bias_col[...] = column(bias, rows)
-        weight_t[...] = weight[...].astype(jnp.float32).T.astype(jnp.bfloat16)
-
-    cols = pl.num_programs(0) * keys
-    valid = unit_mask(mask, rows, cols)
-    eye = identity(chans)
-    row_eye = eye if rows == chans else identity(rows)
-    spread(pair, wide)
+    set_columns(gain, bias, weight, gain_col, bias_col, weight_t)
+    valid = unit_mask(mask, rows, pl.num_programs(0) * keys)
     for chunk in range(CHUNKS):
         own, up, down = (rights[i * CHUNKS + chunk][...].astype(jnp.float32) for i in range(3))
         place = slice(chunk * part * keys, (chunk + 1) * part * keys)
         right_flat[place, :] = (own + up + down).reshape(part * keys, rows)
         left_flat[place, :] = lefts[chunk][...].reshape(part * keys, rows)
+    turn(pair, flipped, turned)
+    scaled, inverse = normalize(turned[...])
+    turned[...] = scaled
+    inverses[...] = inverse
+    normed[...] = (scaled * gain_col[...] + bias_col[...]).astype(jnp.bfloat16)
     for key in range(keys):
-        scaled, inverse = normalize(wide, eye, key, keys, rows)
-        normed = (scaled * gain_col[...] + bias_col[...]).astype(jnp.bfloat16)
-        projected = jnp.dot(weight_t[...], normed, preferred_element_type=jnp.float32)
-        grads = []
+        projected = jnp.dot(weight_t[...], normed[key], preferred_element_type=jnp.float32)
         for side, source in enumerate((left_flat, right_flat)):
             lin = projected[2 * side * hidden : (2 * side + 1) * hidden]
             sig = jax.nn.sigmoid(projected[(2 * side + 1) * hidden : (2 * side + 2) * hidden])
             through = source[pl.ds(key, hidden, stride=keys), :] * valid * sig
-            grads += [through.astype(jnp.bfloat16), (through * lin * (1.0 - sig)).astype(jnp.bfloat16)]
-        grad_normed = jnp.dot(weight[...], jnp.concatenate(grads, axis=0), preferred_element_type=jnp.float32)
-        scaled_grad = grad_normed * gain_col[...]
-        result = inverse * (
+            grads[key, 2 * side * hidden : (2 * side + 1) * hidden, :] = through.astype(jnp.bfloat16)
+            grads[key, (2 * side + 1) * hidden : (2 * side + 2) * hidden, :] = (through * lin * (1.0 - sig)).astype(
+                jnp.bfloat16
+            )
+    for key in range(keys):
+        scaled = turned[key]
+        scaled_grad = jnp.dot(weight[...], grads[key], preferred_element_type=jnp.float32) * gain_col[...]
+        result = inverses[key] * (
             scaled_grad
             - jnp.mean(scaled_grad, axis=0, keepdims=True)
             - scaled * jnp.mean(scaled_grad * scaled, axis=0, keepdims=True)
         )
-        wide[pl.ds(key, rows, stride=keys), :] = lax.dot_general(
-            row_eye, result.astype(jnp.bfloat16), BY_LAST, preferred_element_type=jnp.float32
-        )
-    out[...] = wide[...].reshape(rows, keys, chans).astype(jnp.bfloat16)
+        normed[key] = result.astype(jnp.bfloat16)
+    eye = identity(rows)
+    for key in range(keys):
+        flipped[key] = lax.dot_general(eye, normed[key], BY_LAST, preferred_element_type=jnp.float32).astype(jnp.bfloat16)
+    out[...] = jnp.transpose(flipped[...], (1, 0, 2))
 
 
 def tail(pair, gain, bias, proj_weight, tile_mask, lefts, rights):
@@ -171,7 +169,11 @@
         + [small] * (4 * CHUNKS),
         out_specs=cells,
         scratch_shapes=[
-            pltpu.VMEM((rows * KEYS, chans), jnp.float32),
+            pltpu.VMEM((KEYS, rows, chans), jnp.bfloat16),
+            pltpu.VMEM((KEYS, chans, rows), jnp.float32),
+            pltpu.VMEM((KEYS, chans, rows), jnp.bfloat16),
+            pltpu.VMEM((KEYS, 1, rows), jnp.float32),
+            pltpu.VMEM((KEYS, width, rows), jnp.bfloat16),
             pltpu.VMEM((width // 4 * KEYS, rows), jnp.float32),
             pltpu.VMEM((width // 4 * KEYS, rows), jnp.float32),
             pltpu.VMEM((chans, rows), jnp.float32),
@@ -190,12 +192,12 @@
     return [m for m in range(0, n_col, 2)] + [m for m in range(1, n_col, 2)]
 
 
+def exchange(value, mask, n_col):
+    return lax.ppermute(value, "col", [(d, d ^ mask) for d in range(n_col)])
+
+
 def gather_columns(block, n_col):
-    def exchange(value, mask):
-        return lax.ppermute(value, "col", [(d, d ^ mask) for d in range(n_col)])
-
-    same = [block] + [exchange(block, m) for m in range(2, n_col, 2)]
-    return same + [exchange(value, 1) for value in same]
+    return [block] + [exchange(block, m, n_col) for m in range(2, n_col, 2)]
 
 
 def load_panel(blocks, panel, sems, first, chans, masks):
@@ -213,7 +215,6 @@
 
 
 def fill_panel(blocks, panel, sems, masks):
-    steps = pl.num_programs(0)
     step = pl.program_id(0)
     total = panel.shape[0] // STEP
 
@@ -225,7 +226,6 @@
 
     for c in load_panel(blocks, panel, sems.at[step], pl.multiple_of(step * STEP, STEP), STEP, masks):
         c.wait()
-    del steps
 
 
 def partial_kernel(n, masks, left, *refs):
@@ -314,10 +314,13 @@
     gain, bias = norm_gain[None, :], norm_bias[None, :]
 
     grad_t = jnp.transpose(grad_x, (2, 1, 0))
-    blocks = [gather_columns(grad_t[chunk * part : (chunk + 1) * part], n_col) for chunk in range(CHUNKS)]
-
+    same_core = [gather_columns(grad_t[chunk * part : (chunk + 1) * part], n_col) for chunk in range(CHUNKS)]
     owns = front(pair, gain, bias, proj_weight, tile_mask, 1)
     left_acts = front(pair, gain, bias, proj_weight, tile_mask, 0)
+    blocks = []
+    for same in same_core:
+        same, _, _ = lax.optimization_barrier((same, owns, left_acts))
+        blocks.append(same + [exchange(value, 1, n_col) for value in same])
 
     ups, downs = [], []
     for own in owns:
@@ -333,7 +336,8 @@
 
     partials, up_sums, down_sums, firsts = [], [], [], []
     for chunk in range(CHUNKS):
-        sums = partial_products(left_acts[chunk], blocks[chunk], n)
+        left_act, _ = lax.optimization_barrier((left_acts[chunk], (ups[chunk][0], downs[chunk][0])))
+        sums = partial_products(left_act, blocks[chunk], n)
         up = down = None
         for step in range(1, n):
             away = n - step

time: 247 us -> 190 us (0.77)
  Pallas kernels: 81.4 us -> 38.3 us
  waiting for transfers between devices: 85 us -> 67.5 us
    pallas_call x2, Pallas kernels: 33.7 us -> 9.44 us  [front(): pl.pallas_call(front_kernel, out_shape=[jax.ShapeDtypeStruct((part, cols,...]
    pallas_call x1, Pallas kernels: 30.1 us -> 11.3 us  [tail(): pl.pallas_call(tail_kernel, out_shape=jax.ShapeDtypeStruct(pair.shape, jn...]
    ppermute x14, waiting for transfers between devices: 40.5 us -> 22.5 us  [exchange(): return lax.ppermute(value, 'col', [(d, d ^ mask) for d in range(n_col)])]
    ppermute x6, waiting for transfers between devices: 3.66 us -> 12.1 us  [shards(): down = lax.ppermute(down, 'row', [(r, r - 1) for r in range(1, n - h + 1)])]
    ppermute x6, waiting for transfers between devices: 29.2 us -> 25.8 us  [shards(): up = lax.ppermute(up_sum, 'row', [(r, r + 1) for r in range(step)])]
    ppermute x6, waiting for transfers between devices: 3.27 us -> 0.02 us  [shards(): up = lax.ppermute(up, 'row', [(r, r + 1) for r in range(h - 1, n - 1)])]
  transfers between devices with their start and end apart: 38 -> 38, of which waited for: 12 -> 12; matrix products, arithmetic and copies ran while one was open for 1% -> 2% of each run, Pallas kernels for 21% -> 14%
where the time goes in v3:
time: 190 us; the launch traced here: 189 us
  starting transfers between devices  73.1 us (38%)
  waiting for transfers between devices  67.5 us (36%)
  Pallas kernels  38.3 us (20%)
  local copies, waits for them, and re-layouts  5.55 us (3%)
  other arithmetic  4.56 us (2%)
    ppermute x6, starting transfers between devices, shards(): up = lax.ppermute(up_sum, 'row', [(r, r + 1) for r in range(step)])  38.7 us
    ppermute x6, waiting for transfers between devices, shards(): up = lax.ppermute(up_sum, 'row', [(r, r + 1) for r in range(step)])  25.8 us
    ppermute x14, waiting for transfers between devices, exchange(): return lax.ppermute(value, 'col', [(d, d ^ mask) for d in range(n_col)])  22.5 us
    ppermute x6, waiting for transfers between devices, shards(): down = lax.ppermute(down, 'row', [(r, r - 1) for r in range(1, n - h + 1)])  12.1 us
    pallas_call x1, Pallas kernels, tail(): pl.pallas_call(tail_kernel, out_shape=jax.ShapeDtypeStruct(pair.shape, jn...  11.3 us
    ppermute x14, starting transfers between devices, exchange(): return lax.ppermute(value, 'col', [(d, d ^ mask) for d in range(n_col)])  11.1 us
    ppermute x6, starting transfers between devices, shards(): up = lax.ppermute(up, 'row', [(r, r + 1) for r in range(h - 1, n - 1)])  9.99 us
    pallas_call x2, Pallas kernels, front(): pl.pallas_call(front_kernel, out_shape=[jax.ShapeDtypeStruct((part, cols,...  9.44 us
  transfers between devices with their start and end apart: 38, of which 12 were waited for; matrix products, arithmetic and copies ran while one was open for 2% of the time, Pallas kernels for 14%

profile of v3, /device:TPU:0, one launch (start us, length us, event | category | flops | bytes accessed | tf_op | source)
XLA Modules:
  0.0 189.4 jit_solution(5485191911462186150)
XLA Ops:
  0.0 2.1 %copy.9 = bf16[128,64,64]{0,1,2:T(8,128)(2,1)S(1)} copy(bf16[128,64,64]{0,2,1:T(8,128)(2,1)} %param.7) | data formatting | bytes 2097152 | tf_op args[1]
  2.1 3.0 %collective-permute-start.2 = (bf16[32,64,128]{2,1,0:T(8,128)(2,1)S(1)}, bf16[32,64,128]{2,1,0:T(8,128)(2,1)S(1)}, u32[]{:S(2)}, u32[]{:S(2)}) collective-permute-start(bf16[32,64,128]{2,1,0:T(8,128)(2,1)S(1)} %get-tuple-element.34.refs_0_.refs_6_), channel_id=1, source_target_pairs={{0,2},{1,3},{2,0},{3,1},{4,6},{5,7},{6,4},{7,5},{8,10},{9,11},{10,... | collective-permute-start | bytes 1572872 | tf_op jit(solution)/shard_map/ppermute | solution.py:196
  5.2 1.5 collective-permute-start.3
  6.7 4.7 %right_front.1 = (bf16[32,64,128]{2,1,0:T(8,128)(2,1)S(1)}, bf16[32,64,128]{2,1,0:T(8,128)(2,1)S(1)}) custom-call(s32[4,4]{1,0:T(4,128)S(1)} %copy-done.8, bf16[128,64,128]{2,1,0:T(8,128)(2,1)S(1)} %copy-done, f32[1,128]{1,0:T(1,128)S(1)} %bitcast.5, f32[1,128]{1,0:T(1,128)S(1)} %bitcast.8, bf16[128,256]{1,0:T(8,128)(2,1)S(1)} %copy-done.7), custom_call_target="tpu_custom_call" | custom-call | flops 536870912 | bytes 6291456 | tf_op jit(solution)/shard_map/right_front/pallas_call | solution.py:78
  11.5 4.0 %collective-permute-start = (bf16[32,64,128]{2,1,0:T(8,128)(2,1)S(1)}, bf16[32,64,128]{2,1,0:T(8,128)(2,1)S(1)}, u32[]{:S(2)}, u32[]{:S(2)}) collective-permute-start(bf16[32,64,128]{2,1,0:T(8,128)(2,1)S(1)} %get-tuple-element.39.own), channel_id=1, source_target_pairs={{0,8},{8,16},{16,24},{1,9},{9,17},{17,25},{2,10},{10,18},{18,26},{... | collective-permute-start | bytes 1572872 | tf_op jit(solution)/shard_map/ppermute | solution.py:330
  15.4 1.3 collective-permute-start.1
  16.7 1.2 collective-permute-done.2.refs_1_.refs_7_
  17.9 2.1 %collective-permute-start.16 = (bf16[32,64,128]{2,1,0:T(8,128)(2,1)S(1)}, bf16[32,64,128]{2,1,0:T(8,128)(2,1)S(1)}, u32[]{:S(2)}, u32[]{:S(2)}) collective-permute-start(bf16[32,64,128]{2,1,0:T(8,128)(2,1)S(1)} %get-tuple-element.41.refs_0_.refs_6_), channel_id=1, source_target_pairs={{0,2},{1,3},{2,0},{3,1},{4,6},{5,7},{6,4},{7,5},{8,10},{9,11},{10,... | collective-permute-start | bytes 1572872 | tf_op jit(solution)/shard_map/ppermute | solution.py:196
  20.0 10.2 %collective-permute-done.3.refs_2_.refs_8_ = bf16[32,64,128]{2,1,0:T(8,128)(2,1)S(1)} collective-permute-done((bf16[32,64,128]{2,1,0:T(8,128)(2,1)S(1)}, bf16[32,64,128]{2,1,0:T(8,128)(2,1)S(1)}, u32[]{:S(2)}, u32[]{:S(2)}) %collective-permute-start.3) | collective-permute-done | bytes 524320 | tf_op jit(solution)/shard_map/ppermute | solution.py:196
  30.2 2.5 %collective-permute-start.17 = (bf16[32,64,128]{2,1,0:T(8,128)(2,1)S(1)}, bf16[32,64,128]{2,1,0:T(8,128)(2,1)S(1)}, u32[]{:S(2)}, u32[]{:S(2)}) collective-permute-start(bf16[32,64,128]{2,1,0:T(8,128)(2,1)S(1)} %get-tuple-element.41.refs_0_.refs_6_), channel_id=1, source_target_pairs={{0,4},{1,5},{2,6},{3,7},{4,0},{5,1},{6,2},{7,3},{8,12},{9,13},{10,... | collective-permute-start | bytes 1572872 | tf_op jit(solution)/shard_map/ppermute | solution.py:196
  32.7 4.7 %left_front.1 = (bf16[32,64,128]{2,1,0:T(8,128)(2,1)S(1)}, bf16[32,64,128]{2,1,0:T(8,128)(2,1)S(1)}) custom-call(s32[4,4]{1,0:T(4,128)S(1)} %copy-done.8, bf16[128,64,128]{2,1,0:T(8,128)(2,1)S(1)} %copy-done, f32[1,128]{1,0:T(1,128)S(1)} %bitcast.6, f32[1,128]{1,0:T(1,128)S(1)} %bitcast.9, bf16[128,256]{1,0:T(8,128)(2,1)S(1)} %copy-done.7), custom_call_target="tpu_custom_call" | custom-call | flops 536870912 | bytes 6291456 | tf_op jit(solution)/shard_map/left_front/pallas_call | solution.py:78
  37.4 3.3 %collective-permute-start.14 = (bf16[32,64,128]{2,1,0:T(8,128)(2,1)S(1)}, bf16[32,64,128]{2,1,0:T(8,128)(2,1)S(1)}, u32[]{:S(2)}, u32[]{:S(2)}) collective-permute-start(bf16[32,64,128]{2,1,0:T(8,128)(2,1)S(1)} %get-tuple-element.46.own), channel_id=1, source_target_pairs={{0,8},{8,16},{16,24},{1,9},{9,17},{17,25},{2,10},{10,18},{18,26},{... | collective-permute-start | bytes 1572872 | tf_op jit(solution)/shard_map/ppermute | solution.py:330
  41.3 11.0 %collective-permute-done.17.refs_2_.refs_8_ = bf16[32,64,128]{2,1,0:T(8,128)(2,1)S(1)} collective-permute-done((bf16[32,64,128]{2,1,0:T(8,128)(2,1)S(1)}, bf16[32,64,128]{2,1,0:T(8,128)(2,1)S(1)}, u32[]{:S(2)}, u32[]{:S(2)}) %collective-permute-start.17) | collective-permute-done | bytes 524320 | tf_op jit(solution)/shard_map/ppermute | solution.py:196
  52.8 1.3 collective-permute-start.15
  55.7 4.7 %right_partials.2 = (bf16[32,64,128]{2,1,0:T(8,128)(2,1)S(1)}, bf16[32,64,128]{2,1,0:T(8,128)(2,1)S(1)}, bf16[32,64,128]{2,1,0:T(8,128)(2,1)S(1)}, bf16[32,64,128]{2,1,0:T(8,128)(2,1)S(1)}) custom-call(bf16[32,64,128]{2,1,0:T(8,128)(2,1)S(1)} %get-tuple-element.31.left, bf16[32,64,128]{2,1,0:T(8,128)(2,1)S(1)} %get-tuple-element.34.refs_0_.refs_6_, ...), custom_call_target="tpu_custom_call" | custom-call | flops 268435456 | bytes 6815744 | tf_op jit(solution)/shard_map/right_partials/pallas_call | solution.py:251
  60.4 8.1 %collective-permute-done.15.refs_3_ = bf16[32,64,128]{2,1,0:T(8,128)(2,1)S(1)} collective-permute-done((bf16[32,64,128]{2,1,0:T(8,128)(2,1)S(1)}, bf16[32,64,128]{2,1,0:T(8,128)(2,1)S(1)}, u32[]{:S(2)}, u32[]{:S(2)}) %collective-permute-start.15) | collective-permute-done | bytes 524320 | tf_op jit(solution)/shard_map/ppermute | solution.py:331
  68.5 3.5 %collective-permute-start.9 = (bf16[32,64,128]{2,1,0:T(8,128)(2,1)S(1)}, bf16[32,64,128]{2,1,0:T(8,128)(2,1)S(1)}, u32[]{:S(2)}, u32[]{:S(2)}) collective-permute-start(bf16[32,64,128]{2,1,0:T(8,128)(2,1)S(1)} %get-tuple-element.38), channel_id=1, source_target_pairs={{0,8},{1,9},{2,10},{3,11},{4,12},{5,13},{6,14},{7,15}} | collective-permute-start | bytes 1572872 | tf_op jit(solution)/shard_map/ppermute | solution.py:348
  72.0 0.7 collective-permute-start.32
  72.8 0.8 copy-done.13
  73.6 0.8 copy-done.14
  74.4 4.7 %right_partials.3 = (bf16[32,64,128]{2,1,0:T(8,128)(2,1)S(1)}, bf16[32,64,128]{2,1,0:T(8,128)(2,1)S(1)}, bf16[32,64,128]{2,1,0:T(8,128)(2,1)S(1)}, bf16[32,64,128]{2,1,0:T(8,128)(2,1)S(1)}) custom-call(bf16[32,64,128]{2,1,0:T(8,128)(2,1)S(1)} %get-tuple-element.40.left, bf16[32,64,128]{2,1,0:T(8,128)(2,1)S(1)} %get-tuple-element.41.refs_0_.refs_6_, ...), custom_call_target="tpu_custom_call" | custom-call | flops 268435456 | bytes 6815744 | tf_op jit(solution)/shard_map/right_partials/pallas_call | solution.py:251
  79.1 1.3 collective-permute-start.23
  80.4 0.7 collective-permute-start.35
  81.8 2.5 %collective-permute-done.9 = bf16[32,64,128]{2,1,0:T(8,128)(2,1)S(1)} collective-permute-done((bf16[32,64,128]{2,1,0:T(8,128)(2,1)S(1)}, bf16[32,64,128]{2,1,0:T(8,128)(2,1)S(1)}, u32[]{:S(2)}, u32[]{:S(2)}) %collective-permute-start.9) | collective-permute-done | bytes 524320 | tf_op jit(solution)/shard_map/ppermute | solution.py:348
  84.7 4.4 %collective-permute-start.28 = (bf16[32,64,128]{2,1,0:T(8,128)(2,1)S(1)}, bf16[32,64,128]{2,1,0:T(8,128)(2,1)S(1)}, u32[]{:S(2)}, u32[]{:S(2)}) collective-permute-start(bf16[32,64,128]{2,1,0:T(8,128)(2,1)S(1)} %get-tuple-element.58), channel_id=1, source_target_pairs={{0,8},{8,16},{1,9},{9,17},{2,10},{10,18},{3,11},{11,19},{4,12},{12... | collective-permute-start | bytes 1572872 | tf_op jit(solution)/shard_map/ppermute | solution.py:348
  89.1 6.5 %collective-permute-done.23 = bf16[32,64,128]{2,1,0:T(8,128)(2,1)S(1)} collective-permute-done((bf16[32,64,128]{2,1,0:T(8,128)(2,1)S(1)}, bf16[32,64,128]{2,1,0:T(8,128)(2,1)S(1)}, u32[]{:S(2)}, u32[]{:S(2)}) %collective-permute-start.23) | collective-permute-done | bytes 524320 | tf_op jit(solution)/shard_map/ppermute | solution.py:348
  95.9 4.4 %collective-permute-start.30 = (bf16[32,64,128]{2,1,0:T(8,128)(2,1)S(1)}, bf16[32,64,128]{2,1,0:T(8,128)(2,1)S(1)}, u32[]{:S(2)}, u32[]{:S(2)}) collective-permute-start(bf16[32,64,128]{2,1,0:T(8,128)(2,1)S(1)} %get-tuple-element.56), channel_id=1, source_target_pairs={{0,8},{8,16},{1,9},{9,17},{2,10},{10,18},{3,11},{11,19},{4,12},{12... | collective-permute-start | bytes 1572872 | tf_op jit(solution)/shard_map/ppermute | solution.py:348
  100.3 1.3 collective-permute-start.12
  102.3 1.3 collective-permute-start.26
  103.6 3.2 %collective-permute-done.28 = bf16[32,64,128]{2,1,0:T(8,128)(2,1)S(1)} collective-permute-done((bf16[32,64,128]{2,1,0:T(8,128)(2,1)S(1)}, bf16[32,64,128]{2,1,0:T(8,128)(2,1)S(1)}, u32[]{:S(2)}, u32[]{:S(2)}) %collective-permute-start.28) | collective-permute-done | bytes 524320 | tf_op jit(solution)/shard_map/ppermute | solution.py:348
  107.5 1.0 add_convert_fusion.3
  108.5 7.7 %collective-permute-done.30 = bf16[32,64,128]{2,1,0:T(8,128)(2,1)S(1)} collective-permute-done((bf16[32,64,128]{2,1,0:T(8,128)(2,1)S(1)}, bf16[32,64,128]{2,1,0:T(8,128)(2,1)S(1)}, u32[]{:S(2)}, u32[]{:S(2)}) %collective-permute-start.30) | collective-permute-done | bytes 524320 | tf_op jit(solution)/shard_map/ppermute | solution.py:348
  116.9 1.0 add_convert_fusion.2
  118.6 1.3 collective-permute-start.13
  119.9 4.0 %collective-permute-done.26.refs_4_ = bf16[32,64,128]{2,1,0:T(8,128)(2,1)S(1)} collective-permute-done((bf16[32,64,128]{2,1,0:T(8,128)(2,1)S(1)}, bf16[32,64,128]{2,1,0:T(8,128)(2,1)S(1)}, u32[]{:S(2)}, u32[]{:S(2)}) %collective-permute-start.26) | collective-permute-done | bytes 524320 | tf_op jit(solution)/shard_map/ppermute | solution.py:331
  124.6 1.3 collective-permute-start.27
  125.9 1.0 add_convert_fusion.1
  126.9 23.1 %collective-permute-start.29 = (bf16[32,64,128]{2,1,0:T(8,128)(2,1)}, bf16[32,64,128]{2,1,0:T(8,128)(2,1)S(1)}, u32[]{:S(2)}, u32[]{:S(2)}) collective-permute-start(bf16[32,64,128]{2,1,0:T(8,128)(2,1)} %add_convert_fusion.3), channel_id=1, source_target_pairs={{0,8},{8,16},{16,24},{1,9},{9,17},{17,25},{2,10},{10,18},{18,26},{... | collective-permute-start | bytes 1572872 | tf_op jit(solution)/shard_map/ppermute | solution.py:348
  150.0 1.0 add_convert_fusion
  151.0 1.9 %collective-permute-start.31 = (bf16[32,64,128]{2,1,0:T(8,128)(2,1)}, bf16[32,64,128]{2,1,0:T(8,128)(2,1)S(1)}, u32[]{:S(2)}, u32[]{:S(2)}) collective-permute-start(bf16[32,64,128]{2,1,0:T(8,128)(2,1)} %add_convert_fusion.2), channel_id=1, source_target_pairs={{0,8},{8,16},{16,24},{1,9},{9,17},{17,25},{2,10},{10,18},{18,26},{... | collective-permute-start | bytes 1572872 | tf_op jit(solution)/shard_map/ppermute | solution.py:348
  152.9 1.3 collective-permute-start.34
  154.3 1.5 collective-permute-start.37
  155.7 4.0 %left_products.2.refs_0_ = f32[32,64,128]{2,1,0:T(8,128)} custom-call(bf16[32,64,128]{2,1,0:T(8,128)(2,1)S(1)} %get-tuple-element.39.own, bf16[32,64,128]{2,1,0:T(8,128)(2,1)S(1)} %collective-permute-done.refs_0_, bf16[32,64,128]{2,1,0:T(8,128)(2,1)S(1)} %collective-permute-done.10.refs_1_, bf16[32,64,128]{2,1,0:T(8,128)(2,1)S(1)} %collective-permute-done.11.refs_2_, ...), custom_call_target="tpu_custom_call" | custom-call | flops 268435456 | bytes 7340032 | tf_op jit(solution)/shard_map/left_products/pallas_call | solution.py:292
  159.8 4.1 %left_products.3.refs_1_ = f32[32,64,128]{2,1,0:T(8,128)} custom-call(bf16[32,64,128]{2,1,0:T(8,128)(2,1)S(1)} %get-tuple-element.46.own, bf16[32,64,128]{2,1,0:T(8,128)(2,1)S(1)} %collective-permute-done.14.refs_0_, bf16[32,64,128]{2,1,0:T(8,128)(2,1)S(1)} %collective-permute-done.24.refs_1_, bf16[32,64,128]{2,1,0:T(8,128)(2,1)S(1)} %collective-permute-done.25.refs_2_, ...), custom_call_target="tpu_custom_call" | custom-call | flops 268435456 | bytes 7340032 | tf_op jit(solution)/shard_map/left_products/pallas_call | solution.py:292
  164.0 6.0 %collective-permute-done.31.refs_5_ = bf16[32,64,128]{2,1,0:T(8,128)(2,1)S(1)} collective-permute-done((bf16[32,64,128]{2,1,0:T(8,128)(2,1)}, bf16[32,64,128]{2,1,0:T(8,128)(2,1)S(1)}, u32[]{:S(2)}, u32[]{:S(2)}) %collective-permute-start.31) | collective-permute-done | bytes 524320 | tf_op jit(solution)/shard_map/ppermute | solution.py:348
  169.9 7.0 %collective-permute-done.37.refs_7_ = bf16[32,64,128]{2,1,0:T(8,128)(2,1)S(1)} collective-permute-done((bf16[32,64,128]{2,1,0:T(8,128)(2,1)}, bf16[32,64,128]{2,1,0:T(8,128)(2,1)S(1)}, u32[]{:S(2)}, u32[]{:S(2)}) %collective-permute-start.37) | collective-permute-done | bytes 524320 | tf_op jit(solution)/shard_map/ppermute | solution.py:349
  176.9 1.2 copy-done.2
  178.1 11.3 %tail.1 = bf16[128,64,128]{2,1,0:T(8,128)(2,1)} custom-call(s32[4,4]{1,0:T(4,128)S(1)} %copy-done.8, bf16[128,64,128]{2,1,0:T(8,128)(2,1)} %pair.5, f32[1,128]{1,0:T(1,128)S(1)} %bitcast.7, f32[1,128]{1,0:T(1,128)S(1)} %bitcast.10, bf16[128,256]{1,0:T(8,128)(2,1)S(1)} %copy-done.7, f32[32,64,128]{2,1,0:T(8,128)S(1)} %copy-done.1, ...), custom_call_target="tpu_custom_call" | custom-call | flops 2147483648 | bytes 10485760 | tf_op jit(solution)/shard_map/tail/pallas_call | solution.py:158
  (73 shorter events, 7.6 us)
Async XLA Ops:
  0.0 6.7 %copy-start.8 = (s32[4,4]{1,0:T(4,128)S(1)}, s32[4,4]{1,0:T(4,128)}, u32[]{:S(2)}) copy-start(s32[4,4]{1,0:T(4,128)} %mask.5) | copy-start | bytes 196
  0.0 6.7 %copy-start = (bf16[128,64,128]{2,1,0:T(8,128)(2,1)S(1)}, bf16[128,64,128]{2,1,0:T(8,128)(2,1)}, u32[]{:S(2)}) copy-start(bf16[128,64,128]{2,1,0:T(8,128)(2,1)} %pair.5) | copy-start | bytes 6291460
  0.0 6.7 %copy-start.9 = (f32[128]{0:T(128)S(1)}, f32[128]{0:T(128)}, u32[]{:S(2)}) copy-start(f32[128]{0:T(128)} %param.8) | copy-start | bytes 1540
  0.0 6.7 %copy-start.10 = (f32[128]{0:T(128)S(1)}, f32[128]{0:T(128)}, u32[]{:S(2)}) copy-start(f32[128]{0:T(128)} %param.9) | copy-start | bytes 1540
  0.0 6.7 %copy-start.7 = (bf16[128,256]{1,0:T(8,128)(2,1)S(1)}, bf16[128,256]{1,0:T(8,128)(2,1)}, u32[]{:S(2)}) copy-start(bf16[128,256]{1,0:T(8,128)(2,1)} %weight.5) | copy-start | bytes 196612
  2.1 15.8 %collective-permute-start.2 = (bf16[32,64,128]{2,1,0:T(8,128)(2,1)S(1)}, bf16[32,64,128]{2,1,0:T(8,128)(2,1)S(1)}, u32[]{:S(2)}, u32[]{:S(2)}) collective-permute-start(bf16[32,64,128]{2,1,0:T(8,128)(2,1)S(1)} %get-tuple-element.34.refs_0_.refs_6_), channel_id=1, source_target_pairs={{0,2},{1,3},{2,0},{3,1},{4,6},{5,7},{6,4},{7,5},{8,10},{9,11},{10,... | collective-permute-start | bytes 1572872 | tf_op jit(solution)/shard_map/ppermute | solution.py:196
  5.2 25.0 %collective-permute-start.3 = (bf16[32,64,128]{2,1,0:T(8,128)(2,1)S(1)}, bf16[32,64,128]{2,1,0:T(8,128)(2,1)S(1)}, u32[]{:S(2)}, u32[]{:S(2)}) collective-permute-start(bf16[32,64,128]{2,1,0:T(8,128)(2,1)S(1)} %get-tuple-element.34.refs_0_.refs_6_), channel_id=1, source_target_pairs={{0,4},{1,5},{2,6},{3,7},{4,0},{5,1},{6,2},{7,3},{8,12},{9,13},{10,... | collective-permute-start | bytes 1572872 | tf_op jit(solution)/shard_map/ppermute | solution.py:196
  6.7 26.0 %collective-permute-start.4 = (bf16[32,64,128]{2,1,0:T(8,128)(2,1)S(1)}, bf16[32,64,128]{2,1,0:T(8,128)(2,1)S(1)}, u32[]{:S(2)}, u32[]{:S(2)}) collective-permute-start(bf16[32,64,128]{2,1,0:T(8,128)(2,1)S(1)} %get-tuple-element.34.refs_0_.refs_6_), channel_id=1, source_target_pairs={{0,6},{1,7},{2,4},{3,5},{4,2},{5,3},{6,0},{7,1},{8,14},{9,15},{10,... | collective-permute-start | bytes 1572872 | tf_op jit(solution)/shard_map/ppermute | solution.py:196
  11.5 25.9 %collective-permute-start = (bf16[32,64,128]{2,1,0:T(8,128)(2,1)S(1)}, bf16[32,64,128]{2,1,0:T(8,128)(2,1)S(1)}, u32[]{:S(2)}, u32[]{:S(2)}) collective-permute-start(bf16[32,64,128]{2,1,0:T(8,128)(2,1)S(1)} %get-tuple-element.39.own), channel_id=1, source_target_pairs={{0,8},{8,16},{16,24},{1,9},{9,17},{17,25},{2,10},{10,18},{18,26},{... | collective-permute-start | bytes 1572872 | tf_op jit(solution)/shard_map/ppermute | solution.py:330
  15.4 25.2 %collective-permute-start.1 = (bf16[32,64,128]{2,1,0:T(8,128)(2,1)S(1)}, bf16[32,64,128]{2,1,0:T(8,128)(2,1)S(1)}, u32[]{:S(2)}, u32[]{:S(2)}) collective-permute-start(bf16[32,64,128]{2,1,0:T(8,128)(2,1)S(1)} %get-tuple-element.39.own), channel_id=1, source_target_pairs={{8,0},{16,8},{24,16},{9,1},{17,9},{25,17},{10,2},{18,10},{26,18},{... | collective-permute-start | bytes 1572872 | tf_op jit(solution)/shard_map/ppermute | solution.py:331
  17.9 22.8 %collective-permute-start.16 = (bf16[32,64,128]{2,1,0:T(8,128)(2,1)S(1)}, bf16[32,64,128]{2,1,0:T(8,128)(2,1)S(1)}, u32[]{:S(2)}, u32[]{:S(2)}) collective-permute-start(bf16[32,64,128]{2,1,0:T(8,128)(2,1)S(1)} %get-tuple-element.41.refs_0_.refs_6_), channel_id=1, source_target_pairs={{0,2},{1,3},{2,0},{3,1},{4,6},{5,7},{6,4},{7,5},{8,10},{9,11},{10,... | collective-permute-start | bytes 1572872 | tf_op jit(solution)/shard_map/ppermute | solution.py:196
  30.2 22.1 %collective-permute-start.17 = (bf16[32,64,128]{2,1,0:T(8,128)(2,1)S(1)}, bf16[32,64,128]{2,1,0:T(8,128)(2,1)S(1)}, u32[]{:S(2)}, u32[]{:S(2)}) collective-permute-start(bf16[32,64,128]{2,1,0:T(8,128)(2,1)S(1)} %get-tuple-element.41.refs_0_.refs_6_), channel_id=1, source_target_pairs={{0,4},{1,5},{2,6},{3,7},{4,0},{5,1},{6,2},{7,3},{8,12},{9,13},{10,... | collective-permute-start | bytes 1572872 | tf_op jit(solution)/shard_map/ppermute | solution.py:196
  32.7 19.6 %collective-permute-start.18 = (bf16[32,64,128]{2,1,0:T(8,128)(2,1)S(1)}, bf16[32,64,128]{2,1,0:T(8,128)(2,1)S(1)}, u32[]{:S(2)}, u32[]{:S(2)}) collective-permute-start(bf16[32,64,128]{2,1,0:T(8,128)(2,1)S(1)} %get-tuple-element.41.refs_0_.refs_6_), channel_id=1, source_target_pairs={{0,6},{1,7},{2,4},{3,5},{4,2},{5,3},{6,0},{7,1},{8,14},{9,15},{10,... | collective-permute-start | bytes 1572872 | tf_op jit(solution)/shard_map/ppermute | solution.py:196
  37.4 15.4 %collective-permute-start.14 = (bf16[32,64,128]{2,1,0:T(8,128)(2,1)S(1)}, bf16[32,64,128]{2,1,0:T(8,128)(2,1)S(1)}, u32[]{:S(2)}, u32[]{:S(2)}) collective-permute-start(bf16[32,64,128]{2,1,0:T(8,128)(2,1)S(1)} %get-tuple-element.46.own), channel_id=1, source_target_pairs={{0,8},{8,16},{16,24},{1,9},{9,17},{17,25},{2,10},{10,18},{18,26},{... | collective-permute-start | bytes 1572872 | tf_op jit(solution)/shard_map/ppermute | solution.py:330
  40.7 13.4 %collective-permute-start.5 = (bf16[32,64,128]{2,1,0:T(8,128)(2,1)S(1)}, bf16[32,64,128]{2,1,0:T(8,128)(2,1)S(1)}, u32[]{:S(2)}, u32[]{:S(2)}) collective-permute-start(bf16[32,64,128]{2,1,0:T(8,128)(2,1)S(1)} %get-tuple-element.34.refs_0_.refs_6_), channel_id=1, source_target_pairs={{0,1},{1,0},{2,3},{3,2},{4,5},{5,4},{6,7},{7,6},{8,9},{9,8},{10,11... | collective-permute-start | bytes 1572872 | tf_op jit(solution)/shard_map/ppermute | solution.py:196
  40.8 13.4 %collective-permute-start.6 = (bf16[32,64,128]{2,1,0:T(8,128)(2,1)S(1)}, bf16[32,64,128]{2,1,0:T(8,128)(2,1)S(1)}, u32[]{:S(2)}, u32[]{:S(2)}) collective-permute-start(bf16[32,64,128]{2,1,0:T(8,128)(2,1)S(1)} %collective-permute-done.2.refs_1_.refs_7_), channel_id=1, source_target_pairs={{0,1},{1,0},{2,3},{3,2},{4,5},{5,4},{6,7},{7,6},{8,9},{9,8},{10,11... | collective-permute-start | bytes 1572872 | tf_op jit(solution)/shard_map/ppermute | solution.py:196
  52.3 2.4 %collective-permute-start.7 = (bf16[32,64,128]{2,1,0:T(8,128)(2,1)S(1)}, bf16[32,64,128]{2,1,0:T(8,128)(2,1)S(1)}, u32[]{:S(2)}, u32[]{:S(2)}) collective-permute-start(bf16[32,64,128]{2,1,0:T(8,128)(2,1)S(1)} %collective-permute-done.3.refs_2_.refs_8_), channel_id=1, source_target_pairs={{0,1},{1,0},{2,3},{3,2},{4,5},{5,4},{6,7},{7,6},{8,9},{9,8},{10,11... | collective-permute-start | bytes 1572872 | tf_op jit(solution)/shard_map/ppermute | solution.py:196
  52.3 2.7 %collective-permute-start.8 = (bf16[32,64,128]{2,1,0:T(8,128)(2,1)S(1)}, bf16[32,64,128]{2,1,0:T(8,128)(2,1)S(1)}, u32[]{:S(2)}, u32[]{:S(2)}) collective-permute-start(bf16[32,64,128]{2,1,0:T(8,128)(2,1)S(1)} %collective-permute-done.4.refs_3_.refs_9_), channel_id=1, source_target_pairs={{0,1},{1,0},{2,3},{3,2},{4,5},{5,4},{6,7},{7,6},{8,9},{9,8},{10,11... | collective-permute-start | bytes 1572872 | tf_op jit(solution)/shard_map/ppermute | solution.py:196
  52.8 15.7 %collective-permute-start.15 = (bf16[32,64,128]{2,1,0:T(8,128)(2,1)S(1)}, bf16[32,64,128]{2,1,0:T(8,128)(2,1)S(1)}, u32[]{:S(2)}, u32[]{:S(2)}) collective-permute-start(bf16[32,64,128]{2,1,0:T(8,128)(2,1)S(1)} %get-tuple-element.46.own), channel_id=1, source_target_pairs={{8,0},{16,8},{24,16},{9,1},{17,9},{25,17},{10,2},{18,10},{26,18},{... | collective-permute-start | bytes 1572872 | tf_op jit(solution)/shard_map/ppermute | solution.py:331
  54.1 6.3 %copy-start.3 = (bf16[32,64,128]{2,1,0:T(8,128)(2,1)}, bf16[32,64,128]{2,1,0:T(8,128)(2,1)S(1)}, u32[]{:S(2)}) copy-start(bf16[32,64,128]{2,1,0:T(8,128)(2,1)S(1)} %collective-permute-done.5.refs_4_.refs_10_) | copy-start | bytes 1572868
  54.1 17.9 %collective-permute-start.19 = (bf16[32,64,128]{2,1,0:T(8,128)(2,1)S(1)}, bf16[32,64,128]{2,1,0:T(8,128)(2,1)S(1)}, u32[]{:S(2)}, u32[]{:S(2)}) collective-permute-start(bf16[32,64,128]{2,1,0:T(8,128)(2,1)S(1)} %get-tuple-element.41.refs_0_.refs_6_), channel_id=1, source_target_pairs={{0,1},{1,0},{2,3},{3,2},{4,5},{5,4},{6,7},{7,6},{8,9},{9,8},{10,11... | collective-permute-start | bytes 1572872 | tf_op jit(solution)/shard_map/ppermute | solution.py:196
  54.2 6.2 %copy-start.4 = (bf16[32,64,128]{2,1,0:T(8,128)(2,1)}, bf16[32,64,128]{2,1,0:T(8,128)(2,1)S(1)}, u32[]{:S(2)}) copy-start(bf16[32,64,128]{2,1,0:T(8,128)(2,1)S(1)} %collective-permute-done.6.refs_5_.refs_11_) | copy-start | bytes 1572868
  54.2 18.6 %collective-permute-start.20 = (bf16[32,64,128]{2,1,0:T(8,128)(2,1)S(1)}, bf16[32,64,128]{2,1,0:T(8,128)(2,1)S(1)}, u32[]{:S(2)}, u32[]{:S(2)}) collective-permute-start(bf16[32,64,128]{2,1,0:T(8,128)(2,1)S(1)} %collective-permute-done.16.refs_1_.refs_7_), channel_id=1, source_target_pairs={{0,1},{1,0},{2,3},{3,2},{4,5},{5,4},{6,7},{7,6},{8,9},{9,8},{10,11... | collective-permute-start | bytes 1572872 | tf_op jit(solution)/shard_map/ppermute | solution.py:196
  54.7 18.1 %collective-permute-start.21 = (bf16[32,64,128]{2,1,0:T(8,128)(2,1)S(1)}, bf16[32,64,128]{2,1,0:T(8,128)(2,1)S(1)}, u32[]{:S(2)}, u32[]{:S(2)}) collective-permute-start(bf16[32,64,128]{2,1,0:T(8,128)(2,1)S(1)} %collective-permute-done.17.refs_2_.refs_8_), channel_id=1, source_target_pairs={{0,1},{1,0},{2,3},{3,2},{4,5},{5,4},{6,7},{7,6},{8,9},{9,8},{10,11... | collective-permute-start | bytes 1572872 | tf_op jit(solution)/shard_map/ppermute | solution.py:196
  54.9 17.9 %collective-permute-start.22 = (bf16[32,64,128]{2,1,0:T(8,128)(2,1)S(1)}, bf16[32,64,128]{2,1,0:T(8,128)(2,1)S(1)}, u32[]{:S(2)}, u32[]{:S(2)}) collective-permute-start(bf16[32,64,128]{2,1,0:T(8,128)(2,1)S(1)} %collective-permute-done.18.refs_3_.refs_9_), channel_id=1, source_target_pairs={{0,1},{1,0},{2,3},{3,2},{4,5},{5,4},{6,7},{7,6},{8,9},{9,8},{10,11... | collective-permute-start | bytes 1572872 | tf_op jit(solution)/shard_map/ppermute | solution.py:196
  68.5 15.8 %collective-permute-start.9 = (bf16[32,64,128]{2,1,0:T(8,128)(2,1)S(1)}, bf16[32,64,128]{2,1,0:T(8,128)(2,1)S(1)}, u32[]{:S(2)}, u32[]{:S(2)}) collective-permute-start(bf16[32,64,128]{2,1,0:T(8,128)(2,1)S(1)} %get-tuple-element.38), channel_id=1, source_target_pairs={{0,8},{1,9},{2,10},{3,11},{4,12},{5,13},{6,14},{7,15}} | collective-permute-start | bytes 1572872 | tf_op jit(solution)/shard_map/ppermute | solution.py:348
  72.0 7.1 %copy-start.5 = (bf16[32,64,128]{2,1,0:T(8,128)(2,1)}, bf16[32,64,128]{2,1,0:T(8,128)(2,1)S(1)}, u32[]{:S(2)}) copy-start(bf16[32,64,128]{2,1,0:T(8,128)(2,1)S(1)} %collective-permute-done.19.refs_4_.refs_10_) | copy-start | bytes 1572868
  72.0 12.3 %collective-permute-start.32 = (bf16[32,64,128]{2,1,0:T(8,128)(2,1)S(1)}, bf16[32,64,128]{2,1,0:T(8,128)(2,1)S(1)}, u32[]{:S(2)}, u32[]{:S(2)}) collective-permute-start(bf16[32,64,128]{2,1,0:T(8,128)(2,1)S(1)} %get-tuple-element.49), channel_id=1, source_target_pairs={{24,16},{25,17},{26,18},{27,19},{28,20},{29,21},{30,22},{31,23}} | collective-permute-start | bytes 1572872 | tf_op jit(solution)/shard_map/ppermute | solution.py:349
  72.7 6.4 %copy-start.6 = (bf16[32,64,128]{2,1,0:T(8,128)(2,1)}, bf16[32,64,128]{2,1,0:T(8,128)(2,1)S(1)}, u32[]{:S(2)}) copy-start(bf16[32,64,128]{2,1,0:T(8,128)(2,1)S(1)} %collective-permute-done.20.refs_5_.refs_11_) | copy-start | bytes 1572868
  79.1 16.5 %collective-permute-start.23 = (bf16[32,64,128]{2,1,0:T(8,128)(2,1)S(1)}, bf16[32,64,128]{2,1,0:T(8,128)(2,1)S(1)}, u32[]{:S(2)}, u32[]{:S(2)}) collective-permute-start(bf16[32,64,128]{2,1,0:T(8,128)(2,1)S(1)} %get-tuple-element.45), channel_id=1, source_target_pairs={{0,8},{1,9},{2,10},{3,11},{4,12},{5,13},{6,14},{7,15}} | collective-permute-start | bytes 1572872 | tf_op jit(solution)/shard_map/ppermute | solution.py:348
  80.4 15.1 %collective-permute-start.35 = (bf16[32,64,128]{2,1,0:T(8,128)(2,1)S(1)}, bf16[32,64,128]{2,1,0:T(8,128)(2,1)S(1)}, u32[]{:S(2)}, u32[]{:S(2)}) collective-permute-start(bf16[32,64,128]{2,1,0:T(8,128)(2,1)S(1)} %get-tuple-element.51), channel_id=1, source_target_pairs={{24,16},{25,17},{26,18},{27,19},{28,20},{29,21},{30,22},{31,23}} | collective-permute-start | bytes 1572872 | tf_op jit(solution)/shard_map/ppermute | solution.py:349
  81.1 21.1 %collective-permute-start.10 = (bf16[32,64,128]{2,1,0:T(8,128)(2,1)S(1)}, bf16[32,64,128]{2,1,0:T(8,128)(2,1)S(1)}, u32[]{:S(2)}, u32[]{:S(2)}) collective-permute-start(bf16[32,64,128]{2,1,0:T(8,128)(2,1)S(1)} %collective-permute-done.refs_0_), channel_id=1, source_target_pairs={{8,16},{16,24},{9,17},{17,25},{10,18},{18,26},{11,19},{19,27},{12,... | collective-permute-start | bytes 1572872 | tf_op jit(solution)/shard_map/ppermute | solution.py:330
  84.7 22.1 %collective-permute-start.28 = (bf16[32,64,128]{2,1,0:T(8,128)(2,1)S(1)}, bf16[32,64,128]{2,1,0:T(8,128)(2,1)S(1)}, u32[]{:S(2)}, u32[]{:S(2)}) collective-permute-start(bf16[32,64,128]{2,1,0:T(8,128)(2,1)S(1)} %get-tuple-element.58), channel_id=1, source_target_pairs={{0,8},{8,16},{1,9},{9,17},{2,10},{10,18},{3,11},{11,19},{4,12},{12... | collective-permute-start | bytes 1572872 | tf_op jit(solution)/shard_map/ppermute | solution.py:348
  95.9 20.3 %collective-permute-start.30 = (bf16[32,64,128]{2,1,0:T(8,128)(2,1)S(1)}, bf16[32,64,128]{2,1,0:T(8,128)(2,1)S(1)}, u32[]{:S(2)}, u32[]{:S(2)}) collective-permute-start(bf16[32,64,128]{2,1,0:T(8,128)(2,1)S(1)} %get-tuple-element.56), channel_id=1, source_target_pairs={{0,8},{8,16},{1,9},{9,17},{2,10},{10,18},{3,11},{11,19},{4,12},{12... | collective-permute-start | bytes 1572872 | tf_op jit(solution)/shard_map/ppermute | solution.py:348
  100.3 17.6 %collective-permute-start.12 = (bf16[32,64,128]{2,1,0:T(8,128)(2,1)S(1)}, bf16[32,64,128]{2,1,0:T(8,128)(2,1)S(1)}, u32[]{:S(2)}, u32[]{:S(2)}) collective-permute-start(bf16[32,64,128]{2,1,0:T(8,128)(2,1)S(1)} %collective-permute-done.1.refs_3_), channel_id=1, source_target_pairs={{8,0},{16,8},{9,1},{17,9},{10,2},{18,10},{11,3},{19,11},{12,4},{20... | collective-permute-start | bytes 1572872 | tf_op jit(solution)/shard_map/ppermute | solution.py:331
  101.6 17.0 %collective-permute-start.24 = (bf16[32,64,128]{2,1,0:T(8,128)(2,1)S(1)}, bf16[32,64,128]{2,1,0:T(8,128)(2,1)S(1)}, u32[]{:S(2)}, u32[]{:S(2)}) collective-permute-start(bf16[32,64,128]{2,1,0:T(8,128)(2,1)S(1)} %collective-permute-done.14.refs_0_), channel_id=1, source_target_pairs={{8,16},{16,24},{9,17},{17,25},{10,18},{18,26},{11,19},{19,27},{12,... | collective-permute-start | bytes 1572872 | tf_op jit(solution)/shard_map/ppermute | solution.py:330
  102.3 21.6 %collective-permute-start.26 = (bf16[32,64,128]{2,1,0:T(8,128)(2,1)S(1)}, bf16[32,64,128]{2,1,0:T(8,128)(2,1)S(1)}, u32[]{:S(2)}, u32[]{:S(2)}) collective-permute-start(bf16[32,64,128]{2,1,0:T(8,128)(2,1)S(1)} %collective-permute-done.15.refs_3_), channel_id=1, source_target_pairs={{8,0},{16,8},{9,1},{17,9},{10,2},{18,10},{11,3},{19,11},{12,4},{20... | collective-permute-start | bytes 1572872 | tf_op jit(solution)/shard_map/ppermute | solution.py:331
  106.8 17.8 %collective-permute-start.33 = (bf16[32,64,128]{2,1,0:T(8,128)(2,1)S(1)}, bf16[32,64,128]{2,1,0:T(8,128)(2,1)S(1)}, u32[]{:S(2)}, u32[]{:S(2)}) collective-permute-start(bf16[32,64,128]{2,1,0:T(8,128)(2,1)S(1)} %get-tuple-element.57), channel_id=1, source_target_pairs={{16,8},{24,16},{17,9},{25,17},{18,10},{26,18},{19,11},{27,19},{20,... | collective-permute-start | bytes 1572872 | tf_op jit(solution)/shard_map/ppermute | solution.py:349
  116.2 10.7 %collective-permute-start.36 = (bf16[32,64,128]{2,1,0:T(8,128)(2,1)S(1)}, bf16[32,64,128]{2,1,0:T(8,128)(2,1)S(1)}, u32[]{:S(2)}, u32[]{:S(2)}) collective-permute-start(bf16[32,64,128]{2,1,0:T(8,128)(2,1)S(1)} %get-tuple-element.55), channel_id=1, source_target_pairs={{16,8},{24,16},{17,9},{25,17},{18,10},{26,18},{19,11},{27,19},{20,... | collective-permute-start | bytes 1572872 | tf_op jit(solution)/shard_map/ppermute | solution.py:349
  117.9 33.1 %collective-permute-start.11 = (bf16[32,64,128]{2,1,0:T(8,128)(2,1)S(1)}, bf16[32,64,128]{2,1,0:T(8,128)(2,1)S(1)}, u32[]{:S(2)}, u32[]{:S(2)}) collective-permute-start(bf16[32,64,128]{2,1,0:T(8,128)(2,1)S(1)} %collective-permute-done.10.refs_1_), channel_id=1, source_target_pairs={{16,24},{17,25},{18,26},{19,27},{20,28},{21,29},{22,30},{23,31}} | collective-permute-start | bytes 1572872 | tf_op jit(solution)/shard_map/ppermute | solution.py:330
  118.6 34.4 %collective-permute-start.13 = (bf16[32,64,128]{2,1,0:T(8,128)(2,1)S(1)}, bf16[32,64,128]{2,1,0:T(8,128)(2,1)S(1)}, u32[]{:S(2)}, u32[]{:S(2)}) collective-permute-start(bf16[32,64,128]{2,1,0:T(8,128)(2,1)S(1)} %collective-permute-done.12.refs_4_), channel_id=1, source_target_pairs={{8,0},{9,1},{10,2},{11,3},{12,4},{13,5},{14,6},{15,7}} | collective-permute-start | bytes 1572872 | tf_op jit(solution)/shard_map/ppermute | solution.py:331
  123.9 30.4 %collective-permute-start.25 = (bf16[32,64,128]{2,1,0:T(8,128)(2,1)S(1)}, bf16[32,64,128]{2,1,0:T(8,128)(2,1)S(1)}, u32[]{:S(2)}, u32[]{:S(2)}) collective-permute-start(bf16[32,64,128]{2,1,0:T(8,128)(2,1)S(1)} %collective-permute-done.24.refs_1_), channel_id=1, source_target_pairs={{16,24},{17,25},{18,26},{19,27},{20,28},{21,29},{22,30},{23,31}} | collective-permute-start | bytes 1572872 | tf_op jit(solution)/shard_map/ppermute | solution.py:330
  124.6 35.2 %collective-permute-start.27 = (bf16[32,64,128]{2,1,0:T(8,128)(2,1)S(1)}, bf16[32,64,128]{2,1,0:T(8,128)(2,1)S(1)}, u32[]{:S(2)}, u32[]{:S(2)}) collective-permute-start(bf16[32,64,128]{2,1,0:T(8,128)(2,1)S(1)} %collective-permute-done.26.refs_4_), channel_id=1, source_target_pairs={{8,0},{9,1},{10,2},{11,3},{12,4},{13,5},{14,6},{15,7}} | collective-permute-start | bytes 1572872 | tf_op jit(solution)/shard_map/ppermute | solution.py:331
  126.9 37.1 %collective-permute-start.29 = (bf16[32,64,128]{2,1,0:T(8,128)(2,1)}, bf16[32,64,128]{2,1,0:T(8,128)(2,1)S(1)}, u32[]{:S(2)}, u32[]{:S(2)}) collective-permute-start(bf16[32,64,128]{2,1,0:T(8,128)(2,1)} %add_convert_fusion.3), channel_id=1, source_target_pairs={{0,8},{8,16},{16,24},{1,9},{9,17},{17,25},{2,10},{10,18},{18,26},{... | collective-permute-start | bytes 1572872 | tf_op jit(solution)/shard_map/ppermute | solution.py:348
  151.0 18.9 %collective-permute-start.31 = (bf16[32,64,128]{2,1,0:T(8,128)(2,1)}, bf16[32,64,128]{2,1,0:T(8,128)(2,1)S(1)}, u32[]{:S(2)}, u32[]{:S(2)}) collective-permute-start(bf16[32,64,128]{2,1,0:T(8,128)(2,1)} %add_convert_fusion.2), channel_id=1, source_target_pairs={{0,8},{8,16},{16,24},{1,9},{9,17},{17,25},{2,10},{10,18},{18,26},{... | collective-permute-start | bytes 1572872 | tf_op jit(solution)/shard_map/ppermute | solution.py:348
  152.9 17.0 %collective-permute-start.34 = (bf16[32,64,128]{2,1,0:T(8,128)(2,1)}, bf16[32,64,128]{2,1,0:T(8,128)(2,1)S(1)}, u32[]{:S(2)}, u32[]{:S(2)}) collective-permute-start(bf16[32,64,128]{2,1,0:T(8,128)(2,1)} %add_convert_fusion.1), channel_id=1, source_target_pairs={{8,0},{16,8},{24,16},{9,1},{17,9},{25,17},{10,2},{18,10},{26,18},{... | collective-permute-start | bytes 1572872 | tf_op jit(solution)/shard_map/ppermute | solution.py:349
  154.3 22.6 %collective-permute-start.37 = (bf16[32,64,128]{2,1,0:T(8,128)(2,1)}, bf16[32,64,128]{2,1,0:T(8,128)(2,1)S(1)}, u32[]{:S(2)}, u32[]{:S(2)}) collective-permute-start(bf16[32,64,128]{2,1,0:T(8,128)(2,1)} %add_convert_fusion), channel_id=1, source_target_pairs={{8,0},{16,8},{24,16},{9,1},{17,9},{25,17},{10,2},{18,10},{26,18},{... | collective-permute-start | bytes 1572872 | tf_op jit(solution)/shard_map/ppermute | solution.py:349
  159.8 17.1 %copy-start.1 = (f32[32,64,128]{2,1,0:T(8,128)S(1)}, f32[32,64,128]{2,1,0:T(8,128)}, u32[]{:S(2)}) copy-start(f32[32,64,128]{2,1,0:T(8,128)} %left_products.2.refs_0_) | copy-start | bytes 3145732
  (5 other events, 4.5 us)

commit v4 on v3

v4 whole, which is shorter than its diff:
```python
import functools

import jax
import jax.numpy as jnp
from jax import lax
from jax.experimental import pallas as pl
from jax.experimental.pallas import tpu as pltpu
from jax.sharding import PartitionSpec as P

BLK = 128
CHUNKS = 2
STEP = 8
KEYS = 16
CORES = 2
VMEM_LIMIT = 48 * 1024 * 1024
PARAMS = pltpu.CompilerParams(vmem_limit_bytes=VMEM_LIMIT)
BY_LAST = (((1,), (1,)), ((), ()))


def identity(size):
    return (
        lax.broadcasted_iota(jnp.int32, (size, size), 0) == lax.broadcasted_iota(jnp.int32, (size, size), 1)
    ).astype(jnp.bfloat16)


def column(vector_ref, rows):
    return jnp.broadcast_to(vector_ref[...], (rows, vector_ref.shape[1])).T


def unit_mask(mask_ref, rows, cols):
    row, col = lax.axis_index("row"), lax.axis_index("col")
    return mask_ref[(row * rows) // BLK, (col * cols) // BLK].astype(jnp.float32)


def this_core():
    return lax.rem(lax.axis_index("col"), CORES)


def turn(pair, flipped, turned):
    flipped[...] = jnp.transpose(pair[...], (1, 0, 2))
    eye = identity(pair.shape[2])
    for key in range(pair.shape[1]):
        turned[key] = lax.dot_general(eye, flipped[key], BY_LAST, preferred_element_type=jnp.float32)


def normalize(values):
    centred = values - jnp.mean(values, axis=1, keepdims=True)
    inverse = lax.rsqrt(jnp.mean(centred * centred, axis=1, keepdims=True) + 1e-05)
    return centred * inverse, inverse


def set_columns(gain, bias, weight, gain_col, bias_col, weight_t):
    @pl.when(pl.program_id(0) == 0)
    def _():
        gain_col[...] = column(gain, gain_col.shape[1])
        bias_col[...] = column(bias, bias_col.shape[1])
        weight_t[...] = weight[...].astype(jnp.float32).T.astype(jnp.bfloat16)


def front_kernel(mask, pair, gain, bias, weight, mine, theirs, flipped, turned, normed, acts, whole, gain_col, bias_col, weight_t):
    rows, keys, _ = pair.shape
    hidden = weight.shape[1] // 2
    half = hidden // CORES
    set_columns(gain, bias, weight, gain_col, bias_col, weight_t)
    valid = unit_mask(mask, rows, pl.num_programs(0) * keys)
    turn(pair, flipped, turned)
    scaled, _ = normalize(turned[...])
    normed[...] = (scaled * gain_col[...] + bias_col[...]).astype(jnp.bfloat16)
    for key in range(keys):
        projected = jnp.dot(weight_t[...], normed[key], preferred_element_type=jnp.float32)
        acts[key] = (valid * jax.nn.sigmoid(projected[hidden:]) * projected[:hidden]).astype(jnp.bfloat16)
    whole[...] = jnp.transpose(acts[...], (1, 0, 2))
    core = this_core()
    mine[...] = whole[pl.ds(core * half, half)]
    theirs[...] = whole[pl.ds((1 - core) * half, half)]


def front(pair, gain, bias, proj_weight, tile_mask, side):
    rows, cols, chans = pair.shape
    width = proj_weight.shape[1] // 2
    half = width // 2 // CORES
    vector = pl.BlockSpec((1, chans), lambda g: (0, 0))
    return pl.pallas_call(
        front_kernel,
        out_shape=[jax.ShapeDtypeStruct((half, cols, rows), jnp.bfloat16)] * 2,
        grid=(cols // KEYS,),
        in_specs=[
            pl.BlockSpec(memory_space=pltpu.SMEM),
            pl.BlockSpec((rows, KEYS, chans), lambda g: (0, g, 0)),
            vector,
            vector,
            pl.BlockSpec((chans, width), lambda g: (0, side)),
        ],
        out_specs=[pl.BlockSpec((half, KEYS, rows), lambda g: (0, g, 0))] * 2,
        scratch_shapes=[
            pltpu.VMEM((KEYS, rows, chans), jnp.bfloat16),
            pltpu.VMEM((KEYS, chans, rows), jnp.float32),
            pltpu.VMEM((KEYS, chans, rows), jnp.bfloat16),
            pltpu.VMEM((KEYS, width // 2, rows), jnp.bfloat16),
            pltpu.VMEM((width // 2, KEYS, rows), jnp.bfloat16),
            pltpu.VMEM((chans, rows), jnp.float32),
            pltpu.VMEM((chans, rows), jnp.float32),
            pltpu.VMEM((width, chans), jnp.bfloat16),
        ],
        compiler_params=PARAMS,
        cost_estimate=pl.CostEstimate(
            flops=4 * rows * cols * chans * width, bytes_accessed=6 * rows * cols * chans, transcendentals=rows * cols * width
        ),
        name="left_front" if side == 0 else "right_front",
    )(tile_mask, pair, gain, bias, proj_weight)


def pack_kernel(own, other, *outs):
    cols, half, _ = other.shape
    part = half // len(outs)
    core = this_core()
    for block, place in ((own[:, pl.ds(pl.multiple_of(core * half, half), half), :], core), (other[...], 1 - core)):
        block = jnp.transpose(block, (1, 0, 2))
        for chunk, out in enumerate(outs):
            out[:, pl.ds(pl.multiple_of(place * cols, cols), cols), :] = block[chunk * part : (chunk + 1) * part]


def pack(own, other):
    cols, half, rows = other.shape
    return pl.pallas_call(
        pack_kernel,
        out_shape=[jax.ShapeDtypeStruct((half // CHUNKS, CORES * cols, rows), jnp.bfloat16)] * CHUNKS,
        compiler_params=PARAMS,
        cost_estimate=pl.CostEstimate(flops=0, bytes_accessed=10 * cols * half * rows, transcendentals=0),
        name="pack",
    )(own, other)


def partial_kernel(left_mine, left_other, *refs):
    blocks, out = refs[:-1], refs[-1]
    n = out.shape[0]
    row, chip = lax.axis_index("row"), lax.axis_index("col") // CORES
    for c in range(STEP):
        lhs = jnp.concatenate((left_mine[c], left_other[c]), axis=0)
        for m, block in enumerate(blocks):
            away = lax.rem(jnp.bitwise_xor(chip, m) - row + n, n)
            out[away, c] = lax.dot_general(lhs, block[c], BY_LAST, preferred_element_type=jnp.float32).astype(jnp.bfloat16)


def partial_products(left_mine, left_other, blocks, chunk):
    chans, rows, _ = blocks[0].shape
    ks = left_mine.shape[1]
    n = len(blocks)
    first = chunk * chans // STEP
    left = pl.BlockSpec((STEP, ks, rows), lambda g: (first + g, 0, 0))
    return pl.pallas_call(
        partial_kernel,
        out_shape=jax.ShapeDtypeStruct((n, chans, CORES * ks, rows), jnp.bfloat16),
        grid=(chans // STEP,),
        in_specs=[left, left] + [pl.BlockSpec((STEP, rows, rows), lambda g: (g, 0, 0))] * n,
        out_specs=pl.BlockSpec((n, STEP, CORES * ks, rows), lambda g: (0, g, 0, 0)),
        compiler_params=PARAMS,
        cost_estimate=pl.CostEstimate(
            flops=4 * chans * ks * rows * n * rows, bytes_accessed=2 * chans * rows * (n * rows + 2 * ks * (n + 1)), transcendentals=0
        ),
        name="right_partials",
    )(left_mine, left_other, *blocks)


def left_kernel(n, own, *refs):
    ups, downs, refs = refs[: n - 1], refs[n - 1 : 2 * n - 2], refs[2 * n - 2 :]
    blocks, (mine, theirs, panel) = refs[:n], refs[n:]
    row, chip = lax.axis_index("row"), lax.axis_index("col") // CORES
    ks = mine.shape[1]
    for c in range(STEP):
        for m, block in enumerate(blocks):
            panel[c, jnp.bitwise_xor(chip, m)] = block[c]
        acts, grads = [], []
        for s in range(n):
            grads.append(panel[c, lax.rem(row + s, n)])
            acts.append(own[c] if s == 0 else jnp.where(row + s < n, downs[s - 1][c], ups[n - s - 1][c]))
        out = jnp.dot(
            jnp.concatenate(acts, axis=1), jnp.concatenate(grads, axis=0), preferred_element_type=jnp.float32
        )
        mine[c] = out[:ks]
        theirs[c] = out[ks:].astype(jnp.bfloat16)


def left_products(own, ups, downs, blocks):
    chans, ks, rows = own.shape
    n = len(blocks)
    act = pl.BlockSpec((STEP, ks, rows), lambda g: (g, 0, 0))
    out = pl.BlockSpec((STEP, ks // CORES, rows), lambda g: (g, 0, 0))
    return pl.pallas_call(
        functools.partial(left_kernel, n),
        out_shape=[
            jax.ShapeDtypeStruct((chans, ks // CORES, rows), jnp.float32),
            jax.ShapeDtypeStruct((chans, ks // CORES, rows), jnp.bfloat16),
        ],
        grid=(chans // STEP,),
        in_specs=[act] * (2 * n - 1) + [pl.BlockSpec((STEP, rows, rows), lambda g: (g, 0, 0))] * n,
        out_specs=[out] * 2,
        scratch_shapes=[pltpu.VMEM((STEP, n, rows, rows), jnp.bfloat16)],
        compiler_params=PARAMS,
        cost_estimate=pl.CostEstimate(
            flops=2 * chans * ks * rows * n * rows, bytes_accessed=2 * chans * rows * (n * rows + ks * (2 * n + 1)), transcendentals=0
        ),
        name="left_products",
    )(own, *ups, *downs, *blocks)


def tail_kernel(mask, pair, gain, bias, weight, *refs):
    groups = [refs[i * CHUNKS : (i + 1) * CHUNKS] for i in range(6)]
    left_mine, left_other, partials, ups, downs, right_other = groups
    out, flipped, turned, normed, inverses, grads, right_flat, left_flat, gain_col, bias_col, weight_t = refs[6 * CHUNKS :]
    rows, keys, _ = pair.shape
    hidden = weight.shape[1] // 4
    half = hidden // CORES
    part = half // CHUNKS
    core = this_core()
    set_columns(gain, bias, weight, gain_col, bias_col, weight_t)
    valid = unit_mask(mask, rows, pl.num_programs(0) * keys)

    def put(flat, owner, chunk, value):
        first = pl.multiple_of((owner * half + chunk * part) * keys, part * keys)
        flat[pl.ds(first, part * keys), :] = value.astype(jnp.float32).reshape(part * keys, rows)

    for chunk in range(CHUNKS):
        own, up, down = (ref[chunk][...].astype(jnp.float32) for ref in (partials, ups, downs))
        put(right_flat, core, chunk, own[0] + up + down)
        put(right_flat, 1 - core, chunk, right_other[chunk][...])
        put(left_flat, core, chunk, left_mine[chunk][...])
        put(left_flat, 1 - core, chunk, left_other[chunk][...])
    turn(pair, flipped, turned)
    scaled, inverse = normalize(turned[...])
    turned[...] = scaled
    inverses[...] = inverse
    normed[...] = (scaled * gain_col[...] + bias_col[...]).astype(jnp.bfloat16)
    for key in range(keys):
        projected = jnp.dot(weight_t[...], normed[key], preferred_element_type=jnp.float32)
        for side, source in enumerate((left_flat, right_flat)):
            lin = projected[2 * side * hidden : (2 * side + 1) * hidden]
            sig = jax.nn.sigmoid(projected[(2 * side + 1) * hidden : (2 * side + 2) * hidden])
            through = source[pl.ds(key, hidden, stride=keys), :] * valid * sig
            grads[key, 2 * side * hidden : (2 * side + 1) * hidden, :] = through.astype(jnp.bfloat16)
            grads[key, (2 * side + 1) * hidden : (2 * side + 2) * hidden, :] = (through * lin * (1.0 - sig)).astype(
                jnp.bfloat16
            )
    for key in range(keys):
        scaled = turned[key]
        scaled_grad = jnp.dot(weight[...], grads[key], preferred_element_type=jnp.float32) * gain_col[...]
        result = inverses[key] * (
            scaled_grad
            - jnp.mean(scaled_grad, axis=0, keepdims=True)
            - scaled * jnp.mean(scaled_grad * scaled, axis=0, keepdims=True)
        )
        normed[key] = result.astype(jnp.bfloat16)
    eye = identity(rows)
    for key in range(keys):
        flipped[key] = lax.dot_general(eye, normed[key], BY_LAST, preferred_element_type=jnp.float32).astype(jnp.bfloat16)
    out[...] = jnp.transpose(flipped[...], (1, 0, 2))


def tail(pair, gain, bias, proj_weight, tile_mask, left_mine, left_other, partials, ups, downs, right_other):
    rows, cols, chans = pair.shape
    width = proj_weight.shape[1]
    part = width // 4 // CORES // CHUNKS
    vector = pl.BlockSpec((1, chans), lambda g: (0, 0))
    cells = pl.BlockSpec((rows, KEYS, chans), lambda g: (0, g, 0))
    small = [pl.BlockSpec((part, KEYS, rows), lambda g: (0, g, 0))] * CHUNKS
    first = [pl.BlockSpec((1, part, KEYS, rows), lambda g: (0, 0, g, 0))] * CHUNKS
    return pl.pallas_call(
        tail_kernel,
        out_shape=jax.ShapeDtypeStruct(pair.shape, jnp.bfloat16),
        grid=(cols // KEYS,),
        in_specs=[
            pl.BlockSpec(memory_space=pltpu.SMEM),
            cells,
            vector,
            vector,
            pl.BlockSpec((chans, width), lambda g: (0, 0)),
        ]
        + small * 2
        + first
        + small * 3,
        out_specs=cells,
        scratch_shapes=[
            pltpu.VMEM((KEYS, rows, chans), jnp.bfloat16),
            pltpu.VMEM((KEYS, chans, rows), jnp.float32),
            pltpu.VMEM((KEYS, chans, rows), jnp.bfloat16),
            pltpu.VMEM((KEYS, 1, rows), jnp.float32),
            pltpu.VMEM((KEYS, width, rows), jnp.bfloat16),
            pltpu.VMEM((width // 4 * KEYS, rows), jnp.float32),
            pltpu.VMEM((width // 4 * KEYS, rows), jnp.float32),
            pltpu.VMEM((chans, rows), jnp.float32),
            pltpu.VMEM((chans, rows), jnp.float32),
            pltpu.VMEM((width, chans), jnp.bfloat16),
        ],
        compiler_params=PARAMS,
        cost_estimate=pl.CostEstimate(
            flops=8 * rows * cols * chans * width, bytes_accessed=10 * rows * cols * chans, transcendentals=rows * cols * width
        ),
        name="tail",
    )(tile_mask, pair, gain, bias, proj_weight, *left_mine, *left_other, *partials, *ups, *downs, *right_other)


def after(value, *others):
    return lax.optimization_barrier((value, others))[0]


def shards(pair, grad_x, norm_gain, norm_bias, proj_weight, tile_mask):
    n, n_col = lax.axis_size("row"), lax.axis_size("col")
    row = lax.axis_index("row")
    half = grad_x.shape[2] // CORES
    part = half // CHUNKS
    gain, bias = norm_gain[None, :], norm_bias[None, :]

    def exchange(value, mask):
        return lax.ppermute(value, "col", [(d, d ^ mask) for d in range(n_col)])

    def step_up(value):
        return lax.ppermute(value, "row", [(r, r + 1) for r in range(n - 1)])

    def step_down(value):
        return lax.ppermute(value, "row", [(r + 1, r) for r in range(n - 1)])

    raw = jnp.transpose(grad_x, (1, 2, 0))
    other = exchange(lax.dynamic_slice_in_dim(raw, (1 - this_core()) * half, half, 1), 1)
    right_mine, right_theirs = front(pair, gain, bias, proj_weight, tile_mask, 1)
    packed = pack(raw, after(other, right_mine))
    right_other = exchange(right_theirs, 1)
    owns = [
        jnp.concatenate((right_mine[c * part : (c + 1) * part], right_other[c * part : (c + 1) * part]), axis=1)
        for c in range(CHUNKS)
    ]
    left_mine, left_theirs = front(after(pair, owns), gain, bias, proj_weight, tile_mask, 0)
    left_other = exchange(left_theirs, 1)

    bits = [1 << b for b in range(n_col.bit_length() - 2)]
    panels = []
    for c, own in enumerate(packed):
        slots = {0: own}
        order = bits[c % len(bits) :] + bits[: c % len(bits)]
        for bit in order:
            for m in list(slots):
                value = slots[m]
                if c == 0 and m > 0:
                    value = after(value, left_mine)
                if c > 0 and m == 0:
                    value = after(value, panels[-1][bit] if bit != order[0] else panels[-1][1:])
                slots[m | bit] = exchange(value, CORES * bit)
        panels.append([slots[m] for m in range(len(slots))])

    ups, downs, partials = [], [], []
    for c in range(CHUNKS):
        own = owns[c] if c == 0 else after(owns[c], ups[0][0], downs[0][0])
        ups.append([step_up(own)])
        downs.append([step_down(own)])
    for c in range(CHUNKS):
        partials.append(partial_products(left_mine, left_other, panels[c], c))

    def plus(arrived, sums, use):
        return (arrived.astype(jnp.float32) + jnp.where(use, sums.astype(jnp.float32), 0.0)).astype(jnp.bfloat16)

    for t in range(1, n):
        for c in range(CHUNKS):
            ups[c].append(step_up(plus(ups[c][-1], partials[c][n - t], row < t)))
            downs[c].append(step_down(plus(downs[c][-1], partials[c][t], row >= n - t)))

    left_grads = []
    for c in range(CHUNKS):
        own = after(owns[c], ups[-1][n - 2], downs[-1][n - 2])
        left_grads.append(left_products(own, ups[c][: n - 1], downs[c][: n - 1], panels[c]))
    left_grad_other = [exchange(theirs, 1) for _, theirs in left_grads]
    ks = left_mine.shape[1]
    right_grad_other = []
    for c in range(CHUNKS):
        total = sum(v[:, ks:].astype(jnp.float32) for v in (partials[c][0], ups[c][-1], downs[c][-1]))
        right_grad_other.append(exchange(total.astype(jnp.bfloat16), 1))

    return tail(
        pair,
        gain,
        bias,
        proj_weight,
        tile_mask,
        [mine for mine, _ in left_grads],
        left_grad_other,
        partials,
        [u[-1] for u in ups],
        [d[-1] for d in downs],
        right_grad_other,
    )


def solution(mesh):
    placed = (P("row", "col", None), P("row", "col", None), P(), P(), P(), P())
    return jax.shard_map(
        shards, mesh=mesh, in_specs=placed, out_specs=P("row", "col", None), check_vma=False
    )
```

time: 190 us -> 160 us (0.84)
  waiting for transfers between devices: 67.5 us -> 47.5 us
  starting transfers between devices: 73.1 us -> 57.2 us
  local copies, waits for them, and re-layouts: 5.55 us -> 13.8 us
  Pallas kernels: 38.3 us -> 31.4 us
  other arithmetic: 4.56 us -> 8.36 us
    ppermute x24 -> x16, waiting for transfers between devices: 44.9 us -> 26.3 us  [the longest x8 17.1 us: step_up(): return lax.ppermute(value, 'row', [(r, r + 1) for r in range(n - 1)])]
    ppermute x24 -> x16, starting transfers between devices: 62 us -> 45.4 us  [the longest x8 34.6 us: step_up(): return lax.ppermute(value, 'row', [(r, r + 1) for r in range(n - 1)])]
    unnamed x31 -> x66, local copies, waits for them, and re-layouts: 5.48 us -> 12.4 us
    pallas_call x6 -> x7, Pallas kernels: 27 us -> 20.2 us  [the longest x2 9.36 us: front(): pl.pallas_call(front_kernel, out_shape=[jax.ShapeDtypeStruct((half, cols,...]
    convert_element_type x6 -> x8, other arithmetic: 4.56 us -> 7.43 us  [the longest x6 7.21 us: plus(): (arrived.astype(jnp.float32) + jnp.where(use, sums.astype(jnp.float32), 0...]
    ppermute x14 -> x13, waiting for transfers between devices: 22.5 us -> 21.1 us  [exchange(): return lax.ppermute(value, 'col', [(d, d ^ mask) for d in range(n_col)])]
    ppermute x14 -> x13, starting transfers between devices: 11.1 us -> 11.9 us  [exchange(): return lax.ppermute(value, 'col', [(d, d ^ mask) for d in range(n_col)])]
  transfers between devices with their start and end apart: 38 -> 29, of which waited for: 12 -> 13; matrix products, arithmetic and copies ran while one was open for 2% -> 5% of each run, Pallas kernels for 14% -> 13%
where the time goes in v4:
time: 160 us; the launch traced here: 159 us
  starting transfers between devices  57.2 us (36%)
  waiting for transfers between devices  47.5 us (30%)
  Pallas kernels  31.4 us (20%)
  local copies, waits for them, and re-layouts  13.8 us (9%)
  other arithmetic  8.36 us (5%)
    ppermute x8, starting transfers between devices, step_up(): return lax.ppermute(value, 'row', [(r, r + 1) for r in range(n - 1)])  34.6 us
    ppermute x13, waiting for transfers between devices, exchange(): return lax.ppermute(value, 'col', [(d, d ^ mask) for d in range(n_col)])  21.1 us
    ppermute x8, waiting for transfers between devices, step_up(): return lax.ppermute(value, 'row', [(r, r + 1) for r in range(n - 1)])  17.1 us
    unnamed x66, local copies, waits for them, and re-layouts  12.4 us
    ppermute x13, starting transfers between devices, exchange(): return lax.ppermute(value, 'col', [(d, d ^ mask) for d in range(n_col)])  11.9 us
    pallas_call x1, Pallas kernels, tail(): pl.pallas_call(tail_kernel, out_shape=jax.ShapeDtypeStruct(pair.shape, jn...  11.2 us
    ppermute x8, starting transfers between devices, step_down(): return lax.ppermute(value, 'row', [(r + 1, r) for r in range(n - 1)])  10.7 us
    pallas_call x2, Pallas kernels, front(): pl.pallas_call(front_kernel, out_shape=[jax.ShapeDtypeStruct((half, cols,...  9.36 us
  transfers between devices with their start and end apart: 29, of which 13 were waited for; matrix products, arithmetic and copies ran while one was open for 5% of the time, Pallas kernels for 13%

profile of v4, /device:TPU:0, one launch (start us, length us, event | category | flops | bytes accessed | tf_op | source)
XLA Modules:
  0.0 158.8 jit_solution(17664910097465162622)
XLA Ops:
  0.0 1.2 dynamic-slice_bitcast_fusion
  1.7 1.6 %copy-done.3 = bf16[128,64,128]{2,1,0:T(8,128)(2,1)S(1)} copy-done((bf16[128,64,128]{2,1,0:T(8,128)(2,1)S(1)}, bf16[128,64,128]{2,1,0:T(8,128)(2,1)}, u32[]{:S(2)}) %copy-start.3) | copy-done | bytes 2097176
  6.1 4.7 %right_front.1 = (bf16[32,64,128]{2,1,0:T(8,128)(2,1)S(1)}, bf16[32,64,128]{2,1,0:T(8,128)(2,1)S(1)}) custom-call(s32[4,4]{1,0:T(4,128)S(1)} %copy-done.27, bf16[128,64,128]{2,1,0:T(8,128)(2,1)S(1)} %copy-done.3, f32[1,128]{1,0:T(1,128)S(1)} %bitcast.82, f32[1,128]{1,0:T(1,128)S(1)} %bitcast.85, bf16[128,256]{1,0:T(8,128)(2,1)S(1)} %copy-done.25), custom_call_target="tpu_custom_call" | custom-call | flops 536870912 | bytes 6291456 | tf_op jit(solution)/shard_map/right_front/pallas_call | solution.py:83
  11.0 1.2 pack.1
  12.3 2.9 %collective-permute-start.6 = (bf16[16,128,128]{2,1,0:T(8,128)(2,1)S(1)}, bf16[16,128,128]{2,1,0:T(8,128)(2,1)S(1)}, u32[]{:S(2)}, u32[]{:S(2)}) collective-permute-start(bf16[16,128,128]{2,1,0:T(8,128)(2,1)S(1)} %get-tuple-element.31.refs_0_.refs_6_), channel_id=1, source_target_pairs={{0,2},{1,3},{2,0},{3,1},{4,6},{5,7},{6,4},{7,5},{8,10},{9,11},{10,... | collective-permute-start | bytes 1572872 | tf_op jit(solution)/shard_map/ppermute | solution.py:314
  15.2 1.5 collective-permute-start.8
  17.7 4.7 %left_front.1 = (bf16[32,64,128]{2,1,0:T(8,128)(2,1)S(1)}, bf16[32,64,128]{2,1,0:T(8,128)(2,1)S(1)}) custom-call(s32[4,4]{1,0:T(4,128)S(1)} %copy-done.27, bf16[128,64,128]{2,1,0:T(8,128)(2,1)S(1)} %copy-done.4, f32[1,128]{1,0:T(1,128)S(1)} %bitcast.83, f32[1,128]{1,0:T(1,128)S(1)} %bitcast.86, bf16[128,256]{1,0:T(8,128)(2,1)S(1)} %copy-done.26), custom_call_target="tpu_custom_call" | custom-call | flops 536870912 | bytes 6291456 | tf_op jit(solution)/shard_map/left_front/pallas_call | solution.py:83
  22.4 4.9 %collective-permute-done.6.refs_1_.refs_7_ = bf16[16,128,128]{2,1,0:T(8,128)(2,1)S(1)} collective-permute-done((bf16[16,128,128]{2,1,0:T(8,128)(2,1)S(1)}, bf16[16,128,128]{2,1,0:T(8,128)(2,1)S(1)}, u32[]{:S(2)}, u32[]{:S(2)}) %collective-permute-start.6) | collective-permute-done | bytes 524320 | tf_op jit(solution)/shard_map/ppermute | solution.py:314
  27.3 1.8 %collective-permute-start.9 = (bf16[16,128,128]{2,1,0:T(8,128)(2,1)S(1)}, bf16[16,128,128]{2,1,0:T(8,128)(2,1)S(1)}, u32[]{:S(2)}, u32[]{:S(2)}) collective-permute-start(bf16[16,128,128]{2,1,0:T(8,128)(2,1)S(1)} %collective-permute-done.6.refs_1_.refs_7_), channel_id=1, source_target_pairs={{0,4},{1,5},{2,6},{3,7},{4,0},{5,1},{6,2},{7,3},{8,12},{9,13},{10,... | collective-permute-start | bytes 1572872 | tf_op jit(solution)/shard_map/ppermute | solution.py:314
  30.7 9.9 %collective-permute-done.9.refs_3_.refs_9_ = bf16[16,128,128]{2,1,0:T(8,128)(2,1)S(1)} collective-permute-done((bf16[16,128,128]{2,1,0:T(8,128)(2,1)S(1)}, bf16[16,128,128]{2,1,0:T(8,128)(2,1)S(1)}, u32[]{:S(2)}, u32[]{:S(2)}) %collective-permute-start.9) | collective-permute-done | bytes 524320 | tf_op jit(solution)/shard_map/ppermute | solution.py:314
  41.5 1.5 collective-permute-start.10
  42.9 3.5 %collective-permute-start.1 = (bf16[16,128,128]{2,1,0:T(8,128)(2,1)S(1)}, bf16[16,128,128]{2,1,0:T(8,128)(2,1)S(1)}, u32[]{:S(2)}, u32[]{:S(2)}) collective-permute-start(bf16[16,128,128]{2,1,0:T(8,128)(2,1)S(1)} %pad_maximum_fusion.own), channel_id=1, source_target_pairs={{0,8},{8,16},{16,24},{1,9},{9,17},{17,25},{2,10},{10,18},{18,26},{... | collective-permute-start | bytes 1572872 | tf_op jit(solution)/shard_map/ppermute | solution.py:317
  46.5 1.3 collective-permute-start.2
  47.8 1.6 collective-permute-start.7
  49.4 4.8 %collective-permute-done.10.refs_2_.refs_8_ = bf16[16,128,128]{2,1,0:T(8,128)(2,1)} collective-permute-done((bf16[16,128,128]{2,1,0:T(8,128)(2,1)}, bf16[16,128,128]{2,1,0:T(8,128)(2,1)}, u32[]{:S(2)}, u32[]{:S(2)}) %collective-permute-start.10) | collective-permute-done | bytes 524320 | tf_op jit(solution)/shard_map/ppermute | solution.py:314
  54.2 1.1 collective-permute-start.11
  55.7 4.1 %collective-permute-done.2.refs_3_ = bf16[16,128,128]{2,1,0:T(8,128)(2,1)S(1)} collective-permute-done((bf16[16,128,128]{2,1,0:T(8,128)(2,1)S(1)}, bf16[16,128,128]{2,1,0:T(8,128)(2,1)S(1)}, u32[]{:S(2)}, u32[]{:S(2)}) %collective-permute-start.2) | collective-permute-done | bytes 524320 | tf_op jit(solution)/shard_map/ppermute | solution.py:320
  59.9 1.3 collective-permute-start.14
  61.2 5.4 %collective-permute-start.3 = (bf16[16,128,128]{2,1,0:T(8,128)(2,1)}, bf16[16,128,128]{2,1,0:T(8,128)(2,1)}, u32[]{:S(2)}, u32[]{:S(2)}) collective-permute-start(bf16[16,128,128]{2,1,0:T(8,128)(2,1)} %pad_maximum_fusion.1.own), channel_id=1, source_target_pairs={{0,8},{8,16},{16,24},{1,9},{9,17},{17,25},{2,10},{10,18},{18,26},{... | collective-permute-start | bytes 1572872 | tf_op jit(solution)/shard_map/ppermute | solution.py:317
  66.6 1.0 copy-done.7
  69.7 1.0 copy-done.16
  70.8 1.9 %right_partials.3.refs_4_ = bf16[4,16,128,128]{3,2,1,0:T(8,128)(2,1)S(1)} custom-call(bf16[32,64,128]{2,1,0:T(8,128)(2,1)S(1)} %get-tuple-element.27.left_mine, bf16[32,64,128]{2,1,0:T(8,128)(2,1)S(1)} %collective-permute-done.4.left_other, bf16[16,128,128]{2,1,0:T(8,128)(2,1)S(1)} %copy-done.7, bf16[16,128,128]{2,1,0:T(8,128)(2,1)S(1)} %copy-done.10, ...), custom_call_target="tpu_custom_call" | custom-call | flops 268435456 | bytes 4718592 | tf_op jit(solution)/shard_map/right_partials/pallas_call | solution.py:151
  72.7 1.7 %fusion.32 = (bf16[16,128,128]{2,1,0:T(8,128)(2,1)}, bf16[16,128,128]{2,1,0:T(8,128)(2,1)}) fusion(bf16[16,128,128]{2,1,0:T(8,128)(2,1)S(1)} %copy-done.23, pred[]{:T(512)S(6)} %ge.12, bf16[4,16,128,128]{3,2,1,0:T(8,128)(2,1)S(1)} %right_partials.3.refs_4_, pred[]{:T(512)S(6)} %lt.15, bf16[16,128,128]{2,1,0:T(8,128)(2,1)S(1)} %copy-done.20), kind=kLoop, calls=%fused_computation.44 | loop fusion | flops 2621440 | bytes 3145730 | tf_op jit(solution)/shard_map/convert_element_type | solution.py:358
  74.3 3.4 %collective-permute-start.17 = (bf16[16,128,128]{2,1,0:T(8,128)(2,1)}, bf16[16,128,128]{2,1,0:T(8,128)(2,1)}, u32[]{:S(2)}, u32[]{:S(2)}) collective-permute-start(bf16[16,128,128]{2,1,0:T(8,128)(2,1)} %get-tuple-element.48), channel_id=1, source_target_pairs={{0,8},{8,16},{16,24},{1,9},{9,17},{17,25},{2,10},{10,18},{18,26},{... | collective-permute-start | bytes 1572872 | tf_op jit(solution)/shard_map/ppermute | solution.py:317
  77.8 1.3 collective-permute-start.19
  79.1 3.1 %right_partials.2.refs_5_ = bf16[4,16,128,128]{3,2,1,0:T(8,128)(2,1)S(1)} custom-call(bf16[32,64,128]{2,1,0:T(8,128)(2,1)S(1)} %get-tuple-element.27.left_mine, bf16[32,64,128]{2,1,0:T(8,128)(2,1)S(1)} %collective-permute-done.4.left_other, bf16[16,128,128]{2,1,0:T(8,128)(2,1)} %get-tuple-element.34.refs_0_.refs_6_, ...), custom_call_target="tpu_custom_call" | custom-call | flops 268435456 | bytes 4718592 | tf_op jit(solution)/shard_map/right_partials/pallas_call | solution.py:151
  82.2 1.3 copy-done.1
  83.5 2.7 %fusion.14 = (bf16[16,128,128]{2,1,0:T(8,128)(2,1)}, bf16[16,128,128]{2,1,0:T(8,128)(2,1)}) fusion(bf16[16,128,128]{2,1,0:T(8,128)(2,1)} %collective-permute-done.14.refs_3_, pred[]{:T(512)S(6)} %ge.12, bf16[4,16,128,128]{3,2,1,0:T(8,128)(2,1)S(1)} %right_partials.2.refs_5_, pred[]{:T(512)S(6)} %lt.15, bf16[16,128,128]{2,1,0:T(8,128)(2,1)} %collective-permute-done.3.refs_0_), kind=kLoop, calls=%fused_computation.26 | loop fusion | flops 2621440 | bytes 3145730 | tf_op jit(solution)/shard_map/convert_element_type | solution.py:358
  86.2 1.3 collective-permute-start.15
  87.5 5.2 %collective-permute-start.12 = (bf16[16,128,128]{2,1,0:T(8,128)(2,1)}, bf16[16,128,128]{2,1,0:T(8,128)(2,1)S(1)}, u32[]{:S(2)}, u32[]{:S(2)}) collective-permute-start(bf16[16,128,128]{2,1,0:T(8,128)(2,1)} %get-tuple-element.52), channel_id=1, source_target_pairs={{0,8},{8,16},{16,24},{1,9},{9,17},{17,25},{2,10},{10,18},{18,26},{... | collective-permute-start | bytes 1572872 | tf_op jit(solution)/shard_map/ppermute | solution.py:317
  92.7 1.7 %fusion.29 = (bf16[16,128,128]{2,1,0:T(8,128)(2,1)S(1)}, bf16[16,128,128]{2,1,0:T(8,128)(2,1)S(1)}) fusion(bf16[16,128,128]{2,1,0:T(8,128)(2,1)} %collective-permute-done.19.refs_4_, pred[]{:T(512)S(6)} %ge.13, bf16[4,16,128,128]{3,2,1,0:T(8,128)(2,1)S(1)} %right_partials.3.refs_4_, pred[]{:T(512)S(6)} %lt.17, ...), kind=kLoop, calls=%fused_computation.41 | loop fusion | flops 2359296 | bytes 2621442 | tf_op jit(solution)/shard_map/convert_element_type | solution.py:358
  94.4 3.9 %collective-permute-start.18 = (bf16[16,128,128]{2,1,0:T(8,128)(2,1)S(1)}, bf16[16,128,128]{2,1,0:T(8,128)(2,1)S(1)}, u32[]{:S(2)}, u32[]{:S(2)}) collective-permute-start(bf16[16,128,128]{2,1,0:T(8,128)(2,1)S(1)} %get-tuple-element.46), channel_id=1, source_target_pairs={{0,8},{8,16},{16,24},{1,9},{9,17},{17,25},{2,10},{10,18},{18,26},{... | collective-permute-start | bytes 1572872 | tf_op jit(solution)/shard_map/ppermute | solution.py:317
  98.3 1.3 collective-permute-start.20
  99.6 4.1 %collective-permute-done.15.refs_4_ = bf16[16,128,128]{2,1,0:T(8,128)(2,1)S(1)} collective-permute-done((bf16[16,128,128]{2,1,0:T(8,128)(2,1)}, bf16[16,128,128]{2,1,0:T(8,128)(2,1)S(1)}, u32[]{:S(2)}, u32[]{:S(2)}) %collective-permute-start.15) | collective-permute-done | bytes 524320 | tf_op jit(solution)/shard_map/ppermute | solution.py:320
  103.7 1.6 collective-permute-done.12.refs_1_
  105.6 4.3 %collective-permute-start.13 = (bf16[16,128,128]{2,1,0:T(8,128)(2,1)S(1)}, bf16[16,128,128]{2,1,0:T(8,128)(2,1)S(1)}, u32[]{:S(2)}, u32[]{:S(2)}) collective-permute-start(bf16[16,128,128]{2,1,0:T(8,128)(2,1)S(1)} %get-tuple-element.50), channel_id=1, source_target_pairs={{0,8},{8,16},{16,24},{1,9},{9,17},{17,25},{2,10},{10,18},{18,26},{... | collective-permute-start | bytes 1572872 | tf_op jit(solution)/shard_map/ppermute | solution.py:317
  110.0 1.3 collective-permute-start.16
  111.3 5.1 %collective-permute-done.18.refs_2_ = bf16[16,128,128]{2,1,0:T(8,128)(2,1)S(1)} collective-permute-done((bf16[16,128,128]{2,1,0:T(8,128)(2,1)S(1)}, bf16[16,128,128]{2,1,0:T(8,128)(2,1)S(1)}, u32[]{:S(2)}, u32[]{:S(2)}) %collective-permute-start.18) | collective-permute-done | bytes 524320 | tf_op jit(solution)/shard_map/ppermute | solution.py:317
  116.8 4.4 %collective-permute-start.23 = (bf16[16,128,128]{2,1,0:T(8,128)(2,1)S(1)}, bf16[16,128,128]{2,1,0:T(8,128)(2,1)S(1)}, u32[]{:S(2)}, u32[]{:S(2)}) collective-permute-start(bf16[16,128,128]{2,1,0:T(8,128)(2,1)S(1)} %get-tuple-element.44), channel_id=1, source_target_pairs={{0,8},{8,16},{16,24},{1,9},{9,17},{17,25},{2,10},{10,18},{18,26},{... | collective-permute-start | bytes 1572872 | tf_op jit(solution)/shard_map/ppermute | solution.py:317
  121.3 1.6 collective-permute-start.25
  122.9 4.8 %collective-permute-done.13.refs_2_ = bf16[16,128,128]{2,1,0:T(8,128)(2,1)S(1)} collective-permute-done((bf16[16,128,128]{2,1,0:T(8,128)(2,1)S(1)}, bf16[16,128,128]{2,1,0:T(8,128)(2,1)S(1)}, u32[]{:S(2)}, u32[]{:S(2)}) %collective-permute-start.13) | collective-permute-done | bytes 524320 | tf_op jit(solution)/shard_map/ppermute | solution.py:317
  128.1 4.4 %collective-permute-start.24 = (bf16[16,128,128]{2,1,0:T(8,128)(2,1)S(1)}, bf16[16,128,128]{2,1,0:T(8,128)(2,1)S(1)}, u32[]{:S(2)}, u32[]{:S(2)}) collective-permute-start(bf16[16,128,128]{2,1,0:T(8,128)(2,1)S(1)} %get-tuple-element.42), channel_id=1, source_target_pairs={{0,8},{8,16},{16,24},{1,9},{9,17},{17,25},{2,10},{10,18},{18,26},{... | collective-permute-start | bytes 1572872 | tf_op jit(solution)/shard_map/ppermute | solution.py:317
  132.6 1.5 collective-permute-start.26
  134.1 4.8 %collective-permute-done.23.refs_6_ = bf16[16,128,128]{2,1,0:T(8,128)(2,1)S(1)} collective-permute-done((bf16[16,128,128]{2,1,0:T(8,128)(2,1)S(1)}, bf16[16,128,128]{2,1,0:T(8,128)(2,1)S(1)}, u32[]{:S(2)}, u32[]{:S(2)}) %collective-permute-start.23) | collective-permute-done | bytes 524320 | tf_op jit(solution)/shard_map/ppermute | solution.py:317
  139.2 2.2 %left_products.2 = (f32[16,64,128]{2,1,0:T(8,128)S(1)}, bf16[16,64,128]{2,1,0:T(8,128)(2,1)S(1)}) custom-call(bf16[16,128,128]{2,1,0:T(8,128)(2,1)S(1)} %copy-done.18, bf16[16,128,128]{2,1,0:T(8,128)(2,1)S(1)} %copy-done.21, bf16[16,128,128]{2,1,0:T(8,128)(2,1)} %collective-permute-done.17.refs_1_, ...), custom_call_target="tpu_custom_call" | custom-call | flops 268435456 | bytes 6815744 | tf_op jit(solution)/shard_map/left_products/pallas_call | solution.py:189
  141.9 2.5 %left_products.3 = (f32[16,64,128]{2,1,0:T(8,128)S(1)}, bf16[16,64,128]{2,1,0:T(8,128)(2,1)S(1)}) custom-call(bf16[16,128,128]{2,1,0:T(8,128)(2,1)} %pad_maximum_fusion.1.own, bf16[16,128,128]{2,1,0:T(8,128)(2,1)} %collective-permute-done.3.refs_0_, bf16[16,128,128]{2,1,0:T(8,128)(2,1)S(1)} %collective-permute-done.12.refs_1_, ...), custom_call_target="tpu_custom_call" | custom-call | flops 268435456 | bytes 6815744 | tf_op jit(solution)/shard_map/left_products/pallas_call | solution.py:189
  146.1 1.5 collective-permute-done.28.refs_11_
  147.6 11.2 %tail.1 = bf16[128,64,128]{2,1,0:T(8,128)(2,1)} custom-call(s32[4,4]{1,0:T(4,128)S(1)} %copy-done.28, bf16[128,64,128]{2,1,0:T(8,128)(2,1)} %pair.4, f32[1,128]{1,0:T(1,128)S(1)} %bitcast.84, f32[1,128]{1,0:T(1,128)S(1)} %bitcast.87, bf16[128,256]{1,0:T(8,128)(2,1)S(1)} %copy-done.26, f32[16,64,128]{2,1,0:T(8,128)S(1)} %get-tuple-element.36.refs_0_, ...), custom_call_target="tpu_custom_call" | custom-call | flops 2147483648 | bytes 10485760 | tf_op jit(solution)/shard_map/tail/pallas_call | solution.py:267
  (99 shorter events, 13.3 us)
Async XLA Ops:
  0.0 11.0 %copy-start.5 = (bf16[128,64,64]{0,2,1:T(8,128)(2,1)S(1)}, bf16[128,64,64]{0,2,1:T(8,128)(2,1)}, u32[]{:S(2)}) copy-start(bf16[128,64,64]{0,2,1:T(8,128)(2,1)} %param.7) | copy-start | bytes 3145732
  1.2 9.8 %collective-permute-start.5 = (bf16[64,32,128]{2,1,0:T(8,128)(2,1)S(1)}, bf16[64,32,128]{2,1,0:T(8,128)(2,1)S(1)}, u32[]{:S(2)}, u32[]{:S(2)}) collective-permute-start(bf16[64,32,128]{2,1,0:T(8,128)(2,1)S(1)} %dynamic-slice_bitcast_fusion), channel_id=1, source_target_pairs={{0,1},{1,0},{2,3},{3,2},{4,5},{5,4},{6,7},{7,6},{8,9},{9,8},{10,11... | collective-permute-start | bytes 1572872 | tf_op jit(solution)/shard_map/ppermute | solution.py:314
  10.8 5.9 %collective-permute-start = (bf16[32,64,128]{2,1,0:T(8,128)(2,1)S(1)}, bf16[32,64,128]{2,1,0:T(8,128)(2,1)S(1)}, u32[]{:S(2)}, u32[]{:S(2)}) collective-permute-start(bf16[32,64,128]{2,1,0:T(8,128)(2,1)S(1)} %get-tuple-element.24), channel_id=1, source_target_pairs={{0,1},{1,0},{2,3},{3,2},{4,5},{5,4},{6,7},{7,6},{8,9},{9,8},{10,11... | collective-permute-start | bytes 1572872 | tf_op jit(solution)/shard_map/ppermute | solution.py:314
  11.0 6.7 %copy-start.4 = (bf16[128,64,128]{2,1,0:T(8,128)(2,1)S(1)}, bf16[128,64,128]{2,1,0:T(8,128)(2,1)}, u32[]{:S(2)}) copy-start(bf16[128,64,128]{2,1,0:T(8,128)(2,1)} %pair.4) | copy-start | bytes 6291460
  11.0 6.7 %copy-start.26 = (bf16[128,256]{1,0:T(8,128)(2,1)S(1)}, bf16[128,256]{1,0:T(8,128)(2,1)}, u32[]{:S(2)}) copy-start(bf16[128,256]{1,0:T(8,128)(2,1)} %weight.5) | copy-start | bytes 196612
  11.0 6.7 %copy-start.30 = (f32[128]{0:T(128)S(1)}, f32[128]{0:T(128)}, u32[]{:S(2)}) copy-start(f32[128]{0:T(128)} %param.8) | copy-start | bytes 1540
  11.0 6.7 %copy-start.32 = (f32[128]{0:T(128)S(1)}, f32[128]{0:T(128)}, u32[]{:S(2)}) copy-start(f32[128]{0:T(128)} %param.9) | copy-start | bytes 1540
  12.3 10.2 %copy-start.6 = (bf16[16,128,128]{2,1,0:T(8,128)(2,1)}, bf16[16,128,128]{2,1,0:T(8,128)(2,1)S(1)}, u32[]{:S(2)}) copy-start(bf16[16,128,128]{2,1,0:T(8,128)(2,1)S(1)} %get-tuple-element.31.refs_0_.refs_6_) | copy-start | bytes 1572868
  12.3 15.0 %collective-permute-start.6 = (bf16[16,128,128]{2,1,0:T(8,128)(2,1)S(1)}, bf16[16,128,128]{2,1,0:T(8,128)(2,1)S(1)}, u32[]{:S(2)}, u32[]{:S(2)}) collective-permute-start(bf16[16,128,128]{2,1,0:T(8,128)(2,1)S(1)} %get-tuple-element.31.refs_0_.refs_6_), channel_id=1, source_target_pairs={{0,2},{1,3},{2,0},{3,1},{4,6},{5,7},{6,4},{7,5},{8,10},{9,11},{10,... | collective-permute-start | bytes 1572872 | tf_op jit(solution)/shard_map/ppermute | solution.py:314
  15.2 14.7 %collective-permute-start.8 = (bf16[16,128,128]{2,1,0:T(8,128)(2,1)S(1)}, bf16[16,128,128]{2,1,0:T(8,128)(2,1)S(1)}, u32[]{:S(2)}, u32[]{:S(2)}) collective-permute-start(bf16[16,128,128]{2,1,0:T(8,128)(2,1)S(1)} %get-tuple-element.31.refs_0_.refs_6_), channel_id=1, source_target_pairs={{0,4},{1,5},{2,6},{3,7},{4,0},{5,1},{6,2},{7,3},{8,12},{9,13},{10,... | collective-permute-start | bytes 1572872 | tf_op jit(solution)/shard_map/ppermute | solution.py:314
  16.8 30.9 %copy-start.17 = (bf16[16,128,128]{2,1,0:T(8,128)(2,1)}, bf16[16,128,128]{2,1,0:T(8,128)(2,1)S(1)}, u32[]{:S(2)}) copy-start(bf16[16,128,128]{2,1,0:T(8,128)(2,1)S(1)} %pad_maximum_fusion.own) | copy-start | bytes 1572868
  27.3 13.3 %collective-permute-start.9 = (bf16[16,128,128]{2,1,0:T(8,128)(2,1)S(1)}, bf16[16,128,128]{2,1,0:T(8,128)(2,1)S(1)}, u32[]{:S(2)}, u32[]{:S(2)}) collective-permute-start(bf16[16,128,128]{2,1,0:T(8,128)(2,1)S(1)} %collective-permute-done.6.refs_1_.refs_7_), channel_id=1, source_target_pairs={{0,4},{1,5},{2,6},{3,7},{4,0},{5,1},{6,2},{7,3},{8,12},{9,13},{10,... | collective-permute-start | bytes 1572872 | tf_op jit(solution)/shard_map/ppermute | solution.py:314
  41.5 12.7 %collective-permute-start.10 = (bf16[16,128,128]{2,1,0:T(8,128)(2,1)}, bf16[16,128,128]{2,1,0:T(8,128)(2,1)}, u32[]{:S(2)}, u32[]{:S(2)}) collective-permute-start(bf16[16,128,128]{2,1,0:T(8,128)(2,1)} %get-tuple-element.34.refs_0_.refs_6_), channel_id=1, source_target_pairs={{0,4},{1,5},{2,6},{3,7},{4,0},{5,1},{6,2},{7,3},{8,12},{9,13},{10,... | collective-permute-start | bytes 1572872 | tf_op jit(solution)/shard_map/ppermute | solution.py:314
  42.9 12.8 %collective-permute-start.1 = (bf16[16,128,128]{2,1,0:T(8,128)(2,1)S(1)}, bf16[16,128,128]{2,1,0:T(8,128)(2,1)S(1)}, u32[]{:S(2)}, u32[]{:S(2)}) collective-permute-start(bf16[16,128,128]{2,1,0:T(8,128)(2,1)S(1)} %pad_maximum_fusion.own), channel_id=1, source_target_pairs={{0,8},{8,16},{16,24},{1,9},{9,17},{17,25},{2,10},{10,18},{18,26},{... | collective-permute-start | bytes 1572872 | tf_op jit(solution)/shard_map/ppermute | solution.py:317
  46.5 13.4 %collective-permute-start.2 = (bf16[16,128,128]{2,1,0:T(8,128)(2,1)S(1)}, bf16[16,128,128]{2,1,0:T(8,128)(2,1)S(1)}, u32[]{:S(2)}, u32[]{:S(2)}) collective-permute-start(bf16[16,128,128]{2,1,0:T(8,128)(2,1)S(1)} %pad_maximum_fusion.own), channel_id=1, source_target_pairs={{8,0},{16,8},{24,16},{9,1},{17,9},{25,17},{10,2},{18,10},{26,18},{... | collective-permute-start | bytes 1572872 | tf_op jit(solution)/shard_map/ppermute | solution.py:320
  47.8 18.8 %collective-permute-start.4 = (bf16[32,64,128]{2,1,0:T(8,128)(2,1)S(1)}, bf16[32,64,128]{2,1,0:T(8,128)(2,1)S(1)}, u32[]{:S(2)}, u32[]{:S(2)}) collective-permute-start(bf16[32,64,128]{2,1,0:T(8,128)(2,1)S(1)} %get-tuple-element.28), channel_id=1, source_target_pairs={{0,1},{1,0},{2,3},{3,2},{4,5},{5,4},{6,7},{7,6},{8,9},{9,8},{10,11... | collective-permute-start | bytes 1572872 | tf_op jit(solution)/shard_map/ppermute | solution.py:314
  47.8 29.9 %collective-permute-start.7 = (bf16[16,128,128]{2,1,0:T(8,128)(2,1)}, bf16[16,128,128]{2,1,0:T(8,128)(2,1)}, u32[]{:S(2)}, u32[]{:S(2)}) collective-permute-start(bf16[16,128,128]{2,1,0:T(8,128)(2,1)} %get-tuple-element.34.refs_0_.refs_6_), channel_id=1, source_target_pairs={{0,2},{1,3},{2,0},{3,1},{4,6},{5,7},{6,4},{7,5},{8,10},{9,11},{10,... | collective-permute-start | bytes 1572872 | tf_op jit(solution)/shard_map/ppermute | solution.py:314
  54.2 24.8 %collective-permute-start.11 = (bf16[16,128,128]{2,1,0:T(8,128)(2,1)}, bf16[16,128,128]{2,1,0:T(8,128)(2,1)}, u32[]{:S(2)}, u32[]{:S(2)}) collective-permute-start(bf16[16,128,128]{2,1,0:T(8,128)(2,1)} %collective-permute-done.10.refs_2_.refs_8_), channel_id=1, source_target_pairs={{0,2},{1,3},{2,0},{3,1},{4,6},{5,7},{6,4},{7,5},{8,10},{9,11},{10,... | collective-permute-start | bytes 1572872 | tf_op jit(solution)/shard_map/ppermute | solution.py:314
  55.7 4.1 %copy-start.19 = (bf16[16,128,128]{2,1,0:T(8,128)(2,1)}, bf16[16,128,128]{2,1,0:T(8,128)(2,1)S(1)}, u32[]{:S(2)}) copy-start(bf16[16,128,128]{2,1,0:T(8,128)(2,1)S(1)} %collective-permute-done.1.refs_0_) | copy-start | bytes 1572868
  59.9 22.3 %collective-permute-start.14 = (bf16[16,128,128]{2,1,0:T(8,128)(2,1)}, bf16[16,128,128]{2,1,0:T(8,128)(2,1)}, u32[]{:S(2)}, u32[]{:S(2)}) collective-permute-start(bf16[16,128,128]{2,1,0:T(8,128)(2,1)} %pad_maximum_fusion.1.own), channel_id=1, source_target_pairs={{8,0},{16,8},{24,16},{9,1},{17,9},{25,17},{10,2},{18,10},{26,18},{... | collective-permute-start | bytes 1572872 | tf_op jit(solution)/shard_map/ppermute | solution.py:320
  61.2 21.0 %collective-permute-start.3 = (bf16[16,128,128]{2,1,0:T(8,128)(2,1)}, bf16[16,128,128]{2,1,0:T(8,128)(2,1)}, u32[]{:S(2)}, u32[]{:S(2)}) collective-permute-start(bf16[16,128,128]{2,1,0:T(8,128)(2,1)} %pad_maximum_fusion.1.own), channel_id=1, source_target_pairs={{0,8},{8,16},{16,24},{1,9},{9,17},{17,25},{2,10},{10,18},{18,26},{... | collective-permute-start | bytes 1572872 | tf_op jit(solution)/shard_map/ppermute | solution.py:317
  70.8 1.9 %copy-start.20 = (bf16[16,128,128]{2,1,0:T(8,128)(2,1)S(1)}, bf16[16,128,128]{2,1,0:T(8,128)(2,1)}, u32[]{:S(2)}) copy-start(bf16[16,128,128]{2,1,0:T(8,128)(2,1)} %copy-done.19) | copy-start | bytes 1572868
  70.8 1.9 %copy-start.23 = (bf16[16,128,128]{2,1,0:T(8,128)(2,1)S(1)}, bf16[16,128,128]{2,1,0:T(8,128)(2,1)}, u32[]{:S(2)}) copy-start(bf16[16,128,128]{2,1,0:T(8,128)(2,1)} %copy-done.22) | copy-start | bytes 1572868
  72.6 43.8 %copy-start = (bf16[4,16,128,128]{3,2,1,0:T(8,128)(2,1)}, bf16[4,16,128,128]{3,2,1,0:T(8,128)(2,1)S(1)}, u32[]{:S(2)}) copy-start(bf16[4,16,128,128]{3,2,1,0:T(8,128)(2,1)S(1)} %right_partials.3.refs_4_) | copy-start | bytes 6291460
  74.3 18.4 %collective-permute-start.17 = (bf16[16,128,128]{2,1,0:T(8,128)(2,1)}, bf16[16,128,128]{2,1,0:T(8,128)(2,1)}, u32[]{:S(2)}, u32[]{:S(2)}) collective-permute-start(bf16[16,128,128]{2,1,0:T(8,128)(2,1)} %get-tuple-element.48), channel_id=1, source_target_pairs={{0,8},{8,16},{16,24},{1,9},{9,17},{17,25},{2,10},{10,18},{18,26},{... | collective-permute-start | bytes 1572872 | tf_op jit(solution)/shard_map/ppermute | solution.py:317
  77.8 14.9 %collective-permute-start.19 = (bf16[16,128,128]{2,1,0:T(8,128)(2,1)}, bf16[16,128,128]{2,1,0:T(8,128)(2,1)}, u32[]{:S(2)}, u32[]{:S(2)}) collective-permute-start(bf16[16,128,128]{2,1,0:T(8,128)(2,1)} %get-tuple-element.47), channel_id=1, source_target_pairs={{8,0},{16,8},{24,16},{9,1},{17,9},{25,17},{10,2},{18,10},{26,18},{... | collective-permute-start | bytes 1572872 | tf_op jit(solution)/shard_map/ppermute | solution.py:320
  86.2 17.6 %collective-permute-start.15 = (bf16[16,128,128]{2,1,0:T(8,128)(2,1)}, bf16[16,128,128]{2,1,0:T(8,128)(2,1)S(1)}, u32[]{:S(2)}, u32[]{:S(2)}) collective-permute-start(bf16[16,128,128]{2,1,0:T(8,128)(2,1)} %get-tuple-element.51), channel_id=1, source_target_pairs={{8,0},{16,8},{24,16},{9,1},{17,9},{25,17},{10,2},{18,10},{26,18},{... | collective-permute-start | bytes 1572872 | tf_op jit(solution)/shard_map/ppermute | solution.py:320
  87.5 17.9 %collective-permute-start.12 = (bf16[16,128,128]{2,1,0:T(8,128)(2,1)}, bf16[16,128,128]{2,1,0:T(8,128)(2,1)S(1)}, u32[]{:S(2)}, u32[]{:S(2)}) collective-permute-start(bf16[16,128,128]{2,1,0:T(8,128)(2,1)} %get-tuple-element.52), channel_id=1, source_target_pairs={{0,8},{8,16},{16,24},{1,9},{9,17},{17,25},{2,10},{10,18},{18,26},{... | collective-permute-start | bytes 1572872 | tf_op jit(solution)/shard_map/ppermute | solution.py:317
  92.7 12.6 %copy-start.2 = (bf16[4,16,128,128]{3,2,1,0:T(8,128)(2,1)S(1)}, bf16[4,16,128,128]{3,2,1,0:T(8,128)(2,1)}, u32[]{:S(2)}) copy-start(bf16[4,16,128,128]{3,2,1,0:T(8,128)(2,1)} %copy-done.1) | copy-start | bytes 6291460
  94.4 22.0 %collective-permute-start.18 = (bf16[16,128,128]{2,1,0:T(8,128)(2,1)S(1)}, bf16[16,128,128]{2,1,0:T(8,128)(2,1)S(1)}, u32[]{:S(2)}, u32[]{:S(2)}) collective-permute-start(bf16[16,128,128]{2,1,0:T(8,128)(2,1)S(1)} %get-tuple-element.46), channel_id=1, source_target_pairs={{0,8},{8,16},{16,24},{1,9},{9,17},{17,25},{2,10},{10,18},{18,26},{... | collective-permute-start | bytes 1572872 | tf_op jit(solution)/shard_map/ppermute | solution.py:317
  98.3 18.1 %collective-permute-start.20 = (bf16[16,128,128]{2,1,0:T(8,128)(2,1)S(1)}, bf16[16,128,128]{2,1,0:T(8,128)(2,1)S(1)}, u32[]{:S(2)}, u32[]{:S(2)}) collective-permute-start(bf16[16,128,128]{2,1,0:T(8,128)(2,1)S(1)} %get-tuple-element.45), channel_id=1, source_target_pairs={{8,0},{16,8},{24,16},{9,1},{17,9},{25,17},{10,2},{18,10},{26,18},{... | collective-permute-start | bytes 1572872 | tf_op jit(solution)/shard_map/ppermute | solution.py:320
  105.6 22.0 %collective-permute-start.13 = (bf16[16,128,128]{2,1,0:T(8,128)(2,1)S(1)}, bf16[16,128,128]{2,1,0:T(8,128)(2,1)S(1)}, u32[]{:S(2)}, u32[]{:S(2)}) collective-permute-start(bf16[16,128,128]{2,1,0:T(8,128)(2,1)S(1)} %get-tuple-element.50), channel_id=1, source_target_pairs={{0,8},{8,16},{16,24},{1,9},{9,17},{17,25},{2,10},{10,18},{18,26},{... | collective-permute-start | bytes 1572872 | tf_op jit(solution)/shard_map/ppermute | solution.py:317
  110.0 17.7 %collective-permute-start.16 = (bf16[16,128,128]{2,1,0:T(8,128)(2,1)S(1)}, bf16[16,128,128]{2,1,0:T(8,128)(2,1)S(1)}, u32[]{:S(2)}, u32[]{:S(2)}) collective-permute-start(bf16[16,128,128]{2,1,0:T(8,128)(2,1)S(1)} %get-tuple-element.49), channel_id=1, source_target_pairs={{8,0},{16,8},{24,16},{9,1},{17,9},{25,17},{10,2},{18,10},{26,18},{... | collective-permute-start | bytes 1572872 | tf_op jit(solution)/shard_map/ppermute | solution.py:320
  116.8 22.1 %collective-permute-start.23 = (bf16[16,128,128]{2,1,0:T(8,128)(2,1)S(1)}, bf16[16,128,128]{2,1,0:T(8,128)(2,1)S(1)}, u32[]{:S(2)}, u32[]{:S(2)}) collective-permute-start(bf16[16,128,128]{2,1,0:T(8,128)(2,1)S(1)} %get-tuple-element.44), channel_id=1, source_target_pairs={{0,8},{8,16},{16,24},{1,9},{9,17},{17,25},{2,10},{10,18},{18,26},{... | collective-permute-start | bytes 1572872 | tf_op jit(solution)/shard_map/ppermute | solution.py:317
  121.2 17.9 %copy-start.8 = (bf16[16,128,128]{2,1,0:T(8,128)(2,1)S(1)}, bf16[16,128,128]{2,1,0:T(8,128)(2,1)}, u32[]{:S(2)}) copy-start(bf16[16,128,128]{2,1,0:T(8,128)(2,1)} %copy-done.6) | copy-start | bytes 1572868
  121.3 17.9 %copy-start.11 = (bf16[16,128,128]{2,1,0:T(8,128)(2,1)S(1)}, bf16[16,128,128]{2,1,0:T(8,128)(2,1)}, u32[]{:S(2)}) copy-start(bf16[16,128,128]{2,1,0:T(8,128)(2,1)} %copy-done.9) | copy-start | bytes 1572868
  121.3 17.9 %copy-start.14 = (bf16[16,128,128]{2,1,0:T(8,128)(2,1)S(1)}, bf16[16,128,128]{2,1,0:T(8,128)(2,1)}, u32[]{:S(2)}) copy-start(bf16[16,128,128]{2,1,0:T(8,128)(2,1)} %copy-done.12) | copy-start | bytes 1572868
  121.3 17.9 %copy-start.18 = (bf16[16,128,128]{2,1,0:T(8,128)(2,1)S(1)}, bf16[16,128,128]{2,1,0:T(8,128)(2,1)}, u32[]{:S(2)}) copy-start(bf16[16,128,128]{2,1,0:T(8,128)(2,1)} %copy-done.17) | copy-start | bytes 1572868
  121.3 17.9 %copy-start.21 = (bf16[16,128,128]{2,1,0:T(8,128)(2,1)S(1)}, bf16[16,128,128]{2,1,0:T(8,128)(2,1)}, u32[]{:S(2)}) copy-start(bf16[16,128,128]{2,1,0:T(8,128)(2,1)} %copy-done.19) | copy-start | bytes 1572868
  121.3 17.9 %copy-start.24 = (bf16[16,128,128]{2,1,0:T(8,128)(2,1)S(1)}, bf16[16,128,128]{2,1,0:T(8,128)(2,1)}, u32[]{:S(2)}) copy-start(bf16[16,128,128]{2,1,0:T(8,128)(2,1)} %copy-done.22) | copy-start | bytes 1572868
  121.3 17.6 %collective-permute-start.25 = (bf16[16,128,128]{2,1,0:T(8,128)(2,1)S(1)}, bf16[16,128,128]{2,1,0:T(8,128)(2,1)S(1)}, u32[]{:S(2)}, u32[]{:S(2)}) collective-permute-start(bf16[16,128,128]{2,1,0:T(8,128)(2,1)S(1)} %get-tuple-element.43), channel_id=1, source_target_pairs={{8,0},{16,8},{24,16},{9,1},{17,9},{25,17},{10,2},{18,10},{26,18},{... | collective-permute-start | bytes 1572872 | tf_op jit(solution)/shard_map/ppermute | solution.py:320
  128.1 16.7 %collective-permute-start.24 = (bf16[16,128,128]{2,1,0:T(8,128)(2,1)S(1)}, bf16[16,128,128]{2,1,0:T(8,128)(2,1)S(1)}, u32[]{:S(2)}, u32[]{:S(2)}) collective-permute-start(bf16[16,128,128]{2,1,0:T(8,128)(2,1)S(1)} %get-tuple-element.42), channel_id=1, source_target_pairs={{0,8},{8,16},{16,24},{1,9},{9,17},{17,25},{2,10},{10,18},{18,26},{... | collective-permute-start | bytes 1572872 | tf_op jit(solution)/shard_map/ppermute | solution.py:317
  132.6 13.3 %collective-permute-start.26 = (bf16[16,128,128]{2,1,0:T(8,128)(2,1)S(1)}, bf16[16,128,128]{2,1,0:T(8,128)(2,1)S(1)}, u32[]{:S(2)}, u32[]{:S(2)}) collective-permute-start(bf16[16,128,128]{2,1,0:T(8,128)(2,1)S(1)} %get-tuple-element.41), channel_id=1, source_target_pairs={{8,0},{16,8},{24,16},{9,1},{17,9},{25,17},{10,2},{18,10},{26,18},{... | collective-permute-start | bytes 1572872 | tf_op jit(solution)/shard_map/ppermute | solution.py:320
  139.0 7.1 %collective-permute-start.27 = (bf16[16,64,128]{2,1,0:T(8,128)(2,1)S(1)}, bf16[16,64,128]{2,1,0:T(8,128)(2,1)S(1)}, u32[]{:S(2)}, u32[]{:S(2)}) collective-permute-start(bf16[16,64,128]{2,1,0:T(8,128)(2,1)S(1)} %add_convert_fusion.1), channel_id=1, source_target_pairs={{0,1},{1,0},{2,3},{3,2},{4,5},{5,4},{6,7},{7,6},{8,9},{9,8},{10,11... | collective-permute-start | bytes 786440 | tf_op jit(solution)/shard_map/ppermute | solution.py:314
  141.3 6.3 %copy-start.28 = (s32[4,4]{1,0:T(4,128)S(1)}, s32[4,4]{1,0:T(4,128)}, u32[]{:S(2)}) copy-start(s32[4,4]{1,0:T(4,128)} %mask.5) | copy-start | bytes 196
  141.4 4.8 %collective-permute-start.21 = (bf16[16,64,128]{2,1,0:T(8,128)(2,1)S(1)}, bf16[16,64,128]{2,1,0:T(8,128)(2,1)S(1)}, u32[]{:S(2)}, u32[]{:S(2)}) collective-permute-start(bf16[16,64,128]{2,1,0:T(8,128)(2,1)S(1)} %get-tuple-element.39), channel_id=1, source_target_pairs={{0,1},{1,0},{2,3},{3,2},{4,5},{5,4},{6,7},{7,6},{8,9},{9,8},{10,11... | collective-permute-start | bytes 786440 | tf_op jit(solution)/shard_map/ppermute | solution.py:314
  144.4 1.7 %collective-permute-start.22 = (bf16[16,64,128]{2,1,0:T(8,128)(2,1)S(1)}, bf16[16,64,128]{2,1,0:T(8,128)(2,1)S(1)}, u32[]{:S(2)}, u32[]{:S(2)}) collective-permute-start(bf16[16,64,128]{2,1,0:T(8,128)(2,1)S(1)} %get-tuple-element.40), channel_id=1, source_target_pairs={{0,1},{1,0},{2,3},{3,2},{4,5},{5,4},{6,7},{7,6},{8,9},{9,8},{10,11... | collective-permute-start | bytes 786440 | tf_op jit(solution)/shard_map/ppermute | solution.py:314
  146.0 1.6 %collective-permute-start.28 = (bf16[16,64,128]{2,1,0:T(8,128)(2,1)S(1)}, bf16[16,64,128]{2,1,0:T(8,128)(2,1)S(1)}, u32[]{:S(2)}, u32[]{:S(2)}) collective-permute-start(bf16[16,64,128]{2,1,0:T(8,128)(2,1)S(1)} %add_convert_fusion), channel_id=1, source_target_pairs={{0,1},{1,0},{2,3},{3,2},{4,5},{5,4},{6,7},{7,6},{8,9},{9,8},{10,11... | collective-permute-start | bytes 786440 | tf_op jit(solution)/shard_map/ppermute | solution.py:314
  (14 other events, 13.7 us)

commit v5 on v4

--- a/solution.py
+++ b/solution.py
@@ -12,8 +12,10 @@
 STEP = 8
 KEYS = 16
 CORES = 2
-VMEM_LIMIT = 48 * 1024 * 1024
+VMEM_LIMIT = 12 * 1024 * 1024
 PARAMS = pltpu.CompilerParams(vmem_limit_bytes=VMEM_LIMIT)
+FRONT_COST = pl.CostEstimate(flops=1, bytes_accessed=18_000_000, transcendentals=0)
+COST = pl.CostEstimate(flops=1, bytes_accessed=8_000_000, transcendentals=0)
 BY_LAST = (((1,), (1,)), ((), ()))
 
 
@@ -103,63 +105,64 @@
             pltpu.VMEM((width, chans), jnp.bfloat16),
         ],
         compiler_params=PARAMS,
-        cost_estimate=pl.CostEstimate(
-            flops=4 * rows * cols * chans * width, bytes_accessed=6 * rows * cols * chans, transcendentals=rows * cols * width
-        ),
+        cost_estimate=FRONT_COST,
         name="left_front" if side == 0 else "right_front",
-    )(tile_mask, pair, gain, bias, proj_weight)
-
-
-def pack_kernel(own, other, *outs):
+    )(tile_mask, *(pltpu.with_memory_space_constraint(v, pltpu.HBM) for v in (pair, gain, bias, proj_weight)))
+
+
+def pack_kernel(own, other, out):
     cols, half, _ = other.shape
-    part = half // len(outs)
     core = this_core()
     for block, place in ((own[:, pl.ds(pl.multiple_of(core * half, half), half), :], core), (other[...], 1 - core)):
-        block = jnp.transpose(block, (1, 0, 2))
-        for chunk, out in enumerate(outs):
-            out[:, pl.ds(pl.multiple_of(place * cols, cols), cols), :] = block[chunk * part : (chunk + 1) * part]
+        out[:, pl.ds(pl.multiple_of(place * cols, cols), cols), :] = jnp.transpose(block, (1, 0, 2))
 
 
 def pack(own, other):
     cols, half, rows = other.shape
     return pl.pallas_call(
         pack_kernel,
-        out_shape=[jax.ShapeDtypeStruct((half // CHUNKS, CORES * cols, rows), jnp.bfloat16)] * CHUNKS,
-        compiler_params=PARAMS,
-        cost_estimate=pl.CostEstimate(flops=0, bytes_accessed=10 * cols * half * rows, transcendentals=0),
+        out_shape=jax.ShapeDtypeStruct((half, CORES * cols, rows), jnp.bfloat16),
+        compiler_params=PARAMS,
+        cost_estimate=COST,
         name="pack",
     )(own, other)
 
 
-def partial_kernel(left_mine, left_other, *refs):
-    blocks, out = refs[:-1], refs[-1]
-    n = out.shape[0]
+def chunk_spec(array, chans, chunk):
+    first = chunk * chans // STEP if array.shape[0] > chans else 0
+    return pl.BlockSpec((STEP,) + array.shape[1:], lambda g: (first + g, 0, 0))
+
+
+def partial_kernel(n, left_mine, left_other, up, down, *refs):
+    blocks, outs, (up_next, down_next, sums) = refs[:n], refs[n : 2 * n], refs[2 * n :]
     row, chip = lax.axis_index("row"), lax.axis_index("col") // CORES
     for c in range(STEP):
         lhs = jnp.concatenate((left_mine[c], left_other[c]), axis=0)
         for m, block in enumerate(blocks):
             away = lax.rem(jnp.bitwise_xor(chip, m) - row + n, n)
-            out[away, c] = lax.dot_general(lhs, block[c], BY_LAST, preferred_element_type=jnp.float32).astype(jnp.bfloat16)
-
-
-def partial_products(left_mine, left_other, blocks, chunk):
-    chans, rows, _ = blocks[0].shape
-    ks = left_mine.shape[1]
+            sums[away, c] = lax.dot_general(lhs, block[c], BY_LAST, preferred_element_type=jnp.float32).astype(jnp.bfloat16)
+    for s, out in enumerate(outs):
+        out[...] = sums[s]
+    up_next[...] = jnp.where(row < 1, sums[n - 1], up[...])
+    down_next[...] = jnp.where(row >= n - 1, sums[1], down[...])
+
+
+def partial_products(left_mine, left_other, up, down, blocks, chunk):
+    rows = blocks[0].shape[1]
+    ks, chans = left_mine.shape[1], left_mine.shape[0] // CHUNKS
     n = len(blocks)
-    first = chunk * chans // STEP
-    left = pl.BlockSpec((STEP, ks, rows), lambda g: (first + g, 0, 0))
-    return pl.pallas_call(
-        partial_kernel,
-        out_shape=jax.ShapeDtypeStruct((n, chans, CORES * ks, rows), jnp.bfloat16),
+    args = (left_mine, left_other, up, down, *blocks)
+    return pl.pallas_call(
+        functools.partial(partial_kernel, n),
+        out_shape=[pltpu.HBM((chans, CORES * ks, rows), jnp.bfloat16)] * (n + 2),
         grid=(chans // STEP,),
-        in_specs=[left, left] + [pl.BlockSpec((STEP, rows, rows), lambda g: (g, 0, 0))] * n,
-        out_specs=pl.BlockSpec((n, STEP, CORES * ks, rows), lambda g: (0, g, 0, 0)),
-        compiler_params=PARAMS,
-        cost_estimate=pl.CostEstimate(
-            flops=4 * chans * ks * rows * n * rows, bytes_accessed=2 * chans * rows * (n * rows + 2 * ks * (n + 1)), transcendentals=0
-        ),
+        in_specs=[chunk_spec(v, chans, chunk) for v in args],
+        out_specs=[pl.BlockSpec((STEP, CORES * ks, rows), lambda g: (g, 0, 0))] * (n + 2),
+        scratch_shapes=[pltpu.VMEM((n, STEP, CORES * ks, rows), jnp.bfloat16)],
+        compiler_params=PARAMS,
+        cost_estimate=COST,
         name="right_partials",
-    )(left_mine, left_other, *blocks)
+    )(*args)
 
 
 def left_kernel(n, own, *refs):
@@ -181,11 +184,11 @@
         theirs[c] = out[ks:].astype(jnp.bfloat16)
 
 
-def left_products(own, ups, downs, blocks):
-    chans, ks, rows = own.shape
+def left_products(own, ups, downs, blocks, chunk):
+    chans, ks, rows = ups[-1].shape
     n = len(blocks)
-    act = pl.BlockSpec((STEP, ks, rows), lambda g: (g, 0, 0))
     out = pl.BlockSpec((STEP, ks // CORES, rows), lambda g: (g, 0, 0))
+    args = (own, *ups, *downs, *blocks)
     return pl.pallas_call(
         functools.partial(left_kernel, n),
         out_shape=[
@@ -193,15 +196,13 @@
             jax.ShapeDtypeStruct((chans, ks // CORES, rows), jnp.bfloat16),
         ],
         grid=(chans // STEP,),
-        in_specs=[act] * (2 * n - 1) + [pl.BlockSpec((STEP, rows, rows), lambda g: (g, 0, 0))] * n,
+        in_specs=[chunk_spec(v, chans, chunk) for v in args],
         out_specs=[out] * 2,
         scratch_shapes=[pltpu.VMEM((STEP, n, rows, rows), jnp.bfloat16)],
         compiler_params=PARAMS,
-        cost_estimate=pl.CostEstimate(
-            flops=2 * chans * ks * rows * n * rows, bytes_accessed=2 * chans * rows * (n * rows + ks * (2 * n + 1)), transcendentals=0
-        ),
+        cost_estimate=COST,
         name="left_products",
-    )(own, *ups, *downs, *blocks)
+    )(*args)
 
 
 def tail_kernel(mask, pair, gain, bias, weight, *refs):
@@ -222,7 +223,7 @@
 
     for chunk in range(CHUNKS):
         own, up, down = (ref[chunk][...].astype(jnp.float32) for ref in (partials, ups, downs))
-        put(right_flat, core, chunk, own[0] + up + down)
+        put(right_flat, core, chunk, own + up + down)
         put(right_flat, 1 - core, chunk, right_other[chunk][...])
         put(left_flat, core, chunk, left_mine[chunk][...])
         put(left_flat, 1 - core, chunk, left_other[chunk][...])
@@ -263,7 +264,6 @@
     vector = pl.BlockSpec((1, chans), lambda g: (0, 0))
     cells = pl.BlockSpec((rows, KEYS, chans), lambda g: (0, g, 0))
     small = [pl.BlockSpec((part, KEYS, rows), lambda g: (0, g, 0))] * CHUNKS
-    first = [pl.BlockSpec((1, part, KEYS, rows), lambda g: (0, 0, g, 0))] * CHUNKS
     return pl.pallas_call(
         tail_kernel,
         out_shape=jax.ShapeDtypeStruct(pair.shape, jnp.bfloat16),
@@ -275,9 +275,7 @@
             vector,
             pl.BlockSpec((chans, width), lambda g: (0, 0)),
         ]
-        + small * 2
-        + first
-        + small * 3,
+        + small * 6,
         out_specs=cells,
         scratch_shapes=[
             pltpu.VMEM((KEYS, rows, chans), jnp.bfloat16),
@@ -292,9 +290,7 @@
             pltpu.VMEM((width, chans), jnp.bfloat16),
         ],
         compiler_params=PARAMS,
-        cost_estimate=pl.CostEstimate(
-            flops=8 * rows * cols * chans * width, bytes_accessed=10 * rows * cols * chans, transcendentals=rows * cols * width
-        ),
+        cost_estimate=COST,
         name="tail",
     )(tile_mask, pair, gain, bias, proj_weight, *left_mine, *left_other, *partials, *ups, *downs, *right_other)
 
@@ -320,52 +316,48 @@
         return lax.ppermute(value, "row", [(r + 1, r) for r in range(n - 1)])
 
     raw = jnp.transpose(grad_x, (1, 2, 0))
-    other = exchange(lax.dynamic_slice_in_dim(raw, (1 - this_core()) * half, half, 1), 1)
-    right_mine, right_theirs = front(pair, gain, bias, proj_weight, tile_mask, 1)
-    packed = pack(raw, after(other, right_mine))
-    right_other = exchange(right_theirs, 1)
-    owns = [
-        jnp.concatenate((right_mine[c * part : (c + 1) * part], right_other[c * part : (c + 1) * part]), axis=1)
-        for c in range(CHUNKS)
-    ]
-    left_mine, left_theirs = front(after(pair, owns), gain, bias, proj_weight, tile_mask, 0)
+    packed = pack(raw, exchange(lax.dynamic_slice_in_dim(raw, (1 - this_core()) * half, half, 1), 1))
+
+    slots = [[packed] * CHUNKS]
+    for m in range(1, n_col // CORES):
+        axes = [1 << b for b in range(m.bit_length()) if m >> b & 1]
+        if len(axes) == 1:
+            slots.append([exchange(packed, CORES * m)] * CHUNKS)
+            continue
+        slots.append([])
+        for c in range(CHUNKS):
+            bit = axes[(c + 1) % len(axes)]
+            value = slots[m ^ bit][c]
+            value = value if value.shape[0] == part else value[c * part : (c + 1) * part]
+            slots[m].append(exchange(value, CORES * bit))
+    panels = [[slot[c] for slot in slots] for c in range(CHUNKS)]
+
+    right_mine, right_theirs = front(after(pair, packed), gain, bias, proj_weight, tile_mask, 1)
+    own = jnp.concatenate((right_mine, exchange(right_theirs, 1)), axis=1)
+    first_up, first_down = step_up(own), step_down(own)
+    left_mine, left_theirs = front(after(pair, own), gain, bias, proj_weight, tile_mask, 0)
     left_other = exchange(left_theirs, 1)
-
-    bits = [1 << b for b in range(n_col.bit_length() - 2)]
-    panels = []
-    for c, own in enumerate(packed):
-        slots = {0: own}
-        order = bits[c % len(bits) :] + bits[: c % len(bits)]
-        for bit in order:
-            for m in list(slots):
-                value = slots[m]
-                if c == 0 and m > 0:
-                    value = after(value, left_mine)
-                if c > 0 and m == 0:
-                    value = after(value, panels[-1][bit] if bit != order[0] else panels[-1][1:])
-                slots[m | bit] = exchange(value, CORES * bit)
-        panels.append([slots[m] for m in range(len(slots))])
 
     ups, downs, partials = [], [], []
     for c in range(CHUNKS):
-        own = owns[c] if c == 0 else after(owns[c], ups[0][0], downs[0][0])
-        ups.append([step_up(own)])
-        downs.append([step_down(own)])
-    for c in range(CHUNKS):
-        partials.append(partial_products(left_mine, left_other, panels[c], c))
+        *sums, up, down = partial_products(left_mine, left_other, first_up, first_down, panels[c], c)
+        partials.append(sums)
+        ups.append([first_up, step_up(up)])
+        downs.append([first_down, step_down(down)])
 
     def plus(arrived, sums, use):
         return (arrived.astype(jnp.float32) + jnp.where(use, sums.astype(jnp.float32), 0.0)).astype(jnp.bfloat16)
 
-    for t in range(1, n):
+    left_grads = []
+    for t in range(2, n):
         for c in range(CHUNKS):
-            ups[c].append(step_up(plus(ups[c][-1], partials[c][n - t], row < t)))
-            downs[c].append(step_down(plus(downs[c][-1], partials[c][t], row >= n - t)))
-
-    left_grads = []
-    for c in range(CHUNKS):
-        own = after(owns[c], ups[-1][n - 2], downs[-1][n - 2])
-        left_grads.append(left_products(own, ups[c][: n - 1], downs[c][: n - 1], panels[c]))
+            up, down = ups[c][-1], downs[c][-1]
+            if t == n - 1 and c > 0:
+                up = after(up, left_grads[c - 1])
+            ups[c].append(step_up(plus(up, partials[c][n - t], row < t)))
+            downs[c].append(step_down(plus(down, partials[c][t], row >= n - t)))
+            if t == n - 1:
+                left_grads.append(left_products(own, ups[c][: n - 1], downs[c][: n - 1], panels[c], c))
     left_grad_other = [exchange(theirs, 1) for _, theirs in left_grads]
     ks = left_mine.shape[1]
     right_grad_other = []
@@ -381,7 +373,7 @@
         tile_mask,
         [mine for mine, _ in left_grads],
         left_grad_other,
-        partials,
+        [sums[0] for sums in partials],
         [u[-1] for u in ups],
         [d[-1] for d in downs],
         right_grad_other,

time: 160 us -> 146 us (0.912)
  local copies, waits for them, and re-layouts: 13.8 us -> 7.93 us
  starting transfers between devices: 57.2 us -> 52 us
  waiting for transfers between devices: 47.5 us -> 44 us
  Pallas kernels: 31.4 us -> 33.5 us
  other arithmetic: 8.36 us -> 6.66 us
    ppermute x8 -> x7, waiting for transfers between devices: 17.1 us -> 1.19 us  [step_up(): return lax.ppermute(value, 'row', [(r, r + 1) for r in range(n - 1)])]
    ppermute x8 -> x7, waiting for transfers between devices: 9.29 us -> 21.2 us  [step_down(): return lax.ppermute(value, 'row', [(r + 1, r) for r in range(n - 1)])]
    unnamed x66 -> x53, local copies, waits for them, and re-layouts: 12.4 us -> 5.88 us
    ppermute x13 -> x11, starting transfers between devices: 11.9 us -> 9.31 us  [exchange(): return lax.ppermute(value, 'col', [(d, d ^ mask) for d in range(n_col)])]
    ppermute x8 -> x7, starting transfers between devices: 10.7 us -> 9.27 us  [step_down(): return lax.ppermute(value, 'row', [(r + 1, r) for r in range(n - 1)])]
    ppermute x8 -> x7, starting transfers between devices: 34.6 us -> 33.5 us  [step_up(): return lax.ppermute(value, 'row', [(r, r + 1) for r in range(n - 1)])]
    ppermute x13 -> x11, waiting for transfers between devices: 21.1 us -> 21.7 us  [exchange(): return lax.ppermute(value, 'col', [(d, d ^ mask) for d in range(n_col)])]
  transfers between devices with their start and end apart: 29 -> 25, of which waited for: 13 -> 10; matrix products, arithmetic and copies ran while one was open for 5% -> 5% of each run, Pallas kernels for 13% -> 12%
where the time goes in v5:
time: 146 us; the launch traced here: 145 us
  starting transfers between devices  52 us (36%)
  waiting for transfers between devices  44 us (30%)
  Pallas kernels  33.5 us (23%)
  local copies, waits for them, and re-layouts  7.93 us (5%)
  other arithmetic  6.66 us (5%)
    ppermute x7, starting transfers between devices, step_up(): return lax.ppermute(value, 'row', [(r, r + 1) for r in range(n - 1)])  33.5 us
    ppermute x11, waiting for transfers between devices, exchange(): return lax.ppermute(value, 'col', [(d, d ^ mask) for d in range(n_col)])  21.7 us
    ppermute x7, waiting for transfers between devices, step_down(): return lax.ppermute(value, 'row', [(r + 1, r) for r in range(n - 1)])  21.2 us
    pallas_call x1, Pallas kernels, tail(): pl.pallas_call(tail_kernel, out_shape=jax.ShapeDtypeStruct(pair.shape, jn...  11.2 us
    pallas_call x2, Pallas kernels, front(): pl.pallas_call(front_kernel, out_shape=[jax.ShapeDtypeStruct((half, cols,...  10.3 us
    ppermute x11, starting transfers between devices, exchange(): return lax.ppermute(value, 'col', [(d, d ^ mask) for d in range(n_col)])  9.31 us
    ppermute x7, starting transfers between devices, step_down(): return lax.ppermute(value, 'row', [(r + 1, r) for r in range(n - 1)])  9.27 us
    pallas_call x2, Pallas kernels, partial_products(): pl.pallas_call(functools.partial(partial_kernel, n), out_shape=[pltpu.HBM...  7.08 us
  transfers between devices with their start and end apart: 25, of which 10 were waited for; matrix products, arithmetic and copies ran while one was open for 5% of the time, Pallas kernels for 12%

profile of v5, /device:TPU:0, one launch (start us, length us, event | category | flops | bytes accessed | tf_op | source)
XLA Modules:
  0.0 144.8 jit_solution(11547702017980689615)
XLA Ops:
  0.0 1.1 dynamic-slice_bitcast_fusion
  1.1 0.5 collective-permute-start
  1.6 1.5 %collective-permute-done.other = bf16[64,32,128]{2,1,0:T(8,128)(2,1)S(1)} collective-permute-done((bf16[64,32,128]{2,1,0:T(8,128)(2,1)S(1)}, bf16[64,32,128]{2,1,0:T(8,128)(2,1)S(1)}, u32[]{:S(2)}, u32[]{:S(2)}) %collective-permute-start) | collective-permute-done | bytes 524320 | tf_op jit(solution)/shard_map/ppermute | solution.py:310
  3.2 1.2 copy-done.9
  4.8 5.2 %right_front.1 = (bf16[32,64,128]{2,1,0:T(8,128)(2,1)S(1)}, bf16[32,64,128]{2,1,0:T(8,128)(2,1)S(1)}) custom-call(s32[4,4]{1,0:T(4,128)S(1)} %copy-done.19, bf16[128,64,128]{2,1,0:T(8,128)(2,1)} %pair.3, f32[1,128]{1,0:T(1,128)} %bitcast.6, f32[1,128]{1,0:T(1,128)} %bitcast.9, bf16[128,256]{1,0:T(8,128)(2,1)} %weight.5), custom_call_target="tpu_custom_call" | custom-call | flops 1 | bytes 18000000 | tf_op jit(solution)/shard_map/right_front/pallas_call | solution.py:85
  10.0 0.4 collective-permute-start.1
  10.4 2.6 %collective-permute-start.5 = (bf16[32,128,128]{2,1,0:T(8,128)(2,1)S(1)}, bf16[32,128,128]{2,1,0:T(8,128)(2,1)S(1)}, u32[]{:S(2)}, u32[]{:S(2)}) collective-permute-start(bf16[32,128,128]{2,1,0:T(8,128)(2,1)S(1)} %pack.1.refs_0_.refs_6_), channel_id=1, source_target_pairs={{0,2},{1,3},{2,0},{3,1},{4,6},{5,7},{6,4},{7,5},{8,10},{9,11},{10,... | collective-permute-start | bytes 3145736 | tf_op jit(solution)/shard_map/ppermute | solution.py:310
  13.0 1.5 %collective-permute-start.6 = (bf16[32,128,128]{2,1,0:T(8,128)(2,1)S(1)}, bf16[32,128,128]{2,1,0:T(8,128)(2,1)S(1)}, u32[]{:S(2)}, u32[]{:S(2)}) collective-permute-start(bf16[32,128,128]{2,1,0:T(8,128)(2,1)S(1)} %pack.1.refs_0_.refs_6_), channel_id=1, source_target_pairs={{0,4},{1,5},{2,6},{3,7},{4,0},{5,1},{6,2},{7,3},{8,12},{9,13},{10,... | collective-permute-start | bytes 3145736 | tf_op jit(solution)/shard_map/ppermute | solution.py:310
  14.7 1.3 collective-permute-start.4
  16.0 4.6 %collective-permute-start.2 = (bf16[32,128,128]{2,1,0:T(8,128)(2,1)S(1)}, bf16[32,128,128]{2,1,0:T(8,128)(2,1)S(1)}, u32[]{:S(2)}, u32[]{:S(2)}) collective-permute-start(bf16[32,128,128]{2,1,0:T(8,128)(2,1)S(1)} %constant_dynamic-update-slice_fusion.own), channel_id=1, source_target_pairs={{0,8},{8,16},{16,24},{1,9},{9,17},{17,25},{2,10},{10,18},{18,26},{... | collective-permute-start | bytes 3145736 | tf_op jit(solution)/shard_map/ppermute | solution.py:313
  20.6 5.2 %left_front.1 = (bf16[32,64,128]{2,1,0:T(8,128)(2,1)S(1)}, bf16[32,64,128]{2,1,0:T(8,128)(2,1)S(1)}) custom-call(s32[4,4]{1,0:T(4,128)S(1)} %copy-done.19, bf16[128,64,128]{2,1,0:T(8,128)(2,1)} %pair.3, f32[1,128]{1,0:T(1,128)} %bitcast.7, f32[1,128]{1,0:T(1,128)} %bitcast.10, bf16[128,256]{1,0:T(8,128)(2,1)} %weight.5), custom_call_target="tpu_custom_call" | custom-call | flops 1 | bytes 18000000 | tf_op jit(solution)/shard_map/left_front/pallas_call | solution.py:85
  25.9 10.8 %collective-permute-done.5.refs_1_.refs_7_ = bf16[32,128,128]{2,1,0:T(8,128)(2,1)S(1)} collective-permute-done((bf16[32,128,128]{2,1,0:T(8,128)(2,1)S(1)}, bf16[32,128,128]{2,1,0:T(8,128)(2,1)S(1)}, u32[]{:S(2)}, u32[]{:S(2)}) %collective-permute-start.5) | collective-permute-done | bytes 1048608 | tf_op jit(solution)/shard_map/ppermute | solution.py:310
  36.8 1.8 %collective-permute-start.7 = (bf16[16,128,128]{2,1,0:T(8,128)(2,1)S(1)}, bf16[16,128,128]{2,1,0:T(8,128)(2,1)S(1)}, u32[]{:S(2)}, u32[]{:S(2)}) collective-permute-start(bf16[16,128,128]{2,1,0:T(8,128)(2,1)S(1)} %slice.32), channel_id=1, source_target_pairs={{0,4},{1,5},{2,6},{3,7},{4,0},{5,1},{6,2},{7,3},{8,12},{9,13},{10,... | collective-permute-start | bytes 1572872 | tf_op jit(solution)/shard_map/ppermute | solution.py:310
  38.6 0.8 slice.33
  39.4 1.5 %collective-permute-start.12 = (bf16[16,128,128]{2,1,0:T(8,128)(2,1)}, bf16[16,128,128]{2,1,0:T(8,128)(2,1)}, u32[]{:S(2)}, u32[]{:S(2)}) collective-permute-start(bf16[16,128,128]{2,1,0:T(8,128)(2,1)} %slice.33), channel_id=1, source_target_pairs={{0,2},{1,3},{2,0},{3,1},{4,6},{5,7},{6,4},{7,5},{8,10},{9,11},{10,... | collective-permute-start | bytes 1572872 | tf_op jit(solution)/shard_map/ppermute | solution.py:310
  40.9 0.5 collective-permute-done.4.down.refs_3_
  41.5 1.2 collective-permute-done.2.up.refs_0_
  42.6 7.8 %collective-permute-done.7.refs_3_.refs_9_ = bf16[16,128,128]{2,1,0:T(8,128)(2,1)S(1)} collective-permute-done((bf16[16,128,128]{2,1,0:T(8,128)(2,1)S(1)}, bf16[16,128,128]{2,1,0:T(8,128)(2,1)S(1)}, u32[]{:S(2)}, u32[]{:S(2)}) %collective-permute-start.7) | collective-permute-done | bytes 524320 | tf_op jit(solution)/shard_map/ppermute | solution.py:310
  50.4 3.1 %right_partials.2 = (bf16[16,128,128]{2,1,0:T(8,128)(2,1)}, bf16[16,128,128]{2,1,0:T(8,128)(2,1)}, bf16[16,128,128]{2,1,0:T(8,128)(2,1)}, bf16[16,128,128]{2,1,0...) custom-call(bf16[32,64,128]{2,1,0:T(8,128)(2,1)S(1)} %get-tuple-element.32.left_mine, ...), custom_call_target="tpu_custom_call" | custom-call | flops 1 | bytes 8000000 | tf_op jit(solution)/shard_map/right_partials/pallas_call | solution.py:155
  53.6 4.3 %collective-permute-start.8 = (bf16[16,128,128]{2,1,0:T(8,128)(2,1)}, bf16[16,128,128]{2,1,0:T(8,128)(2,1)}, u32[]{:S(2)}, u32[]{:S(2)}) collective-permute-start(bf16[16,128,128]{2,1,0:T(8,128)(2,1)} %get-tuple-element.34), channel_id=1, source_target_pairs={{0,8},{8,16},{16,24},{1,9},{9,17},{17,25},{2,10},{10,18},{18,26},{... | collective-permute-start | bytes 1572872 | tf_op jit(solution)/shard_map/ppermute | solution.py:313
  57.9 1.3 collective-permute-start.10
  59.2 1.2 copy-done.2
  60.4 1.2 copy-done.5
  61.6 1.0 copy-done.13
  62.7 1.0 copy-done.15
  63.7 4.0 %right_partials.3 = (bf16[16,128,128]{2,1,0:T(8,128)(2,1)}, bf16[16,128,128]{2,1,0:T(8,128)(2,1)}, bf16[16,128,128]{2,1,0:T(8,128)(2,1)}, bf16[16,128,128]{2,1,0...) custom-call(bf16[32,64,128]{2,1,0:T(8,128)(2,1)S(1)} %copy-done.13, ...), custom_call_target="tpu_custom_call" | custom-call | flops 1 | bytes 8000000 | tf_op jit(solution)/shard_map/right_partials/pallas_call | solution.py:155
  67.7 5.3 %collective-permute-start.13 = (bf16[16,128,128]{2,1,0:T(8,128)(2,1)}, bf16[16,128,128]{2,1,0:T(8,128)(2,1)}, u32[]{:S(2)}, u32[]{:S(2)}) collective-permute-start(bf16[16,128,128]{2,1,0:T(8,128)(2,1)} %get-tuple-element.38), channel_id=1, source_target_pairs={{0,8},{8,16},{16,24},{1,9},{9,17},{17,25},{2,10},{10,18},{18,26},{... | collective-permute-start | bytes 1572872 | tf_op jit(solution)/shard_map/ppermute | solution.py:313
  73.1 1.3 collective-permute-start.15
  74.4 2.7 %fusion.3 = (bf16[16,128,128]{2,1,0:T(8,128)(2,1)}, bf16[16,128,128]{2,1,0:T(8,128)(2,1)}) fusion(bf16[16,128,128]{2,1,0:T(8,128)(2,1)} %get-tuple-element.35, bf16[16,128,128]{2,1,0:T(8,128)(2,1)} %collective-permute-done.10.refs_4_, pred[]{:T(512)S(6)} %ge.8, pred[]{:T(512)S(6)} %lt.12, bf16[16,128,128]{2,1,0:T(8,128)(2,1)} %collective-permute-done.8.refs_1_), kind=kLoop, calls=%fused_computation.7 | loop fusion | flops 2359296 | bytes 2621442 | tf_op jit(solution)/shard_map/convert_element_type | solution.py:349
  77.1 1.3 collective-permute-start.11
  78.4 5.3 %collective-permute-start.9 = (bf16[16,128,128]{2,1,0:T(8,128)(2,1)}, bf16[16,128,128]{2,1,0:T(8,128)(2,1)S(1)}, u32[]{:S(2)}, u32[]{:S(2)}) collective-permute-start(bf16[16,128,128]{2,1,0:T(8,128)(2,1)} %get-tuple-element.54), channel_id=1, source_target_pairs={{0,8},{8,16},{16,24},{1,9},{9,17},{17,25},{2,10},{10,18},{18,26},{... | collective-permute-start | bytes 1572872 | tf_op jit(solution)/shard_map/ppermute | solution.py:313
  83.7 6.4 %collective-permute-done.15.refs_4_ = bf16[16,128,128]{2,1,0:T(8,128)(2,1)} collective-permute-done((bf16[16,128,128]{2,1,0:T(8,128)(2,1)}, bf16[16,128,128]{2,1,0:T(8,128)(2,1)}, u32[]{:S(2)}, u32[]{:S(2)}) %collective-permute-start.15) | collective-permute-done | bytes 524320 | tf_op jit(solution)/shard_map/ppermute | solution.py:316
  90.1 1.8 %fusion.7 = (bf16[16,128,128]{2,1,0:T(8,128)(2,1)S(1)}, bf16[16,128,128]{2,1,0:T(8,128)(2,1)S(1)}) fusion(bf16[16,128,128]{2,1,0:T(8,128)(2,1)} %get-tuple-element.39, bf16[16,128,128]{2,1,0:T(8,128)(2,1)} %collective-permute-done.15.refs_4_, pred[]{:T(512)S(6)} %ge.8, pred[]{:T(512)S(6)} %lt.12, bf16[16,128,128]{2,1,0:T(8,128)(2,1)} %collective-permute-done.13.refs_1_), kind=kLoop, calls=%fused_computation.11 | loop fusion | flops 2359296 | bytes 2621442 | tf_op jit(solution)/shard_map/convert_element_type | solution.py:349
  91.9 1.4 collective-permute-start.16
  93.3 4.6 %collective-permute-start.14 = (bf16[16,128,128]{2,1,0:T(8,128)(2,1)S(1)}, bf16[16,128,128]{2,1,0:T(8,128)(2,1)S(1)}, u32[]{:S(2)}, u32[]{:S(2)}) collective-permute-start(bf16[16,128,128]{2,1,0:T(8,128)(2,1)S(1)} %get-tuple-element.52), channel_id=1, source_target_pairs={{0,8},{8,16},{16,24},{1,9},{9,17},{17,25},{2,10},{10,18},{18,26},{... | collective-permute-start | bytes 1572872 | tf_op jit(solution)/shard_map/ppermute | solution.py:313
  97.9 3.4 %collective-permute-done.11.refs_5_ = bf16[16,128,128]{2,1,0:T(8,128)(2,1)} collective-permute-done((bf16[16,128,128]{2,1,0:T(8,128)(2,1)}, bf16[16,128,128]{2,1,0:T(8,128)(2,1)}, u32[]{:S(2)}, u32[]{:S(2)}) %collective-permute-start.11) | collective-permute-done | bytes 524320 | tf_op jit(solution)/shard_map/ppermute | solution.py:316
  101.4 1.4 add_convert_fusion.1
  102.8 1.3 collective-permute-start.21
  104.3 4.6 %collective-permute-start.19 = (bf16[16,128,128]{2,1,0:T(8,128)(2,1)S(1)}, bf16[16,128,128]{2,1,0:T(8,128)(2,1)S(1)}, u32[]{:S(2)}, u32[]{:S(2)}) collective-permute-start(bf16[16,128,128]{2,1,0:T(8,128)(2,1)S(1)} %add_convert_fusion.3), channel_id=1, source_target_pairs={{0,8},{8,16},{16,24},{1,9},{9,17},{17,25},{2,10},{10,18},{18,26},{... | collective-permute-start | bytes 1572872 | tf_op jit(solution)/shard_map/ppermute | solution.py:313
  108.9 3.6 %collective-permute-done.16.refs_5_ = bf16[16,128,128]{2,1,0:T(8,128)(2,1)S(1)} collective-permute-done((bf16[16,128,128]{2,1,0:T(8,128)(2,1)S(1)}, bf16[16,128,128]{2,1,0:T(8,128)(2,1)S(1)}, u32[]{:S(2)}, u32[]{:S(2)}) %collective-permute-start.16) | collective-permute-done | bytes 524320 | tf_op jit(solution)/shard_map/ppermute | solution.py:316
  112.7 1.4 collective-permute-start.22
  114.1 2.3 %left_products.2 = (f32[16,64,128]{2,1,0:T(8,128)S(1)}, bf16[16,64,128]{2,1,0:T(8,128)(2,1)S(1)}) custom-call(bf16[32,128,128]{2,1,0:T(8,128)(2,1)S(1)} %copy-done.8, bf16[32,128,128]{2,1,0:T(8,128)(2,1)S(1)} %copy-done.6, bf16[16,128,128]{2,1,0:T(8,128)(2,1)} %collective-permute-done.8.refs_1_, bf16[16,128,128]{2,1,0:T(8,128)(2,1)S(1)} %collective-permute-done.9.refs_2_, ...), custom_call_target="tpu_custom_call" | custom-call | flops 1 | bytes 8000000 | tf_op jit(solution)/shard_map/left_products/pallas_call | solution.py:192
  116.7 4.7 %collective-permute-start.20 = (bf16[16,128,128]{2,1,0:T(8,128)(2,1)S(1)}, bf16[16,128,128]{2,1,0:T(8,128)(2,1)S(1)}, u32[]{:S(2)}, u32[]{:S(2)}) collective-permute-start(bf16[16,128,128]{2,1,0:T(8,128)(2,1)S(1)} %add_convert_fusion.2), channel_id=1, source_target_pairs={{0,8},{8,16},{16,24},{1,9},{9,17},{17,25},{2,10},{10,18},{18,26},{... | collective-permute-start | bytes 1572872 | tf_op jit(solution)/shard_map/ppermute | solution.py:313
  121.5 2.3 %left_products.3 = (f32[16,64,128]{2,1,0:T(8,128)S(1)}, bf16[16,64,128]{2,1,0:T(8,128)(2,1)S(1)}) custom-call(bf16[32,128,128]{2,1,0:T(8,128)(2,1)S(1)} %copy-done.8, bf16[32,128,128]{2,1,0:T(8,128)(2,1)S(1)} %copy-done.6, bf16[16,128,128]{2,1,0:T(8,128)(2,1)} %collective-permute-done.13.refs_1_, bf16[16,128,128]{2,1,0:T(8,128)(2,1)S(1)} %collective-permute-done.14.refs_2_, ...), custom_call_target="tpu_custom_call" | custom-call | flops 1 | bytes 8000000 | tf_op jit(solution)/shard_map/left_products/pallas_call | solution.py:192
  123.8 0.6 collective-permute-start.18
  124.6 7.3 %collective-permute-done.22.refs_9_ = bf16[16,128,128]{2,1,0:T(8,128)(2,1)S(1)} collective-permute-done((bf16[16,128,128]{2,1,0:T(8,128)(2,1)S(1)}, bf16[16,128,128]{2,1,0:T(8,128)(2,1)S(1)}, u32[]{:S(2)}, u32[]{:S(2)}) %collective-permute-start.22) | collective-permute-done | bytes 524320 | tf_op jit(solution)/shard_map/ppermute | solution.py:316
  132.1 1.5 %collective-permute-done.24.refs_11_ = bf16[16,64,128]{2,1,0:T(8,128)(2,1)S(1)} collective-permute-done((bf16[16,64,128]{2,1,0:T(8,128)(2,1)S(1)}, bf16[16,64,128]{2,1,0:T(8,128)(2,1)S(1)}, u32[]{:S(2)}, u32[]{:S(2)}) %collective-permute-start.24) | collective-permute-done | bytes 262176 | tf_op jit(solution)/shard_map/ppermute | solution.py:310
  133.6 11.2 %tail.1 = bf16[128,64,128]{2,1,0:T(8,128)(2,1)} custom-call(s32[4,4]{1,0:T(4,128)S(1)} %copy-done.19, bf16[128,64,128]{2,1,0:T(8,128)(2,1)S(1)} %copy-done, f32[1,128]{1,0:T(1,128)S(1)} %bitcast.8, f32[1,128]{1,0:T(1,128)S(1)} %bitcast.11, bf16[128,256]{1,0:T(8,128)(2,1)S(1)} %copy-done.18, f32[16,64,128]{2,1,0:T(8,128)S(1)} %get-tuple-element.37.refs_0_, ...), custom_call_target="tpu_custom_call" | custom-call | flops 1 | bytes 8000000 | tf_op jit(solution)/shard_map/tail/pallas_call | solution.py:267
  (75 shorter events, 1.7 us)
Async XLA Ops:
  0.0 4.8 %copy-start.19 = (s32[4,4]{1,0:T(4,128)S(1)}, s32[4,4]{1,0:T(4,128)}, u32[]{:S(2)}) copy-start(s32[4,4]{1,0:T(4,128)} %mask.5) | copy-start | bytes 196
  1.1 2.1 %collective-permute-start = (bf16[64,32,128]{2,1,0:T(8,128)(2,1)S(1)}, bf16[64,32,128]{2,1,0:T(8,128)(2,1)S(1)}, u32[]{:S(2)}, u32[]{:S(2)}) collective-permute-start(bf16[64,32,128]{2,1,0:T(8,128)(2,1)S(1)} %dynamic-slice_bitcast_fusion), channel_id=1, source_target_pairs={{0,1},{1,0},{2,3},{3,2},{4,5},{5,4},{6,7},{7,6},{8,9},{9,8},{10,11... | collective-permute-start | bytes 1572872 | tf_op jit(solution)/shard_map/ppermute | solution.py:310
  3.2 1.2 copy-start.9
  10.0 4.6 %collective-permute-start.1 = (bf16[32,64,128]{2,1,0:T(8,128)(2,1)S(1)}, bf16[32,64,128]{2,1,0:T(8,128)(2,1)S(1)}, u32[]{:S(2)}, u32[]{:S(2)}) collective-permute-start(bf16[32,64,128]{2,1,0:T(8,128)(2,1)S(1)} %get-tuple-element.30), channel_id=1, source_target_pairs={{0,1},{1,0},{2,3},{3,2},{4,5},{5,4},{6,7},{7,6},{8,9},{9,8},{10,11... | collective-permute-start | bytes 1572872 | tf_op jit(solution)/shard_map/ppermute | solution.py:310
  10.4 26.3 %collective-permute-start.5 = (bf16[32,128,128]{2,1,0:T(8,128)(2,1)S(1)}, bf16[32,128,128]{2,1,0:T(8,128)(2,1)S(1)}, u32[]{:S(2)}, u32[]{:S(2)}) collective-permute-start(bf16[32,128,128]{2,1,0:T(8,128)(2,1)S(1)} %pack.1.refs_0_.refs_6_), channel_id=1, source_target_pairs={{0,2},{1,3},{2,0},{3,1},{4,6},{5,7},{6,4},{7,5},{8,10},{9,11},{10,... | collective-permute-start | bytes 3145736 | tf_op jit(solution)/shard_map/ppermute | solution.py:310
  13.0 25.5 %collective-permute-start.6 = (bf16[32,128,128]{2,1,0:T(8,128)(2,1)S(1)}, bf16[32,128,128]{2,1,0:T(8,128)(2,1)S(1)}, u32[]{:S(2)}, u32[]{:S(2)}) collective-permute-start(bf16[32,128,128]{2,1,0:T(8,128)(2,1)S(1)} %pack.1.refs_0_.refs_6_), channel_id=1, source_target_pairs={{0,4},{1,5},{2,6},{3,7},{4,0},{5,1},{6,2},{7,3},{8,12},{9,13},{10,... | collective-permute-start | bytes 3145736 | tf_op jit(solution)/shard_map/ppermute | solution.py:310
  14.7 24.7 %copy-start.7 = (bf16[32,128,128]{2,1,0:T(8,128)(2,1)}, bf16[32,128,128]{2,1,0:T(8,128)(2,1)S(1)}, u32[]{:S(2)}) copy-start(bf16[32,128,128]{2,1,0:T(8,128)(2,1)S(1)} %constant_dynamic-update-slice_fusion.own) | copy-start | bytes 3145732
  14.7 26.8 %collective-permute-start.4 = (bf16[32,128,128]{2,1,0:T(8,128)(2,1)S(1)}, bf16[32,128,128]{2,1,0:T(8,128)(2,1)S(1)}, u32[]{:S(2)}, u32[]{:S(2)}) collective-permute-start(bf16[32,128,128]{2,1,0:T(8,128)(2,1)S(1)} %constant_dynamic-update-slice_fusion.own), channel_id=1, source_target_pairs={{8,0},{16,8},{24,16},{9,1},{17,9},{25,17},{10,2},{18,10},{26,18},{... | collective-permute-start | bytes 3145736 | tf_op jit(solution)/shard_map/ppermute | solution.py:316
  16.0 26.6 %collective-permute-start.2 = (bf16[32,128,128]{2,1,0:T(8,128)(2,1)S(1)}, bf16[32,128,128]{2,1,0:T(8,128)(2,1)S(1)}, u32[]{:S(2)}, u32[]{:S(2)}) collective-permute-start(bf16[32,128,128]{2,1,0:T(8,128)(2,1)S(1)} %constant_dynamic-update-slice_fusion.own), channel_id=1, source_target_pairs={{0,8},{8,16},{16,24},{1,9},{9,17},{17,25},{2,10},{10,18},{18,26},{... | collective-permute-start | bytes 3145736 | tf_op jit(solution)/shard_map/ppermute | solution.py:313
  25.8 27.7 %copy-start.12 = (bf16[32,64,128]{2,1,0:T(8,128)(2,1)}, bf16[32,64,128]{2,1,0:T(8,128)(2,1)S(1)}, u32[]{:S(2)}) copy-start(bf16[32,64,128]{2,1,0:T(8,128)(2,1)S(1)} %get-tuple-element.32.left_mine) | copy-start | bytes 1572868
  25.8 15.1 %collective-permute-start.3 = (bf16[32,64,128]{2,1,0:T(8,128)(2,1)S(1)}, bf16[32,64,128]{2,1,0:T(8,128)(2,1)S(1)}, u32[]{:S(2)}, u32[]{:S(2)}) collective-permute-start(bf16[32,64,128]{2,1,0:T(8,128)(2,1)S(1)} %get-tuple-element.33), channel_id=1, source_target_pairs={{0,1},{1,0},{2,3},{3,2},{4,5},{5,4},{6,7},{7,6},{8,9},{9,8},{10,11... | collective-permute-start | bytes 1572872 | tf_op jit(solution)/shard_map/ppermute | solution.py:310
  36.8 13.7 %collective-permute-start.7 = (bf16[16,128,128]{2,1,0:T(8,128)(2,1)S(1)}, bf16[16,128,128]{2,1,0:T(8,128)(2,1)S(1)}, u32[]{:S(2)}, u32[]{:S(2)}) collective-permute-start(bf16[16,128,128]{2,1,0:T(8,128)(2,1)S(1)} %slice.32), channel_id=1, source_target_pairs={{0,4},{1,5},{2,6},{3,7},{4,0},{5,1},{6,2},{7,3},{8,12},{9,13},{10,... | collective-permute-start | bytes 1572872 | tf_op jit(solution)/shard_map/ppermute | solution.py:310
  39.4 19.7 %collective-permute-start.12 = (bf16[16,128,128]{2,1,0:T(8,128)(2,1)}, bf16[16,128,128]{2,1,0:T(8,128)(2,1)}, u32[]{:S(2)}, u32[]{:S(2)}) collective-permute-start(bf16[16,128,128]{2,1,0:T(8,128)(2,1)} %slice.33), channel_id=1, source_target_pairs={{0,2},{1,3},{2,0},{3,1},{4,6},{5,7},{6,4},{7,5},{8,10},{9,11},{10,... | collective-permute-start | bytes 1572872 | tf_op jit(solution)/shard_map/ppermute | solution.py:310
  40.9 12.6 %copy-start.14 = (bf16[32,64,128]{2,1,0:T(8,128)(2,1)}, bf16[32,64,128]{2,1,0:T(8,128)(2,1)S(1)}, u32[]{:S(2)}) copy-start(bf16[32,64,128]{2,1,0:T(8,128)(2,1)S(1)} %collective-permute-done.3.left_other) | copy-start | bytes 1572868
  41.5 12.1 %copy-start.1 = (bf16[32,128,128]{2,1,0:T(8,128)(2,1)}, bf16[32,128,128]{2,1,0:T(8,128)(2,1)S(1)}, u32[]{:S(2)}) copy-start(bf16[32,128,128]{2,1,0:T(8,128)(2,1)S(1)} %collective-permute-done.4.down.refs_3_) | copy-start | bytes 3145732
  42.6 10.9 %copy-start.4 = (bf16[32,128,128]{2,1,0:T(8,128)(2,1)}, bf16[32,128,128]{2,1,0:T(8,128)(2,1)S(1)}, u32[]{:S(2)}) copy-start(bf16[32,128,128]{2,1,0:T(8,128)(2,1)S(1)} %collective-permute-done.2.up.refs_0_) | copy-start | bytes 3145732
  50.4 3.1 %copy-start.10 = (bf16[16,128,128]{2,1,0:T(8,128)(2,1)}, bf16[16,128,128]{2,1,0:T(8,128)(2,1)S(1)}, u32[]{:S(2)}) copy-start(bf16[16,128,128]{2,1,0:T(8,128)(2,1)S(1)} %collective-permute-done.7.refs_3_.refs_9_) | copy-start | bytes 1572868
  53.6 20.8 %collective-permute-start.8 = (bf16[16,128,128]{2,1,0:T(8,128)(2,1)}, bf16[16,128,128]{2,1,0:T(8,128)(2,1)}, u32[]{:S(2)}, u32[]{:S(2)}) collective-permute-start(bf16[16,128,128]{2,1,0:T(8,128)(2,1)} %get-tuple-element.34), channel_id=1, source_target_pairs={{0,8},{8,16},{16,24},{1,9},{9,17},{17,25},{2,10},{10,18},{18,26},{... | collective-permute-start | bytes 1572872 | tf_op jit(solution)/shard_map/ppermute | solution.py:313
  57.9 16.5 %collective-permute-start.10 = (bf16[16,128,128]{2,1,0:T(8,128)(2,1)}, bf16[16,128,128]{2,1,0:T(8,128)(2,1)}, u32[]{:S(2)}, u32[]{:S(2)}) collective-permute-start(bf16[16,128,128]{2,1,0:T(8,128)(2,1)} %get-tuple-element.36), channel_id=1, source_target_pairs={{8,0},{16,8},{24,16},{9,1},{17,9},{25,17},{10,2},{18,10},{26,18},{... | collective-permute-start | bytes 1572872 | tf_op jit(solution)/shard_map/ppermute | solution.py:316
  59.2 1.2 copy-start.2
  67.7 16.0 %collective-permute-start.13 = (bf16[16,128,128]{2,1,0:T(8,128)(2,1)}, bf16[16,128,128]{2,1,0:T(8,128)(2,1)}, u32[]{:S(2)}, u32[]{:S(2)}) collective-permute-start(bf16[16,128,128]{2,1,0:T(8,128)(2,1)} %get-tuple-element.38), channel_id=1, source_target_pairs={{0,8},{8,16},{16,24},{1,9},{9,17},{17,25},{2,10},{10,18},{18,26},{... | collective-permute-start | bytes 1572872 | tf_op jit(solution)/shard_map/ppermute | solution.py:313
  73.1 17.1 %collective-permute-start.15 = (bf16[16,128,128]{2,1,0:T(8,128)(2,1)}, bf16[16,128,128]{2,1,0:T(8,128)(2,1)}, u32[]{:S(2)}, u32[]{:S(2)}) collective-permute-start(bf16[16,128,128]{2,1,0:T(8,128)(2,1)} %get-tuple-element.40), channel_id=1, source_target_pairs={{8,0},{16,8},{24,16},{9,1},{17,9},{25,17},{10,2},{18,10},{26,18},{... | collective-permute-start | bytes 1572872 | tf_op jit(solution)/shard_map/ppermute | solution.py:316
  77.1 24.3 %collective-permute-start.11 = (bf16[16,128,128]{2,1,0:T(8,128)(2,1)}, bf16[16,128,128]{2,1,0:T(8,128)(2,1)}, u32[]{:S(2)}, u32[]{:S(2)}) collective-permute-start(bf16[16,128,128]{2,1,0:T(8,128)(2,1)} %get-tuple-element.53), channel_id=1, source_target_pairs={{8,0},{16,8},{24,16},{9,1},{17,9},{25,17},{10,2},{18,10},{26,18},{... | collective-permute-start | bytes 1572872 | tf_op jit(solution)/shard_map/ppermute | solution.py:316
  78.4 23.0 %copy-start.24 = (bf16[16,128,128]{2,1,0:T(8,128)(2,1)S(1)}, bf16[16,128,128]{2,1,0:T(8,128)(2,1)}, u32[]{:S(2)}) copy-start(bf16[16,128,128]{2,1,0:T(8,128)(2,1)} %get-tuple-element.49) | copy-start | bytes 1572868
  78.4 25.7 %collective-permute-start.9 = (bf16[16,128,128]{2,1,0:T(8,128)(2,1)}, bf16[16,128,128]{2,1,0:T(8,128)(2,1)S(1)}, u32[]{:S(2)}, u32[]{:S(2)}) collective-permute-start(bf16[16,128,128]{2,1,0:T(8,128)(2,1)} %get-tuple-element.54), channel_id=1, source_target_pairs={{0,8},{8,16},{16,24},{1,9},{9,17},{17,25},{2,10},{10,18},{18,26},{... | collective-permute-start | bytes 1572872 | tf_op jit(solution)/shard_map/ppermute | solution.py:313
  90.1 14.0 %copy-start.23 = (bf16[16,128,128]{2,1,0:T(8,128)(2,1)S(1)}, bf16[16,128,128]{2,1,0:T(8,128)(2,1)}, u32[]{:S(2)}) copy-start(bf16[16,128,128]{2,1,0:T(8,128)(2,1)} %get-tuple-element.46) | copy-start | bytes 1572868
  91.9 20.6 %copy-start.25 = (bf16[16,128,128]{2,1,0:T(8,128)(2,1)S(1)}, bf16[16,128,128]{2,1,0:T(8,128)(2,1)}, u32[]{:S(2)}) copy-start(bf16[16,128,128]{2,1,0:T(8,128)(2,1)} %get-tuple-element.50) | copy-start | bytes 1572868
  91.9 20.6 %collective-permute-start.16 = (bf16[16,128,128]{2,1,0:T(8,128)(2,1)S(1)}, bf16[16,128,128]{2,1,0:T(8,128)(2,1)S(1)}, u32[]{:S(2)}, u32[]{:S(2)}) collective-permute-start(bf16[16,128,128]{2,1,0:T(8,128)(2,1)S(1)} %get-tuple-element.51), channel_id=1, source_target_pairs={{8,0},{16,8},{24,16},{9,1},{17,9},{25,17},{10,2},{18,10},{26,18},{... | collective-permute-start | bytes 1572872 | tf_op jit(solution)/shard_map/ppermute | solution.py:316
  93.3 23.1 %collective-permute-start.14 = (bf16[16,128,128]{2,1,0:T(8,128)(2,1)S(1)}, bf16[16,128,128]{2,1,0:T(8,128)(2,1)S(1)}, u32[]{:S(2)}, u32[]{:S(2)}) collective-permute-start(bf16[16,128,128]{2,1,0:T(8,128)(2,1)S(1)} %get-tuple-element.52), channel_id=1, source_target_pairs={{0,8},{8,16},{16,24},{1,9},{9,17},{17,25},{2,10},{10,18},{18,26},{... | collective-permute-start | bytes 1572872 | tf_op jit(solution)/shard_map/ppermute | solution.py:313
  101.3 12.8 %copy-start.3 = (bf16[32,128,128]{2,1,0:T(8,128)(2,1)S(1)}, bf16[32,128,128]{2,1,0:T(8,128)(2,1)}, u32[]{:S(2)}) copy-start(bf16[32,128,128]{2,1,0:T(8,128)(2,1)} %copy-done.1) | copy-start | bytes 3145732
  101.4 12.8 %copy-start.6 = (bf16[32,128,128]{2,1,0:T(8,128)(2,1)S(1)}, bf16[32,128,128]{2,1,0:T(8,128)(2,1)}, u32[]{:S(2)}) copy-start(bf16[32,128,128]{2,1,0:T(8,128)(2,1)} %copy-done.4) | copy-start | bytes 3145732
  101.4 12.8 %copy-start.8 = (bf16[32,128,128]{2,1,0:T(8,128)(2,1)S(1)}, bf16[32,128,128]{2,1,0:T(8,128)(2,1)}, u32[]{:S(2)}) copy-start(bf16[32,128,128]{2,1,0:T(8,128)(2,1)} %copy-done.7) | copy-start | bytes 3145732
  101.4 12.8 %copy-start.11 = (bf16[16,128,128]{2,1,0:T(8,128)(2,1)S(1)}, bf16[16,128,128]{2,1,0:T(8,128)(2,1)}, u32[]{:S(2)}) copy-start(bf16[16,128,128]{2,1,0:T(8,128)(2,1)} %copy-done.10) | copy-start | bytes 1572868
  102.8 21.0 %collective-permute-start.21 = (bf16[16,128,128]{2,1,0:T(8,128)(2,1)S(1)}, bf16[16,128,128]{2,1,0:T(8,128)(2,1)S(1)}, u32[]{:S(2)}, u32[]{:S(2)}) collective-permute-start(bf16[16,128,128]{2,1,0:T(8,128)(2,1)S(1)} %add_convert_fusion.1), channel_id=1, source_target_pairs={{8,0},{16,8},{24,16},{9,1},{17,9},{25,17},{10,2},{18,10},{26,18},{... | collective-permute-start | bytes 1572872 | tf_op jit(solution)/shard_map/ppermute | solution.py:316
  104.3 20.0 %collective-permute-start.19 = (bf16[16,128,128]{2,1,0:T(8,128)(2,1)S(1)}, bf16[16,128,128]{2,1,0:T(8,128)(2,1)S(1)}, u32[]{:S(2)}, u32[]{:S(2)}) collective-permute-start(bf16[16,128,128]{2,1,0:T(8,128)(2,1)S(1)} %add_convert_fusion.3), channel_id=1, source_target_pairs={{0,8},{8,16},{16,24},{1,9},{9,17},{17,25},{2,10},{10,18},{18,26},{... | collective-permute-start | bytes 1572872 | tf_op jit(solution)/shard_map/ppermute | solution.py:313
  112.7 3.8 %copy-start.22 = (bf16[16,128,128]{2,1,0:T(8,128)(2,1)S(1)}, bf16[16,128,128]{2,1,0:T(8,128)(2,1)}, u32[]{:S(2)}) copy-start(bf16[16,128,128]{2,1,0:T(8,128)(2,1)} %get-tuple-element.48) | copy-start | bytes 1572868
  112.7 19.1 %collective-permute-start.22 = (bf16[16,128,128]{2,1,0:T(8,128)(2,1)S(1)}, bf16[16,128,128]{2,1,0:T(8,128)(2,1)S(1)}, u32[]{:S(2)}, u32[]{:S(2)}) collective-permute-start(bf16[16,128,128]{2,1,0:T(8,128)(2,1)S(1)} %add_convert_fusion), channel_id=1, source_target_pairs={{8,0},{16,8},{24,16},{9,1},{17,9},{25,17},{10,2},{18,10},{26,18},{... | collective-permute-start | bytes 1572872 | tf_op jit(solution)/shard_map/ppermute | solution.py:316
  116.6 7.7 %copy-start.16 = (bf16[16,128,128]{2,1,0:T(8,128)(2,1)S(1)}, bf16[16,128,128]{2,1,0:T(8,128)(2,1)}, u32[]{:S(2)}) copy-start(bf16[16,128,128]{2,1,0:T(8,128)(2,1)} %get-tuple-element.44.refs_4_) | copy-start | bytes 1572868
  116.7 15.2 %copy-start.17 = (bf16[16,128,128]{2,1,0:T(8,128)(2,1)S(1)}, bf16[16,128,128]{2,1,0:T(8,128)(2,1)}, u32[]{:S(2)}) copy-start(bf16[16,128,128]{2,1,0:T(8,128)(2,1)} %get-tuple-element.45.refs_5_) | copy-start | bytes 1572868
  116.7 15.2 %collective-permute-start.20 = (bf16[16,128,128]{2,1,0:T(8,128)(2,1)S(1)}, bf16[16,128,128]{2,1,0:T(8,128)(2,1)S(1)}, u32[]{:S(2)}, u32[]{:S(2)}) collective-permute-start(bf16[16,128,128]{2,1,0:T(8,128)(2,1)S(1)} %add_convert_fusion.2), channel_id=1, source_target_pairs={{0,8},{8,16},{16,24},{1,9},{9,17},{17,25},{2,10},{10,18},{18,26},{... | collective-permute-start | bytes 1572872 | tf_op jit(solution)/shard_map/ppermute | solution.py:313
  121.4 10.7 %collective-permute-start.17 = (bf16[16,64,128]{2,1,0:T(8,128)(2,1)S(1)}, bf16[16,64,128]{2,1,0:T(8,128)(2,1)S(1)}, u32[]{:S(2)}, u32[]{:S(2)}) collective-permute-start(bf16[16,64,128]{2,1,0:T(8,128)(2,1)S(1)} %get-tuple-element.42), channel_id=1, source_target_pairs={{0,1},{1,0},{2,3},{3,2},{4,5},{5,4},{6,7},{7,6},{8,9},{9,8},{10,11... | collective-permute-start | bytes 786440 | tf_op jit(solution)/shard_map/ppermute | solution.py:310
  121.4 12.1 %copy-start.18 = (bf16[128,256]{1,0:T(8,128)(2,1)S(1)}, bf16[128,256]{1,0:T(8,128)(2,1)}, u32[]{:S(2)}) copy-start(bf16[128,256]{1,0:T(8,128)(2,1)} %weight.5) | copy-start | bytes 196612
  123.7 9.8 %copy-start = (bf16[128,64,128]{2,1,0:T(8,128)(2,1)S(1)}, bf16[128,64,128]{2,1,0:T(8,128)(2,1)}, u32[]{:S(2)}) copy-start(bf16[128,64,128]{2,1,0:T(8,128)(2,1)} %pair.3) | copy-start | bytes 6291460
  123.7 9.8 %copy-start.20 = (f32[128]{0:T(128)S(1)}, f32[128]{0:T(128)}, u32[]{:S(2)}) copy-start(f32[128]{0:T(128)} %param.8) | copy-start | bytes 1540
  123.8 9.8 %copy-start.21 = (f32[128]{0:T(128)S(1)}, f32[128]{0:T(128)}, u32[]{:S(2)}) copy-start(f32[128]{0:T(128)} %param.9) | copy-start | bytes 1540
  123.8 8.3 %collective-permute-start.18 = (bf16[16,64,128]{2,1,0:T(8,128)(2,1)S(1)}, bf16[16,64,128]{2,1,0:T(8,128)(2,1)S(1)}, u32[]{:S(2)}, u32[]{:S(2)}) collective-permute-start(bf16[16,64,128]{2,1,0:T(8,128)(2,1)S(1)} %get-tuple-element.43), channel_id=1, source_target_pairs={{0,1},{1,0},{2,3},{3,2},{4,5},{5,4},{6,7},{7,6},{8,9},{9,8},{10,11... | collective-permute-start | bytes 786440 | tf_op jit(solution)/shard_map/ppermute | solution.py:310
  124.5 7.6 %collective-permute-start.23 = (bf16[16,64,128]{2,1,0:T(8,128)(2,1)S(1)}, bf16[16,64,128]{2,1,0:T(8,128)(2,1)S(1)}, u32[]{:S(2)}, u32[]{:S(2)}) collective-permute-start(bf16[16,64,128]{2,1,0:T(8,128)(2,1)S(1)} %add_convert_fusion.5), channel_id=1, source_target_pairs={{0,1},{1,0},{2,3},{3,2},{4,5},{5,4},{6,7},{7,6},{8,9},{9,8},{10,11... | collective-permute-start | bytes 786440 | tf_op jit(solution)/shard_map/ppermute | solution.py:310
  131.9 1.6 %collective-permute-start.24 = (bf16[16,64,128]{2,1,0:T(8,128)(2,1)S(1)}, bf16[16,64,128]{2,1,0:T(8,128)(2,1)S(1)}, u32[]{:S(2)}, u32[]{:S(2)}) collective-permute-start(bf16[16,64,128]{2,1,0:T(8,128)(2,1)S(1)} %add_convert_fusion.4), channel_id=1, source_target_pairs={{0,1},{1,0},{2,3},{3,2},{4,5},{5,4},{6,7},{7,6},{8,9},{9,8},{10,11... | collective-permute-start | bytes 786440 | tf_op jit(solution)/shard_map/ppermute | solution.py:310
  (3 other events, 3.3 us)

commit v6 on v5

--- a/solution.py
+++ b/solution.py
@@ -12,7 +12,7 @@
 STEP = 8
 KEYS = 16
 CORES = 2
-VMEM_LIMIT = 12 * 1024 * 1024
+VMEM_LIMIT = 18 * 1024 * 1024
 PARAMS = pltpu.CompilerParams(vmem_limit_bytes=VMEM_LIMIT)
 FRONT_COST = pl.CostEstimate(flops=1, bytes_accessed=18_000_000, transcendentals=0)
 COST = pl.CostEstimate(flops=1, bytes_accessed=8_000_000, transcendentals=0)
@@ -133,8 +133,24 @@
     return pl.BlockSpec((STEP,) + array.shape[1:], lambda g: (first + g, 0, 0))
 
 
-def partial_kernel(n, left_mine, left_other, up, down, *refs):
-    blocks, outs, (up_next, down_next, sums) = refs[:n], refs[n : 2 * n], refs[2 * n :]
+def lanes(n):
+    row = lax.axis_index("row")
+    even = lax.rem(row, 2) == 0
+    return even, jnp.where(even, row + 1 < n, True), jnp.where(even, row > 0, row + 1 < n)
+
+
+def onward(by_a, by_b, up_sums, down_sums, t, n):
+    row = lax.axis_index("row")
+    even, use_a, use_b = lanes(n)
+    up = jnp.where(row < t, up_sums.astype(jnp.float32), 0.0)
+    down = jnp.where(row >= n - t, down_sums.astype(jnp.float32), 0.0)
+    out_a = jnp.where(use_b, by_b.astype(jnp.float32), 0.0) + jnp.where(even, up, down)
+    out_b = jnp.where(use_a, by_a.astype(jnp.float32), 0.0) + jnp.where(even, down, up)
+    return out_a.astype(jnp.bfloat16), out_b.astype(jnp.bfloat16)
+
+
+def partial_kernel(n, left_mine, left_other, by_a, by_b, *refs):
+    blocks, outs, (next_a, next_b, sums) = refs[:n], refs[n : 2 * n], refs[2 * n :]
     row, chip = lax.axis_index("row"), lax.axis_index("col") // CORES
     for c in range(STEP):
         lhs = jnp.concatenate((left_mine[c], left_other[c]), axis=0)
@@ -143,18 +159,22 @@
             sums[away, c] = lax.dot_general(lhs, block[c], BY_LAST, preferred_element_type=jnp.float32).astype(jnp.bfloat16)
     for s, out in enumerate(outs):
         out[...] = sums[s]
-    up_next[...] = jnp.where(row < 1, sums[n - 1], up[...])
-    down_next[...] = jnp.where(row >= n - 1, sums[1], down[...])
-
-
-def partial_products(left_mine, left_other, up, down, blocks, chunk):
+    next_a[...], next_b[...] = onward(by_a[...], by_b[...], sums[n - 1], sums[1], 1, n)
+
+
+def in_hbm(*values):
+    return [pltpu.with_memory_space_constraint(v, pltpu.HBM) for v in values]
+
+
+def partial_products(left_mine, left_other, by_a, by_b, blocks, chunk):
     rows = blocks[0].shape[1]
     ks, chans = left_mine.shape[1], left_mine.shape[0] // CHUNKS
     n = len(blocks)
-    args = (left_mine, left_other, up, down, *blocks)
+    args = (left_mine, left_other, by_a, by_b, *blocks)
     return pl.pallas_call(
         functools.partial(partial_kernel, n),
-        out_shape=[pltpu.HBM((chans, CORES * ks, rows), jnp.bfloat16)] * (n + 2),
+        out_shape=[pltpu.HBM((chans, CORES * ks, rows), jnp.bfloat16)] * n
+        + [jax.ShapeDtypeStruct((chans, CORES * ks, rows), jnp.bfloat16)] * 2,
         grid=(chans // STEP,),
         in_specs=[chunk_spec(v, chans, chunk) for v in args],
         out_specs=[pl.BlockSpec((STEP, CORES * ks, rows), lambda g: (g, 0, 0))] * (n + 2),
@@ -166,17 +186,20 @@
 
 
 def left_kernel(n, own, *refs):
-    ups, downs, refs = refs[: n - 1], refs[n - 1 : 2 * n - 2], refs[2 * n - 2 :]
+    by_a, by_b, refs = refs[: n - 1], refs[n - 1 : 2 * n - 2], refs[2 * n - 2 :]
     blocks, (mine, theirs, panel) = refs[:n], refs[n:]
     row, chip = lax.axis_index("row"), lax.axis_index("col") // CORES
+    even = lanes(n)[0]
     ks = mine.shape[1]
     for c in range(STEP):
         for m, block in enumerate(blocks):
             panel[c, jnp.bitwise_xor(chip, m)] = block[c]
-        acts, grads = [], []
-        for s in range(n):
+        acts, grads = [own[c]], [panel[c, row]]
+        for s in range(1, n):
+            from_above = jnp.where(even, by_a[s - 1][c], by_b[s - 1][c])
+            from_below = jnp.where(even, by_b[n - s - 1][c], by_a[n - s - 1][c])
+            acts.append(jnp.where(row + s < n, from_above, from_below))
             grads.append(panel[c, lax.rem(row + s, n)])
-            acts.append(own[c] if s == 0 else jnp.where(row + s < n, downs[s - 1][c], ups[n - s - 1][c]))
         out = jnp.dot(
             jnp.concatenate(acts, axis=1), jnp.concatenate(grads, axis=0), preferred_element_type=jnp.float32
         )
@@ -184,11 +207,11 @@
         theirs[c] = out[ks:].astype(jnp.bfloat16)
 
 
-def left_products(own, ups, downs, blocks, chunk):
-    chans, ks, rows = ups[-1].shape
+def left_products(own, by_a, by_b, blocks, chunk):
+    chans, ks, rows = by_a[-1].shape
     n = len(blocks)
     out = pl.BlockSpec((STEP, ks // CORES, rows), lambda g: (g, 0, 0))
-    args = (own, *ups, *downs, *blocks)
+    args = (own, *by_a, *by_b, *blocks)
     return pl.pallas_call(
         functools.partial(left_kernel, n),
         out_shape=[
@@ -205,9 +228,15 @@
     )(*args)
 
 
-def tail_kernel(mask, pair, gain, bias, weight, *refs):
+def arrived_total(own, by_a, by_b, n):
+    _, use_a, use_b = lanes(n)
+    total = own.astype(jnp.float32) + jnp.where(use_a, by_a.astype(jnp.float32), 0.0)
+    return total + jnp.where(use_b, by_b.astype(jnp.float32), 0.0)
+
+
+def tail_kernel(n, mask, pair, gain, bias, weight, *refs):
     groups = [refs[i * CHUNKS : (i + 1) * CHUNKS] for i in range(6)]
-    left_mine, left_other, partials, ups, downs, right_other = groups
+    left_mine, left_other, partials, by_a, by_b, right_other = groups
     out, flipped, turned, normed, inverses, grads, right_flat, left_flat, gain_col, bias_col, weight_t = refs[6 * CHUNKS :]
     rows, keys, _ = pair.shape
     hidden = weight.shape[1] // 4
@@ -222,8 +251,8 @@
         flat[pl.ds(first, part * keys), :] = value.astype(jnp.float32).reshape(part * keys, rows)
 
     for chunk in range(CHUNKS):
-        own, up, down = (ref[chunk][...].astype(jnp.float32) for ref in (partials, ups, downs))
-        put(right_flat, core, chunk, own + up + down)
+        total = arrived_total(partials[chunk][...], by_a[chunk][...], by_b[chunk][...], n)
+        put(right_flat, core, chunk, total)
         put(right_flat, 1 - core, chunk, right_other[chunk][...])
         put(left_flat, core, chunk, left_mine[chunk][...])
         put(left_flat, 1 - core, chunk, left_other[chunk][...])
@@ -257,7 +286,7 @@
     out[...] = jnp.transpose(flipped[...], (1, 0, 2))
 
 
-def tail(pair, gain, bias, proj_weight, tile_mask, left_mine, left_other, partials, ups, downs, right_other):
+def tail(pair, gain, bias, proj_weight, tile_mask, left_mine, left_other, partials, by_a, by_b, right_other):
     rows, cols, chans = pair.shape
     width = proj_weight.shape[1]
     part = width // 4 // CORES // CHUNKS
@@ -265,7 +294,7 @@
     cells = pl.BlockSpec((rows, KEYS, chans), lambda g: (0, g, 0))
     small = [pl.BlockSpec((part, KEYS, rows), lambda g: (0, g, 0))] * CHUNKS
     return pl.pallas_call(
-        tail_kernel,
+        functools.partial(tail_kernel, lax.axis_size("row")),
         out_shape=jax.ShapeDtypeStruct(pair.shape, jnp.bfloat16),
         grid=(cols // KEYS,),
         in_specs=[
@@ -292,7 +321,7 @@
         compiler_params=PARAMS,
         cost_estimate=COST,
         name="tail",
-    )(tile_mask, pair, gain, bias, proj_weight, *left_mine, *left_other, *partials, *ups, *downs, *right_other)
+    )(tile_mask, pair, gain, bias, proj_weight, *left_mine, *left_other, *partials, *by_a, *by_b, *right_other)
 
 
 def after(value, *others):
@@ -301,7 +330,6 @@
 
 def shards(pair, grad_x, norm_gain, norm_bias, proj_weight, tile_mask):
     n, n_col = lax.axis_size("row"), lax.axis_size("col")
-    row = lax.axis_index("row")
     half = grad_x.shape[2] // CORES
     part = half // CHUNKS
     gain, bias = norm_gain[None, :], norm_bias[None, :]
@@ -309,14 +337,18 @@
     def exchange(value, mask):
         return lax.ppermute(value, "col", [(d, d ^ mask) for d in range(n_col)])
 
-    def step_up(value):
-        return lax.ppermute(value, "row", [(r, r + 1) for r in range(n - 1)])
-
-    def step_down(value):
-        return lax.ppermute(value, "row", [(r + 1, r) for r in range(n - 1)])
+    def hop(value, first):
+        pairs = {r: r + 1 for r in range(first, n - 1, 2)}
+        pairs.update({above: r for r, above in pairs.items()})
+        perm = [
+            (r * n_col + d, pairs[r] * n_col + d if r in pairs else r * n_col + (d ^ 1)) for r in range(n) for d in range(n_col)
+        ]
+        return lax.ppermute(value, ("row", "col"), perm)
 
     raw = jnp.transpose(grad_x, (1, 2, 0))
-    packed = pack(raw, exchange(lax.dynamic_slice_in_dim(raw, (1 - this_core()) * half, half, 1), 1))
+    other = exchange(lax.dynamic_slice_in_dim(raw, (1 - this_core()) * half, half, 1), 1)
+    right_mine, right_theirs = front(pair, gain, bias, proj_weight, tile_mask, 1)
+    packed = pack(raw, after(other, right_mine))
 
     slots = [[packed] * CHUNKS]
     for m in range(1, n_col // CORES):
@@ -332,37 +364,34 @@
             slots[m].append(exchange(value, CORES * bit))
     panels = [[slot[c] for slot in slots] for c in range(CHUNKS)]
 
-    right_mine, right_theirs = front(after(pair, packed), gain, bias, proj_weight, tile_mask, 1)
     own = jnp.concatenate((right_mine, exchange(right_theirs, 1)), axis=1)
-    first_up, first_down = step_up(own), step_down(own)
+    first_a, first_b = hop(own, 0), hop(own, 1)
     left_mine, left_theirs = front(after(pair, own), gain, bias, proj_weight, tile_mask, 0)
     left_other = exchange(left_theirs, 1)
 
-    ups, downs, partials = [], [], []
+    by_a, by_b, partials = [], [], []
     for c in range(CHUNKS):
-        *sums, up, down = partial_products(left_mine, left_other, first_up, first_down, panels[c], c)
+        *sums, next_a, next_b = partial_products(left_mine, left_other, first_a, first_b, panels[c], c)
         partials.append(sums)
-        ups.append([first_up, step_up(up)])
-        downs.append([first_down, step_down(down)])
-
-    def plus(arrived, sums, use):
-        return (arrived.astype(jnp.float32) + jnp.where(use, sums.astype(jnp.float32), 0.0)).astype(jnp.bfloat16)
+        by_a.append([first_a, hop(next_a, 0)])
+        by_b.append([first_b, hop(next_b, 1)])
 
     left_grads = []
     for t in range(2, n):
         for c in range(CHUNKS):
-            up, down = ups[c][-1], downs[c][-1]
+            value = by_a[c][-1]
             if t == n - 1 and c > 0:
-                up = after(up, left_grads[c - 1])
-            ups[c].append(step_up(plus(up, partials[c][n - t], row < t)))
-            downs[c].append(step_down(plus(down, partials[c][t], row >= n - t)))
+                value = after(value, left_grads[c - 1])
+            next_a, next_b = onward(value, by_b[c][-1], partials[c][n - t], partials[c][t], t, n)
+            by_a[c].append(hop(next_a, 0))
+            by_b[c].append(hop(next_b, 1))
             if t == n - 1:
-                left_grads.append(left_products(own, ups[c][: n - 1], downs[c][: n - 1], panels[c], c))
+                left_grads.append(left_products(own, by_a[c][: n - 1], by_b[c][: n - 1], panels[c], c))
     left_grad_other = [exchange(theirs, 1) for _, theirs in left_grads]
     ks = left_mine.shape[1]
     right_grad_other = []
     for c in range(CHUNKS):
-        total = sum(v[:, ks:].astype(jnp.float32) for v in (partials[c][0], ups[c][-1], downs[c][-1]))
+        total = arrived_total(partials[c][0][:, ks:], by_a[c][-1][:, ks:], by_b[c][-1][:, ks:], n)
         right_grad_other.append(exchange(total.astype(jnp.bfloat16), 1))
 
     return tail(
@@ -374,8 +403,8 @@
         [mine for mine, _ in left_grads],
         left_grad_other,
         [sums[0] for sums in partials],
-        [u[-1] for u in ups],
-        [d[-1] for d in downs],
+        [v[-1] for v in by_a],
+        [v[-1] for v in by_b],
         right_grad_other,
     )
 

time: 146 us -> 133 us (0.911)
  starting transfers between devices: 52 us -> 34.2 us
  waiting for transfers between devices: 44 us -> 52.7 us
  local copies, waits for them, and re-layouts: 7.93 us -> 3.16 us
  other arithmetic: 6.66 us -> 9.59 us
    ppermute x14, starting transfers between devices: 42.7 us -> 24.8 us  [hop(): return lax.ppermute(value, ('row', 'col'), perm)]
    ppermute x14, waiting for transfers between devices: 22.4 us -> 28.6 us  [hop(): return lax.ppermute(value, ('row', 'col'), perm)]
    unnamed x53 -> x45, local copies, waits for them, and re-layouts: 5.88 us -> 1.84 us
    convert_element_type x6 -> x4, other arithmetic: 6.43 us -> 9.3 us  [onward(): return (out_a.astype(jnp.bfloat16), out_b.astype(jnp.bfloat16))]
    ppermute x11, waiting for transfers between devices: 21.7 us -> 24.1 us  [exchange(): return lax.ppermute(value, 'col', [(d, d ^ mask) for d in range(n_col)])]
  transfers between devices with their start and end apart: 25 -> 25, of which waited for: 10 -> 10; matrix products, arithmetic and copies ran while one was open for 5% -> 7% of each run, Pallas kernels for 12% -> 16%
where the time goes in v6:
time: 133 us
  waiting for transfers between devices  52.7 us (40%)
  starting transfers between devices  34.2 us (26%)
  Pallas kernels  32.8 us (25%)
  other arithmetic  9.59 us (7%)
  local copies, waits for them, and re-layouts  3.16 us (2%)
    ppermute x14, waiting for transfers between devices, hop(): return lax.ppermute(value, ('row', 'col'), perm)  28.6 us
    ppermute x14, starting transfers between devices, hop(): return lax.ppermute(value, ('row', 'col'), perm)  24.8 us
    ppermute x11, waiting for transfers between devices, exchange(): return lax.ppermute(value, 'col', [(d, d ^ mask) for d in range(n_col)])  24.1 us
    pallas_call x1, Pallas kernels, tail(): pl.pallas_call(functools.partial(tail_kernel, lax.axis_size('row')), out_...  11.3 us
    pallas_call x2, Pallas kernels, front(): pl.pallas_call(front_kernel, out_shape=[jax.ShapeDtypeStruct((half, cols,...  10.3 us
    ppermute x11, starting transfers between devices, exchange(): return lax.ppermute(value, 'col', [(d, d ^ mask) for d in range(n_col)])  9.34 us
    convert_element_type x4, other arithmetic, onward(): return (out_a.astype(jnp.bfloat16), out_b.astype(jnp.bfloat16))  9.3 us
    pallas_call x2, Pallas kernels, partial_products(): pl.pallas_call(functools.partial(partial_kernel, n), out_shape=[pltpu.HBM...  6.19 us
  transfers between devices with their start and end apart: 25, of which 10 were waited for; matrix products, arithmetic and copies ran while one was open for 7% of the time, Pallas kernels for 16%

profile of v6, /device:TPU:0, one launch (start us, length us, event | category | flops | bytes accessed | tf_op | source)
XLA Modules:
  0.0 132.8 jit_solution(17342641254722405834)
XLA Ops:
  0.0 1.2 dynamic-slice_bitcast_fusion
  1.2 0.5 collective-permute-start.4
  1.7 0.7 copy-done.15
  2.4 5.1 %right_front.1 = (bf16[32,64,128]{2,1,0:T(8,128)(2,1)S(1)}, bf16[32,64,128]{2,1,0:T(8,128)(2,1)S(1)}) custom-call(s32[4,4]{1,0:T(4,128)S(1)} %copy-done.15, bf16[128,64,128]{2,1,0:T(8,128)(2,1)} %pair.4, f32[1,128]{1,0:T(1,128)} %bitcast.6, f32[1,128]{1,0:T(1,128)} %bitcast.9, bf16[128,256]{1,0:T(8,128)(2,1)} %weight.5), custom_call_target="tpu_custom_call" | custom-call | flops 1 | bytes 18000000 | tf_op jit(solution)/shard_map/right_front/pallas_call | solution.py:85
  7.5 0.1 collective-permute-start
  7.7 0.4 pack.1.refs_0_.refs_6_
  8.1 3.0 %collective-permute-start.5 = (bf16[32,128,128]{2,1,0:T(8,128)(2,1)S(1)}, bf16[32,128,128]{2,1,0:T(8,128)(2,1)S(1)}, u32[]{:S(2)}, u32[]{:S(2)}) collective-permute-start(bf16[32,128,128]{2,1,0:T(8,128)(2,1)S(1)} %pack.1.refs_0_.refs_6_), channel_id=1, source_target_pairs={{0,2},{1,3},{2,0},{3,1},{4,6},{5,7},{6,4},{7,5},{8,10},{9,11},{10,... | collective-permute-start | bytes 3145736 | tf_op jit(solution)/shard_map/ppermute | solution.py:338
  11.1 1.5 %collective-permute-start.6 = (bf16[32,128,128]{2,1,0:T(8,128)(2,1)S(1)}, bf16[32,128,128]{2,1,0:T(8,128)(2,1)S(1)}, u32[]{:S(2)}, u32[]{:S(2)}) collective-permute-start(bf16[32,128,128]{2,1,0:T(8,128)(2,1)S(1)} %pack.1.refs_0_.refs_6_), channel_id=1, source_target_pairs={{0,4},{1,5},{2,6},{3,7},{4,0},{5,1},{6,2},{7,3},{8,12},{9,13},{10,... | collective-permute-start | bytes 3145736 | tf_op jit(solution)/shard_map/ppermute | solution.py:338
  12.6 0.1 constant_dynamic-update-slice_fusion.own
  12.7 0.1 collective-permute-start.3
  12.8 3.1 %collective-permute-start.1 = (bf16[32,128,128]{2,1,0:T(8,128)(2,1)S(1)}, bf16[32,128,128]{2,1,0:T(8,128)(2,1)S(1)}, u32[]{:S(2)}, u32[]{:S(2)}) collective-permute-start(bf16[32,128,128]{2,1,0:T(8,128)(2,1)S(1)} %constant_dynamic-update-slice_fusion.own), channel_id=1, source_target_pairs={{0,8},{1,9},{2,10},{3,11},{4,12},{5,13},{6,14},{7,15},{8,0},{9,1},... | collective-permute-start | bytes 3145736 | tf_op jit(solution)/shard_map/ppermute | solution.py:346
  15.9 5.1 %left_front.1 = (bf16[32,64,128]{2,1,0:T(8,128)(2,1)S(1)}, bf16[32,64,128]{2,1,0:T(8,128)(2,1)S(1)}) custom-call(s32[4,4]{1,0:T(4,128)S(1)} %copy-done.15, bf16[128,64,128]{2,1,0:T(8,128)(2,1)} %pair.4, f32[1,128]{1,0:T(1,128)} %bitcast.7, f32[1,128]{1,0:T(1,128)} %bitcast.10, bf16[128,256]{1,0:T(8,128)(2,1)} %weight.5), custom_call_target="tpu_custom_call" | custom-call | flops 1 | bytes 18000000 | tf_op jit(solution)/shard_map/left_front/pallas_call | solution.py:85
  21.1 0.1 collective-permute-start.2
  21.2 13.2 %collective-permute-done.5.refs_1_.refs_7_ = bf16[32,128,128]{2,1,0:T(8,128)(2,1)S(1)} collective-permute-done((bf16[32,128,128]{2,1,0:T(8,128)(2,1)S(1)}, bf16[32,128,128]{2,1,0:T(8,128)(2,1)S(1)}, u32[]{:S(2)}, u32[]{:S(2)}) %collective-permute-start.5) | collective-permute-done | bytes 1048608 | tf_op jit(solution)/shard_map/ppermute | solution.py:338
  34.5 1.8 %collective-permute-start.7 = (bf16[16,128,128]{2,1,0:T(8,128)(2,1)S(1)}, bf16[16,128,128]{2,1,0:T(8,128)(2,1)S(1)}, u32[]{:S(2)}, u32[]{:S(2)}) collective-permute-start(bf16[16,128,128]{2,1,0:T(8,128)(2,1)S(1)} %slice.32), channel_id=1, source_target_pairs={{0,4},{1,5},{2,6},{3,7},{4,0},{5,1},{6,2},{7,3},{8,12},{9,13},{10,... | collective-permute-start | bytes 1572872 | tf_op jit(solution)/shard_map/ppermute | solution.py:338
  36.4 1.6 %collective-permute-start.12 = (bf16[16,128,128]{2,1,0:T(8,128)(2,1)S(1)}, bf16[16,128,128]{2,1,0:T(8,128)(2,1)S(1)}, u32[]{:S(2)}, u32[]{:S(2)}) collective-permute-start(bf16[16,128,128]{2,1,0:T(8,128)(2,1)S(1)} %slice.33), channel_id=1, source_target_pairs={{0,2},{1,3},{2,0},{3,1},{4,6},{5,7},{6,4},{7,5},{8,10},{9,11},{10,... | collective-permute-start | bytes 1572872 | tf_op jit(solution)/shard_map/ppermute | solution.py:338
  37.9 0.5 collective-permute-done.1.by_a.refs_0_
  38.5 9.4 %collective-permute-done.7.refs_3_.refs_9_ = bf16[16,128,128]{2,1,0:T(8,128)(2,1)S(1)} collective-permute-done((bf16[16,128,128]{2,1,0:T(8,128)(2,1)S(1)}, bf16[16,128,128]{2,1,0:T(8,128)(2,1)S(1)}, u32[]{:S(2)}, u32[]{:S(2)}) %collective-permute-start.7) | collective-permute-done | bytes 524320 | tf_op jit(solution)/shard_map/ppermute | solution.py:338
  47.9 3.1 %right_partials.2 = (bf16[16,128,128]{2,1,0:T(8,128)(2,1)}, bf16[16,128,128]{2,1,0:T(8,128)(2,1)}, bf16[16,128,128]{2,1,0:T(8,128)(2,1)}, bf16[16,128,128]{2,1,0...) custom-call(bf16[32,64,128]{2,1,0:T(8,128)(2,1)S(1)} %get-tuple-element.31.left_mine, ...), custom_call_target="tpu_custom_call" | custom-call | flops 1 | bytes 8000000 | tf_op jit(solution)/shard_map/right_partials/pallas_call | solution.py:174
  50.9 1.5 %collective-permute-start.8 = (bf16[16,128,128]{2,1,0:T(8,128)(2,1)}, bf16[16,128,128]{2,1,0:T(8,128)(2,1)}, u32[]{:S(2)}, u32[]{:S(2)}) collective-permute-start(bf16[16,128,128]{2,1,0:T(8,128)(2,1)} %get-tuple-element.34), channel_id=1, source_target_pairs={{0,8},{1,9},{2,10},{3,11},{4,12},{5,13},{6,14},{7,15},{8,0},{9,1},... | collective-permute-start | bytes 1572872 | tf_op jit(solution)/shard_map/ppermute | solution.py:346
  52.5 3.1 %right_partials.3 = (bf16[16,128,128]{2,1,0:T(8,128)(2,1)}, bf16[16,128,128]{2,1,0:T(8,128)(2,1)}, bf16[16,128,128]{2,1,0:T(8,128)(2,1)}, bf16[16,128,128]{2,1,0...) custom-call(bf16[32,64,128]{2,1,0:T(8,128)(2,1)S(1)} %get-tuple-element.31.left_mine, ...), custom_call_target="tpu_custom_call" | custom-call | flops 1 | bytes 8000000 | tf_op jit(solution)/shard_map/right_partials/pallas_call | solution.py:174
  55.6 3.2 %collective-permute-start.13 = (bf16[16,128,128]{2,1,0:T(8,128)(2,1)}, bf16[16,128,128]{2,1,0:T(8,128)(2,1)}, u32[]{:S(2)}, u32[]{:S(2)}) collective-permute-start(bf16[16,128,128]{2,1,0:T(8,128)(2,1)} %get-tuple-element.38), channel_id=1, source_target_pairs={{0,8},{1,9},{2,10},{3,11},{4,12},{5,13},{6,14},{7,15},{8,0},{9,1},... | collective-permute-start | bytes 1572872 | tf_op jit(solution)/shard_map/ppermute | solution.py:346
  58.8 7.3 %collective-permute-done.8.refs_1_ = bf16[16,128,128]{2,1,0:T(8,128)(2,1)} collective-permute-done((bf16[16,128,128]{2,1,0:T(8,128)(2,1)}, bf16[16,128,128]{2,1,0:T(8,128)(2,1)}, u32[]{:S(2)}, u32[]{:S(2)}) %collective-permute-start.8) | collective-permute-done | bytes 524320 | tf_op jit(solution)/shard_map/ppermute | solution.py:346
  66.1 2.9 %fusion.11 = (bf16[16,128,128]{2,1,0:T(8,128)(2,1)}, bf16[16,128,128]{2,1,0:T(8,128)(2,1)}) fusion(bf16[16,128,128]{2,1,0:T(8,128)(2,1)} %get-tuple-element.36, bf16[16,128,128]{2,1,0:T(8,128)(2,1)} %collective-permute-done.8.refs_1_, pred[]{:T(512)S(6)} %select_n.167, pred[]{:T(512)S(6)} %ge.8, pred[]{:T(512)S(6)} %lt.10, pred[]{:T(512)S(6)} %eq.2, ...), kind=kLoop, calls=%fused_computation.15 | loop fusion | flops 3407872 | bytes 2621445 | tf_op jit(solution)/shard_map/convert_element_type | solution.py:149
  69.0 4.7 %collective-permute-start.10 = (bf16[16,128,128]{2,1,0:T(8,128)(2,1)}, bf16[16,128,128]{2,1,0:T(8,128)(2,1)}, u32[]{:S(2)}, u32[]{:S(2)}) collective-permute-start(bf16[16,128,128]{2,1,0:T(8,128)(2,1)} %get-tuple-element.58), channel_id=1, source_target_pairs={{0,8},{1,9},{2,10},{3,11},{4,12},{5,13},{6,14},{7,15},{8,0},{9,1},... | collective-permute-start | bytes 1572872 | tf_op jit(solution)/shard_map/ppermute | solution.py:346
  73.7 3.6 %collective-permute-done.13.refs_1_ = bf16[16,128,128]{2,1,0:T(8,128)(2,1)} collective-permute-done((bf16[16,128,128]{2,1,0:T(8,128)(2,1)}, bf16[16,128,128]{2,1,0:T(8,128)(2,1)}, u32[]{:S(2)}, u32[]{:S(2)}) %collective-permute-start.13) | collective-permute-done | bytes 524320 | tf_op jit(solution)/shard_map/ppermute | solution.py:346
  77.3 2.6 %fusion.7 = (bf16[16,128,128]{2,1,0:T(8,128)(2,1)}, bf16[16,128,128]{2,1,0:T(8,128)(2,1)}) fusion(bf16[16,128,128]{2,1,0:T(8,128)(2,1)S(1)} %copy-done.19, bf16[16,128,128]{2,1,0:T(8,128)(2,1)} %collective-permute-done.13.refs_1_, pred[]{:T(512)S(6)} %select_n.167, pred[]{:T(512)S(6)} %ge.8, pred[]{:T(512)S(6)} %lt.10, pred[]{:T(512)S(6)} %eq.2, ...), kind=kLoop, calls=%fused_computation.11 | loop fusion | flops 3407872 | bytes 2621445 | tf_op jit(solution)/shard_map/convert_element_type | solution.py:149
  80.0 2.7 %collective-permute-start.15 = (bf16[16,128,128]{2,1,0:T(8,128)(2,1)}, bf16[16,128,128]{2,1,0:T(8,128)(2,1)}, u32[]{:S(2)}, u32[]{:S(2)}) collective-permute-start(bf16[16,128,128]{2,1,0:T(8,128)(2,1)} %get-tuple-element.56), channel_id=1, source_target_pairs={{0,8},{1,9},{2,10},{3,11},{4,12},{5,13},{6,14},{7,15},{8,0},{9,1},... | collective-permute-start | bytes 1572872 | tf_op jit(solution)/shard_map/ppermute | solution.py:346
  82.7 5.9 %collective-permute-done.10.refs_2_ = bf16[16,128,128]{2,1,0:T(8,128)(2,1)} collective-permute-done((bf16[16,128,128]{2,1,0:T(8,128)(2,1)}, bf16[16,128,128]{2,1,0:T(8,128)(2,1)}, u32[]{:S(2)}, u32[]{:S(2)}) %collective-permute-start.10) | collective-permute-done | bytes 524320 | tf_op jit(solution)/shard_map/ppermute | solution.py:346
  88.6 2.0 %add_convert_fusion.1 = (bf16[16,128,128]{2,1,0:T(8,128)(2,1)S(1)}, bf16[16,128,128]{2,1,0:T(8,128)(2,1)S(1)}) fusion(bf16[16,128,128]{2,1,0:T(8,128)(2,1)} %collective-permute-done.10.refs_2_, bf16[16,128,128]{2,1,0:T(8,128)(2,1)} %get-tuple-element.47, bf16[16,128,128]{2,1,0:T(8,128)(2,1)} %get-tuple-element.46, pred[]{:T(512)S(6)} %ge.9, pred[]{:T(512)S(6)} %lt.11, ...), kind=kLoop, calls=%fused_computation.17 | loop fusion | flops 3670016 | bytes 3145733 | tf_op jit(solution)/shard_map/convert_element_type | solution.py:149
  90.6 0.1 collective-permute-start.21
  90.7 4.7 %collective-permute-start.19 = (bf16[16,128,128]{2,1,0:T(8,128)(2,1)S(1)}, bf16[16,128,128]{2,1,0:T(8,128)(2,1)S(1)}, u32[]{:S(2)}, u32[]{:S(2)}) collective-permute-start(bf16[16,128,128]{2,1,0:T(8,128)(2,1)S(1)} %get-tuple-element.54), channel_id=1, source_target_pairs={{0,8},{1,9},{2,10},{3,11},{4,12},{5,13},{6,14},{7,15},{8,0},{9,1},... | collective-permute-start | bytes 1572872 | tf_op jit(solution)/shard_map/ppermute | solution.py:346
  95.4 1.0 copy-done.11
  96.5 2.4 %left_products.2 = (f32[16,64,128]{2,1,0:T(8,128)S(1)}, bf16[16,64,128]{2,1,0:T(8,128)(2,1)S(1)}) custom-call(bf16[32,128,128]{2,1,0:T(8,128)(2,1)S(1)} %copy-done.6, bf16[32,128,128]{2,1,0:T(8,128)(2,1)S(1)} %copy-done.4, bf16[16,128,128]{2,1,0:T(8,128)(2,1)} %collective-permute-done.8.refs_1_, bf16[16,128,128]{2,1,0:T(8,128)(2,1)} %collective-permute-done.10.refs_2_, ...), custom_call_target="tpu_custom_call" | custom-call | flops 1 | bytes 8000000 | tf_op jit(solution)/shard_map/left_products/pallas_call | solution.py:215
  98.8 1.0 collective-permute-done.15.refs_2_
  99.8 1.7 %add_convert_fusion = (bf16[16,128,128]{2,1,0:T(8,128)(2,1)S(1)}, bf16[16,128,128]{2,1,0:T(8,128)(2,1)S(1)}) fusion(bf16[16,128,128]{2,1,0:T(8,128)(2,1)} %collective-permute-done.15.refs_2_, bf16[16,128,128]{2,1,0:T(8,128)(2,1)S(1)} %copy-done.21, bf16[16,128,128]{2,1,0:T(8,128)(2,1)S(1)} %copy-done.20, pred[]{:T(512)S(6)} %ge.9, pred[]{:T(512)S(6)} %lt.11, ...), kind=kLoop, calls=%fused_computation.16 | loop fusion | flops 3670016 | bytes 3145733 | tf_op jit(solution)/shard_map/convert_element_type | solution.py:149
  101.6 0.1 collective-permute-start.22
  101.7 4.7 %collective-permute-start.20 = (bf16[16,128,128]{2,1,0:T(8,128)(2,1)S(1)}, bf16[16,128,128]{2,1,0:T(8,128)(2,1)S(1)}, u32[]{:S(2)}, u32[]{:S(2)}) collective-permute-start(bf16[16,128,128]{2,1,0:T(8,128)(2,1)S(1)} %get-tuple-element.52), channel_id=1, source_target_pairs={{0,8},{1,9},{2,10},{3,11},{4,12},{5,13},{6,14},{7,15},{8,0},{9,1},... | collective-permute-start | bytes 1572872 | tf_op jit(solution)/shard_map/ppermute | solution.py:346
  106.3 2.3 %left_products.3 = (f32[16,64,128]{2,1,0:T(8,128)S(1)}, bf16[16,64,128]{2,1,0:T(8,128)(2,1)S(1)}) custom-call(bf16[32,128,128]{2,1,0:T(8,128)(2,1)S(1)} %copy-done.6, bf16[32,128,128]{2,1,0:T(8,128)(2,1)S(1)} %copy-done.4, bf16[16,128,128]{2,1,0:T(8,128)(2,1)} %collective-permute-done.13.refs_1_, bf16[16,128,128]{2,1,0:T(8,128)(2,1)} %collective-permute-done.15.refs_2_, ...), custom_call_target="tpu_custom_call" | custom-call | flops 1 | bytes 8000000 | tf_op jit(solution)/shard_map/left_products/pallas_call | solution.py:215
  108.7 0.6 collective-permute-start.18
  109.3 1.7 %collective-permute-done.19.refs_6_ = bf16[16,128,128]{2,1,0:T(8,128)(2,1)S(1)} collective-permute-done((bf16[16,128,128]{2,1,0:T(8,128)(2,1)S(1)}, bf16[16,128,128]{2,1,0:T(8,128)(2,1)S(1)}, u32[]{:S(2)}, u32[]{:S(2)}) %collective-permute-start.19) | collective-permute-done | bytes 524320 | tf_op jit(solution)/shard_map/ppermute | solution.py:346
  110.9 0.1 add_convert_fusion.5
  111.1 0.1 collective-permute-start.23
  111.2 8.5 %collective-permute-done.20.refs_7_ = bf16[16,128,128]{2,1,0:T(8,128)(2,1)S(1)} collective-permute-done((bf16[16,128,128]{2,1,0:T(8,128)(2,1)S(1)}, bf16[16,128,128]{2,1,0:T(8,128)(2,1)S(1)}, u32[]{:S(2)}, u32[]{:S(2)}) %collective-permute-start.20) | collective-permute-done | bytes 524320 | tf_op jit(solution)/shard_map/ppermute | solution.py:346
  119.7 0.1 add_convert_fusion.4
  119.9 0.1 collective-permute-start.24
  120.0 1.5 %collective-permute-done.24.refs_11_ = bf16[16,64,128]{2,1,0:T(8,128)(2,1)S(1)} collective-permute-done((bf16[16,64,128]{2,1,0:T(8,128)(2,1)S(1)}, bf16[16,64,128]{2,1,0:T(8,128)(2,1)S(1)}, u32[]{:S(2)}, u32[]{:S(2)}) %collective-permute-start.24) | collective-permute-done | bytes 262176 | tf_op jit(solution)/shard_map/ppermute | solution.py:338
  121.5 11.3 %tail.1 = bf16[128,64,128]{2,1,0:T(8,128)(2,1)} custom-call(s32[4,4]{1,0:T(4,128)S(1)} %copy-done.16, bf16[128,64,128]{2,1,0:T(8,128)(2,1)S(1)} %copy-done, f32[1,128]{1,0:T(1,128)S(1)} %bitcast.8, f32[1,128]{1,0:T(1,128)S(1)} %bitcast.11, bf16[128,256]{1,0:T(8,128)(2,1)S(1)} %copy-done.14, f32[16,64,128]{2,1,0:T(8,128)S(1)} %get-tuple-element.37.refs_0_, ...), custom_call_target="tpu_custom_call" | custom-call | flops 1 | bytes 8000000 | tf_op jit(solution)/shard_map/tail/pallas_call | solution.py:296
  (65 shorter events, 0.3 us)
Async XLA Ops:
  0.0 7.7 %copy-start.7 = (bf16[128,64,64]{0,2,1:T(8,128)(2,1)S(1)}, bf16[128,64,64]{0,2,1:T(8,128)(2,1)}, u32[]{:S(2)}) copy-start(bf16[128,64,64]{0,2,1:T(8,128)(2,1)} %param.7) | copy-start | bytes 3145732
  1.2 6.5 %collective-permute-start.4 = (bf16[64,32,128]{2,1,0:T(8,128)(2,1)S(1)}, bf16[64,32,128]{2,1,0:T(8,128)(2,1)S(1)}, u32[]{:S(2)}, u32[]{:S(2)}) collective-permute-start(bf16[64,32,128]{2,1,0:T(8,128)(2,1)S(1)} %dynamic-slice_bitcast_fusion), channel_id=1, source_target_pairs={{0,1},{1,0},{2,3},{3,2},{4,5},{5,4},{6,7},{7,6},{8,9},{9,8},{10,11... | collective-permute-start | bytes 1572872 | tf_op jit(solution)/shard_map/ppermute | solution.py:338
  1.7 0.7 copy-start.15
  7.5 5.1 %collective-permute-start = (bf16[32,64,128]{2,1,0:T(8,128)(2,1)S(1)}, bf16[32,64,128]{2,1,0:T(8,128)(2,1)S(1)}, u32[]{:S(2)}, u32[]{:S(2)}) collective-permute-start(bf16[32,64,128]{2,1,0:T(8,128)(2,1)S(1)} %get-tuple-element.29), channel_id=1, source_target_pairs={{0,1},{1,0},{2,3},{3,2},{4,5},{5,4},{6,7},{7,6},{8,9},{9,8},{10,11... | collective-permute-start | bytes 1572872 | tf_op jit(solution)/shard_map/ppermute | solution.py:338
  8.1 26.4 %collective-permute-start.5 = (bf16[32,128,128]{2,1,0:T(8,128)(2,1)S(1)}, bf16[32,128,128]{2,1,0:T(8,128)(2,1)S(1)}, u32[]{:S(2)}, u32[]{:S(2)}) collective-permute-start(bf16[32,128,128]{2,1,0:T(8,128)(2,1)S(1)} %pack.1.refs_0_.refs_6_), channel_id=1, source_target_pairs={{0,2},{1,3},{2,0},{3,1},{4,6},{5,7},{6,4},{7,5},{8,10},{9,11},{10,... | collective-permute-start | bytes 3145736 | tf_op jit(solution)/shard_map/ppermute | solution.py:338
  11.1 25.2 %collective-permute-start.6 = (bf16[32,128,128]{2,1,0:T(8,128)(2,1)S(1)}, bf16[32,128,128]{2,1,0:T(8,128)(2,1)S(1)}, u32[]{:S(2)}, u32[]{:S(2)}) collective-permute-start(bf16[32,128,128]{2,1,0:T(8,128)(2,1)S(1)} %pack.1.refs_0_.refs_6_), channel_id=1, source_target_pairs={{0,4},{1,5},{2,6},{3,7},{4,0},{5,1},{6,2},{7,3},{8,12},{9,13},{10,... | collective-permute-start | bytes 3145736 | tf_op jit(solution)/shard_map/ppermute | solution.py:338
  12.7 23.6 %copy-start.5 = (bf16[32,128,128]{2,1,0:T(8,128)(2,1)}, bf16[32,128,128]{2,1,0:T(8,128)(2,1)S(1)}, u32[]{:S(2)}) copy-start(bf16[32,128,128]{2,1,0:T(8,128)(2,1)S(1)} %constant_dynamic-update-slice_fusion.own) | copy-start | bytes 3145732
  12.7 25.2 %collective-permute-start.3 = (bf16[32,128,128]{2,1,0:T(8,128)(2,1)S(1)}, bf16[32,128,128]{2,1,0:T(8,128)(2,1)S(1)}, u32[]{:S(2)}, u32[]{:S(2)}) collective-permute-start(bf16[32,128,128]{2,1,0:T(8,128)(2,1)S(1)} %constant_dynamic-update-slice_fusion.own), channel_id=1, source_target_pairs={{0,1},{1,0},{2,3},{3,2},{4,5},{5,4},{6,7},{7,6},{8,16},{9,17},{10,... | collective-permute-start | bytes 3145736 | tf_op jit(solution)/shard_map/ppermute | solution.py:346
  12.8 25.7 %collective-permute-start.1 = (bf16[32,128,128]{2,1,0:T(8,128)(2,1)S(1)}, bf16[32,128,128]{2,1,0:T(8,128)(2,1)S(1)}, u32[]{:S(2)}, u32[]{:S(2)}) collective-permute-start(bf16[32,128,128]{2,1,0:T(8,128)(2,1)S(1)} %constant_dynamic-update-slice_fusion.own), channel_id=1, source_target_pairs={{0,8},{1,9},{2,10},{3,11},{4,12},{5,13},{6,14},{7,15},{8,0},{9,1},... | collective-permute-start | bytes 3145736 | tf_op jit(solution)/shard_map/ppermute | solution.py:346
  21.1 16.8 %collective-permute-start.2 = (bf16[32,64,128]{2,1,0:T(8,128)(2,1)S(1)}, bf16[32,64,128]{2,1,0:T(8,128)(2,1)S(1)}, u32[]{:S(2)}, u32[]{:S(2)}) collective-permute-start(bf16[32,64,128]{2,1,0:T(8,128)(2,1)S(1)} %get-tuple-element.32), channel_id=1, source_target_pairs={{0,1},{1,0},{2,3},{3,2},{4,5},{5,4},{6,7},{7,6},{8,9},{9,8},{10,11... | collective-permute-start | bytes 1572872 | tf_op jit(solution)/shard_map/ppermute | solution.py:338
  34.5 13.4 %collective-permute-start.7 = (bf16[16,128,128]{2,1,0:T(8,128)(2,1)S(1)}, bf16[16,128,128]{2,1,0:T(8,128)(2,1)S(1)}, u32[]{:S(2)}, u32[]{:S(2)}) collective-permute-start(bf16[16,128,128]{2,1,0:T(8,128)(2,1)S(1)} %slice.32), channel_id=1, source_target_pairs={{0,4},{1,5},{2,6},{3,7},{4,0},{5,1},{6,2},{7,3},{8,12},{9,13},{10,... | collective-permute-start | bytes 1572872 | tf_op jit(solution)/shard_map/ppermute | solution.py:338
  36.4 16.1 %collective-permute-start.12 = (bf16[16,128,128]{2,1,0:T(8,128)(2,1)S(1)}, bf16[16,128,128]{2,1,0:T(8,128)(2,1)S(1)}, u32[]{:S(2)}, u32[]{:S(2)}) collective-permute-start(bf16[16,128,128]{2,1,0:T(8,128)(2,1)S(1)} %slice.33), channel_id=1, source_target_pairs={{0,2},{1,3},{2,0},{3,1},{4,6},{5,7},{6,4},{7,5},{8,10},{9,11},{10,... | collective-permute-start | bytes 1572872 | tf_op jit(solution)/shard_map/ppermute | solution.py:338
  37.9 14.5 %copy-start.1 = (bf16[32,128,128]{2,1,0:T(8,128)(2,1)}, bf16[32,128,128]{2,1,0:T(8,128)(2,1)S(1)}, u32[]{:S(2)}) copy-start(bf16[32,128,128]{2,1,0:T(8,128)(2,1)S(1)} %collective-permute-done.3.by_b.refs_3_) | copy-start | bytes 3145732
  38.5 14.0 %copy-start.3 = (bf16[32,128,128]{2,1,0:T(8,128)(2,1)}, bf16[32,128,128]{2,1,0:T(8,128)(2,1)S(1)}, u32[]{:S(2)}) copy-start(bf16[32,128,128]{2,1,0:T(8,128)(2,1)S(1)} %collective-permute-done.1.by_a.refs_0_) | copy-start | bytes 3145732
  47.8 3.1 %copy-start.10 = (bf16[16,128,128]{2,1,0:T(8,128)(2,1)}, bf16[16,128,128]{2,1,0:T(8,128)(2,1)S(1)}, u32[]{:S(2)}) copy-start(bf16[16,128,128]{2,1,0:T(8,128)(2,1)S(1)} %collective-permute-done.7.refs_3_.refs_9_) | copy-start | bytes 1572868
  50.9 15.2 %collective-permute-start.8 = (bf16[16,128,128]{2,1,0:T(8,128)(2,1)}, bf16[16,128,128]{2,1,0:T(8,128)(2,1)}, u32[]{:S(2)}, u32[]{:S(2)}) collective-permute-start(bf16[16,128,128]{2,1,0:T(8,128)(2,1)} %get-tuple-element.34), channel_id=1, source_target_pairs={{0,8},{1,9},{2,10},{3,11},{4,12},{5,13},{6,14},{7,15},{8,0},{9,1},... | collective-permute-start | bytes 1572872 | tf_op jit(solution)/shard_map/ppermute | solution.py:346
  52.4 13.7 %collective-permute-start.9 = (bf16[16,128,128]{2,1,0:T(8,128)(2,1)}, bf16[16,128,128]{2,1,0:T(8,128)(2,1)}, u32[]{:S(2)}, u32[]{:S(2)}) collective-permute-start(bf16[16,128,128]{2,1,0:T(8,128)(2,1)} %get-tuple-element.35), channel_id=1, source_target_pairs={{0,1},{1,0},{2,3},{3,2},{4,5},{5,4},{6,7},{7,6},{8,16},{9,17},{10,... | collective-permute-start | bytes 1572872 | tf_op jit(solution)/shard_map/ppermute | solution.py:346
  52.5 3.1 %copy-start.8 = (bf16[16,128,128]{2,1,0:T(8,128)(2,1)}, bf16[16,128,128]{2,1,0:T(8,128)(2,1)S(1)}, u32[]{:S(2)}) copy-start(bf16[16,128,128]{2,1,0:T(8,128)(2,1)S(1)} %collective-permute-done.12.refs_3_.refs_9_) | copy-start | bytes 1572868
  55.6 21.8 %collective-permute-start.13 = (bf16[16,128,128]{2,1,0:T(8,128)(2,1)}, bf16[16,128,128]{2,1,0:T(8,128)(2,1)}, u32[]{:S(2)}, u32[]{:S(2)}) collective-permute-start(bf16[16,128,128]{2,1,0:T(8,128)(2,1)} %get-tuple-element.38), channel_id=1, source_target_pairs={{0,8},{1,9},{2,10},{3,11},{4,12},{5,13},{6,14},{7,15},{8,0},{9,1},... | collective-permute-start | bytes 1572872 | tf_op jit(solution)/shard_map/ppermute | solution.py:346
  58.8 18.6 %collective-permute-start.14 = (bf16[16,128,128]{2,1,0:T(8,128)(2,1)}, bf16[16,128,128]{2,1,0:T(8,128)(2,1)}, u32[]{:S(2)}, u32[]{:S(2)}) collective-permute-start(bf16[16,128,128]{2,1,0:T(8,128)(2,1)} %get-tuple-element.39), channel_id=1, source_target_pairs={{0,1},{1,0},{2,3},{3,2},{4,5},{5,4},{6,7},{7,6},{8,16},{9,17},{10,... | collective-permute-start | bytes 1572872 | tf_op jit(solution)/shard_map/ppermute | solution.py:346
  58.8 18.6 %copy-start.19 = (bf16[16,128,128]{2,1,0:T(8,128)(2,1)S(1)}, bf16[16,128,128]{2,1,0:T(8,128)(2,1)}, u32[]{:S(2)}) copy-start(bf16[16,128,128]{2,1,0:T(8,128)(2,1)} %get-tuple-element.40) | copy-start | bytes 1572868
  69.0 13.7 %collective-permute-start.11 = (bf16[16,128,128]{2,1,0:T(8,128)(2,1)}, bf16[16,128,128]{2,1,0:T(8,128)(2,1)}, u32[]{:S(2)}, u32[]{:S(2)}) collective-permute-start(bf16[16,128,128]{2,1,0:T(8,128)(2,1)} %get-tuple-element.57), channel_id=1, source_target_pairs={{0,1},{1,0},{2,3},{3,2},{4,5},{5,4},{6,7},{7,6},{8,16},{9,17},{10,... | collective-permute-start | bytes 1572872 | tf_op jit(solution)/shard_map/ppermute | solution.py:346
  69.0 19.6 %collective-permute-start.10 = (bf16[16,128,128]{2,1,0:T(8,128)(2,1)}, bf16[16,128,128]{2,1,0:T(8,128)(2,1)}, u32[]{:S(2)}, u32[]{:S(2)}) collective-permute-start(bf16[16,128,128]{2,1,0:T(8,128)(2,1)} %get-tuple-element.58), channel_id=1, source_target_pairs={{0,8},{1,9},{2,10},{3,11},{4,12},{5,13},{6,14},{7,15},{8,0},{9,1},... | collective-permute-start | bytes 1572872 | tf_op jit(solution)/shard_map/ppermute | solution.py:346
  80.0 19.8 %collective-permute-start.15 = (bf16[16,128,128]{2,1,0:T(8,128)(2,1)}, bf16[16,128,128]{2,1,0:T(8,128)(2,1)}, u32[]{:S(2)}, u32[]{:S(2)}) collective-permute-start(bf16[16,128,128]{2,1,0:T(8,128)(2,1)} %get-tuple-element.56), channel_id=1, source_target_pairs={{0,8},{1,9},{2,10},{3,11},{4,12},{5,13},{6,14},{7,15},{8,0},{9,1},... | collective-permute-start | bytes 1572872 | tf_op jit(solution)/shard_map/ppermute | solution.py:346
  82.6 17.2 %collective-permute-start.16 = (bf16[16,128,128]{2,1,0:T(8,128)(2,1)}, bf16[16,128,128]{2,1,0:T(8,128)(2,1)}, u32[]{:S(2)}, u32[]{:S(2)}) collective-permute-start(bf16[16,128,128]{2,1,0:T(8,128)(2,1)} %get-tuple-element.55), channel_id=1, source_target_pairs={{0,1},{1,0},{2,3},{3,2},{4,5},{5,4},{6,7},{7,6},{8,16},{9,17},{10,... | collective-permute-start | bytes 1572872 | tf_op jit(solution)/shard_map/ppermute | solution.py:346
  82.7 12.8 %copy-start.2 = (bf16[32,128,128]{2,1,0:T(8,128)(2,1)S(1)}, bf16[32,128,128]{2,1,0:T(8,128)(2,1)}, u32[]{:S(2)}) copy-start(bf16[32,128,128]{2,1,0:T(8,128)(2,1)} %copy-done.1) | copy-start | bytes 3145732
  82.7 12.8 %copy-start.4 = (bf16[32,128,128]{2,1,0:T(8,128)(2,1)S(1)}, bf16[32,128,128]{2,1,0:T(8,128)(2,1)}, u32[]{:S(2)}) copy-start(bf16[32,128,128]{2,1,0:T(8,128)(2,1)} %copy-done.3) | copy-start | bytes 3145732
  82.7 12.8 %copy-start.6 = (bf16[32,128,128]{2,1,0:T(8,128)(2,1)S(1)}, bf16[32,128,128]{2,1,0:T(8,128)(2,1)}, u32[]{:S(2)}) copy-start(bf16[32,128,128]{2,1,0:T(8,128)(2,1)} %copy-done.5) | copy-start | bytes 3145732
  90.6 18.1 %collective-permute-start.21 = (bf16[16,128,128]{2,1,0:T(8,128)(2,1)S(1)}, bf16[16,128,128]{2,1,0:T(8,128)(2,1)S(1)}, u32[]{:S(2)}, u32[]{:S(2)}) collective-permute-start(bf16[16,128,128]{2,1,0:T(8,128)(2,1)S(1)} %get-tuple-element.53), channel_id=1, source_target_pairs={{0,1},{1,0},{2,3},{3,2},{4,5},{5,4},{6,7},{7,6},{8,16},{9,17},{10,... | collective-permute-start | bytes 1572872 | tf_op jit(solution)/shard_map/ppermute | solution.py:346
  90.7 20.2 %collective-permute-start.19 = (bf16[16,128,128]{2,1,0:T(8,128)(2,1)S(1)}, bf16[16,128,128]{2,1,0:T(8,128)(2,1)S(1)}, u32[]{:S(2)}, u32[]{:S(2)}) collective-permute-start(bf16[16,128,128]{2,1,0:T(8,128)(2,1)S(1)} %get-tuple-element.54), channel_id=1, source_target_pairs={{0,8},{1,9},{2,10},{3,11},{4,12},{5,13},{6,14},{7,15},{8,0},{9,1},... | collective-permute-start | bytes 1572872 | tf_op jit(solution)/shard_map/ppermute | solution.py:346
  95.4 1.0 copy-start.11
  96.5 3.4 %copy-start.20 = (bf16[16,128,128]{2,1,0:T(8,128)(2,1)S(1)}, bf16[16,128,128]{2,1,0:T(8,128)(2,1)}, u32[]{:S(2)}) copy-start(bf16[16,128,128]{2,1,0:T(8,128)(2,1)} %get-tuple-element.48) | copy-start | bytes 1572868
  96.5 3.4 %copy-start.21 = (bf16[16,128,128]{2,1,0:T(8,128)(2,1)S(1)}, bf16[16,128,128]{2,1,0:T(8,128)(2,1)}, u32[]{:S(2)}) copy-start(bf16[16,128,128]{2,1,0:T(8,128)(2,1)} %get-tuple-element.49) | copy-start | bytes 1572868
  98.8 7.5 %copy-start.9 = (bf16[16,128,128]{2,1,0:T(8,128)(2,1)S(1)}, bf16[16,128,128]{2,1,0:T(8,128)(2,1)}, u32[]{:S(2)}) copy-start(bf16[16,128,128]{2,1,0:T(8,128)(2,1)} %copy-done.8) | copy-start | bytes 1572868
  101.6 9.6 %collective-permute-start.22 = (bf16[16,128,128]{2,1,0:T(8,128)(2,1)S(1)}, bf16[16,128,128]{2,1,0:T(8,128)(2,1)S(1)}, u32[]{:S(2)}, u32[]{:S(2)}) collective-permute-start(bf16[16,128,128]{2,1,0:T(8,128)(2,1)S(1)} %get-tuple-element.51), channel_id=1, source_target_pairs={{0,1},{1,0},{2,3},{3,2},{4,5},{5,4},{6,7},{7,6},{8,16},{9,17},{10,... | collective-permute-start | bytes 1572872 | tf_op jit(solution)/shard_map/ppermute | solution.py:346
  101.6 9.3 %copy-start.12 = (bf16[16,128,128]{2,1,0:T(8,128)(2,1)S(1)}, bf16[16,128,128]{2,1,0:T(8,128)(2,1)}, u32[]{:S(2)}) copy-start(bf16[16,128,128]{2,1,0:T(8,128)(2,1)} %get-tuple-element.44.refs_4_) | copy-start | bytes 1572868
  101.7 18.1 %copy-start.13 = (bf16[16,128,128]{2,1,0:T(8,128)(2,1)S(1)}, bf16[16,128,128]{2,1,0:T(8,128)(2,1)}, u32[]{:S(2)}) copy-start(bf16[16,128,128]{2,1,0:T(8,128)(2,1)} %get-tuple-element.45.refs_5_) | copy-start | bytes 1572868
  101.7 18.1 %collective-permute-start.20 = (bf16[16,128,128]{2,1,0:T(8,128)(2,1)S(1)}, bf16[16,128,128]{2,1,0:T(8,128)(2,1)S(1)}, u32[]{:S(2)}, u32[]{:S(2)}) collective-permute-start(bf16[16,128,128]{2,1,0:T(8,128)(2,1)S(1)} %get-tuple-element.52), channel_id=1, source_target_pairs={{0,8},{1,9},{2,10},{3,11},{4,12},{5,13},{6,14},{7,15},{8,0},{9,1},... | collective-permute-start | bytes 1572872 | tf_op jit(solution)/shard_map/ppermute | solution.py:346
  106.3 13.6 %collective-permute-start.17 = (bf16[16,64,128]{2,1,0:T(8,128)(2,1)S(1)}, bf16[16,64,128]{2,1,0:T(8,128)(2,1)S(1)}, u32[]{:S(2)}, u32[]{:S(2)}) collective-permute-start(bf16[16,64,128]{2,1,0:T(8,128)(2,1)S(1)} %get-tuple-element.42), channel_id=1, source_target_pairs={{0,1},{1,0},{2,3},{3,2},{4,5},{5,4},{6,7},{7,6},{8,9},{9,8},{10,11... | collective-permute-start | bytes 786440 | tf_op jit(solution)/shard_map/ppermute | solution.py:338
  106.3 15.1 %copy-start.14 = (bf16[128,256]{1,0:T(8,128)(2,1)S(1)}, bf16[128,256]{1,0:T(8,128)(2,1)}, u32[]{:S(2)}) copy-start(bf16[128,256]{1,0:T(8,128)(2,1)} %weight.5) | copy-start | bytes 196612
  108.7 12.8 %copy-start = (bf16[128,64,128]{2,1,0:T(8,128)(2,1)S(1)}, bf16[128,64,128]{2,1,0:T(8,128)(2,1)}, u32[]{:S(2)}) copy-start(bf16[128,64,128]{2,1,0:T(8,128)(2,1)} %pair.4) | copy-start | bytes 6291460
  108.7 12.8 %copy-start.16 = (s32[4,4]{1,0:T(4,128)S(1)}, s32[4,4]{1,0:T(4,128)}, u32[]{:S(2)}) copy-start(s32[4,4]{1,0:T(4,128)} %mask.5) | copy-start | bytes 196
  108.7 12.8 %copy-start.17 = (f32[128]{0:T(128)S(1)}, f32[128]{0:T(128)}, u32[]{:S(2)}) copy-start(f32[128]{0:T(128)} %param.8) | copy-start | bytes 1540
  108.7 12.8 %copy-start.18 = (f32[128]{0:T(128)S(1)}, f32[128]{0:T(128)}, u32[]{:S(2)}) copy-start(f32[128]{0:T(128)} %param.9) | copy-start | bytes 1540
  108.7 11.3 %collective-permute-start.18 = (bf16[16,64,128]{2,1,0:T(8,128)(2,1)S(1)}, bf16[16,64,128]{2,1,0:T(8,128)(2,1)S(1)}, u32[]{:S(2)}, u32[]{:S(2)}) collective-permute-start(bf16[16,64,128]{2,1,0:T(8,128)(2,1)S(1)} %get-tuple-element.43), channel_id=1, source_target_pairs={{0,1},{1,0},{2,3},{3,2},{4,5},{5,4},{6,7},{7,6},{8,9},{9,8},{10,11... | collective-permute-start | bytes 786440 | tf_op jit(solution)/shard_map/ppermute | solution.py:338
  111.1 8.9 %collective-permute-start.23 = (bf16[16,64,128]{2,1,0:T(8,128)(2,1)S(1)}, bf16[16,64,128]{2,1,0:T(8,128)(2,1)S(1)}, u32[]{:S(2)}, u32[]{:S(2)}) collective-permute-start(bf16[16,64,128]{2,1,0:T(8,128)(2,1)S(1)} %add_convert_fusion.5), channel_id=1, source_target_pairs={{0,1},{1,0},{2,3},{3,2},{4,5},{5,4},{6,7},{7,6},{8,9},{9,8},{10,11... | collective-permute-start | bytes 786440 | tf_op jit(solution)/shard_map/ppermute | solution.py:338
  119.9 1.6 %collective-permute-start.24 = (bf16[16,64,128]{2,1,0:T(8,128)(2,1)S(1)}, bf16[16,64,128]{2,1,0:T(8,128)(2,1)S(1)}, u32[]{:S(2)}, u32[]{:S(2)}) collective-permute-start(bf16[16,64,128]{2,1,0:T(8,128)(2,1)S(1)} %add_convert_fusion.4), channel_id=1, source_target_pairs={{0,1},{1,0},{2,3},{3,2},{4,5},{5,4},{6,7},{7,6},{8,9},{9,8},{10,11... | collective-permute-start | bytes 786440 | tf_op jit(solution)/shard_map/ppermute | solution.py:338

commit v7 on v6

--- a/solution.py
+++ b/solution.py
@@ -34,6 +34,10 @@
     return mask_ref[(row * rows) // BLK, (col * cols) // BLK].astype(jnp.float32)
 
 
+def in_hbm(*values):
+    return [pltpu.with_memory_space_constraint(v, pltpu.HBM) for v in values]
+
+
 def this_core():
     return lax.rem(lax.axis_index("col"), CORES)
 
@@ -59,55 +63,102 @@
         weight_t[...] = weight[...].astype(jnp.float32).T.astype(jnp.bfloat16)
 
 
-def front_kernel(mask, pair, gain, bias, weight, mine, theirs, flipped, turned, normed, acts, whole, gain_col, bias_col, weight_t):
-    rows, keys, _ = pair.shape
-    hidden = weight.shape[1] // 2
-    half = hidden // CORES
-    set_columns(gain, bias, weight, gain_col, bias_col, weight_t)
-    valid = unit_mask(mask, rows, pl.num_programs(0) * keys)
+def normalized(pair, gain_col, bias_col, flipped, turned, normed):
     turn(pair, flipped, turned)
-    scaled, _ = normalize(turned[...])
+    scaled, inverse = normalize(turned[...])
     normed[...] = (scaled * gain_col[...] + bias_col[...]).astype(jnp.bfloat16)
-    for key in range(keys):
-        projected = jnp.dot(weight_t[...], normed[key], preferred_element_type=jnp.float32)
-        acts[key] = (valid * jax.nn.sigmoid(projected[hidden:]) * projected[:hidden]).astype(jnp.bfloat16)
+    return scaled, inverse
+
+
+def split_channels(acts, whole, mine, theirs):
+    half = mine.shape[0]
     whole[...] = jnp.transpose(acts[...], (1, 0, 2))
     core = this_core()
     mine[...] = whole[pl.ds(core * half, half)]
     theirs[...] = whole[pl.ds((1 - core) * half, half)]
 
 
-def front(pair, gain, bias, proj_weight, tile_mask, side):
+def right_kernel(mask, pair, gain, bias, weight, mine, theirs, flipped, turned, normed, acts, whole, gain_col, bias_col, weight_t):
+    rows, keys, _ = pair.shape
+    hidden = acts.shape[1]
+    set_columns(gain, bias, weight, gain_col, bias_col, weight_t)
+    valid = unit_mask(mask, rows, pl.num_programs(0) * keys)
+    normalized(pair, gain_col, bias_col, flipped, turned, normed)
+    for key in range(keys):
+        projected = jnp.dot(weight_t[...], normed[key], preferred_element_type=jnp.float32)
+        acts[key] = (valid * jax.nn.sigmoid(projected[hidden:]) * projected[:hidden]).astype(jnp.bfloat16)
+    split_channels(acts, whole, mine, theirs)
+
+
+def left_forward_kernel(
+    mask, pair, gain, bias, weight, mine, theirs, scaled_out, inverse_out, factors,
+    flipped, turned, normed, acts, whole, gain_col, bias_col, weight_t,
+):
+    rows, keys, _ = pair.shape
+    hidden = acts.shape[1]
+    set_columns(gain, bias, weight, gain_col, bias_col, weight_t)
+    valid = unit_mask(mask, rows, pl.num_programs(0) * keys)
+    scaled, inverse = normalized(pair, gain_col, bias_col, flipped, turned, normed)
+    scaled_out[...] = scaled.astype(jnp.bfloat16)
+    inverse_out[...] = inverse
+    for key in range(keys):
+        projected = jnp.dot(weight_t[...], normed[key], preferred_element_type=jnp.float32)
+        for side in range(2):
+            first = 2 * side * hidden
+            lin = projected[first : first + hidden]
+            sig = jax.nn.sigmoid(projected[first + hidden : first + 2 * hidden])
+            masked = valid * sig
+            act = masked * lin
+            if side == 0:
+                acts[key] = act.astype(jnp.bfloat16)
+            factors[key, first : first + hidden, :] = masked.astype(jnp.bfloat16)
+            factors[key, first + hidden : first + 2 * hidden, :] = (act * (1.0 - sig)).astype(jnp.bfloat16)
+    split_channels(acts, whole, mine, theirs)
+
+
+def front(pair, gain, bias, proj_weight, tile_mask, right):
     rows, cols, chans = pair.shape
-    width = proj_weight.shape[1] // 2
-    half = width // 2 // CORES
+    width = proj_weight.shape[1]
+    hidden = width // 4
+    half = hidden // CORES
+    used = width // 2 if right else width
     vector = pl.BlockSpec((1, chans), lambda g: (0, 0))
-    return pl.pallas_call(
-        front_kernel,
-        out_shape=[jax.ShapeDtypeStruct((half, cols, rows), jnp.bfloat16)] * 2,
+    by_key = lambda *shape: pl.BlockSpec((KEYS,) + shape, lambda g: (g, 0, 0))
+    out_shape = [jax.ShapeDtypeStruct((half, cols, rows), jnp.bfloat16)] * 2
+    out_specs = [pl.BlockSpec((half, KEYS, rows), lambda g: (0, g, 0))] * 2
+    if not right:
+        out_shape += [
+            jax.ShapeDtypeStruct((cols, chans, rows), jnp.bfloat16),
+            jax.ShapeDtypeStruct((cols, 1, rows), jnp.float32),
+            jax.ShapeDtypeStruct((cols, width, rows), jnp.bfloat16),
+        ]
+        out_specs += [by_key(chans, rows), by_key(1, rows), by_key(width, rows)]
+    return pl.pallas_call(
+        right_kernel if right else left_forward_kernel,
+        out_shape=out_shape,
         grid=(cols // KEYS,),
         in_specs=[
             pl.BlockSpec(memory_space=pltpu.SMEM),
             pl.BlockSpec((rows, KEYS, chans), lambda g: (0, g, 0)),
             vector,
             vector,
-            pl.BlockSpec((chans, width), lambda g: (0, side)),
+            pl.BlockSpec((chans, used), lambda g: (0, 1 if right else 0)),
         ],
-        out_specs=[pl.BlockSpec((half, KEYS, rows), lambda g: (0, g, 0))] * 2,
+        out_specs=out_specs,
         scratch_shapes=[
             pltpu.VMEM((KEYS, rows, chans), jnp.bfloat16),
             pltpu.VMEM((KEYS, chans, rows), jnp.float32),
             pltpu.VMEM((KEYS, chans, rows), jnp.bfloat16),
-            pltpu.VMEM((KEYS, width // 2, rows), jnp.bfloat16),
-            pltpu.VMEM((width // 2, KEYS, rows), jnp.bfloat16),
+            pltpu.VMEM((KEYS, hidden, rows), jnp.bfloat16),
+            pltpu.VMEM((hidden, KEYS, rows), jnp.bfloat16),
             pltpu.VMEM((chans, rows), jnp.float32),
             pltpu.VMEM((chans, rows), jnp.float32),
-            pltpu.VMEM((width, chans), jnp.bfloat16),
+            pltpu.VMEM((used, chans), jnp.bfloat16),
         ],
         compiler_params=PARAMS,
         cost_estimate=FRONT_COST,
-        name="left_front" if side == 0 else "right_front",
-    )(tile_mask, *(pltpu.with_memory_space_constraint(v, pltpu.HBM) for v in (pair, gain, bias, proj_weight)))
+        name="right_front" if right else "left_front",
+    )(tile_mask, *in_hbm(pair, gain, bias, proj_weight))
 
 
 def pack_kernel(own, other, out):
@@ -131,6 +182,27 @@
 def chunk_spec(array, chans, chunk):
     first = chunk * chans // STEP if array.shape[0] > chans else 0
     return pl.BlockSpec((STEP,) + array.shape[1:], lambda g: (first + g, 0, 0))
+
+
+def cut_kernel(*refs):
+    count = len(refs) // 2
+    for source, out in zip(refs[:count], refs[count:]):
+        out[...] = source[...]
+
+
+def cut(arrays, chunks):
+    chans = arrays[0].shape[0] // CHUNKS
+    shape = (chans,) + arrays[0].shape[1:]
+    return pl.pallas_call(
+        cut_kernel,
+        out_shape=[jax.ShapeDtypeStruct(shape, jnp.bfloat16)] * len(arrays),
+        grid=(chans // STEP,),
+        in_specs=[chunk_spec(v, chans, c) for v, c in zip(arrays, chunks)],
+        out_specs=[pl.BlockSpec((STEP,) + shape[1:], lambda g: (g, 0, 0))] * len(arrays),
+        compiler_params=PARAMS,
+        cost_estimate=FRONT_COST,
+        name="cut",
+    )(*arrays)
 
 
 def lanes(n):
@@ -160,10 +232,6 @@
     for s, out in enumerate(outs):
         out[...] = sums[s]
     next_a[...], next_b[...] = onward(by_a[...], by_b[...], sums[n - 1], sums[1], 1, n)
-
-
-def in_hbm(*values):
-    return [pltpu.with_memory_space_constraint(v, pltpu.HBM) for v in values]
 
 
 def partial_products(left_mine, left_other, by_a, by_b, blocks, chunk):
@@ -234,17 +302,19 @@
     return total + jnp.where(use_b, by_b.astype(jnp.float32), 0.0)
 
 
-def tail_kernel(n, mask, pair, gain, bias, weight, *refs):
+def tail_kernel(n, scaled, inverse, factors, gain, weight, *refs):
     groups = [refs[i * CHUNKS : (i + 1) * CHUNKS] for i in range(6)]
     left_mine, left_other, partials, by_a, by_b, right_other = groups
-    out, flipped, turned, normed, inverses, grads, right_flat, left_flat, gain_col, bias_col, weight_t = refs[6 * CHUNKS :]
-    rows, keys, _ = pair.shape
+    out, results, flipped, grads, right_flat, left_flat, gain_col = refs[6 * CHUNKS :]
+    keys, chans, rows = scaled.shape
     hidden = weight.shape[1] // 4
     half = hidden // CORES
     part = half // CHUNKS
     core = this_core()
-    set_columns(gain, bias, weight, gain_col, bias_col, weight_t)
-    valid = unit_mask(mask, rows, pl.num_programs(0) * keys)
+
+    @pl.when(pl.program_id(0) == 0)
+    def _():
+        gain_col[...] = column(gain, rows)
 
     def put(flat, owner, chunk, value):
         first = pl.multiple_of((owner * half + chunk * part) * keys, part * keys)
@@ -256,72 +326,58 @@
         put(right_flat, 1 - core, chunk, right_other[chunk][...])
         put(left_flat, core, chunk, left_mine[chunk][...])
         put(left_flat, 1 - core, chunk, left_other[chunk][...])
-    turn(pair, flipped, turned)
-    scaled, inverse = normalize(turned[...])
-    turned[...] = scaled
-    inverses[...] = inverse
-    normed[...] = (scaled * gain_col[...] + bias_col[...]).astype(jnp.bfloat16)
     for key in range(keys):
-        projected = jnp.dot(weight_t[...], normed[key], preferred_element_type=jnp.float32)
         for side, source in enumerate((left_flat, right_flat)):
-            lin = projected[2 * side * hidden : (2 * side + 1) * hidden]
-            sig = jax.nn.sigmoid(projected[(2 * side + 1) * hidden : (2 * side + 2) * hidden])
-            through = source[pl.ds(key, hidden, stride=keys), :] * valid * sig
-            grads[key, 2 * side * hidden : (2 * side + 1) * hidden, :] = through.astype(jnp.bfloat16)
-            grads[key, (2 * side + 1) * hidden : (2 * side + 2) * hidden, :] = (through * lin * (1.0 - sig)).astype(
-                jnp.bfloat16
-            )
+            grad = source[pl.ds(key, hidden, stride=keys), :]
+            for i in (2 * side, 2 * side + 1):
+                place = slice(i * hidden, (i + 1) * hidden)
+                grads[key, place, :] = (grad * factors[key, place, :].astype(jnp.float32)).astype(jnp.bfloat16)
     for key in range(keys):
-        scaled = turned[key]
+        scaled_key = scaled[key].astype(jnp.float32)
         scaled_grad = jnp.dot(weight[...], grads[key], preferred_element_type=jnp.float32) * gain_col[...]
-        result = inverses[key] * (
+        result = inverse[key] * (
             scaled_grad
             - jnp.mean(scaled_grad, axis=0, keepdims=True)
-            - scaled * jnp.mean(scaled_grad * scaled, axis=0, keepdims=True)
+            - scaled_key * jnp.mean(scaled_grad * scaled_key, axis=0, keepdims=True)
         )
-        normed[key] = result.astype(jnp.bfloat16)
+        results[key] = result.astype(jnp.bfloat16)
     eye = identity(rows)
     for key in range(keys):
-        flipped[key] = lax.dot_general(eye, normed[key], BY_LAST, preferred_element_type=jnp.float32).astype(jnp.bfloat16)
+        flipped[key] = lax.dot_general(eye, results[key], BY_LAST, preferred_element_type=jnp.float32).astype(jnp.bfloat16)
     out[...] = jnp.transpose(flipped[...], (1, 0, 2))
 
 
-def tail(pair, gain, bias, proj_weight, tile_mask, left_mine, left_other, partials, by_a, by_b, right_other):
-    rows, cols, chans = pair.shape
+def tail(scaled, inverse, factors, gain, proj_weight, left_mine, left_other, partials, by_a, by_b, right_other):
+    cols, chans, rows = scaled.shape
     width = proj_weight.shape[1]
-    part = width // 4 // CORES // CHUNKS
-    vector = pl.BlockSpec((1, chans), lambda g: (0, 0))
-    cells = pl.BlockSpec((rows, KEYS, chans), lambda g: (0, g, 0))
-    small = [pl.BlockSpec((part, KEYS, rows), lambda g: (0, g, 0))] * CHUNKS
+    hidden = width // 4
+    part = hidden // CORES // CHUNKS
+    by_key = lambda *shape: pl.BlockSpec((KEYS,) + shape, lambda g: (g, 0, 0))
     return pl.pallas_call(
         functools.partial(tail_kernel, lax.axis_size("row")),
-        out_shape=jax.ShapeDtypeStruct(pair.shape, jnp.bfloat16),
+        out_shape=jax.ShapeDtypeStruct((rows, cols, chans), jnp.bfloat16),
         grid=(cols // KEYS,),
         in_specs=[
-            pl.BlockSpec(memory_space=pltpu.SMEM),
-            cells,
-            vector,
-            vector,
+            by_key(chans, rows),
+            by_key(1, rows),
+            by_key(width, rows),
+            pl.BlockSpec((1, chans), lambda g: (0, 0)),
             pl.BlockSpec((chans, width), lambda g: (0, 0)),
         ]
-        + small * 6,
-        out_specs=cells,
+        + [pl.BlockSpec((part, KEYS, rows), lambda g: (0, g, 0))] * (6 * CHUNKS),
+        out_specs=pl.BlockSpec((rows, KEYS, chans), lambda g: (0, g, 0)),
         scratch_shapes=[
+            pltpu.VMEM((KEYS, chans, rows), jnp.bfloat16),
             pltpu.VMEM((KEYS, rows, chans), jnp.bfloat16),
-            pltpu.VMEM((KEYS, chans, rows), jnp.float32),
-            pltpu.VMEM((KEYS, chans, rows), jnp.bfloat16),
-            pltpu.VMEM((KEYS, 1, rows), jnp.float32),
             pltpu.VMEM((KEYS, width, rows), jnp.bfloat16),
-            pltpu.VMEM((width // 4 * KEYS, rows), jnp.float32),
-            pltpu.VMEM((width // 4 * KEYS, rows), jnp.float32),
+            pltpu.VMEM((hidden * KEYS, rows), jnp.float32),
+            pltpu.VMEM((hidden * KEYS, rows), jnp.float32),
             pltpu.VMEM((chans, rows), jnp.float32),
-            pltpu.VMEM((chans, rows), jnp.float32),
-            pltpu.VMEM((width, chans), jnp.bfloat16),
         ],
         compiler_params=PARAMS,
         cost_estimate=COST,
         name="tail",
-    )(tile_mask, pair, gain, bias, proj_weight, *left_mine, *left_other, *partials, *by_a, *by_b, *right_other)
+    )(scaled, inverse, factors, gain, proj_weight, *left_mine, *left_other, *partials, *by_a, *by_b, *right_other)
 
 
 def after(value, *others):
@@ -347,26 +403,25 @@
 
     raw = jnp.transpose(grad_x, (1, 2, 0))
     other = exchange(lax.dynamic_slice_in_dim(raw, (1 - this_core()) * half, half, 1), 1)
-    right_mine, right_theirs = front(pair, gain, bias, proj_weight, tile_mask, 1)
-    packed = pack(raw, after(other, right_mine))
-
-    slots = [[packed] * CHUNKS]
-    for m in range(1, n_col // CORES):
-        axes = [1 << b for b in range(m.bit_length()) if m >> b & 1]
-        if len(axes) == 1:
-            slots.append([exchange(packed, CORES * m)] * CHUNKS)
-            continue
-        slots.append([])
-        for c in range(CHUNKS):
-            bit = axes[(c + 1) % len(axes)]
-            value = slots[m ^ bit][c]
-            value = value if value.shape[0] == part else value[c * part : (c + 1) * part]
-            slots[m].append(exchange(value, CORES * bit))
-    panels = [[slot[c] for slot in slots] for c in range(CHUNKS)]
-
-    own = jnp.concatenate((right_mine, exchange(right_theirs, 1)), axis=1)
+    packed = pack(raw, other)
+
+    axes = {m: [1 << b for b in range(m.bit_length()) if m >> b & 1] for m in range(n_col // CORES)}
+    whole = {m: exchange(packed, CORES * m) for m in axes if len(axes[m]) == 1}
+    turns = [(m, c, axes[m][(c + 1) % 2]) for m in axes if len(axes[m]) == 2 for c in range(CHUNKS)]
+    cuts = cut([whole[m ^ bit] for m, _, bit in turns], [c for _, c, _ in turns])
+    relayed = {(m, c): exchange(value, CORES * bit) for (m, c, bit), value in zip(turns, cuts)}
+    for m in axes:
+        for c in range(CHUNKS if len(axes[m]) > 2 else 0):
+            bit = axes[m][c % len(axes[m])]
+            relayed[m, c] = exchange(relayed[m ^ bit, c], CORES * bit)
+    whole[0] = packed
+    panels = [[whole[m] if m in whole else relayed[m, c] for m in axes] for c in range(CHUNKS)]
+
+    right_mine, right_theirs = front(after(pair, packed), gain, bias, proj_weight, tile_mask, True)
+    right_other = [exchange(right_theirs[c * part : (c + 1) * part], 1) for c in range(CHUNKS)]
+    own = jnp.concatenate((right_mine, jnp.concatenate(right_other)), axis=1)
     first_a, first_b = hop(own, 0), hop(own, 1)
-    left_mine, left_theirs = front(after(pair, own), gain, bias, proj_weight, tile_mask, 0)
+    left_mine, left_theirs, *forward = front(after(pair, own), gain, bias, proj_weight, tile_mask, False)
     left_other = exchange(left_theirs, 1)
 
     by_a, by_b, partials = [], [], []
@@ -395,11 +450,9 @@
         right_grad_other.append(exchange(total.astype(jnp.bfloat16), 1))
 
     return tail(
-        pair,
+        *forward,
         gain,
-        bias,
         proj_weight,
-        tile_mask,
         [mine for mine, _ in left_grads],
         left_grad_other,
         [sums[0] for sums in partials],

time: 133 us -> 128 us (0.962)
  starting transfers between devices: 34.2 us -> 27.3 us
  local copies, waits for them, and re-layouts: 3.16 us -> 6.78 us
  Pallas kernels: 32.8 us -> 30.6 us
    ppermute x11 -> x12, waiting for transfers between devices: 24.1 us -> 13.2 us  [exchange(): return lax.ppermute(value, 'col', [(d, d ^ mask) for d in range(n_col)])]
    ppermute x14, waiting for transfers between devices: 28.6 us -> 39.3 us  [hop(): return lax.ppermute(value, ('row', 'col'), perm)]
    ppermute x14, starting transfers between devices: 24.8 us -> 18 us  [hop(): return lax.ppermute(value, ('row', 'col'), perm)]
    unnamed x45 -> x46, local copies, waits for them, and re-layouts: 1.84 us -> 5.65 us
    pallas_call x1, Pallas kernels: 11.3 us -> 8.27 us  [tail(): pl.pallas_call(functools.partial(tail_kernel, lax.axis_size('row')), out_...]
    pallas_call x2 -> x3, Pallas kernels: 10.3 us -> 11 us  [the longest x2 10.9 us: front(): pl.pallas_call(right_kernel if right else left_forward_kernel, out_shape=...]
    ppermute x11 -> x12, starting transfers between devices: 9.34 us -> 9.31 us  [exchange(): return lax.ppermute(value, 'col', [(d, d ^ mask) for d in range(n_col)])]
  transfers between devices with their start and end apart: 25 -> 26, of which waited for: 10 -> 14; matrix products, arithmetic and copies ran while one was open for 7% -> 8% of each run, Pallas kernels for 16% -> 17%
where the time goes in v7:
time: 128 us; the launch traced here: 127 us
  waiting for transfers between devices  52.4 us (41%)
  Pallas kernels  30.6 us (24%)
  starting transfers between devices  27.3 us (21%)
  other arithmetic  9.6 us (8%)
  local copies, waits for them, and re-layouts  6.78 us (5%)
    ppermute x14, waiting for transfers between devices, hop(): return lax.ppermute(value, ('row', 'col'), perm)  39.3 us
    ppermute x14, starting transfers between devices, hop(): return lax.ppermute(value, ('row', 'col'), perm)  18 us
    ppermute x12, waiting for transfers between devices, exchange(): return lax.ppermute(value, 'col', [(d, d ^ mask) for d in range(n_col)])  13.2 us
    pallas_call x2, Pallas kernels, front(): pl.pallas_call(right_kernel if right else left_forward_kernel, out_shape=...  10.9 us
    ppermute x12, starting transfers between devices, exchange(): return lax.ppermute(value, 'col', [(d, d ^ mask) for d in range(n_col)])  9.31 us
    convert_element_type x4, other arithmetic, onward(): return (out_a.astype(jnp.bfloat16), out_b.astype(jnp.bfloat16))  9.23 us
    pallas_call x1, Pallas kernels, tail(): pl.pallas_call(functools.partial(tail_kernel, lax.axis_size('row')), out_...  8.27 us
    pallas_call x2, Pallas kernels, partial_products(): pl.pallas_call(functools.partial(partial_kernel, n), out_shape=[pltpu.HBM...  6.17 us
  transfers between devices with their start and end apart: 26, of which 14 were waited for; matrix products, arithmetic and copies ran while one was open for 8% of the time, Pallas kernels for 17%

profile of v7, /device:TPU:0, one launch (start us, length us, event | category | flops | bytes accessed | tf_op | source)
XLA Modules:
  0.0 127.0 jit_solution(14586102657518455702)
XLA Ops:
  0.0 1.1 dynamic-slice_bitcast_fusion
  1.1 0.5 collective-permute-start
  1.6 1.5 %collective-permute-done.other = bf16[64,32,128]{2,1,0:T(8,128)(2,1)S(1)} collective-permute-done((bf16[64,32,128]{2,1,0:T(8,128)(2,1)S(1)}, bf16[64,32,128]{2,1,0:T(8,128)(2,1)S(1)}, u32[]{:S(2)}, u32[]{:S(2)}) %collective-permute-start) | collective-permute-done | bytes 524320 | tf_op jit(solution)/shard_map/ppermute | solution.py:394
  3.2 1.2 copy-done.8
  4.4 0.4 pack.1.refs_0_.refs_6_
  4.8 2.9 %collective-permute-start.6 = (bf16[32,128,128]{2,1,0:T(8,128)(2,1)S(1)}, bf16[32,128,128]{2,1,0:T(8,128)(2,1)S(1)}, u32[]{:S(2)}, u32[]{:S(2)}) collective-permute-start(bf16[32,128,128]{2,1,0:T(8,128)(2,1)S(1)} %pack.1.refs_0_.refs_6_), channel_id=1, source_target_pairs={{0,2},{1,3},{2,0},{3,1},{4,6},{5,7},{6,4},{7,5},{8,10},{9,11},{10,... | collective-permute-start | bytes 3145736 | tf_op jit(solution)/shard_map/ppermute | solution.py:394
  7.7 1.5 %collective-permute-start.7 = (bf16[32,128,128]{2,1,0:T(8,128)(2,1)S(1)}, bf16[32,128,128]{2,1,0:T(8,128)(2,1)S(1)}, u32[]{:S(2)}, u32[]{:S(2)}) collective-permute-start(bf16[32,128,128]{2,1,0:T(8,128)(2,1)S(1)} %pack.1.refs_0_.refs_6_), channel_id=1, source_target_pairs={{0,4},{1,5},{2,6},{3,7},{4,0},{5,1},{6,2},{7,3},{8,12},{9,13},{10,... | collective-permute-start | bytes 3145736 | tf_op jit(solution)/shard_map/ppermute | solution.py:394
  9.2 5.1 %right_front.1 = (bf16[32,64,128]{2,1,0:T(8,128)(2,1)S(1)}, bf16[32,64,128]{2,1,0:T(8,128)(2,1)S(1)}) custom-call(s32[4,4]{1,0:T(4,128)S(1)} %copy-done.18, bf16[128,64,128]{2,1,0:T(8,128)(2,1)} %pair.1, f32[1,128]{1,0:T(1,128)} %bitcast.6, f32[1,128]{1,0:T(1,128)} %bitcast.9, bf16[128,256]{1,0:T(8,128)(2,1)} %weight.5), custom_call_target="tpu_custom_call" | custom-call | flops 1 | bytes 18000000 | tf_op jit(solution)/shard_map/right_front/pallas_call | solution.py:136
  14.5 0.5 collective-permute-start.1
  15.0 1.0 collective-permute-done.2
  16.0 0.4 collective-permute-done.1
  16.5 1.6 %collective-permute-start.3 = (bf16[32,128,128]{2,1,0:T(8,128)(2,1)S(1)}, bf16[32,128,128]{2,1,0:T(8,128)(2,1)S(1)}, u32[]{:S(2)}, u32[]{:S(2)}) collective-permute-start(bf16[32,128,128]{2,1,0:T(8,128)(2,1)S(1)} %maximum_maximum_fusion.own), channel_id=1, source_target_pairs={{0,8},{1,9},{2,10},{3,11},{4,12},{5,13},{6,14},{7,15},{8,0},{9,1},... | collective-permute-start | bytes 3145736 | tf_op jit(solution)/shard_map/ppermute | solution.py:402
  18.1 5.8 %left_front.1 = (bf16[32,64,128]{2,1,0:T(8,128)(2,1)S(1)}, bf16[32,64,128]{2,1,0:T(8,128)(2,1)S(1)}, bf16[64,128,128]{2,1,0:T(8,128)(2,1)S(1)}, f32[64,1,128]{2,1,0:T(1,128)S(1)}, bf16[64,256,128]{2,1,0:T(8,128)(2,1)S(1)}) custom-call(s32[4,4]{1,0:T(4,128)S(1)} %copy-done.18, bf16[128,64,128]{2,1,0:T(8,128)(2,1)} %pair.1, f32[1,128]{1,0:T(1,128)} %bitcast.7, ...), custom_call_target="tpu_custom_call" | custom-call | flops 1 | bytes 18000000 | tf_op jit(solution)/shard_map/left_front/pallas_call | solution.py:136
  23.9 2.0 %copy-done.6 = bf16[64,256,128]{2,1,0:T(8,128)(2,1)} copy-done((bf16[64,256,128]{2,1,0:T(8,128)(2,1)}, bf16[64,256,128]{2,1,0:T(8,128)(2,1)S(1)}, u32[]{:S(2)}) %copy-start.6) | copy-done | bytes 4194328
  25.9 1.3 %copy-done.9 = bf16[64,128,128]{2,1,0:T(8,128)(2,1)} copy-done((bf16[64,128,128]{2,1,0:T(8,128)(2,1)}, bf16[64,128,128]{2,1,0:T(8,128)(2,1)S(1)}, u32[]{:S(2)}) %copy-start.9) | copy-done | bytes 2097176
  27.2 0.5 collective-permute-start.4
  27.8 3.4 %collective-permute-done.6.refs_0_.refs_1_.refs_7_ = bf16[32,128,128]{2,1,0:T(8,128)(2,1)S(1)} collective-permute-done((bf16[32,128,128]{2,1,0:T(8,128)(2,1)S(1)}, bf16[32,128,128]{2,1,0:T(8,128)(2,1)S(1)}, u32[]{:S(2)}, u32[]{:S(2)}) %collective-permute-start.6) | collective-permute-done | bytes 1048608 | tf_op jit(solution)/shard_map/ppermute | solution.py:394
  31.2 1.5 %collective-permute-done.7.refs_1_.refs_2_.refs_8_ = bf16[32,128,128]{2,1,0:T(8,128)(2,1)S(1)} collective-permute-done((bf16[32,128,128]{2,1,0:T(8,128)(2,1)S(1)}, bf16[32,128,128]{2,1,0:T(8,128)(2,1)S(1)}, u32[]{:S(2)}, u32[]{:S(2)}) %collective-permute-start.7) | collective-permute-done | bytes 1048608 | tf_op jit(solution)/shard_map/ppermute | solution.py:394
  32.7 1.6 %collective-permute-start.8 = (bf16[16,128,128]{2,1,0:T(8,128)(2,1)S(1)}, bf16[16,128,128]{2,1,0:T(8,128)(2,1)S(1)}, u32[]{:S(2)}, u32[]{:S(2)}) collective-permute-start(bf16[16,128,128]{2,1,0:T(8,128)(2,1)S(1)} %get-tuple-element.42), channel_id=1, source_target_pairs={{0,4},{1,5},{2,6},{3,7},{4,0},{5,1},{6,2},{7,3},{8,12},{9,13},{10,... | collective-permute-start | bytes 1572872 | tf_op jit(solution)/shard_map/ppermute | solution.py:394
  34.3 0.5 collective-permute-start.13
  34.9 6.9 %collective-permute-done.3.by_a.refs_0_ = bf16[32,128,128]{2,1,0:T(8,128)(2,1)S(1)} collective-permute-done((bf16[32,128,128]{2,1,0:T(8,128)(2,1)S(1)}, bf16[32,128,128]{2,1,0:T(8,128)(2,1)S(1)}, u32[]{:S(2)}, u32[]{:S(2)}) %collective-permute-start.3) | collective-permute-done | bytes 1048608 | tf_op jit(solution)/shard_map/ppermute | solution.py:402
  41.8 3.9 %collective-permute-done.8.refs_3_.refs_9_ = bf16[16,128,128]{2,1,0:T(8,128)(2,1)S(1)} collective-permute-done((bf16[16,128,128]{2,1,0:T(8,128)(2,1)S(1)}, bf16[16,128,128]{2,1,0:T(8,128)(2,1)S(1)}, u32[]{:S(2)}, u32[]{:S(2)}) %collective-permute-start.8) | collective-permute-done | bytes 524320 | tf_op jit(solution)/shard_map/ppermute | solution.py:394
  45.6 3.1 %right_partials.2 = (bf16[16,128,128]{2,1,0:T(8,128)(2,1)}, bf16[16,128,128]{2,1,0:T(8,128)(2,1)}, bf16[16,128,128]{2,1,0:T(8,128)(2,1)}, bf16[16,128,128]{2,1,0...) custom-call(bf16[32,64,128]{2,1,0:T(8,128)(2,1)S(1)} %get-tuple-element.40.left_mine, ...), custom_call_target="tpu_custom_call" | custom-call | flops 1 | bytes 8000000 | tf_op jit(solution)/shard_map/right_partials/pallas_call | solution.py:242
  48.7 1.6 %collective-permute-start.9 = (bf16[16,128,128]{2,1,0:T(8,128)(2,1)}, bf16[16,128,128]{2,1,0:T(8,128)(2,1)}, u32[]{:S(2)}, u32[]{:S(2)}) collective-permute-start(bf16[16,128,128]{2,1,0:T(8,128)(2,1)} %get-tuple-element.43), channel_id=1, source_target_pairs={{0,8},{1,9},{2,10},{3,11},{4,12},{5,13},{6,14},{7,15},{8,0},{9,1},... | collective-permute-start | bytes 1572872 | tf_op jit(solution)/shard_map/ppermute | solution.py:402
  50.3 3.1 %right_partials.3 = (bf16[16,128,128]{2,1,0:T(8,128)(2,1)}, bf16[16,128,128]{2,1,0:T(8,128)(2,1)}, bf16[16,128,128]{2,1,0:T(8,128)(2,1)}, bf16[16,128,128]{2,1,0...) custom-call(bf16[32,64,128]{2,1,0:T(8,128)(2,1)S(1)} %get-tuple-element.40.left_mine, ...), custom_call_target="tpu_custom_call" | custom-call | flops 1 | bytes 8000000 | tf_op jit(solution)/shard_map/right_partials/pallas_call | solution.py:242
  53.4 3.2 %collective-permute-start.14 = (bf16[16,128,128]{2,1,0:T(8,128)(2,1)}, bf16[16,128,128]{2,1,0:T(8,128)(2,1)}, u32[]{:S(2)}, u32[]{:S(2)}) collective-permute-start(bf16[16,128,128]{2,1,0:T(8,128)(2,1)} %get-tuple-element.48), channel_id=1, source_target_pairs={{0,8},{1,9},{2,10},{3,11},{4,12},{5,13},{6,14},{7,15},{8,0},{9,1},... | collective-permute-start | bytes 1572872 | tf_op jit(solution)/shard_map/ppermute | solution.py:402
  56.6 7.3 %collective-permute-done.9.refs_1_ = bf16[16,128,128]{2,1,0:T(8,128)(2,1)} collective-permute-done((bf16[16,128,128]{2,1,0:T(8,128)(2,1)}, bf16[16,128,128]{2,1,0:T(8,128)(2,1)}, u32[]{:S(2)}, u32[]{:S(2)}) %collective-permute-start.9) | collective-permute-done | bytes 524320 | tf_op jit(solution)/shard_map/ppermute | solution.py:402
  63.9 2.8 %fusion.11 = (bf16[16,128,128]{2,1,0:T(8,128)(2,1)}, bf16[16,128,128]{2,1,0:T(8,128)(2,1)}) fusion(bf16[16,128,128]{2,1,0:T(8,128)(2,1)} %get-tuple-element.45, bf16[16,128,128]{2,1,0:T(8,128)(2,1)} %collective-permute-done.9.refs_1_, pred[]{:T(512)S(6)} %select_n.167, pred[]{:T(512)S(6)} %ge.8, pred[]{:T(512)S(6)} %lt.10, pred[]{:T(512)S(6)} %eq.2, ...), kind=kLoop, calls=%fused_computation.15 | loop fusion | flops 3407872 | bytes 2621445 | tf_op jit(solution)/shard_map/convert_element_type | solution.py:221
  66.7 2.8 %collective-permute-start.11 = (bf16[16,128,128]{2,1,0:T(8,128)(2,1)}, bf16[16,128,128]{2,1,0:T(8,128)(2,1)}, u32[]{:S(2)}, u32[]{:S(2)}) collective-permute-start(bf16[16,128,128]{2,1,0:T(8,128)(2,1)} %get-tuple-element.68), channel_id=1, source_target_pairs={{0,8},{1,9},{2,10},{3,11},{4,12},{5,13},{6,14},{7,15},{8,0},{9,1},... | collective-permute-start | bytes 1572872 | tf_op jit(solution)/shard_map/ppermute | solution.py:402
  69.5 5.7 %collective-permute-done.14.refs_1_ = bf16[16,128,128]{2,1,0:T(8,128)(2,1)} collective-permute-done((bf16[16,128,128]{2,1,0:T(8,128)(2,1)}, bf16[16,128,128]{2,1,0:T(8,128)(2,1)}, u32[]{:S(2)}, u32[]{:S(2)}) %collective-permute-start.14) | collective-permute-done | bytes 524320 | tf_op jit(solution)/shard_map/ppermute | solution.py:402
  75.1 2.6 %fusion.7 = (bf16[16,128,128]{2,1,0:T(8,128)(2,1)}, bf16[16,128,128]{2,1,0:T(8,128)(2,1)}) fusion(bf16[16,128,128]{2,1,0:T(8,128)(2,1)S(1)} %copy-done.20, bf16[16,128,128]{2,1,0:T(8,128)(2,1)} %collective-permute-done.14.refs_1_, pred[]{:T(512)S(6)} %select_n.167, pred[]{:T(512)S(6)} %ge.8, pred[]{:T(512)S(6)} %lt.10, pred[]{:T(512)S(6)} %eq.2, ...), kind=kLoop, calls=%fused_computation.11 | loop fusion | flops 3407872 | bytes 2621445 | tf_op jit(solution)/shard_map/convert_element_type | solution.py:221
  77.7 2.8 %collective-permute-start.16 = (bf16[16,128,128]{2,1,0:T(8,128)(2,1)}, bf16[16,128,128]{2,1,0:T(8,128)(2,1)}, u32[]{:S(2)}, u32[]{:S(2)}) collective-permute-start(bf16[16,128,128]{2,1,0:T(8,128)(2,1)} %get-tuple-element.66), channel_id=1, source_target_pairs={{0,8},{1,9},{2,10},{3,11},{4,12},{5,13},{6,14},{7,15},{8,0},{9,1},... | collective-permute-start | bytes 1572872 | tf_op jit(solution)/shard_map/ppermute | solution.py:402
  80.5 5.8 %collective-permute-done.11.refs_2_ = bf16[16,128,128]{2,1,0:T(8,128)(2,1)} collective-permute-done((bf16[16,128,128]{2,1,0:T(8,128)(2,1)}, bf16[16,128,128]{2,1,0:T(8,128)(2,1)}, u32[]{:S(2)}, u32[]{:S(2)}) %collective-permute-start.11) | collective-permute-done | bytes 524320 | tf_op jit(solution)/shard_map/ppermute | solution.py:402
  86.3 2.1 %add_convert_fusion.1 = (bf16[16,128,128]{2,1,0:T(8,128)(2,1)S(1)}, bf16[16,128,128]{2,1,0:T(8,128)(2,1)S(1)}) fusion(bf16[16,128,128]{2,1,0:T(8,128)(2,1)} %collective-permute-done.11.refs_2_, bf16[16,128,128]{2,1,0:T(8,128)(2,1)} %get-tuple-element.57, bf16[16,128,128]{2,1,0:T(8,128)(2,1)} %get-tuple-element.56, pred[]{:T(512)S(6)} %ge.9, pred[]{:T(512)S(6)} %lt.11, ...), kind=kLoop, calls=%fused_computation.18 | loop fusion | flops 3670016 | bytes 3145733 | tf_op jit(solution)/shard_map/convert_element_type | solution.py:221
  88.4 2.8 %collective-permute-start.20 = (bf16[16,128,128]{2,1,0:T(8,128)(2,1)S(1)}, bf16[16,128,128]{2,1,0:T(8,128)(2,1)S(1)}, u32[]{:S(2)}, u32[]{:S(2)}) collective-permute-start(bf16[16,128,128]{2,1,0:T(8,128)(2,1)S(1)} %get-tuple-element.64), channel_id=1, source_target_pairs={{0,8},{1,9},{2,10},{3,11},{4,12},{5,13},{6,14},{7,15},{8,0},{9,1},... | collective-permute-start | bytes 1572872 | tf_op jit(solution)/shard_map/ppermute | solution.py:402
  91.2 1.0 copy-done.14
  92.3 2.4 %left_products.2 = (f32[16,64,128]{2,1,0:T(8,128)S(1)}, bf16[16,64,128]{2,1,0:T(8,128)(2,1)S(1)}) custom-call(bf16[32,128,128]{2,1,0:T(8,128)(2,1)S(1)} %copy-done.5, bf16[32,128,128]{2,1,0:T(8,128)(2,1)S(1)} %copy-done.1, bf16[16,128,128]{2,1,0:T(8,128)(2,1)} %collective-permute-done.9.refs_1_, bf16[16,128,128]{2,1,0:T(8,128)(2,1)} %collective-permute-done.11.refs_2_, ...), custom_call_target="tpu_custom_call" | custom-call | flops 1 | bytes 8000000 | tf_op jit(solution)/shard_map/left_products/pallas_call | solution.py:283
  94.6 2.9 %collective-permute-done.16.refs_2_ = bf16[16,128,128]{2,1,0:T(8,128)(2,1)} collective-permute-done((bf16[16,128,128]{2,1,0:T(8,128)(2,1)}, bf16[16,128,128]{2,1,0:T(8,128)(2,1)}, u32[]{:S(2)}, u32[]{:S(2)}) %collective-permute-start.16) | collective-permute-done | bytes 524320 | tf_op jit(solution)/shard_map/ppermute | solution.py:402
  97.6 1.7 %add_convert_fusion = (bf16[16,128,128]{2,1,0:T(8,128)(2,1)S(1)}, bf16[16,128,128]{2,1,0:T(8,128)(2,1)S(1)}) fusion(bf16[16,128,128]{2,1,0:T(8,128)(2,1)} %collective-permute-done.16.refs_2_, bf16[16,128,128]{2,1,0:T(8,128)(2,1)S(1)} %copy-done.22, bf16[16,128,128]{2,1,0:T(8,128)(2,1)S(1)} %copy-done.21, pred[]{:T(512)S(6)} %ge.9, pred[]{:T(512)S(6)} %lt.11, ...), kind=kLoop, calls=%fused_computation.17 | loop fusion | flops 3670016 | bytes 3145733 | tf_op jit(solution)/shard_map/convert_element_type | solution.py:221
  99.3 3.2 %collective-permute-start.21 = (bf16[16,128,128]{2,1,0:T(8,128)(2,1)S(1)}, bf16[16,128,128]{2,1,0:T(8,128)(2,1)S(1)}, u32[]{:S(2)}, u32[]{:S(2)}) collective-permute-start(bf16[16,128,128]{2,1,0:T(8,128)(2,1)S(1)} %get-tuple-element.62), channel_id=1, source_target_pairs={{0,8},{1,9},{2,10},{3,11},{4,12},{5,13},{6,14},{7,15},{8,0},{9,1},... | collective-permute-start | bytes 1572872 | tf_op jit(solution)/shard_map/ppermute | solution.py:402
  102.6 0.5 collective-permute-start.18
  103.1 2.4 %left_products.3 = (f32[16,64,128]{2,1,0:T(8,128)S(1)}, bf16[16,64,128]{2,1,0:T(8,128)(2,1)S(1)}) custom-call(bf16[32,128,128]{2,1,0:T(8,128)(2,1)S(1)} %copy-done.5, bf16[32,128,128]{2,1,0:T(8,128)(2,1)S(1)} %copy-done.1, bf16[16,128,128]{2,1,0:T(8,128)(2,1)} %collective-permute-done.14.refs_1_, bf16[16,128,128]{2,1,0:T(8,128)(2,1)} %collective-permute-done.16.refs_2_, ...), custom_call_target="tpu_custom_call" | custom-call | flops 1 | bytes 8000000 | tf_op jit(solution)/shard_map/left_products/pallas_call | solution.py:283
  105.6 3.2 %collective-permute-done.20.refs_6_ = bf16[16,128,128]{2,1,0:T(8,128)(2,1)S(1)} collective-permute-done((bf16[16,128,128]{2,1,0:T(8,128)(2,1)S(1)}, bf16[16,128,128]{2,1,0:T(8,128)(2,1)S(1)}, u32[]{:S(2)}, u32[]{:S(2)}) %collective-permute-start.20) | collective-permute-done | bytes 524320 | tf_op jit(solution)/shard_map/ppermute | solution.py:402
  108.7 0.1 add_convert_fusion.5
  108.9 0.6 collective-permute-start.24
  109.4 7.5 %collective-permute-done.21.refs_7_ = bf16[16,128,128]{2,1,0:T(8,128)(2,1)S(1)} collective-permute-done((bf16[16,128,128]{2,1,0:T(8,128)(2,1)S(1)}, bf16[16,128,128]{2,1,0:T(8,128)(2,1)S(1)}, u32[]{:S(2)}, u32[]{:S(2)}) %collective-permute-start.21) | collective-permute-done | bytes 524320 | tf_op jit(solution)/shard_map/ppermute | solution.py:402
  117.2 1.5 %collective-permute-done.25.refs_11_ = bf16[16,64,128]{2,1,0:T(8,128)(2,1)S(1)} collective-permute-done((bf16[16,64,128]{2,1,0:T(8,128)(2,1)S(1)}, bf16[16,64,128]{2,1,0:T(8,128)(2,1)S(1)}, u32[]{:S(2)}, u32[]{:S(2)}) %collective-permute-start.25) | collective-permute-done | bytes 262176 | tf_op jit(solution)/shard_map/ppermute | solution.py:394
  118.8 8.3 %tail.1 = bf16[128,64,128]{2,1,0:T(8,128)(2,1)} custom-call(bf16[64,128,128]{2,1,0:T(8,128)(2,1)S(1)} %copy-done.10, f32[64,1,128]{2,1,0:T(1,128)S(1)} %get-tuple-element.38.inverse, bf16[64,256,128]{2,1,0:T(8,128)(2,1)S(1)} %copy-done.7, f32[1,128]{1,0:T(1,128)S(1)} %bitcast.8, bf16[128,256]{1,0:T(8,128)(2,1)S(1)} %copy-done.17, ...), custom_call_target="tpu_custom_call" | custom-call | flops 1 | bytes 8000000 | tf_op jit(solution)/shard_map/tail/pallas_call | solution.py:356
  (68 shorter events, 0.6 us)
Async XLA Ops:
  0.0 9.2 %copy-start.18 = (s32[4,4]{1,0:T(4,128)S(1)}, s32[4,4]{1,0:T(4,128)}, u32[]{:S(2)}) copy-start(s32[4,4]{1,0:T(4,128)} %mask.3) | copy-start | bytes 196
  1.1 2.1 %collective-permute-start = (bf16[64,32,128]{2,1,0:T(8,128)(2,1)S(1)}, bf16[64,32,128]{2,1,0:T(8,128)(2,1)S(1)}, u32[]{:S(2)}, u32[]{:S(2)}) collective-permute-start(bf16[64,32,128]{2,1,0:T(8,128)(2,1)S(1)} %dynamic-slice_bitcast_fusion), channel_id=1, source_target_pairs={{0,1},{1,0},{2,3},{3,2},{4,5},{5,4},{6,7},{7,6},{8,9},{9,8},{10,11... | collective-permute-start | bytes 1572872 | tf_op jit(solution)/shard_map/ppermute | solution.py:394
  3.2 1.2 copy-start.8
  4.8 26.4 %collective-permute-start.6 = (bf16[32,128,128]{2,1,0:T(8,128)(2,1)S(1)}, bf16[32,128,128]{2,1,0:T(8,128)(2,1)S(1)}, u32[]{:S(2)}, u32[]{:S(2)}) collective-permute-start(bf16[32,128,128]{2,1,0:T(8,128)(2,1)S(1)} %pack.1.refs_0_.refs_6_), channel_id=1, source_target_pairs={{0,2},{1,3},{2,0},{3,1},{4,6},{5,7},{6,4},{7,5},{8,10},{9,11},{10,... | collective-permute-start | bytes 3145736 | tf_op jit(solution)/shard_map/ppermute | solution.py:394
  7.7 24.9 %collective-permute-start.7 = (bf16[32,128,128]{2,1,0:T(8,128)(2,1)S(1)}, bf16[32,128,128]{2,1,0:T(8,128)(2,1)S(1)}, u32[]{:S(2)}, u32[]{:S(2)}) collective-permute-start(bf16[32,128,128]{2,1,0:T(8,128)(2,1)S(1)} %pack.1.refs_0_.refs_6_), channel_id=1, source_target_pairs={{0,4},{1,5},{2,6},{3,7},{4,0},{5,1},{6,2},{7,3},{8,12},{9,13},{10,... | collective-permute-start | bytes 3145736 | tf_op jit(solution)/shard_map/ppermute | solution.py:394
  14.4 1.6 %collective-permute-start.2 = (bf16[16,64,128]{2,1,0:T(8,128)(2,1)S(1)}, bf16[16,64,128]{2,1,0:T(8,128)(2,1)S(1)}, u32[]{:S(2)}, u32[]{:S(2)}) collective-permute-start(bf16[16,64,128]{2,1,0:T(8,128)(2,1)S(1)} %get-tuple-element.70), channel_id=1, source_target_pairs={{0,1},{1,0},{2,3},{3,2},{4,5},{5,4},{6,7},{7,6},{8,9},{9,8},{10,11... | collective-permute-start | bytes 786440 | tf_op jit(solution)/shard_map/ppermute | solution.py:394
  14.5 1.9 %collective-permute-start.1 = (bf16[16,64,128]{2,1,0:T(8,128)(2,1)S(1)}, bf16[16,64,128]{2,1,0:T(8,128)(2,1)S(1)}, u32[]{:S(2)}, u32[]{:S(2)}) collective-permute-start(bf16[16,64,128]{2,1,0:T(8,128)(2,1)S(1)} %get-tuple-element.69), channel_id=1, source_target_pairs={{0,1},{1,0},{2,3},{3,2},{4,5},{5,4},{6,7},{7,6},{8,9},{9,8},{10,11... | collective-permute-start | bytes 786440 | tf_op jit(solution)/shard_map/ppermute | solution.py:394
  16.5 16.2 %copy-start.4 = (bf16[32,128,128]{2,1,0:T(8,128)(2,1)}, bf16[32,128,128]{2,1,0:T(8,128)(2,1)S(1)}, u32[]{:S(2)}) copy-start(bf16[32,128,128]{2,1,0:T(8,128)(2,1)S(1)} %maximum_maximum_fusion.own) | copy-start | bytes 3145732
  16.5 25.3 %collective-permute-start.3 = (bf16[32,128,128]{2,1,0:T(8,128)(2,1)S(1)}, bf16[32,128,128]{2,1,0:T(8,128)(2,1)S(1)}, u32[]{:S(2)}, u32[]{:S(2)}) collective-permute-start(bf16[32,128,128]{2,1,0:T(8,128)(2,1)S(1)} %maximum_maximum_fusion.own), channel_id=1, source_target_pairs={{0,8},{1,9},{2,10},{3,11},{4,12},{5,13},{6,14},{7,15},{8,0},{9,1},... | collective-permute-start | bytes 3145736 | tf_op jit(solution)/shard_map/ppermute | solution.py:402
  18.1 23.6 %collective-permute-start.5 = (bf16[32,128,128]{2,1,0:T(8,128)(2,1)S(1)}, bf16[32,128,128]{2,1,0:T(8,128)(2,1)S(1)}, u32[]{:S(2)}, u32[]{:S(2)}) collective-permute-start(bf16[32,128,128]{2,1,0:T(8,128)(2,1)S(1)} %maximum_maximum_fusion.own), channel_id=1, source_target_pairs={{0,1},{1,0},{2,3},{3,2},{4,5},{5,4},{6,7},{7,6},{8,16},{9,17},{10,... | collective-permute-start | bytes 3145736 | tf_op jit(solution)/shard_map/ppermute | solution.py:402
  23.9 2.0 %copy-start.6 = (bf16[64,256,128]{2,1,0:T(8,128)(2,1)}, bf16[64,256,128]{2,1,0:T(8,128)(2,1)S(1)}, u32[]{:S(2)}) copy-start(bf16[64,256,128]{2,1,0:T(8,128)(2,1)S(1)} %get-tuple-element.39.factors) | copy-start | bytes 12582916
  25.9 1.3 %copy-start.9 = (bf16[64,128,128]{2,1,0:T(8,128)(2,1)}, bf16[64,128,128]{2,1,0:T(8,128)(2,1)S(1)}, u32[]{:S(2)}) copy-start(bf16[64,128,128]{2,1,0:T(8,128)(2,1)S(1)} %get-tuple-element.37.scaled) | copy-start | bytes 6291460
  27.2 7.6 %collective-permute-start.4 = (bf16[32,64,128]{2,1,0:T(8,128)(2,1)S(1)}, bf16[32,64,128]{2,1,0:T(8,128)(2,1)S(1)}, u32[]{:S(2)}, u32[]{:S(2)}) collective-permute-start(bf16[32,64,128]{2,1,0:T(8,128)(2,1)S(1)} %get-tuple-element.41), channel_id=1, source_target_pairs={{0,1},{1,0},{2,3},{3,2},{4,5},{5,4},{6,7},{7,6},{8,9},{9,8},{10,11... | collective-permute-start | bytes 1572872 | tf_op jit(solution)/shard_map/ppermute | solution.py:394
  32.7 12.9 %collective-permute-start.8 = (bf16[16,128,128]{2,1,0:T(8,128)(2,1)S(1)}, bf16[16,128,128]{2,1,0:T(8,128)(2,1)S(1)}, u32[]{:S(2)}, u32[]{:S(2)}) collective-permute-start(bf16[16,128,128]{2,1,0:T(8,128)(2,1)S(1)} %get-tuple-element.42), channel_id=1, source_target_pairs={{0,4},{1,5},{2,6},{3,7},{4,0},{5,1},{6,2},{7,3},{8,12},{9,13},{10,... | collective-permute-start | bytes 1572872 | tf_op jit(solution)/shard_map/ppermute | solution.py:394
  34.3 16.0 %collective-permute-start.13 = (bf16[16,128,128]{2,1,0:T(8,128)(2,1)S(1)}, bf16[16,128,128]{2,1,0:T(8,128)(2,1)S(1)}, u32[]{:S(2)}, u32[]{:S(2)}) collective-permute-start(bf16[16,128,128]{2,1,0:T(8,128)(2,1)S(1)} %get-tuple-element.47), channel_id=1, source_target_pairs={{0,2},{1,3},{2,0},{3,1},{4,6},{5,7},{6,4},{7,5},{8,10},{9,11},{10,... | collective-permute-start | bytes 1572872 | tf_op jit(solution)/shard_map/ppermute | solution.py:394
  41.8 8.5 %copy-start = (bf16[32,128,128]{2,1,0:T(8,128)(2,1)}, bf16[32,128,128]{2,1,0:T(8,128)(2,1)S(1)}, u32[]{:S(2)}) copy-start(bf16[32,128,128]{2,1,0:T(8,128)(2,1)S(1)} %collective-permute-done.3.by_a.refs_0_) | copy-start | bytes 3145732
  41.8 8.5 %copy-start.2 = (bf16[32,128,128]{2,1,0:T(8,128)(2,1)}, bf16[32,128,128]{2,1,0:T(8,128)(2,1)S(1)}, u32[]{:S(2)}) copy-start(bf16[32,128,128]{2,1,0:T(8,128)(2,1)S(1)} %collective-permute-done.5.by_b.refs_3_) | copy-start | bytes 3145732
  45.6 3.1 %copy-start.13 = (bf16[16,128,128]{2,1,0:T(8,128)(2,1)}, bf16[16,128,128]{2,1,0:T(8,128)(2,1)S(1)}, u32[]{:S(2)}) copy-start(bf16[16,128,128]{2,1,0:T(8,128)(2,1)S(1)} %collective-permute-done.8.refs_3_.refs_9_) | copy-start | bytes 1572868
  48.7 15.2 %collective-permute-start.9 = (bf16[16,128,128]{2,1,0:T(8,128)(2,1)}, bf16[16,128,128]{2,1,0:T(8,128)(2,1)}, u32[]{:S(2)}, u32[]{:S(2)}) collective-permute-start(bf16[16,128,128]{2,1,0:T(8,128)(2,1)} %get-tuple-element.43), channel_id=1, source_target_pairs={{0,8},{1,9},{2,10},{3,11},{4,12},{5,13},{6,14},{7,15},{8,0},{9,1},... | collective-permute-start | bytes 1572872 | tf_op jit(solution)/shard_map/ppermute | solution.py:402
  50.3 13.6 %collective-permute-start.10 = (bf16[16,128,128]{2,1,0:T(8,128)(2,1)}, bf16[16,128,128]{2,1,0:T(8,128)(2,1)}, u32[]{:S(2)}, u32[]{:S(2)}) collective-permute-start(bf16[16,128,128]{2,1,0:T(8,128)(2,1)} %get-tuple-element.44), channel_id=1, source_target_pairs={{0,1},{1,0},{2,3},{3,2},{4,5},{5,4},{6,7},{7,6},{8,16},{9,17},{10,... | collective-permute-start | bytes 1572872 | tf_op jit(solution)/shard_map/ppermute | solution.py:402
  50.3 3.1 %copy-start.11 = (bf16[16,128,128]{2,1,0:T(8,128)(2,1)}, bf16[16,128,128]{2,1,0:T(8,128)(2,1)S(1)}, u32[]{:S(2)}) copy-start(bf16[16,128,128]{2,1,0:T(8,128)(2,1)S(1)} %collective-permute-done.13.refs_3_.refs_9_) | copy-start | bytes 1572868
  53.4 21.7 %collective-permute-start.14 = (bf16[16,128,128]{2,1,0:T(8,128)(2,1)}, bf16[16,128,128]{2,1,0:T(8,128)(2,1)}, u32[]{:S(2)}, u32[]{:S(2)}) collective-permute-start(bf16[16,128,128]{2,1,0:T(8,128)(2,1)} %get-tuple-element.48), channel_id=1, source_target_pairs={{0,8},{1,9},{2,10},{3,11},{4,12},{5,13},{6,14},{7,15},{8,0},{9,1},... | collective-permute-start | bytes 1572872 | tf_op jit(solution)/shard_map/ppermute | solution.py:402
  56.6 18.5 %collective-permute-start.15 = (bf16[16,128,128]{2,1,0:T(8,128)(2,1)}, bf16[16,128,128]{2,1,0:T(8,128)(2,1)}, u32[]{:S(2)}, u32[]{:S(2)}) collective-permute-start(bf16[16,128,128]{2,1,0:T(8,128)(2,1)} %get-tuple-element.49), channel_id=1, source_target_pairs={{0,1},{1,0},{2,3},{3,2},{4,5},{5,4},{6,7},{7,6},{8,16},{9,17},{10,... | collective-permute-start | bytes 1572872 | tf_op jit(solution)/shard_map/ppermute | solution.py:402
  56.6 18.5 %copy-start.20 = (bf16[16,128,128]{2,1,0:T(8,128)(2,1)S(1)}, bf16[16,128,128]{2,1,0:T(8,128)(2,1)}, u32[]{:S(2)}) copy-start(bf16[16,128,128]{2,1,0:T(8,128)(2,1)} %get-tuple-element.50) | copy-start | bytes 1572868
  66.7 19.6 %collective-permute-start.11 = (bf16[16,128,128]{2,1,0:T(8,128)(2,1)}, bf16[16,128,128]{2,1,0:T(8,128)(2,1)}, u32[]{:S(2)}, u32[]{:S(2)}) collective-permute-start(bf16[16,128,128]{2,1,0:T(8,128)(2,1)} %get-tuple-element.68), channel_id=1, source_target_pairs={{0,8},{1,9},{2,10},{3,11},{4,12},{5,13},{6,14},{7,15},{8,0},{9,1},... | collective-permute-start | bytes 1572872 | tf_op jit(solution)/shard_map/ppermute | solution.py:402
  69.5 16.9 %collective-permute-start.12 = (bf16[16,128,128]{2,1,0:T(8,128)(2,1)}, bf16[16,128,128]{2,1,0:T(8,128)(2,1)}, u32[]{:S(2)}, u32[]{:S(2)}) collective-permute-start(bf16[16,128,128]{2,1,0:T(8,128)(2,1)} %get-tuple-element.67), channel_id=1, source_target_pairs={{0,1},{1,0},{2,3},{3,2},{4,5},{5,4},{6,7},{7,6},{8,16},{9,17},{10,... | collective-permute-start | bytes 1572872 | tf_op jit(solution)/shard_map/ppermute | solution.py:402
  77.7 19.8 %collective-permute-start.16 = (bf16[16,128,128]{2,1,0:T(8,128)(2,1)}, bf16[16,128,128]{2,1,0:T(8,128)(2,1)}, u32[]{:S(2)}, u32[]{:S(2)}) collective-permute-start(bf16[16,128,128]{2,1,0:T(8,128)(2,1)} %get-tuple-element.66), channel_id=1, source_target_pairs={{0,8},{1,9},{2,10},{3,11},{4,12},{5,13},{6,14},{7,15},{8,0},{9,1},... | collective-permute-start | bytes 1572872 | tf_op jit(solution)/shard_map/ppermute | solution.py:402
  80.5 17.1 %collective-permute-start.17 = (bf16[16,128,128]{2,1,0:T(8,128)(2,1)}, bf16[16,128,128]{2,1,0:T(8,128)(2,1)}, u32[]{:S(2)}, u32[]{:S(2)}) collective-permute-start(bf16[16,128,128]{2,1,0:T(8,128)(2,1)} %get-tuple-element.65), channel_id=1, source_target_pairs={{0,1},{1,0},{2,3},{3,2},{4,5},{5,4},{6,7},{7,6},{8,16},{9,17},{10,... | collective-permute-start | bytes 1572872 | tf_op jit(solution)/shard_map/ppermute | solution.py:402
  80.5 10.7 %copy-start.1 = (bf16[32,128,128]{2,1,0:T(8,128)(2,1)S(1)}, bf16[32,128,128]{2,1,0:T(8,128)(2,1)}, u32[]{:S(2)}) copy-start(bf16[32,128,128]{2,1,0:T(8,128)(2,1)} %copy-done) | copy-start | bytes 3145732
  80.5 10.7 %copy-start.3 = (bf16[32,128,128]{2,1,0:T(8,128)(2,1)S(1)}, bf16[32,128,128]{2,1,0:T(8,128)(2,1)}, u32[]{:S(2)}) copy-start(bf16[32,128,128]{2,1,0:T(8,128)(2,1)} %copy-done.2) | copy-start | bytes 3145732
  80.5 10.7 %copy-start.5 = (bf16[32,128,128]{2,1,0:T(8,128)(2,1)S(1)}, bf16[32,128,128]{2,1,0:T(8,128)(2,1)}, u32[]{:S(2)}) copy-start(bf16[32,128,128]{2,1,0:T(8,128)(2,1)} %copy-done.4) | copy-start | bytes 3145732
  88.4 20.3 %collective-permute-start.20 = (bf16[16,128,128]{2,1,0:T(8,128)(2,1)S(1)}, bf16[16,128,128]{2,1,0:T(8,128)(2,1)S(1)}, u32[]{:S(2)}, u32[]{:S(2)}) collective-permute-start(bf16[16,128,128]{2,1,0:T(8,128)(2,1)S(1)} %get-tuple-element.64), channel_id=1, source_target_pairs={{0,8},{1,9},{2,10},{3,11},{4,12},{5,13},{6,14},{7,15},{8,0},{9,1},... | collective-permute-start | bytes 1572872 | tf_op jit(solution)/shard_map/ppermute | solution.py:402
  92.3 5.3 %copy-start.21 = (bf16[16,128,128]{2,1,0:T(8,128)(2,1)S(1)}, bf16[16,128,128]{2,1,0:T(8,128)(2,1)}, u32[]{:S(2)}) copy-start(bf16[16,128,128]{2,1,0:T(8,128)(2,1)} %get-tuple-element.58) | copy-start | bytes 1572868
  92.3 5.3 %copy-start.22 = (bf16[16,128,128]{2,1,0:T(8,128)(2,1)S(1)}, bf16[16,128,128]{2,1,0:T(8,128)(2,1)}, u32[]{:S(2)}) copy-start(bf16[16,128,128]{2,1,0:T(8,128)(2,1)} %get-tuple-element.59) | copy-start | bytes 1572868
  94.6 8.5 %copy-start.12 = (bf16[16,128,128]{2,1,0:T(8,128)(2,1)S(1)}, bf16[16,128,128]{2,1,0:T(8,128)(2,1)}, u32[]{:S(2)}) copy-start(bf16[16,128,128]{2,1,0:T(8,128)(2,1)} %copy-done.11) | copy-start | bytes 1572868
  97.6 11.1 %collective-permute-start.22 = (bf16[16,128,128]{2,1,0:T(8,128)(2,1)S(1)}, bf16[16,128,128]{2,1,0:T(8,128)(2,1)S(1)}, u32[]{:S(2)}, u32[]{:S(2)}) collective-permute-start(bf16[16,128,128]{2,1,0:T(8,128)(2,1)S(1)} %get-tuple-element.63), channel_id=1, source_target_pairs={{0,1},{1,0},{2,3},{3,2},{4,5},{5,4},{6,7},{7,6},{8,16},{9,17},{10,... | collective-permute-start | bytes 1572872 | tf_op jit(solution)/shard_map/ppermute | solution.py:402
  99.3 17.6 %collective-permute-start.21 = (bf16[16,128,128]{2,1,0:T(8,128)(2,1)S(1)}, bf16[16,128,128]{2,1,0:T(8,128)(2,1)S(1)}, u32[]{:S(2)}, u32[]{:S(2)}) collective-permute-start(bf16[16,128,128]{2,1,0:T(8,128)(2,1)S(1)} %get-tuple-element.62), channel_id=1, source_target_pairs={{0,8},{1,9},{2,10},{3,11},{4,12},{5,13},{6,14},{7,15},{8,0},{9,1},... | collective-permute-start | bytes 1572872 | tf_op jit(solution)/shard_map/ppermute | solution.py:402
  102.6 6.1 %copy-start.15 = (bf16[16,128,128]{2,1,0:T(8,128)(2,1)S(1)}, bf16[16,128,128]{2,1,0:T(8,128)(2,1)}, u32[]{:S(2)}) copy-start(bf16[16,128,128]{2,1,0:T(8,128)(2,1)} %get-tuple-element.54.refs_4_) | copy-start | bytes 1572868
  102.6 14.4 %copy-start.16 = (bf16[16,128,128]{2,1,0:T(8,128)(2,1)S(1)}, bf16[16,128,128]{2,1,0:T(8,128)(2,1)}, u32[]{:S(2)}) copy-start(bf16[16,128,128]{2,1,0:T(8,128)(2,1)} %get-tuple-element.55.refs_5_) | copy-start | bytes 1572868
  102.6 14.4 %collective-permute-start.23 = (bf16[16,128,128]{2,1,0:T(8,128)(2,1)S(1)}, bf16[16,128,128]{2,1,0:T(8,128)(2,1)S(1)}, u32[]{:S(2)}, u32[]{:S(2)}) collective-permute-start(bf16[16,128,128]{2,1,0:T(8,128)(2,1)S(1)} %get-tuple-element.61), channel_id=1, source_target_pairs={{0,1},{1,0},{2,3},{3,2},{4,5},{5,4},{6,7},{7,6},{8,16},{9,17},{10,... | collective-permute-start | bytes 1572872 | tf_op jit(solution)/shard_map/ppermute | solution.py:402
  102.6 14.6 %collective-permute-start.18 = (bf16[16,64,128]{2,1,0:T(8,128)(2,1)S(1)}, bf16[16,64,128]{2,1,0:T(8,128)(2,1)S(1)}, u32[]{:S(2)}, u32[]{:S(2)}) collective-permute-start(bf16[16,64,128]{2,1,0:T(8,128)(2,1)S(1)} %get-tuple-element.52), channel_id=1, source_target_pairs={{0,1},{1,0},{2,3},{3,2},{4,5},{5,4},{6,7},{7,6},{8,9},{9,8},{10,11... | collective-permute-start | bytes 786440 | tf_op jit(solution)/shard_map/ppermute | solution.py:394
  103.1 15.6 %copy-start.7 = (bf16[64,256,128]{2,1,0:T(8,128)(2,1)S(1)}, bf16[64,256,128]{2,1,0:T(8,128)(2,1)}, u32[]{:S(2)}) copy-start(bf16[64,256,128]{2,1,0:T(8,128)(2,1)} %copy-done.6) | copy-start | bytes 12582916
  103.1 15.6 %copy-start.17 = (bf16[128,256]{1,0:T(8,128)(2,1)S(1)}, bf16[128,256]{1,0:T(8,128)(2,1)}, u32[]{:S(2)}) copy-start(bf16[128,256]{1,0:T(8,128)(2,1)} %weight.5) | copy-start | bytes 196612
  105.5 13.2 %copy-start.10 = (bf16[64,128,128]{2,1,0:T(8,128)(2,1)S(1)}, bf16[64,128,128]{2,1,0:T(8,128)(2,1)}, u32[]{:S(2)}) copy-start(bf16[64,128,128]{2,1,0:T(8,128)(2,1)} %copy-done.9) | copy-start | bytes 6291460
  105.5 13.2 %copy-start.19 = (f32[128]{0:T(128)S(1)}, f32[128]{0:T(128)}, u32[]{:S(2)}) copy-start(f32[128]{0:T(128)} %param.8) | copy-start | bytes 1540
  108.7 8.5 %collective-permute-start.19 = (bf16[16,64,128]{2,1,0:T(8,128)(2,1)S(1)}, bf16[16,64,128]{2,1,0:T(8,128)(2,1)S(1)}, u32[]{:S(2)}, u32[]{:S(2)}) collective-permute-start(bf16[16,64,128]{2,1,0:T(8,128)(2,1)S(1)} %get-tuple-element.53), channel_id=1, source_target_pairs={{0,1},{1,0},{2,3},{3,2},{4,5},{5,4},{6,7},{7,6},{8,9},{9,8},{10,11... | collective-permute-start | bytes 786440 | tf_op jit(solution)/shard_map/ppermute | solution.py:394
  108.9 8.4 %collective-permute-start.24 = (bf16[16,64,128]{2,1,0:T(8,128)(2,1)S(1)}, bf16[16,64,128]{2,1,0:T(8,128)(2,1)S(1)}, u32[]{:S(2)}, u32[]{:S(2)}) collective-permute-start(bf16[16,64,128]{2,1,0:T(8,128)(2,1)S(1)} %add_convert_fusion.5), channel_id=1, source_target_pairs={{0,1},{1,0},{2,3},{3,2},{4,5},{5,4},{6,7},{7,6},{8,9},{9,8},{10,11... | collective-permute-start | bytes 786440 | tf_op jit(solution)/shard_map/ppermute | solution.py:394
  117.1 1.6 %collective-permute-start.25 = (bf16[16,64,128]{2,1,0:T(8,128)(2,1)S(1)}, bf16[16,64,128]{2,1,0:T(8,128)(2,1)S(1)}, u32[]{:S(2)}, u32[]{:S(2)}) collective-permute-start(bf16[16,64,128]{2,1,0:T(8,128)(2,1)S(1)} %add_convert_fusion.4), channel_id=1, source_target_pairs={{0,1},{1,0},{2,3},{3,2},{4,5},{5,4},{6,7},{7,6},{8,9},{9,8},{10,11... | collective-permute-start | bytes 786440 | tf_op jit(solution)/shard_map/ppermute | solution.py:394
  (1 other events, 1.0 us)

commit v8 on v7

--- a/solution.py
+++ b/solution.py
@@ -90,8 +90,13 @@
     split_channels(acts, whole, mine, theirs)
 
 
+def last_rows(hidden):
+    part = hidden // CORES // CHUNKS
+    return [((2 + kind) * hidden + (core * CHUNKS + CHUNKS - 1) * part, part) for kind in range(2) for core in range(CORES)]
+
+
 def left_forward_kernel(
-    mask, pair, gain, bias, weight, mine, theirs, scaled_out, inverse_out, factors,
+    mask, pair, gain, bias, weight, mine, theirs, scaled_out, inverse_out, factors, last,
     flipped, turned, normed, acts, whole, gain_col, bias_col, weight_t,
 ):
     rows, keys, _ = pair.shape
@@ -113,6 +118,8 @@
                 acts[key] = act.astype(jnp.bfloat16)
             factors[key, first : first + hidden, :] = masked.astype(jnp.bfloat16)
             factors[key, first + hidden : first + 2 * hidden, :] = (act * (1.0 - sig)).astype(jnp.bfloat16)
+    for i, (first, size) in enumerate(last_rows(hidden)):
+        last[:, i * size : (i + 1) * size, :] = factors[:, first : first + size, :]
     split_channels(acts, whole, mine, theirs)
 
 
@@ -131,8 +138,9 @@
             jax.ShapeDtypeStruct((cols, chans, rows), jnp.bfloat16),
             jax.ShapeDtypeStruct((cols, 1, rows), jnp.float32),
             jax.ShapeDtypeStruct((cols, width, rows), jnp.bfloat16),
+            jax.ShapeDtypeStruct((cols, 2 * hidden // CHUNKS, rows), jnp.bfloat16),
         ]
-        out_specs += [by_key(chans, rows), by_key(1, rows), by_key(width, rows)]
+        out_specs += [by_key(chans, rows), by_key(1, rows), by_key(width, rows), by_key(2 * hidden // CHUNKS, rows)]
     return pl.pallas_call(
         right_kernel if right else left_forward_kernel,
         out_shape=out_shape,
@@ -161,11 +169,14 @@
     )(tile_mask, *in_hbm(pair, gain, bias, proj_weight))
 
 
-def pack_kernel(own, other, out):
+def pack_kernel(own, other, out, mine, sem):
     cols, half, _ = other.shape
     core = this_core()
-    for block, place in ((own[:, pl.ds(pl.multiple_of(core * half, half), half), :], core), (other[...], 1 - core)):
-        out[:, pl.ds(pl.multiple_of(place * cols, cols), cols), :] = jnp.transpose(block, (1, 0, 2))
+    copy = pltpu.make_async_copy(own.at[:, pl.ds(pl.multiple_of(core * half, half), half), :], mine, sem)
+    copy.start()
+    out[:, pl.ds(pl.multiple_of((1 - core) * cols, cols), cols), :] = jnp.transpose(other[...], (1, 0, 2))
+    copy.wait()
+    out[:, pl.ds(pl.multiple_of(core * cols, cols), cols), :] = jnp.transpose(mine[...], (1, 0, 2))
 
 
 def pack(own, other):
@@ -173,10 +184,12 @@
     return pl.pallas_call(
         pack_kernel,
         out_shape=jax.ShapeDtypeStruct((half, CORES * cols, rows), jnp.bfloat16),
+        in_specs=[pl.BlockSpec(memory_space=pl.ANY), pl.BlockSpec(memory_space=pltpu.VMEM)],
+        scratch_shapes=[pltpu.VMEM((cols, half, rows), jnp.bfloat16), pltpu.SemaphoreType.DMA],
         compiler_params=PARAMS,
         cost_estimate=COST,
         name="pack",
-    )(own, other)
+    )(*in_hbm(own), other)
 
 
 def chunk_spec(array, chans, chunk):
@@ -302,39 +315,89 @@
     return total + jnp.where(use_b, by_b.astype(jnp.float32), 0.0)
 
 
-def tail_kernel(n, scaled, inverse, factors, gain, weight, *refs):
-    groups = [refs[i * CHUNKS : (i + 1) * CHUNKS] for i in range(6)]
-    left_mine, left_other, partials, by_a, by_b, right_other = groups
-    out, results, flipped, grads, right_flat, left_flat, gain_col = refs[6 * CHUNKS :]
+def put(flat, owner, value):
+    size = value.shape[0] * value.shape[1]
+    flat[pl.ds(pl.multiple_of(owner * size, size), size), :] = value.astype(jnp.float32).reshape(size, value.shape[2])
+
+
+def known_kernel(n, factors, weight, *refs):
+    known = CHUNKS - 1
+    left_mine, left_other = refs[:CHUNKS], refs[CHUNKS : 2 * CHUNKS]
+    partials, by_a, by_b, right_other = (refs[2 * CHUNKS + i * known : 2 * CHUNKS + (i + 1) * known] for i in range(4))
+    out, grads, *flats = refs[2 * CHUNKS + 4 * known :]
+    keys, width, _ = factors.shape
+    hidden = width // 4
+    part = hidden // CORES // CHUNKS
+    core = this_core()
+
+    @pl.when(pl.program_id(0) == 0)
+    def _():
+        grads[...] = jnp.zeros_like(grads)
+
+    for chunk in range(CHUNKS):
+        put(flats[chunk], core, left_mine[chunk][...])
+        put(flats[chunk], 1 - core, left_other[chunk][...])
+    for chunk in range(known):
+        put(flats[CHUNKS + chunk], core, arrived_total(partials[chunk][...], by_a[chunk][...], by_b[chunk][...], n))
+        put(flats[CHUNKS + chunk], 1 - core, right_other[chunk][...])
+    for key in range(keys):
+        for i, flat in enumerate(flats):
+            side, chunk = divmod(i, CHUNKS)
+            grad = flat[pl.ds(key, CORES * part, stride=keys), :]
+            for owner in range(CORES):
+                for kind in range(2):
+                    first = (2 * side + kind) * hidden + (owner * CHUNKS + chunk) * part
+                    place = slice(first, first + part)
+                    factor = factors[key, place, :].astype(jnp.float32)
+                    grads[key, place, :] = (grad[owner * part : (owner + 1) * part] * factor).astype(jnp.bfloat16)
+    for key in range(keys):
+        out[key] = jnp.dot(weight[...], grads[key], preferred_element_type=jnp.float32)
+
+
+def known(factors, proj_weight, left_mine, left_other, partials, by_a, by_b, right_other):
+    cols, width, rows = factors.shape
+    chans, hidden = proj_weight.shape[0], width // 4
+    part = hidden // CORES // CHUNKS
+    by_key = lambda *shape: pl.BlockSpec((KEYS,) + shape, lambda g: (g, 0, 0))
+    args = (*left_mine, *left_other, *partials, *by_a, *by_b, *right_other)
+    return pl.pallas_call(
+        functools.partial(known_kernel, lax.axis_size("row")),
+        out_shape=jax.ShapeDtypeStruct((cols, chans, rows), jnp.float32),
+        grid=(cols // KEYS,),
+        in_specs=[by_key(width, rows), pl.BlockSpec((chans, width), lambda g: (0, 0))]
+        + [pl.BlockSpec((part, KEYS, rows), lambda g: (0, g, 0))] * len(args),
+        out_specs=by_key(chans, rows),
+        scratch_shapes=[pltpu.VMEM((KEYS, width, rows), jnp.bfloat16)]
+        + [pltpu.VMEM((CORES * part * KEYS, rows), jnp.float32)] * (2 * CHUNKS - 1),
+        compiler_params=PARAMS,
+        cost_estimate=COST,
+        name="known",
+    )(factors, proj_weight, *args)
+
+
+def tail_kernel(n, base, scaled, inverse, last, gain, weight, partials, by_a, by_b, right_other, out, results, flipped, grads, flat, gain_col):
     keys, chans, rows = scaled.shape
     hidden = weight.shape[1] // 4
-    half = hidden // CORES
-    part = half // CHUNKS
     core = this_core()
 
     @pl.when(pl.program_id(0) == 0)
     def _():
         gain_col[...] = column(gain, rows)
-
-    def put(flat, owner, chunk, value):
-        first = pl.multiple_of((owner * half + chunk * part) * keys, part * keys)
-        flat[pl.ds(first, part * keys), :] = value.astype(jnp.float32).reshape(part * keys, rows)
-
-    for chunk in range(CHUNKS):
-        total = arrived_total(partials[chunk][...], by_a[chunk][...], by_b[chunk][...], n)
-        put(right_flat, core, chunk, total)
-        put(right_flat, 1 - core, chunk, right_other[chunk][...])
-        put(left_flat, core, chunk, left_mine[chunk][...])
-        put(left_flat, 1 - core, chunk, left_other[chunk][...])
-    for key in range(keys):
-        for side, source in enumerate((left_flat, right_flat)):
-            grad = source[pl.ds(key, hidden, stride=keys), :]
-            for i in (2 * side, 2 * side + 1):
-                place = slice(i * hidden, (i + 1) * hidden)
-                grads[key, place, :] = (grad * factors[key, place, :].astype(jnp.float32)).astype(jnp.bfloat16)
+        grads[...] = jnp.zeros_like(grads)
+
+    put(flat, core, arrived_total(partials[...], by_a[...], by_b[...], n))
+    put(flat, 1 - core, right_other[...])
+    places = last_rows(hidden)
+    for key in range(keys):
+        grad = flat[pl.ds(key, 2 * hidden // len(places) // CHUNKS * CORES, stride=keys), :]
+        for i, (first, size) in enumerate(places):
+            factor = last[key, i * size : (i + 1) * size, :].astype(jnp.float32)
+            owner = i % CORES
+            grads[key, first : first + size, :] = (grad[owner * size : (owner + 1) * size] * factor).astype(jnp.bfloat16)
     for key in range(keys):
         scaled_key = scaled[key].astype(jnp.float32)
-        scaled_grad = jnp.dot(weight[...], grads[key], preferred_element_type=jnp.float32) * gain_col[...]
+        added = jnp.dot(weight[...], grads[key], preferred_element_type=jnp.float32)
+        scaled_grad = (base[key] + added) * gain_col[...]
         result = inverse[key] * (
             scaled_grad
             - jnp.mean(scaled_grad, axis=0, keepdims=True)
@@ -347,11 +410,10 @@
     out[...] = jnp.transpose(flipped[...], (1, 0, 2))
 
 
-def tail(scaled, inverse, factors, gain, proj_weight, left_mine, left_other, partials, by_a, by_b, right_other):
+def tail(base, scaled, inverse, last, gain, proj_weight, partials, by_a, by_b, right_other):
     cols, chans, rows = scaled.shape
     width = proj_weight.shape[1]
-    hidden = width // 4
-    part = hidden // CORES // CHUNKS
+    part = width // 4 // CORES // CHUNKS
     by_key = lambda *shape: pl.BlockSpec((KEYS,) + shape, lambda g: (g, 0, 0))
     return pl.pallas_call(
         functools.partial(tail_kernel, lax.axis_size("row")),
@@ -359,25 +421,25 @@
         grid=(cols // KEYS,),
         in_specs=[
             by_key(chans, rows),
+            by_key(chans, rows),
             by_key(1, rows),
-            by_key(width, rows),
+            by_key(last.shape[1], rows),
             pl.BlockSpec((1, chans), lambda g: (0, 0)),
             pl.BlockSpec((chans, width), lambda g: (0, 0)),
         ]
-        + [pl.BlockSpec((part, KEYS, rows), lambda g: (0, g, 0))] * (6 * CHUNKS),
+        + [pl.BlockSpec((part, KEYS, rows), lambda g: (0, g, 0))] * 4,
         out_specs=pl.BlockSpec((rows, KEYS, chans), lambda g: (0, g, 0)),
         scratch_shapes=[
             pltpu.VMEM((KEYS, chans, rows), jnp.bfloat16),
             pltpu.VMEM((KEYS, rows, chans), jnp.bfloat16),
             pltpu.VMEM((KEYS, width, rows), jnp.bfloat16),
-            pltpu.VMEM((hidden * KEYS, rows), jnp.float32),
-            pltpu.VMEM((hidden * KEYS, rows), jnp.float32),
+            pltpu.VMEM((CORES * part * KEYS, rows), jnp.float32),
             pltpu.VMEM((chans, rows), jnp.float32),
         ],
         compiler_params=PARAMS,
         cost_estimate=COST,
         name="tail",
-    )(scaled, inverse, factors, gain, proj_weight, *left_mine, *left_other, *partials, *by_a, *by_b, *right_other)
+    )(base, scaled, inverse, last, gain, proj_weight, partials, by_a, by_b, right_other)
 
 
 def after(value, *others):
@@ -444,21 +506,27 @@
                 left_grads.append(left_products(own, by_a[c][: n - 1], by_b[c][: n - 1], panels[c], c))
     left_grad_other = [exchange(theirs, 1) for _, theirs in left_grads]
     ks = left_mine.shape[1]
+    scaled, inverse, factors, last = forward
+    own_sums, last_a, last_b = [sums[0] for sums in partials], [v[-1] for v in by_a], [v[-1] for v in by_b]
     right_grad_other = []
     for c in range(CHUNKS):
-        total = arrived_total(partials[c][0][:, ks:], by_a[c][-1][:, ks:], by_b[c][-1][:, ks:], n)
+        value = own_sums[c]
+        if c == CHUNKS - 1:
+            base = known(
+                factors,
+                proj_weight,
+                [mine for mine, _ in left_grads],
+                left_grad_other,
+                own_sums[:c],
+                last_a[:c],
+                last_b[:c],
+                right_grad_other,
+            )
+            value = after(value, base)
+        total = arrived_total(value[:, ks:], last_a[c][:, ks:], last_b[c][:, ks:], n)
         right_grad_other.append(exchange(total.astype(jnp.bfloat16), 1))
-
     return tail(
-        *forward,
-        gain,
-        proj_weight,
-        [mine for mine, _ in left_grads],
-        left_grad_other,
-        [sums[0] for sums in partials],
-        [v[-1] for v in by_a],
-        [v[-1] for v in by_b],
-        right_grad_other,
+        base, scaled, inverse, last, gain, proj_weight, own_sums[-1], last_a[-1], last_b[-1], right_grad_other[-1]
     )
 
 

time: 128 us -> 125 us (0.977)
  waiting for transfers between devices: 52.4 us -> 48.8 us
  Pallas kernels: 30.6 us -> 33.2 us
    ppermute x14, waiting for transfers between devices: 39.3 us -> 34.7 us  [hop(): return lax.ppermute(value, ('row', 'col'), perm)]
    pallas_call x0 -> x1, Pallas kernels: none -> 3.74 us  [known(): pl.pallas_call(functools.partial(known_kernel, lax.axis_size('row')), out...]
    pallas_call x1, Pallas kernels: 8.27 us -> 6.1 us  [tail(): pl.pallas_call(functools.partial(tail_kernel, lax.axis_size('row')), out_...]
    unnamed x46 -> x48, local copies, waits for them, and re-layouts: 5.65 us -> 4.42 us
  transfers between devices with their start and end apart: 26 -> 26, of which waited for: 14 -> 16; matrix products, arithmetic and copies ran while one was open for 8% -> 8% of each run, Pallas kernels for 17% -> 21%
where the time goes in v8:
time: 125 us; the launch traced here: 124 us
  waiting for transfers between devices  48.8 us (39%)
  Pallas kernels  33.2 us (27%)
  starting transfers between devices  26.9 us (22%)
  other arithmetic  9.69 us (8%)
  local copies, waits for them, and re-layouts  5.55 us (4%)
    ppermute x14, waiting for transfers between devices, hop(): return lax.ppermute(value, ('row', 'col'), perm)  34.7 us
    ppermute x14, starting transfers between devices, hop(): return lax.ppermute(value, ('row', 'col'), perm)  17.6 us
    ppermute x12, waiting for transfers between devices, exchange(): return lax.ppermute(value, 'col', [(d, d ^ mask) for d in range(n_col)])  14.1 us
    pallas_call x2, Pallas kernels, front(): pl.pallas_call(right_kernel if right else left_forward_kernel, out_shape=...  11.2 us
    convert_element_type x4, other arithmetic, onward(): return (out_a.astype(jnp.bfloat16), out_b.astype(jnp.bfloat16))  9.32 us
    ppermute x12, starting transfers between devices, exchange(): return lax.ppermute(value, 'col', [(d, d ^ mask) for d in range(n_col)])  9.31 us
    pallas_call x2, Pallas kernels, partial_products(): pl.pallas_call(functools.partial(partial_kernel, n), out_shape=[pltpu.HBM...  6.16 us
    pallas_call x1, Pallas kernels, tail(): pl.pallas_call(functools.partial(tail_kernel, lax.axis_size('row')), out_...  6.1 us
  transfers between devices with their start and end apart: 26, of which 16 were waited for; matrix products, arithmetic and copies ran while one was open for 8% of the time, Pallas kernels for 21%

profile of v8, /device:TPU:0, one launch (start us, length us, event | category | flops | bytes accessed | tf_op | source)
XLA Modules:
  0.0 124.4 jit_solution(3861315626038597775)
XLA Ops:
  0.0 1.1 dynamic-slice_bitcast_fusion
  1.1 0.5 collective-permute-start
  1.6 1.5 %collective-permute-done.other = bf16[64,32,128]{2,1,0:T(8,128)(2,1)S(1)} collective-permute-done((bf16[64,32,128]{2,1,0:T(8,128)(2,1)S(1)}, bf16[64,32,128]{2,1,0:T(8,128)(2,1)S(1)}, u32[]{:S(2)}, u32[]{:S(2)}) %collective-permute-start) | collective-permute-done | bytes 524320 | tf_op jit(solution)/shard_map/ppermute | solution.py:456
  3.2 1.2 pack.1.refs_0_.refs_6_
  4.4 2.9 %collective-permute-start.6 = (bf16[32,128,128]{2,1,0:T(8,128)(2,1)S(1)}, bf16[32,128,128]{2,1,0:T(8,128)(2,1)S(1)}, u32[]{:S(2)}, u32[]{:S(2)}) collective-permute-start(bf16[32,128,128]{2,1,0:T(8,128)(2,1)S(1)} %pack.1.refs_0_.refs_6_), channel_id=1, source_target_pairs={{0,2},{1,3},{2,0},{3,1},{4,6},{5,7},{6,4},{7,5},{8,10},{9,11},{10,... | collective-permute-start | bytes 3145736 | tf_op jit(solution)/shard_map/ppermute | solution.py:456
  7.3 1.5 %collective-permute-start.7 = (bf16[32,128,128]{2,1,0:T(8,128)(2,1)S(1)}, bf16[32,128,128]{2,1,0:T(8,128)(2,1)S(1)}, u32[]{:S(2)}, u32[]{:S(2)}) collective-permute-start(bf16[32,128,128]{2,1,0:T(8,128)(2,1)S(1)} %pack.1.refs_0_.refs_6_), channel_id=1, source_target_pairs={{0,4},{1,5},{2,6},{3,7},{4,0},{5,1},{6,2},{7,3},{8,12},{9,13},{10,... | collective-permute-start | bytes 3145736 | tf_op jit(solution)/shard_map/ppermute | solution.py:456
  8.8 5.1 %right_front.1 = (bf16[32,64,128]{2,1,0:T(8,128)(2,1)S(1)}, bf16[32,64,128]{2,1,0:T(8,128)(2,1)S(1)}) custom-call(s32[4,4]{1,0:T(4,128)S(1)} %copy-done.19, bf16[128,64,128]{2,1,0:T(8,128)(2,1)} %pair.1, f32[1,128]{1,0:T(1,128)} %bitcast.5, f32[1,128]{1,0:T(1,128)} %bitcast.9, bf16[128,256]{1,0:T(8,128)(2,1)} %weight.7), custom_call_target="tpu_custom_call" | custom-call | flops 1 | bytes 18000000 | tf_op jit(solution)/shard_map/right_front/pallas_call | solution.py:144
  14.1 0.5 collective-permute-start.1
  14.6 1.0 collective-permute-done.2
  15.6 0.4 collective-permute-done.1
  16.1 1.6 %collective-permute-start.3 = (bf16[32,128,128]{2,1,0:T(8,128)(2,1)S(1)}, bf16[32,128,128]{2,1,0:T(8,128)(2,1)S(1)}, u32[]{:S(2)}, u32[]{:S(2)}) collective-permute-start(bf16[32,128,128]{2,1,0:T(8,128)(2,1)S(1)} %maximum_maximum_fusion.own), channel_id=1, source_target_pairs={{0,8},{1,9},{2,10},{3,11},{4,12},{5,13},{6,14},{7,15},{8,0},{9,1},... | collective-permute-start | bytes 3145736 | tf_op jit(solution)/shard_map/ppermute | solution.py:464
  17.8 6.0 %left_front.1 = (bf16[32,64,128]{2,1,0:T(8,128)(2,1)S(1)}, bf16[32,64,128]{2,1,0:T(8,128)(2,1)S(1)}, bf16[64,128,128]{2,1,0:T(8,128)(2,1)S(1)}, f32[64,1,128]{2,...) custom-call(s32[4,4]{1,0:T(4,128)S(1)} %copy-done.19, bf16[128,64,128]{2,1,0:T(8,128)(2,1)} %pair.1, ...), custom_call_target="tpu_custom_call" | custom-call | flops 1 | bytes 18000000 | tf_op jit(solution)/shard_map/left_front/pallas_call | solution.py:144
  23.8 2.0 %copy-done.6 = bf16[64,256,128]{2,1,0:T(8,128)(2,1)} copy-done((bf16[64,256,128]{2,1,0:T(8,128)(2,1)}, bf16[64,256,128]{2,1,0:T(8,128)(2,1)S(1)}, u32[]{:S(2)}) %copy-start.6) | copy-done | bytes 4194328
  25.8 1.3 %copy-done.8 = bf16[64,128,128]{2,1,0:T(8,128)(2,1)} copy-done((bf16[64,128,128]{2,1,0:T(8,128)(2,1)}, bf16[64,128,128]{2,1,0:T(8,128)(2,1)S(1)}, u32[]{:S(2)}) %copy-start.8) | copy-done | bytes 2097176
  27.1 0.5 collective-permute-start.4
  27.6 3.2 %collective-permute-done.6.refs_0_.refs_1_.refs_7_ = bf16[32,128,128]{2,1,0:T(8,128)(2,1)S(1)} collective-permute-done((bf16[32,128,128]{2,1,0:T(8,128)(2,1)S(1)}, bf16[32,128,128]{2,1,0:T(8,128)(2,1)S(1)}, u32[]{:S(2)}, u32[]{:S(2)}) %collective-permute-start.6) | collective-permute-done | bytes 1048608 | tf_op jit(solution)/shard_map/ppermute | solution.py:456
  30.8 1.5 %collective-permute-done.7.refs_1_.refs_2_.refs_8_ = bf16[32,128,128]{2,1,0:T(8,128)(2,1)S(1)} collective-permute-done((bf16[32,128,128]{2,1,0:T(8,128)(2,1)S(1)}, bf16[32,128,128]{2,1,0:T(8,128)(2,1)S(1)}, u32[]{:S(2)}, u32[]{:S(2)}) %collective-permute-start.7) | collective-permute-done | bytes 1048608 | tf_op jit(solution)/shard_map/ppermute | solution.py:456
  32.4 1.6 %collective-permute-start.8 = (bf16[16,128,128]{2,1,0:T(8,128)(2,1)S(1)}, bf16[16,128,128]{2,1,0:T(8,128)(2,1)S(1)}, u32[]{:S(2)}, u32[]{:S(2)}) collective-permute-start(bf16[16,128,128]{2,1,0:T(8,128)(2,1)S(1)} %get-tuple-element.42), channel_id=1, source_target_pairs={{0,4},{1,5},{2,6},{3,7},{4,0},{5,1},{6,2},{7,3},{8,12},{9,13},{10,... | collective-permute-start | bytes 1572872 | tf_op jit(solution)/shard_map/ppermute | solution.py:456
  33.9 0.5 collective-permute-start.13
  34.5 6.9 %collective-permute-done.3.by_a.refs_0_ = bf16[32,128,128]{2,1,0:T(8,128)(2,1)S(1)} collective-permute-done((bf16[32,128,128]{2,1,0:T(8,128)(2,1)S(1)}, bf16[32,128,128]{2,1,0:T(8,128)(2,1)S(1)}, u32[]{:S(2)}, u32[]{:S(2)}) %collective-permute-start.3) | collective-permute-done | bytes 1048608 | tf_op jit(solution)/shard_map/ppermute | solution.py:464
  41.4 3.9 %collective-permute-done.8.refs_3_.refs_9_ = bf16[16,128,128]{2,1,0:T(8,128)(2,1)S(1)} collective-permute-done((bf16[16,128,128]{2,1,0:T(8,128)(2,1)S(1)}, bf16[16,128,128]{2,1,0:T(8,128)(2,1)S(1)}, u32[]{:S(2)}, u32[]{:S(2)}) %collective-permute-start.8) | collective-permute-done | bytes 524320 | tf_op jit(solution)/shard_map/ppermute | solution.py:456
  45.2 3.0 %right_partials.2 = (bf16[16,128,128]{2,1,0:T(8,128)(2,1)}, bf16[16,128,128]{2,1,0:T(8,128)(2,1)}, bf16[16,128,128]{2,1,0:T(8,128)(2,1)}, bf16[16,128,128]{2,1,0...) custom-call(bf16[32,64,128]{2,1,0:T(8,128)(2,1)S(1)} %get-tuple-element.40.left_mine, ...), custom_call_target="tpu_custom_call" | custom-call | flops 1 | bytes 8000000 | tf_op jit(solution)/shard_map/right_partials/pallas_call | solution.py:255
  48.3 1.6 %collective-permute-start.9 = (bf16[16,128,128]{2,1,0:T(8,128)(2,1)}, bf16[16,128,128]{2,1,0:T(8,128)(2,1)}, u32[]{:S(2)}, u32[]{:S(2)}) collective-permute-start(bf16[16,128,128]{2,1,0:T(8,128)(2,1)} %get-tuple-element.43), channel_id=1, source_target_pairs={{0,8},{1,9},{2,10},{3,11},{4,12},{5,13},{6,14},{7,15},{8,0},{9,1},... | collective-permute-start | bytes 1572872 | tf_op jit(solution)/shard_map/ppermute | solution.py:464
  49.9 3.1 %right_partials.3 = (bf16[16,128,128]{2,1,0:T(8,128)(2,1)}, bf16[16,128,128]{2,1,0:T(8,128)(2,1)}, bf16[16,128,128]{2,1,0:T(8,128)(2,1)}, bf16[16,128,128]{2,1,0...) custom-call(bf16[32,64,128]{2,1,0:T(8,128)(2,1)S(1)} %get-tuple-element.40.left_mine, ...), custom_call_target="tpu_custom_call" | custom-call | flops 1 | bytes 8000000 | tf_op jit(solution)/shard_map/right_partials/pallas_call | solution.py:255
  53.0 3.2 %collective-permute-start.14 = (bf16[16,128,128]{2,1,0:T(8,128)(2,1)}, bf16[16,128,128]{2,1,0:T(8,128)(2,1)}, u32[]{:S(2)}, u32[]{:S(2)}) collective-permute-start(bf16[16,128,128]{2,1,0:T(8,128)(2,1)} %get-tuple-element.48), channel_id=1, source_target_pairs={{0,8},{1,9},{2,10},{3,11},{4,12},{5,13},{6,14},{7,15},{8,0},{9,1},... | collective-permute-start | bytes 1572872 | tf_op jit(solution)/shard_map/ppermute | solution.py:464
  56.2 7.3 %collective-permute-done.9.refs_1_ = bf16[16,128,128]{2,1,0:T(8,128)(2,1)} collective-permute-done((bf16[16,128,128]{2,1,0:T(8,128)(2,1)}, bf16[16,128,128]{2,1,0:T(8,128)(2,1)}, u32[]{:S(2)}, u32[]{:S(2)}) %collective-permute-start.9) | collective-permute-done | bytes 524320 | tf_op jit(solution)/shard_map/ppermute | solution.py:464
  63.5 2.9 %fusion.11 = (bf16[16,128,128]{2,1,0:T(8,128)(2,1)}, bf16[16,128,128]{2,1,0:T(8,128)(2,1)}) fusion(bf16[16,128,128]{2,1,0:T(8,128)(2,1)} %get-tuple-element.45, bf16[16,128,128]{2,1,0:T(8,128)(2,1)} %collective-permute-done.9.refs_1_, pred[]{:T(512)S(6)} %select_n.167, pred[]{:T(512)S(6)} %ge.8, pred[]{:T(512)S(6)} %lt.10, pred[]{:T(512)S(6)} %eq.2, ...), kind=kLoop, calls=%fused_computation.15 | loop fusion | flops 3407872 | bytes 2621445 | tf_op jit(solution)/shard_map/convert_element_type | solution.py:234
  66.3 2.8 %collective-permute-start.11 = (bf16[16,128,128]{2,1,0:T(8,128)(2,1)}, bf16[16,128,128]{2,1,0:T(8,128)(2,1)}, u32[]{:S(2)}, u32[]{:S(2)}) collective-permute-start(bf16[16,128,128]{2,1,0:T(8,128)(2,1)} %get-tuple-element.72), channel_id=1, source_target_pairs={{0,8},{1,9},{2,10},{3,11},{4,12},{5,13},{6,14},{7,15},{8,0},{9,1},... | collective-permute-start | bytes 1572872 | tf_op jit(solution)/shard_map/ppermute | solution.py:464
  69.1 5.6 %collective-permute-done.14.refs_1_ = bf16[16,128,128]{2,1,0:T(8,128)(2,1)} collective-permute-done((bf16[16,128,128]{2,1,0:T(8,128)(2,1)}, bf16[16,128,128]{2,1,0:T(8,128)(2,1)}, u32[]{:S(2)}, u32[]{:S(2)}) %collective-permute-start.14) | collective-permute-done | bytes 524320 | tf_op jit(solution)/shard_map/ppermute | solution.py:464
  74.7 2.7 %fusion.7 = (bf16[16,128,128]{2,1,0:T(8,128)(2,1)}, bf16[16,128,128]{2,1,0:T(8,128)(2,1)}) fusion(bf16[16,128,128]{2,1,0:T(8,128)(2,1)S(1)} %copy-done.21, bf16[16,128,128]{2,1,0:T(8,128)(2,1)} %collective-permute-done.14.refs_1_, pred[]{:T(512)S(6)} %select_n.167, pred[]{:T(512)S(6)} %ge.8, pred[]{:T(512)S(6)} %lt.10, pred[]{:T(512)S(6)} %eq.2, ...), kind=kLoop, calls=%fused_computation.11 | loop fusion | flops 3407872 | bytes 2621445 | tf_op jit(solution)/shard_map/convert_element_type | solution.py:234
  77.4 2.8 %collective-permute-start.16 = (bf16[16,128,128]{2,1,0:T(8,128)(2,1)}, bf16[16,128,128]{2,1,0:T(8,128)(2,1)}, u32[]{:S(2)}, u32[]{:S(2)}) collective-permute-start(bf16[16,128,128]{2,1,0:T(8,128)(2,1)} %get-tuple-element.70), channel_id=1, source_target_pairs={{0,8},{1,9},{2,10},{3,11},{4,12},{5,13},{6,14},{7,15},{8,0},{9,1},... | collective-permute-start | bytes 1572872 | tf_op jit(solution)/shard_map/ppermute | solution.py:464
  80.2 5.8 %collective-permute-done.11.refs_2_ = bf16[16,128,128]{2,1,0:T(8,128)(2,1)} collective-permute-done((bf16[16,128,128]{2,1,0:T(8,128)(2,1)}, bf16[16,128,128]{2,1,0:T(8,128)(2,1)}, u32[]{:S(2)}, u32[]{:S(2)}) %collective-permute-start.11) | collective-permute-done | bytes 524320 | tf_op jit(solution)/shard_map/ppermute | solution.py:464
  85.9 2.1 %add_convert_fusion.2 = (bf16[16,128,128]{2,1,0:T(8,128)(2,1)S(1)}, bf16[16,128,128]{2,1,0:T(8,128)(2,1)S(1)}) fusion(bf16[16,128,128]{2,1,0:T(8,128)(2,1)} %collective-permute-done.11.refs_2_, bf16[16,128,128]{2,1,0:T(8,128)(2,1)} %get-tuple-element.56, bf16[16,128,128]{2,1,0:T(8,128)(2,1)} %get-tuple-element.55, pred[]{:T(512)S(6)} %ge.9, pred[]{:T(512)S(6)} %lt.11, ...), kind=kLoop, calls=%fused_computation.21 | loop fusion | flops 3670016 | bytes 3145733 | tf_op jit(solution)/shard_map/convert_element_type | solution.py:234
  88.0 2.8 %collective-permute-start.20 = (bf16[16,128,128]{2,1,0:T(8,128)(2,1)S(1)}, bf16[16,128,128]{2,1,0:T(8,128)(2,1)S(1)}, u32[]{:S(2)}, u32[]{:S(2)}) collective-permute-start(bf16[16,128,128]{2,1,0:T(8,128)(2,1)S(1)} %get-tuple-element.68), channel_id=1, source_target_pairs={{0,8},{1,9},{2,10},{3,11},{4,12},{5,13},{6,14},{7,15},{8,0},{9,1},... | collective-permute-start | bytes 1572872 | tf_op jit(solution)/shard_map/ppermute | solution.py:464
  90.8 1.0 copy-done.13
  91.9 2.4 %left_products.2 = (f32[16,64,128]{2,1,0:T(8,128)S(1)}, bf16[16,64,128]{2,1,0:T(8,128)(2,1)S(1)}) custom-call(bf16[32,128,128]{2,1,0:T(8,128)(2,1)S(1)} %copy-done.5, bf16[32,128,128]{2,1,0:T(8,128)(2,1)S(1)} %copy-done.1, bf16[16,128,128]{2,1,0:T(8,128)(2,1)} %collective-permute-done.9.refs_1_, bf16[16,128,128]{2,1,0:T(8,128)(2,1)} %collective-permute-done.11.refs_2_, ...), custom_call_target="tpu_custom_call" | custom-call | flops 1 | bytes 8000000 | tf_op jit(solution)/shard_map/left_products/pallas_call | solution.py:296
  94.3 2.9 %collective-permute-done.16.refs_2_ = bf16[16,128,128]{2,1,0:T(8,128)(2,1)} collective-permute-done((bf16[16,128,128]{2,1,0:T(8,128)(2,1)}, bf16[16,128,128]{2,1,0:T(8,128)(2,1)}, u32[]{:S(2)}, u32[]{:S(2)}) %collective-permute-start.16) | collective-permute-done | bytes 524320 | tf_op jit(solution)/shard_map/ppermute | solution.py:464
  97.2 1.7 %add_convert_fusion = (bf16[16,128,128]{2,1,0:T(8,128)(2,1)S(1)}, bf16[16,128,128]{2,1,0:T(8,128)(2,1)S(1)}) fusion(bf16[16,128,128]{2,1,0:T(8,128)(2,1)} %collective-permute-done.16.refs_2_, bf16[16,128,128]{2,1,0:T(8,128)(2,1)S(1)} %copy-done.23, bf16[16,128,128]{2,1,0:T(8,128)(2,1)S(1)} %copy-done.22, pred[]{:T(512)S(6)} %ge.9, pred[]{:T(512)S(6)} %lt.11, ...), kind=kLoop, calls=%fused_computation.17 | loop fusion | flops 3670016 | bytes 3145733 | tf_op jit(solution)/shard_map/convert_element_type | solution.py:234
  98.9 2.8 %collective-permute-start.23 = (bf16[16,128,128]{2,1,0:T(8,128)(2,1)S(1)}, bf16[16,128,128]{2,1,0:T(8,128)(2,1)S(1)}, u32[]{:S(2)}, u32[]{:S(2)}) collective-permute-start(bf16[16,128,128]{2,1,0:T(8,128)(2,1)S(1)} %get-tuple-element.66), channel_id=1, source_target_pairs={{0,8},{1,9},{2,10},{3,11},{4,12},{5,13},{6,14},{7,15},{8,0},{9,1},... | collective-permute-start | bytes 1572872 | tf_op jit(solution)/shard_map/ppermute | solution.py:464
  101.7 0.5 collective-permute-start.18
  102.3 2.4 %left_products.3 = (f32[16,64,128]{2,1,0:T(8,128)S(1)}, bf16[16,64,128]{2,1,0:T(8,128)(2,1)S(1)}) custom-call(bf16[32,128,128]{2,1,0:T(8,128)(2,1)S(1)} %copy-done.5, bf16[32,128,128]{2,1,0:T(8,128)(2,1)S(1)} %copy-done.1, bf16[16,128,128]{2,1,0:T(8,128)(2,1)} %collective-permute-done.14.refs_1_, bf16[16,128,128]{2,1,0:T(8,128)(2,1)} %collective-permute-done.16.refs_2_, ...), custom_call_target="tpu_custom_call" | custom-call | flops 1 | bytes 8000000 | tf_op jit(solution)/shard_map/left_products/pallas_call | solution.py:296
  104.7 3.6 %collective-permute-done.20.refs_5_ = bf16[16,128,128]{2,1,0:T(8,128)(2,1)S(1)} collective-permute-done((bf16[16,128,128]{2,1,0:T(8,128)(2,1)S(1)}, bf16[16,128,128]{2,1,0:T(8,128)(2,1)S(1)}, u32[]{:S(2)}, u32[]{:S(2)}) %collective-permute-start.20) | collective-permute-done | bytes 524320 | tf_op jit(solution)/shard_map/ppermute | solution.py:464
  108.5 0.6 collective-permute-start.22
  109.0 0.8 collective-permute-done.19.refs_3_
  110.2 3.7 %known.1.base = f32[64,128,128]{2,1,0:T(8,128)S(1)} custom-call(bf16[64,256,128]{2,1,0:T(8,128)(2,1)S(1)} %copy-done.7, bf16[128,256]{1,0:T(8,128)(2,1)S(1)} %copy-done.16, f32[16,64,128]{2,1,0:T(8,128)S(1)} %get-tuple-element.46.refs_0_, f32[16,64,128]{2,1,0:T(8,128)S(1)} %get-tuple-element.51.refs_1_, ...), custom_call_target="tpu_custom_call" | custom-call | flops 1 | bytes 8000000 | tf_op jit(solution)/shard_map/known/pallas_call | solution.py:363
  114.0 2.6 %collective-permute-done.23.by_a = bf16[16,128,128]{2,1,0:T(8,128)(2,1)S(1)} collective-permute-done((bf16[16,128,128]{2,1,0:T(8,128)(2,1)S(1)}, bf16[16,128,128]{2,1,0:T(8,128)(2,1)S(1)}, u32[]{:S(2)}, u32[]{:S(2)}) %collective-permute-start.23) | collective-permute-done | bytes 524320 | tf_op jit(solution)/shard_map/ppermute | solution.py:464
  116.8 1.5 %collective-permute-done.25.right_other = bf16[16,64,128]{2,1,0:T(8,128)(2,1)S(1)} collective-permute-done((bf16[16,64,128]{2,1,0:T(8,128)(2,1)S(1)}, bf16[16,64,128]{2,1,0:T(8,128)(2,1)S(1)}, u32[]{:S(2)}, u32[]{:S(2)}) %collective-permute-start.25) | collective-permute-done | bytes 262176 | tf_op jit(solution)/shard_map/ppermute | solution.py:456
  118.3 6.1 %tail.1 = bf16[128,64,128]{2,1,0:T(8,128)(2,1)} custom-call(f32[64,128,128]{2,1,0:T(8,128)S(1)} %known.1.base, bf16[64,128,128]{2,1,0:T(8,128)(2,1)S(1)} %copy-done.9, f32[64,1,128]{2,1,0:T(1,128)S(1)} %get-tuple-element.58.inverse, bf16[64,64,128]{2,1,0:T(8,128)(2,1)S(1)} %copy-done.18, f32[1,128]{1,0:T(1,128)S(1)} %bitcast.7, ...), custom_call_target="tpu_custom_call" | custom-call | flops 1 | bytes 8000000 | tf_op jit(solution)/shard_map/tail/pallas_call | solution.py:418
  (71 shorter events, 1.1 us)
Async XLA Ops:
  0.0 8.8 %copy-start.19 = (s32[4,4]{1,0:T(4,128)S(1)}, s32[4,4]{1,0:T(4,128)}, u32[]{:S(2)}) copy-start(s32[4,4]{1,0:T(4,128)} %mask.3) | copy-start | bytes 196
  1.1 2.1 %collective-permute-start = (bf16[64,32,128]{2,1,0:T(8,128)(2,1)S(1)}, bf16[64,32,128]{2,1,0:T(8,128)(2,1)S(1)}, u32[]{:S(2)}, u32[]{:S(2)}) collective-permute-start(bf16[64,32,128]{2,1,0:T(8,128)(2,1)S(1)} %dynamic-slice_bitcast_fusion), channel_id=1, source_target_pairs={{0,1},{1,0},{2,3},{3,2},{4,5},{5,4},{6,7},{7,6},{8,9},{9,8},{10,11... | collective-permute-start | bytes 1572872 | tf_op jit(solution)/shard_map/ppermute | solution.py:456
  4.4 26.4 %collective-permute-start.6 = (bf16[32,128,128]{2,1,0:T(8,128)(2,1)S(1)}, bf16[32,128,128]{2,1,0:T(8,128)(2,1)S(1)}, u32[]{:S(2)}, u32[]{:S(2)}) collective-permute-start(bf16[32,128,128]{2,1,0:T(8,128)(2,1)S(1)} %pack.1.refs_0_.refs_6_), channel_id=1, source_target_pairs={{0,2},{1,3},{2,0},{3,1},{4,6},{5,7},{6,4},{7,5},{8,10},{9,11},{10,... | collective-permute-start | bytes 3145736 | tf_op jit(solution)/shard_map/ppermute | solution.py:456
  7.3 24.9 %collective-permute-start.7 = (bf16[32,128,128]{2,1,0:T(8,128)(2,1)S(1)}, bf16[32,128,128]{2,1,0:T(8,128)(2,1)S(1)}, u32[]{:S(2)}, u32[]{:S(2)}) collective-permute-start(bf16[32,128,128]{2,1,0:T(8,128)(2,1)S(1)} %pack.1.refs_0_.refs_6_), channel_id=1, source_target_pairs={{0,4},{1,5},{2,6},{3,7},{4,0},{5,1},{6,2},{7,3},{8,12},{9,13},{10,... | collective-permute-start | bytes 3145736 | tf_op jit(solution)/shard_map/ppermute | solution.py:456
  14.0 1.6 %collective-permute-start.2 = (bf16[16,64,128]{2,1,0:T(8,128)(2,1)S(1)}, bf16[16,64,128]{2,1,0:T(8,128)(2,1)S(1)}, u32[]{:S(2)}, u32[]{:S(2)}) collective-permute-start(bf16[16,64,128]{2,1,0:T(8,128)(2,1)S(1)} %get-tuple-element.74), channel_id=1, source_target_pairs={{0,1},{1,0},{2,3},{3,2},{4,5},{5,4},{6,7},{7,6},{8,9},{9,8},{10,11... | collective-permute-start | bytes 786440 | tf_op jit(solution)/shard_map/ppermute | solution.py:456
  14.1 1.9 %collective-permute-start.1 = (bf16[16,64,128]{2,1,0:T(8,128)(2,1)S(1)}, bf16[16,64,128]{2,1,0:T(8,128)(2,1)S(1)}, u32[]{:S(2)}, u32[]{:S(2)}) collective-permute-start(bf16[16,64,128]{2,1,0:T(8,128)(2,1)S(1)} %get-tuple-element.73), channel_id=1, source_target_pairs={{0,1},{1,0},{2,3},{3,2},{4,5},{5,4},{6,7},{7,6},{8,9},{9,8},{10,11... | collective-permute-start | bytes 786440 | tf_op jit(solution)/shard_map/ppermute | solution.py:456
  16.1 16.2 %copy-start.4 = (bf16[32,128,128]{2,1,0:T(8,128)(2,1)}, bf16[32,128,128]{2,1,0:T(8,128)(2,1)S(1)}, u32[]{:S(2)}) copy-start(bf16[32,128,128]{2,1,0:T(8,128)(2,1)S(1)} %maximum_maximum_fusion.own) | copy-start | bytes 3145732
  16.1 25.3 %collective-permute-start.3 = (bf16[32,128,128]{2,1,0:T(8,128)(2,1)S(1)}, bf16[32,128,128]{2,1,0:T(8,128)(2,1)S(1)}, u32[]{:S(2)}, u32[]{:S(2)}) collective-permute-start(bf16[32,128,128]{2,1,0:T(8,128)(2,1)S(1)} %maximum_maximum_fusion.own), channel_id=1, source_target_pairs={{0,8},{1,9},{2,10},{3,11},{4,12},{5,13},{6,14},{7,15},{8,0},{9,1},... | collective-permute-start | bytes 3145736 | tf_op jit(solution)/shard_map/ppermute | solution.py:464
  17.8 23.6 %collective-permute-start.5 = (bf16[32,128,128]{2,1,0:T(8,128)(2,1)S(1)}, bf16[32,128,128]{2,1,0:T(8,128)(2,1)S(1)}, u32[]{:S(2)}, u32[]{:S(2)}) collective-permute-start(bf16[32,128,128]{2,1,0:T(8,128)(2,1)S(1)} %maximum_maximum_fusion.own), channel_id=1, source_target_pairs={{0,1},{1,0},{2,3},{3,2},{4,5},{5,4},{6,7},{7,6},{8,16},{9,17},{10,... | collective-permute-start | bytes 3145736 | tf_op jit(solution)/shard_map/ppermute | solution.py:464
  23.8 2.0 %copy-start.6 = (bf16[64,256,128]{2,1,0:T(8,128)(2,1)}, bf16[64,256,128]{2,1,0:T(8,128)(2,1)S(1)}, u32[]{:S(2)}) copy-start(bf16[64,256,128]{2,1,0:T(8,128)(2,1)S(1)} %get-tuple-element.39.factors) | copy-start | bytes 12582916
  27.1 6.8 %copy-start.17 = (bf16[64,64,128]{2,1,0:T(8,128)(2,1)}, bf16[64,64,128]{2,1,0:T(8,128)(2,1)S(1)}, u32[]{:S(2)}) copy-start(bf16[64,64,128]{2,1,0:T(8,128)(2,1)S(1)} %get-tuple-element.59.last) | copy-start | bytes 3145732
  27.1 7.4 %collective-permute-start.4 = (bf16[32,64,128]{2,1,0:T(8,128)(2,1)S(1)}, bf16[32,64,128]{2,1,0:T(8,128)(2,1)S(1)}, u32[]{:S(2)}, u32[]{:S(2)}) collective-permute-start(bf16[32,64,128]{2,1,0:T(8,128)(2,1)S(1)} %get-tuple-element.41), channel_id=1, source_target_pairs={{0,1},{1,0},{2,3},{3,2},{4,5},{5,4},{6,7},{7,6},{8,9},{9,8},{10,11... | collective-permute-start | bytes 1572872 | tf_op jit(solution)/shard_map/ppermute | solution.py:456
  32.4 12.9 %collective-permute-start.8 = (bf16[16,128,128]{2,1,0:T(8,128)(2,1)S(1)}, bf16[16,128,128]{2,1,0:T(8,128)(2,1)S(1)}, u32[]{:S(2)}, u32[]{:S(2)}) collective-permute-start(bf16[16,128,128]{2,1,0:T(8,128)(2,1)S(1)} %get-tuple-element.42), channel_id=1, source_target_pairs={{0,4},{1,5},{2,6},{3,7},{4,0},{5,1},{6,2},{7,3},{8,12},{9,13},{10,... | collective-permute-start | bytes 1572872 | tf_op jit(solution)/shard_map/ppermute | solution.py:456
  33.9 15.9 %collective-permute-start.13 = (bf16[16,128,128]{2,1,0:T(8,128)(2,1)S(1)}, bf16[16,128,128]{2,1,0:T(8,128)(2,1)S(1)}, u32[]{:S(2)}, u32[]{:S(2)}) collective-permute-start(bf16[16,128,128]{2,1,0:T(8,128)(2,1)S(1)} %get-tuple-element.47), channel_id=1, source_target_pairs={{0,2},{1,3},{2,0},{3,1},{4,6},{5,7},{6,4},{7,5},{8,10},{9,11},{10,... | collective-permute-start | bytes 1572872 | tf_op jit(solution)/shard_map/ppermute | solution.py:456
  41.4 8.5 %copy-start = (bf16[32,128,128]{2,1,0:T(8,128)(2,1)}, bf16[32,128,128]{2,1,0:T(8,128)(2,1)S(1)}, u32[]{:S(2)}) copy-start(bf16[32,128,128]{2,1,0:T(8,128)(2,1)S(1)} %collective-permute-done.3.by_a.refs_0_) | copy-start | bytes 3145732
  41.4 8.5 %copy-start.2 = (bf16[32,128,128]{2,1,0:T(8,128)(2,1)}, bf16[32,128,128]{2,1,0:T(8,128)(2,1)S(1)}, u32[]{:S(2)}) copy-start(bf16[32,128,128]{2,1,0:T(8,128)(2,1)S(1)} %collective-permute-done.5.by_b.refs_3_) | copy-start | bytes 3145732
  45.2 3.1 %copy-start.12 = (bf16[16,128,128]{2,1,0:T(8,128)(2,1)}, bf16[16,128,128]{2,1,0:T(8,128)(2,1)S(1)}, u32[]{:S(2)}) copy-start(bf16[16,128,128]{2,1,0:T(8,128)(2,1)S(1)} %collective-permute-done.8.refs_3_.refs_9_) | copy-start | bytes 1572868
  48.3 15.2 %collective-permute-start.9 = (bf16[16,128,128]{2,1,0:T(8,128)(2,1)}, bf16[16,128,128]{2,1,0:T(8,128)(2,1)}, u32[]{:S(2)}, u32[]{:S(2)}) collective-permute-start(bf16[16,128,128]{2,1,0:T(8,128)(2,1)} %get-tuple-element.43), channel_id=1, source_target_pairs={{0,8},{1,9},{2,10},{3,11},{4,12},{5,13},{6,14},{7,15},{8,0},{9,1},... | collective-permute-start | bytes 1572872 | tf_op jit(solution)/shard_map/ppermute | solution.py:464
  49.9 13.6 %collective-permute-start.10 = (bf16[16,128,128]{2,1,0:T(8,128)(2,1)}, bf16[16,128,128]{2,1,0:T(8,128)(2,1)}, u32[]{:S(2)}, u32[]{:S(2)}) collective-permute-start(bf16[16,128,128]{2,1,0:T(8,128)(2,1)} %get-tuple-element.44), channel_id=1, source_target_pairs={{0,1},{1,0},{2,3},{3,2},{4,5},{5,4},{6,7},{7,6},{8,16},{9,17},{10,... | collective-permute-start | bytes 1572872 | tf_op jit(solution)/shard_map/ppermute | solution.py:464
  49.9 3.1 %copy-start.10 = (bf16[16,128,128]{2,1,0:T(8,128)(2,1)}, bf16[16,128,128]{2,1,0:T(8,128)(2,1)S(1)}, u32[]{:S(2)}) copy-start(bf16[16,128,128]{2,1,0:T(8,128)(2,1)S(1)} %collective-permute-done.13.refs_3_.refs_9_) | copy-start | bytes 1572868
  53.0 21.7 %collective-permute-start.14 = (bf16[16,128,128]{2,1,0:T(8,128)(2,1)}, bf16[16,128,128]{2,1,0:T(8,128)(2,1)}, u32[]{:S(2)}, u32[]{:S(2)}) collective-permute-start(bf16[16,128,128]{2,1,0:T(8,128)(2,1)} %get-tuple-element.48), channel_id=1, source_target_pairs={{0,8},{1,9},{2,10},{3,11},{4,12},{5,13},{6,14},{7,15},{8,0},{9,1},... | collective-permute-start | bytes 1572872 | tf_op jit(solution)/shard_map/ppermute | solution.py:464
  56.2 18.5 %collective-permute-start.15 = (bf16[16,128,128]{2,1,0:T(8,128)(2,1)}, bf16[16,128,128]{2,1,0:T(8,128)(2,1)}, u32[]{:S(2)}, u32[]{:S(2)}) collective-permute-start(bf16[16,128,128]{2,1,0:T(8,128)(2,1)} %get-tuple-element.49), channel_id=1, source_target_pairs={{0,1},{1,0},{2,3},{3,2},{4,5},{5,4},{6,7},{7,6},{8,16},{9,17},{10,... | collective-permute-start | bytes 1572872 | tf_op jit(solution)/shard_map/ppermute | solution.py:464
  56.2 18.5 %copy-start.21 = (bf16[16,128,128]{2,1,0:T(8,128)(2,1)S(1)}, bf16[16,128,128]{2,1,0:T(8,128)(2,1)}, u32[]{:S(2)}) copy-start(bf16[16,128,128]{2,1,0:T(8,128)(2,1)} %get-tuple-element.50) | copy-start | bytes 1572868
  66.3 19.6 %collective-permute-start.11 = (bf16[16,128,128]{2,1,0:T(8,128)(2,1)}, bf16[16,128,128]{2,1,0:T(8,128)(2,1)}, u32[]{:S(2)}, u32[]{:S(2)}) collective-permute-start(bf16[16,128,128]{2,1,0:T(8,128)(2,1)} %get-tuple-element.72), channel_id=1, source_target_pairs={{0,8},{1,9},{2,10},{3,11},{4,12},{5,13},{6,14},{7,15},{8,0},{9,1},... | collective-permute-start | bytes 1572872 | tf_op jit(solution)/shard_map/ppermute | solution.py:464
  69.1 16.9 %collective-permute-start.12 = (bf16[16,128,128]{2,1,0:T(8,128)(2,1)}, bf16[16,128,128]{2,1,0:T(8,128)(2,1)}, u32[]{:S(2)}, u32[]{:S(2)}) collective-permute-start(bf16[16,128,128]{2,1,0:T(8,128)(2,1)} %get-tuple-element.71), channel_id=1, source_target_pairs={{0,1},{1,0},{2,3},{3,2},{4,5},{5,4},{6,7},{7,6},{8,16},{9,17},{10,... | collective-permute-start | bytes 1572872 | tf_op jit(solution)/shard_map/ppermute | solution.py:464
  77.4 19.8 %collective-permute-start.16 = (bf16[16,128,128]{2,1,0:T(8,128)(2,1)}, bf16[16,128,128]{2,1,0:T(8,128)(2,1)}, u32[]{:S(2)}, u32[]{:S(2)}) collective-permute-start(bf16[16,128,128]{2,1,0:T(8,128)(2,1)} %get-tuple-element.70), channel_id=1, source_target_pairs={{0,8},{1,9},{2,10},{3,11},{4,12},{5,13},{6,14},{7,15},{8,0},{9,1},... | collective-permute-start | bytes 1572872 | tf_op jit(solution)/shard_map/ppermute | solution.py:464
  80.1 17.0 %collective-permute-start.17 = (bf16[16,128,128]{2,1,0:T(8,128)(2,1)}, bf16[16,128,128]{2,1,0:T(8,128)(2,1)}, u32[]{:S(2)}, u32[]{:S(2)}) collective-permute-start(bf16[16,128,128]{2,1,0:T(8,128)(2,1)} %get-tuple-element.69), channel_id=1, source_target_pairs={{0,1},{1,0},{2,3},{3,2},{4,5},{5,4},{6,7},{7,6},{8,16},{9,17},{10,... | collective-permute-start | bytes 1572872 | tf_op jit(solution)/shard_map/ppermute | solution.py:464
  80.1 10.7 %copy-start.1 = (bf16[32,128,128]{2,1,0:T(8,128)(2,1)S(1)}, bf16[32,128,128]{2,1,0:T(8,128)(2,1)}, u32[]{:S(2)}) copy-start(bf16[32,128,128]{2,1,0:T(8,128)(2,1)} %copy-done) | copy-start | bytes 3145732
  80.1 10.7 %copy-start.3 = (bf16[32,128,128]{2,1,0:T(8,128)(2,1)S(1)}, bf16[32,128,128]{2,1,0:T(8,128)(2,1)}, u32[]{:S(2)}) copy-start(bf16[32,128,128]{2,1,0:T(8,128)(2,1)} %copy-done.2) | copy-start | bytes 3145732
  80.1 10.7 %copy-start.5 = (bf16[32,128,128]{2,1,0:T(8,128)(2,1)S(1)}, bf16[32,128,128]{2,1,0:T(8,128)(2,1)}, u32[]{:S(2)}) copy-start(bf16[32,128,128]{2,1,0:T(8,128)(2,1)} %copy-done.4) | copy-start | bytes 3145732
  88.0 20.3 %collective-permute-start.20 = (bf16[16,128,128]{2,1,0:T(8,128)(2,1)S(1)}, bf16[16,128,128]{2,1,0:T(8,128)(2,1)S(1)}, u32[]{:S(2)}, u32[]{:S(2)}) collective-permute-start(bf16[16,128,128]{2,1,0:T(8,128)(2,1)S(1)} %get-tuple-element.68), channel_id=1, source_target_pairs={{0,8},{1,9},{2,10},{3,11},{4,12},{5,13},{6,14},{7,15},{8,0},{9,1},... | collective-permute-start | bytes 1572872 | tf_op jit(solution)/shard_map/ppermute | solution.py:464
  90.8 17.5 %collective-permute-start.21 = (bf16[16,128,128]{2,1,0:T(8,128)(2,1)S(1)}, bf16[16,128,128]{2,1,0:T(8,128)(2,1)S(1)}, u32[]{:S(2)}, u32[]{:S(2)}) collective-permute-start(bf16[16,128,128]{2,1,0:T(8,128)(2,1)S(1)} %get-tuple-element.67), channel_id=1, source_target_pairs={{0,1},{1,0},{2,3},{3,2},{4,5},{5,4},{6,7},{7,6},{8,16},{9,17},{10,... | collective-permute-start | bytes 1572872 | tf_op jit(solution)/shard_map/ppermute | solution.py:464
  91.9 5.3 %copy-start.22 = (bf16[16,128,128]{2,1,0:T(8,128)(2,1)S(1)}, bf16[16,128,128]{2,1,0:T(8,128)(2,1)}, u32[]{:S(2)}) copy-start(bf16[16,128,128]{2,1,0:T(8,128)(2,1)} %get-tuple-element.61) | copy-start | bytes 1572868
  91.9 5.3 %copy-start.23 = (bf16[16,128,128]{2,1,0:T(8,128)(2,1)S(1)}, bf16[16,128,128]{2,1,0:T(8,128)(2,1)}, u32[]{:S(2)}) copy-start(bf16[16,128,128]{2,1,0:T(8,128)(2,1)} %get-tuple-element.62) | copy-start | bytes 1572868
  94.2 8.0 %copy-start.11 = (bf16[16,128,128]{2,1,0:T(8,128)(2,1)S(1)}, bf16[16,128,128]{2,1,0:T(8,128)(2,1)}, u32[]{:S(2)}) copy-start(bf16[16,128,128]{2,1,0:T(8,128)(2,1)} %copy-done.10) | copy-start | bytes 1572868
  98.9 17.6 %collective-permute-start.23 = (bf16[16,128,128]{2,1,0:T(8,128)(2,1)S(1)}, bf16[16,128,128]{2,1,0:T(8,128)(2,1)S(1)}, u32[]{:S(2)}, u32[]{:S(2)}) collective-permute-start(bf16[16,128,128]{2,1,0:T(8,128)(2,1)S(1)} %get-tuple-element.66), channel_id=1, source_target_pairs={{0,8},{1,9},{2,10},{3,11},{4,12},{5,13},{6,14},{7,15},{8,0},{9,1},... | collective-permute-start | bytes 1572872 | tf_op jit(solution)/shard_map/ppermute | solution.py:464
  101.7 6.6 %copy-start.15 = (bf16[16,128,128]{2,1,0:T(8,128)(2,1)S(1)}, bf16[16,128,128]{2,1,0:T(8,128)(2,1)}, u32[]{:S(2)}) copy-start(bf16[16,128,128]{2,1,0:T(8,128)(2,1)} %get-tuple-element.54.refs_4_) | copy-start | bytes 1572868
  101.7 8.5 %copy-start.16 = (bf16[128,256]{1,0:T(8,128)(2,1)S(1)}, bf16[128,256]{1,0:T(8,128)(2,1)}, u32[]{:S(2)}) copy-start(bf16[128,256]{1,0:T(8,128)(2,1)} %weight.7) | copy-start | bytes 196612
  101.7 14.8 %collective-permute-start.24 = (bf16[16,128,128]{2,1,0:T(8,128)(2,1)S(1)}, bf16[16,128,128]{2,1,0:T(8,128)(2,1)S(1)}, u32[]{:S(2)}, u32[]{:S(2)}) collective-permute-start(bf16[16,128,128]{2,1,0:T(8,128)(2,1)S(1)} %get-tuple-element.65), channel_id=1, source_target_pairs={{0,1},{1,0},{2,3},{3,2},{4,5},{5,4},{6,7},{7,6},{8,16},{9,17},{10,... | collective-permute-start | bytes 1572872 | tf_op jit(solution)/shard_map/ppermute | solution.py:464
  101.7 7.3 %collective-permute-start.18 = (bf16[16,64,128]{2,1,0:T(8,128)(2,1)S(1)}, bf16[16,64,128]{2,1,0:T(8,128)(2,1)S(1)}, u32[]{:S(2)}, u32[]{:S(2)}) collective-permute-start(bf16[16,64,128]{2,1,0:T(8,128)(2,1)S(1)} %get-tuple-element.52), channel_id=1, source_target_pairs={{0,1},{1,0},{2,3},{3,2},{4,5},{5,4},{6,7},{7,6},{8,9},{9,8},{10,11... | collective-permute-start | bytes 786440 | tf_op jit(solution)/shard_map/ppermute | solution.py:456
  102.3 8.0 %copy-start.7 = (bf16[64,256,128]{2,1,0:T(8,128)(2,1)S(1)}, bf16[64,256,128]{2,1,0:T(8,128)(2,1)}, u32[]{:S(2)}) copy-start(bf16[64,256,128]{2,1,0:T(8,128)(2,1)} %copy-done.6) | copy-start | bytes 12582916
  108.3 1.5 %collective-permute-start.19 = (bf16[16,64,128]{2,1,0:T(8,128)(2,1)S(1)}, bf16[16,64,128]{2,1,0:T(8,128)(2,1)S(1)}, u32[]{:S(2)}, u32[]{:S(2)}) collective-permute-start(bf16[16,64,128]{2,1,0:T(8,128)(2,1)S(1)} %get-tuple-element.53), channel_id=1, source_target_pairs={{0,1},{1,0},{2,3},{3,2},{4,5},{5,4},{6,7},{7,6},{8,9},{9,8},{10,11... | collective-permute-start | bytes 786440 | tf_op jit(solution)/shard_map/ppermute | solution.py:456
  108.5 1.7 %collective-permute-start.22 = (bf16[16,64,128]{2,1,0:T(8,128)(2,1)S(1)}, bf16[16,64,128]{2,1,0:T(8,128)(2,1)S(1)}, u32[]{:S(2)}, u32[]{:S(2)}) collective-permute-start(bf16[16,64,128]{2,1,0:T(8,128)(2,1)S(1)} %add_convert_fusion.5), channel_id=1, source_target_pairs={{0,1},{1,0},{2,3},{3,2},{4,5},{5,4},{6,7},{7,6},{8,9},{9,8},{10,11... | collective-permute-start | bytes 786440 | tf_op jit(solution)/shard_map/ppermute | solution.py:456
  110.2 6.4 %copy-start.14 = (bf16[16,128,128]{2,1,0:T(8,128)(2,1)S(1)}, bf16[16,128,128]{2,1,0:T(8,128)(2,1)}, u32[]{:S(2)}) copy-start(bf16[16,128,128]{2,1,0:T(8,128)(2,1)} %get-tuple-element.64.partials) | copy-start | bytes 1572868
  110.2 8.1 %copy-start.9 = (bf16[64,128,128]{2,1,0:T(8,128)(2,1)S(1)}, bf16[64,128,128]{2,1,0:T(8,128)(2,1)}, u32[]{:S(2)}) copy-start(bf16[64,128,128]{2,1,0:T(8,128)(2,1)} %copy-done.8) | copy-start | bytes 6291460
  110.2 8.1 %copy-start.18 = (bf16[64,64,128]{2,1,0:T(8,128)(2,1)S(1)}, bf16[64,64,128]{2,1,0:T(8,128)(2,1)}, u32[]{:S(2)}) copy-start(bf16[64,64,128]{2,1,0:T(8,128)(2,1)} %copy-done.17) | copy-start | bytes 3145732
  110.2 8.1 %copy-start.20 = (f32[128]{0:T(128)S(1)}, f32[128]{0:T(128)}, u32[]{:S(2)}) copy-start(f32[128]{0:T(128)} %param.8) | copy-start | bytes 1540
  116.7 1.6 %collective-permute-start.25 = (bf16[16,64,128]{2,1,0:T(8,128)(2,1)S(1)}, bf16[16,64,128]{2,1,0:T(8,128)(2,1)S(1)}, u32[]{:S(2)}, u32[]{:S(2)}) collective-permute-start(bf16[16,64,128]{2,1,0:T(8,128)(2,1)S(1)} %add_convert_fusion.4), channel_id=1, source_target_pairs={{0,1},{1,0},{2,3},{3,2},{4,5},{5,4},{6,7},{7,6},{8,9},{9,8},{10,11... | collective-permute-start | bytes 786440 | tf_op jit(solution)/shard_map/ppermute | solution.py:456
  (2 other events, 2.4 us)

commit v9 on v8

--- a/solution.py
+++ b/solution.py
@@ -16,6 +16,7 @@
 PARAMS = pltpu.CompilerParams(vmem_limit_bytes=VMEM_LIMIT)
 FRONT_COST = pl.CostEstimate(flops=1, bytes_accessed=18_000_000, transcendentals=0)
 COST = pl.CostEstimate(flops=1, bytes_accessed=8_000_000, transcendentals=0)
+WHOLE = pl.BlockSpec(memory_space=pltpu.VMEM)
 BY_LAST = (((1,), (1,)), ((), ()))
 
 
@@ -169,14 +170,34 @@
     )(tile_mask, *in_hbm(pair, gain, bias, proj_weight))
 
 
-def pack_kernel(own, other, out, mine, sem):
-    cols, half, _ = other.shape
+def half_kernel(theirs, raw, out, sem):
+    half = out.shape[1]
     core = this_core()
-    copy = pltpu.make_async_copy(own.at[:, pl.ds(pl.multiple_of(core * half, half), half), :], mine, sem)
+    first = pl.multiple_of((1 - core if theirs else core) * half, half)
+    copy = pltpu.make_async_copy(raw.at[:, pl.ds(first, half), :], out, sem)
     copy.start()
-    out[:, pl.ds(pl.multiple_of((1 - core) * cols, cols), cols), :] = jnp.transpose(other[...], (1, 0, 2))
     copy.wait()
-    out[:, pl.ds(pl.multiple_of(core * cols, cols), cols), :] = jnp.transpose(mine[...], (1, 0, 2))
+
+
+def take_half(raw, theirs):
+    cols, hidden, rows = raw.shape
+    return pl.pallas_call(
+        functools.partial(half_kernel, theirs),
+        out_shape=jax.ShapeDtypeStruct((cols, hidden // CORES, rows), raw.dtype),
+        in_specs=[pl.BlockSpec(memory_space=pl.ANY)],
+        out_specs=WHOLE,
+        scratch_shapes=[pltpu.SemaphoreType.DMA],
+        compiler_params=PARAMS,
+        cost_estimate=COST,
+        name="theirs" if theirs else "mine",
+    )(*in_hbm(raw))
+
+
+def pack_kernel(own, other, out):
+    cols = other.shape[0]
+    core = this_core()
+    for block, place in ((own, core), (other, 1 - core)):
+        out[:, pl.ds(pl.multiple_of(place * cols, cols), cols), :] = jnp.transpose(block[...], (1, 0, 2))
 
 
 def pack(own, other):
@@ -184,12 +205,12 @@
     return pl.pallas_call(
         pack_kernel,
         out_shape=jax.ShapeDtypeStruct((half, CORES * cols, rows), jnp.bfloat16),
-        in_specs=[pl.BlockSpec(memory_space=pl.ANY), pl.BlockSpec(memory_space=pltpu.VMEM)],
-        scratch_shapes=[pltpu.VMEM((cols, half, rows), jnp.bfloat16), pltpu.SemaphoreType.DMA],
+        in_specs=[WHOLE] * 2,
+        out_specs=WHOLE,
         compiler_params=PARAMS,
         cost_estimate=COST,
         name="pack",
-    )(*in_hbm(own), other)
+    )(own, other)
 
 
 def chunk_spec(array, chans, chunk):
@@ -197,21 +218,19 @@
     return pl.BlockSpec((STEP,) + array.shape[1:], lambda g: (first + g, 0, 0))
 
 
-def cut_kernel(*refs):
-    count = len(refs) // 2
-    for source, out in zip(refs[:count], refs[count:]):
-        out[...] = source[...]
+def cut_kernel(chunks, *refs):
+    for source, out, chunk in zip(refs, refs[len(chunks) :], chunks):
+        chans = out.shape[0]
+        out[...] = source[chunk * chans : (chunk + 1) * chans]
 
 
 def cut(arrays, chunks):
-    chans = arrays[0].shape[0] // CHUNKS
-    shape = (chans,) + arrays[0].shape[1:]
-    return pl.pallas_call(
-        cut_kernel,
+    shape = (arrays[0].shape[0] // CHUNKS,) + arrays[0].shape[1:]
+    return pl.pallas_call(
+        functools.partial(cut_kernel, chunks),
         out_shape=[jax.ShapeDtypeStruct(shape, jnp.bfloat16)] * len(arrays),
-        grid=(chans // STEP,),
-        in_specs=[chunk_spec(v, chans, c) for v, c in zip(arrays, chunks)],
-        out_specs=[pl.BlockSpec((STEP,) + shape[1:], lambda g: (g, 0, 0))] * len(arrays),
+        in_specs=[WHOLE] * len(arrays),
+        out_specs=[WHOLE] * len(arrays),
         compiler_params=PARAMS,
         cost_estimate=FRONT_COST,
         name="cut",
@@ -234,31 +253,63 @@
     return out_a.astype(jnp.bfloat16), out_b.astype(jnp.bfloat16)
 
 
-def partial_kernel(n, left_mine, left_other, by_a, by_b, *refs):
-    blocks, outs, (next_a, next_b, sums) = refs[:n], refs[n : 2 * n], refs[2 * n :]
+def first_kernel(chunk, left_mine, left_other, by_a, by_b, *refs):
+    *blocks, next_a, next_b = refs
+    n = len(blocks)
+    chip, target = lax.axis_index("col") // CORES, jnp.where(lax.axis_index("row") == 0, n - 1, 0)
+    slot = jnp.bitwise_xor(chip, target)
+    chans = next_a.shape[0]
+    for c in range(chans):
+        at = chunk * chans + c
+        lhs = jnp.concatenate((left_mine[at], left_other[at]), axis=0)
+        rhs = blocks[0][at]
+        for m in range(1, n):
+            rhs = jnp.where(slot == m, blocks[m][at if blocks[m].shape[0] > chans else c], rhs)
+        sums = lax.dot_general(lhs, rhs, BY_LAST, preferred_element_type=jnp.float32).astype(jnp.bfloat16)
+        next_a[c], next_b[c] = onward(by_a[at], by_b[at], sums, sums, 1, n)
+
+
+def first_step(left_mine, left_other, by_a, by_b, blocks, chunk):
+    shape = (left_mine.shape[0] // CHUNKS,) + by_a.shape[1:]
+    args = (left_mine, left_other, by_a, by_b, *blocks)
+    return pl.pallas_call(
+        functools.partial(first_kernel, chunk),
+        out_shape=[jax.ShapeDtypeStruct(shape, jnp.bfloat16)] * 2,
+        in_specs=[WHOLE] * len(args),
+        out_specs=[WHOLE] * 2,
+        compiler_params=PARAMS,
+        cost_estimate=COST,
+        name="first_step",
+    )(*args)
+
+
+def partial_kernel(n, chunk, left_mine, left_other, *refs):
+    blocks, outs, sums = refs[:n], refs[n : 2 * n], refs[2 * n]
     row, chip = lax.axis_index("row"), lax.axis_index("col") // CORES
+    chans = left_mine.shape[0] // CHUNKS
+    step = pl.program_id(0) * STEP
+    first = chunk * chans + step
     for c in range(STEP):
-        lhs = jnp.concatenate((left_mine[c], left_other[c]), axis=0)
+        lhs = jnp.concatenate((left_mine[first + c], left_other[first + c]), axis=0)
         for m, block in enumerate(blocks):
             away = lax.rem(jnp.bitwise_xor(chip, m) - row + n, n)
-            sums[away, c] = lax.dot_general(lhs, block[c], BY_LAST, preferred_element_type=jnp.float32).astype(jnp.bfloat16)
+            rhs = block[(first if block.shape[0] > chans else step) + c]
+            sums[away, c] = lax.dot_general(lhs, rhs, BY_LAST, preferred_element_type=jnp.float32).astype(jnp.bfloat16)
     for s, out in enumerate(outs):
         out[...] = sums[s]
-    next_a[...], next_b[...] = onward(by_a[...], by_b[...], sums[n - 1], sums[1], 1, n)
-
-
-def partial_products(left_mine, left_other, by_a, by_b, blocks, chunk):
+
+
+def partial_products(left_mine, left_other, blocks, chunk):
     rows = blocks[0].shape[1]
     ks, chans = left_mine.shape[1], left_mine.shape[0] // CHUNKS
     n = len(blocks)
-    args = (left_mine, left_other, by_a, by_b, *blocks)
-    return pl.pallas_call(
-        functools.partial(partial_kernel, n),
-        out_shape=[pltpu.HBM((chans, CORES * ks, rows), jnp.bfloat16)] * n
-        + [jax.ShapeDtypeStruct((chans, CORES * ks, rows), jnp.bfloat16)] * 2,
+    args = (left_mine, left_other, *blocks)
+    return pl.pallas_call(
+        functools.partial(partial_kernel, n, chunk),
+        out_shape=[pltpu.HBM((chans, CORES * ks, rows), jnp.bfloat16)] * n,
         grid=(chans // STEP,),
-        in_specs=[chunk_spec(v, chans, chunk) for v in args],
-        out_specs=[pl.BlockSpec((STEP, CORES * ks, rows), lambda g: (g, 0, 0))] * (n + 2),
+        in_specs=[WHOLE] * len(args),
+        out_specs=[pl.BlockSpec((STEP, CORES * ks, rows), lambda g: (g, 0, 0))] * n,
         scratch_shapes=[pltpu.VMEM((n, STEP, CORES * ks, rows), jnp.bfloat16)],
         compiler_params=PARAMS,
         cost_estimate=COST,
@@ -376,29 +427,29 @@
 
 
 def tail_kernel(n, base, scaled, inverse, last, gain, weight, partials, by_a, by_b, right_other, out, results, flipped, grads, flat, gain_col):
-    keys, chans, rows = scaled.shape
-    hidden = weight.shape[1] // 4
+    _, keys, chans = out.shape
+    rows = scaled.shape[2]
     core = this_core()
 
     @pl.when(pl.program_id(0) == 0)
     def _():
         gain_col[...] = column(gain, rows)
-        grads[...] = jnp.zeros_like(grads)
-
-    put(flat, core, arrived_total(partials[...], by_a[...], by_b[...], n))
-    put(flat, 1 - core, right_other[...])
-    places = last_rows(hidden)
-    for key in range(keys):
-        grad = flat[pl.ds(key, 2 * hidden // len(places) // CHUNKS * CORES, stride=keys), :]
-        for i, (first, size) in enumerate(places):
-            factor = last[key, i * size : (i + 1) * size, :].astype(jnp.float32)
-            owner = i % CORES
-            grads[key, first : first + size, :] = (grad[owner * size : (owner + 1) * size] * factor).astype(jnp.bfloat16)
-    for key in range(keys):
-        scaled_key = scaled[key].astype(jnp.float32)
+
+    first_key = pl.program_id(0) * keys
+    here = pl.ds(pl.multiple_of(first_key, keys), keys)
+    put(flat, core, arrived_total(partials[:, here, :], by_a[:, here, :], by_b[:, here, :], n))
+    put(flat, 1 - core, right_other[:, here, :])
+    count = last.shape[1] // 2
+    for key in range(keys):
+        grad = flat[pl.ds(key, count, stride=keys), :]
+        for kind in range(2):
+            place = slice(kind * count, (kind + 1) * count)
+            grads[key, place, :] = (grad * last[first_key + key, place, :].astype(jnp.float32)).astype(jnp.bfloat16)
+    for key in range(keys):
+        scaled_key = scaled[first_key + key].astype(jnp.float32)
         added = jnp.dot(weight[...], grads[key], preferred_element_type=jnp.float32)
-        scaled_grad = (base[key] + added) * gain_col[...]
-        result = inverse[key] * (
+        scaled_grad = (base[first_key + key] + added) * gain_col[...]
+        result = inverse[first_key + key] * (
             scaled_grad
             - jnp.mean(scaled_grad, axis=0, keepdims=True)
             - scaled_key * jnp.mean(scaled_grad * scaled_key, axis=0, keepdims=True)
@@ -412,34 +463,25 @@
 
 def tail(base, scaled, inverse, last, gain, proj_weight, partials, by_a, by_b, right_other):
     cols, chans, rows = scaled.shape
-    width = proj_weight.shape[1]
-    part = width // 4 // CORES // CHUNKS
-    by_key = lambda *shape: pl.BlockSpec((KEYS,) + shape, lambda g: (g, 0, 0))
+    hidden, part = proj_weight.shape[1] // 4, partials.shape[0]
+    weight = jnp.concatenate([proj_weight[:, first : first + size] for first, size in last_rows(hidden)], axis=1)
     return pl.pallas_call(
         functools.partial(tail_kernel, lax.axis_size("row")),
         out_shape=jax.ShapeDtypeStruct((rows, cols, chans), jnp.bfloat16),
         grid=(cols // KEYS,),
-        in_specs=[
-            by_key(chans, rows),
-            by_key(chans, rows),
-            by_key(1, rows),
-            by_key(last.shape[1], rows),
-            pl.BlockSpec((1, chans), lambda g: (0, 0)),
-            pl.BlockSpec((chans, width), lambda g: (0, 0)),
-        ]
-        + [pl.BlockSpec((part, KEYS, rows), lambda g: (0, g, 0))] * 4,
+        in_specs=[WHOLE] * 10,
         out_specs=pl.BlockSpec((rows, KEYS, chans), lambda g: (0, g, 0)),
         scratch_shapes=[
             pltpu.VMEM((KEYS, chans, rows), jnp.bfloat16),
             pltpu.VMEM((KEYS, rows, chans), jnp.bfloat16),
-            pltpu.VMEM((KEYS, width, rows), jnp.bfloat16),
+            pltpu.VMEM((KEYS, last.shape[1], rows), jnp.bfloat16),
             pltpu.VMEM((CORES * part * KEYS, rows), jnp.float32),
             pltpu.VMEM((chans, rows), jnp.float32),
         ],
         compiler_params=PARAMS,
         cost_estimate=COST,
         name="tail",
-    )(base, scaled, inverse, last, gain, proj_weight, partials, by_a, by_b, right_other)
+    )(base, scaled, inverse, last, gain, weight, partials, by_a, by_b, right_other)
 
 
 def after(value, *others):
@@ -464,8 +506,8 @@
         return lax.ppermute(value, ("row", "col"), perm)
 
     raw = jnp.transpose(grad_x, (1, 2, 0))
-    other = exchange(lax.dynamic_slice_in_dim(raw, (1 - this_core()) * half, half, 1), 1)
-    packed = pack(raw, other)
+    other = exchange(take_half(raw, True), 1)
+    packed = pack(take_half(raw, False), other)
 
     axes = {m: [1 << b for b in range(m.bit_length()) if m >> b & 1] for m in range(n_col // CORES)}
     whole = {m: exchange(packed, CORES * m) for m in axes if len(axes[m]) == 1}
@@ -488,8 +530,8 @@
 
     by_a, by_b, partials = [], [], []
     for c in range(CHUNKS):
-        *sums, next_a, next_b = partial_products(left_mine, left_other, first_a, first_b, panels[c], c)
-        partials.append(sums)
+        next_a, next_b = first_step(left_mine, left_other, first_a, first_b, panels[c], c)
+        partials.append(partial_products(left_mine, left_other, panels[c], c))
         by_a.append([first_a, hop(next_a, 0)])
         by_b.append([first_b, hop(next_b, 1)])
 

time: 125 us -> 122 us (0.976)
  waiting for transfers between devices: 48.8 us -> 40.4 us
  Pallas kernels: 33.2 us -> 36.5 us
  local copies, waits for them, and re-layouts: 5.55 us -> 7.68 us
    ppermute x14, waiting for transfers between devices: 34.7 us -> 27.6 us  [hop(): return lax.ppermute(value, ('row', 'col'), perm)]
    pallas_call x3 -> x7, Pallas kernels: 6.25 us -> 11 us  [the longest x2 5.48 us: partial_products(): pl.pallas_call(functools.partial(partial_kernel, n, chunk), out_shape=[pl...]
    unnamed x48 -> x58, local copies, waits for them, and re-layouts: 4.42 us -> 7.54 us
    ppermute x12, waiting for transfers between devices: 14.1 us -> 12.8 us  [exchange(): return lax.ppermute(value, 'col', [(d, d ^ mask) for d in range(n_col)])]
  transfers between devices with their start and end apart: 26 -> 26, of which waited for: 16 -> 16; matrix products, arithmetic and copies ran while one was open for 8% -> 8% of each run, Pallas kernels for 21% -> 24%
where the time goes in v9:
time: 122 us; the launch traced here: 121 us
  waiting for transfers between devices  40.4 us (33%)
  Pallas kernels  36.5 us (30%)
  starting transfers between devices  26.6 us (22%)
  other arithmetic  9.98 us (8%)
  local copies, waits for them, and re-layouts  7.68 us (6%)
    ppermute x14, waiting for transfers between devices, hop(): return lax.ppermute(value, ('row', 'col'), perm)  27.6 us
    ppermute x14, starting transfers between devices, hop(): return lax.ppermute(value, ('row', 'col'), perm)  17.3 us
    ppermute x12, waiting for transfers between devices, exchange(): return lax.ppermute(value, 'col', [(d, d ^ mask) for d in range(n_col)])  12.8 us
    pallas_call x2, Pallas kernels, front(): pl.pallas_call(right_kernel if right else left_forward_kernel, out_shape=...  11.2 us
    convert_element_type x4, other arithmetic, onward(): return (out_a.astype(jnp.bfloat16), out_b.astype(jnp.bfloat16))  9.51 us
    ppermute x12, starting transfers between devices, exchange(): return lax.ppermute(value, 'col', [(d, d ^ mask) for d in range(n_col)])  9.32 us
    unnamed x58, local copies, waits for them, and re-layouts  7.54 us
    pallas_call x2, Pallas kernels, partial_products(): pl.pallas_call(functools.partial(partial_kernel, n, chunk), out_shape=[pl...  5.48 us
  transfers between devices with their start and end apart: 26, of which 16 were waited for; matrix products, arithmetic and copies ran while one was open for 8% of the time, Pallas kernels for 24%

profile of v9, /device:TPU:0, one launch (start us, length us, event | category | flops | bytes accessed | tf_op | source)
XLA Modules:
  0.0 121.5 jit_solution(2848169340910181543)
XLA Ops:
  0.0 1.0 theirs.1
  1.6 1.0 mine.1.own
  3.5 2.9 %collective-permute-start.6 = (bf16[32,128,128]{2,1,0:T(8,128)(2,1)S(1)}, bf16[32,128,128]{2,1,0:T(8,128)(2,1)S(1)}, u32[]{:S(2)}, u32[]{:S(2)}) collective-permute-start(bf16[32,128,128]{2,1,0:T(8,128)(2,1)S(1)} %pack.1.refs_0_.refs_6_), channel_id=1, source_target_pairs={{0,2},{1,3},{2,0},{3,1},{4,6},{5,7},{6,4},{7,5},{8,10},{9,11},{10,... | collective-permute-start | bytes 3145736 | tf_op jit(solution)/shard_map/ppermute | solution.py:498
  6.4 1.5 %collective-permute-start.7 = (bf16[32,128,128]{2,1,0:T(8,128)(2,1)S(1)}, bf16[32,128,128]{2,1,0:T(8,128)(2,1)S(1)}, u32[]{:S(2)}, u32[]{:S(2)}) collective-permute-start(bf16[32,128,128]{2,1,0:T(8,128)(2,1)S(1)} %pack.1.refs_0_.refs_6_), channel_id=1, source_target_pairs={{0,4},{1,5},{2,6},{3,7},{4,0},{5,1},{6,2},{7,3},{8,12},{9,13},{10,... | collective-permute-start | bytes 3145736 | tf_op jit(solution)/shard_map/ppermute | solution.py:498
  7.9 5.1 %right_front.1 = (bf16[32,64,128]{2,1,0:T(8,128)(2,1)S(1)}, bf16[32,64,128]{2,1,0:T(8,128)(2,1)S(1)}) custom-call(s32[4,4]{1,0:T(4,128)S(1)} %copy-done.25, bf16[128,64,128]{2,1,0:T(8,128)(2,1)} %pair.1, f32[1,128]{1,0:T(1,128)} %bitcast.3, f32[1,128]{1,0:T(1,128)} %bitcast.8, bf16[128,256]{1,0:T(8,128)(2,1)} %weight.5), custom_call_target="tpu_custom_call" | custom-call | flops 1 | bytes 18000000 | tf_op jit(solution)/shard_map/right_front/pallas_call | solution.py:145
  13.7 1.0 collective-permute-done.2
  15.2 1.6 %collective-permute-start.3 = (bf16[32,128,128]{2,1,0:T(8,128)(2,1)S(1)}, bf16[32,128,128]{2,1,0:T(8,128)(2,1)S(1)}, u32[]{:S(2)}, u32[]{:S(2)}) collective-permute-start(bf16[32,128,128]{2,1,0:T(8,128)(2,1)S(1)} %maximum_maximum_fusion.own), channel_id=1, source_target_pairs={{0,8},{1,9},{2,10},{3,11},{4,12},{5,13},{6,14},{7,15},{8,0},{9,1},... | collective-permute-start | bytes 3145736 | tf_op jit(solution)/shard_map/ppermute | solution.py:506
  16.8 6.0 %left_front.1 = (bf16[32,64,128]{2,1,0:T(8,128)(2,1)S(1)}, bf16[32,64,128]{2,1,0:T(8,128)(2,1)S(1)}, bf16[64,128,128]{2,1,0:T(8,128)(2,1)S(1)}, f32[64,1,128]{2,...) custom-call(s32[4,4]{1,0:T(4,128)S(1)} %copy-done.25, bf16[128,64,128]{2,1,0:T(8,128)(2,1)} %pair.1, ...), custom_call_target="tpu_custom_call" | custom-call | flops 1 | bytes 18000000 | tf_op jit(solution)/shard_map/left_front/pallas_call | solution.py:145
  22.9 2.0 %copy-done.16 = bf16[64,256,128]{2,1,0:T(8,128)(2,1)} copy-done((bf16[64,256,128]{2,1,0:T(8,128)(2,1)}, bf16[64,256,128]{2,1,0:T(8,128)(2,1)S(1)}, u32[]{:S(2)}) %copy-start.16) | copy-done | bytes 4194328
  24.8 1.3 %copy-done.18 = bf16[64,128,128]{2,1,0:T(8,128)(2,1)} copy-done((bf16[64,128,128]{2,1,0:T(8,128)(2,1)}, bf16[64,128,128]{2,1,0:T(8,128)(2,1)S(1)}, u32[]{:S(2)}) %copy-start.18) | copy-done | bytes 2097176
  26.2 0.5 collective-permute-start.4
  26.7 3.2 %collective-permute-done.6.refs_0_.refs_1_.refs_7_ = bf16[32,128,128]{2,1,0:T(8,128)(2,1)S(1)} collective-permute-done((bf16[32,128,128]{2,1,0:T(8,128)(2,1)S(1)}, bf16[32,128,128]{2,1,0:T(8,128)(2,1)S(1)}, u32[]{:S(2)}, u32[]{:S(2)}) %collective-permute-start.6) | collective-permute-done | bytes 1048608 | tf_op jit(solution)/shard_map/ppermute | solution.py:498
  29.8 1.5 %collective-permute-done.7.refs_1_.refs_2_.refs_8_ = bf16[32,128,128]{2,1,0:T(8,128)(2,1)S(1)} collective-permute-done((bf16[32,128,128]{2,1,0:T(8,128)(2,1)S(1)}, bf16[32,128,128]{2,1,0:T(8,128)(2,1)S(1)}, u32[]{:S(2)}, u32[]{:S(2)}) %collective-permute-start.7) | collective-permute-done | bytes 1048608 | tf_op jit(solution)/shard_map/ppermute | solution.py:498
  31.4 1.6 %collective-permute-start.8 = (bf16[16,128,128]{2,1,0:T(8,128)(2,1)S(1)}, bf16[16,128,128]{2,1,0:T(8,128)(2,1)S(1)}, u32[]{:S(2)}, u32[]{:S(2)}) collective-permute-start(bf16[16,128,128]{2,1,0:T(8,128)(2,1)S(1)} %get-tuple-element.42), channel_id=1, source_target_pairs={{0,4},{1,5},{2,6},{3,7},{4,0},{5,1},{6,2},{7,3},{8,12},{9,13},{10,... | collective-permute-start | bytes 1572872 | tf_op jit(solution)/shard_map/ppermute | solution.py:498
  33.0 0.5 collective-permute-start.13
  33.5 6.9 %collective-permute-done.3.by_a.refs_0_ = bf16[32,128,128]{2,1,0:T(8,128)(2,1)S(1)} collective-permute-done((bf16[32,128,128]{2,1,0:T(8,128)(2,1)S(1)}, bf16[32,128,128]{2,1,0:T(8,128)(2,1)S(1)}, u32[]{:S(2)}, u32[]{:S(2)}) %collective-permute-start.3) | collective-permute-done | bytes 1048608 | tf_op jit(solution)/shard_map/ppermute | solution.py:506
  40.4 3.8 %collective-permute-done.8.refs_3_.refs_9_ = bf16[16,128,128]{2,1,0:T(8,128)(2,1)S(1)} collective-permute-done((bf16[16,128,128]{2,1,0:T(8,128)(2,1)S(1)}, bf16[16,128,128]{2,1,0:T(8,128)(2,1)S(1)}, u32[]{:S(2)}, u32[]{:S(2)}) %collective-permute-start.8) | collective-permute-done | bytes 524320 | tf_op jit(solution)/shard_map/ppermute | solution.py:498
  44.3 1.7 %first_step.2 = (bf16[16,128,128]{2,1,0:T(8,128)(2,1)}, bf16[16,128,128]{2,1,0:T(8,128)(2,1)}) custom-call(bf16[32,64,128]{2,1,0:T(8,128)(2,1)S(1)} %get-tuple-element.40.left_mine, bf16[32,64,128]{2,1,0:T(8,128)(2,1)S(1)} %collective-permute-done.4.left_other, bf16[32,128,128]{2,1,0:T(8,128)(2,1)S(1)} %collective-permute-done.3.by_a.refs_0_, ...), custom_call_target="tpu_custom_call" | custom-call | flops 1 | bytes 8000000 | tf_op jit(solution)/shard_map/first_step/pallas_call | solution.py:275
  46.0 1.6 %collective-permute-start.9 = (bf16[16,128,128]{2,1,0:T(8,128)(2,1)}, bf16[16,128,128]{2,1,0:T(8,128)(2,1)}, u32[]{:S(2)}, u32[]{:S(2)}) collective-permute-start(bf16[16,128,128]{2,1,0:T(8,128)(2,1)} %get-tuple-element.43), channel_id=1, source_target_pairs={{0,8},{1,9},{2,10},{3,11},{4,12},{5,13},{6,14},{7,15},{8,0},{9,1},... | collective-permute-start | bytes 1572872 | tf_op jit(solution)/shard_map/ppermute | solution.py:506
  47.6 1.7 %first_step.3 = (bf16[16,128,128]{2,1,0:T(8,128)(2,1)}, bf16[16,128,128]{2,1,0:T(8,128)(2,1)}) custom-call(bf16[32,64,128]{2,1,0:T(8,128)(2,1)S(1)} %get-tuple-element.40.left_mine, bf16[32,64,128]{2,1,0:T(8,128)(2,1)S(1)} %collective-permute-done.4.left_other, bf16[32,128,128]{2,1,0:T(8,128)(2,1)S(1)} %collective-permute-done.3.by_a.refs_0_, ...), custom_call_target="tpu_custom_call" | custom-call | flops 1 | bytes 8000000 | tf_op jit(solution)/shard_map/first_step/pallas_call | solution.py:275
  49.3 3.1 %collective-permute-start.14 = (bf16[16,128,128]{2,1,0:T(8,128)(2,1)}, bf16[16,128,128]{2,1,0:T(8,128)(2,1)}, u32[]{:S(2)}, u32[]{:S(2)}) collective-permute-start(bf16[16,128,128]{2,1,0:T(8,128)(2,1)} %get-tuple-element.48), channel_id=1, source_target_pairs={{0,8},{1,9},{2,10},{3,11},{4,12},{5,13},{6,14},{7,15},{8,0},{9,1},... | collective-permute-start | bytes 1572872 | tf_op jit(solution)/shard_map/ppermute | solution.py:506
  52.4 1.0 copy-done.7
  53.5 1.0 copy-done.9
  54.5 1.0 copy-done.14
  55.6 2.7 %right_partials.2 = (bf16[16,128,128]{2,1,0:T(8,128)(2,1)}, bf16[16,128,128]{2,1,0:T(8,128)(2,1)}, bf16[16,128,128]{2,1,0:T(8,128)(2,1)}, bf16[16,128,128]{2,1,0:T(8,128)(2,1)}) custom-call(bf16[32,64,128]{2,1,0:T(8,128)(2,1)S(1)} %copy-done.7, bf16[32,64,128]{2,1,0:T(8,128)(2,1)S(1)} %copy-done.9, bf16[32,128,128]{2,1,0:T(8,128)(2,1)S(1)} %pack.1.refs_0_.refs_6_, ...), custom_call_target="tpu_custom_call" | custom-call | flops 1 | bytes 8000000 | tf_op jit(solution)/shard_map/right_partials/pallas_call | solution.py:307
  58.3 2.9 %collective-permute-done.9.refs_1_ = bf16[16,128,128]{2,1,0:T(8,128)(2,1)} collective-permute-done((bf16[16,128,128]{2,1,0:T(8,128)(2,1)}, bf16[16,128,128]{2,1,0:T(8,128)(2,1)}, u32[]{:S(2)}, u32[]{:S(2)}) %collective-permute-start.9) | collective-permute-done | bytes 524320 | tf_op jit(solution)/shard_map/ppermute | solution.py:506
  61.2 2.8 %fusion.11 = (bf16[16,128,128]{2,1,0:T(8,128)(2,1)}, bf16[16,128,128]{2,1,0:T(8,128)(2,1)}) fusion(bf16[16,128,128]{2,1,0:T(8,128)(2,1)} %get-tuple-element.45, bf16[16,128,128]{2,1,0:T(8,128)(2,1)} %collective-permute-done.9.refs_1_, pred[]{:T(512)S(6)} %select_n.163, pred[]{:T(512)S(6)} %ge.8, pred[]{:T(512)S(6)} %lt.7, pred[]{:T(512)S(6)} %eq.2, ...), kind=kLoop, calls=%fused_computation.15 | loop fusion | flops 3407872 | bytes 2621445 | tf_op jit(solution)/shard_map/convert_element_type | solution.py:253
  64.0 2.7 %collective-permute-start.11 = (bf16[16,128,128]{2,1,0:T(8,128)(2,1)}, bf16[16,128,128]{2,1,0:T(8,128)(2,1)}, u32[]{:S(2)}, u32[]{:S(2)}) collective-permute-start(bf16[16,128,128]{2,1,0:T(8,128)(2,1)} %get-tuple-element.72), channel_id=1, source_target_pairs={{0,8},{1,9},{2,10},{3,11},{4,12},{5,13},{6,14},{7,15},{8,0},{9,1},... | collective-permute-start | bytes 1572872 | tf_op jit(solution)/shard_map/ppermute | solution.py:506
  66.7 2.8 %right_partials.3 = (bf16[16,128,128]{2,1,0:T(8,128)(2,1)}, bf16[16,128,128]{2,1,0:T(8,128)(2,1)}, bf16[16,128,128]{2,1,0:T(8,128)(2,1)}, bf16[16,128,128]{2,1,0:T(8,128)(2,1)}) custom-call(bf16[32,64,128]{2,1,0:T(8,128)(2,1)S(1)} %copy-done.7, bf16[32,64,128]{2,1,0:T(8,128)(2,1)S(1)} %copy-done.9, bf16[32,128,128]{2,1,0:T(8,128)(2,1)S(1)} %pack.1.refs_0_.refs_6_, ...), custom_call_target="tpu_custom_call" | custom-call | flops 1 | bytes 8000000 | tf_op jit(solution)/shard_map/right_partials/pallas_call | solution.py:307
  69.5 2.9 %collective-permute-done.14.refs_1_ = bf16[16,128,128]{2,1,0:T(8,128)(2,1)} collective-permute-done((bf16[16,128,128]{2,1,0:T(8,128)(2,1)}, bf16[16,128,128]{2,1,0:T(8,128)(2,1)}, u32[]{:S(2)}, u32[]{:S(2)}) %collective-permute-start.14) | collective-permute-done | bytes 524320 | tf_op jit(solution)/shard_map/ppermute | solution.py:506
  72.4 2.9 %fusion.7 = (bf16[16,128,128]{2,1,0:T(8,128)(2,1)}, bf16[16,128,128]{2,1,0:T(8,128)(2,1)}) fusion(bf16[16,128,128]{2,1,0:T(8,128)(2,1)} %get-tuple-element.50, bf16[16,128,128]{2,1,0:T(8,128)(2,1)} %collective-permute-done.14.refs_1_, pred[]{:T(512)S(6)} %select_n.163, pred[]{:T(512)S(6)} %ge.8, pred[]{:T(512)S(6)} %lt.7, pred[]{:T(512)S(6)} %eq.2, ...), kind=kLoop, calls=%fused_computation.11 | loop fusion | flops 3407872 | bytes 2621445 | tf_op jit(solution)/shard_map/convert_element_type | solution.py:253
  75.3 2.7 %collective-permute-start.16 = (bf16[16,128,128]{2,1,0:T(8,128)(2,1)}, bf16[16,128,128]{2,1,0:T(8,128)(2,1)}, u32[]{:S(2)}, u32[]{:S(2)}) collective-permute-start(bf16[16,128,128]{2,1,0:T(8,128)(2,1)} %get-tuple-element.70), channel_id=1, source_target_pairs={{0,8},{1,9},{2,10},{3,11},{4,12},{5,13},{6,14},{7,15},{8,0},{9,1},... | collective-permute-start | bytes 1572872 | tf_op jit(solution)/shard_map/ppermute | solution.py:506
  78.0 5.6 %collective-permute-done.11.refs_2_ = bf16[16,128,128]{2,1,0:T(8,128)(2,1)} collective-permute-done((bf16[16,128,128]{2,1,0:T(8,128)(2,1)}, bf16[16,128,128]{2,1,0:T(8,128)(2,1)}, u32[]{:S(2)}, u32[]{:S(2)}) %collective-permute-start.11) | collective-permute-done | bytes 524320 | tf_op jit(solution)/shard_map/ppermute | solution.py:506
  83.6 2.1 %add_convert_fusion.2 = (bf16[16,128,128]{2,1,0:T(8,128)(2,1)S(1)}, bf16[16,128,128]{2,1,0:T(8,128)(2,1)S(1)}) fusion(bf16[16,128,128]{2,1,0:T(8,128)(2,1)} %collective-permute-done.11.refs_2_, bf16[16,128,128]{2,1,0:T(8,128)(2,1)} %get-tuple-element.56, bf16[16,128,128]{2,1,0:T(8,128)(2,1)} %get-tuple-element.55, pred[]{:T(512)S(6)} %ge.9, pred[]{:T(512)S(6)} %lt.8, ...), kind=kLoop, calls=%fused_computation.21 | loop fusion | flops 3670016 | bytes 3145733 | tf_op jit(solution)/shard_map/convert_element_type | solution.py:253
  85.7 2.8 %collective-permute-start.20 = (bf16[16,128,128]{2,1,0:T(8,128)(2,1)S(1)}, bf16[16,128,128]{2,1,0:T(8,128)(2,1)S(1)}, u32[]{:S(2)}, u32[]{:S(2)}) collective-permute-start(bf16[16,128,128]{2,1,0:T(8,128)(2,1)S(1)} %get-tuple-element.68), channel_id=1, source_target_pairs={{0,8},{1,9},{2,10},{3,11},{4,12},{5,13},{6,14},{7,15},{8,0},{9,1},... | collective-permute-start | bytes 1572872 | tf_op jit(solution)/shard_map/ppermute | solution.py:506
  88.5 1.0 copy-done.15
  89.5 2.4 %left_products.2 = (f32[16,64,128]{2,1,0:T(8,128)S(1)}, bf16[16,64,128]{2,1,0:T(8,128)(2,1)S(1)}) custom-call(bf16[32,128,128]{2,1,0:T(8,128)(2,1)S(1)} %copy-done.5, bf16[32,128,128]{2,1,0:T(8,128)(2,1)S(1)} %copy-done.1, bf16[16,128,128]{2,1,0:T(8,128)(2,1)} %collective-permute-done.9.refs_1_, bf16[16,128,128]{2,1,0:T(8,128)(2,1)} %collective-permute-done.11.refs_2_, ...), custom_call_target="tpu_custom_call" | custom-call | flops 1 | bytes 8000000 | tf_op jit(solution)/shard_map/left_products/pallas_call | solution.py:347
  91.9 3.0 %collective-permute-done.16.refs_2_ = bf16[16,128,128]{2,1,0:T(8,128)(2,1)} collective-permute-done((bf16[16,128,128]{2,1,0:T(8,128)(2,1)}, bf16[16,128,128]{2,1,0:T(8,128)(2,1)}, u32[]{:S(2)}, u32[]{:S(2)}) %collective-permute-start.16) | collective-permute-done | bytes 524320 | tf_op jit(solution)/shard_map/ppermute | solution.py:506
  94.9 1.7 %add_convert_fusion = (bf16[16,128,128]{2,1,0:T(8,128)(2,1)S(1)}, bf16[16,128,128]{2,1,0:T(8,128)(2,1)S(1)}) fusion(bf16[16,128,128]{2,1,0:T(8,128)(2,1)} %collective-permute-done.16.refs_2_, bf16[16,128,128]{2,1,0:T(8,128)(2,1)S(1)} %copy-done.28, bf16[16,128,128]{2,1,0:T(8,128)(2,1)S(1)} %copy-done.27, pred[]{:T(512)S(6)} %ge.9, pred[]{:T(512)S(6)} %lt.8, ...), kind=kLoop, calls=%fused_computation.17 | loop fusion | flops 3670016 | bytes 3145733 | tf_op jit(solution)/shard_map/convert_element_type | solution.py:253
  96.6 2.8 %collective-permute-start.23 = (bf16[16,128,128]{2,1,0:T(8,128)(2,1)S(1)}, bf16[16,128,128]{2,1,0:T(8,128)(2,1)S(1)}, u32[]{:S(2)}, u32[]{:S(2)}) collective-permute-start(bf16[16,128,128]{2,1,0:T(8,128)(2,1)S(1)} %get-tuple-element.66), channel_id=1, source_target_pairs={{0,8},{1,9},{2,10},{3,11},{4,12},{5,13},{6,14},{7,15},{8,0},{9,1},... | collective-permute-start | bytes 1572872 | tf_op jit(solution)/shard_map/ppermute | solution.py:506
  99.9 2.4 %left_products.3 = (f32[16,64,128]{2,1,0:T(8,128)S(1)}, bf16[16,64,128]{2,1,0:T(8,128)(2,1)S(1)}) custom-call(bf16[32,128,128]{2,1,0:T(8,128)(2,1)S(1)} %copy-done.5, bf16[32,128,128]{2,1,0:T(8,128)(2,1)S(1)} %copy-done.1, bf16[16,128,128]{2,1,0:T(8,128)(2,1)} %collective-permute-done.14.refs_1_, bf16[16,128,128]{2,1,0:T(8,128)(2,1)} %collective-permute-done.16.refs_2_, ...), custom_call_target="tpu_custom_call" | custom-call | flops 1 | bytes 8000000 | tf_op jit(solution)/shard_map/left_products/pallas_call | solution.py:347
  102.3 3.7 %collective-permute-done.20.refs_5_ = bf16[16,128,128]{2,1,0:T(8,128)(2,1)S(1)} collective-permute-done((bf16[16,128,128]{2,1,0:T(8,128)(2,1)S(1)}, bf16[16,128,128]{2,1,0:T(8,128)(2,1)S(1)}, u32[]{:S(2)}, u32[]{:S(2)}) %collective-permute-start.20) | collective-permute-done | bytes 524320 | tf_op jit(solution)/shard_map/ppermute | solution.py:506
  106.2 0.6 collective-permute-start.22
  106.7 0.8 collective-permute-done.19.refs_3_
  107.9 3.7 %known.1.base = f32[64,128,128]{2,1,0:T(8,128)S(1)} custom-call(bf16[64,256,128]{2,1,0:T(8,128)(2,1)S(1)} %copy-done.17, bf16[128,256]{1,0:T(8,128)(2,1)S(1)} %copy-done.20, f32[16,64,128]{2,1,0:T(8,128)S(1)} %get-tuple-element.46.refs_0_, f32[16,64,128]{2,1,0:T(8,128)S(1)} %get-tuple-element.51.refs_1_, ...), custom_call_target="tpu_custom_call" | custom-call | flops 1 | bytes 8000000 | tf_op jit(solution)/shard_map/known/pallas_call | solution.py:414
  111.7 2.6 %collective-permute-done.23.by_a = bf16[16,128,128]{2,1,0:T(8,128)(2,1)S(1)} collective-permute-done((bf16[16,128,128]{2,1,0:T(8,128)(2,1)S(1)}, bf16[16,128,128]{2,1,0:T(8,128)(2,1)S(1)}, u32[]{:S(2)}, u32[]{:S(2)}) %collective-permute-start.23) | collective-permute-done | bytes 524320 | tf_op jit(solution)/shard_map/ppermute | solution.py:506
  114.7 1.3 %collective-permute-done.25.right_other = bf16[16,64,128]{2,1,0:T(8,128)(2,1)S(1)} collective-permute-done((bf16[16,64,128]{2,1,0:T(8,128)(2,1)S(1)}, bf16[16,64,128]{2,1,0:T(8,128)(2,1)S(1)}, u32[]{:S(2)}, u32[]{:S(2)}) %collective-permute-start.25) | collective-permute-done | bytes 262176 | tf_op jit(solution)/shard_map/ppermute | solution.py:498
  116.0 5.4 %tail.1 = bf16[128,64,128]{2,1,0:T(8,128)(2,1)} custom-call(f32[64,128,128]{2,1,0:T(8,128)S(1)} %known.1.base, bf16[64,128,128]{2,1,0:T(8,128)(2,1)S(1)} %copy-done.19, f32[64,1,128]{2,1,0:T(1,128)S(1)} %get-tuple-element.58.inverse, bf16[64,64,128]{2,1,0:T(8,128)(2,1)S(1)} %copy-done.24, f32[1,128]{1,0:T(1,128)S(1)} %bitcast.5, ...), custom_call_target="tpu_custom_call" | custom-call | flops 1 | bytes 8000000 | tf_op jit(solution)/shard_map/tail/pallas_call | solution.py:468
  (86 shorter events, 4.1 us)
Async XLA Ops:
  1.1 6.9 %copy-start.25 = (s32[4,4]{1,0:T(4,128)S(1)}, s32[4,4]{1,0:T(4,128)}, u32[]{:S(2)}) copy-start(s32[4,4]{1,0:T(4,128)} %mask.3) | copy-start | bytes 196
  1.1 2.1 %collective-permute-start = (bf16[64,32,128]{2,1,0:T(8,128)(2,1)S(1)}, bf16[64,32,128]{2,1,0:T(8,128)(2,1)S(1)}, u32[]{:S(2)}, u32[]{:S(2)}) collective-permute-start(bf16[64,32,128]{2,1,0:T(8,128)(2,1)S(1)} %theirs.1), channel_id=1, source_target_pairs={{0,1},{1,0},{2,3},{3,2},{4,5},{5,4},{6,7},{7,6},{8,9},{9,8},{10,11... | collective-permute-start | bytes 1572872 | tf_op jit(solution)/shard_map/ppermute | solution.py:498
  3.5 26.4 %collective-permute-start.6 = (bf16[32,128,128]{2,1,0:T(8,128)(2,1)S(1)}, bf16[32,128,128]{2,1,0:T(8,128)(2,1)S(1)}, u32[]{:S(2)}, u32[]{:S(2)}) collective-permute-start(bf16[32,128,128]{2,1,0:T(8,128)(2,1)S(1)} %pack.1.refs_0_.refs_6_), channel_id=1, source_target_pairs={{0,2},{1,3},{2,0},{3,1},{4,6},{5,7},{6,4},{7,5},{8,10},{9,11},{10,... | collective-permute-start | bytes 3145736 | tf_op jit(solution)/shard_map/ppermute | solution.py:498
  6.4 24.9 %collective-permute-start.7 = (bf16[32,128,128]{2,1,0:T(8,128)(2,1)S(1)}, bf16[32,128,128]{2,1,0:T(8,128)(2,1)S(1)}, u32[]{:S(2)}, u32[]{:S(2)}) collective-permute-start(bf16[32,128,128]{2,1,0:T(8,128)(2,1)S(1)} %pack.1.refs_0_.refs_6_), channel_id=1, source_target_pairs={{0,4},{1,5},{2,6},{3,7},{4,0},{5,1},{6,2},{7,3},{8,12},{9,13},{10,... | collective-permute-start | bytes 3145736 | tf_op jit(solution)/shard_map/ppermute | solution.py:498
  13.1 1.6 %collective-permute-start.2 = (bf16[16,64,128]{2,1,0:T(8,128)(2,1)S(1)}, bf16[16,64,128]{2,1,0:T(8,128)(2,1)S(1)}, u32[]{:S(2)}, u32[]{:S(2)}) collective-permute-start(bf16[16,64,128]{2,1,0:T(8,128)(2,1)S(1)} %get-tuple-element.74), channel_id=1, source_target_pairs={{0,1},{1,0},{2,3},{3,2},{4,5},{5,4},{6,7},{7,6},{8,9},{9,8},{10,11... | collective-permute-start | bytes 786440 | tf_op jit(solution)/shard_map/ppermute | solution.py:498
  13.2 1.9 %collective-permute-start.1 = (bf16[16,64,128]{2,1,0:T(8,128)(2,1)S(1)}, bf16[16,64,128]{2,1,0:T(8,128)(2,1)S(1)}, u32[]{:S(2)}, u32[]{:S(2)}) collective-permute-start(bf16[16,64,128]{2,1,0:T(8,128)(2,1)S(1)} %get-tuple-element.73), channel_id=1, source_target_pairs={{0,1},{1,0},{2,3},{3,2},{4,5},{5,4},{6,7},{7,6},{8,9},{9,8},{10,11... | collective-permute-start | bytes 786440 | tf_op jit(solution)/shard_map/ppermute | solution.py:498
  15.2 16.2 %copy-start.4 = (bf16[32,128,128]{2,1,0:T(8,128)(2,1)}, bf16[32,128,128]{2,1,0:T(8,128)(2,1)S(1)}, u32[]{:S(2)}) copy-start(bf16[32,128,128]{2,1,0:T(8,128)(2,1)S(1)} %maximum_maximum_fusion.own) | copy-start | bytes 3145732
  15.2 25.3 %collective-permute-start.3 = (bf16[32,128,128]{2,1,0:T(8,128)(2,1)S(1)}, bf16[32,128,128]{2,1,0:T(8,128)(2,1)S(1)}, u32[]{:S(2)}, u32[]{:S(2)}) collective-permute-start(bf16[32,128,128]{2,1,0:T(8,128)(2,1)S(1)} %maximum_maximum_fusion.own), channel_id=1, source_target_pairs={{0,8},{1,9},{2,10},{3,11},{4,12},{5,13},{6,14},{7,15},{8,0},{9,1},... | collective-permute-start | bytes 3145736 | tf_op jit(solution)/shard_map/ppermute | solution.py:506
  16.8 23.6 %collective-permute-start.5 = (bf16[32,128,128]{2,1,0:T(8,128)(2,1)S(1)}, bf16[32,128,128]{2,1,0:T(8,128)(2,1)S(1)}, u32[]{:S(2)}, u32[]{:S(2)}) collective-permute-start(bf16[32,128,128]{2,1,0:T(8,128)(2,1)S(1)} %maximum_maximum_fusion.own), channel_id=1, source_target_pairs={{0,1},{1,0},{2,3},{3,2},{4,5},{5,4},{6,7},{7,6},{8,16},{9,17},{10,... | collective-permute-start | bytes 3145736 | tf_op jit(solution)/shard_map/ppermute | solution.py:506
  22.8 2.0 %copy-start.16 = (bf16[64,256,128]{2,1,0:T(8,128)(2,1)}, bf16[64,256,128]{2,1,0:T(8,128)(2,1)S(1)}, u32[]{:S(2)}) copy-start(bf16[64,256,128]{2,1,0:T(8,128)(2,1)S(1)} %get-tuple-element.39.factors) | copy-start | bytes 12582916
  26.1 6.8 %copy-start.23 = (bf16[64,64,128]{2,1,0:T(8,128)(2,1)}, bf16[64,64,128]{2,1,0:T(8,128)(2,1)S(1)}, u32[]{:S(2)}) copy-start(bf16[64,64,128]{2,1,0:T(8,128)(2,1)S(1)} %get-tuple-element.59.last) | copy-start | bytes 3145732
  26.2 21.4 %copy-start.6 = (bf16[32,64,128]{2,1,0:T(8,128)(2,1)}, bf16[32,64,128]{2,1,0:T(8,128)(2,1)S(1)}, u32[]{:S(2)}) copy-start(bf16[32,64,128]{2,1,0:T(8,128)(2,1)S(1)} %get-tuple-element.40.left_mine) | copy-start | bytes 1572868
  26.2 7.4 %collective-permute-start.4 = (bf16[32,64,128]{2,1,0:T(8,128)(2,1)S(1)}, bf16[32,64,128]{2,1,0:T(8,128)(2,1)S(1)}, u32[]{:S(2)}, u32[]{:S(2)}) collective-permute-start(bf16[32,64,128]{2,1,0:T(8,128)(2,1)S(1)} %get-tuple-element.41), channel_id=1, source_target_pairs={{0,1},{1,0},{2,3},{3,2},{4,5},{5,4},{6,7},{7,6},{8,9},{9,8},{10,11... | collective-permute-start | bytes 1572872 | tf_op jit(solution)/shard_map/ppermute | solution.py:498
  31.4 12.9 %collective-permute-start.8 = (bf16[16,128,128]{2,1,0:T(8,128)(2,1)S(1)}, bf16[16,128,128]{2,1,0:T(8,128)(2,1)S(1)}, u32[]{:S(2)}, u32[]{:S(2)}) collective-permute-start(bf16[16,128,128]{2,1,0:T(8,128)(2,1)S(1)} %get-tuple-element.42), channel_id=1, source_target_pairs={{0,4},{1,5},{2,6},{3,7},{4,0},{5,1},{6,2},{7,3},{8,12},{9,13},{10,... | collective-permute-start | bytes 1572872 | tf_op jit(solution)/shard_map/ppermute | solution.py:498
  33.0 14.6 %collective-permute-start.13 = (bf16[16,128,128]{2,1,0:T(8,128)(2,1)S(1)}, bf16[16,128,128]{2,1,0:T(8,128)(2,1)S(1)}, u32[]{:S(2)}, u32[]{:S(2)}) collective-permute-start(bf16[16,128,128]{2,1,0:T(8,128)(2,1)S(1)} %get-tuple-element.47), channel_id=1, source_target_pairs={{0,2},{1,3},{2,0},{3,1},{4,6},{5,7},{6,4},{7,5},{8,10},{9,11},{10,... | collective-permute-start | bytes 1572872 | tf_op jit(solution)/shard_map/ppermute | solution.py:498
  33.5 14.0 %copy-start.8 = (bf16[32,64,128]{2,1,0:T(8,128)(2,1)}, bf16[32,64,128]{2,1,0:T(8,128)(2,1)S(1)}, u32[]{:S(2)}) copy-start(bf16[32,64,128]{2,1,0:T(8,128)(2,1)S(1)} %collective-permute-done.4.left_other) | copy-start | bytes 1572868
  40.4 7.1 %copy-start = (bf16[32,128,128]{2,1,0:T(8,128)(2,1)}, bf16[32,128,128]{2,1,0:T(8,128)(2,1)S(1)}, u32[]{:S(2)}) copy-start(bf16[32,128,128]{2,1,0:T(8,128)(2,1)S(1)} %collective-permute-done.3.by_a.refs_0_) | copy-start | bytes 3145732
  40.4 7.1 %copy-start.2 = (bf16[32,128,128]{2,1,0:T(8,128)(2,1)}, bf16[32,128,128]{2,1,0:T(8,128)(2,1)S(1)}, u32[]{:S(2)}) copy-start(bf16[32,128,128]{2,1,0:T(8,128)(2,1)S(1)} %collective-permute-done.5.by_b.refs_3_) | copy-start | bytes 3145732
  46.0 15.2 %collective-permute-start.9 = (bf16[16,128,128]{2,1,0:T(8,128)(2,1)}, bf16[16,128,128]{2,1,0:T(8,128)(2,1)}, u32[]{:S(2)}, u32[]{:S(2)}) collective-permute-start(bf16[16,128,128]{2,1,0:T(8,128)(2,1)} %get-tuple-element.43), channel_id=1, source_target_pairs={{0,8},{1,9},{2,10},{3,11},{4,12},{5,13},{6,14},{7,15},{8,0},{9,1},... | collective-permute-start | bytes 1572872 | tf_op jit(solution)/shard_map/ppermute | solution.py:506
  47.5 13.6 %collective-permute-start.10 = (bf16[16,128,128]{2,1,0:T(8,128)(2,1)}, bf16[16,128,128]{2,1,0:T(8,128)(2,1)}, u32[]{:S(2)}, u32[]{:S(2)}) collective-permute-start(bf16[16,128,128]{2,1,0:T(8,128)(2,1)} %get-tuple-element.44), channel_id=1, source_target_pairs={{0,1},{1,0},{2,3},{3,2},{4,5},{5,4},{6,7},{7,6},{8,16},{9,17},{10,... | collective-permute-start | bytes 1572872 | tf_op jit(solution)/shard_map/ppermute | solution.py:506
  49.3 23.1 %collective-permute-start.14 = (bf16[16,128,128]{2,1,0:T(8,128)(2,1)}, bf16[16,128,128]{2,1,0:T(8,128)(2,1)}, u32[]{:S(2)}, u32[]{:S(2)}) collective-permute-start(bf16[16,128,128]{2,1,0:T(8,128)(2,1)} %get-tuple-element.48), channel_id=1, source_target_pairs={{0,8},{1,9},{2,10},{3,11},{4,12},{5,13},{6,14},{7,15},{8,0},{9,1},... | collective-permute-start | bytes 1572872 | tf_op jit(solution)/shard_map/ppermute | solution.py:506
  52.4 19.9 %collective-permute-start.15 = (bf16[16,128,128]{2,1,0:T(8,128)(2,1)}, bf16[16,128,128]{2,1,0:T(8,128)(2,1)}, u32[]{:S(2)}, u32[]{:S(2)}) collective-permute-start(bf16[16,128,128]{2,1,0:T(8,128)(2,1)} %get-tuple-element.49), channel_id=1, source_target_pairs={{0,1},{1,0},{2,3},{3,2},{4,5},{5,4},{6,7},{7,6},{8,16},{9,17},{10,... | collective-permute-start | bytes 1572872 | tf_op jit(solution)/shard_map/ppermute | solution.py:506
  58.3 8.4 %copy-start.11 = (bf16[16,128,128]{2,1,0:T(8,128)(2,1)S(1)}, bf16[16,128,128]{2,1,0:T(8,128)(2,1)}, u32[]{:S(2)}) copy-start(bf16[16,128,128]{2,1,0:T(8,128)(2,1)} %copy-done.10) | copy-start | bytes 1572868
  64.0 19.6 %collective-permute-start.11 = (bf16[16,128,128]{2,1,0:T(8,128)(2,1)}, bf16[16,128,128]{2,1,0:T(8,128)(2,1)}, u32[]{:S(2)}, u32[]{:S(2)}) collective-permute-start(bf16[16,128,128]{2,1,0:T(8,128)(2,1)} %get-tuple-element.72), channel_id=1, source_target_pairs={{0,8},{1,9},{2,10},{3,11},{4,12},{5,13},{6,14},{7,15},{8,0},{9,1},... | collective-permute-start | bytes 1572872 | tf_op jit(solution)/shard_map/ppermute | solution.py:506
  66.7 16.9 %collective-permute-start.12 = (bf16[16,128,128]{2,1,0:T(8,128)(2,1)}, bf16[16,128,128]{2,1,0:T(8,128)(2,1)}, u32[]{:S(2)}, u32[]{:S(2)}) collective-permute-start(bf16[16,128,128]{2,1,0:T(8,128)(2,1)} %get-tuple-element.71), channel_id=1, source_target_pairs={{0,1},{1,0},{2,3},{3,2},{4,5},{5,4},{6,7},{7,6},{8,16},{9,17},{10,... | collective-permute-start | bytes 1572872 | tf_op jit(solution)/shard_map/ppermute | solution.py:506
  75.3 19.6 %collective-permute-start.16 = (bf16[16,128,128]{2,1,0:T(8,128)(2,1)}, bf16[16,128,128]{2,1,0:T(8,128)(2,1)}, u32[]{:S(2)}, u32[]{:S(2)}) collective-permute-start(bf16[16,128,128]{2,1,0:T(8,128)(2,1)} %get-tuple-element.70), channel_id=1, source_target_pairs={{0,8},{1,9},{2,10},{3,11},{4,12},{5,13},{6,14},{7,15},{8,0},{9,1},... | collective-permute-start | bytes 1572872 | tf_op jit(solution)/shard_map/ppermute | solution.py:506
  78.0 16.9 %collective-permute-start.17 = (bf16[16,128,128]{2,1,0:T(8,128)(2,1)}, bf16[16,128,128]{2,1,0:T(8,128)(2,1)}, u32[]{:S(2)}, u32[]{:S(2)}) collective-permute-start(bf16[16,128,128]{2,1,0:T(8,128)(2,1)} %get-tuple-element.69), channel_id=1, source_target_pairs={{0,1},{1,0},{2,3},{3,2},{4,5},{5,4},{6,7},{7,6},{8,16},{9,17},{10,... | collective-permute-start | bytes 1572872 | tf_op jit(solution)/shard_map/ppermute | solution.py:506
  78.0 10.5 %copy-start.1 = (bf16[32,128,128]{2,1,0:T(8,128)(2,1)S(1)}, bf16[32,128,128]{2,1,0:T(8,128)(2,1)}, u32[]{:S(2)}) copy-start(bf16[32,128,128]{2,1,0:T(8,128)(2,1)} %copy-done) | copy-start | bytes 3145732
  78.0 10.5 %copy-start.3 = (bf16[32,128,128]{2,1,0:T(8,128)(2,1)S(1)}, bf16[32,128,128]{2,1,0:T(8,128)(2,1)}, u32[]{:S(2)}) copy-start(bf16[32,128,128]{2,1,0:T(8,128)(2,1)} %copy-done.2) | copy-start | bytes 3145732
  78.0 10.5 %copy-start.5 = (bf16[32,128,128]{2,1,0:T(8,128)(2,1)S(1)}, bf16[32,128,128]{2,1,0:T(8,128)(2,1)}, u32[]{:S(2)}) copy-start(bf16[32,128,128]{2,1,0:T(8,128)(2,1)} %copy-done.4) | copy-start | bytes 3145732
  85.7 20.3 %collective-permute-start.20 = (bf16[16,128,128]{2,1,0:T(8,128)(2,1)S(1)}, bf16[16,128,128]{2,1,0:T(8,128)(2,1)S(1)}, u32[]{:S(2)}, u32[]{:S(2)}) collective-permute-start(bf16[16,128,128]{2,1,0:T(8,128)(2,1)S(1)} %get-tuple-element.68), channel_id=1, source_target_pairs={{0,8},{1,9},{2,10},{3,11},{4,12},{5,13},{6,14},{7,15},{8,0},{9,1},... | collective-permute-start | bytes 1572872 | tf_op jit(solution)/shard_map/ppermute | solution.py:506
  88.5 17.5 %collective-permute-start.21 = (bf16[16,128,128]{2,1,0:T(8,128)(2,1)S(1)}, bf16[16,128,128]{2,1,0:T(8,128)(2,1)S(1)}, u32[]{:S(2)}, u32[]{:S(2)}) collective-permute-start(bf16[16,128,128]{2,1,0:T(8,128)(2,1)S(1)} %get-tuple-element.67), channel_id=1, source_target_pairs={{0,1},{1,0},{2,3},{3,2},{4,5},{5,4},{6,7},{7,6},{8,16},{9,17},{10,... | collective-permute-start | bytes 1572872 | tf_op jit(solution)/shard_map/ppermute | solution.py:506
  89.5 5.3 %copy-start.27 = (bf16[16,128,128]{2,1,0:T(8,128)(2,1)S(1)}, bf16[16,128,128]{2,1,0:T(8,128)(2,1)}, u32[]{:S(2)}) copy-start(bf16[16,128,128]{2,1,0:T(8,128)(2,1)} %get-tuple-element.61) | copy-start | bytes 1572868
  89.5 5.3 %copy-start.28 = (bf16[16,128,128]{2,1,0:T(8,128)(2,1)S(1)}, bf16[16,128,128]{2,1,0:T(8,128)(2,1)}, u32[]{:S(2)}) copy-start(bf16[16,128,128]{2,1,0:T(8,128)(2,1)} %get-tuple-element.62) | copy-start | bytes 1572868
  91.9 8.0 %copy-start.12 = (bf16[16,128,128]{2,1,0:T(8,128)(2,1)S(1)}, bf16[16,128,128]{2,1,0:T(8,128)(2,1)}, u32[]{:S(2)}) copy-start(bf16[16,128,128]{2,1,0:T(8,128)(2,1)} %copy-done.10) | copy-start | bytes 1572868
  96.6 17.6 %collective-permute-start.23 = (bf16[16,128,128]{2,1,0:T(8,128)(2,1)S(1)}, bf16[16,128,128]{2,1,0:T(8,128)(2,1)S(1)}, u32[]{:S(2)}, u32[]{:S(2)}) collective-permute-start(bf16[16,128,128]{2,1,0:T(8,128)(2,1)S(1)} %get-tuple-element.66), channel_id=1, source_target_pairs={{0,8},{1,9},{2,10},{3,11},{4,12},{5,13},{6,14},{7,15},{8,0},{9,1},... | collective-permute-start | bytes 1572872 | tf_op jit(solution)/shard_map/ppermute | solution.py:506
  99.4 6.6 %copy-start.22 = (bf16[16,128,128]{2,1,0:T(8,128)(2,1)S(1)}, bf16[16,128,128]{2,1,0:T(8,128)(2,1)}, u32[]{:S(2)}) copy-start(bf16[16,128,128]{2,1,0:T(8,128)(2,1)} %get-tuple-element.54.refs_4_) | copy-start | bytes 1572868
  99.4 8.5 %copy-start.20 = (bf16[128,256]{1,0:T(8,128)(2,1)S(1)}, bf16[128,256]{1,0:T(8,128)(2,1)}, u32[]{:S(2)}) copy-start(bf16[128,256]{1,0:T(8,128)(2,1)} %weight.5) | copy-start | bytes 196612
  99.4 14.9 %collective-permute-start.24 = (bf16[16,128,128]{2,1,0:T(8,128)(2,1)S(1)}, bf16[16,128,128]{2,1,0:T(8,128)(2,1)S(1)}, u32[]{:S(2)}, u32[]{:S(2)}) collective-permute-start(bf16[16,128,128]{2,1,0:T(8,128)(2,1)S(1)} %get-tuple-element.65), channel_id=1, source_target_pairs={{0,1},{1,0},{2,3},{3,2},{4,5},{5,4},{6,7},{7,6},{8,16},{9,17},{10,... | collective-permute-start | bytes 1572872 | tf_op jit(solution)/shard_map/ppermute | solution.py:506
  99.4 7.3 %collective-permute-start.18 = (bf16[16,64,128]{2,1,0:T(8,128)(2,1)S(1)}, bf16[16,64,128]{2,1,0:T(8,128)(2,1)S(1)}, u32[]{:S(2)}, u32[]{:S(2)}) collective-permute-start(bf16[16,64,128]{2,1,0:T(8,128)(2,1)S(1)} %get-tuple-element.52), channel_id=1, source_target_pairs={{0,1},{1,0},{2,3},{3,2},{4,5},{5,4},{6,7},{7,6},{8,9},{9,8},{10,11... | collective-permute-start | bytes 786440 | tf_op jit(solution)/shard_map/ppermute | solution.py:498
  99.9 8.0 %copy-start.17 = (bf16[64,256,128]{2,1,0:T(8,128)(2,1)S(1)}, bf16[64,256,128]{2,1,0:T(8,128)(2,1)}, u32[]{:S(2)}) copy-start(bf16[64,256,128]{2,1,0:T(8,128)(2,1)} %copy-done.16) | copy-start | bytes 12582916
  106.0 1.5 %collective-permute-start.19 = (bf16[16,64,128]{2,1,0:T(8,128)(2,1)S(1)}, bf16[16,64,128]{2,1,0:T(8,128)(2,1)S(1)}, u32[]{:S(2)}, u32[]{:S(2)}) collective-permute-start(bf16[16,64,128]{2,1,0:T(8,128)(2,1)S(1)} %get-tuple-element.53), channel_id=1, source_target_pairs={{0,1},{1,0},{2,3},{3,2},{4,5},{5,4},{6,7},{7,6},{8,9},{9,8},{10,11... | collective-permute-start | bytes 786440 | tf_op jit(solution)/shard_map/ppermute | solution.py:498
  106.2 1.7 %collective-permute-start.22 = (bf16[16,64,128]{2,1,0:T(8,128)(2,1)S(1)}, bf16[16,64,128]{2,1,0:T(8,128)(2,1)S(1)}, u32[]{:S(2)}, u32[]{:S(2)}) collective-permute-start(bf16[16,64,128]{2,1,0:T(8,128)(2,1)S(1)} %add_convert_fusion.5), channel_id=1, source_target_pairs={{0,1},{1,0},{2,3},{3,2},{4,5},{5,4},{6,7},{7,6},{8,9},{9,8},{10,11... | collective-permute-start | bytes 786440 | tf_op jit(solution)/shard_map/ppermute | solution.py:498
  107.9 6.4 %copy-start.21 = (bf16[16,128,128]{2,1,0:T(8,128)(2,1)S(1)}, bf16[16,128,128]{2,1,0:T(8,128)(2,1)}, u32[]{:S(2)}) copy-start(bf16[16,128,128]{2,1,0:T(8,128)(2,1)} %get-tuple-element.64.partials) | copy-start | bytes 1572868
  107.9 8.1 %copy-start.19 = (bf16[64,128,128]{2,1,0:T(8,128)(2,1)S(1)}, bf16[64,128,128]{2,1,0:T(8,128)(2,1)}, u32[]{:S(2)}) copy-start(bf16[64,128,128]{2,1,0:T(8,128)(2,1)} %copy-done.18) | copy-start | bytes 6291460
  107.9 8.1 %copy-start.26 = (f32[128]{0:T(128)S(1)}, f32[128]{0:T(128)}, u32[]{:S(2)}) copy-start(f32[128]{0:T(128)} %param.8) | copy-start | bytes 1540
  111.7 4.3 %copy-start.24 = (bf16[64,64,128]{2,1,0:T(8,128)(2,1)S(1)}, bf16[64,64,128]{2,1,0:T(8,128)(2,1)}, u32[]{:S(2)}) copy-start(bf16[64,64,128]{2,1,0:T(8,128)(2,1)} %copy-done.23) | copy-start | bytes 3145732
  114.4 1.6 %collective-permute-start.25 = (bf16[16,64,128]{2,1,0:T(8,128)(2,1)S(1)}, bf16[16,64,128]{2,1,0:T(8,128)(2,1)S(1)}, u32[]{:S(2)}, u32[]{:S(2)}) collective-permute-start(bf16[16,64,128]{2,1,0:T(8,128)(2,1)S(1)} %add_convert_fusion.4), channel_id=1, source_target_pairs={{0,1},{1,0},{2,3},{3,2},{4,5},{5,4},{6,7},{7,6},{8,9},{9,8},{10,11... | collective-permute-start | bytes 786440 | tf_op jit(solution)/shard_map/ppermute | solution.py:498
  (7 other events, 8.9 us)

commit v10 on v9

--- a/solution.py
+++ b/solution.py
@@ -193,20 +193,23 @@
     )(*in_hbm(raw))
 
 
-def pack_kernel(own, other, out):
+def pack_kernel(own, other, *outs):
     cols = other.shape[0]
     core = this_core()
     for block, place in ((own, core), (other, 1 - core)):
-        out[:, pl.ds(pl.multiple_of(place * cols, cols), cols), :] = jnp.transpose(block[...], (1, 0, 2))
+        flipped = jnp.transpose(block[...], (1, 0, 2))
+        for chunk, out in enumerate(outs):
+            chans = out.shape[0]
+            out[:, pl.ds(pl.multiple_of(place * cols, cols), cols), :] = flipped[chunk * chans : (chunk + 1) * chans]
 
 
 def pack(own, other):
     cols, half, rows = other.shape
     return pl.pallas_call(
         pack_kernel,
-        out_shape=jax.ShapeDtypeStruct((half, CORES * cols, rows), jnp.bfloat16),
+        out_shape=[jax.ShapeDtypeStruct((half // CHUNKS, CORES * cols, rows), jnp.bfloat16)] * CHUNKS,
         in_specs=[WHOLE] * 2,
-        out_specs=WHOLE,
+        out_specs=[WHOLE] * CHUNKS,
         compiler_params=PARAMS,
         cost_estimate=COST,
         name="pack",
@@ -218,23 +221,16 @@
     return pl.BlockSpec((STEP,) + array.shape[1:], lambda g: (first + g, 0, 0))
 
 
-def cut_kernel(chunks, *refs):
-    for source, out, chunk in zip(refs, refs[len(chunks) :], chunks):
-        chans = out.shape[0]
-        out[...] = source[chunk * chans : (chunk + 1) * chans]
-
-
-def cut(arrays, chunks):
-    shape = (arrays[0].shape[0] // CHUNKS,) + arrays[0].shape[1:]
-    return pl.pallas_call(
-        functools.partial(cut_kernel, chunks),
-        out_shape=[jax.ShapeDtypeStruct(shape, jnp.bfloat16)] * len(arrays),
-        in_specs=[WHOLE] * len(arrays),
-        out_specs=[WHOLE] * len(arrays),
-        compiler_params=PARAMS,
-        cost_estimate=FRONT_COST,
-        name="cut",
-    )(*arrays)
+def slot_mask(m, core, chips):
+    width = chips.bit_length() - 1
+    return m if core == 0 else sum(1 << (width - 1 - b) for b in range(width) if m >> b & 1)
+
+
+def slot_chips(chips):
+    chip = lax.axis_index("col") // CORES
+    return [
+        jnp.bitwise_xor(chip, jnp.where(this_core() == 0, m, slot_mask(m, 1, chips))) for m in range(chips)
+    ]
 
 
 def lanes(n):
@@ -256,15 +252,14 @@
 def first_kernel(chunk, left_mine, left_other, by_a, by_b, *refs):
     *blocks, next_a, next_b = refs
     n = len(blocks)
-    chip, target = lax.axis_index("col") // CORES, jnp.where(lax.axis_index("row") == 0, n - 1, 0)
-    slot = jnp.bitwise_xor(chip, target)
+    holders, target = slot_chips(n), jnp.where(lax.axis_index("row") == 0, n - 1, 0)
     chans = next_a.shape[0]
     for c in range(chans):
         at = chunk * chans + c
         lhs = jnp.concatenate((left_mine[at], left_other[at]), axis=0)
-        rhs = blocks[0][at]
+        rhs = blocks[0][c]
         for m in range(1, n):
-            rhs = jnp.where(slot == m, blocks[m][at if blocks[m].shape[0] > chans else c], rhs)
+            rhs = jnp.where(holders[m] == target, blocks[m][c], rhs)
         sums = lax.dot_general(lhs, rhs, BY_LAST, preferred_element_type=jnp.float32).astype(jnp.bfloat16)
         next_a[c], next_b[c] = onward(by_a[at], by_b[at], sums, sums, 1, n)
 
@@ -283,32 +278,28 @@
     )(*args)
 
 
-def partial_kernel(n, chunk, left_mine, left_other, *refs):
+def partial_kernel(n, left_mine, left_other, *refs):
     blocks, outs, sums = refs[:n], refs[n : 2 * n], refs[2 * n]
-    row, chip = lax.axis_index("row"), lax.axis_index("col") // CORES
-    chans = left_mine.shape[0] // CHUNKS
-    step = pl.program_id(0) * STEP
-    first = chunk * chans + step
+    row, holders = lax.axis_index("row"), slot_chips(n)
     for c in range(STEP):
-        lhs = jnp.concatenate((left_mine[first + c], left_other[first + c]), axis=0)
-        for m, block in enumerate(blocks):
-            away = lax.rem(jnp.bitwise_xor(chip, m) - row + n, n)
-            rhs = block[(first if block.shape[0] > chans else step) + c]
-            sums[away, c] = lax.dot_general(lhs, rhs, BY_LAST, preferred_element_type=jnp.float32).astype(jnp.bfloat16)
+        lhs = jnp.concatenate((left_mine[c], left_other[c]), axis=0)
+        for holder, block in zip(holders, blocks):
+            away = lax.rem(holder - row + n, n)
+            sums[away, c] = lax.dot_general(lhs, block[c], BY_LAST, preferred_element_type=jnp.float32).astype(jnp.bfloat16)
     for s, out in enumerate(outs):
         out[...] = sums[s]
 
 
 def partial_products(left_mine, left_other, blocks, chunk):
-    rows = blocks[0].shape[1]
-    ks, chans = left_mine.shape[1], left_mine.shape[0] // CHUNKS
+    chans, rows, _ = blocks[0].shape
+    ks = left_mine.shape[1]
     n = len(blocks)
     args = (left_mine, left_other, *blocks)
     return pl.pallas_call(
-        functools.partial(partial_kernel, n, chunk),
+        functools.partial(partial_kernel, n),
         out_shape=[pltpu.HBM((chans, CORES * ks, rows), jnp.bfloat16)] * n,
         grid=(chans // STEP,),
-        in_specs=[WHOLE] * len(args),
+        in_specs=[chunk_spec(v, chans, chunk) for v in args],
         out_specs=[pl.BlockSpec((STEP, CORES * ks, rows), lambda g: (g, 0, 0))] * n,
         scratch_shapes=[pltpu.VMEM((n, STEP, CORES * ks, rows), jnp.bfloat16)],
         compiler_params=PARAMS,
@@ -320,12 +311,12 @@
 def left_kernel(n, own, *refs):
     by_a, by_b, refs = refs[: n - 1], refs[n - 1 : 2 * n - 2], refs[2 * n - 2 :]
     blocks, (mine, theirs, panel) = refs[:n], refs[n:]
-    row, chip = lax.axis_index("row"), lax.axis_index("col") // CORES
+    row, holders = lax.axis_index("row"), slot_chips(n)
     even = lanes(n)[0]
     ks = mine.shape[1]
     for c in range(STEP):
-        for m, block in enumerate(blocks):
-            panel[c, jnp.bitwise_xor(chip, m)] = block[c]
+        for holder, block in zip(holders, blocks):
+            panel[c, holder] = block[c]
         acts, grads = [own[c]], [panel[c, row]]
         for s in range(1, n):
             from_above = jnp.where(even, by_a[s - 1][c], by_b[s - 1][c])
@@ -509,28 +500,31 @@
     other = exchange(take_half(raw, True), 1)
     packed = pack(take_half(raw, False), other)
 
-    axes = {m: [1 << b for b in range(m.bit_length()) if m >> b & 1] for m in range(n_col // CORES)}
-    whole = {m: exchange(packed, CORES * m) for m in axes if len(axes[m]) == 1}
-    turns = [(m, c, axes[m][(c + 1) % 2]) for m in axes if len(axes[m]) == 2 for c in range(CHUNKS)]
-    cuts = cut([whole[m ^ bit] for m, _, bit in turns], [c for _, c, _ in turns])
-    relayed = {(m, c): exchange(value, CORES * bit) for (m, c, bit), value in zip(turns, cuts)}
-    for m in axes:
-        for c in range(CHUNKS if len(axes[m]) > 2 else 0):
-            bit = axes[m][c % len(axes[m])]
-            relayed[m, c] = exchange(relayed[m ^ bit, c], CORES * bit)
-    whole[0] = packed
-    panels = [[whole[m] if m in whole else relayed[m, c] for m in axes] for c in range(CHUNKS)]
+    chips = n_col // CORES
+
+    def along(value, bit):
+        mask = [CORES * slot_mask(bit, core, chips) for core in range(CORES)]
+        return lax.ppermute(value, "col", [(d, d ^ mask[d % CORES]) for d in range(n_col)])
+
+    panels = []
+    for block in packed:
+        slots = [after(block, panels[-1][1:]) if panels else block]
+        for m in range(1, chips):
+            bit = 1 << (m.bit_length() - 1)
+            slots.append(along(slots[m ^ bit], bit))
+        panels.append(slots)
 
     right_mine, right_theirs = front(after(pair, packed), gain, bias, proj_weight, tile_mask, True)
     right_other = [exchange(right_theirs[c * part : (c + 1) * part], 1) for c in range(CHUNKS)]
     own = jnp.concatenate((right_mine, jnp.concatenate(right_other)), axis=1)
     first_a, first_b = hop(own, 0), hop(own, 1)
-    left_mine, left_theirs, *forward = front(after(pair, own), gain, bias, proj_weight, tile_mask, False)
+    left_mine, left_theirs, *forward = front(after(pair, own, panels[0][-2]), gain, bias, proj_weight, tile_mask, False)
     left_other = exchange(left_theirs, 1)
 
     by_a, by_b, partials = [], [], []
     for c in range(CHUNKS):
-        next_a, next_b = first_step(left_mine, left_other, first_a, first_b, panels[c], c)
+        ready = after(left_other, partials[-1]) if partials else left_other
+        next_a, next_b = first_step(left_mine, ready, first_a, first_b, panels[c], c)
         partials.append(partial_products(left_mine, left_other, panels[c], c))
         by_a.append([first_a, hop(next_a, 0)])
         by_b.append([first_b, hop(next_b, 1)])

time: 122 us -> 120 us (0.984)
  local copies, waits for them, and re-layouts: 7.68 us -> 4.61 us
  starting transfers between devices: 26.6 us -> 28.8 us
  waiting for transfers between devices: 40.4 us -> 39.1 us
    ppermute x0 -> x6, waiting for transfers between devices: none -> 14.6 us  [along(): lax.ppermute(value, 'col', [(d, d ^ mask[d % CORES]) for d in range(n_col)])]
    ppermute x12 -> x8, waiting for transfers between devices: 12.8 us -> 3.01 us  [exchange(): return lax.ppermute(value, 'col', [(d, d ^ mask) for d in range(n_col)])]
    ppermute x0 -> x6, starting transfers between devices: none -> 9.34 us  [along(): lax.ppermute(value, 'col', [(d, d ^ mask[d % CORES]) for d in range(n_col)])]
    ppermute x12 -> x8, starting transfers between devices: 9.32 us -> 2.12 us  [exchange(): return lax.ppermute(value, 'col', [(d, d ^ mask) for d in range(n_col)])]
    ppermute x14, waiting for transfers between devices: 27.6 us -> 21.5 us  [hop(): return lax.ppermute(value, ('row', 'col'), perm)]
    unnamed x58 -> x74, local copies, waits for them, and re-layouts: 7.54 us -> 4.48 us
    pallas_call x4 -> x3, Pallas kernels: 5.88 us -> 5.94 us  [the longest x2 5.58 us: partial_products(): pl.pallas_call(functools.partial(partial_kernel, n), out_shape=[pltpu.HBM...]
  transfers between devices with their start and end apart: 26 -> 28, of which waited for: 16 -> 12; matrix products, arithmetic and copies ran while one was open for 8% -> 9% of each run, Pallas kernels for 24% -> 25%
where the time goes in v10:
time: 120 us
  waiting for transfers between devices  39.1 us (33%)
  Pallas kernels  36.7 us (31%)
  starting transfers between devices  28.8 us (24%)
  other arithmetic  10.2 us (8%)
  local copies, waits for them, and re-layouts  4.61 us (4%)
    ppermute x14, waiting for transfers between devices, hop(): return lax.ppermute(value, ('row', 'col'), perm)  21.5 us
    ppermute x14, starting transfers between devices, hop(): return lax.ppermute(value, ('row', 'col'), perm)  17.3 us
    ppermute x6, waiting for transfers between devices, along(): lax.ppermute(value, 'col', [(d, d ^ mask[d % CORES]) for d in range(n_col)])  14.6 us
    pallas_call x2, Pallas kernels, front(): pl.pallas_call(right_kernel if right else left_forward_kernel, out_shape=...  11.2 us
    convert_element_type x4, other arithmetic, onward(): return (out_a.astype(jnp.bfloat16), out_b.astype(jnp.bfloat16))  9.76 us
    ppermute x6, starting transfers between devices, along(): lax.ppermute(value, 'col', [(d, d ^ mask[d % CORES]) for d in range(n_col)])  9.34 us
    pallas_call x2, Pallas kernels, partial_products(): pl.pallas_call(functools.partial(partial_kernel, n), out_shape=[pltpu.HBM...  5.58 us
    pallas_call x1, Pallas kernels, tail(): pl.pallas_call(functools.partial(tail_kernel, lax.axis_size('row')), out_...  5.43 us
  transfers between devices with their start and end apart: 28, of which 12 were waited for; matrix products, arithmetic and copies ran while one was open for 9% of the time, Pallas kernels for 25%

profile of v10, /device:TPU:0, one launch (start us, length us, event | category | flops | bytes accessed | tf_op | source)
XLA Modules:
  0.0 119.8 jit_solution(13515158329350174486)
XLA Ops:
  0.0 1.1 theirs.1
  1.1 0.5 collective-permute-start
  1.6 1.0 mine.1.own
  2.6 0.5 collective-permute-done.other
  3.5 2.9 %collective-permute-start.7 = (bf16[16,128,128]{2,1,0:T(8,128)(2,1)S(1)}, bf16[16,128,128]{2,1,0:T(8,128)(2,1)S(1)}, u32[]{:S(2)}, u32[]{:S(2)}) collective-permute-start(bf16[16,128,128]{2,1,0:T(8,128)(2,1)S(1)} %get-tuple-element.37.refs_0_.refs_6_), channel_id=1, source_target_pairs={{0,2},{1,5},{2,0},{3,7},{4,6},{5,1},{6,4},{7,3},{8,10},{9,13},{10,... | collective-permute-start | bytes 1572872 | tf_op jit(solution)/shard_map/ppermute | solution.py:507
  6.4 5.1 %right_front.1 = (bf16[32,64,128]{2,1,0:T(8,128)(2,1)S(1)}, bf16[32,64,128]{2,1,0:T(8,128)(2,1)S(1)}) custom-call(s32[4,4]{1,0:T(4,128)S(1)} %copy-done.33, bf16[128,64,128]{2,1,0:T(8,128)(2,1)} %pair.1, f32[1,128]{1,0:T(1,128)} %bitcast.3, f32[1,128]{1,0:T(1,128)} %bitcast.8, bf16[128,256]{1,0:T(8,128)(2,1)} %weight.5), custom_call_target="tpu_custom_call" | custom-call | flops 1 | bytes 18000000 | tf_op jit(solution)/shard_map/right_front/pallas_call | solution.py:145
  11.7 0.5 collective-permute-start.1
  12.2 1.5 %collective-permute-start.3 = (bf16[16,128,128]{2,1,0:T(8,128)(2,1)S(1)}, bf16[16,128,128]{2,1,0:T(8,128)(2,1)S(1)}, u32[]{:S(2)}, u32[]{:S(2)}) collective-permute-start(bf16[16,128,128]{2,1,0:T(8,128)(2,1)S(1)} %get-tuple-element.37.refs_0_.refs_6_), channel_id=1, source_target_pairs={{0,4},{1,3},{2,6},{3,1},{4,0},{5,7},{6,2},{7,5},{8,12},{9,11},{10,... | collective-permute-start | bytes 1572872 | tf_op jit(solution)/shard_map/ppermute | solution.py:507
  13.7 1.9 %collective-permute-start.8 = (bf16[16,128,128]{2,1,0:T(8,128)(2,1)S(1)}, bf16[16,128,128]{2,1,0:T(8,128)(2,1)S(1)}, u32[]{:S(2)}, u32[]{:S(2)}) collective-permute-start(bf16[16,128,128]{2,1,0:T(8,128)(2,1)S(1)} %collective-permute-done.7.refs_1_.refs_7_), channel_id=1, source_target_pairs={{0,4},{1,3},{2,6},{3,1},{4,0},{5,7},{6,2},{7,5},{8,12},{9,11},{10,... | collective-permute-start | bytes 1572872 | tf_op jit(solution)/shard_map/ppermute | solution.py:507
  15.7 1.6 %collective-permute-start.4 = (bf16[32,128,128]{2,1,0:T(8,128)(2,1)S(1)}, bf16[32,128,128]{2,1,0:T(8,128)(2,1)S(1)}, u32[]{:S(2)}, u32[]{:S(2)}) collective-permute-start(bf16[32,128,128]{2,1,0:T(8,128)(2,1)S(1)} %maximum_maximum_fusion.own), channel_id=1, source_target_pairs={{0,8},{1,9},{2,10},{3,11},{4,12},{5,13},{6,14},{7,15},{8,0},{9,1},... | collective-permute-start | bytes 3145736 | tf_op jit(solution)/shard_map/ppermute | solution.py:497
  17.4 4.0 %collective-permute-done.3.refs_2_.refs_8_ = bf16[16,128,128]{2,1,0:T(8,128)(2,1)S(1)} collective-permute-done((bf16[16,128,128]{2,1,0:T(8,128)(2,1)S(1)}, bf16[16,128,128]{2,1,0:T(8,128)(2,1)S(1)}, u32[]{:S(2)}, u32[]{:S(2)}) %collective-permute-start.3) | collective-permute-done | bytes 524320 | tf_op jit(solution)/shard_map/ppermute | solution.py:507
  21.4 5.6 %collective-permute-done.8.refs_3_.refs_9_ = bf16[16,128,128]{2,1,0:T(8,128)(2,1)S(1)} collective-permute-done((bf16[16,128,128]{2,1,0:T(8,128)(2,1)S(1)}, bf16[16,128,128]{2,1,0:T(8,128)(2,1)S(1)}, u32[]{:S(2)}, u32[]{:S(2)}) %collective-permute-start.8) | collective-permute-done | bytes 524320 | tf_op jit(solution)/shard_map/ppermute | solution.py:507
  27.0 1.0 collective-permute-start.13
  28.0 6.0 %left_front.1 = (bf16[32,64,128]{2,1,0:T(8,128)(2,1)S(1)}, bf16[32,64,128]{2,1,0:T(8,128)(2,1)S(1)}, bf16[64,128,128]{2,1,0:T(8,128)(2,1)S(1)}, f32[64,1,128]{2,...) custom-call(s32[4,4]{1,0:T(4,128)S(1)} %copy-done.33, bf16[128,64,128]{2,1,0:T(8,128)(2,1)} %pair.1, ...), custom_call_target="tpu_custom_call" | custom-call | flops 1 | bytes 18000000 | tf_op jit(solution)/shard_map/left_front/pallas_call | solution.py:145
  34.0 2.0 %copy-done.24 = bf16[64,256,128]{2,1,0:T(8,128)(2,1)} copy-done((bf16[64,256,128]{2,1,0:T(8,128)(2,1)}, bf16[64,256,128]{2,1,0:T(8,128)(2,1)S(1)}, u32[]{:S(2)}) %copy-start.24) | copy-done | bytes 4194328
  36.0 1.3 %copy-done.26 = bf16[64,128,128]{2,1,0:T(8,128)(2,1)} copy-done((bf16[64,128,128]{2,1,0:T(8,128)(2,1)}, bf16[64,128,128]{2,1,0:T(8,128)(2,1)S(1)}, u32[]{:S(2)}) %copy-start.26) | copy-done | bytes 2097176
  37.3 1.1 collective-permute-start.14
  38.4 0.9 collective-permute-start.15
  39.4 0.5 collective-permute-done.4.by_a.refs_0_
  39.9 1.8 %first_step.2 = (bf16[16,128,128]{2,1,0:T(8,128)(2,1)}, bf16[16,128,128]{2,1,0:T(8,128)(2,1)}) custom-call(bf16[32,64,128]{2,1,0:T(8,128)(2,1)S(1)} %get-tuple-element.44.left_mine, bf16[32,64,128]{2,1,0:T(8,128)(2,1)S(1)} %collective-permute-done.5.left_other, bf16[32,128,128]{2,1,0:T(8,128)(2,1)S(1)} %collective-permute-done.4.by_a.refs_0_, ...), custom_call_target="tpu_custom_call" | custom-call | flops 1 | bytes 8000000 | tf_op jit(solution)/shard_map/first_step/pallas_call | solution.py:270
  41.6 2.7 %collective-permute-start.9 = (bf16[16,128,128]{2,1,0:T(8,128)(2,1)}, bf16[16,128,128]{2,1,0:T(8,128)(2,1)}, u32[]{:S(2)}, u32[]{:S(2)}) collective-permute-start(bf16[16,128,128]{2,1,0:T(8,128)(2,1)} %get-tuple-element.46), channel_id=1, source_target_pairs={{0,8},{1,9},{2,10},{3,11},{4,12},{5,13},{6,14},{7,15},{8,0},{9,1},... | collective-permute-start | bytes 1572872 | tf_op jit(solution)/shard_map/ppermute | solution.py:497
  44.3 2.8 %right_partials.2 = (bf16[16,128,128]{2,1,0:T(8,128)(2,1)}, bf16[16,128,128]{2,1,0:T(8,128)(2,1)}, bf16[16,128,128]{2,1,0:T(8,128)(2,1)}, bf16[16,128,128]{2,1,0:T(8,128)(2,1)}) custom-call(bf16[32,64,128]{2,1,0:T(8,128)(2,1)S(1)} %get-tuple-element.44.left_mine, bf16[32,64,128]{2,1,0:T(8,128)(2,1)S(1)} %collective-permute-done.5.left_other, ...), custom_call_target="tpu_custom_call" | custom-call | flops 1 | bytes 8000000 | tf_op jit(solution)/shard_map/right_partials/pallas_call | solution.py:298
  47.2 5.0 %collective-permute-done.15.refs_3_.refs_9_ = bf16[16,128,128]{2,1,0:T(8,128)(2,1)S(1)} collective-permute-done((bf16[16,128,128]{2,1,0:T(8,128)(2,1)S(1)}, bf16[16,128,128]{2,1,0:T(8,128)(2,1)S(1)}, u32[]{:S(2)}, u32[]{:S(2)}) %collective-permute-start.15) | collective-permute-done | bytes 524320 | tf_op jit(solution)/shard_map/ppermute | solution.py:507
  52.1 1.7 %first_step.3 = (bf16[16,128,128]{2,1,0:T(8,128)(2,1)}, bf16[16,128,128]{2,1,0:T(8,128)(2,1)}) custom-call(bf16[32,64,128]{2,1,0:T(8,128)(2,1)S(1)} %get-tuple-element.44.left_mine, bf16[32,64,128]{2,1,0:T(8,128)(2,1)S(1)} %collective-permute-done.5.left_other, bf16[32,128,128]{2,1,0:T(8,128)(2,1)S(1)} %collective-permute-done.4.by_a.refs_0_, ...), custom_call_target="tpu_custom_call" | custom-call | flops 1 | bytes 8000000 | tf_op jit(solution)/shard_map/first_step/pallas_call | solution.py:270
  53.9 1.6 %collective-permute-start.16 = (bf16[16,128,128]{2,1,0:T(8,128)(2,1)}, bf16[16,128,128]{2,1,0:T(8,128)(2,1)}, u32[]{:S(2)}, u32[]{:S(2)}) collective-permute-start(bf16[16,128,128]{2,1,0:T(8,128)(2,1)} %get-tuple-element.55), channel_id=1, source_target_pairs={{0,8},{1,9},{2,10},{3,11},{4,12},{5,13},{6,14},{7,15},{8,0},{9,1},... | collective-permute-start | bytes 1572872 | tf_op jit(solution)/shard_map/ppermute | solution.py:497
  55.5 3.0 %fusion.11 = (bf16[16,128,128]{2,1,0:T(8,128)(2,1)}, bf16[16,128,128]{2,1,0:T(8,128)(2,1)}) fusion(bf16[16,128,128]{2,1,0:T(8,128)(2,1)} %get-tuple-element.48, bf16[16,128,128]{2,1,0:T(8,128)(2,1)} %collective-permute-done.9.refs_1_, pred[]{:T(512)S(6)} %select_n.163, pred[]{:T(512)S(6)} %ge.8, pred[]{:T(512)S(6)} %lt.7, pred[]{:T(512)S(6)} %eq.2, ...), kind=kLoop, calls=%fused_computation.15 | loop fusion | flops 3407872 | bytes 2621445 | tf_op jit(solution)/shard_map/convert_element_type | solution.py:249
  58.5 3.1 %collective-permute-start.11 = (bf16[16,128,128]{2,1,0:T(8,128)(2,1)}, bf16[16,128,128]{2,1,0:T(8,128)(2,1)}, u32[]{:S(2)}, u32[]{:S(2)}) collective-permute-start(bf16[16,128,128]{2,1,0:T(8,128)(2,1)} %get-tuple-element.76), channel_id=1, source_target_pairs={{0,8},{1,9},{2,10},{3,11},{4,12},{5,13},{6,14},{7,15},{8,0},{9,1},... | collective-permute-start | bytes 1572872 | tf_op jit(solution)/shard_map/ppermute | solution.py:497
  61.7 1.0 copy-done.20
  62.8 2.8 %right_partials.3 = (bf16[16,128,128]{2,1,0:T(8,128)(2,1)}, bf16[16,128,128]{2,1,0:T(8,128)(2,1)}, bf16[16,128,128]{2,1,0:T(8,128)(2,1)}, bf16[16,128,128]{2,1,0:T(8,128)(2,1)}) custom-call(bf16[32,64,128]{2,1,0:T(8,128)(2,1)S(1)} %copy-done.1, bf16[32,64,128]{2,1,0:T(8,128)(2,1)S(1)} %copy-done.3, bf16[16,128,128]{2,1,0:T(8,128)(2,1)S(1)} %copy-done.5, ...), custom_call_target="tpu_custom_call" | custom-call | flops 1 | bytes 8000000 | tf_op jit(solution)/shard_map/right_partials/pallas_call | solution.py:298
  65.5 3.5 %collective-permute-done.16.refs_1_ = bf16[16,128,128]{2,1,0:T(8,128)(2,1)} collective-permute-done((bf16[16,128,128]{2,1,0:T(8,128)(2,1)}, bf16[16,128,128]{2,1,0:T(8,128)(2,1)}, u32[]{:S(2)}, u32[]{:S(2)}) %collective-permute-start.16) | collective-permute-done | bytes 524320 | tf_op jit(solution)/shard_map/ppermute | solution.py:497
  69.0 2.8 %fusion.7 = (bf16[16,128,128]{2,1,0:T(8,128)(2,1)}, bf16[16,128,128]{2,1,0:T(8,128)(2,1)}) fusion(bf16[16,128,128]{2,1,0:T(8,128)(2,1)} %get-tuple-element.57, bf16[16,128,128]{2,1,0:T(8,128)(2,1)} %collective-permute-done.16.refs_1_, pred[]{:T(512)S(6)} %select_n.163, pred[]{:T(512)S(6)} %ge.8, pred[]{:T(512)S(6)} %lt.7, pred[]{:T(512)S(6)} %eq.2, ...), kind=kLoop, calls=%fused_computation.11 | loop fusion | flops 3407872 | bytes 2621445 | tf_op jit(solution)/shard_map/convert_element_type | solution.py:249
  71.9 2.7 %collective-permute-start.18 = (bf16[16,128,128]{2,1,0:T(8,128)(2,1)}, bf16[16,128,128]{2,1,0:T(8,128)(2,1)}, u32[]{:S(2)}, u32[]{:S(2)}) collective-permute-start(bf16[16,128,128]{2,1,0:T(8,128)(2,1)} %get-tuple-element.74), channel_id=1, source_target_pairs={{0,8},{1,9},{2,10},{3,11},{4,12},{5,13},{6,14},{7,15},{8,0},{9,1},... | collective-permute-start | bytes 1572872 | tf_op jit(solution)/shard_map/ppermute | solution.py:497
  74.6 5.7 %collective-permute-done.11.refs_2_ = bf16[16,128,128]{2,1,0:T(8,128)(2,1)} collective-permute-done((bf16[16,128,128]{2,1,0:T(8,128)(2,1)}, bf16[16,128,128]{2,1,0:T(8,128)(2,1)}, u32[]{:S(2)}, u32[]{:S(2)}) %collective-permute-start.11) | collective-permute-done | bytes 524320 | tf_op jit(solution)/shard_map/ppermute | solution.py:497
  80.3 2.1 %add_convert_fusion.2 = (bf16[16,128,128]{2,1,0:T(8,128)(2,1)S(1)}, bf16[16,128,128]{2,1,0:T(8,128)(2,1)S(1)}) fusion(bf16[16,128,128]{2,1,0:T(8,128)(2,1)} %collective-permute-done.11.refs_2_, bf16[16,128,128]{2,1,0:T(8,128)(2,1)} %get-tuple-element.52, bf16[16,128,128]{2,1,0:T(8,128)(2,1)} %get-tuple-element.51, pred[]{:T(512)S(6)} %ge.9, pred[]{:T(512)S(6)} %lt.8, ...), kind=kLoop, calls=%fused_computation.21 | loop fusion | flops 3670016 | bytes 3145733 | tf_op jit(solution)/shard_map/convert_element_type | solution.py:249
  82.3 2.8 %collective-permute-start.22 = (bf16[16,128,128]{2,1,0:T(8,128)(2,1)S(1)}, bf16[16,128,128]{2,1,0:T(8,128)(2,1)S(1)}, u32[]{:S(2)}, u32[]{:S(2)}) collective-permute-start(bf16[16,128,128]{2,1,0:T(8,128)(2,1)S(1)} %get-tuple-element.72), channel_id=1, source_target_pairs={{0,8},{1,9},{2,10},{3,11},{4,12},{5,13},{6,14},{7,15},{8,0},{9,1},... | collective-permute-start | bytes 1572872 | tf_op jit(solution)/shard_map/ppermute | solution.py:497
  85.1 2.4 %left_products.2 = (f32[16,64,128]{2,1,0:T(8,128)S(1)}, bf16[16,64,128]{2,1,0:T(8,128)(2,1)S(1)}) custom-call(bf16[32,128,128]{2,1,0:T(8,128)(2,1)S(1)} %maximum_maximum_fusion.own, bf16[32,128,128]{2,1,0:T(8,128)(2,1)S(1)} %collective-permute-done.4.by_a.refs_0_, bf16[16,128,128]{2,1,0:T(8,128)(2,1)} %collective-permute-done.9.refs_1_, ...), custom_call_target="tpu_custom_call" | custom-call | flops 1 | bytes 8000000 | tf_op jit(solution)/shard_map/left_products/pallas_call | solution.py:338
  87.5 4.0 %collective-permute-done.18.refs_2_ = bf16[16,128,128]{2,1,0:T(8,128)(2,1)} collective-permute-done((bf16[16,128,128]{2,1,0:T(8,128)(2,1)}, bf16[16,128,128]{2,1,0:T(8,128)(2,1)}, u32[]{:S(2)}, u32[]{:S(2)}) %collective-permute-start.18) | collective-permute-done | bytes 524320 | tf_op jit(solution)/shard_map/ppermute | solution.py:497
  91.6 1.9 %add_convert_fusion = (bf16[16,128,128]{2,1,0:T(8,128)(2,1)S(1)}, bf16[16,128,128]{2,1,0:T(8,128)(2,1)S(1)}) fusion(bf16[16,128,128]{2,1,0:T(8,128)(2,1)} %collective-permute-done.18.refs_2_, bf16[16,128,128]{2,1,0:T(8,128)(2,1)S(1)} %copy-done.36, bf16[16,128,128]{2,1,0:T(8,128)(2,1)S(1)} %copy-done.35, pred[]{:T(512)S(6)} %ge.9, pred[]{:T(512)S(6)} %lt.8, ...), kind=kLoop, calls=%fused_computation.17 | loop fusion | flops 3670016 | bytes 3145733 | tf_op jit(solution)/shard_map/convert_element_type | solution.py:249
  93.4 2.8 %collective-permute-start.25 = (bf16[16,128,128]{2,1,0:T(8,128)(2,1)S(1)}, bf16[16,128,128]{2,1,0:T(8,128)(2,1)S(1)}, u32[]{:S(2)}, u32[]{:S(2)}) collective-permute-start(bf16[16,128,128]{2,1,0:T(8,128)(2,1)S(1)} %get-tuple-element.70), channel_id=1, source_target_pairs={{0,8},{1,9},{2,10},{3,11},{4,12},{5,13},{6,14},{7,15},{8,0},{9,1},... | collective-permute-start | bytes 1572872 | tf_op jit(solution)/shard_map/ppermute | solution.py:497
  96.2 0.5 collective-permute-start.20
  96.7 5.9 %collective-permute-done.22.refs_5_ = bf16[16,128,128]{2,1,0:T(8,128)(2,1)S(1)} collective-permute-done((bf16[16,128,128]{2,1,0:T(8,128)(2,1)S(1)}, bf16[16,128,128]{2,1,0:T(8,128)(2,1)S(1)}, u32[]{:S(2)}, u32[]{:S(2)}) %collective-permute-start.22) | collective-permute-done | bytes 524320 | tf_op jit(solution)/shard_map/ppermute | solution.py:497
  102.9 2.4 %left_products.3 = (f32[16,64,128]{2,1,0:T(8,128)S(1)}, bf16[16,64,128]{2,1,0:T(8,128)(2,1)S(1)}) custom-call(bf16[32,128,128]{2,1,0:T(8,128)(2,1)S(1)} %maximum_maximum_fusion.own, bf16[32,128,128]{2,1,0:T(8,128)(2,1)S(1)} %collective-permute-done.4.by_a.refs_0_, bf16[16,128,128]{2,1,0:T(8,128)(2,1)} %collective-permute-done.16.refs_1_, ...), custom_call_target="tpu_custom_call" | custom-call | flops 1 | bytes 8000000 | tf_op jit(solution)/shard_map/left_products/pallas_call | solution.py:338
  105.4 0.4 collective-permute-start.21
  105.8 1.2 %collective-permute-done.21.refs_3_ = bf16[16,64,128]{2,1,0:T(8,128)(2,1)S(1)} collective-permute-done((bf16[16,64,128]{2,1,0:T(8,128)(2,1)S(1)}, bf16[16,64,128]{2,1,0:T(8,128)(2,1)S(1)}, u32[]{:S(2)}, u32[]{:S(2)}) %collective-permute-start.21) | collective-permute-done | bytes 262176 | tf_op jit(solution)/shard_map/ppermute | solution.py:489
  107.0 3.7 %known.1.base = f32[64,128,128]{2,1,0:T(8,128)S(1)} custom-call(bf16[64,256,128]{2,1,0:T(8,128)(2,1)S(1)} %copy-done.25, bf16[128,256]{1,0:T(8,128)(2,1)S(1)} %copy-done.28, f32[16,64,128]{2,1,0:T(8,128)S(1)} %get-tuple-element.49.refs_0_, f32[16,64,128]{2,1,0:T(8,128)S(1)} %get-tuple-element.58.refs_1_, ...), custom_call_target="tpu_custom_call" | custom-call | flops 1 | bytes 8000000 | tf_op jit(solution)/shard_map/known/pallas_call | solution.py:405
  110.7 1.9 %collective-permute-done.25.by_a = bf16[16,128,128]{2,1,0:T(8,128)(2,1)S(1)} collective-permute-done((bf16[16,128,128]{2,1,0:T(8,128)(2,1)S(1)}, bf16[16,128,128]{2,1,0:T(8,128)(2,1)S(1)}, u32[]{:S(2)}, u32[]{:S(2)}) %collective-permute-start.25) | collective-permute-done | bytes 524320 | tf_op jit(solution)/shard_map/ppermute | solution.py:497
  113.1 1.3 %collective-permute-done.27.right_other = bf16[16,64,128]{2,1,0:T(8,128)(2,1)S(1)} collective-permute-done((bf16[16,64,128]{2,1,0:T(8,128)(2,1)S(1)}, bf16[16,64,128]{2,1,0:T(8,128)(2,1)S(1)}, u32[]{:S(2)}, u32[]{:S(2)}) %collective-permute-start.27) | collective-permute-done | bytes 262176 | tf_op jit(solution)/shard_map/ppermute | solution.py:489
  114.4 5.4 %tail.1 = bf16[128,64,128]{2,1,0:T(8,128)(2,1)} custom-call(f32[64,128,128]{2,1,0:T(8,128)S(1)} %known.1.base, bf16[64,128,128]{2,1,0:T(8,128)(2,1)S(1)} %copy-done.27, f32[64,1,128]{2,1,0:T(1,128)S(1)} %get-tuple-element.62.inverse, bf16[64,64,128]{2,1,0:T(8,128)(2,1)S(1)} %copy-done.32, f32[1,128]{1,0:T(1,128)S(1)} %bitcast.5, ...), custom_call_target="tpu_custom_call" | custom-call | flops 1 | bytes 8000000 | tf_op jit(solution)/shard_map/tail/pallas_call | solution.py:459
  (105 shorter events, 1.4 us)
Async XLA Ops:
  1.1 2.1 %collective-permute-start = (bf16[64,32,128]{2,1,0:T(8,128)(2,1)S(1)}, bf16[64,32,128]{2,1,0:T(8,128)(2,1)S(1)}, u32[]{:S(2)}, u32[]{:S(2)}) collective-permute-start(bf16[64,32,128]{2,1,0:T(8,128)(2,1)S(1)} %theirs.1), channel_id=1, source_target_pairs={{0,1},{1,0},{2,3},{3,2},{4,5},{5,4},{6,7},{7,6},{8,9},{9,8},{10,11... | collective-permute-start | bytes 1572872 | tf_op jit(solution)/shard_map/ppermute | solution.py:489
  3.5 40.8 %copy-start.7 = (bf16[16,128,128]{2,1,0:T(8,128)(2,1)}, bf16[16,128,128]{2,1,0:T(8,128)(2,1)S(1)}, u32[]{:S(2)}) copy-start(bf16[16,128,128]{2,1,0:T(8,128)(2,1)S(1)} %get-tuple-element.37.refs_0_.refs_6_) | copy-start | bytes 1572868
  3.5 48.6 %copy-start.4 = (bf16[16,128,128]{2,1,0:T(8,128)(2,1)}, bf16[16,128,128]{2,1,0:T(8,128)(2,1)S(1)}, u32[]{:S(2)}) copy-start(bf16[16,128,128]{2,1,0:T(8,128)(2,1)S(1)} %get-tuple-element.54.refs_0_.refs_6_) | copy-start | bytes 1572868
  3.5 10.2 %collective-permute-start.7 = (bf16[16,128,128]{2,1,0:T(8,128)(2,1)S(1)}, bf16[16,128,128]{2,1,0:T(8,128)(2,1)S(1)}, u32[]{:S(2)}, u32[]{:S(2)}) collective-permute-start(bf16[16,128,128]{2,1,0:T(8,128)(2,1)S(1)} %get-tuple-element.37.refs_0_.refs_6_), channel_id=1, source_target_pairs={{0,2},{1,5},{2,0},{3,7},{4,6},{5,1},{6,4},{7,3},{8,10},{9,13},{10,... | collective-permute-start | bytes 1572872 | tf_op jit(solution)/shard_map/ppermute | solution.py:507
  11.6 4.0 %collective-permute-start.2 = (bf16[16,64,128]{2,1,0:T(8,128)(2,1)S(1)}, bf16[16,64,128]{2,1,0:T(8,128)(2,1)S(1)}, u32[]{:S(2)}, u32[]{:S(2)}) collective-permute-start(bf16[16,64,128]{2,1,0:T(8,128)(2,1)S(1)} %get-tuple-element.78), channel_id=1, source_target_pairs={{0,1},{1,0},{2,3},{3,2},{4,5},{5,4},{6,7},{7,6},{8,9},{9,8},{10,11... | collective-permute-start | bytes 786440 | tf_op jit(solution)/shard_map/ppermute | solution.py:489
  11.7 3.9 %collective-permute-start.1 = (bf16[16,64,128]{2,1,0:T(8,128)(2,1)S(1)}, bf16[16,64,128]{2,1,0:T(8,128)(2,1)S(1)}, u32[]{:S(2)}, u32[]{:S(2)}) collective-permute-start(bf16[16,64,128]{2,1,0:T(8,128)(2,1)S(1)} %get-tuple-element.77), channel_id=1, source_target_pairs={{0,1},{1,0},{2,3},{3,2},{4,5},{5,4},{6,7},{7,6},{8,9},{9,8},{10,11... | collective-permute-start | bytes 786440 | tf_op jit(solution)/shard_map/ppermute | solution.py:489
  12.2 9.2 %collective-permute-start.3 = (bf16[16,128,128]{2,1,0:T(8,128)(2,1)S(1)}, bf16[16,128,128]{2,1,0:T(8,128)(2,1)S(1)}, u32[]{:S(2)}, u32[]{:S(2)}) collective-permute-start(bf16[16,128,128]{2,1,0:T(8,128)(2,1)S(1)} %get-tuple-element.37.refs_0_.refs_6_), channel_id=1, source_target_pairs={{0,4},{1,3},{2,6},{3,1},{4,0},{5,7},{6,2},{7,5},{8,12},{9,11},{10,... | collective-permute-start | bytes 1572872 | tf_op jit(solution)/shard_map/ppermute | solution.py:507
  13.7 30.6 %copy-start.9 = (bf16[16,128,128]{2,1,0:T(8,128)(2,1)}, bf16[16,128,128]{2,1,0:T(8,128)(2,1)S(1)}, u32[]{:S(2)}) copy-start(bf16[16,128,128]{2,1,0:T(8,128)(2,1)S(1)} %collective-permute-done.7.refs_1_.refs_7_) | copy-start | bytes 1572868
  13.7 13.3 %collective-permute-start.8 = (bf16[16,128,128]{2,1,0:T(8,128)(2,1)S(1)}, bf16[16,128,128]{2,1,0:T(8,128)(2,1)S(1)}, u32[]{:S(2)}, u32[]{:S(2)}) collective-permute-start(bf16[16,128,128]{2,1,0:T(8,128)(2,1)S(1)} %collective-permute-done.7.refs_1_.refs_7_), channel_id=1, source_target_pairs={{0,4},{1,3},{2,6},{3,1},{4,0},{5,7},{6,2},{7,5},{8,12},{9,11},{10,... | collective-permute-start | bytes 1572872 | tf_op jit(solution)/shard_map/ppermute | solution.py:507
  15.7 24.1 %collective-permute-start.4 = (bf16[32,128,128]{2,1,0:T(8,128)(2,1)S(1)}, bf16[32,128,128]{2,1,0:T(8,128)(2,1)S(1)}, u32[]{:S(2)}, u32[]{:S(2)}) collective-permute-start(bf16[32,128,128]{2,1,0:T(8,128)(2,1)S(1)} %maximum_maximum_fusion.own), channel_id=1, source_target_pairs={{0,8},{1,9},{2,10},{3,11},{4,12},{5,13},{6,14},{7,15},{8,0},{9,1},... | collective-permute-start | bytes 3145736 | tf_op jit(solution)/shard_map/ppermute | solution.py:497
  17.4 22.5 %collective-permute-start.6 = (bf16[32,128,128]{2,1,0:T(8,128)(2,1)S(1)}, bf16[32,128,128]{2,1,0:T(8,128)(2,1)S(1)}, u32[]{:S(2)}, u32[]{:S(2)}) collective-permute-start(bf16[32,128,128]{2,1,0:T(8,128)(2,1)S(1)} %maximum_maximum_fusion.own), channel_id=1, source_target_pairs={{0,1},{1,0},{2,3},{3,2},{4,5},{5,4},{6,7},{7,6},{8,16},{9,17},{10,... | collective-permute-start | bytes 3145736 | tf_op jit(solution)/shard_map/ppermute | solution.py:497
  21.4 22.9 %copy-start.17 = (bf16[16,128,128]{2,1,0:T(8,128)(2,1)}, bf16[16,128,128]{2,1,0:T(8,128)(2,1)S(1)}, u32[]{:S(2)}) copy-start(bf16[16,128,128]{2,1,0:T(8,128)(2,1)S(1)} %collective-permute-done.3.refs_2_.refs_8_) | copy-start | bytes 1572868
  27.0 17.3 %copy-start.22 = (bf16[16,128,128]{2,1,0:T(8,128)(2,1)}, bf16[16,128,128]{2,1,0:T(8,128)(2,1)S(1)}, u32[]{:S(2)}) copy-start(bf16[16,128,128]{2,1,0:T(8,128)(2,1)S(1)} %collective-permute-done.8.refs_3_.refs_9_) | copy-start | bytes 1572868
  27.0 11.4 %collective-permute-start.13 = (bf16[16,128,128]{2,1,0:T(8,128)(2,1)S(1)}, bf16[16,128,128]{2,1,0:T(8,128)(2,1)S(1)}, u32[]{:S(2)}, u32[]{:S(2)}) collective-permute-start(bf16[16,128,128]{2,1,0:T(8,128)(2,1)S(1)} %get-tuple-element.54.refs_0_.refs_6_), channel_id=1, source_target_pairs={{0,2},{1,5},{2,0},{3,7},{4,6},{5,1},{6,4},{7,3},{8,10},{9,13},{10,... | collective-permute-start | bytes 1572872 | tf_op jit(solution)/shard_map/ppermute | solution.py:507
  37.3 14.8 %copy-start = (bf16[32,64,128]{2,1,0:T(8,128)(2,1)}, bf16[32,64,128]{2,1,0:T(8,128)(2,1)S(1)}, u32[]{:S(2)}) copy-start(bf16[32,64,128]{2,1,0:T(8,128)(2,1)S(1)} %get-tuple-element.44.left_mine) | copy-start | bytes 1572868
  37.3 2.0 %collective-permute-start.5 = (bf16[32,64,128]{2,1,0:T(8,128)(2,1)S(1)}, bf16[32,64,128]{2,1,0:T(8,128)(2,1)S(1)}, u32[]{:S(2)}, u32[]{:S(2)}) collective-permute-start(bf16[32,64,128]{2,1,0:T(8,128)(2,1)S(1)} %get-tuple-element.45), channel_id=1, source_target_pairs={{0,1},{1,0},{2,3},{3,2},{4,5},{5,4},{6,7},{7,6},{8,9},{9,8},{10,11... | collective-permute-start | bytes 1572872 | tf_op jit(solution)/shard_map/ppermute | solution.py:489
  37.3 9.8 %collective-permute-start.14 = (bf16[16,128,128]{2,1,0:T(8,128)(2,1)S(1)}, bf16[16,128,128]{2,1,0:T(8,128)(2,1)S(1)}, u32[]{:S(2)}, u32[]{:S(2)}) collective-permute-start(bf16[16,128,128]{2,1,0:T(8,128)(2,1)S(1)} %get-tuple-element.54.refs_0_.refs_6_), channel_id=1, source_target_pairs={{0,4},{1,3},{2,6},{3,1},{4,0},{5,7},{6,2},{7,5},{8,12},{9,11},{10,... | collective-permute-start | bytes 1572872 | tf_op jit(solution)/shard_map/ppermute | solution.py:507
  38.4 13.7 %copy-start.11 = (bf16[16,128,128]{2,1,0:T(8,128)(2,1)}, bf16[16,128,128]{2,1,0:T(8,128)(2,1)S(1)}, u32[]{:S(2)}) copy-start(bf16[16,128,128]{2,1,0:T(8,128)(2,1)S(1)} %collective-permute-done.13.refs_1_.refs_7_) | copy-start | bytes 1572868
  38.4 13.7 %collective-permute-start.15 = (bf16[16,128,128]{2,1,0:T(8,128)(2,1)S(1)}, bf16[16,128,128]{2,1,0:T(8,128)(2,1)S(1)}, u32[]{:S(2)}, u32[]{:S(2)}) collective-permute-start(bf16[16,128,128]{2,1,0:T(8,128)(2,1)S(1)} %collective-permute-done.13.refs_1_.refs_7_), channel_id=1, source_target_pairs={{0,4},{1,3},{2,6},{3,1},{4,0},{5,7},{6,2},{7,5},{8,12},{9,11},{10,... | collective-permute-start | bytes 1572872 | tf_op jit(solution)/shard_map/ppermute | solution.py:507
  39.4 12.8 %copy-start.2 = (bf16[32,64,128]{2,1,0:T(8,128)(2,1)}, bf16[32,64,128]{2,1,0:T(8,128)(2,1)S(1)}, u32[]{:S(2)}) copy-start(bf16[32,64,128]{2,1,0:T(8,128)(2,1)S(1)} %collective-permute-done.5.left_other) | copy-start | bytes 1572868
  41.6 13.9 %collective-permute-start.9 = (bf16[16,128,128]{2,1,0:T(8,128)(2,1)}, bf16[16,128,128]{2,1,0:T(8,128)(2,1)}, u32[]{:S(2)}, u32[]{:S(2)}) collective-permute-start(bf16[16,128,128]{2,1,0:T(8,128)(2,1)} %get-tuple-element.46), channel_id=1, source_target_pairs={{0,8},{1,9},{2,10},{3,11},{4,12},{5,13},{6,14},{7,15},{8,0},{9,1},... | collective-permute-start | bytes 1572872 | tf_op jit(solution)/shard_map/ppermute | solution.py:497
  44.3 11.2 %collective-permute-start.10 = (bf16[16,128,128]{2,1,0:T(8,128)(2,1)}, bf16[16,128,128]{2,1,0:T(8,128)(2,1)}, u32[]{:S(2)}, u32[]{:S(2)}) collective-permute-start(bf16[16,128,128]{2,1,0:T(8,128)(2,1)} %get-tuple-element.47), channel_id=1, source_target_pairs={{0,1},{1,0},{2,3},{3,2},{4,5},{5,4},{6,7},{7,6},{8,16},{9,17},{10,... | collective-permute-start | bytes 1572872 | tf_op jit(solution)/shard_map/ppermute | solution.py:497
  47.2 6.7 %copy-start.14 = (bf16[16,128,128]{2,1,0:T(8,128)(2,1)}, bf16[16,128,128]{2,1,0:T(8,128)(2,1)S(1)}, u32[]{:S(2)}) copy-start(bf16[16,128,128]{2,1,0:T(8,128)(2,1)S(1)} %collective-permute-done.14.refs_2_.refs_8_) | copy-start | bytes 1572868
  53.9 15.1 %collective-permute-start.16 = (bf16[16,128,128]{2,1,0:T(8,128)(2,1)}, bf16[16,128,128]{2,1,0:T(8,128)(2,1)}, u32[]{:S(2)}, u32[]{:S(2)}) collective-permute-start(bf16[16,128,128]{2,1,0:T(8,128)(2,1)} %get-tuple-element.55), channel_id=1, source_target_pairs={{0,8},{1,9},{2,10},{3,11},{4,12},{5,13},{6,14},{7,15},{8,0},{9,1},... | collective-permute-start | bytes 1572872 | tf_op jit(solution)/shard_map/ppermute | solution.py:497
  55.5 13.6 %collective-permute-start.17 = (bf16[16,128,128]{2,1,0:T(8,128)(2,1)}, bf16[16,128,128]{2,1,0:T(8,128)(2,1)}, u32[]{:S(2)}, u32[]{:S(2)}) collective-permute-start(bf16[16,128,128]{2,1,0:T(8,128)(2,1)} %get-tuple-element.56), channel_id=1, source_target_pairs={{0,1},{1,0},{2,3},{3,2},{4,5},{5,4},{6,7},{7,6},{8,16},{9,17},{10,... | collective-permute-start | bytes 1572872 | tf_op jit(solution)/shard_map/ppermute | solution.py:497
  58.5 21.7 %collective-permute-start.11 = (bf16[16,128,128]{2,1,0:T(8,128)(2,1)}, bf16[16,128,128]{2,1,0:T(8,128)(2,1)}, u32[]{:S(2)}, u32[]{:S(2)}) collective-permute-start(bf16[16,128,128]{2,1,0:T(8,128)(2,1)} %get-tuple-element.76), channel_id=1, source_target_pairs={{0,8},{1,9},{2,10},{3,11},{4,12},{5,13},{6,14},{7,15},{8,0},{9,1},... | collective-permute-start | bytes 1572872 | tf_op jit(solution)/shard_map/ppermute | solution.py:497
  61.7 18.6 %collective-permute-start.12 = (bf16[16,128,128]{2,1,0:T(8,128)(2,1)}, bf16[16,128,128]{2,1,0:T(8,128)(2,1)}, u32[]{:S(2)}, u32[]{:S(2)}) collective-permute-start(bf16[16,128,128]{2,1,0:T(8,128)(2,1)} %get-tuple-element.75), channel_id=1, source_target_pairs={{0,1},{1,0},{2,3},{3,2},{4,5},{5,4},{6,7},{7,6},{8,16},{9,17},{10,... | collective-permute-start | bytes 1572872 | tf_op jit(solution)/shard_map/ppermute | solution.py:497
  71.9 19.6 %collective-permute-start.18 = (bf16[16,128,128]{2,1,0:T(8,128)(2,1)}, bf16[16,128,128]{2,1,0:T(8,128)(2,1)}, u32[]{:S(2)}, u32[]{:S(2)}) collective-permute-start(bf16[16,128,128]{2,1,0:T(8,128)(2,1)} %get-tuple-element.74), channel_id=1, source_target_pairs={{0,8},{1,9},{2,10},{3,11},{4,12},{5,13},{6,14},{7,15},{8,0},{9,1},... | collective-permute-start | bytes 1572872 | tf_op jit(solution)/shard_map/ppermute | solution.py:497
  74.6 16.9 %collective-permute-start.19 = (bf16[16,128,128]{2,1,0:T(8,128)(2,1)}, bf16[16,128,128]{2,1,0:T(8,128)(2,1)}, u32[]{:S(2)}, u32[]{:S(2)}) collective-permute-start(bf16[16,128,128]{2,1,0:T(8,128)(2,1)} %get-tuple-element.73), channel_id=1, source_target_pairs={{0,1},{1,0},{2,3},{3,2},{4,5},{5,4},{6,7},{7,6},{8,16},{9,17},{10,... | collective-permute-start | bytes 1572872 | tf_op jit(solution)/shard_map/ppermute | solution.py:497
  74.6 10.5 %copy-start.8 = (bf16[16,128,128]{2,1,0:T(8,128)(2,1)S(1)}, bf16[16,128,128]{2,1,0:T(8,128)(2,1)}, u32[]{:S(2)}) copy-start(bf16[16,128,128]{2,1,0:T(8,128)(2,1)} %copy-done.7) | copy-start | bytes 1572868
  74.6 10.5 %copy-start.10 = (bf16[16,128,128]{2,1,0:T(8,128)(2,1)S(1)}, bf16[16,128,128]{2,1,0:T(8,128)(2,1)}, u32[]{:S(2)}) copy-start(bf16[16,128,128]{2,1,0:T(8,128)(2,1)} %copy-done.9) | copy-start | bytes 1572868
  74.6 10.5 %copy-start.18 = (bf16[16,128,128]{2,1,0:T(8,128)(2,1)S(1)}, bf16[16,128,128]{2,1,0:T(8,128)(2,1)}, u32[]{:S(2)}) copy-start(bf16[16,128,128]{2,1,0:T(8,128)(2,1)} %copy-done.17) | copy-start | bytes 1572868
  74.6 10.6 %copy-start.23 = (bf16[16,128,128]{2,1,0:T(8,128)(2,1)S(1)}, bf16[16,128,128]{2,1,0:T(8,128)(2,1)}, u32[]{:S(2)}) copy-start(bf16[16,128,128]{2,1,0:T(8,128)(2,1)} %copy-done.22) | copy-start | bytes 1572868
  82.3 20.3 %collective-permute-start.22 = (bf16[16,128,128]{2,1,0:T(8,128)(2,1)S(1)}, bf16[16,128,128]{2,1,0:T(8,128)(2,1)S(1)}, u32[]{:S(2)}, u32[]{:S(2)}) collective-permute-start(bf16[16,128,128]{2,1,0:T(8,128)(2,1)S(1)} %get-tuple-element.72), channel_id=1, source_target_pairs={{0,8},{1,9},{2,10},{3,11},{4,12},{5,13},{6,14},{7,15},{8,0},{9,1},... | collective-permute-start | bytes 1572872 | tf_op jit(solution)/shard_map/ppermute | solution.py:497
  85.1 17.5 %collective-permute-start.23 = (bf16[16,128,128]{2,1,0:T(8,128)(2,1)S(1)}, bf16[16,128,128]{2,1,0:T(8,128)(2,1)S(1)}, u32[]{:S(2)}, u32[]{:S(2)}) collective-permute-start(bf16[16,128,128]{2,1,0:T(8,128)(2,1)S(1)} %get-tuple-element.71), channel_id=1, source_target_pairs={{0,1},{1,0},{2,3},{3,2},{4,5},{5,4},{6,7},{7,6},{8,16},{9,17},{10,... | collective-permute-start | bytes 1572872 | tf_op jit(solution)/shard_map/ppermute | solution.py:497
  87.5 15.1 %copy-start.29 = (bf16[16,128,128]{2,1,0:T(8,128)(2,1)S(1)}, bf16[16,128,128]{2,1,0:T(8,128)(2,1)}, u32[]{:S(2)}) copy-start(bf16[16,128,128]{2,1,0:T(8,128)(2,1)} %get-tuple-element.50.refs_4_) | copy-start | bytes 1572868
  91.5 11.4 %copy-start.6 = (bf16[16,128,128]{2,1,0:T(8,128)(2,1)S(1)}, bf16[16,128,128]{2,1,0:T(8,128)(2,1)}, u32[]{:S(2)}) copy-start(bf16[16,128,128]{2,1,0:T(8,128)(2,1)} %copy-done.4) | copy-start | bytes 1572868
  91.5 11.4 %copy-start.13 = (bf16[16,128,128]{2,1,0:T(8,128)(2,1)S(1)}, bf16[16,128,128]{2,1,0:T(8,128)(2,1)}, u32[]{:S(2)}) copy-start(bf16[16,128,128]{2,1,0:T(8,128)(2,1)} %copy-done.11) | copy-start | bytes 1572868
  91.5 11.4 %copy-start.16 = (bf16[16,128,128]{2,1,0:T(8,128)(2,1)S(1)}, bf16[16,128,128]{2,1,0:T(8,128)(2,1)}, u32[]{:S(2)}) copy-start(bf16[16,128,128]{2,1,0:T(8,128)(2,1)} %copy-done.14) | copy-start | bytes 1572868
  91.5 11.4 %copy-start.21 = (bf16[16,128,128]{2,1,0:T(8,128)(2,1)S(1)}, bf16[16,128,128]{2,1,0:T(8,128)(2,1)}, u32[]{:S(2)}) copy-start(bf16[16,128,128]{2,1,0:T(8,128)(2,1)} %copy-done.19) | copy-start | bytes 1572868
  93.4 19.2 %collective-permute-start.25 = (bf16[16,128,128]{2,1,0:T(8,128)(2,1)S(1)}, bf16[16,128,128]{2,1,0:T(8,128)(2,1)S(1)}, u32[]{:S(2)}, u32[]{:S(2)}) collective-permute-start(bf16[16,128,128]{2,1,0:T(8,128)(2,1)S(1)} %get-tuple-element.70), channel_id=1, source_target_pairs={{0,8},{1,9},{2,10},{3,11},{4,12},{5,13},{6,14},{7,15},{8,0},{9,1},... | collective-permute-start | bytes 1572872 | tf_op jit(solution)/shard_map/ppermute | solution.py:497
  96.2 16.4 %collective-permute-start.26 = (bf16[16,128,128]{2,1,0:T(8,128)(2,1)S(1)}, bf16[16,128,128]{2,1,0:T(8,128)(2,1)S(1)}, u32[]{:S(2)}, u32[]{:S(2)}) collective-permute-start(bf16[16,128,128]{2,1,0:T(8,128)(2,1)S(1)} %get-tuple-element.69), channel_id=1, source_target_pairs={{0,1},{1,0},{2,3},{3,2},{4,5},{5,4},{6,7},{7,6},{8,16},{9,17},{10,... | collective-permute-start | bytes 1572872 | tf_op jit(solution)/shard_map/ppermute | solution.py:497
  96.2 9.6 %collective-permute-start.20 = (bf16[16,64,128]{2,1,0:T(8,128)(2,1)S(1)}, bf16[16,64,128]{2,1,0:T(8,128)(2,1)S(1)}, u32[]{:S(2)}, u32[]{:S(2)}) collective-permute-start(bf16[16,64,128]{2,1,0:T(8,128)(2,1)S(1)} %get-tuple-element.59), channel_id=1, source_target_pairs={{0,1},{1,0},{2,3},{3,2},{4,5},{5,4},{6,7},{7,6},{8,9},{9,8},{10,11... | collective-permute-start | bytes 786440 | tf_op jit(solution)/shard_map/ppermute | solution.py:489
  102.8 2.9 %collective-permute-start.24 = (bf16[16,64,128]{2,1,0:T(8,128)(2,1)S(1)}, bf16[16,64,128]{2,1,0:T(8,128)(2,1)S(1)}, u32[]{:S(2)}, u32[]{:S(2)}) collective-permute-start(bf16[16,64,128]{2,1,0:T(8,128)(2,1)S(1)} %add_convert_fusion.5), channel_id=1, source_target_pairs={{0,1},{1,0},{2,3},{3,2},{4,5},{5,4},{6,7},{7,6},{8,9},{9,8},{10,11... | collective-permute-start | bytes 786440 | tf_op jit(solution)/shard_map/ppermute | solution.py:489
  105.4 1.6 %collective-permute-start.21 = (bf16[16,64,128]{2,1,0:T(8,128)(2,1)S(1)}, bf16[16,64,128]{2,1,0:T(8,128)(2,1)S(1)}, u32[]{:S(2)}, u32[]{:S(2)}) collective-permute-start(bf16[16,64,128]{2,1,0:T(8,128)(2,1)S(1)} %get-tuple-element.60), channel_id=1, source_target_pairs={{0,1},{1,0},{2,3},{3,2},{4,5},{5,4},{6,7},{7,6},{8,9},{9,8},{10,11... | collective-permute-start | bytes 786440 | tf_op jit(solution)/shard_map/ppermute | solution.py:489
  107.0 7.4 %copy-start.27 = (bf16[64,128,128]{2,1,0:T(8,128)(2,1)S(1)}, bf16[64,128,128]{2,1,0:T(8,128)(2,1)}, u32[]{:S(2)}) copy-start(bf16[64,128,128]{2,1,0:T(8,128)(2,1)} %copy-done.26) | copy-start | bytes 6291460
  107.0 7.4 %copy-start.34 = (f32[128]{0:T(128)S(1)}, f32[128]{0:T(128)}, u32[]{:S(2)}) copy-start(f32[128]{0:T(128)} %param.8) | copy-start | bytes 1540
  112.8 1.6 %collective-permute-start.27 = (bf16[16,64,128]{2,1,0:T(8,128)(2,1)S(1)}, bf16[16,64,128]{2,1,0:T(8,128)(2,1)S(1)}, u32[]{:S(2)}, u32[]{:S(2)}) collective-permute-start(bf16[16,64,128]{2,1,0:T(8,128)(2,1)S(1)} %add_convert_fusion.4), channel_id=1, source_target_pairs={{0,1},{1,0},{2,3},{3,2},{4,5},{5,4},{6,7},{7,6},{8,9},{9,8},{10,11... | collective-permute-start | bytes 786440 | tf_op jit(solution)/shard_map/ppermute | solution.py:489
  (17 other events, 78.4 us)

commit v11 on v10

--- a/solution.py
+++ b/solution.py
@@ -47,7 +47,10 @@
     flipped[...] = jnp.transpose(pair[...], (1, 0, 2))
     eye = identity(pair.shape[2])
     for key in range(pair.shape[1]):
-        turned[key] = lax.dot_general(eye, flipped[key], BY_LAST, preferred_element_type=jnp.float32)
+        if key % 2:
+            turned[key] = lax.dot_general(eye, flipped[key], BY_LAST, preferred_element_type=jnp.float32)
+        else:
+            turned[key] = flipped[key].T.astype(jnp.float32)
 
 
 def normalize(values):
@@ -410,7 +413,7 @@
         + [pl.BlockSpec((part, KEYS, rows), lambda g: (0, g, 0))] * len(args),
         out_specs=by_key(chans, rows),
         scratch_shapes=[pltpu.VMEM((KEYS, width, rows), jnp.bfloat16)]
-        + [pltpu.VMEM((CORES * part * KEYS, rows), jnp.float32)] * (2 * CHUNKS - 1),
+        + [pltpu.VMEM(((CORES * part + 1) * KEYS, rows), jnp.float32)] * (2 * CHUNKS - 1),
         compiler_params=PARAMS,
         cost_estimate=COST,
         name="known",
@@ -448,7 +451,11 @@
         results[key] = result.astype(jnp.bfloat16)
     eye = identity(rows)
     for key in range(keys):
-        flipped[key] = lax.dot_general(eye, results[key], BY_LAST, preferred_element_type=jnp.float32).astype(jnp.bfloat16)
+        if key % 2:
+            turned = lax.dot_general(eye, results[key], BY_LAST, preferred_element_type=jnp.float32)
+            flipped[key] = turned.astype(jnp.bfloat16)
+        else:
+            flipped[key] = results[key].T
     out[...] = jnp.transpose(flipped[...], (1, 0, 2))
 
 
@@ -466,7 +473,7 @@
             pltpu.VMEM((KEYS, chans, rows), jnp.bfloat16),
             pltpu.VMEM((KEYS, rows, chans), jnp.bfloat16),
             pltpu.VMEM((KEYS, last.shape[1], rows), jnp.bfloat16),
-            pltpu.VMEM((CORES * part * KEYS, rows), jnp.float32),
+            pltpu.VMEM(((CORES * part + 1) * KEYS, rows), jnp.float32),
             pltpu.VMEM((chans, rows), jnp.float32),
         ],
         compiler_params=PARAMS,
@@ -515,8 +522,7 @@
         panels.append(slots)
 
     right_mine, right_theirs = front(after(pair, packed), gain, bias, proj_weight, tile_mask, True)
-    right_other = [exchange(right_theirs[c * part : (c + 1) * part], 1) for c in range(CHUNKS)]
-    own = jnp.concatenate((right_mine, jnp.concatenate(right_other)), axis=1)
+    own = jnp.concatenate((right_mine, exchange(right_theirs, 1)), axis=1)
     first_a, first_b = hop(own, 0), hop(own, 1)
     left_mine, left_theirs, *forward = front(after(pair, own, panels[0][-2]), gain, bias, proj_weight, tile_mask, False)
     left_other = exchange(left_theirs, 1)

time: 120 us -> 120 us (level)
    ppermute x14, waiting for transfers between devices: 21.5 us -> 23.1 us  [hop(): return lax.ppermute(value, ('row', 'col'), perm)]
    unnamed x74 -> x71, local copies, waits for them, and re-layouts: 4.48 us -> 3.45 us
    ppermute x8 -> x7, waiting for transfers between devices: 3.01 us -> 2.97 us  [exchange(): return lax.ppermute(value, 'col', [(d, d ^ mask) for d in range(n_col)])]
  transfers between devices with their start and end apart: 28 -> 27, of which waited for: 12 -> 14; matrix products, arithmetic and copies ran while one was open for 9% -> 8% of each run, Pallas kernels for 25% -> 25%
where the time goes in v11:
time: 120 us; the launch traced here: 119 us
  waiting for transfers between devices  40 us (33%)
  Pallas kernels  36.1 us (30%)
  starting transfers between devices  28.9 us (24%)
  other arithmetic  10 us (8%)
  local copies, waits for them, and re-layouts  3.62 us (3%)
    ppermute x14, waiting for transfers between devices, hop(): return lax.ppermute(value, ('row', 'col'), perm)  23.1 us
    ppermute x14, starting transfers between devices, hop(): return lax.ppermute(value, ('row', 'col'), perm)  17.3 us
    ppermute x6, waiting for transfers between devices, along(): lax.ppermute(value, 'col', [(d, d ^ mask[d % CORES]) for d in range(n_col)])  13.9 us
    pallas_call x2, Pallas kernels, front(): pl.pallas_call(right_kernel if right else left_forward_kernel, out_shape=...  10.8 us
    ppermute x6, starting transfers between devices, along(): lax.ppermute(value, 'col', [(d, d ^ mask[d % CORES]) for d in range(n_col)])  9.89 us
    convert_element_type x4, other arithmetic, onward(): return (out_a.astype(jnp.bfloat16), out_b.astype(jnp.bfloat16))  9.63 us
    pallas_call x2, Pallas kernels, partial_products(): pl.pallas_call(functools.partial(partial_kernel, n), out_shape=[pltpu.HBM...  5.65 us
    pallas_call x1, Pallas kernels, tail(): pl.pallas_call(functools.partial(tail_kernel, lax.axis_size('row')), out_...  5.14 us
  transfers between devices with their start and end apart: 27, of which 14 were waited for; matrix products, arithmetic and copies ran while one was open for 8% of the time, Pallas kernels for 25%

profile of v11, /device:TPU:0, one launch (start us, length us, event | category | flops | bytes accessed | tf_op | source)
XLA Modules:
  0.0 119.0 jit_solution(4161173271552521185)
XLA Ops:
  0.0 1.1 theirs.1
  1.1 0.5 collective-permute-start
  1.6 1.0 mine.1.own
  2.6 0.5 collective-permute-done.other
  3.5 2.9 %collective-permute-start.6 = (bf16[16,128,128]{2,1,0:T(8,128)(2,1)S(1)}, bf16[16,128,128]{2,1,0:T(8,128)(2,1)S(1)}, u32[]{:S(2)}, u32[]{:S(2)}) collective-permute-start(bf16[16,128,128]{2,1,0:T(8,128)(2,1)S(1)} %get-tuple-element.37.refs_0_.refs_6_), channel_id=1, source_target_pairs={{0,2},{1,5},{2,0},{3,7},{4,6},{5,1},{6,4},{7,3},{8,10},{9,13},{10,... | collective-permute-start | bytes 1572872 | tf_op jit(solution)/shard_map/ppermute | solution.py:514
  6.4 4.9 %right_front.1 = (bf16[32,64,128]{2,1,0:T(8,128)(2,1)S(1)}, bf16[32,64,128]{2,1,0:T(8,128)(2,1)S(1)}) custom-call(s32[4,4]{1,0:T(4,128)S(1)} %copy-done.31, bf16[128,64,128]{2,1,0:T(8,128)(2,1)} %pair.1, f32[1,128]{1,0:T(1,128)} %bitcast.3, f32[1,128]{1,0:T(1,128)} %bitcast.8, bf16[128,256]{1,0:T(8,128)(2,1)} %weight.5), custom_call_target="tpu_custom_call" | custom-call | flops 1 | bytes 18000000 | tf_op jit(solution)/shard_map/right_front/pallas_call | solution.py:148
  11.5 1.6 %collective-permute-start.2 = (bf16[16,128,128]{2,1,0:T(8,128)(2,1)S(1)}, bf16[16,128,128]{2,1,0:T(8,128)(2,1)S(1)}, u32[]{:S(2)}, u32[]{:S(2)}) collective-permute-start(bf16[16,128,128]{2,1,0:T(8,128)(2,1)S(1)} %get-tuple-element.37.refs_0_.refs_6_), channel_id=1, source_target_pairs={{0,4},{1,3},{2,6},{3,1},{4,0},{5,7},{6,2},{7,5},{8,12},{9,11},{10,... | collective-permute-start | bytes 1572872 | tf_op jit(solution)/shard_map/ppermute | solution.py:514
  13.1 0.5 collective-permute-done.6.refs_1_.refs_7_
  13.6 2.0 %collective-permute-start.7 = (bf16[16,128,128]{2,1,0:T(8,128)(2,1)S(1)}, bf16[16,128,128]{2,1,0:T(8,128)(2,1)S(1)}, u32[]{:S(2)}, u32[]{:S(2)}) collective-permute-start(bf16[16,128,128]{2,1,0:T(8,128)(2,1)S(1)} %collective-permute-done.6.refs_1_.refs_7_), channel_id=1, source_target_pairs={{0,4},{1,3},{2,6},{3,1},{4,0},{5,7},{6,2},{7,5},{8,12},{9,11},{10,... | collective-permute-start | bytes 1572872 | tf_op jit(solution)/shard_map/ppermute | solution.py:514
  15.7 1.6 %collective-permute-start.3 = (bf16[32,128,128]{2,1,0:T(8,128)(2,1)S(1)}, bf16[32,128,128]{2,1,0:T(8,128)(2,1)S(1)}, u32[]{:S(2)}, u32[]{:S(2)}) collective-permute-start(bf16[32,128,128]{2,1,0:T(8,128)(2,1)S(1)} %constant_dynamic-update-slice_fusion.own), channel_id=1, source_target_pairs={{0,8},{1,9},{2,10},{3,11},{4,12},{5,13},{6,14},{7,15},{8,0},{9,1},... | collective-permute-start | bytes 3145736 | tf_op jit(solution)/shard_map/ppermute | solution.py:504
  17.4 3.3 %collective-permute-done.2.refs_2_.refs_8_ = bf16[16,128,128]{2,1,0:T(8,128)(2,1)S(1)} collective-permute-done((bf16[16,128,128]{2,1,0:T(8,128)(2,1)S(1)}, bf16[16,128,128]{2,1,0:T(8,128)(2,1)S(1)}, u32[]{:S(2)}, u32[]{:S(2)}) %collective-permute-start.2) | collective-permute-done | bytes 524320 | tf_op jit(solution)/shard_map/ppermute | solution.py:514
  20.7 5.6 %collective-permute-done.7.refs_3_.refs_9_ = bf16[16,128,128]{2,1,0:T(8,128)(2,1)S(1)} collective-permute-done((bf16[16,128,128]{2,1,0:T(8,128)(2,1)S(1)}, bf16[16,128,128]{2,1,0:T(8,128)(2,1)S(1)}, u32[]{:S(2)}, u32[]{:S(2)}) %collective-permute-start.7) | collective-permute-done | bytes 524320 | tf_op jit(solution)/shard_map/ppermute | solution.py:514
  26.3 1.3 %collective-permute-start.12 = (bf16[16,128,128]{2,1,0:T(8,128)(2,1)S(1)}, bf16[16,128,128]{2,1,0:T(8,128)(2,1)S(1)}, u32[]{:S(2)}, u32[]{:S(2)}) collective-permute-start(bf16[16,128,128]{2,1,0:T(8,128)(2,1)S(1)} %get-tuple-element.54.refs_0_.refs_6_), channel_id=1, source_target_pairs={{0,2},{1,5},{2,0},{3,7},{4,6},{5,1},{6,4},{7,3},{8,10},{9,13},{10,... | collective-permute-start | bytes 1572872 | tf_op jit(solution)/shard_map/ppermute | solution.py:514
  27.6 5.9 %left_front.1 = (bf16[32,64,128]{2,1,0:T(8,128)(2,1)S(1)}, bf16[32,64,128]{2,1,0:T(8,128)(2,1)S(1)}, bf16[64,128,128]{2,1,0:T(8,128)(2,1)S(1)}, f32[64,1,128]{2,...) custom-call(s32[4,4]{1,0:T(4,128)S(1)} %copy-done.31, bf16[128,64,128]{2,1,0:T(8,128)(2,1)} %pair.1, ...), custom_call_target="tpu_custom_call" | custom-call | flops 1 | bytes 18000000 | tf_op jit(solution)/shard_map/left_front/pallas_call | solution.py:148
  33.5 2.0 %copy-done.22 = bf16[64,256,128]{2,1,0:T(8,128)(2,1)} copy-done((bf16[64,256,128]{2,1,0:T(8,128)(2,1)}, bf16[64,256,128]{2,1,0:T(8,128)(2,1)S(1)}, u32[]{:S(2)}) %copy-start.22) | copy-done | bytes 4194328
  35.5 1.3 %copy-done.24 = bf16[64,128,128]{2,1,0:T(8,128)(2,1)} copy-done((bf16[64,128,128]{2,1,0:T(8,128)(2,1)}, bf16[64,128,128]{2,1,0:T(8,128)(2,1)S(1)}, u32[]{:S(2)}) %copy-start.24) | copy-done | bytes 2097176
  36.8 0.7 collective-permute-start.13
  37.6 1.3 %collective-permute-start.14 = (bf16[16,128,128]{2,1,0:T(8,128)(2,1)S(1)}, bf16[16,128,128]{2,1,0:T(8,128)(2,1)S(1)}, u32[]{:S(2)}, u32[]{:S(2)}) collective-permute-start(bf16[16,128,128]{2,1,0:T(8,128)(2,1)S(1)} %collective-permute-done.12.refs_1_.refs_7_), channel_id=1, source_target_pairs={{0,4},{1,3},{2,6},{3,1},{4,0},{5,7},{6,2},{7,5},{8,12},{9,11},{10,... | collective-permute-start | bytes 1572872 | tf_op jit(solution)/shard_map/ppermute | solution.py:514
  38.9 1.0 collective-permute-done.3.by_a.refs_0_
  39.8 1.7 %first_step.2 = (bf16[16,128,128]{2,1,0:T(8,128)(2,1)}, bf16[16,128,128]{2,1,0:T(8,128)(2,1)}) custom-call(bf16[32,64,128]{2,1,0:T(8,128)(2,1)S(1)} %get-tuple-element.44.left_mine, bf16[32,64,128]{2,1,0:T(8,128)(2,1)S(1)} %collective-permute-done.4.left_other, bf16[32,128,128]{2,1,0:T(8,128)(2,1)S(1)} %collective-permute-done.3.by_a.refs_0_, ...), custom_call_target="tpu_custom_call" | custom-call | flops 1 | bytes 8000000 | tf_op jit(solution)/shard_map/first_step/pallas_call | solution.py:273
  41.6 2.7 %collective-permute-start.8 = (bf16[16,128,128]{2,1,0:T(8,128)(2,1)}, bf16[16,128,128]{2,1,0:T(8,128)(2,1)}, u32[]{:S(2)}, u32[]{:S(2)}) collective-permute-start(bf16[16,128,128]{2,1,0:T(8,128)(2,1)} %get-tuple-element.46), channel_id=1, source_target_pairs={{0,8},{1,9},{2,10},{3,11},{4,12},{5,13},{6,14},{7,15},{8,0},{9,1},... | collective-permute-start | bytes 1572872 | tf_op jit(solution)/shard_map/ppermute | solution.py:504
  44.3 2.8 %right_partials.2 = (bf16[16,128,128]{2,1,0:T(8,128)(2,1)}, bf16[16,128,128]{2,1,0:T(8,128)(2,1)}, bf16[16,128,128]{2,1,0:T(8,128)(2,1)}, bf16[16,128,128]{2,1,0:T(8,128)(2,1)}) custom-call(bf16[32,64,128]{2,1,0:T(8,128)(2,1)S(1)} %get-tuple-element.44.left_mine, bf16[32,64,128]{2,1,0:T(8,128)(2,1)S(1)} %collective-permute-done.4.left_other, ...), custom_call_target="tpu_custom_call" | custom-call | flops 1 | bytes 8000000 | tf_op jit(solution)/shard_map/right_partials/pallas_call | solution.py:301
  47.2 4.5 %collective-permute-done.14.refs_3_.refs_9_ = bf16[16,128,128]{2,1,0:T(8,128)(2,1)S(1)} collective-permute-done((bf16[16,128,128]{2,1,0:T(8,128)(2,1)S(1)}, bf16[16,128,128]{2,1,0:T(8,128)(2,1)S(1)}, u32[]{:S(2)}, u32[]{:S(2)}) %collective-permute-start.14) | collective-permute-done | bytes 524320 | tf_op jit(solution)/shard_map/ppermute | solution.py:514
  51.6 1.7 %first_step.3 = (bf16[16,128,128]{2,1,0:T(8,128)(2,1)}, bf16[16,128,128]{2,1,0:T(8,128)(2,1)}) custom-call(bf16[32,64,128]{2,1,0:T(8,128)(2,1)S(1)} %get-tuple-element.44.left_mine, bf16[32,64,128]{2,1,0:T(8,128)(2,1)S(1)} %collective-permute-done.4.left_other, bf16[32,128,128]{2,1,0:T(8,128)(2,1)S(1)} %collective-permute-done.3.by_a.refs_0_, ...), custom_call_target="tpu_custom_call" | custom-call | flops 1 | bytes 8000000 | tf_op jit(solution)/shard_map/first_step/pallas_call | solution.py:273
  53.4 1.6 %collective-permute-start.15 = (bf16[16,128,128]{2,1,0:T(8,128)(2,1)}, bf16[16,128,128]{2,1,0:T(8,128)(2,1)}, u32[]{:S(2)}, u32[]{:S(2)}) collective-permute-start(bf16[16,128,128]{2,1,0:T(8,128)(2,1)} %get-tuple-element.55), channel_id=1, source_target_pairs={{0,8},{1,9},{2,10},{3,11},{4,12},{5,13},{6,14},{7,15},{8,0},{9,1},... | collective-permute-start | bytes 1572872 | tf_op jit(solution)/shard_map/ppermute | solution.py:504
  55.0 3.0 %fusion.11 = (bf16[16,128,128]{2,1,0:T(8,128)(2,1)}, bf16[16,128,128]{2,1,0:T(8,128)(2,1)}) fusion(bf16[16,128,128]{2,1,0:T(8,128)(2,1)} %get-tuple-element.48, bf16[16,128,128]{2,1,0:T(8,128)(2,1)} %collective-permute-done.8.refs_1_, pred[]{:T(512)S(6)} %select_n.163, pred[]{:T(512)S(6)} %ge.8, pred[]{:T(512)S(6)} %lt.7, pred[]{:T(512)S(6)} %eq.2, ...), kind=kLoop, calls=%fused_computation.15 | loop fusion | flops 3407872 | bytes 2621445 | tf_op jit(solution)/shard_map/convert_element_type | solution.py:252
  58.0 3.1 %collective-permute-start.10 = (bf16[16,128,128]{2,1,0:T(8,128)(2,1)}, bf16[16,128,128]{2,1,0:T(8,128)(2,1)}, u32[]{:S(2)}, u32[]{:S(2)}) collective-permute-start(bf16[16,128,128]{2,1,0:T(8,128)(2,1)} %get-tuple-element.76), channel_id=1, source_target_pairs={{0,8},{1,9},{2,10},{3,11},{4,12},{5,13},{6,14},{7,15},{8,0},{9,1},... | collective-permute-start | bytes 1572872 | tf_op jit(solution)/shard_map/ppermute | solution.py:504
  61.2 2.8 %right_partials.3 = (bf16[16,128,128]{2,1,0:T(8,128)(2,1)}, bf16[16,128,128]{2,1,0:T(8,128)(2,1)}, bf16[16,128,128]{2,1,0:T(8,128)(2,1)}, bf16[16,128,128]{2,1,0:T(8,128)(2,1)}) custom-call(bf16[32,64,128]{2,1,0:T(8,128)(2,1)S(1)} %get-tuple-element.44.left_mine, bf16[32,64,128]{2,1,0:T(8,128)(2,1)S(1)} %collective-permute-done.4.left_other, ...), custom_call_target="tpu_custom_call" | custom-call | flops 1 | bytes 8000000 | tf_op jit(solution)/shard_map/right_partials/pallas_call | solution.py:301
  64.0 4.5 %collective-permute-done.15.refs_1_ = bf16[16,128,128]{2,1,0:T(8,128)(2,1)} collective-permute-done((bf16[16,128,128]{2,1,0:T(8,128)(2,1)}, bf16[16,128,128]{2,1,0:T(8,128)(2,1)}, u32[]{:S(2)}, u32[]{:S(2)}) %collective-permute-start.15) | collective-permute-done | bytes 524320 | tf_op jit(solution)/shard_map/ppermute | solution.py:504
  68.5 2.8 %fusion.7 = (bf16[16,128,128]{2,1,0:T(8,128)(2,1)}, bf16[16,128,128]{2,1,0:T(8,128)(2,1)}) fusion(bf16[16,128,128]{2,1,0:T(8,128)(2,1)} %get-tuple-element.57, bf16[16,128,128]{2,1,0:T(8,128)(2,1)} %collective-permute-done.15.refs_1_, pred[]{:T(512)S(6)} %select_n.163, pred[]{:T(512)S(6)} %ge.8, pred[]{:T(512)S(6)} %lt.7, pred[]{:T(512)S(6)} %eq.2, ...), kind=kLoop, calls=%fused_computation.11 | loop fusion | flops 3407872 | bytes 2621445 | tf_op jit(solution)/shard_map/convert_element_type | solution.py:252
  71.4 2.7 %collective-permute-start.17 = (bf16[16,128,128]{2,1,0:T(8,128)(2,1)}, bf16[16,128,128]{2,1,0:T(8,128)(2,1)}, u32[]{:S(2)}, u32[]{:S(2)}) collective-permute-start(bf16[16,128,128]{2,1,0:T(8,128)(2,1)} %get-tuple-element.74), channel_id=1, source_target_pairs={{0,8},{1,9},{2,10},{3,11},{4,12},{5,13},{6,14},{7,15},{8,0},{9,1},... | collective-permute-start | bytes 1572872 | tf_op jit(solution)/shard_map/ppermute | solution.py:504
  74.1 5.7 %collective-permute-done.10.refs_2_ = bf16[16,128,128]{2,1,0:T(8,128)(2,1)} collective-permute-done((bf16[16,128,128]{2,1,0:T(8,128)(2,1)}, bf16[16,128,128]{2,1,0:T(8,128)(2,1)}, u32[]{:S(2)}, u32[]{:S(2)}) %collective-permute-start.10) | collective-permute-done | bytes 524320 | tf_op jit(solution)/shard_map/ppermute | solution.py:504
  79.8 2.1 %add_convert_fusion.2 = (bf16[16,128,128]{2,1,0:T(8,128)(2,1)S(1)}, bf16[16,128,128]{2,1,0:T(8,128)(2,1)S(1)}) fusion(bf16[16,128,128]{2,1,0:T(8,128)(2,1)} %collective-permute-done.10.refs_2_, bf16[16,128,128]{2,1,0:T(8,128)(2,1)} %get-tuple-element.52, bf16[16,128,128]{2,1,0:T(8,128)(2,1)} %get-tuple-element.51, pred[]{:T(512)S(6)} %ge.9, pred[]{:T(512)S(6)} %lt.8, ...), kind=kLoop, calls=%fused_computation.20 | loop fusion | flops 3670016 | bytes 3145733 | tf_op jit(solution)/shard_map/convert_element_type | solution.py:252
  81.8 2.8 %collective-permute-start.21 = (bf16[16,128,128]{2,1,0:T(8,128)(2,1)S(1)}, bf16[16,128,128]{2,1,0:T(8,128)(2,1)S(1)}, u32[]{:S(2)}, u32[]{:S(2)}) collective-permute-start(bf16[16,128,128]{2,1,0:T(8,128)(2,1)S(1)} %get-tuple-element.72), channel_id=1, source_target_pairs={{0,8},{1,9},{2,10},{3,11},{4,12},{5,13},{6,14},{7,15},{8,0},{9,1},... | collective-permute-start | bytes 1572872 | tf_op jit(solution)/shard_map/ppermute | solution.py:504
  84.6 2.4 %left_products.2 = (f32[16,64,128]{2,1,0:T(8,128)S(1)}, bf16[16,64,128]{2,1,0:T(8,128)(2,1)S(1)}) custom-call(bf16[32,128,128]{2,1,0:T(8,128)(2,1)S(1)} %copy-done.1, bf16[32,128,128]{2,1,0:T(8,128)(2,1)S(1)} %collective-permute-done.3.by_a.refs_0_, bf16[16,128,128]{2,1,0:T(8,128)(2,1)} %collective-permute-done.8.refs_1_, ...), custom_call_target="tpu_custom_call" | custom-call | flops 1 | bytes 8000000 | tf_op jit(solution)/shard_map/left_products/pallas_call | solution.py:341
  87.0 4.0 %collective-permute-done.17.refs_2_ = bf16[16,128,128]{2,1,0:T(8,128)(2,1)} collective-permute-done((bf16[16,128,128]{2,1,0:T(8,128)(2,1)}, bf16[16,128,128]{2,1,0:T(8,128)(2,1)}, u32[]{:S(2)}, u32[]{:S(2)}) %collective-permute-start.17) | collective-permute-done | bytes 524320 | tf_op jit(solution)/shard_map/ppermute | solution.py:504
  91.0 1.7 %add_convert_fusion = (bf16[16,128,128]{2,1,0:T(8,128)(2,1)S(1)}, bf16[16,128,128]{2,1,0:T(8,128)(2,1)S(1)}) fusion(bf16[16,128,128]{2,1,0:T(8,128)(2,1)} %collective-permute-done.17.refs_2_, bf16[16,128,128]{2,1,0:T(8,128)(2,1)S(1)} %copy-done.34, bf16[16,128,128]{2,1,0:T(8,128)(2,1)S(1)} %copy-done.33, pred[]{:T(512)S(6)} %ge.9, pred[]{:T(512)S(6)} %lt.8, ...), kind=kLoop, calls=%fused_computation.16 | loop fusion | flops 3670016 | bytes 3145733 | tf_op jit(solution)/shard_map/convert_element_type | solution.py:252
  92.8 2.8 %collective-permute-start.24 = (bf16[16,128,128]{2,1,0:T(8,128)(2,1)S(1)}, bf16[16,128,128]{2,1,0:T(8,128)(2,1)S(1)}, u32[]{:S(2)}, u32[]{:S(2)}) collective-permute-start(bf16[16,128,128]{2,1,0:T(8,128)(2,1)S(1)} %get-tuple-element.70), channel_id=1, source_target_pairs={{0,8},{1,9},{2,10},{3,11},{4,12},{5,13},{6,14},{7,15},{8,0},{9,1},... | collective-permute-start | bytes 1572872 | tf_op jit(solution)/shard_map/ppermute | solution.py:504
  95.5 0.5 collective-permute-start.19
  96.1 2.4 %left_products.3 = (f32[16,64,128]{2,1,0:T(8,128)S(1)}, bf16[16,64,128]{2,1,0:T(8,128)(2,1)S(1)}) custom-call(bf16[32,128,128]{2,1,0:T(8,128)(2,1)S(1)} %copy-done.1, bf16[32,128,128]{2,1,0:T(8,128)(2,1)S(1)} %collective-permute-done.3.by_a.refs_0_, bf16[16,128,128]{2,1,0:T(8,128)(2,1)} %collective-permute-done.15.refs_1_, ...), custom_call_target="tpu_custom_call" | custom-call | flops 1 | bytes 8000000 | tf_op jit(solution)/shard_map/left_products/pallas_call | solution.py:341
  98.5 3.6 %collective-permute-done.21.refs_5_ = bf16[16,128,128]{2,1,0:T(8,128)(2,1)S(1)} collective-permute-done((bf16[16,128,128]{2,1,0:T(8,128)(2,1)S(1)}, bf16[16,128,128]{2,1,0:T(8,128)(2,1)S(1)}, u32[]{:S(2)}, u32[]{:S(2)}) %collective-permute-start.21) | collective-permute-done | bytes 524320 | tf_op jit(solution)/shard_map/ppermute | solution.py:504
  102.3 0.6 collective-permute-start.23
  102.9 0.8 collective-permute-done.20.refs_3_
  103.7 0.4 collective-permute-done.23.refs_7_
  104.1 3.7 %known.1.base = f32[64,128,128]{2,1,0:T(8,128)S(1)} custom-call(bf16[64,256,128]{2,1,0:T(8,128)(2,1)S(1)} %copy-done.23, bf16[128,256]{1,0:T(8,128)(2,1)S(1)} %copy-done.26, f32[16,64,128]{2,1,0:T(8,128)S(1)} %get-tuple-element.49.refs_0_, f32[16,64,128]{2,1,0:T(8,128)S(1)} %get-tuple-element.58.refs_1_, ...), custom_call_target="tpu_custom_call" | custom-call | flops 1 | bytes 8000000 | tf_op jit(solution)/shard_map/known/pallas_call | solution.py:408
  107.8 4.3 %collective-permute-done.24.by_a = bf16[16,128,128]{2,1,0:T(8,128)(2,1)S(1)} collective-permute-done((bf16[16,128,128]{2,1,0:T(8,128)(2,1)S(1)}, bf16[16,128,128]{2,1,0:T(8,128)(2,1)S(1)}, u32[]{:S(2)}, u32[]{:S(2)}) %collective-permute-start.24) | collective-permute-done | bytes 524320 | tf_op jit(solution)/shard_map/ppermute | solution.py:504
  112.6 1.3 %collective-permute-done.26.right_other = bf16[16,64,128]{2,1,0:T(8,128)(2,1)S(1)} collective-permute-done((bf16[16,64,128]{2,1,0:T(8,128)(2,1)S(1)}, bf16[16,64,128]{2,1,0:T(8,128)(2,1)S(1)}, u32[]{:S(2)}, u32[]{:S(2)}) %collective-permute-start.26) | collective-permute-done | bytes 262176 | tf_op jit(solution)/shard_map/ppermute | solution.py:496
  113.9 5.1 %tail.1 = bf16[128,64,128]{2,1,0:T(8,128)(2,1)} custom-call(f32[64,128,128]{2,1,0:T(8,128)S(1)} %known.1.base, bf16[64,128,128]{2,1,0:T(8,128)(2,1)S(1)} %copy-done.25, f32[64,1,128]{2,1,0:T(1,128)S(1)} %get-tuple-element.62.inverse, bf16[64,64,128]{2,1,0:T(8,128)(2,1)S(1)} %copy-done.30, f32[1,128]{1,0:T(1,128)S(1)} %bitcast.5, ...), custom_call_target="tpu_custom_call" | custom-call | flops 1 | bytes 8000000 | tf_op jit(solution)/shard_map/tail/pallas_call | solution.py:466
  (99 shorter events, 1.3 us)
Async XLA Ops:
  1.1 2.1 %collective-permute-start = (bf16[64,32,128]{2,1,0:T(8,128)(2,1)S(1)}, bf16[64,32,128]{2,1,0:T(8,128)(2,1)S(1)}, u32[]{:S(2)}, u32[]{:S(2)}) collective-permute-start(bf16[64,32,128]{2,1,0:T(8,128)(2,1)S(1)} %theirs.1), channel_id=1, source_target_pairs={{0,1},{1,0},{2,3},{3,2},{4,5},{5,4},{6,7},{7,6},{8,9},{9,8},{10,11... | collective-permute-start | bytes 1572872 | tf_op jit(solution)/shard_map/ppermute | solution.py:496
  3.5 40.8 %copy-start.5 = (bf16[16,128,128]{2,1,0:T(8,128)(2,1)}, bf16[16,128,128]{2,1,0:T(8,128)(2,1)S(1)}, u32[]{:S(2)}) copy-start(bf16[16,128,128]{2,1,0:T(8,128)(2,1)S(1)} %get-tuple-element.37.refs_0_.refs_6_) | copy-start | bytes 1572868
  3.5 48.1 %copy-start.2 = (bf16[16,128,128]{2,1,0:T(8,128)(2,1)}, bf16[16,128,128]{2,1,0:T(8,128)(2,1)S(1)}, u32[]{:S(2)}) copy-start(bf16[16,128,128]{2,1,0:T(8,128)(2,1)S(1)} %get-tuple-element.54.refs_0_.refs_6_) | copy-start | bytes 1572868
  3.5 10.1 %collective-permute-start.6 = (bf16[16,128,128]{2,1,0:T(8,128)(2,1)S(1)}, bf16[16,128,128]{2,1,0:T(8,128)(2,1)S(1)}, u32[]{:S(2)}, u32[]{:S(2)}) collective-permute-start(bf16[16,128,128]{2,1,0:T(8,128)(2,1)S(1)} %get-tuple-element.37.refs_0_.refs_6_), channel_id=1, source_target_pairs={{0,2},{1,5},{2,0},{3,7},{4,6},{5,1},{6,4},{7,3},{8,10},{9,13},{10,... | collective-permute-start | bytes 1572872 | tf_op jit(solution)/shard_map/ppermute | solution.py:514
  11.4 4.3 %collective-permute-start.1 = (bf16[32,64,128]{2,1,0:T(8,128)(2,1)S(1)}, bf16[32,64,128]{2,1,0:T(8,128)(2,1)S(1)}, u32[]{:S(2)}, u32[]{:S(2)}) collective-permute-start(bf16[32,64,128]{2,1,0:T(8,128)(2,1)S(1)} %get-tuple-element.41), channel_id=1, source_target_pairs={{0,1},{1,0},{2,3},{3,2},{4,5},{5,4},{6,7},{7,6},{8,9},{9,8},{10,11... | collective-permute-start | bytes 1572872 | tf_op jit(solution)/shard_map/ppermute | solution.py:496
  11.5 9.2 %collective-permute-start.2 = (bf16[16,128,128]{2,1,0:T(8,128)(2,1)S(1)}, bf16[16,128,128]{2,1,0:T(8,128)(2,1)S(1)}, u32[]{:S(2)}, u32[]{:S(2)}) collective-permute-start(bf16[16,128,128]{2,1,0:T(8,128)(2,1)S(1)} %get-tuple-element.37.refs_0_.refs_6_), channel_id=1, source_target_pairs={{0,4},{1,3},{2,6},{3,1},{4,0},{5,7},{6,2},{7,5},{8,12},{9,11},{10,... | collective-permute-start | bytes 1572872 | tf_op jit(solution)/shard_map/ppermute | solution.py:514
  13.6 30.7 %copy-start.7 = (bf16[16,128,128]{2,1,0:T(8,128)(2,1)}, bf16[16,128,128]{2,1,0:T(8,128)(2,1)S(1)}, u32[]{:S(2)}) copy-start(bf16[16,128,128]{2,1,0:T(8,128)(2,1)S(1)} %collective-permute-done.6.refs_1_.refs_7_) | copy-start | bytes 1572868
  13.6 12.7 %collective-permute-start.7 = (bf16[16,128,128]{2,1,0:T(8,128)(2,1)S(1)}, bf16[16,128,128]{2,1,0:T(8,128)(2,1)S(1)}, u32[]{:S(2)}, u32[]{:S(2)}) collective-permute-start(bf16[16,128,128]{2,1,0:T(8,128)(2,1)S(1)} %collective-permute-done.6.refs_1_.refs_7_), channel_id=1, source_target_pairs={{0,4},{1,3},{2,6},{3,1},{4,0},{5,7},{6,2},{7,5},{8,12},{9,11},{10,... | collective-permute-start | bytes 1572872 | tf_op jit(solution)/shard_map/ppermute | solution.py:514
  15.7 25.9 %copy-start = (bf16[32,128,128]{2,1,0:T(8,128)(2,1)}, bf16[32,128,128]{2,1,0:T(8,128)(2,1)S(1)}, u32[]{:S(2)}) copy-start(bf16[32,128,128]{2,1,0:T(8,128)(2,1)S(1)} %constant_dynamic-update-slice_fusion.own) | copy-start | bytes 3145732
  15.7 24.1 %collective-permute-start.3 = (bf16[32,128,128]{2,1,0:T(8,128)(2,1)S(1)}, bf16[32,128,128]{2,1,0:T(8,128)(2,1)S(1)}, u32[]{:S(2)}, u32[]{:S(2)}) collective-permute-start(bf16[32,128,128]{2,1,0:T(8,128)(2,1)S(1)} %constant_dynamic-update-slice_fusion.own), channel_id=1, source_target_pairs={{0,8},{1,9},{2,10},{3,11},{4,12},{5,13},{6,14},{7,15},{8,0},{9,1},... | collective-permute-start | bytes 3145736 | tf_op jit(solution)/shard_map/ppermute | solution.py:504
  17.4 22.5 %collective-permute-start.5 = (bf16[32,128,128]{2,1,0:T(8,128)(2,1)S(1)}, bf16[32,128,128]{2,1,0:T(8,128)(2,1)S(1)}, u32[]{:S(2)}, u32[]{:S(2)}) collective-permute-start(bf16[32,128,128]{2,1,0:T(8,128)(2,1)S(1)} %constant_dynamic-update-slice_fusion.own), channel_id=1, source_target_pairs={{0,1},{1,0},{2,3},{3,2},{4,5},{5,4},{6,7},{7,6},{8,16},{9,17},{10,... | collective-permute-start | bytes 3145736 | tf_op jit(solution)/shard_map/ppermute | solution.py:504
  20.7 23.6 %copy-start.12 = (bf16[16,128,128]{2,1,0:T(8,128)(2,1)}, bf16[16,128,128]{2,1,0:T(8,128)(2,1)S(1)}, u32[]{:S(2)}) copy-start(bf16[16,128,128]{2,1,0:T(8,128)(2,1)S(1)} %collective-permute-done.2.refs_2_.refs_8_) | copy-start | bytes 1572868
  26.3 18.0 %copy-start.17 = (bf16[16,128,128]{2,1,0:T(8,128)(2,1)}, bf16[16,128,128]{2,1,0:T(8,128)(2,1)S(1)}, u32[]{:S(2)}) copy-start(bf16[16,128,128]{2,1,0:T(8,128)(2,1)S(1)} %collective-permute-done.7.refs_3_.refs_9_) | copy-start | bytes 1572868
  26.3 11.3 %collective-permute-start.12 = (bf16[16,128,128]{2,1,0:T(8,128)(2,1)S(1)}, bf16[16,128,128]{2,1,0:T(8,128)(2,1)S(1)}, u32[]{:S(2)}, u32[]{:S(2)}) collective-permute-start(bf16[16,128,128]{2,1,0:T(8,128)(2,1)S(1)} %get-tuple-element.54.refs_0_.refs_6_), channel_id=1, source_target_pairs={{0,2},{1,5},{2,0},{3,7},{4,6},{5,1},{6,4},{7,3},{8,10},{9,13},{10,... | collective-permute-start | bytes 1572872 | tf_op jit(solution)/shard_map/ppermute | solution.py:514
  36.8 2.0 %collective-permute-start.4 = (bf16[32,64,128]{2,1,0:T(8,128)(2,1)S(1)}, bf16[32,64,128]{2,1,0:T(8,128)(2,1)S(1)}, u32[]{:S(2)}, u32[]{:S(2)}) collective-permute-start(bf16[32,64,128]{2,1,0:T(8,128)(2,1)S(1)} %get-tuple-element.45), channel_id=1, source_target_pairs={{0,1},{1,0},{2,3},{3,2},{4,5},{5,4},{6,7},{7,6},{8,9},{9,8},{10,11... | collective-permute-start | bytes 1572872 | tf_op jit(solution)/shard_map/ppermute | solution.py:496
  36.8 10.3 %collective-permute-start.13 = (bf16[16,128,128]{2,1,0:T(8,128)(2,1)S(1)}, bf16[16,128,128]{2,1,0:T(8,128)(2,1)S(1)}, u32[]{:S(2)}, u32[]{:S(2)}) collective-permute-start(bf16[16,128,128]{2,1,0:T(8,128)(2,1)S(1)} %get-tuple-element.54.refs_0_.refs_6_), channel_id=1, source_target_pairs={{0,4},{1,3},{2,6},{3,1},{4,0},{5,7},{6,2},{7,5},{8,12},{9,11},{10,... | collective-permute-start | bytes 1572872 | tf_op jit(solution)/shard_map/ppermute | solution.py:514
  37.6 14.1 %copy-start.9 = (bf16[16,128,128]{2,1,0:T(8,128)(2,1)}, bf16[16,128,128]{2,1,0:T(8,128)(2,1)S(1)}, u32[]{:S(2)}) copy-start(bf16[16,128,128]{2,1,0:T(8,128)(2,1)S(1)} %collective-permute-done.12.refs_1_.refs_7_) | copy-start | bytes 1572868
  37.6 14.0 %collective-permute-start.14 = (bf16[16,128,128]{2,1,0:T(8,128)(2,1)S(1)}, bf16[16,128,128]{2,1,0:T(8,128)(2,1)S(1)}, u32[]{:S(2)}, u32[]{:S(2)}) collective-permute-start(bf16[16,128,128]{2,1,0:T(8,128)(2,1)S(1)} %collective-permute-done.12.refs_1_.refs_7_), channel_id=1, source_target_pairs={{0,4},{1,3},{2,6},{3,1},{4,0},{5,7},{6,2},{7,5},{8,12},{9,11},{10,... | collective-permute-start | bytes 1572872 | tf_op jit(solution)/shard_map/ppermute | solution.py:514
  41.6 13.4 %collective-permute-start.8 = (bf16[16,128,128]{2,1,0:T(8,128)(2,1)}, bf16[16,128,128]{2,1,0:T(8,128)(2,1)}, u32[]{:S(2)}, u32[]{:S(2)}) collective-permute-start(bf16[16,128,128]{2,1,0:T(8,128)(2,1)} %get-tuple-element.46), channel_id=1, source_target_pairs={{0,8},{1,9},{2,10},{3,11},{4,12},{5,13},{6,14},{7,15},{8,0},{9,1},... | collective-permute-start | bytes 1572872 | tf_op jit(solution)/shard_map/ppermute | solution.py:504
  44.3 10.7 %collective-permute-start.9 = (bf16[16,128,128]{2,1,0:T(8,128)(2,1)}, bf16[16,128,128]{2,1,0:T(8,128)(2,1)}, u32[]{:S(2)}, u32[]{:S(2)}) collective-permute-start(bf16[16,128,128]{2,1,0:T(8,128)(2,1)} %get-tuple-element.47), channel_id=1, source_target_pairs={{0,1},{1,0},{2,3},{3,2},{4,5},{5,4},{6,7},{7,6},{8,16},{9,17},{10,... | collective-permute-start | bytes 1572872 | tf_op jit(solution)/shard_map/ppermute | solution.py:504
  53.4 15.1 %collective-permute-start.15 = (bf16[16,128,128]{2,1,0:T(8,128)(2,1)}, bf16[16,128,128]{2,1,0:T(8,128)(2,1)}, u32[]{:S(2)}, u32[]{:S(2)}) collective-permute-start(bf16[16,128,128]{2,1,0:T(8,128)(2,1)} %get-tuple-element.55), channel_id=1, source_target_pairs={{0,8},{1,9},{2,10},{3,11},{4,12},{5,13},{6,14},{7,15},{8,0},{9,1},... | collective-permute-start | bytes 1572872 | tf_op jit(solution)/shard_map/ppermute | solution.py:504
  55.0 13.6 %collective-permute-start.16 = (bf16[16,128,128]{2,1,0:T(8,128)(2,1)}, bf16[16,128,128]{2,1,0:T(8,128)(2,1)}, u32[]{:S(2)}, u32[]{:S(2)}) collective-permute-start(bf16[16,128,128]{2,1,0:T(8,128)(2,1)} %get-tuple-element.56), channel_id=1, source_target_pairs={{0,1},{1,0},{2,3},{3,2},{4,5},{5,4},{6,7},{7,6},{8,16},{9,17},{10,... | collective-permute-start | bytes 1572872 | tf_op jit(solution)/shard_map/ppermute | solution.py:504
  58.0 21.8 %collective-permute-start.10 = (bf16[16,128,128]{2,1,0:T(8,128)(2,1)}, bf16[16,128,128]{2,1,0:T(8,128)(2,1)}, u32[]{:S(2)}, u32[]{:S(2)}) collective-permute-start(bf16[16,128,128]{2,1,0:T(8,128)(2,1)} %get-tuple-element.76), channel_id=1, source_target_pairs={{0,8},{1,9},{2,10},{3,11},{4,12},{5,13},{6,14},{7,15},{8,0},{9,1},... | collective-permute-start | bytes 1572872 | tf_op jit(solution)/shard_map/ppermute | solution.py:504
  61.2 18.6 %collective-permute-start.11 = (bf16[16,128,128]{2,1,0:T(8,128)(2,1)}, bf16[16,128,128]{2,1,0:T(8,128)(2,1)}, u32[]{:S(2)}, u32[]{:S(2)}) collective-permute-start(bf16[16,128,128]{2,1,0:T(8,128)(2,1)} %get-tuple-element.75), channel_id=1, source_target_pairs={{0,1},{1,0},{2,3},{3,2},{4,5},{5,4},{6,7},{7,6},{8,16},{9,17},{10,... | collective-permute-start | bytes 1572872 | tf_op jit(solution)/shard_map/ppermute | solution.py:504
  71.4 13.2 %copy-start.1 = (bf16[32,128,128]{2,1,0:T(8,128)(2,1)S(1)}, bf16[32,128,128]{2,1,0:T(8,128)(2,1)}, u32[]{:S(2)}) copy-start(bf16[32,128,128]{2,1,0:T(8,128)(2,1)} %copy-done) | copy-start | bytes 3145732
  71.4 19.6 %collective-permute-start.17 = (bf16[16,128,128]{2,1,0:T(8,128)(2,1)}, bf16[16,128,128]{2,1,0:T(8,128)(2,1)}, u32[]{:S(2)}, u32[]{:S(2)}) collective-permute-start(bf16[16,128,128]{2,1,0:T(8,128)(2,1)} %get-tuple-element.74), channel_id=1, source_target_pairs={{0,8},{1,9},{2,10},{3,11},{4,12},{5,13},{6,14},{7,15},{8,0},{9,1},... | collective-permute-start | bytes 1572872 | tf_op jit(solution)/shard_map/ppermute | solution.py:504
  74.1 16.9 %collective-permute-start.18 = (bf16[16,128,128]{2,1,0:T(8,128)(2,1)}, bf16[16,128,128]{2,1,0:T(8,128)(2,1)}, u32[]{:S(2)}, u32[]{:S(2)}) collective-permute-start(bf16[16,128,128]{2,1,0:T(8,128)(2,1)} %get-tuple-element.73), channel_id=1, source_target_pairs={{0,1},{1,0},{2,3},{3,2},{4,5},{5,4},{6,7},{7,6},{8,16},{9,17},{10,... | collective-permute-start | bytes 1572872 | tf_op jit(solution)/shard_map/ppermute | solution.py:504
  74.1 10.5 %copy-start.6 = (bf16[16,128,128]{2,1,0:T(8,128)(2,1)S(1)}, bf16[16,128,128]{2,1,0:T(8,128)(2,1)}, u32[]{:S(2)}) copy-start(bf16[16,128,128]{2,1,0:T(8,128)(2,1)} %copy-done.5) | copy-start | bytes 1572868
  74.1 10.5 %copy-start.8 = (bf16[16,128,128]{2,1,0:T(8,128)(2,1)S(1)}, bf16[16,128,128]{2,1,0:T(8,128)(2,1)}, u32[]{:S(2)}) copy-start(bf16[16,128,128]{2,1,0:T(8,128)(2,1)} %copy-done.7) | copy-start | bytes 1572868
  74.1 10.5 %copy-start.13 = (bf16[16,128,128]{2,1,0:T(8,128)(2,1)S(1)}, bf16[16,128,128]{2,1,0:T(8,128)(2,1)}, u32[]{:S(2)}) copy-start(bf16[16,128,128]{2,1,0:T(8,128)(2,1)} %copy-done.12) | copy-start | bytes 1572868
  74.1 10.5 %copy-start.18 = (bf16[16,128,128]{2,1,0:T(8,128)(2,1)S(1)}, bf16[16,128,128]{2,1,0:T(8,128)(2,1)}, u32[]{:S(2)}) copy-start(bf16[16,128,128]{2,1,0:T(8,128)(2,1)} %copy-done.17) | copy-start | bytes 1572868
  81.8 20.3 %collective-permute-start.21 = (bf16[16,128,128]{2,1,0:T(8,128)(2,1)S(1)}, bf16[16,128,128]{2,1,0:T(8,128)(2,1)S(1)}, u32[]{:S(2)}, u32[]{:S(2)}) collective-permute-start(bf16[16,128,128]{2,1,0:T(8,128)(2,1)S(1)} %get-tuple-element.72), channel_id=1, source_target_pairs={{0,8},{1,9},{2,10},{3,11},{4,12},{5,13},{6,14},{7,15},{8,0},{9,1},... | collective-permute-start | bytes 1572872 | tf_op jit(solution)/shard_map/ppermute | solution.py:504
  84.6 17.5 %collective-permute-start.22 = (bf16[16,128,128]{2,1,0:T(8,128)(2,1)S(1)}, bf16[16,128,128]{2,1,0:T(8,128)(2,1)S(1)}, u32[]{:S(2)}, u32[]{:S(2)}) collective-permute-start(bf16[16,128,128]{2,1,0:T(8,128)(2,1)S(1)} %get-tuple-element.71), channel_id=1, source_target_pairs={{0,1},{1,0},{2,3},{3,2},{4,5},{5,4},{6,7},{7,6},{8,16},{9,17},{10,... | collective-permute-start | bytes 1572872 | tf_op jit(solution)/shard_map/ppermute | solution.py:504
  87.0 9.0 %copy-start.4 = (bf16[16,128,128]{2,1,0:T(8,128)(2,1)S(1)}, bf16[16,128,128]{2,1,0:T(8,128)(2,1)}, u32[]{:S(2)}) copy-start(bf16[16,128,128]{2,1,0:T(8,128)(2,1)} %copy-done.2) | copy-start | bytes 1572868
  87.0 9.0 %copy-start.11 = (bf16[16,128,128]{2,1,0:T(8,128)(2,1)S(1)}, bf16[16,128,128]{2,1,0:T(8,128)(2,1)}, u32[]{:S(2)}) copy-start(bf16[16,128,128]{2,1,0:T(8,128)(2,1)} %copy-done.9) | copy-start | bytes 1572868
  87.0 9.0 %copy-start.16 = (bf16[16,128,128]{2,1,0:T(8,128)(2,1)S(1)}, bf16[16,128,128]{2,1,0:T(8,128)(2,1)}, u32[]{:S(2)}) copy-start(bf16[16,128,128]{2,1,0:T(8,128)(2,1)} %copy-done.14) | copy-start | bytes 1572868
  87.0 9.0 %copy-start.21 = (bf16[16,128,128]{2,1,0:T(8,128)(2,1)S(1)}, bf16[16,128,128]{2,1,0:T(8,128)(2,1)}, u32[]{:S(2)}) copy-start(bf16[16,128,128]{2,1,0:T(8,128)(2,1)} %copy-done.19) | copy-start | bytes 1572868
  92.8 19.4 %collective-permute-start.24 = (bf16[16,128,128]{2,1,0:T(8,128)(2,1)S(1)}, bf16[16,128,128]{2,1,0:T(8,128)(2,1)S(1)}, u32[]{:S(2)}, u32[]{:S(2)}) collective-permute-start(bf16[16,128,128]{2,1,0:T(8,128)(2,1)S(1)} %get-tuple-element.70), channel_id=1, source_target_pairs={{0,8},{1,9},{2,10},{3,11},{4,12},{5,13},{6,14},{7,15},{8,0},{9,1},... | collective-permute-start | bytes 1572872 | tf_op jit(solution)/shard_map/ppermute | solution.py:504
  95.5 8.5 %copy-start.26 = (bf16[128,256]{1,0:T(8,128)(2,1)S(1)}, bf16[128,256]{1,0:T(8,128)(2,1)}, u32[]{:S(2)}) copy-start(bf16[128,256]{1,0:T(8,128)(2,1)} %weight.5) | copy-start | bytes 196612
  95.5 16.6 %collective-permute-start.25 = (bf16[16,128,128]{2,1,0:T(8,128)(2,1)S(1)}, bf16[16,128,128]{2,1,0:T(8,128)(2,1)S(1)}, u32[]{:S(2)}, u32[]{:S(2)}) collective-permute-start(bf16[16,128,128]{2,1,0:T(8,128)(2,1)S(1)} %get-tuple-element.69), channel_id=1, source_target_pairs={{0,1},{1,0},{2,3},{3,2},{4,5},{5,4},{6,7},{7,6},{8,16},{9,17},{10,... | collective-permute-start | bytes 1572872 | tf_op jit(solution)/shard_map/ppermute | solution.py:504
  95.5 7.3 %collective-permute-start.19 = (bf16[16,64,128]{2,1,0:T(8,128)(2,1)S(1)}, bf16[16,64,128]{2,1,0:T(8,128)(2,1)S(1)}, u32[]{:S(2)}, u32[]{:S(2)}) collective-permute-start(bf16[16,64,128]{2,1,0:T(8,128)(2,1)S(1)} %get-tuple-element.59), channel_id=1, source_target_pairs={{0,1},{1,0},{2,3},{3,2},{4,5},{5,4},{6,7},{7,6},{8,9},{9,8},{10,11... | collective-permute-start | bytes 786440 | tf_op jit(solution)/shard_map/ppermute | solution.py:496
  96.0 8.0 %copy-start.23 = (bf16[64,256,128]{2,1,0:T(8,128)(2,1)S(1)}, bf16[64,256,128]{2,1,0:T(8,128)(2,1)}, u32[]{:S(2)}) copy-start(bf16[64,256,128]{2,1,0:T(8,128)(2,1)} %copy-done.22) | copy-start | bytes 12582916
  102.1 1.5 %collective-permute-start.20 = (bf16[16,64,128]{2,1,0:T(8,128)(2,1)S(1)}, bf16[16,64,128]{2,1,0:T(8,128)(2,1)S(1)}, u32[]{:S(2)}, u32[]{:S(2)}) collective-permute-start(bf16[16,64,128]{2,1,0:T(8,128)(2,1)S(1)} %get-tuple-element.60), channel_id=1, source_target_pairs={{0,1},{1,0},{2,3},{3,2},{4,5},{5,4},{6,7},{7,6},{8,9},{9,8},{10,11... | collective-permute-start | bytes 786440 | tf_op jit(solution)/shard_map/ppermute | solution.py:496
  102.3 1.7 %collective-permute-start.23 = (bf16[16,64,128]{2,1,0:T(8,128)(2,1)S(1)}, bf16[16,64,128]{2,1,0:T(8,128)(2,1)S(1)}, u32[]{:S(2)}, u32[]{:S(2)}) collective-permute-start(bf16[16,64,128]{2,1,0:T(8,128)(2,1)S(1)} %add_convert_fusion.5), channel_id=1, source_target_pairs={{0,1},{1,0},{2,3},{3,2},{4,5},{5,4},{6,7},{7,6},{8,9},{9,8},{10,11... | collective-permute-start | bytes 786440 | tf_op jit(solution)/shard_map/ppermute | solution.py:496
  104.0 8.1 %copy-start.28 = (bf16[16,128,128]{2,1,0:T(8,128)(2,1)S(1)}, bf16[16,128,128]{2,1,0:T(8,128)(2,1)}, u32[]{:S(2)}) copy-start(bf16[16,128,128]{2,1,0:T(8,128)(2,1)} %get-tuple-element.68.partials) | copy-start | bytes 1572868
  104.0 9.8 %copy-start.25 = (bf16[64,128,128]{2,1,0:T(8,128)(2,1)S(1)}, bf16[64,128,128]{2,1,0:T(8,128)(2,1)}, u32[]{:S(2)}) copy-start(bf16[64,128,128]{2,1,0:T(8,128)(2,1)} %copy-done.24) | copy-start | bytes 6291460
  104.1 9.8 %copy-start.32 = (f32[128]{0:T(128)S(1)}, f32[128]{0:T(128)}, u32[]{:S(2)}) copy-start(f32[128]{0:T(128)} %param.8) | copy-start | bytes 1540
  112.3 1.6 %collective-permute-start.26 = (bf16[16,64,128]{2,1,0:T(8,128)(2,1)S(1)}, bf16[16,64,128]{2,1,0:T(8,128)(2,1)S(1)}, u32[]{:S(2)}, u32[]{:S(2)}) collective-permute-start(bf16[16,64,128]{2,1,0:T(8,128)(2,1)S(1)} %add_convert_fusion.4), channel_id=1, source_target_pairs={{0,1},{1,0},{2,3},{3,2},{4,5},{5,4},{6,7},{7,6},{8,9},{9,8},{10,11... | collective-permute-start | bytes 786440 | tf_op jit(solution)/shard_map/ppermute | solution.py:496
  (14 other events, 72.8 us)

commit v12 on v11

--- a/solution.py
+++ b/solution.py
@@ -300,7 +300,10 @@
     args = (left_mine, left_other, *blocks)
     return pl.pallas_call(
         functools.partial(partial_kernel, n),
-        out_shape=[pltpu.HBM((chans, CORES * ks, rows), jnp.bfloat16)] * n,
+        out_shape=[
+            (jax.ShapeDtypeStruct if s in (2, n - 2) else pltpu.HBM)((chans, CORES * ks, rows), jnp.bfloat16)
+            for s in range(n)
+        ],
         grid=(chans // STEP,),
         in_specs=[chunk_spec(v, chans, chunk) for v in args],
         out_specs=[pl.BlockSpec((STEP, CORES * ks, rows), lambda g: (g, 0, 0))] * n,
@@ -309,6 +312,23 @@
         cost_estimate=COST,
         name="right_partials",
     )(*args)
+
+
+def advance_kernel(t, n, by_a, by_b, up_sums, down_sums, next_a, next_b):
+    next_a[...], next_b[...] = onward(by_a[...], by_b[...], up_sums[...], down_sums[...], t, n)
+
+
+def advance(by_a, by_b, sums, t):
+    n = len(sums)
+    return pl.pallas_call(
+        functools.partial(advance_kernel, t, n),
+        out_shape=[jax.ShapeDtypeStruct(by_a.shape, by_a.dtype)] * 2,
+        in_specs=[WHOLE] * 4,
+        out_specs=[WHOLE] * 2,
+        compiler_params=PARAMS,
+        cost_estimate=COST,
+        name="advance",
+    )(by_a, by_b, sums[n - t], sums[t])
 
 
 def left_kernel(n, own, *refs):
@@ -541,7 +561,10 @@
             value = by_a[c][-1]
             if t == n - 1 and c > 0:
                 value = after(value, left_grads[c - 1])
-            next_a, next_b = onward(value, by_b[c][-1], partials[c][n - t], partials[c][t], t, n)
+            if t == 2:
+                next_a, next_b = advance(value, by_b[c][-1], partials[c], t)
+            else:
+                next_a, next_b = onward(value, by_b[c][-1], partials[c][n - t], partials[c][t], t, n)
             by_a[c].append(hop(next_a, 0))
             by_b[c].append(hop(next_b, 1))
             if t == n - 1:

time: 120 us -> 117 us (0.975)
  other arithmetic: 10 us -> 4.18 us
  waiting for transfers between devices: 40 us -> 44.6 us
    convert_element_type x4 -> x2, other arithmetic: 9.63 us -> 3.79 us  [onward(): return (out_a.astype(jnp.bfloat16), out_b.astype(jnp.bfloat16))]
    ppermute x14, waiting for transfers between devices: 23.1 us -> 27.9 us  [hop(): return lax.ppermute(value, ('row', 'col'), perm)]
    pallas_call x2 -> x4, Pallas kernels: 5.65 us -> 8.06 us  [the longest x2 5.42 us: partial_products(): pl.pallas_call(functools.partial(partial_kernel, n), out_shape=[(jax.Shap...]
    pallas_call x2, Pallas kernels: 3.48 us -> 1.41 us  [first_step(): pl.pallas_call(functools.partial(first_kernel, chunk), out_shape=[jax.Sha...]
    unnamed x71 -> x75, local copies, waits for them, and re-layouts: 3.45 us -> 2.93 us
  transfers between devices with their start and end apart: 27 -> 27, of which waited for: 14 -> 15; matrix products, arithmetic and copies ran while one was open for 8% -> 4% of each run, Pallas kernels for 25% -> 25%
where the time goes in v12:
time: 117 us
  waiting for transfers between devices  44.6 us (38%)
  Pallas kernels  36.1 us (31%)
  starting transfers between devices  28.2 us (24%)
  other arithmetic  4.18 us (4%)
  local copies, waits for them, and re-layouts  3.1 us (3%)
    ppermute x14, waiting for transfers between devices, hop(): return lax.ppermute(value, ('row', 'col'), perm)  27.9 us
    ppermute x14, starting transfers between devices, hop(): return lax.ppermute(value, ('row', 'col'), perm)  16.6 us
    ppermute x6, waiting for transfers between devices, along(): lax.ppermute(value, 'col', [(d, d ^ mask[d % CORES]) for d in range(n_col)])  13.7 us
    pallas_call x2, Pallas kernels, front(): pl.pallas_call(right_kernel if right else left_forward_kernel, out_shape=...  10.8 us
    ppermute x6, starting transfers between devices, along(): lax.ppermute(value, 'col', [(d, d ^ mask[d % CORES]) for d in range(n_col)])  9.89 us
    pallas_call x2, Pallas kernels, partial_products(): pl.pallas_call(functools.partial(partial_kernel, n), out_shape=[(jax.Shap...  5.42 us
    pallas_call x1, Pallas kernels, tail(): pl.pallas_call(functools.partial(tail_kernel, lax.axis_size('row')), out_...  5.14 us
    pallas_call x2, Pallas kernels, left_products(): pl.pallas_call(functools.partial(left_kernel, n), out_shape=[jax.ShapeDty...  4.43 us
  transfers between devices with their start and end apart: 27, of which 15 were waited for; matrix products, arithmetic and copies ran while one was open for 4% of the time, Pallas kernels for 25%

profile of v12, /device:TPU:0, one launch (start us, length us, event | category | flops | bytes accessed | tf_op | source)
XLA Modules:
  0.0 116.6 jit_solution(474531446158565239)
XLA Ops:
  0.0 1.1 theirs.1
  1.1 0.5 collective-permute-start
  1.6 1.0 mine.1.own
  2.6 0.5 collective-permute-done.other
  3.5 2.9 %collective-permute-start.6 = (bf16[16,128,128]{2,1,0:T(8,128)(2,1)S(1)}, bf16[16,128,128]{2,1,0:T(8,128)(2,1)S(1)}, u32[]{:S(2)}, u32[]{:S(2)}) collective-permute-start(bf16[16,128,128]{2,1,0:T(8,128)(2,1)S(1)} %get-tuple-element.41.refs_0_.refs_6_), channel_id=1, source_target_pairs={{0,2},{1,5},{2,0},{3,7},{4,6},{5,1},{6,4},{7,3},{8,10},{9,13},{10,... | collective-permute-start | bytes 1572872 | tf_op jit(solution)/shard_map/ppermute | solution.py:534
  6.4 4.9 %right_front.1 = (bf16[32,64,128]{2,1,0:T(8,128)(2,1)S(1)}, bf16[32,64,128]{2,1,0:T(8,128)(2,1)S(1)}) custom-call(s32[4,4]{1,0:T(4,128)S(1)} %copy-done.33, bf16[128,64,128]{2,1,0:T(8,128)(2,1)} %pair.1, f32[1,128]{1,0:T(1,128)} %bitcast.3, f32[1,128]{1,0:T(1,128)} %bitcast.8, bf16[128,256]{1,0:T(8,128)(2,1)} %weight.5), custom_call_target="tpu_custom_call" | custom-call | flops 1 | bytes 18000000 | tf_op jit(solution)/shard_map/right_front/pallas_call | solution.py:148
  11.5 1.6 %collective-permute-start.2 = (bf16[16,128,128]{2,1,0:T(8,128)(2,1)S(1)}, bf16[16,128,128]{2,1,0:T(8,128)(2,1)S(1)}, u32[]{:S(2)}, u32[]{:S(2)}) collective-permute-start(bf16[16,128,128]{2,1,0:T(8,128)(2,1)S(1)} %get-tuple-element.41.refs_0_.refs_6_), channel_id=1, source_target_pairs={{0,4},{1,3},{2,6},{3,1},{4,0},{5,7},{6,2},{7,5},{8,12},{9,11},{10,... | collective-permute-start | bytes 1572872 | tf_op jit(solution)/shard_map/ppermute | solution.py:534
  13.1 0.5 collective-permute-done.6.refs_1_.refs_7_
  13.6 2.0 %collective-permute-start.7 = (bf16[16,128,128]{2,1,0:T(8,128)(2,1)S(1)}, bf16[16,128,128]{2,1,0:T(8,128)(2,1)S(1)}, u32[]{:S(2)}, u32[]{:S(2)}) collective-permute-start(bf16[16,128,128]{2,1,0:T(8,128)(2,1)S(1)} %collective-permute-done.6.refs_1_.refs_7_), channel_id=1, source_target_pairs={{0,4},{1,3},{2,6},{3,1},{4,0},{5,7},{6,2},{7,5},{8,12},{9,11},{10,... | collective-permute-start | bytes 1572872 | tf_op jit(solution)/shard_map/ppermute | solution.py:534
  15.7 1.6 %collective-permute-start.3 = (bf16[32,128,128]{2,1,0:T(8,128)(2,1)S(1)}, bf16[32,128,128]{2,1,0:T(8,128)(2,1)S(1)}, u32[]{:S(2)}, u32[]{:S(2)}) collective-permute-start(bf16[32,128,128]{2,1,0:T(8,128)(2,1)S(1)} %constant_dynamic-update-slice_fusion.own), channel_id=1, source_target_pairs={{0,8},{1,9},{2,10},{3,11},{4,12},{5,13},{6,14},{7,15},{8,0},{9,1},... | collective-permute-start | bytes 3145736 | tf_op jit(solution)/shard_map/ppermute | solution.py:524
  17.4 3.3 %collective-permute-done.2.refs_2_.refs_8_ = bf16[16,128,128]{2,1,0:T(8,128)(2,1)S(1)} collective-permute-done((bf16[16,128,128]{2,1,0:T(8,128)(2,1)S(1)}, bf16[16,128,128]{2,1,0:T(8,128)(2,1)S(1)}, u32[]{:S(2)}, u32[]{:S(2)}) %collective-permute-start.2) | collective-permute-done | bytes 524320 | tf_op jit(solution)/shard_map/ppermute | solution.py:534
  20.7 5.6 %collective-permute-done.7.refs_3_.refs_9_ = bf16[16,128,128]{2,1,0:T(8,128)(2,1)S(1)} collective-permute-done((bf16[16,128,128]{2,1,0:T(8,128)(2,1)S(1)}, bf16[16,128,128]{2,1,0:T(8,128)(2,1)S(1)}, u32[]{:S(2)}, u32[]{:S(2)}) %collective-permute-start.7) | collective-permute-done | bytes 524320 | tf_op jit(solution)/shard_map/ppermute | solution.py:534
  26.3 1.3 %collective-permute-start.12 = (bf16[16,128,128]{2,1,0:T(8,128)(2,1)S(1)}, bf16[16,128,128]{2,1,0:T(8,128)(2,1)S(1)}, u32[]{:S(2)}, u32[]{:S(2)}) collective-permute-start(bf16[16,128,128]{2,1,0:T(8,128)(2,1)S(1)} %get-tuple-element.60.refs_0_.refs_6_), channel_id=1, source_target_pairs={{0,2},{1,5},{2,0},{3,7},{4,6},{5,1},{6,4},{7,3},{8,10},{9,13},{10,... | collective-permute-start | bytes 1572872 | tf_op jit(solution)/shard_map/ppermute | solution.py:534
  27.6 5.9 %left_front.1 = (bf16[32,64,128]{2,1,0:T(8,128)(2,1)S(1)}, bf16[32,64,128]{2,1,0:T(8,128)(2,1)S(1)}, bf16[64,128,128]{2,1,0:T(8,128)(2,1)S(1)}, f32[64,1,128]{2,...) custom-call(s32[4,4]{1,0:T(4,128)S(1)} %copy-done.33, bf16[128,64,128]{2,1,0:T(8,128)(2,1)} %pair.1, ...), custom_call_target="tpu_custom_call" | custom-call | flops 1 | bytes 18000000 | tf_op jit(solution)/shard_map/left_front/pallas_call | solution.py:148
  33.5 2.0 %copy-done.16 = bf16[64,256,128]{2,1,0:T(8,128)(2,1)} copy-done((bf16[64,256,128]{2,1,0:T(8,128)(2,1)}, bf16[64,256,128]{2,1,0:T(8,128)(2,1)S(1)}, u32[]{:S(2)}) %copy-start.16) | copy-done | bytes 4194328
  35.5 0.7 collective-permute-start.13
  36.3 1.3 %collective-permute-start.14 = (bf16[16,128,128]{2,1,0:T(8,128)(2,1)S(1)}, bf16[16,128,128]{2,1,0:T(8,128)(2,1)S(1)}, u32[]{:S(2)}, u32[]{:S(2)}) collective-permute-start(bf16[16,128,128]{2,1,0:T(8,128)(2,1)S(1)} %collective-permute-done.12.refs_1_.refs_7_), channel_id=1, source_target_pairs={{0,4},{1,3},{2,6},{3,1},{4,0},{5,7},{6,2},{7,5},{8,12},{9,11},{10,... | collective-permute-start | bytes 1572872 | tf_op jit(solution)/shard_map/ppermute | solution.py:534
  37.5 2.3 %collective-permute-done.3.by_a.refs_0_ = bf16[32,128,128]{2,1,0:T(8,128)(2,1)S(1)} collective-permute-done((bf16[32,128,128]{2,1,0:T(8,128)(2,1)S(1)}, bf16[32,128,128]{2,1,0:T(8,128)(2,1)S(1)}, u32[]{:S(2)}, u32[]{:S(2)}) %collective-permute-start.3) | collective-permute-done | bytes 1048608 | tf_op jit(solution)/shard_map/ppermute | solution.py:524
  39.8 0.7 first_step.2
  40.6 2.8 %collective-permute-start.8 = (bf16[16,128,128]{2,1,0:T(8,128)(2,1)S(1)}, bf16[16,128,128]{2,1,0:T(8,128)(2,1)S(1)}, u32[]{:S(2)}, u32[]{:S(2)}) collective-permute-start(bf16[16,128,128]{2,1,0:T(8,128)(2,1)S(1)} %get-tuple-element.50), channel_id=1, source_target_pairs={{0,8},{1,9},{2,10},{3,11},{4,12},{5,13},{6,14},{7,15},{8,0},{9,1},... | collective-permute-start | bytes 1572872 | tf_op jit(solution)/shard_map/ppermute | solution.py:524
  43.4 2.7 %right_partials.2 = (bf16[16,128,128]{2,1,0:T(8,128)(2,1)}, bf16[16,128,128]{2,1,0:T(8,128)(2,1)}, bf16[16,128,128]{2,1,0:T(8,128)(2,1)S(1)}, bf16[16,128,128]{2,1,0:T(8,128)(2,1)}) custom-call(bf16[32,64,128]{2,1,0:T(8,128)(2,1)S(1)} %get-tuple-element.48.left_mine, bf16[32,64,128]{2,1,0:T(8,128)(2,1)S(1)} %collective-permute-done.4.left_other, ...), custom_call_target="tpu_custom_call" | custom-call | flops 1 | bytes 8000000 | tf_op jit(solution)/shard_map/right_partials/pallas_call | solution.py:301
  46.1 4.2 %collective-permute-done.14.refs_3_.refs_9_ = bf16[16,128,128]{2,1,0:T(8,128)(2,1)S(1)} collective-permute-done((bf16[16,128,128]{2,1,0:T(8,128)(2,1)S(1)}, bf16[16,128,128]{2,1,0:T(8,128)(2,1)S(1)}, u32[]{:S(2)}, u32[]{:S(2)}) %collective-permute-start.14) | collective-permute-done | bytes 524320 | tf_op jit(solution)/shard_map/ppermute | solution.py:534
  50.3 0.7 first_step.3
  51.0 1.6 %collective-permute-start.15 = (bf16[16,128,128]{2,1,0:T(8,128)(2,1)S(1)}, bf16[16,128,128]{2,1,0:T(8,128)(2,1)S(1)}, u32[]{:S(2)}, u32[]{:S(2)}) collective-permute-start(bf16[16,128,128]{2,1,0:T(8,128)(2,1)S(1)} %get-tuple-element.61), channel_id=1, source_target_pairs={{0,8},{1,9},{2,10},{3,11},{4,12},{5,13},{6,14},{7,15},{8,0},{9,1},... | collective-permute-start | bytes 1572872 | tf_op jit(solution)/shard_map/ppermute | solution.py:524
  52.7 0.9 collective-permute-done.8.by_a.refs_1_
  53.5 1.3 %advance.2 = (bf16[16,128,128]{2,1,0:T(8,128)(2,1)}, bf16[16,128,128]{2,1,0:T(8,128)(2,1)}) custom-call(bf16[16,128,128]{2,1,0:T(8,128)(2,1)S(1)} %collective-permute-done.8.by_a.refs_1_, bf16[16,128,128]{2,1,0:T(8,128)(2,1)S(1)} %collective-permute-done.9.by_b.refs_4_, bf16[16,128,128]{2,1,0:T(8,128)(2,1)S(1)} %get-tuple-element.52.up_sums.down_sums, ...), custom_call_target="tpu_custom_call" | custom-call | flops 1 | bytes 8000000 | tf_op jit(solution)/shard_map/advance/pallas_call | solution.py:323
  54.9 2.3 %collective-permute-start.10 = (bf16[16,128,128]{2,1,0:T(8,128)(2,1)}, bf16[16,128,128]{2,1,0:T(8,128)(2,1)}, u32[]{:S(2)}, u32[]{:S(2)}) collective-permute-start(bf16[16,128,128]{2,1,0:T(8,128)(2,1)} %get-tuple-element.53), channel_id=1, source_target_pairs={{0,8},{1,9},{2,10},{3,11},{4,12},{5,13},{6,14},{7,15},{8,0},{9,1},... | collective-permute-start | bytes 1572872 | tf_op jit(solution)/shard_map/ppermute | solution.py:524
  57.2 2.7 %right_partials.3 = (bf16[16,128,128]{2,1,0:T(8,128)(2,1)}, bf16[16,128,128]{2,1,0:T(8,128)(2,1)}, bf16[16,128,128]{2,1,0:T(8,128)(2,1)S(1)}, bf16[16,128,128]{2,1,0:T(8,128)(2,1)}) custom-call(bf16[32,64,128]{2,1,0:T(8,128)(2,1)S(1)} %get-tuple-element.48.left_mine, bf16[32,64,128]{2,1,0:T(8,128)(2,1)S(1)} %collective-permute-done.4.left_other, ...), custom_call_target="tpu_custom_call" | custom-call | flops 1 | bytes 8000000 | tf_op jit(solution)/shard_map/right_partials/pallas_call | solution.py:301
  59.9 6.0 %collective-permute-done.15.by_a.refs_1_ = bf16[16,128,128]{2,1,0:T(8,128)(2,1)S(1)} collective-permute-done((bf16[16,128,128]{2,1,0:T(8,128)(2,1)S(1)}, bf16[16,128,128]{2,1,0:T(8,128)(2,1)S(1)}, u32[]{:S(2)}, u32[]{:S(2)}) %collective-permute-start.15) | collective-permute-done | bytes 524320 | tf_op jit(solution)/shard_map/ppermute | solution.py:524
  65.9 1.3 %advance.3 = (bf16[16,128,128]{2,1,0:T(8,128)(2,1)}, bf16[16,128,128]{2,1,0:T(8,128)(2,1)}) custom-call(bf16[16,128,128]{2,1,0:T(8,128)(2,1)S(1)} %collective-permute-done.15.by_a.refs_1_, bf16[16,128,128]{2,1,0:T(8,128)(2,1)S(1)} %collective-permute-done.16.by_b.refs_4_, bf16[16,128,128]{2,1,0:T(8,128)(2,1)S(1)} %get-tuple-element.63.up_sums.down_sums, ...), custom_call_target="tpu_custom_call" | custom-call | flops 1 | bytes 8000000 | tf_op jit(solution)/shard_map/advance/pallas_call | solution.py:323
  67.2 0.8 copy-done.18
  68.0 2.7 %collective-permute-start.17 = (bf16[16,128,128]{2,1,0:T(8,128)(2,1)}, bf16[16,128,128]{2,1,0:T(8,128)(2,1)}, u32[]{:S(2)}, u32[]{:S(2)}) collective-permute-start(bf16[16,128,128]{2,1,0:T(8,128)(2,1)} %get-tuple-element.64), channel_id=1, source_target_pairs={{0,8},{1,9},{2,10},{3,11},{4,12},{5,13},{6,14},{7,15},{8,0},{9,1},... | collective-permute-start | bytes 1572872 | tf_op jit(solution)/shard_map/ppermute | solution.py:524
  70.8 6.5 %collective-permute-done.10.refs_2_ = bf16[16,128,128]{2,1,0:T(8,128)(2,1)} collective-permute-done((bf16[16,128,128]{2,1,0:T(8,128)(2,1)}, bf16[16,128,128]{2,1,0:T(8,128)(2,1)}, u32[]{:S(2)}, u32[]{:S(2)}) %collective-permute-start.10) | collective-permute-done | bytes 524320 | tf_op jit(solution)/shard_map/ppermute | solution.py:524
  77.3 2.1 %add_convert_fusion.2 = (bf16[16,128,128]{2,1,0:T(8,128)(2,1)S(1)}, bf16[16,128,128]{2,1,0:T(8,128)(2,1)S(1)}) fusion(bf16[16,128,128]{2,1,0:T(8,128)(2,1)} %collective-permute-done.10.refs_2_, bf16[16,128,128]{2,1,0:T(8,128)(2,1)} %get-tuple-element.58, bf16[16,128,128]{2,1,0:T(8,128)(2,1)} %get-tuple-element.57, pred[]{:T(512)S(6)} %select_n.107, ...), kind=kLoop, calls=%fused_computation.4 | loop fusion | flops 3670016 | bytes 3145733 | tf_op jit(solution)/shard_map/convert_element_type | solution.py:252
  79.3 2.8 %collective-permute-start.21 = (bf16[16,128,128]{2,1,0:T(8,128)(2,1)S(1)}, bf16[16,128,128]{2,1,0:T(8,128)(2,1)S(1)}, u32[]{:S(2)}, u32[]{:S(2)}) collective-permute-start(bf16[16,128,128]{2,1,0:T(8,128)(2,1)S(1)} %get-tuple-element.80), channel_id=1, source_target_pairs={{0,8},{1,9},{2,10},{3,11},{4,12},{5,13},{6,14},{7,15},{8,0},{9,1},... | collective-permute-start | bytes 1572872 | tf_op jit(solution)/shard_map/ppermute | solution.py:524
  82.2 2.2 %left_products.2 = (f32[16,64,128]{2,1,0:T(8,128)S(1)}, bf16[16,64,128]{2,1,0:T(8,128)(2,1)S(1)}) custom-call(bf16[32,128,128]{2,1,0:T(8,128)(2,1)S(1)} %constant_dynamic-update-slice_fusion.own, bf16[32,128,128]{2,1,0:T(8,128)(2,1)S(1)} %collective-permute-done.3.by_a.refs_0_, bf16[16,128,128]{2,1,0:T(8,128)(2,1)S(1)} %copy-done.23, ...), custom_call_target="tpu_custom_call" | custom-call | flops 1 | bytes 8000000 | tf_op jit(solution)/shard_map/left_products/pallas_call | solution.py:361
  84.4 4.1 %collective-permute-done.17.refs_2_ = bf16[16,128,128]{2,1,0:T(8,128)(2,1)} collective-permute-done((bf16[16,128,128]{2,1,0:T(8,128)(2,1)}, bf16[16,128,128]{2,1,0:T(8,128)(2,1)}, u32[]{:S(2)}, u32[]{:S(2)}) %collective-permute-start.17) | collective-permute-done | bytes 524320 | tf_op jit(solution)/shard_map/ppermute | solution.py:524
  88.5 1.7 %add_convert_fusion = (bf16[16,128,128]{2,1,0:T(8,128)(2,1)S(1)}, bf16[16,128,128]{2,1,0:T(8,128)(2,1)S(1)}) fusion(bf16[16,128,128]{2,1,0:T(8,128)(2,1)} %collective-permute-done.17.refs_2_, bf16[16,128,128]{2,1,0:T(8,128)(2,1)S(1)} %copy-done.36, bf16[16,128,128]{2,1,0:T(8,128)(2,1)S(1)} %copy-done.35, pred[]{:T(512)S(6)} %select_n.107, pred[]{:T(512)S(6)} %ge.4, ...), kind=kLoop, calls=%fused_computation | loop fusion | flops 3670016 | bytes 3145733 | tf_op jit(solution)/shard_map/convert_element_type | solution.py:252
  90.3 2.8 %collective-permute-start.24 = (bf16[16,128,128]{2,1,0:T(8,128)(2,1)S(1)}, bf16[16,128,128]{2,1,0:T(8,128)(2,1)S(1)}, u32[]{:S(2)}, u32[]{:S(2)}) collective-permute-start(bf16[16,128,128]{2,1,0:T(8,128)(2,1)S(1)} %get-tuple-element.78), channel_id=1, source_target_pairs={{0,8},{1,9},{2,10},{3,11},{4,12},{5,13},{6,14},{7,15},{8,0},{9,1},... | collective-permute-start | bytes 1572872 | tf_op jit(solution)/shard_map/ppermute | solution.py:524
  93.0 0.5 collective-permute-start.19
  93.6 2.3 %left_products.3 = (f32[16,64,128]{2,1,0:T(8,128)S(1)}, bf16[16,64,128]{2,1,0:T(8,128)(2,1)S(1)}) custom-call(bf16[32,128,128]{2,1,0:T(8,128)(2,1)S(1)} %constant_dynamic-update-slice_fusion.own, bf16[32,128,128]{2,1,0:T(8,128)(2,1)S(1)} %collective-permute-done.3.by_a.refs_0_, bf16[16,128,128]{2,1,0:T(8,128)(2,1)S(1)} %copy-done.19, ...), custom_call_target="tpu_custom_call" | custom-call | flops 1 | bytes 8000000 | tf_op jit(solution)/shard_map/left_products/pallas_call | solution.py:361
  95.8 3.8 %collective-permute-done.21.refs_5_ = bf16[16,128,128]{2,1,0:T(8,128)(2,1)S(1)} collective-permute-done((bf16[16,128,128]{2,1,0:T(8,128)(2,1)S(1)}, bf16[16,128,128]{2,1,0:T(8,128)(2,1)S(1)}, u32[]{:S(2)}, u32[]{:S(2)}) %collective-permute-start.21) | collective-permute-done | bytes 524320 | tf_op jit(solution)/shard_map/ppermute | solution.py:524
  99.8 0.6 collective-permute-start.23
  100.4 0.8 collective-permute-done.20.refs_3_
  101.6 3.7 %known.1.base = f32[64,128,128]{2,1,0:T(8,128)S(1)} custom-call(bf16[64,256,128]{2,1,0:T(8,128)(2,1)S(1)} %copy-done.17, bf16[128,256]{1,0:T(8,128)(2,1)S(1)} %copy-done.28, f32[16,64,128]{2,1,0:T(8,128)S(1)} %get-tuple-element.55.refs_0_, f32[16,64,128]{2,1,0:T(8,128)S(1)} %get-tuple-element.66.refs_1_, ...), custom_call_target="tpu_custom_call" | custom-call | flops 1 | bytes 8000000 | tf_op jit(solution)/shard_map/known/pallas_call | solution.py:428
  105.3 4.3 %collective-permute-done.24.by_a = bf16[16,128,128]{2,1,0:T(8,128)(2,1)S(1)} collective-permute-done((bf16[16,128,128]{2,1,0:T(8,128)(2,1)S(1)}, bf16[16,128,128]{2,1,0:T(8,128)(2,1)S(1)}, u32[]{:S(2)}, u32[]{:S(2)}) %collective-permute-start.24) | collective-permute-done | bytes 524320 | tf_op jit(solution)/shard_map/ppermute | solution.py:524
  110.1 1.3 %collective-permute-done.26.right_other = bf16[16,64,128]{2,1,0:T(8,128)(2,1)S(1)} collective-permute-done((bf16[16,64,128]{2,1,0:T(8,128)(2,1)S(1)}, bf16[16,64,128]{2,1,0:T(8,128)(2,1)S(1)}, u32[]{:S(2)}, u32[]{:S(2)}) %collective-permute-start.26) | collective-permute-done | bytes 262176 | tf_op jit(solution)/shard_map/ppermute | solution.py:516
  111.4 5.1 %tail.1 = bf16[128,64,128]{2,1,0:T(8,128)(2,1)} custom-call(f32[64,128,128]{2,1,0:T(8,128)S(1)} %known.1.base, bf16[64,128,128]{2,1,0:T(8,128)(2,1)S(1)} %copy-done.27, f32[64,1,128]{2,1,0:T(1,128)S(1)} %get-tuple-element.70.inverse, bf16[64,64,128]{2,1,0:T(8,128)(2,1)S(1)} %copy-done.32, f32[1,128]{1,0:T(1,128)S(1)} %bitcast.5, ...), custom_call_target="tpu_custom_call" | custom-call | flops 1 | bytes 8000000 | tf_op jit(solution)/shard_map/tail/pallas_call | solution.py:486
  (103 shorter events, 1.7 us)
Async XLA Ops:
  1.1 2.1 %collective-permute-start = (bf16[64,32,128]{2,1,0:T(8,128)(2,1)S(1)}, bf16[64,32,128]{2,1,0:T(8,128)(2,1)S(1)}, u32[]{:S(2)}, u32[]{:S(2)}) collective-permute-start(bf16[64,32,128]{2,1,0:T(8,128)(2,1)S(1)} %theirs.1), channel_id=1, source_target_pairs={{0,1},{1,0},{2,3},{3,2},{4,5},{5,4},{6,7},{7,6},{8,9},{9,8},{10,11... | collective-permute-start | bytes 1572872 | tf_op jit(solution)/shard_map/ppermute | solution.py:516
  3.5 39.8 %copy-start.2 = (bf16[16,128,128]{2,1,0:T(8,128)(2,1)}, bf16[16,128,128]{2,1,0:T(8,128)(2,1)S(1)}, u32[]{:S(2)}) copy-start(bf16[16,128,128]{2,1,0:T(8,128)(2,1)S(1)} %get-tuple-element.41.refs_0_.refs_6_) | copy-start | bytes 1572868
  3.5 53.7 %copy-start = (bf16[16,128,128]{2,1,0:T(8,128)(2,1)}, bf16[16,128,128]{2,1,0:T(8,128)(2,1)S(1)}, u32[]{:S(2)}) copy-start(bf16[16,128,128]{2,1,0:T(8,128)(2,1)S(1)} %get-tuple-element.60.refs_0_.refs_6_) | copy-start | bytes 1572868
  3.5 10.1 %collective-permute-start.6 = (bf16[16,128,128]{2,1,0:T(8,128)(2,1)S(1)}, bf16[16,128,128]{2,1,0:T(8,128)(2,1)S(1)}, u32[]{:S(2)}, u32[]{:S(2)}) collective-permute-start(bf16[16,128,128]{2,1,0:T(8,128)(2,1)S(1)} %get-tuple-element.41.refs_0_.refs_6_), channel_id=1, source_target_pairs={{0,2},{1,5},{2,0},{3,7},{4,6},{5,1},{6,4},{7,3},{8,10},{9,13},{10,... | collective-permute-start | bytes 1572872 | tf_op jit(solution)/shard_map/ppermute | solution.py:534
  11.4 4.3 %collective-permute-start.1 = (bf16[32,64,128]{2,1,0:T(8,128)(2,1)S(1)}, bf16[32,64,128]{2,1,0:T(8,128)(2,1)S(1)}, u32[]{:S(2)}, u32[]{:S(2)}) collective-permute-start(bf16[32,64,128]{2,1,0:T(8,128)(2,1)S(1)} %get-tuple-element.45), channel_id=1, source_target_pairs={{0,1},{1,0},{2,3},{3,2},{4,5},{5,4},{6,7},{7,6},{8,9},{9,8},{10,11... | collective-permute-start | bytes 1572872 | tf_op jit(solution)/shard_map/ppermute | solution.py:516
  11.5 9.2 %collective-permute-start.2 = (bf16[16,128,128]{2,1,0:T(8,128)(2,1)S(1)}, bf16[16,128,128]{2,1,0:T(8,128)(2,1)S(1)}, u32[]{:S(2)}, u32[]{:S(2)}) collective-permute-start(bf16[16,128,128]{2,1,0:T(8,128)(2,1)S(1)} %get-tuple-element.41.refs_0_.refs_6_), channel_id=1, source_target_pairs={{0,4},{1,3},{2,6},{3,1},{4,0},{5,7},{6,2},{7,5},{8,12},{9,11},{10,... | collective-permute-start | bytes 1572872 | tf_op jit(solution)/shard_map/ppermute | solution.py:534
  13.6 29.7 %copy-start.4 = (bf16[16,128,128]{2,1,0:T(8,128)(2,1)}, bf16[16,128,128]{2,1,0:T(8,128)(2,1)S(1)}, u32[]{:S(2)}) copy-start(bf16[16,128,128]{2,1,0:T(8,128)(2,1)S(1)} %collective-permute-done.6.refs_1_.refs_7_) | copy-start | bytes 1572868
  13.6 12.7 %collective-permute-start.7 = (bf16[16,128,128]{2,1,0:T(8,128)(2,1)S(1)}, bf16[16,128,128]{2,1,0:T(8,128)(2,1)S(1)}, u32[]{:S(2)}, u32[]{:S(2)}) collective-permute-start(bf16[16,128,128]{2,1,0:T(8,128)(2,1)S(1)} %collective-permute-done.6.refs_1_.refs_7_), channel_id=1, source_target_pairs={{0,4},{1,3},{2,6},{3,1},{4,0},{5,7},{6,2},{7,5},{8,12},{9,11},{10,... | collective-permute-start | bytes 1572872 | tf_op jit(solution)/shard_map/ppermute | solution.py:534
  15.7 24.1 %collective-permute-start.3 = (bf16[32,128,128]{2,1,0:T(8,128)(2,1)S(1)}, bf16[32,128,128]{2,1,0:T(8,128)(2,1)S(1)}, u32[]{:S(2)}, u32[]{:S(2)}) collective-permute-start(bf16[32,128,128]{2,1,0:T(8,128)(2,1)S(1)} %constant_dynamic-update-slice_fusion.own), channel_id=1, source_target_pairs={{0,8},{1,9},{2,10},{3,11},{4,12},{5,13},{6,14},{7,15},{8,0},{9,1},... | collective-permute-start | bytes 3145736 | tf_op jit(solution)/shard_map/ppermute | solution.py:524
  17.4 22.5 %collective-permute-start.5 = (bf16[32,128,128]{2,1,0:T(8,128)(2,1)S(1)}, bf16[32,128,128]{2,1,0:T(8,128)(2,1)S(1)}, u32[]{:S(2)}, u32[]{:S(2)}) collective-permute-start(bf16[32,128,128]{2,1,0:T(8,128)(2,1)S(1)} %constant_dynamic-update-slice_fusion.own), channel_id=1, source_target_pairs={{0,1},{1,0},{2,3},{3,2},{4,5},{5,4},{6,7},{7,6},{8,16},{9,17},{10,... | collective-permute-start | bytes 3145736 | tf_op jit(solution)/shard_map/ppermute | solution.py:524
  20.7 22.6 %copy-start.8 = (bf16[16,128,128]{2,1,0:T(8,128)(2,1)}, bf16[16,128,128]{2,1,0:T(8,128)(2,1)S(1)}, u32[]{:S(2)}) copy-start(bf16[16,128,128]{2,1,0:T(8,128)(2,1)S(1)} %collective-permute-done.2.refs_2_.refs_8_) | copy-start | bytes 1572868
  26.3 17.0 %copy-start.12 = (bf16[16,128,128]{2,1,0:T(8,128)(2,1)}, bf16[16,128,128]{2,1,0:T(8,128)(2,1)S(1)}, u32[]{:S(2)}) copy-start(bf16[16,128,128]{2,1,0:T(8,128)(2,1)S(1)} %collective-permute-done.7.refs_3_.refs_9_) | copy-start | bytes 1572868
  26.3 9.9 %collective-permute-start.12 = (bf16[16,128,128]{2,1,0:T(8,128)(2,1)S(1)}, bf16[16,128,128]{2,1,0:T(8,128)(2,1)S(1)}, u32[]{:S(2)}, u32[]{:S(2)}) collective-permute-start(bf16[16,128,128]{2,1,0:T(8,128)(2,1)S(1)} %get-tuple-element.60.refs_0_.refs_6_), channel_id=1, source_target_pairs={{0,2},{1,5},{2,0},{3,7},{4,6},{5,1},{6,4},{7,3},{8,10},{9,13},{10,... | collective-permute-start | bytes 1572872 | tf_op jit(solution)/shard_map/ppermute | solution.py:534
  35.5 2.0 %collective-permute-start.4 = (bf16[32,64,128]{2,1,0:T(8,128)(2,1)S(1)}, bf16[32,64,128]{2,1,0:T(8,128)(2,1)S(1)}, u32[]{:S(2)}, u32[]{:S(2)}) collective-permute-start(bf16[32,64,128]{2,1,0:T(8,128)(2,1)S(1)} %get-tuple-element.49), channel_id=1, source_target_pairs={{0,1},{1,0},{2,3},{3,2},{4,5},{5,4},{6,7},{7,6},{8,9},{9,8},{10,11... | collective-permute-start | bytes 1572872 | tf_op jit(solution)/shard_map/ppermute | solution.py:516
  35.5 10.6 %collective-permute-start.13 = (bf16[16,128,128]{2,1,0:T(8,128)(2,1)S(1)}, bf16[16,128,128]{2,1,0:T(8,128)(2,1)S(1)}, u32[]{:S(2)}, u32[]{:S(2)}) collective-permute-start(bf16[16,128,128]{2,1,0:T(8,128)(2,1)S(1)} %get-tuple-element.60.refs_0_.refs_6_), channel_id=1, source_target_pairs={{0,4},{1,3},{2,6},{3,1},{4,0},{5,7},{6,2},{7,5},{8,12},{9,11},{10,... | collective-permute-start | bytes 1572872 | tf_op jit(solution)/shard_map/ppermute | solution.py:534
  36.3 20.9 %copy-start.6 = (bf16[16,128,128]{2,1,0:T(8,128)(2,1)}, bf16[16,128,128]{2,1,0:T(8,128)(2,1)S(1)}, u32[]{:S(2)}) copy-start(bf16[16,128,128]{2,1,0:T(8,128)(2,1)S(1)} %collective-permute-done.12.refs_1_.refs_7_) | copy-start | bytes 1572868
  36.3 14.0 %collective-permute-start.14 = (bf16[16,128,128]{2,1,0:T(8,128)(2,1)S(1)}, bf16[16,128,128]{2,1,0:T(8,128)(2,1)S(1)}, u32[]{:S(2)}, u32[]{:S(2)}) collective-permute-start(bf16[16,128,128]{2,1,0:T(8,128)(2,1)S(1)} %collective-permute-done.12.refs_1_.refs_7_), channel_id=1, source_target_pairs={{0,4},{1,3},{2,6},{3,1},{4,0},{5,7},{6,2},{7,5},{8,12},{9,11},{10,... | collective-permute-start | bytes 1572872 | tf_op jit(solution)/shard_map/ppermute | solution.py:534
  40.6 13.0 %collective-permute-start.8 = (bf16[16,128,128]{2,1,0:T(8,128)(2,1)S(1)}, bf16[16,128,128]{2,1,0:T(8,128)(2,1)S(1)}, u32[]{:S(2)}, u32[]{:S(2)}) collective-permute-start(bf16[16,128,128]{2,1,0:T(8,128)(2,1)S(1)} %get-tuple-element.50), channel_id=1, source_target_pairs={{0,8},{1,9},{2,10},{3,11},{4,12},{5,13},{6,14},{7,15},{8,0},{9,1},... | collective-permute-start | bytes 1572872 | tf_op jit(solution)/shard_map/ppermute | solution.py:524
  43.3 10.2 %collective-permute-start.9 = (bf16[16,128,128]{2,1,0:T(8,128)(2,1)S(1)}, bf16[16,128,128]{2,1,0:T(8,128)(2,1)S(1)}, u32[]{:S(2)}, u32[]{:S(2)}) collective-permute-start(bf16[16,128,128]{2,1,0:T(8,128)(2,1)S(1)} %get-tuple-element.51), channel_id=1, source_target_pairs={{0,1},{1,0},{2,3},{3,2},{4,5},{5,4},{6,7},{7,6},{8,16},{9,17},{10,... | collective-permute-start | bytes 1572872 | tf_op jit(solution)/shard_map/ppermute | solution.py:524
  46.1 11.1 %copy-start.10 = (bf16[16,128,128]{2,1,0:T(8,128)(2,1)}, bf16[16,128,128]{2,1,0:T(8,128)(2,1)S(1)}, u32[]{:S(2)}) copy-start(bf16[16,128,128]{2,1,0:T(8,128)(2,1)S(1)} %collective-permute-done.13.refs_2_.refs_8_) | copy-start | bytes 1572868
  51.0 14.9 %collective-permute-start.15 = (bf16[16,128,128]{2,1,0:T(8,128)(2,1)S(1)}, bf16[16,128,128]{2,1,0:T(8,128)(2,1)S(1)}, u32[]{:S(2)}, u32[]{:S(2)}) collective-permute-start(bf16[16,128,128]{2,1,0:T(8,128)(2,1)S(1)} %get-tuple-element.61), channel_id=1, source_target_pairs={{0,8},{1,9},{2,10},{3,11},{4,12},{5,13},{6,14},{7,15},{8,0},{9,1},... | collective-permute-start | bytes 1572872 | tf_op jit(solution)/shard_map/ppermute | solution.py:524
  52.7 13.3 %collective-permute-start.16 = (bf16[16,128,128]{2,1,0:T(8,128)(2,1)S(1)}, bf16[16,128,128]{2,1,0:T(8,128)(2,1)S(1)}, u32[]{:S(2)}, u32[]{:S(2)}) collective-permute-start(bf16[16,128,128]{2,1,0:T(8,128)(2,1)S(1)} %get-tuple-element.62), channel_id=1, source_target_pairs={{0,1},{1,0},{2,3},{3,2},{4,5},{5,4},{6,7},{7,6},{8,16},{9,17},{10,... | collective-permute-start | bytes 1572872 | tf_op jit(solution)/shard_map/ppermute | solution.py:524
  54.9 22.4 %collective-permute-start.10 = (bf16[16,128,128]{2,1,0:T(8,128)(2,1)}, bf16[16,128,128]{2,1,0:T(8,128)(2,1)}, u32[]{:S(2)}, u32[]{:S(2)}) collective-permute-start(bf16[16,128,128]{2,1,0:T(8,128)(2,1)} %get-tuple-element.53), channel_id=1, source_target_pairs={{0,8},{1,9},{2,10},{3,11},{4,12},{5,13},{6,14},{7,15},{8,0},{9,1},... | collective-permute-start | bytes 1572872 | tf_op jit(solution)/shard_map/ppermute | solution.py:524
  57.2 20.1 %collective-permute-start.11 = (bf16[16,128,128]{2,1,0:T(8,128)(2,1)}, bf16[16,128,128]{2,1,0:T(8,128)(2,1)}, u32[]{:S(2)}, u32[]{:S(2)}) collective-permute-start(bf16[16,128,128]{2,1,0:T(8,128)(2,1)} %get-tuple-element.54), channel_id=1, source_target_pairs={{0,1},{1,0},{2,3},{3,2},{4,5},{5,4},{6,7},{7,6},{8,16},{9,17},{10,... | collective-permute-start | bytes 1572872 | tf_op jit(solution)/shard_map/ppermute | solution.py:524
  68.0 20.5 %collective-permute-start.17 = (bf16[16,128,128]{2,1,0:T(8,128)(2,1)}, bf16[16,128,128]{2,1,0:T(8,128)(2,1)}, u32[]{:S(2)}, u32[]{:S(2)}) collective-permute-start(bf16[16,128,128]{2,1,0:T(8,128)(2,1)} %get-tuple-element.64), channel_id=1, source_target_pairs={{0,8},{1,9},{2,10},{3,11},{4,12},{5,13},{6,14},{7,15},{8,0},{9,1},... | collective-permute-start | bytes 1572872 | tf_op jit(solution)/shard_map/ppermute | solution.py:524
  70.7 17.8 %collective-permute-start.18 = (bf16[16,128,128]{2,1,0:T(8,128)(2,1)}, bf16[16,128,128]{2,1,0:T(8,128)(2,1)}, u32[]{:S(2)}, u32[]{:S(2)}) collective-permute-start(bf16[16,128,128]{2,1,0:T(8,128)(2,1)} %get-tuple-element.65), channel_id=1, source_target_pairs={{0,1},{1,0},{2,3},{3,2},{4,5},{5,4},{6,7},{7,6},{8,16},{9,17},{10,... | collective-permute-start | bytes 1572872 | tf_op jit(solution)/shard_map/ppermute | solution.py:524
  70.7 11.4 %copy-start.3 = (bf16[16,128,128]{2,1,0:T(8,128)(2,1)S(1)}, bf16[16,128,128]{2,1,0:T(8,128)(2,1)}, u32[]{:S(2)}) copy-start(bf16[16,128,128]{2,1,0:T(8,128)(2,1)} %copy-done.2) | copy-start | bytes 1572868
  70.7 11.4 %copy-start.5 = (bf16[16,128,128]{2,1,0:T(8,128)(2,1)S(1)}, bf16[16,128,128]{2,1,0:T(8,128)(2,1)}, u32[]{:S(2)}) copy-start(bf16[16,128,128]{2,1,0:T(8,128)(2,1)} %copy-done.4) | copy-start | bytes 1572868
  70.7 11.4 %copy-start.9 = (bf16[16,128,128]{2,1,0:T(8,128)(2,1)S(1)}, bf16[16,128,128]{2,1,0:T(8,128)(2,1)}, u32[]{:S(2)}) copy-start(bf16[16,128,128]{2,1,0:T(8,128)(2,1)} %copy-done.8) | copy-start | bytes 1572868
  70.7 11.4 %copy-start.13 = (bf16[16,128,128]{2,1,0:T(8,128)(2,1)S(1)}, bf16[16,128,128]{2,1,0:T(8,128)(2,1)}, u32[]{:S(2)}) copy-start(bf16[16,128,128]{2,1,0:T(8,128)(2,1)} %copy-done.12) | copy-start | bytes 1572868
  70.8 11.4 %copy-start.23 = (bf16[16,128,128]{2,1,0:T(8,128)(2,1)S(1)}, bf16[16,128,128]{2,1,0:T(8,128)(2,1)}, u32[]{:S(2)}) copy-start(bf16[16,128,128]{2,1,0:T(8,128)(2,1)} %copy-done.22) | copy-start | bytes 1572868
  70.8 11.4 %copy-start.25 = (bf16[16,128,128]{2,1,0:T(8,128)(2,1)S(1)}, bf16[16,128,128]{2,1,0:T(8,128)(2,1)}, u32[]{:S(2)}) copy-start(bf16[16,128,128]{2,1,0:T(8,128)(2,1)} %copy-done.24) | copy-start | bytes 1572868
  79.3 20.3 %collective-permute-start.21 = (bf16[16,128,128]{2,1,0:T(8,128)(2,1)S(1)}, bf16[16,128,128]{2,1,0:T(8,128)(2,1)S(1)}, u32[]{:S(2)}, u32[]{:S(2)}) collective-permute-start(bf16[16,128,128]{2,1,0:T(8,128)(2,1)S(1)} %get-tuple-element.80), channel_id=1, source_target_pairs={{0,8},{1,9},{2,10},{3,11},{4,12},{5,13},{6,14},{7,15},{8,0},{9,1},... | collective-permute-start | bytes 1572872 | tf_op jit(solution)/shard_map/ppermute | solution.py:524
  82.1 17.5 %collective-permute-start.22 = (bf16[16,128,128]{2,1,0:T(8,128)(2,1)S(1)}, bf16[16,128,128]{2,1,0:T(8,128)(2,1)S(1)}, u32[]{:S(2)}, u32[]{:S(2)}) collective-permute-start(bf16[16,128,128]{2,1,0:T(8,128)(2,1)S(1)} %get-tuple-element.79), channel_id=1, source_target_pairs={{0,1},{1,0},{2,3},{3,2},{4,5},{5,4},{6,7},{7,6},{8,16},{9,17},{10,... | collective-permute-start | bytes 1572872 | tf_op jit(solution)/shard_map/ppermute | solution.py:524
  84.3 9.2 %copy-start.1 = (bf16[16,128,128]{2,1,0:T(8,128)(2,1)S(1)}, bf16[16,128,128]{2,1,0:T(8,128)(2,1)}, u32[]{:S(2)}) copy-start(bf16[16,128,128]{2,1,0:T(8,128)(2,1)} %copy-done) | copy-start | bytes 1572868
  84.3 9.2 %copy-start.7 = (bf16[16,128,128]{2,1,0:T(8,128)(2,1)S(1)}, bf16[16,128,128]{2,1,0:T(8,128)(2,1)}, u32[]{:S(2)}) copy-start(bf16[16,128,128]{2,1,0:T(8,128)(2,1)} %copy-done.6) | copy-start | bytes 1572868
  84.4 9.2 %copy-start.11 = (bf16[16,128,128]{2,1,0:T(8,128)(2,1)S(1)}, bf16[16,128,128]{2,1,0:T(8,128)(2,1)}, u32[]{:S(2)}) copy-start(bf16[16,128,128]{2,1,0:T(8,128)(2,1)} %copy-done.10) | copy-start | bytes 1572868
  84.4 9.2 %copy-start.15 = (bf16[16,128,128]{2,1,0:T(8,128)(2,1)S(1)}, bf16[16,128,128]{2,1,0:T(8,128)(2,1)}, u32[]{:S(2)}) copy-start(bf16[16,128,128]{2,1,0:T(8,128)(2,1)} %copy-done.14) | copy-start | bytes 1572868
  84.4 9.2 %copy-start.19 = (bf16[16,128,128]{2,1,0:T(8,128)(2,1)S(1)}, bf16[16,128,128]{2,1,0:T(8,128)(2,1)}, u32[]{:S(2)}) copy-start(bf16[16,128,128]{2,1,0:T(8,128)(2,1)} %copy-done.18) | copy-start | bytes 1572868
  84.4 9.2 %copy-start.21 = (bf16[16,128,128]{2,1,0:T(8,128)(2,1)S(1)}, bf16[16,128,128]{2,1,0:T(8,128)(2,1)}, u32[]{:S(2)}) copy-start(bf16[16,128,128]{2,1,0:T(8,128)(2,1)} %copy-done.20) | copy-start | bytes 1572868
  90.3 19.4 %collective-permute-start.24 = (bf16[16,128,128]{2,1,0:T(8,128)(2,1)S(1)}, bf16[16,128,128]{2,1,0:T(8,128)(2,1)S(1)}, u32[]{:S(2)}, u32[]{:S(2)}) collective-permute-start(bf16[16,128,128]{2,1,0:T(8,128)(2,1)S(1)} %get-tuple-element.78), channel_id=1, source_target_pairs={{0,8},{1,9},{2,10},{3,11},{4,12},{5,13},{6,14},{7,15},{8,0},{9,1},... | collective-permute-start | bytes 1572872 | tf_op jit(solution)/shard_map/ppermute | solution.py:524
  93.0 16.6 %collective-permute-start.25 = (bf16[16,128,128]{2,1,0:T(8,128)(2,1)S(1)}, bf16[16,128,128]{2,1,0:T(8,128)(2,1)S(1)}, u32[]{:S(2)}, u32[]{:S(2)}) collective-permute-start(bf16[16,128,128]{2,1,0:T(8,128)(2,1)S(1)} %get-tuple-element.77), channel_id=1, source_target_pairs={{0,1},{1,0},{2,3},{3,2},{4,5},{5,4},{6,7},{7,6},{8,16},{9,17},{10,... | collective-permute-start | bytes 1572872 | tf_op jit(solution)/shard_map/ppermute | solution.py:524
  93.0 7.3 %collective-permute-start.19 = (bf16[16,64,128]{2,1,0:T(8,128)(2,1)S(1)}, bf16[16,64,128]{2,1,0:T(8,128)(2,1)S(1)}, u32[]{:S(2)}, u32[]{:S(2)}) collective-permute-start(bf16[16,64,128]{2,1,0:T(8,128)(2,1)S(1)} %get-tuple-element.67), channel_id=1, source_target_pairs={{0,1},{1,0},{2,3},{3,2},{4,5},{5,4},{6,7},{7,6},{8,9},{9,8},{10,11... | collective-permute-start | bytes 786440 | tf_op jit(solution)/shard_map/ppermute | solution.py:516
  99.6 1.5 %collective-permute-start.20 = (bf16[16,64,128]{2,1,0:T(8,128)(2,1)S(1)}, bf16[16,64,128]{2,1,0:T(8,128)(2,1)S(1)}, u32[]{:S(2)}, u32[]{:S(2)}) collective-permute-start(bf16[16,64,128]{2,1,0:T(8,128)(2,1)S(1)} %get-tuple-element.68), channel_id=1, source_target_pairs={{0,1},{1,0},{2,3},{3,2},{4,5},{5,4},{6,7},{7,6},{8,9},{9,8},{10,11... | collective-permute-start | bytes 786440 | tf_op jit(solution)/shard_map/ppermute | solution.py:516
  99.8 1.7 %collective-permute-start.23 = (bf16[16,64,128]{2,1,0:T(8,128)(2,1)S(1)}, bf16[16,64,128]{2,1,0:T(8,128)(2,1)S(1)}, u32[]{:S(2)}, u32[]{:S(2)}) collective-permute-start(bf16[16,64,128]{2,1,0:T(8,128)(2,1)S(1)} %add_convert_fusion.5), channel_id=1, source_target_pairs={{0,1},{1,0},{2,3},{3,2},{4,5},{5,4},{6,7},{7,6},{8,9},{9,8},{10,11... | collective-permute-start | bytes 786440 | tf_op jit(solution)/shard_map/ppermute | solution.py:516
  101.5 9.9 %copy-start.27 = (bf16[64,128,128]{2,1,0:T(8,128)(2,1)S(1)}, bf16[64,128,128]{2,1,0:T(8,128)(2,1)}, u32[]{:S(2)}) copy-start(bf16[64,128,128]{2,1,0:T(8,128)(2,1)} %copy-done.26) | copy-start | bytes 6291460
  101.6 9.9 %copy-start.34 = (f32[128]{0:T(128)S(1)}, f32[128]{0:T(128)}, u32[]{:S(2)}) copy-start(f32[128]{0:T(128)} %param.8) | copy-start | bytes 1540
  109.8 1.6 %collective-permute-start.26 = (bf16[16,64,128]{2,1,0:T(8,128)(2,1)S(1)}, bf16[16,64,128]{2,1,0:T(8,128)(2,1)S(1)}, u32[]{:S(2)}, u32[]{:S(2)}) collective-permute-start(bf16[16,64,128]{2,1,0:T(8,128)(2,1)S(1)} %add_convert_fusion.4), channel_id=1, source_target_pairs={{0,1},{1,0},{2,3},{3,2},{4,5},{5,4},{6,7},{7,6},{8,9},{9,8},{10,11... | collective-permute-start | bytes 786440 | tf_op jit(solution)/shard_map/ppermute | solution.py:516
  (16 other events, 90.4 us)

commit v13 on v12

--- a/solution.py
+++ b/solution.py
@@ -371,7 +371,7 @@
         compiler_params=PARAMS,
         cost_estimate=COST,
         name="left_products",
-    )(*args)
+    )(*in_hbm(*args))
 
 
 def arrived_total(own, by_a, by_b, n):
@@ -561,10 +561,7 @@
             value = by_a[c][-1]
             if t == n - 1 and c > 0:
                 value = after(value, left_grads[c - 1])
-            if t == 2:
-                next_a, next_b = advance(value, by_b[c][-1], partials[c], t)
-            else:
-                next_a, next_b = onward(value, by_b[c][-1], partials[c][n - t], partials[c][t], t, n)
+            next_a, next_b = advance(value, by_b[c][-1], partials[c], t)
             by_a[c].append(hop(next_a, 0))
             by_b[c].append(hop(next_b, 1))
             if t == n - 1:

time: 117 us -> 118 us (level)
  other arithmetic: 4.18 us -> 0.39 us
  Pallas kernels: 36.1 us -> 39.4 us
    convert_element_type x2 -> x0, other arithmetic: 3.79 us -> none  [onward(): return (out_a.astype(jnp.bfloat16), out_b.astype(jnp.bfloat16))]
    pallas_call x2, Pallas kernels: 4.43 us -> 6.58 us  [left_products(): pl.pallas_call(functools.partial(left_kernel, n), out_shape=[jax.ShapeDty...]
    ppermute x14, waiting for transfers between devices: 27.9 us -> 26.7 us  [hop(): return lax.ppermute(value, ('row', 'col'), perm)]
    unnamed x75 -> x73, local copies, waits for them, and re-layouts: 2.93 us -> 3.93 us
    pallas_call x2 -> x4, Pallas kernels: 2.65 us -> 3.54 us  [advance(): pl.pallas_call(functools.partial(advance_kernel, t, n), out_shape=[jax.Sh...]
  transfers between devices with their start and end apart: 27 -> 27, of which waited for: 15 -> 14; matrix products, arithmetic and copies ran while one was open for 4% -> 0% of each run, Pallas kernels for 25% -> 28%
where the time goes in v13:
time: 118 us
  waiting for transfers between devices  44.3 us (38%)
  Pallas kernels  39.4 us (33%)
  starting transfers between devices  29 us (25%)
  local copies, waits for them, and re-layouts  4.1 us (3%)
    ppermute x14, waiting for transfers between devices, hop(): return lax.ppermute(value, ('row', 'col'), perm)  26.7 us
    ppermute x14, starting transfers between devices, hop(): return lax.ppermute(value, ('row', 'col'), perm)  17.4 us
    ppermute x6, waiting for transfers between devices, along(): lax.ppermute(value, 'col', [(d, d ^ mask[d % CORES]) for d in range(n_col)])  14.6 us
    pallas_call x2, Pallas kernels, front(): pl.pallas_call(right_kernel if right else left_forward_kernel, out_shape=...  10.8 us
    ppermute x6, starting transfers between devices, along(): lax.ppermute(value, 'col', [(d, d ^ mask[d % CORES]) for d in range(n_col)])  9.89 us
    pallas_call x2, Pallas kernels, left_products(): pl.pallas_call(functools.partial(left_kernel, n), out_shape=[jax.ShapeDty...  6.58 us
    pallas_call x2, Pallas kernels, partial_products(): pl.pallas_call(functools.partial(partial_kernel, n), out_shape=[(jax.Shap...  5.47 us
    pallas_call x1, Pallas kernels, tail(): pl.pallas_call(functools.partial(tail_kernel, lax.axis_size('row')), out_...  5.22 us
  transfers between devices with their start and end apart: 27, of which 14 were waited for; matrix products, arithmetic and copies ran while one was open for 0% of the time, Pallas kernels for 28%

profile of v13, /device:TPU:0, one launch (start us, length us, event | category | flops | bytes accessed | tf_op | source)
XLA Modules:
  0.0 117.5 jit_solution(7838755682551507406)
XLA Ops:
  0.0 1.1 theirs.1
  1.1 0.5 collective-permute-start
  1.6 1.0 mine.1.own
  2.6 0.5 collective-permute-done.other
  3.5 2.9 %collective-permute-start.6 = (bf16[16,128,128]{2,1,0:T(8,128)(2,1)S(1)}, bf16[16,128,128]{2,1,0:T(8,128)(2,1)S(1)}, u32[]{:S(2)}, u32[]{:S(2)}) collective-permute-start(bf16[16,128,128]{2,1,0:T(8,128)(2,1)S(1)} %get-tuple-element.45.refs_0_.refs_6_), channel_id=1, source_target_pairs={{0,2},{1,5},{2,0},{3,7},{4,6},{5,1},{6,4},{7,3},{8,10},{9,13},{10,... | collective-permute-start | bytes 1572872 | tf_op jit(solution)/shard_map/ppermute | solution.py:534
  6.4 4.9 %right_front.1 = (bf16[32,64,128]{2,1,0:T(8,128)(2,1)S(1)}, bf16[32,64,128]{2,1,0:T(8,128)(2,1)S(1)}) custom-call(s32[4,4]{1,0:T(4,128)S(1)} %copy-done.33, bf16[128,64,128]{2,1,0:T(8,128)(2,1)} %pair.1, f32[1,128]{1,0:T(1,128)} %bitcast.3, f32[1,128]{1,0:T(1,128)} %bitcast.8, bf16[128,256]{1,0:T(8,128)(2,1)} %weight.5), custom_call_target="tpu_custom_call" | custom-call | flops 1 | bytes 18000000 | tf_op jit(solution)/shard_map/right_front/pallas_call | solution.py:148
  11.5 1.6 %collective-permute-start.2 = (bf16[16,128,128]{2,1,0:T(8,128)(2,1)S(1)}, bf16[16,128,128]{2,1,0:T(8,128)(2,1)S(1)}, u32[]{:S(2)}, u32[]{:S(2)}) collective-permute-start(bf16[16,128,128]{2,1,0:T(8,128)(2,1)S(1)} %get-tuple-element.45.refs_0_.refs_6_), channel_id=1, source_target_pairs={{0,4},{1,3},{2,6},{3,1},{4,0},{5,7},{6,2},{7,5},{8,12},{9,11},{10,... | collective-permute-start | bytes 1572872 | tf_op jit(solution)/shard_map/ppermute | solution.py:534
  13.1 0.5 collective-permute-done.6.refs_1_.refs_7_
  13.6 2.0 %collective-permute-start.7 = (bf16[16,128,128]{2,1,0:T(8,128)(2,1)S(1)}, bf16[16,128,128]{2,1,0:T(8,128)(2,1)S(1)}, u32[]{:S(2)}, u32[]{:S(2)}) collective-permute-start(bf16[16,128,128]{2,1,0:T(8,128)(2,1)S(1)} %collective-permute-done.6.refs_1_.refs_7_), channel_id=1, source_target_pairs={{0,4},{1,3},{2,6},{3,1},{4,0},{5,7},{6,2},{7,5},{8,12},{9,11},{10,... | collective-permute-start | bytes 1572872 | tf_op jit(solution)/shard_map/ppermute | solution.py:534
  15.7 1.6 %collective-permute-start.3 = (bf16[32,128,128]{2,1,0:T(8,128)(2,1)S(1)}, bf16[32,128,128]{2,1,0:T(8,128)(2,1)S(1)}, u32[]{:S(2)}, u32[]{:S(2)}) collective-permute-start(bf16[32,128,128]{2,1,0:T(8,128)(2,1)S(1)} %constant_dynamic-update-slice_fusion.own), channel_id=1, source_target_pairs={{0,8},{1,9},{2,10},{3,11},{4,12},{5,13},{6,14},{7,15},{8,0},{9,1},... | collective-permute-start | bytes 3145736 | tf_op jit(solution)/shard_map/ppermute | solution.py:524
  17.4 3.3 %collective-permute-done.2.refs_2_.refs_8_ = bf16[16,128,128]{2,1,0:T(8,128)(2,1)S(1)} collective-permute-done((bf16[16,128,128]{2,1,0:T(8,128)(2,1)S(1)}, bf16[16,128,128]{2,1,0:T(8,128)(2,1)S(1)}, u32[]{:S(2)}, u32[]{:S(2)}) %collective-permute-start.2) | collective-permute-done | bytes 524320 | tf_op jit(solution)/shard_map/ppermute | solution.py:534
  20.7 5.6 %collective-permute-done.7.refs_3_.refs_9_ = bf16[16,128,128]{2,1,0:T(8,128)(2,1)S(1)} collective-permute-done((bf16[16,128,128]{2,1,0:T(8,128)(2,1)S(1)}, bf16[16,128,128]{2,1,0:T(8,128)(2,1)S(1)}, u32[]{:S(2)}, u32[]{:S(2)}) %collective-permute-start.7) | collective-permute-done | bytes 524320 | tf_op jit(solution)/shard_map/ppermute | solution.py:534
  26.3 1.3 %collective-permute-start.12 = (bf16[16,128,128]{2,1,0:T(8,128)(2,1)S(1)}, bf16[16,128,128]{2,1,0:T(8,128)(2,1)S(1)}, u32[]{:S(2)}, u32[]{:S(2)}) collective-permute-start(bf16[16,128,128]{2,1,0:T(8,128)(2,1)S(1)} %get-tuple-element.64.refs_0_.refs_6_), channel_id=1, source_target_pairs={{0,2},{1,5},{2,0},{3,7},{4,6},{5,1},{6,4},{7,3},{8,10},{9,13},{10,... | collective-permute-start | bytes 1572872 | tf_op jit(solution)/shard_map/ppermute | solution.py:534
  27.6 5.9 %left_front.1 = (bf16[32,64,128]{2,1,0:T(8,128)(2,1)S(1)}, bf16[32,64,128]{2,1,0:T(8,128)(2,1)S(1)}, bf16[64,128,128]{2,1,0:T(8,128)(2,1)S(1)}, f32[64,1,128]{2,...) custom-call(s32[4,4]{1,0:T(4,128)S(1)} %copy-done.33, bf16[128,64,128]{2,1,0:T(8,128)(2,1)} %pair.1, ...), custom_call_target="tpu_custom_call" | custom-call | flops 1 | bytes 18000000 | tf_op jit(solution)/shard_map/left_front/pallas_call | solution.py:148
  33.5 2.0 %copy-done.10 = bf16[64,256,128]{2,1,0:T(8,128)(2,1)} copy-done((bf16[64,256,128]{2,1,0:T(8,128)(2,1)}, bf16[64,256,128]{2,1,0:T(8,128)(2,1)S(1)}, u32[]{:S(2)}) %copy-start.10) | copy-done | bytes 4194328
  35.5 1.0 copy-done.25
  36.5 0.7 collective-permute-start.13
  37.3 1.3 %collective-permute-start.14 = (bf16[16,128,128]{2,1,0:T(8,128)(2,1)S(1)}, bf16[16,128,128]{2,1,0:T(8,128)(2,1)S(1)}, u32[]{:S(2)}, u32[]{:S(2)}) collective-permute-start(bf16[16,128,128]{2,1,0:T(8,128)(2,1)S(1)} %collective-permute-done.12.refs_1_.refs_7_), channel_id=1, source_target_pairs={{0,4},{1,3},{2,6},{3,1},{4,0},{5,7},{6,2},{7,5},{8,12},{9,11},{10,... | collective-permute-start | bytes 1572872 | tf_op jit(solution)/shard_map/ppermute | solution.py:534
  38.5 1.3 %collective-permute-done.3.by_a.refs_0_ = bf16[32,128,128]{2,1,0:T(8,128)(2,1)S(1)} collective-permute-done((bf16[32,128,128]{2,1,0:T(8,128)(2,1)S(1)}, bf16[32,128,128]{2,1,0:T(8,128)(2,1)S(1)}, u32[]{:S(2)}, u32[]{:S(2)}) %collective-permute-start.3) | collective-permute-done | bytes 1048608 | tf_op jit(solution)/shard_map/ppermute | solution.py:524
  39.8 0.7 first_step.2
  40.6 2.8 %collective-permute-start.8 = (bf16[16,128,128]{2,1,0:T(8,128)(2,1)S(1)}, bf16[16,128,128]{2,1,0:T(8,128)(2,1)S(1)}, u32[]{:S(2)}, u32[]{:S(2)}) collective-permute-start(bf16[16,128,128]{2,1,0:T(8,128)(2,1)S(1)} %get-tuple-element.54), channel_id=1, source_target_pairs={{0,8},{1,9},{2,10},{3,11},{4,12},{5,13},{6,14},{7,15},{8,0},{9,1},... | collective-permute-start | bytes 1572872 | tf_op jit(solution)/shard_map/ppermute | solution.py:524
  43.4 2.8 %right_partials.2 = (bf16[16,128,128]{2,1,0:T(8,128)(2,1)}, bf16[16,128,128]{2,1,0:T(8,128)(2,1)}, bf16[16,128,128]{2,1,0:T(8,128)(2,1)S(1)}, bf16[16,128,128]{2,1,0:T(8,128)(2,1)}) custom-call(bf16[32,64,128]{2,1,0:T(8,128)(2,1)S(1)} %get-tuple-element.52.left_mine, bf16[32,64,128]{2,1,0:T(8,128)(2,1)S(1)} %collective-permute-done.4.left_other, ...), custom_call_target="tpu_custom_call" | custom-call | flops 1 | bytes 8000000 | tf_op jit(solution)/shard_map/right_partials/pallas_call | solution.py:301
  46.2 5.1 %collective-permute-done.14.refs_3_.refs_9_ = bf16[16,128,128]{2,1,0:T(8,128)(2,1)S(1)} collective-permute-done((bf16[16,128,128]{2,1,0:T(8,128)(2,1)S(1)}, bf16[16,128,128]{2,1,0:T(8,128)(2,1)S(1)}, u32[]{:S(2)}, u32[]{:S(2)}) %collective-permute-start.14) | collective-permute-done | bytes 524320 | tf_op jit(solution)/shard_map/ppermute | solution.py:534
  51.3 0.7 first_step.3
  52.0 1.6 %collective-permute-start.15 = (bf16[16,128,128]{2,1,0:T(8,128)(2,1)S(1)}, bf16[16,128,128]{2,1,0:T(8,128)(2,1)S(1)}, u32[]{:S(2)}, u32[]{:S(2)}) collective-permute-start(bf16[16,128,128]{2,1,0:T(8,128)(2,1)S(1)} %get-tuple-element.65), channel_id=1, source_target_pairs={{0,8},{1,9},{2,10},{3,11},{4,12},{5,13},{6,14},{7,15},{8,0},{9,1},... | collective-permute-start | bytes 1572872 | tf_op jit(solution)/shard_map/ppermute | solution.py:524
  53.7 0.5 advance.4
  54.2 3.2 %collective-permute-start.10 = (bf16[16,128,128]{2,1,0:T(8,128)(2,1)S(1)}, bf16[16,128,128]{2,1,0:T(8,128)(2,1)S(1)}, u32[]{:S(2)}, u32[]{:S(2)}) collective-permute-start(bf16[16,128,128]{2,1,0:T(8,128)(2,1)S(1)} %get-tuple-element.57), channel_id=1, source_target_pairs={{0,8},{1,9},{2,10},{3,11},{4,12},{5,13},{6,14},{7,15},{8,0},{9,1},... | collective-permute-start | bytes 1572872 | tf_op jit(solution)/shard_map/ppermute | solution.py:524
  57.4 2.7 %right_partials.3 = (bf16[16,128,128]{2,1,0:T(8,128)(2,1)}, bf16[16,128,128]{2,1,0:T(8,128)(2,1)}, bf16[16,128,128]{2,1,0:T(8,128)(2,1)S(1)}, bf16[16,128,128]{2,1,0:T(8,128)(2,1)}) custom-call(bf16[32,64,128]{2,1,0:T(8,128)(2,1)S(1)} %get-tuple-element.52.left_mine, bf16[32,64,128]{2,1,0:T(8,128)(2,1)S(1)} %collective-permute-done.4.left_other, ...), custom_call_target="tpu_custom_call" | custom-call | flops 1 | bytes 8000000 | tf_op jit(solution)/shard_map/right_partials/pallas_call | solution.py:301
  60.1 6.8 %collective-permute-done.15.by_a.refs_1_ = bf16[16,128,128]{2,1,0:T(8,128)(2,1)S(1)} collective-permute-done((bf16[16,128,128]{2,1,0:T(8,128)(2,1)S(1)}, bf16[16,128,128]{2,1,0:T(8,128)(2,1)S(1)}, u32[]{:S(2)}, u32[]{:S(2)}) %collective-permute-start.15) | collective-permute-done | bytes 524320 | tf_op jit(solution)/shard_map/ppermute | solution.py:524
  67.0 0.5 advance.5
  67.4 2.8 %collective-permute-start.17 = (bf16[16,128,128]{2,1,0:T(8,128)(2,1)S(1)}, bf16[16,128,128]{2,1,0:T(8,128)(2,1)S(1)}, u32[]{:S(2)}, u32[]{:S(2)}) collective-permute-start(bf16[16,128,128]{2,1,0:T(8,128)(2,1)S(1)} %get-tuple-element.68), channel_id=1, source_target_pairs={{0,8},{1,9},{2,10},{3,11},{4,12},{5,13},{6,14},{7,15},{8,0},{9,1},... | collective-permute-start | bytes 1572872 | tf_op jit(solution)/shard_map/ppermute | solution.py:524
  70.2 8.0 %collective-permute-done.10.refs_2_.by_a = bf16[16,128,128]{2,1,0:T(8,128)(2,1)S(1)} collective-permute-done((bf16[16,128,128]{2,1,0:T(8,128)(2,1)S(1)}, bf16[16,128,128]{2,1,0:T(8,128)(2,1)S(1)}, u32[]{:S(2)}, u32[]{:S(2)}) %collective-permute-start.10) | collective-permute-done | bytes 524320 | tf_op jit(solution)/shard_map/ppermute | solution.py:524
  78.2 1.3 %advance.6 = (bf16[16,128,128]{2,1,0:T(8,128)(2,1)}, bf16[16,128,128]{2,1,0:T(8,128)(2,1)}) custom-call(bf16[16,128,128]{2,1,0:T(8,128)(2,1)S(1)} %collective-permute-done.10.refs_2_.by_a, bf16[16,128,128]{2,1,0:T(8,128)(2,1)S(1)} %collective-permute-done.11.refs_5_.by_b, bf16[16,128,128]{2,1,0:T(8,128)(2,1)S(1)} %copy-done.29, ...), custom_call_target="tpu_custom_call" | custom-call | flops 1 | bytes 8000000 | tf_op jit(solution)/shard_map/advance/pallas_call | solution.py:323
  79.5 2.7 %collective-permute-start.21 = (bf16[16,128,128]{2,1,0:T(8,128)(2,1)}, bf16[16,128,128]{2,1,0:T(8,128)(2,1)S(1)}, u32[]{:S(2)}, u32[]{:S(2)}) collective-permute-start(bf16[16,128,128]{2,1,0:T(8,128)(2,1)} %get-tuple-element.73), channel_id=1, source_target_pairs={{0,8},{1,9},{2,10},{3,11},{4,12},{5,13},{6,14},{7,15},{8,0},{9,1},... | collective-permute-start | bytes 1572872 | tf_op jit(solution)/shard_map/ppermute | solution.py:524
  82.2 3.3 %left_products.2 = (f32[16,64,128]{2,1,0:T(8,128)S(1)}, bf16[16,64,128]{2,1,0:T(8,128)(2,1)S(1)}) custom-call(bf16[32,128,128]{2,1,0:T(8,128)(2,1)} %copy-done.35, bf16[32,128,128]{2,1,0:T(8,128)(2,1)} %copy-done, bf16[16,128,128]{2,1,0:T(8,128)(2,1)} %copy-done.16, bf16[16,128,128]{2,1,0:T(8,128)(2,1)} %copy-done.18, bf16[32,128,128]{2,1,0:T(8,128)(2,1)} %copy-done.1, ...), custom_call_target="tpu_custom_call" | custom-call | flops 1 | bytes 8000000 | tf_op jit(solution)/shard_map/left_products/pallas_call | solution.py:361
  85.5 0.8 copy-done.27
  86.3 3.1 %collective-permute-done.17.refs_2_.by_a = bf16[16,128,128]{2,1,0:T(8,128)(2,1)S(1)} collective-permute-done((bf16[16,128,128]{2,1,0:T(8,128)(2,1)S(1)}, bf16[16,128,128]{2,1,0:T(8,128)(2,1)S(1)}, u32[]{:S(2)}, u32[]{:S(2)}) %collective-permute-start.17) | collective-permute-done | bytes 524320 | tf_op jit(solution)/shard_map/ppermute | solution.py:524
  89.4 1.3 %advance.7 = (bf16[16,128,128]{2,1,0:T(8,128)(2,1)}, bf16[16,128,128]{2,1,0:T(8,128)(2,1)}) custom-call(bf16[16,128,128]{2,1,0:T(8,128)(2,1)S(1)} %collective-permute-done.17.refs_2_.by_a, bf16[16,128,128]{2,1,0:T(8,128)(2,1)S(1)} %collective-permute-done.18.refs_5_.by_b, bf16[16,128,128]{2,1,0:T(8,128)(2,1)S(1)} %copy-done.31, ...), custom_call_target="tpu_custom_call" | custom-call | flops 1 | bytes 8000000 | tf_op jit(solution)/shard_map/advance/pallas_call | solution.py:323
  90.8 2.7 %collective-permute-start.24 = (bf16[16,128,128]{2,1,0:T(8,128)(2,1)}, bf16[16,128,128]{2,1,0:T(8,128)(2,1)S(1)}, u32[]{:S(2)}, u32[]{:S(2)}) collective-permute-start(bf16[16,128,128]{2,1,0:T(8,128)(2,1)} %get-tuple-element.82), channel_id=1, source_target_pairs={{0,8},{1,9},{2,10},{3,11},{4,12},{5,13},{6,14},{7,15},{8,0},{9,1},... | collective-permute-start | bytes 1572872 | tf_op jit(solution)/shard_map/ppermute | solution.py:524
  93.4 0.5 collective-permute-start.19
  94.0 3.3 %left_products.3 = (f32[16,64,128]{2,1,0:T(8,128)S(1)}, bf16[16,64,128]{2,1,0:T(8,128)(2,1)S(1)}) custom-call(bf16[32,128,128]{2,1,0:T(8,128)(2,1)} %copy-done.35, bf16[32,128,128]{2,1,0:T(8,128)(2,1)} %copy-done, bf16[16,128,128]{2,1,0:T(8,128)(2,1)} %copy-done.12, bf16[16,128,128]{2,1,0:T(8,128)(2,1)} %copy-done.14, bf16[32,128,128]{2,1,0:T(8,128)(2,1)} %copy-done.1, ...), custom_call_target="tpu_custom_call" | custom-call | flops 1 | bytes 8000000 | tf_op jit(solution)/shard_map/left_products/pallas_call | solution.py:361
  97.3 3.4 %collective-permute-done.21.refs_5_ = bf16[16,128,128]{2,1,0:T(8,128)(2,1)S(1)} collective-permute-done((bf16[16,128,128]{2,1,0:T(8,128)(2,1)}, bf16[16,128,128]{2,1,0:T(8,128)(2,1)S(1)}, u32[]{:S(2)}, u32[]{:S(2)}) %collective-permute-start.21) | collective-permute-done | bytes 524320 | tf_op jit(solution)/shard_map/ppermute | solution.py:524
  100.8 0.6 collective-permute-start.23
  101.4 0.8 collective-permute-done.20.refs_3_
  102.6 3.8 %known.1.base = f32[64,128,128]{2,1,0:T(8,128)S(1)} custom-call(bf16[64,256,128]{2,1,0:T(8,128)(2,1)S(1)} %copy-done.11, bf16[128,256]{1,0:T(8,128)(2,1)S(1)} %copy-done.22, f32[16,64,128]{2,1,0:T(8,128)S(1)} %copy-done.28, f32[16,64,128]{2,1,0:T(8,128)S(1)} %get-tuple-element.70.refs_1_, bf16[16,64,128]{2,1,0:T(8,128)(2,1)S(1)} %collective-permute-done.19.refs_2_, ...), custom_call_target="tpu_custom_call" | custom-call | flops 1 | bytes 8000000 | tf_op jit(solution)/shard_map/known/pallas_call | solution.py:428
  106.4 4.1 %collective-permute-done.24.by_a = bf16[16,128,128]{2,1,0:T(8,128)(2,1)S(1)} collective-permute-done((bf16[16,128,128]{2,1,0:T(8,128)(2,1)}, bf16[16,128,128]{2,1,0:T(8,128)(2,1)S(1)}, u32[]{:S(2)}, u32[]{:S(2)}) %collective-permute-start.24) | collective-permute-done | bytes 524320 | tf_op jit(solution)/shard_map/ppermute | solution.py:524
  111.0 1.3 %collective-permute-done.26.right_other = bf16[16,64,128]{2,1,0:T(8,128)(2,1)S(1)} collective-permute-done((bf16[16,64,128]{2,1,0:T(8,128)(2,1)S(1)}, bf16[16,64,128]{2,1,0:T(8,128)(2,1)S(1)}, u32[]{:S(2)}, u32[]{:S(2)}) %collective-permute-start.26) | collective-permute-done | bytes 262176 | tf_op jit(solution)/shard_map/ppermute | solution.py:516
  112.3 5.2 %tail.1 = bf16[128,64,128]{2,1,0:T(8,128)(2,1)} custom-call(f32[64,128,128]{2,1,0:T(8,128)S(1)} %known.1.base, bf16[64,128,128]{2,1,0:T(8,128)(2,1)S(1)} %copy-done.21, f32[64,1,128]{2,1,0:T(1,128)S(1)} %get-tuple-element.76.inverse, bf16[64,64,128]{2,1,0:T(8,128)(2,1)S(1)} %copy-done.26, f32[1,128]{1,0:T(1,128)S(1)} %bitcast.5, ...), custom_call_target="tpu_custom_call" | custom-call | flops 1 | bytes 8000000 | tf_op jit(solution)/shard_map/tail/pallas_call | solution.py:486
  (101 shorter events, 1.7 us)
Async XLA Ops:
  1.1 2.1 %collective-permute-start = (bf16[64,32,128]{2,1,0:T(8,128)(2,1)S(1)}, bf16[64,32,128]{2,1,0:T(8,128)(2,1)S(1)}, u32[]{:S(2)}, u32[]{:S(2)}) collective-permute-start(bf16[64,32,128]{2,1,0:T(8,128)(2,1)S(1)} %theirs.1), channel_id=1, source_target_pairs={{0,1},{1,0},{2,3},{3,2},{4,5},{5,4},{6,7},{7,6},{8,9},{9,8},{10,11... | collective-permute-start | bytes 1572872 | tf_op jit(solution)/shard_map/ppermute | solution.py:516
  3.5 39.9 %copy-start.6 = (bf16[16,128,128]{2,1,0:T(8,128)(2,1)}, bf16[16,128,128]{2,1,0:T(8,128)(2,1)S(1)}, u32[]{:S(2)}) copy-start(bf16[16,128,128]{2,1,0:T(8,128)(2,1)S(1)} %get-tuple-element.45.refs_0_.refs_6_) | copy-start | bytes 1572868
  3.5 53.9 %copy-start.2 = (bf16[16,128,128]{2,1,0:T(8,128)(2,1)}, bf16[16,128,128]{2,1,0:T(8,128)(2,1)S(1)}, u32[]{:S(2)}) copy-start(bf16[16,128,128]{2,1,0:T(8,128)(2,1)S(1)} %get-tuple-element.64.refs_0_.refs_6_) | copy-start | bytes 1572868
  3.5 10.1 %collective-permute-start.6 = (bf16[16,128,128]{2,1,0:T(8,128)(2,1)S(1)}, bf16[16,128,128]{2,1,0:T(8,128)(2,1)S(1)}, u32[]{:S(2)}, u32[]{:S(2)}) collective-permute-start(bf16[16,128,128]{2,1,0:T(8,128)(2,1)S(1)} %get-tuple-element.45.refs_0_.refs_6_), channel_id=1, source_target_pairs={{0,2},{1,5},{2,0},{3,7},{4,6},{5,1},{6,4},{7,3},{8,10},{9,13},{10,... | collective-permute-start | bytes 1572872 | tf_op jit(solution)/shard_map/ppermute | solution.py:534
  11.4 4.3 %collective-permute-start.1 = (bf16[32,64,128]{2,1,0:T(8,128)(2,1)S(1)}, bf16[32,64,128]{2,1,0:T(8,128)(2,1)S(1)}, u32[]{:S(2)}, u32[]{:S(2)}) collective-permute-start(bf16[32,64,128]{2,1,0:T(8,128)(2,1)S(1)} %get-tuple-element.49), channel_id=1, source_target_pairs={{0,1},{1,0},{2,3},{3,2},{4,5},{5,4},{6,7},{7,6},{8,9},{9,8},{10,11... | collective-permute-start | bytes 1572872 | tf_op jit(solution)/shard_map/ppermute | solution.py:516
  11.5 9.2 %collective-permute-start.2 = (bf16[16,128,128]{2,1,0:T(8,128)(2,1)S(1)}, bf16[16,128,128]{2,1,0:T(8,128)(2,1)S(1)}, u32[]{:S(2)}, u32[]{:S(2)}) collective-permute-start(bf16[16,128,128]{2,1,0:T(8,128)(2,1)S(1)} %get-tuple-element.45.refs_0_.refs_6_), channel_id=1, source_target_pairs={{0,4},{1,3},{2,6},{3,1},{4,0},{5,7},{6,2},{7,5},{8,12},{9,11},{10,... | collective-permute-start | bytes 1572872 | tf_op jit(solution)/shard_map/ppermute | solution.py:534
  13.6 29.8 %copy-start.7 = (bf16[16,128,128]{2,1,0:T(8,128)(2,1)}, bf16[16,128,128]{2,1,0:T(8,128)(2,1)S(1)}, u32[]{:S(2)}) copy-start(bf16[16,128,128]{2,1,0:T(8,128)(2,1)S(1)} %collective-permute-done.6.refs_1_.refs_7_) | copy-start | bytes 1572868
  13.6 12.7 %collective-permute-start.7 = (bf16[16,128,128]{2,1,0:T(8,128)(2,1)S(1)}, bf16[16,128,128]{2,1,0:T(8,128)(2,1)S(1)}, u32[]{:S(2)}, u32[]{:S(2)}) collective-permute-start(bf16[16,128,128]{2,1,0:T(8,128)(2,1)S(1)} %collective-permute-done.6.refs_1_.refs_7_), channel_id=1, source_target_pairs={{0,4},{1,3},{2,6},{3,1},{4,0},{5,7},{6,2},{7,5},{8,12},{9,11},{10,... | collective-permute-start | bytes 1572872 | tf_op jit(solution)/shard_map/ppermute | solution.py:534
  15.7 24.8 %copy-start.35 = (bf16[32,128,128]{2,1,0:T(8,128)(2,1)}, bf16[32,128,128]{2,1,0:T(8,128)(2,1)S(1)}, u32[]{:S(2)}) copy-start(bf16[32,128,128]{2,1,0:T(8,128)(2,1)S(1)} %constant_dynamic-update-slice_fusion.own) | copy-start | bytes 3145732
  15.7 24.1 %collective-permute-start.3 = (bf16[32,128,128]{2,1,0:T(8,128)(2,1)S(1)}, bf16[32,128,128]{2,1,0:T(8,128)(2,1)S(1)}, u32[]{:S(2)}, u32[]{:S(2)}) collective-permute-start(bf16[32,128,128]{2,1,0:T(8,128)(2,1)S(1)} %constant_dynamic-update-slice_fusion.own), channel_id=1, source_target_pairs={{0,8},{1,9},{2,10},{3,11},{4,12},{5,13},{6,14},{7,15},{8,0},{9,1},... | collective-permute-start | bytes 3145736 | tf_op jit(solution)/shard_map/ppermute | solution.py:524
  17.4 22.5 %collective-permute-start.5 = (bf16[32,128,128]{2,1,0:T(8,128)(2,1)S(1)}, bf16[32,128,128]{2,1,0:T(8,128)(2,1)S(1)}, u32[]{:S(2)}, u32[]{:S(2)}) collective-permute-start(bf16[32,128,128]{2,1,0:T(8,128)(2,1)S(1)} %constant_dynamic-update-slice_fusion.own), channel_id=1, source_target_pairs={{0,1},{1,0},{2,3},{3,2},{4,5},{5,4},{6,7},{7,6},{8,16},{9,17},{10,... | collective-permute-start | bytes 3145736 | tf_op jit(solution)/shard_map/ppermute | solution.py:524
  20.7 22.7 %copy-start.8 = (bf16[16,128,128]{2,1,0:T(8,128)(2,1)}, bf16[16,128,128]{2,1,0:T(8,128)(2,1)S(1)}, u32[]{:S(2)}) copy-start(bf16[16,128,128]{2,1,0:T(8,128)(2,1)S(1)} %collective-permute-done.2.refs_2_.refs_8_) | copy-start | bytes 1572868
  26.3 17.1 %copy-start.9 = (bf16[16,128,128]{2,1,0:T(8,128)(2,1)}, bf16[16,128,128]{2,1,0:T(8,128)(2,1)S(1)}, u32[]{:S(2)}) copy-start(bf16[16,128,128]{2,1,0:T(8,128)(2,1)S(1)} %collective-permute-done.7.refs_3_.refs_9_) | copy-start | bytes 1572868
  26.3 10.9 %collective-permute-start.12 = (bf16[16,128,128]{2,1,0:T(8,128)(2,1)S(1)}, bf16[16,128,128]{2,1,0:T(8,128)(2,1)S(1)}, u32[]{:S(2)}, u32[]{:S(2)}) collective-permute-start(bf16[16,128,128]{2,1,0:T(8,128)(2,1)S(1)} %get-tuple-element.64.refs_0_.refs_6_), channel_id=1, source_target_pairs={{0,2},{1,5},{2,0},{3,7},{4,6},{5,1},{6,4},{7,3},{8,10},{9,13},{10,... | collective-permute-start | bytes 1572872 | tf_op jit(solution)/shard_map/ppermute | solution.py:534
  36.5 2.0 %collective-permute-start.4 = (bf16[32,64,128]{2,1,0:T(8,128)(2,1)S(1)}, bf16[32,64,128]{2,1,0:T(8,128)(2,1)S(1)}, u32[]{:S(2)}, u32[]{:S(2)}) collective-permute-start(bf16[32,64,128]{2,1,0:T(8,128)(2,1)S(1)} %get-tuple-element.53), channel_id=1, source_target_pairs={{0,1},{1,0},{2,3},{3,2},{4,5},{5,4},{6,7},{7,6},{8,9},{9,8},{10,11... | collective-permute-start | bytes 1572872 | tf_op jit(solution)/shard_map/ppermute | solution.py:516
  36.5 9.7 %collective-permute-start.13 = (bf16[16,128,128]{2,1,0:T(8,128)(2,1)S(1)}, bf16[16,128,128]{2,1,0:T(8,128)(2,1)S(1)}, u32[]{:S(2)}, u32[]{:S(2)}) collective-permute-start(bf16[16,128,128]{2,1,0:T(8,128)(2,1)S(1)} %get-tuple-element.64.refs_0_.refs_6_), channel_id=1, source_target_pairs={{0,4},{1,3},{2,6},{3,1},{4,0},{5,7},{6,2},{7,5},{8,12},{9,11},{10,... | collective-permute-start | bytes 1572872 | tf_op jit(solution)/shard_map/ppermute | solution.py:534
  37.3 20.1 %copy-start.3 = (bf16[16,128,128]{2,1,0:T(8,128)(2,1)}, bf16[16,128,128]{2,1,0:T(8,128)(2,1)S(1)}, u32[]{:S(2)}) copy-start(bf16[16,128,128]{2,1,0:T(8,128)(2,1)S(1)} %collective-permute-done.12.refs_1_.refs_7_) | copy-start | bytes 1572868
  37.3 14.0 %collective-permute-start.14 = (bf16[16,128,128]{2,1,0:T(8,128)(2,1)S(1)}, bf16[16,128,128]{2,1,0:T(8,128)(2,1)S(1)}, u32[]{:S(2)}, u32[]{:S(2)}) collective-permute-start(bf16[16,128,128]{2,1,0:T(8,128)(2,1)S(1)} %collective-permute-done.12.refs_1_.refs_7_), channel_id=1, source_target_pairs={{0,4},{1,3},{2,6},{3,1},{4,0},{5,7},{6,2},{7,5},{8,12},{9,11},{10,... | collective-permute-start | bytes 1572872 | tf_op jit(solution)/shard_map/ppermute | solution.py:534
  39.8 11.5 %copy-start = (bf16[32,128,128]{2,1,0:T(8,128)(2,1)}, bf16[32,128,128]{2,1,0:T(8,128)(2,1)S(1)}, u32[]{:S(2)}) copy-start(bf16[32,128,128]{2,1,0:T(8,128)(2,1)S(1)} %collective-permute-done.3.by_a.refs_0_) | copy-start | bytes 3145732
  39.8 11.5 %copy-start.1 = (bf16[32,128,128]{2,1,0:T(8,128)(2,1)}, bf16[32,128,128]{2,1,0:T(8,128)(2,1)S(1)}, u32[]{:S(2)}) copy-start(bf16[32,128,128]{2,1,0:T(8,128)(2,1)S(1)} %collective-permute-done.5.by_b.refs_3_) | copy-start | bytes 3145732
  40.6 13.1 %collective-permute-start.8 = (bf16[16,128,128]{2,1,0:T(8,128)(2,1)S(1)}, bf16[16,128,128]{2,1,0:T(8,128)(2,1)S(1)}, u32[]{:S(2)}, u32[]{:S(2)}) collective-permute-start(bf16[16,128,128]{2,1,0:T(8,128)(2,1)S(1)} %get-tuple-element.54), channel_id=1, source_target_pairs={{0,8},{1,9},{2,10},{3,11},{4,12},{5,13},{6,14},{7,15},{8,0},{9,1},... | collective-permute-start | bytes 1572872 | tf_op jit(solution)/shard_map/ppermute | solution.py:524
  43.4 10.3 %collective-permute-start.9 = (bf16[16,128,128]{2,1,0:T(8,128)(2,1)S(1)}, bf16[16,128,128]{2,1,0:T(8,128)(2,1)S(1)}, u32[]{:S(2)}, u32[]{:S(2)}) collective-permute-start(bf16[16,128,128]{2,1,0:T(8,128)(2,1)S(1)} %get-tuple-element.55), channel_id=1, source_target_pairs={{0,1},{1,0},{2,3},{3,2},{4,5},{5,4},{6,7},{7,6},{8,16},{9,17},{10,... | collective-permute-start | bytes 1572872 | tf_op jit(solution)/shard_map/ppermute | solution.py:524
  46.2 11.2 %copy-start.4 = (bf16[16,128,128]{2,1,0:T(8,128)(2,1)}, bf16[16,128,128]{2,1,0:T(8,128)(2,1)S(1)}, u32[]{:S(2)}) copy-start(bf16[16,128,128]{2,1,0:T(8,128)(2,1)S(1)} %collective-permute-done.13.refs_2_.refs_8_) | copy-start | bytes 1572868
  52.0 14.9 %collective-permute-start.15 = (bf16[16,128,128]{2,1,0:T(8,128)(2,1)S(1)}, bf16[16,128,128]{2,1,0:T(8,128)(2,1)S(1)}, u32[]{:S(2)}, u32[]{:S(2)}) collective-permute-start(bf16[16,128,128]{2,1,0:T(8,128)(2,1)S(1)} %get-tuple-element.65), channel_id=1, source_target_pairs={{0,8},{1,9},{2,10},{3,11},{4,12},{5,13},{6,14},{7,15},{8,0},{9,1},... | collective-permute-start | bytes 1572872 | tf_op jit(solution)/shard_map/ppermute | solution.py:524
  53.7 13.3 %collective-permute-start.16 = (bf16[16,128,128]{2,1,0:T(8,128)(2,1)S(1)}, bf16[16,128,128]{2,1,0:T(8,128)(2,1)S(1)}, u32[]{:S(2)}, u32[]{:S(2)}) collective-permute-start(bf16[16,128,128]{2,1,0:T(8,128)(2,1)S(1)} %get-tuple-element.66), channel_id=1, source_target_pairs={{0,1},{1,0},{2,3},{3,2},{4,5},{5,4},{6,7},{7,6},{8,16},{9,17},{10,... | collective-permute-start | bytes 1572872 | tf_op jit(solution)/shard_map/ppermute | solution.py:524
  54.2 24.0 %collective-permute-start.10 = (bf16[16,128,128]{2,1,0:T(8,128)(2,1)S(1)}, bf16[16,128,128]{2,1,0:T(8,128)(2,1)S(1)}, u32[]{:S(2)}, u32[]{:S(2)}) collective-permute-start(bf16[16,128,128]{2,1,0:T(8,128)(2,1)S(1)} %get-tuple-element.57), channel_id=1, source_target_pairs={{0,8},{1,9},{2,10},{3,11},{4,12},{5,13},{6,14},{7,15},{8,0},{9,1},... | collective-permute-start | bytes 1572872 | tf_op jit(solution)/shard_map/ppermute | solution.py:524
  57.4 20.8 %copy-start.29 = (bf16[16,128,128]{2,1,0:T(8,128)(2,1)S(1)}, bf16[16,128,128]{2,1,0:T(8,128)(2,1)}, u32[]{:S(2)}) copy-start(bf16[16,128,128]{2,1,0:T(8,128)(2,1)} %get-tuple-element.61.up_sums) | copy-start | bytes 1572868
  57.4 20.8 %copy-start.30 = (bf16[16,128,128]{2,1,0:T(8,128)(2,1)S(1)}, bf16[16,128,128]{2,1,0:T(8,128)(2,1)}, u32[]{:S(2)}) copy-start(bf16[16,128,128]{2,1,0:T(8,128)(2,1)} %get-tuple-element.62.down_sums) | copy-start | bytes 1572868
  57.4 20.8 %collective-permute-start.11 = (bf16[16,128,128]{2,1,0:T(8,128)(2,1)S(1)}, bf16[16,128,128]{2,1,0:T(8,128)(2,1)S(1)}, u32[]{:S(2)}, u32[]{:S(2)}) collective-permute-start(bf16[16,128,128]{2,1,0:T(8,128)(2,1)S(1)} %get-tuple-element.58), channel_id=1, source_target_pairs={{0,1},{1,0},{2,3},{3,2},{4,5},{5,4},{6,7},{7,6},{8,16},{9,17},{10,... | collective-permute-start | bytes 1572872 | tf_op jit(solution)/shard_map/ppermute | solution.py:524
  66.9 12.6 %copy-start.12 = (bf16[16,128,128]{2,1,0:T(8,128)(2,1)}, bf16[16,128,128]{2,1,0:T(8,128)(2,1)S(1)}, u32[]{:S(2)}) copy-start(bf16[16,128,128]{2,1,0:T(8,128)(2,1)S(1)} %collective-permute-done.15.by_a.refs_1_) | copy-start | bytes 1572868
  67.0 12.6 %copy-start.13 = (bf16[16,128,128]{2,1,0:T(8,128)(2,1)}, bf16[16,128,128]{2,1,0:T(8,128)(2,1)S(1)}, u32[]{:S(2)}) copy-start(bf16[16,128,128]{2,1,0:T(8,128)(2,1)S(1)} %collective-permute-done.16.by_b.refs_4_) | copy-start | bytes 1572868
  67.4 22.0 %collective-permute-start.17 = (bf16[16,128,128]{2,1,0:T(8,128)(2,1)S(1)}, bf16[16,128,128]{2,1,0:T(8,128)(2,1)S(1)}, u32[]{:S(2)}, u32[]{:S(2)}) collective-permute-start(bf16[16,128,128]{2,1,0:T(8,128)(2,1)S(1)} %get-tuple-element.68), channel_id=1, source_target_pairs={{0,8},{1,9},{2,10},{3,11},{4,12},{5,13},{6,14},{7,15},{8,0},{9,1},... | collective-permute-start | bytes 1572872 | tf_op jit(solution)/shard_map/ppermute | solution.py:524
  70.2 19.2 %collective-permute-start.18 = (bf16[16,128,128]{2,1,0:T(8,128)(2,1)S(1)}, bf16[16,128,128]{2,1,0:T(8,128)(2,1)S(1)}, u32[]{:S(2)}, u32[]{:S(2)}) collective-permute-start(bf16[16,128,128]{2,1,0:T(8,128)(2,1)S(1)} %get-tuple-element.69), channel_id=1, source_target_pairs={{0,1},{1,0},{2,3},{3,2},{4,5},{5,4},{6,7},{7,6},{8,16},{9,17},{10,... | collective-permute-start | bytes 1572872 | tf_op jit(solution)/shard_map/ppermute | solution.py:524
  79.5 21.1 %collective-permute-start.21 = (bf16[16,128,128]{2,1,0:T(8,128)(2,1)}, bf16[16,128,128]{2,1,0:T(8,128)(2,1)S(1)}, u32[]{:S(2)}, u32[]{:S(2)}) collective-permute-start(bf16[16,128,128]{2,1,0:T(8,128)(2,1)} %get-tuple-element.73), channel_id=1, source_target_pairs={{0,8},{1,9},{2,10},{3,11},{4,12},{5,13},{6,14},{7,15},{8,0},{9,1},... | collective-permute-start | bytes 1572872 | tf_op jit(solution)/shard_map/ppermute | solution.py:524
  82.2 7.2 %copy-start.32 = (bf16[16,128,128]{2,1,0:T(8,128)(2,1)S(1)}, bf16[16,128,128]{2,1,0:T(8,128)(2,1)}, u32[]{:S(2)}) copy-start(bf16[16,128,128]{2,1,0:T(8,128)(2,1)} %get-tuple-element.81.down_sums) | copy-start | bytes 1572868
  82.2 18.5 %collective-permute-start.22 = (bf16[16,128,128]{2,1,0:T(8,128)(2,1)}, bf16[16,128,128]{2,1,0:T(8,128)(2,1)S(1)}, u32[]{:S(2)}, u32[]{:S(2)}) collective-permute-start(bf16[16,128,128]{2,1,0:T(8,128)(2,1)} %get-tuple-element.74), channel_id=1, source_target_pairs={{0,1},{1,0},{2,3},{3,2},{4,5},{5,4},{6,7},{7,6},{8,16},{9,17},{10,... | collective-permute-start | bytes 1572872 | tf_op jit(solution)/shard_map/ppermute | solution.py:524
  90.8 19.8 %collective-permute-start.24 = (bf16[16,128,128]{2,1,0:T(8,128)(2,1)}, bf16[16,128,128]{2,1,0:T(8,128)(2,1)S(1)}, u32[]{:S(2)}, u32[]{:S(2)}) collective-permute-start(bf16[16,128,128]{2,1,0:T(8,128)(2,1)} %get-tuple-element.82), channel_id=1, source_target_pairs={{0,8},{1,9},{2,10},{3,11},{4,12},{5,13},{6,14},{7,15},{8,0},{9,1},... | collective-permute-start | bytes 1572872 | tf_op jit(solution)/shard_map/ppermute | solution.py:524
  93.4 17.1 %collective-permute-start.25 = (bf16[16,128,128]{2,1,0:T(8,128)(2,1)}, bf16[16,128,128]{2,1,0:T(8,128)(2,1)S(1)}, u32[]{:S(2)}, u32[]{:S(2)}) collective-permute-start(bf16[16,128,128]{2,1,0:T(8,128)(2,1)} %get-tuple-element.83), channel_id=1, source_target_pairs={{0,1},{1,0},{2,3},{3,2},{4,5},{5,4},{6,7},{7,6},{8,16},{9,17},{10,... | collective-permute-start | bytes 1572872 | tf_op jit(solution)/shard_map/ppermute | solution.py:524
  93.4 9.1 %copy-start.22 = (bf16[128,256]{1,0:T(8,128)(2,1)S(1)}, bf16[128,256]{1,0:T(8,128)(2,1)}, u32[]{:S(2)}) copy-start(bf16[128,256]{1,0:T(8,128)(2,1)} %weight.5) | copy-start | bytes 196612
  93.4 9.1 %copy-start.28 = (f32[16,64,128]{2,1,0:T(8,128)S(1)}, f32[16,64,128]{2,1,0:T(8,128)}, u32[]{:S(2)}) copy-start(f32[16,64,128]{2,1,0:T(8,128)} %copy-done.27) | copy-start | bytes 1572868
  93.4 7.9 %collective-permute-start.19 = (bf16[16,64,128]{2,1,0:T(8,128)(2,1)S(1)}, bf16[16,64,128]{2,1,0:T(8,128)(2,1)S(1)}, u32[]{:S(2)}, u32[]{:S(2)}) collective-permute-start(bf16[16,64,128]{2,1,0:T(8,128)(2,1)S(1)} %get-tuple-element.71), channel_id=1, source_target_pairs={{0,1},{1,0},{2,3},{3,2},{4,5},{5,4},{6,7},{7,6},{8,9},{9,8},{10,11... | collective-permute-start | bytes 786440 | tf_op jit(solution)/shard_map/ppermute | solution.py:516
  94.0 8.6 %copy-start.11 = (bf16[64,256,128]{2,1,0:T(8,128)(2,1)S(1)}, bf16[64,256,128]{2,1,0:T(8,128)(2,1)}, u32[]{:S(2)}) copy-start(bf16[64,256,128]{2,1,0:T(8,128)(2,1)} %copy-done.10) | copy-start | bytes 12582916
  100.7 1.5 %collective-permute-start.20 = (bf16[16,64,128]{2,1,0:T(8,128)(2,1)S(1)}, bf16[16,64,128]{2,1,0:T(8,128)(2,1)S(1)}, u32[]{:S(2)}, u32[]{:S(2)}) collective-permute-start(bf16[16,64,128]{2,1,0:T(8,128)(2,1)S(1)} %get-tuple-element.72), channel_id=1, source_target_pairs={{0,1},{1,0},{2,3},{3,2},{4,5},{5,4},{6,7},{7,6},{8,9},{9,8},{10,11... | collective-permute-start | bytes 786440 | tf_op jit(solution)/shard_map/ppermute | solution.py:516
  100.8 1.7 %collective-permute-start.23 = (bf16[16,64,128]{2,1,0:T(8,128)(2,1)S(1)}, bf16[16,64,128]{2,1,0:T(8,128)(2,1)S(1)}, u32[]{:S(2)}, u32[]{:S(2)}) collective-permute-start(bf16[16,64,128]{2,1,0:T(8,128)(2,1)S(1)} %add_convert_fusion.1), channel_id=1, source_target_pairs={{0,1},{1,0},{2,3},{3,2},{4,5},{5,4},{6,7},{7,6},{8,9},{9,8},{10,11... | collective-permute-start | bytes 786440 | tf_op jit(solution)/shard_map/ppermute | solution.py:516
  102.6 8.0 %copy-start.24 = (bf16[16,128,128]{2,1,0:T(8,128)(2,1)S(1)}, bf16[16,128,128]{2,1,0:T(8,128)(2,1)}, u32[]{:S(2)}) copy-start(bf16[16,128,128]{2,1,0:T(8,128)(2,1)} %get-tuple-element.84.partials) | copy-start | bytes 1572868
  102.6 9.7 %copy-start.21 = (bf16[64,128,128]{2,1,0:T(8,128)(2,1)S(1)}, bf16[64,128,128]{2,1,0:T(8,128)(2,1)}, u32[]{:S(2)}) copy-start(bf16[64,128,128]{2,1,0:T(8,128)(2,1)} %copy-done.20) | copy-start | bytes 6291460
  102.6 9.7 %copy-start.34 = (f32[128]{0:T(128)S(1)}, f32[128]{0:T(128)}, u32[]{:S(2)}) copy-start(f32[128]{0:T(128)} %param.8) | copy-start | bytes 1540
  110.7 1.6 %collective-permute-start.26 = (bf16[16,64,128]{2,1,0:T(8,128)(2,1)S(1)}, bf16[16,64,128]{2,1,0:T(8,128)(2,1)S(1)}, u32[]{:S(2)}, u32[]{:S(2)}) collective-permute-start(bf16[16,64,128]{2,1,0:T(8,128)(2,1)S(1)} %add_convert_fusion), channel_id=1, source_target_pairs={{0,1},{1,0},{2,3},{3,2},{4,5},{5,4},{6,7},{7,6},{8,9},{9,8},{10,11... | collective-permute-start | bytes 786440 | tf_op jit(solution)/shard_map/ppermute | solution.py:516
  (15 other events, 70.7 us)
